TPU v7x, 32 devices: a whole 2x2x4 slice. The times are simulated.
32 devices in a mesh: groups: 2 (over y), dp: 4 (over z), din: 2 (over x), dout: 2 (over core).
Axes of the slice: x: 2, y: 2, z: 4, core: 2. Of those that a mesh axis runs over, the one named last changes fastest.
Arguments:
- activations: bfloat16 [2048, 4096], P(('groups', 'dp'), 'din'), parts along dimension 0, may hold values from -6 to 6
- out_grads: bfloat16 [2048, 14336], P(('groups', 'dp'), 'dout'), parts along dimension 0, may hold values from -6 to 6
- queries: bfloat16 [2, 2, 7168, 4096], P(None, 'dout', 'dp', 'din'), may hold values from -0.0007324219 to 0.0007324219
Outputs:
- scores: float32 [2, 2048], P(None, ('groups', 'dp')), parts along dimension 1
There are 2 independent parts, one for each index of `groups`. A program takes and returns all parts, laid end to end along the dimension named above; an argument that names none is the same for every part. Nothing has to cross between parts.
All inputs are finite; a program needn't handle non-finite values.
Results may differ from a plain program's by a relative error of at most 0.0003.
Values may be sent and summed in bfloat16 or wider, within the bound.
No kernel may reach another device: no remote copies, remote signals or barrier semaphores. Data moves between devices by JAX's collectives and lax.ppermute only.
A program may use at most 128 MiB of HBM per device.

v0:
```python
import jax
import jax.numpy as jnp
from jax import lax
from jax.sharding import PartitionSpec as P


def from_behind(block, axis, distance):
    devices = range(lax.axis_size(axis))
    route = [((i - distance) % len(devices), i) for i in devices]
    return lax.ppermute(block, axis, route)


def block_terms(grad_cols, piece, act_f):
    proj = jnp.einsum("tc,qci->qti", grad_cols, piece[:, 0], preferred_element_type=jnp.float32)
    return jnp.sum(act_f[None] * proj, axis=2)


def on_device(activations, out_grads, queries):
    act_f = activations.astype(jnp.float32)
    count = lax.axis_size("dp")
    me = lax.axis_index("dp")
    rows = queries.shape[2]
    zeros = jnp.zeros((queries.shape[0], activations.shape[0]), jnp.float32)

    def columns(anchor):
        return lax.dynamic_slice_in_dim(out_grads, anchor * rows, rows, 1)

    def advance(step, carry):
        held, total = carry
        anchor = (me - step) % count
        total = total + block_terms(columns(anchor), held, act_f)
        held = from_behind(held, "dp", 1)
        return (held, total)

    held, total = lax.fori_loop(0, count - 1, advance, (queries, zeros))
    total = total + block_terms(columns((me - (count - 1)) % count), held, act_f)
    return lax.psum(total, ("din", "dout"))


def solution(mesh):
    placed = (P(("groups", "dp"), "din"), P(("groups", "dp"), "dout"), P(None, "dout", "dp", "din"))
    return jax.shard_map(
        on_device, mesh=mesh, in_specs=placed, out_specs=P(None, ("groups", "dp")), check_vma=False
    )
```

profile of v0, /device:TPU:0, one launch (start us, length us, event | category | flops | bytes accessed | tf_op | source)
XLA Modules:
  0.0 1028.1 jit_solution(13410993020322626950)
XLA Ops:
  0.0 0.0 copy-start
  0.0 13.5 %copy.18 = bf16[2,1,1792,2048]{3,2,1,0:T(8,128)(2,1)} copy(bf16[2,1,1792,2048]{3,2,1,0:T(8,128)(2,1)} %param.7) | data formatting | bytes 29360128
  13.5 0.0 copy-done
  13.5 0.2 convert_element_type.3
  13.8 997.4 %while.18 = (s32[]{:T(128)}, bf16[2,1,1792,2048]{3,2,0,1:T(8,128)(2,1)}, f32[2,256]{1,0:T(2,128)S(1)}, f32[256,2048]{1,0:T(8,128)S(1)}, s32[]{:T(128)}, /*index=...) while((s32[]{:T(128)}, ...), condition=%wide.region_2.3_spmd.clone, body=%wide.region_0.2_spmd.clone.sunk | while | flops 3760194048 | bytes 105783632 | solution.py:35
  13.8 13.5 %copy.12 = bf16[2,1,1792,2048]{3,2,0,1:T(8,128)(2,1)} copy(bf16[2,1,1792,2048]{3,2,0,1:T(8,128)(2,1)} %get-tuple-element.252) | data formatting | bytes 29360128 | tf_op jit(solution)/shard_map/while
  27.3 3.0 collective-permute-start
  30.3 9.6 multiply_reduce_fusion.2
  40.0 308.0 %collective-permute-done = bf16[2,1,1792,2048]{3,2,0,1:T(8,128)(2,1)} collective-permute-done((bf16[2,1,1792,2048]{3,2,0,1:T(8,128)(2,1)}, bf16[2,1,1792,2048]{3,2,0,1:T(8,128)(2,1)}, u32[]{:S(2)}, u32[]{:S(2)}) %collective-permute-start) | collective-permute-done | bytes 14680096 | tf_op jit(solution)/shard_map/while/body/eval_jaxpr/ppermute | solution.py:10
  347.9 13.5 %copy.12 = bf16[2,1,1792,2048]{3,2,0,1:T(8,128)(2,1)} copy(bf16[2,1,1792,2048]{3,2,0,1:T(8,128)(2,1)} %get-tuple-element.252) | data formatting | bytes 29360128 | tf_op jit(solution)/shard_map/while
  361.5 0.0 collective-permute-start
  361.5 9.6 multiply_reduce_fusion.2
  371.1 308.9 %collective-permute-done = bf16[2,1,1792,2048]{3,2,0,1:T(8,128)(2,1)} collective-permute-done((bf16[2,1,1792,2048]{3,2,0,1:T(8,128)(2,1)}, bf16[2,1,1792,2048]{3,2,0,1:T(8,128)(2,1)}, u32[]{:S(2)}, u32[]{:S(2)}) %collective-permute-start) | collective-permute-done | bytes 14680096 | tf_op jit(solution)/shard_map/while/body/eval_jaxpr/ppermute | solution.py:10
  680.0 13.5 %copy.12 = bf16[2,1,1792,2048]{3,2,0,1:T(8,128)(2,1)} copy(bf16[2,1,1792,2048]{3,2,0,1:T(8,128)(2,1)} %get-tuple-element.252) | data formatting | bytes 29360128 | tf_op jit(solution)/shard_map/while
  693.5 0.0 collective-permute-start
  693.5 9.6 multiply_reduce_fusion.2
  703.2 308.0 %collective-permute-done = bf16[2,1,1792,2048]{3,2,0,1:T(8,128)(2,1)} collective-permute-done((bf16[2,1,1792,2048]{3,2,0,1:T(8,128)(2,1)}, bf16[2,1,1792,2048]{3,2,0,1:T(8,128)(2,1)}, u32[]{:S(2)}, u32[]{:S(2)}) %collective-permute-start) | collective-permute-done | bytes 14680096 | tf_op jit(solution)/shard_map/while/body/eval_jaxpr/ppermute | solution.py:10
  1011.2 0.5 copy.5
  1011.7 10.1 fusion.9
  1021.8 6.2 psum.7
  (5 shorter events, 0.0 us)
Async XLA Ops:
  0.0 13.5 %copy-start = (bf16[256,2048]{1,0:T(8,128)(2,1)S(1)}, bf16[256,2048]{1,0:T(8,128)(2,1)}, u32[]{:S(2)}) copy-start(bf16[256,2048]{1,0:T(8,128)(2,1)} %param.5) | copy-start | bytes 3145732
  27.3 320.6 %collective-permute-start = (bf16[2,1,1792,2048]{3,2,0,1:T(8,128)(2,1)}, bf16[2,1,1792,2048]{3,2,0,1:T(8,128)(2,1)}, u32[]{:S(2)}, u32[]{:S(2)}) collective-permute-start(bf16[2,1,1792,2048]{3,2,0,1:T(8,128)(2,1)} %copy.12), channel_id=1, source_target_pairs={{12,0},{0,4},{4,8},{8,12},{13,1},{1,5},{5,9},{9,13},{14,2},{2,6},{... | collective-permute-start | bytes 44040200 | tf_op jit(solution)/shard_map/while/body/eval_jaxpr/ppermute | solution.py:10
  361.5 318.6 %collective-permute-start = (bf16[2,1,1792,2048]{3,2,0,1:T(8,128)(2,1)}, bf16[2,1,1792,2048]{3,2,0,1:T(8,128)(2,1)}, u32[]{:S(2)}, u32[]{:S(2)}) collective-permute-start(bf16[2,1,1792,2048]{3,2,0,1:T(8,128)(2,1)} %copy.12), channel_id=1, source_target_pairs={{12,0},{0,4},{4,8},{8,12},{13,1},{1,5},{5,9},{9,13},{14,2},{2,6},{... | collective-permute-start | bytes 44040200 | tf_op jit(solution)/shard_map/while/body/eval_jaxpr/ppermute | solution.py:10
  693.5 317.7 %collective-permute-start = (bf16[2,1,1792,2048]{3,2,0,1:T(8,128)(2,1)}, bf16[2,1,1792,2048]{3,2,0,1:T(8,128)(2,1)}, u32[]{:S(2)}, u32[]{:S(2)}) collective-permute-start(bf16[2,1,1792,2048]{3,2,0,1:T(8,128)(2,1)} %copy.12), channel_id=1, source_target_pairs={{12,0},{0,4},{4,8},{8,12},{13,1},{1,5},{5,9},{9,13},{14,2},{2,6},{... | collective-permute-start | bytes 44040200 | tf_op jit(solution)/shard_map/while/body/eval_jaxpr/ppermute | solution.py:10
where the time goes:
time: 1030 us
  waiting for transfers between devices  925 us (90%)
  local copies, waits for them, and re-layouts  54.6 us (5%)
  matrix products  39 us (4%)
    ppermute x3, waiting for transfers between devices, from_behind(): return lax.ppermute(block, axis, route)  925 us
    while x3, local copies, waits for them, and re-layouts  40.5 us
    dot_general x4, matrix products, block_terms(): jnp.einsum('tc,qci->qti', grad_cols, piece[:, 0], preferred_element_type=...  39 us
  transfers between devices with their start and end apart: 3, of which 3 were waited for; matrix products, arithmetic and copies ran while one was open for 3% of the time, Pallas kernels for 0%

commit v1 on v0

v1 whole, which is shorter than its diff:
```python
import jax
import jax.numpy as jnp
from jax import lax
from jax.sharding import PartitionSpec as P


def share(block, axis):
    part = block.shape[0] // lax.axis_size(axis)
    return lax.dynamic_slice_in_dim(block, lax.axis_index(axis) * part, part, 0)


def on_device(activations, out_grads, queries):
    count = lax.axis_size("dp")
    tokens = activations.shape[0]
    rows = queries.shape[2]

    mine = share(out_grads, "din")
    part = mine.shape[0]
    blocks = mine.reshape(part, count, rows).transpose(1, 0, 2)
    blocks = lax.all_to_all(blocks, "dp", 0, 0)
    grads = lax.all_gather(blocks, "din", axis=1).reshape(count * tokens, rows)

    acts = lax.all_gather(share(activations, "dout"), ("dp", "dout"), axis=0, tiled=True)

    proj = jnp.einsum("tc,qci->qti", grads, queries[:, 0], preferred_element_type=jnp.float32)
    total = jnp.sum(acts.astype(jnp.float32)[None] * proj, axis=2)
    total = lax.psum(total, ("dp", "din", "dout"))
    return lax.dynamic_slice_in_dim(total, lax.axis_index("dp") * tokens, tokens, 1)


def solution(mesh):
    placed = (P(("groups", "dp"), "din"), P(("groups", "dp"), "dout"), P(None, "dout", "dp", "din"))
    return jax.shard_map(
        on_device, mesh=mesh, in_specs=placed, out_specs=P(None, ("groups", "dp")), check_vma=False
    )
```

time: 1030 us -> 222 us (0.22)
  waiting for transfers between devices: 925 us -> 92 us
  blocking collectives: 6.24 us -> 80.7 us
  local copies, waits for them, and re-layouts: 54.6 us -> 13.7 us
  matrix products: 39 us -> 18.4 us
  between operations: 0.04 us -> 13.5 us
    ppermute x3 -> x0, waiting for transfers between devices: 925 us -> none  [from_behind(): return lax.ppermute(block, axis, route)]
    all_gather x0 -> x2, waiting for transfers between devices: none -> 92 us  [the longest x1 49.2 us: on_device(): grads = lax.all_gather(blocks, 'din', axis=1).reshape(count * tokens, rows)]
    all_to_all x0 -> x1, blocking collectives: none -> 48.8 us  [on_device(): blocks = lax.all_to_all(blocks, 'dp', 0, 0)]
    while x3 -> x0, local copies, waits for them, and re-layouts: 40.5 us -> none
    psum x1, blocking collectives: 6.24 us -> 31.9 us  [on_device(): total = lax.psum(total, ('dp', 'din', 'dout'))]
    dot_general x4 -> x1, matrix products: 39 us -> 18.4 us  [on_device(): jnp.einsum('tc,qci->qti', grads, queries[:, 0], preferred_element_type=jn...]
  transfers between devices with their start and end apart: 3 -> 2, of which waited for: 3 -> 2; matrix products, arithmetic and copies ran while one was open for 3% -> 3% of each run, Pallas kernels for 0% -> 0%
where the time goes in v1:
time: 222 us
  waiting for transfers between devices  92 us (41%)
  blocking collectives  80.7 us (36%)
  matrix products  18.4 us (8%)
  local copies, waits for them, and re-layouts  13.7 us (6%)
  between operations  13.5 us (6%)
  other arithmetic  3.41 us (2%)
    all_gather x1, waiting for transfers between devices, on_device(): grads = lax.all_gather(blocks, 'din', axis=1).reshape(count * tokens, rows)  49.2 us
    all_to_all x1, blocking collectives, on_device(): blocks = lax.all_to_all(blocks, 'dp', 0, 0)  48.8 us
    all_gather x1, waiting for transfers between devices, on_device(): lax.all_gather(share(activations, 'dout'), ('dp', 'dout'), axis=0, tiled=...  42.8 us
    psum x1, blocking collectives, on_device(): total = lax.psum(total, ('dp', 'din', 'dout'))  31.9 us
    dot_general x1, matrix products, on_device(): jnp.einsum('tc,qci->qti', grads, queries[:, 0], preferred_element_type=jn...  18.4 us
    all_gather x1, local copies, waits for them, and re-layouts, on_device(): grads = lax.all_gather(blocks, 'din', axis=1).reshape(count * tokens, rows)  6.03 us
  transfers between devices with their start and end apart: 2, of which 2 were waited for; matrix products, arithmetic and copies ran while one was open for 3% of the time, Pallas kernels for 0%

profile of v1, /device:TPU:0, one launch (start us, length us, event | category | flops | bytes accessed | tf_op | source)
XLA Modules:
  0.0 221.7 jit_solution(6930255896583028844)
XLA Ops:
  6.5 0.0 copy-start
  6.5 0.0 all-gather.6.cloned.1.call-start
  6.5 3.0 %constant_dynamic-slice_fusion.1 = bf16[128,7168]{1,0:T(8,128)(2,1)} fusion(bf16[256,7168]{1,0:T(8,128)(2,1)} %param.4, s32[]{:T(128)S(6)} %select_n.10), kind=kLoop, calls=%fused_computation.4 | loop fusion | bytes 3670020 | tf_op jit(solution)/shard_map/dynamic_slice | solution.py:9
  9.5 3.3 %copy.6 = bf16[128,7168]{0,1:T(8,128)(2,1)S(1)} copy(bf16[128,7168]{1,0:T(8,128)(2,1)} %constant_dynamic-slice_fusion.1) | data formatting | bytes 3670016
  12.8 48.8 %all_to_all.5 = bf16[4,128,1792]{1,2,0:T(8,128)(2,1)} all-to-all(bf16[4,128,1792]{1,2,0:T(8,128)(2,1)S(1)} %bitcast.13), channel_id=1, replica_groups=mesh['groups'=2,'dp'=4,'din'=2,'dout'=2] {'dp'}, dimensions={0} | all-to-all | bytes 3670016 | tf_op jit(solution)/shard_map/all_to_all | solution.py:20
  61.6 0.0 all-gather.6.cloned.1.call-update
  61.6 0.0 all-gather.4.cloned.1.call-start
  61.7 0.0 copy-done
  61.7 0.8 constant_dynamic-slice_fusion.2
  62.5 0.0 all-gather.4.cloned.1.call-update
  62.6 49.2 %all-gather.6.cloned.1.call-done = bf16[4,256,1792]{1,2,0:T(8,128)(2,1)} async-done(((bf16[4,128,1792]{1,2,0:T(8,128)(2,1)}), bf16[4,256,1792]{1,2,0:T(8,128)(2,1)}) %all-gather.6.cloned.1.call-update) | async-done | bytes 3670032 | tf_op jit(solution)/shard_map/all_gather | solution.py:21
  111.8 6.0 %copy.5 = bf16[4,256,1792]{2,1,0:T(8,128)(2,1)} copy(bf16[4,256,1792]{1,2,0:T(8,128)(2,1)} %all-gather.6.cloned.1.call-done) | data formatting | bytes 7340032 | tf_op jit(solution)/shard_map/all_gather | solution.py:21
  117.8 42.8 %all-gather.4.cloned.1.call-done = bf16[1024,2048]{1,0:T(8,128)(2,1)} async-done(((bf16[128,2048]{1,0:T(8,128)(2,1)}), bf16[1024,2048]{1,0:T(8,128)(2,1)}) %all-gather.4.cloned.1.call-update) | async-done | bytes 4194320 | tf_op jit(solution)/shard_map/all_gather | solution.py:23
  160.5 0.0 copy-start.1
  160.6 3.4 %convert_element_type.3 = f32[1024,2048]{1,0:T(8,128)S(1)} convert(bf16[1024,2048]{1,0:T(8,128)(2,1)} %all-gather.4.cloned.1.call-done) | non-fusion elementwise | flops 2097152 | bytes 12582912 | tf_op jit(solution)/shard_map/convert_element_type | solution.py:26
  164.0 0.0 copy-done.1
  164.0 18.4 %multiply_reduce_fusion = f32[1024,2]{0,1:T(2,128)S(1)} fusion(f32[1024,2048]{1,0:T(8,128)S(1)} %convert_element_type.3, bf16[1024,1792,1]{1,0,2:T(8,128)(2,1)S(1)} %bitcast.14, bf16[2,1,1792,2048]{3,2,1,0:T(8,128)(2,1)} %param.5), kind=kOutput, calls=%fused_computation | convolution fusion | flops 15040772096 | bytes 26746880 | tf_op jit(solution)/shard_map/tc,qci->qti/dot_general | solution.py:25
  182.4 31.9 %psum.7 = f32[2,1024]{1,0:T(2,128)S(1)} all-reduce(f32[2,1024]{1,0:T(2,128)S(1)} %bitcast.15), channel_id=1, replica_groups=mesh['groups'=2,'dp'=4,'din'=2,'dout'=2] {'dp','din','dout'}, use_global_device_ids=true, to_apply=%region_1.0 | all-reduce | flops 2048 | bytes 16384 | tf_op jit(solution)/shard_map/psum | solution.py:27
  214.3 0.6 constant_dynamic-slice_fusion
Async XLA Ops:
  6.5 55.1 %copy-start = (bf16[256,2048]{1,0:T(8,128)(2,1)S(1)}, bf16[256,2048]{1,0:T(8,128)(2,1)}, u32[]{:S(2)}) copy-start(bf16[256,2048]{1,0:T(8,128)(2,1)} %param.3) | copy-start | bytes 3145732
  6.5 105.2 %all-gather.6.cloned.1.call-start = ((), (), s32[]{:S(2)}) async-start(), calls=%async_computation.2 | async-start | bytes 5505024 | tf_op jit(solution)/shard_map/all_gather | solution.py:21
  61.6 98.9 %all-gather.4.cloned.1.call-start = ((), (), s32[]{:S(2)}) async-start(), calls=%async_computation.1 | async-start | bytes 4718592 | tf_op jit(solution)/shard_map/all_gather | solution.py:23
  160.5 3.4 %copy-start.1 = (bf16[4,256,1792]{2,1,0:T(8,128)(2,1)S(1)}, bf16[4,256,1792]{2,1,0:T(8,128)(2,1)}, u32[]{:S(2)}) copy-start(bf16[4,256,1792]{2,1,0:T(8,128)(2,1)} %copy.5) | copy-start | bytes 11010052
Sparse Core Ops, SparseCore 0:
  61.7 49.9 all-gather.5
  113.4 47.1 all-gather.3

commit v2 on v1

v2 whole, which is shorter than its diff:
```python
import functools

import jax
import jax.numpy as jnp
from jax import lax
from jax.experimental import pallas as pl
from jax.experimental.pallas import tpu as pltpu
from jax.sharding import PartitionSpec as P


def partner(index, step, count):
    if count & (count - 1) == 0:
        return index ^ step
    return (step - index) % count


def trade(block, steps):
    axes = tuple(steps)
    sizes = [lax.axis_size(axis) for axis in axes]
    route = []
    for source in range(functools.reduce(lambda a, b: a * b, sizes)):
        rest, target, scale = source, 0, 1
        for axis, size in zip(reversed(axes), reversed(sizes)):
            target += partner(rest % size, steps[axis], size) * scale
            rest //= size
            scale *= size
        route.append((source, target))
    return lax.ppermute(block, axes, route)


def slot_kernel(where, *refs):
    parts, (acts_ref, query_ref, out_ref, grads, sums) = refs[:-5], refs[-5:]
    query, tile = pl.program_id(0), pl.program_id(1)
    rows = parts[0].shape[0]

    @pl.when((query == 0) & (tile == 0))
    def _():
        for r, part in enumerate(parts):
            at = pl.multiple_of(where[1 + r] * rows, rows)
            grads[pl.ds(at, rows), :] = part[...]

    @pl.when(tile == 0)
    def _():
        sums[...] = jnp.zeros_like(sums)

    proj = jnp.dot(grads[...], query_ref[0, 0], preferred_element_type=jnp.float32)
    terms = acts_ref[...].astype(jnp.float32) * proj
    lanes = sums.shape[1]
    total = sums[...]
    for at in range(0, terms.shape[1], lanes):
        total = total + terms[:, at : at + lanes]
    sums[...] = total

    @pl.when(tile == pl.num_programs(1) - 1)
    def _():
        out_ref[pl.ds(query, 1), :] = jnp.sum(total.T, axis=0, keepdims=True)


def slot_scores(parts, order, acts, block, queries):
    nq, _, depth, width = queries.shape
    tokens = sum(part.shape[0] for part in parts)
    tile = min(512, width)
    where = jnp.stack([block] + list(order)).astype(jnp.int32)
    spec = pltpu.PrefetchScalarGridSpec(
        num_scalar_prefetch=1,
        grid=(nq, width // tile),
        in_specs=[pl.BlockSpec(part.shape, lambda q, i, where: (0, 0)) for part in parts]
        + [
            pl.BlockSpec((tokens, tile), lambda q, i, where: (where[0], i)),
            pl.BlockSpec((1, 1, depth, tile), lambda q, i, where: (q, 0, 0, i)),
        ],
        out_specs=pl.BlockSpec((nq, tokens), lambda q, i, where: (0, 0)),
        scratch_shapes=[pltpu.VMEM((tokens, depth), parts[0].dtype), pltpu.VMEM((tokens, 128), jnp.float32)],
    )
    return pl.pallas_call(
        slot_kernel,
        grid_spec=spec,
        out_shape=jax.ShapeDtypeStruct((nq, tokens), jnp.float32),
        compiler_params=pltpu.CompilerParams(vmem_limit_bytes=52 * 1024 * 1024),
        cost_estimate=pl.CostEstimate(
            flops=2 * nq * tokens * depth * width,
            bytes_accessed=2 * (nq * depth * width + tokens * (depth + width)),
            transcendentals=0,
        ),
    )(where, *parts, acts, queries)


def on_device(activations, out_grads, queries):
    count, spread = lax.axis_size("dp"), lax.axis_size("din")
    me, column = lax.axis_index("dp"), lax.axis_index("din")
    tokens, rows = activations.shape[0], queries.shape[2]
    part, half = tokens // spread, tokens // lax.axis_size("dout")

    def grads_for(device):
        return lax.dynamic_slice(out_grads, (column * part, device * rows), (part, rows))

    acts = lax.dynamic_slice_in_dim(activations, lax.axis_index("dout") * half, half, 0)
    acts = lax.all_gather(acts, ("dp", "dout"), axis=0, tiled=True)

    steps = sorted(range(1, count), key=lambda d: -d)
    arrived = {d: trade(grads_for(partner(me, d, count)), {"dp": d}) for d in steps}

    own = lax.dynamic_slice_in_dim(out_grads, me * rows, rows, 1)
    zero = jnp.zeros((), jnp.int32)
    home = slot_scores([own], [zero], activations, zero, queries)

    sides = range(spread)
    order = [partner(column, r, spread) for r in sides]
    last = None
    for d in steps:
        parts = [arrived[d]] + [trade(arrived[d], {"din": r}) for r in sides[1:]]
        last = slot_scores(parts, order, acts, partner(me, d, count), queries)
        if d != steps[-1]:
            home = home + trade(last, {"dp": d})
    pairs = [(r, c) for r in sides for c in range(lax.axis_size("dout"))]
    total = home
    for r, c in pairs[1:]:
        total = total + trade(home, {"din": r, "dout": c})
    for r, c in pairs:
        total = total + trade(last, {"dp": steps[-1], "din": r, "dout": c})
    return total


def solution(mesh):
    placed = (P(("groups", "dp"), "din"), P(("groups", "dp"), "dout"), P(None, "dout", "dp", "din"))
    return jax.shard_map(
        on_device, mesh=mesh, in_specs=placed, out_specs=P(None, ("groups", "dp")), check_vma=False
    )
```

time: 222 us -> 143 us (0.64)
  blocking collectives: 80.7 us -> 0 us
  Pallas kernels: 0 us -> 43.3 us
  waiting for transfers between devices: 92 us -> 61.6 us
  matrix products: 18.4 us -> 0 us
  starting transfers between devices: 0.04 us -> 18 us
  local copies, waits for them, and re-layouts: 13.7 us -> 5.39 us
  other arithmetic: 3.41 us -> 0.82 us
    all_gather x2 -> x1, waiting for transfers between devices: 92 us -> 0.01 us  [on_device(): acts = lax.all_gather(acts, ('dp', 'dout'), axis=0, tiled=True)]
    ppermute x0 -> x15, waiting for transfers between devices: none -> 61.6 us  [trade(): return lax.ppermute(block, axes, route)]
    all_to_all x1 -> x0, blocking collectives: 48.8 us -> none  [on_device(): blocks = lax.all_to_all(blocks, 'dp', 0, 0)]
    pallas_call x0 -> x4, Pallas kernels: none -> 43.3 us  [slot_scores(): pl.pallas_call(slot_kernel, grid_spec=spec, out_shape=jax.ShapeDtypeStruc...]
    psum x1 -> x0, blocking collectives: 31.9 us -> none  [on_device(): total = lax.psum(total, ('dp', 'din', 'dout'))]
    dot_general x1 -> x0, matrix products: 18.4 us -> none  [on_device(): jnp.einsum('tc,qci->qti', grads, queries[:, 0], preferred_element_type=jn...]
    ppermute x0 -> x15, starting transfers between devices: none -> 18 us  [trade(): return lax.ppermute(block, axes, route)]
    all_gather x1 -> x0, local copies, waits for them, and re-layouts: 6.03 us -> none  [on_device(): grads = lax.all_gather(blocks, 'din', axis=1).reshape(count * tokens, rows)]
  transfers between devices with their start and end apart: 2 -> 16, of which waited for: 2 -> 4; matrix products, arithmetic and copies ran while one was open for 3% -> 3% of each run, Pallas kernels for 0% -> 30%
where the time goes in v2:
time: 143 us
  waiting for transfers between devices  61.6 us (43%)
  Pallas kernels  43.3 us (30%)
  starting transfers between devices  18 us (13%)
  between operations  13.5 us (9%)
  local copies, waits for them, and re-layouts  5.39 us (4%)
    ppermute x15, waiting for transfers between devices, trade(): return lax.ppermute(block, axes, route)  61.6 us
    pallas_call x4, Pallas kernels, slot_scores(): pl.pallas_call(slot_kernel, grid_spec=spec, out_shape=jax.ShapeDtypeStruc...  43.3 us
    ppermute x15, starting transfers between devices, trade(): return lax.ppermute(block, axes, route)  18 us
  transfers between devices with their start and end apart: 16, of which 4 were waited for; matrix products, arithmetic and copies ran while one was open for 3% of the time, Pallas kernels for 30%

profile of v2, /device:TPU:0, one launch (start us, length us, event | category | flops | bytes accessed | tf_op | source)
XLA Modules:
  0.0 142.7 jit_solution(1156886876746005643)
XLA Ops:
  6.5 2.0 %constant_dynamic-slice_fusion = bf16[128,2048]{1,0:T(8,128)(2,1)} fusion(bf16[256,2048]{1,0:T(8,128)(2,1)} %refs_1_.1, s32[]{:T(128)S(6)} %select_n.23), kind=kLoop, calls=%fused_computation.5 | loop fusion | bytes 1048580 | tf_op jit(solution)/shard_map/dynamic_slice | solution.py:97
  8.5 0.0 all-gather.2.cloned.1.call-update
  8.6 2.2 %fusion = (bf16[128,1792]{1,0:T(8,128)(2,1)S(1)}, bf16[128,1792]{1,0:T(8,128)(2,1)S(1)}, bf16[128,1792]{1,0:T(8,128)(2,1)}) fusion(bf16[256,7168]{1,0:T(8,128)(2,1)} %param.4, s32[]{:T(128)S(6)} %select_n.21, s32[]{:T(128)S(6)} %select_n.22, s32[]{:T(128)S(6)} %select_n.25, s32[]{:T(128)S(6)} %select_n.24), kind=kLoop, calls=%fused_computation.7 | loop fusion | bytes 2752528 | tf_op jit(solution)/shard_map/dynamic_slice | solution.py:95
  10.7 5.0 %collective-permute-start = (bf16[128,1792]{1,0:T(8,128)(2,1)S(1)}, bf16[128,1792]{1,0:T(8,128)(2,1)S(1)}, u32[]{:S(2)}, u32[]{:S(2)}) collective-permute-start(bf16[128,1792]{1,0:T(8,128)(2,1)S(1)} %get-tuple-element.5), channel_id=1, source_target_pairs={{0,12},{4,8},{8,4},{12,0},{1,13},{5,9},{9,5},{13,1},{2,14},{6,10},... | collective-permute-start | bytes 1376264 | tf_op jit(solution)/shard_map/ppermute | solution.py:28
  15.8 0.6 collective-permute-start.3
  16.4 0.1 add_add_fusion.2.where
  16.4 1.2 constant_dynamic-slice_fusion.1.refs_0_
  17.7 0.1 add_add_fusion.3.where
  17.8 15.6 %collective-permute-done.refs_0_ = bf16[128,1792]{1,0:T(8,128)(2,1)S(1)} collective-permute-done((bf16[128,1792]{1,0:T(8,128)(2,1)S(1)}, bf16[128,1792]{1,0:T(8,128)(2,1)S(1)}, u32[]{:S(2)}, u32[]{:S(2)}) %collective-permute-start) | collective-permute-done | bytes 458784 | tf_op jit(solution)/shard_map/ppermute | solution.py:28
  33.4 1.3 collective-permute-start.1
  34.6 10.7 %shard_map.37 = f32[2,256]{1,0:T(2,128)S(1)} custom-call(s32[2]{0:T(128)S(1)} %broadcast_1_where.2.where, bf16[256,1792]{1,0:T(8,128)(2,1)S(1)} %constant_dynamic-slice_fusion.1.refs_0_, bf16[256,2048]{1,0:T(8,128)(2,1)S(1)} %copy-done, bf16[2,1,1792,2048]{3,2,1,0:T(8,128)(2,1)} %refs_3_.5), custom_call_target="tpu_custom_call" | custom-call | flops 3758096384 | bytes 16646144 | tf_op jit(solution)/shard_map/pallas_call | solution.py:75
  45.3 43.3 %collective-permute-done.3.refs_0_ = bf16[128,1792]{1,0:T(8,128)(2,1)S(1)} collective-permute-done((bf16[128,1792]{1,0:T(8,128)(2,1)}, bf16[128,1792]{1,0:T(8,128)(2,1)S(1)}, u32[]{:S(2)}, u32[]{:S(2)}) %collective-permute-start.3) | collective-permute-done | bytes 458784 | tf_op jit(solution)/shard_map/ppermute | solution.py:28
  88.7 1.5 %collective-permute-start.4 = (bf16[128,1792]{1,0:T(8,128)(2,1)S(1)}, bf16[128,1792]{1,0:T(8,128)(2,1)S(1)}, u32[]{:S(2)}, u32[]{:S(2)}) collective-permute-start(bf16[128,1792]{1,0:T(8,128)(2,1)S(1)} %collective-permute-done.3.refs_0_), channel_id=1, source_target_pairs={{0,2},{2,0},{1,3},{3,1},{4,6},{6,4},{5,7},{7,5},{8,10},{10,8},{9,1... | collective-permute-start | bytes 1376264 | tf_op jit(solution)/shard_map/ppermute | solution.py:28
  90.1 0.1 add_add_fusion.4.where
  90.2 0.5 collective-permute-start.10
  90.8 0.0 collective-permute-done.1.refs_1_
  90.8 10.9 %shard_map.38 = f32[2,256]{1,0:T(2,128)S(1)} custom-call(s32[3]{0:T(128)S(1)} %add_add_fusion.2.where, bf16[128,1792]{1,0:T(8,128)(2,1)S(1)} %collective-permute-done.refs_0_, bf16[128,1792]{1,0:T(8,128)(2,1)S(1)} %collective-permute-done.1.refs_1_, bf16[1024,2048]{1,0:T(8,128)(2,1)} %all-gather.2.cloned.1.call-done.refs_2_, bf16[2,1,1792,2048]{3,2,1,0:T(8,128)(2,1)} %refs_3_.5), custom_call_target="tpu_custom_call" | custom-call | flops 3758096384 | bytes 16646144 | tf_op jit(solution)/shard_map/pallas_call | solution.py:75
  101.7 2.5 %collective-permute-start.2 = (f32[2,256]{1,0:T(2,128)S(1)}, f32[2,256]{1,0:T(2,128)S(1)}, u32[]{:S(2)}, u32[]{:S(2)}) collective-permute-start(f32[2,256]{1,0:T(2,128)S(1)} %shard_map.38), channel_id=1, source_target_pairs={{0,12},{4,8},{8,4},{12,0},{1,13},{5,9},{9,5},{13,1},{2,14},{6,10},... | collective-permute-start | bytes 6152 | tf_op jit(solution)/shard_map/ppermute | solution.py:28
  104.2 0.0 collective-permute-done.4.refs_1_
  104.2 10.9 %shard_map.39 = f32[2,256]{1,0:T(2,128)S(1)} custom-call(s32[3]{0:T(128)S(1)} %add_add_fusion.3.where, bf16[128,1792]{1,0:T(8,128)(2,1)S(1)} %collective-permute-done.3.refs_0_, bf16[128,1792]{1,0:T(8,128)(2,1)S(1)} %collective-permute-done.4.refs_1_, bf16[1024,2048]{1,0:T(8,128)(2,1)} %all-gather.2.cloned.1.call-done.refs_2_, bf16[2,1,1792,2048]{3,2,1,0:T(8,128)(2,1)} %refs_3_.5), custom_call_target="tpu_custom_call" | custom-call | flops 3758096384 | bytes 16646144 | tf_op jit(solution)/shard_map/pallas_call | solution.py:75
  115.1 0.1 collective-permute-start.5
  115.2 10.9 %shard_map.40 = f32[2,256]{1,0:T(2,128)S(1)} custom-call(s32[3]{0:T(128)S(1)} %add_add_fusion.4.where, bf16[128,1792]{1,0:T(8,128)(2,1)S(1)} %collective-permute-done.9.refs_0_, bf16[128,1792]{1,0:T(8,128)(2,1)S(1)} %collective-permute-done.10.refs_1_, bf16[1024,2048]{1,0:T(8,128)(2,1)} %all-gather.2.cloned.1.call-done.refs_2_, ...), custom_call_target="tpu_custom_call" | custom-call | flops 3758096384 | bytes 16646144 | tf_op jit(solution)/shard_map/pallas_call | solution.py:75
  126.1 0.5 collective-permute-start.14
  126.6 2.4 %collective-permute-start.13 = (f32[2,256]{1,0:T(2,128)S(1)}, f32[2,256]{1,0:T(2,128)S(1)}, u32[]{:S(2)}, u32[]{:S(2)}) collective-permute-start(f32[2,256]{1,0:T(2,128)S(1)} %shard_map.40), channel_id=1, source_target_pairs={{0,6},{1,7},{2,4},{3,5},{4,2},{5,3},{6,0},{7,1},{8,14},{9,15},{10,... | collective-permute-start | bytes 6152 | tf_op jit(solution)/shard_map/ppermute | solution.py:28
  129.0 1.4 collective-permute-start.12
  130.4 0.3 collective-permute-start.11
  130.7 0.9 collective-permute-start.8
  131.7 0.9 collective-permute-start.7
  132.6 0.0 collective-permute-start.6
  132.6 1.4 collective-permute-done.11
  134.0 1.2 collective-permute-done.7
  135.3 0.6 add_add_fusion
  (16 shorter events, 0.0 us)
Async XLA Ops:
  6.5 28.1 %copy-start = (bf16[256,2048]{1,0:T(8,128)(2,1)S(1)}, bf16[256,2048]{1,0:T(8,128)(2,1)}, u32[]{:S(2)}) copy-start(bf16[256,2048]{1,0:T(8,128)(2,1)} %refs_1_.1) | copy-start | bytes 3145732
  6.5 84.2 %all-gather.2.cloned.1.call-start = ((), (), s32[]{:S(2)}) async-start(), calls=%async_computation | async-start | bytes 4718592 | tf_op jit(solution)/shard_map/all_gather | solution.py:98
  10.7 22.6 %collective-permute-start = (bf16[128,1792]{1,0:T(8,128)(2,1)S(1)}, bf16[128,1792]{1,0:T(8,128)(2,1)S(1)}, u32[]{:S(2)}, u32[]{:S(2)}) collective-permute-start(bf16[128,1792]{1,0:T(8,128)(2,1)S(1)} %get-tuple-element.5), channel_id=1, source_target_pairs={{0,12},{4,8},{8,4},{12,0},{1,13},{5,9},{9,5},{13,1},{2,14},{6,10},... | collective-permute-start | bytes 1376264 | tf_op jit(solution)/shard_map/ppermute | solution.py:28
  15.8 74.4 %collective-permute-start.9 = (bf16[128,1792]{1,0:T(8,128)(2,1)S(1)}, bf16[128,1792]{1,0:T(8,128)(2,1)S(1)}, u32[]{:S(2)}, u32[]{:S(2)}) collective-permute-start(bf16[128,1792]{1,0:T(8,128)(2,1)S(1)} %get-tuple-element.6), channel_id=1, source_target_pairs={{0,4},{4,0},{8,12},{12,8},{1,5},{5,1},{9,13},{13,9},{2,6},{6,2},{1... | collective-permute-start | bytes 1376264 | tf_op jit(solution)/shard_map/ppermute | solution.py:28
  15.8 72.9 %collective-permute-start.3 = (bf16[128,1792]{1,0:T(8,128)(2,1)}, bf16[128,1792]{1,0:T(8,128)(2,1)S(1)}, u32[]{:S(2)}, u32[]{:S(2)}) collective-permute-start(bf16[128,1792]{1,0:T(8,128)(2,1)} %get-tuple-element.7), channel_id=1, source_target_pairs={{0,8},{4,12},{8,0},{12,4},{1,9},{5,13},{9,1},{13,5},{2,10},{6,14},... | collective-permute-start | bytes 1376264 | tf_op jit(solution)/shard_map/ppermute | solution.py:28
  33.4 57.4 %collective-permute-start.1 = (bf16[128,1792]{1,0:T(8,128)(2,1)S(1)}, bf16[128,1792]{1,0:T(8,128)(2,1)S(1)}, u32[]{:S(2)}, u32[]{:S(2)}) collective-permute-start(bf16[128,1792]{1,0:T(8,128)(2,1)S(1)} %collective-permute-done.refs_0_), channel_id=1, source_target_pairs={{0,2},{2,0},{1,3},{3,1},{4,6},{6,4},{5,7},{7,5},{8,10},{10,8},{9,1... | collective-permute-start | bytes 1376264 | tf_op jit(solution)/shard_map/ppermute | solution.py:28
  88.7 15.6 %collective-permute-start.4 = (bf16[128,1792]{1,0:T(8,128)(2,1)S(1)}, bf16[128,1792]{1,0:T(8,128)(2,1)S(1)}, u32[]{:S(2)}, u32[]{:S(2)}) collective-permute-start(bf16[128,1792]{1,0:T(8,128)(2,1)S(1)} %collective-permute-done.3.refs_0_), channel_id=1, source_target_pairs={{0,2},{2,0},{1,3},{3,1},{4,6},{6,4},{5,7},{7,5},{8,10},{10,8},{9,1... | collective-permute-start | bytes 1376264 | tf_op jit(solution)/shard_map/ppermute | solution.py:28
  90.2 25.0 %collective-permute-start.10 = (bf16[128,1792]{1,0:T(8,128)(2,1)S(1)}, bf16[128,1792]{1,0:T(8,128)(2,1)S(1)}, u32[]{:S(2)}, u32[]{:S(2)}) collective-permute-start(bf16[128,1792]{1,0:T(8,128)(2,1)S(1)} %collective-permute-done.9.refs_0_), channel_id=1, source_target_pairs={{0,2},{2,0},{1,3},{3,1},{4,6},{6,4},{5,7},{7,5},{8,10},{10,8},{9,1... | collective-permute-start | bytes 1376264 | tf_op jit(solution)/shard_map/ppermute | solution.py:28
  101.7 28.7 %collective-permute-start.2 = (f32[2,256]{1,0:T(2,128)S(1)}, f32[2,256]{1,0:T(2,128)S(1)}, u32[]{:S(2)}, u32[]{:S(2)}) collective-permute-start(f32[2,256]{1,0:T(2,128)S(1)} %shard_map.38), channel_id=1, source_target_pairs={{0,12},{4,8},{8,4},{12,0},{1,13},{5,9},{9,5},{13,1},{2,14},{6,10},... | collective-permute-start | bytes 6152 | tf_op jit(solution)/shard_map/ppermute | solution.py:28
  115.1 15.6 %collective-permute-start.5 = (f32[2,256]{1,0:T(2,128)S(1)}, f32[2,256]{1,0:T(2,128)S(1)}, u32[]{:S(2)}, u32[]{:S(2)}) collective-permute-start(f32[2,256]{1,0:T(2,128)S(1)} %shard_map.39), channel_id=1, source_target_pairs={{0,8},{4,12},{8,0},{12,4},{1,9},{5,13},{9,1},{13,5},{2,10},{6,14},... | collective-permute-start | bytes 6152 | tf_op jit(solution)/shard_map/ppermute | solution.py:28
  126.1 5.6 %collective-permute-start.14 = (f32[2,256]{1,0:T(2,128)S(1)}, f32[2,256]{1,0:T(2,128)S(1)}, u32[]{:S(2)}, u32[]{:S(2)}) collective-permute-start(f32[2,256]{1,0:T(2,128)S(1)} %shard_map.40), channel_id=1, source_target_pairs={{0,7},{1,6},{2,5},{3,4},{4,3},{5,2},{6,1},{7,0},{8,15},{9,14},{10,... | collective-permute-start | bytes 6152 | tf_op jit(solution)/shard_map/ppermute | solution.py:28
  126.6 6.0 %collective-permute-start.13 = (f32[2,256]{1,0:T(2,128)S(1)}, f32[2,256]{1,0:T(2,128)S(1)}, u32[]{:S(2)}, u32[]{:S(2)}) collective-permute-start(f32[2,256]{1,0:T(2,128)S(1)} %shard_map.40), channel_id=1, source_target_pairs={{0,6},{1,7},{2,4},{3,5},{4,2},{5,3},{6,0},{7,1},{8,14},{9,15},{10,... | collective-permute-start | bytes 6152 | tf_op jit(solution)/shard_map/ppermute | solution.py:28
  129.0 3.6 %collective-permute-start.12 = (f32[2,256]{1,0:T(2,128)S(1)}, f32[2,256]{1,0:T(2,128)S(1)}, u32[]{:S(2)}, u32[]{:S(2)}) collective-permute-start(f32[2,256]{1,0:T(2,128)S(1)} %shard_map.40), channel_id=1, source_target_pairs={{0,5},{1,4},{2,7},{3,6},{4,1},{5,0},{6,3},{7,2},{8,13},{9,12},{10,... | collective-permute-start | bytes 6152 | tf_op jit(solution)/shard_map/ppermute | solution.py:28
  130.4 3.6 %collective-permute-start.11 = (f32[2,256]{1,0:T(2,128)S(1)}, f32[2,256]{1,0:T(2,128)S(1)}, u32[]{:S(2)}, u32[]{:S(2)}) collective-permute-start(f32[2,256]{1,0:T(2,128)S(1)} %shard_map.40), channel_id=1, source_target_pairs={{0,4},{1,5},{2,6},{3,7},{4,0},{5,1},{6,2},{7,3},{8,12},{9,13},{10,... | collective-permute-start | bytes 6152 | tf_op jit(solution)/shard_map/ppermute | solution.py:28
  130.7 3.3 %collective-permute-start.8 = (f32[2,256]{1,0:T(2,128)S(1)}, f32[2,256]{1,0:T(2,128)S(1)}, u32[]{:S(2)}, u32[]{:S(2)}) collective-permute-start(f32[2,256]{1,0:T(2,128)S(1)} %add_add_fusion.1), channel_id=1, source_target_pairs={{0,3},{1,2},{2,1},{3,0},{4,7},{5,6},{6,5},{7,4},{8,11},{9,10},{10,... | collective-permute-start | bytes 6152 | tf_op jit(solution)/shard_map/ppermute | solution.py:28
  131.7 3.6 %collective-permute-start.7 = (f32[2,256]{1,0:T(2,128)S(1)}, f32[2,256]{1,0:T(2,128)S(1)}, u32[]{:S(2)}, u32[]{:S(2)}) collective-permute-start(f32[2,256]{1,0:T(2,128)S(1)} %add_add_fusion.1), channel_id=1, source_target_pairs={{0,2},{1,3},{2,0},{3,1},{4,6},{5,7},{6,4},{7,5},{8,10},{9,11},{10,... | collective-permute-start | bytes 6152 | tf_op jit(solution)/shard_map/ppermute | solution.py:28
  132.6 2.7 %collective-permute-start.6 = (f32[2,256]{1,0:T(2,128)S(1)}, f32[2,256]{1,0:T(2,128)S(1)}, u32[]{:S(2)}, u32[]{:S(2)}) collective-permute-start(f32[2,256]{1,0:T(2,128)S(1)} %add_add_fusion.1), channel_id=1, source_target_pairs={{0,1},{1,0},{2,3},{3,2},{4,5},{5,4},{6,7},{7,6},{8,9},{9,8},{10,11... | collective-permute-start | bytes 6152 | tf_op jit(solution)/shard_map/ppermute | solution.py:28
Sparse Core Ops, SparseCore 0:
  9.0 79.3 all-gather.1

commit v3 on v1

v3 whole, which is shorter than its diff:
```python
import functools
import math

import jax
import jax.numpy as jnp
from jax import lax
from jax.experimental import pallas as pl
from jax.experimental.pallas import tpu as pltpu
from jax.sharding import PartitionSpec as P


def trade(block, steps):
    axes = tuple(steps)
    sizes = [lax.axis_size(axis) for axis in axes]
    mask = 0
    for axis, size in zip(axes, sizes):
        mask = mask * size + steps[axis]
    return lax.ppermute(block, axes, [(i, i ^ mask) for i in range(math.prod(sizes))])


def after(value, *others):
    return lax.optimization_barrier((value, *others))[0]


def pass_on(block, step, count):
    up = lax.ppermute(block[0], "dp", [(i, i + 1) for i in range(step - 1, count - 1)])
    down = lax.ppermute(block[1], "dp", [(i, i - 1) for i in range(1, count - step + 1)])
    return up, down


def from_partner(hops, me, d, count):
    groups = {}
    for z in range(count):
        away = z - (z ^ d)
        groups.setdefault((abs(away), away < 0), []).append(z)
    chosen = None
    for (step, down), members in groups.items():
        block = hops[step][int(down)]
        if chosen is None:
            chosen = block
        else:
            chosen = jnp.where(functools.reduce(jnp.logical_or, [me == z for z in members]), block, chosen)
    return chosen


def mix_kernel(where, mine_ref, other_ref, query_ref, out_ref, acts):
    half = mine_ref.shape[0]

    @pl.when((pl.program_id(0) == 0) & (pl.program_id(1) == 0))
    def _():
        acts[pl.ds(pl.multiple_of(where[0] * half, half), half), :] = mine_ref[...]
        acts[pl.ds(pl.multiple_of(where[1] * half, half), half), :] = other_ref[...]

    out_ref[0] = lax.dot_general(
        query_ref[0, 0], acts[...], (((1,), (1,)), ((), ())), preferred_element_type=jnp.float32
    )


def mixed(mine, other, core, queries):
    nq, _, depth, width = queries.shape
    half = mine.shape[0]
    tokens = 2 * half
    tile = depth // 2
    spec = pltpu.PrefetchScalarGridSpec(
        num_scalar_prefetch=1,
        grid=(nq, depth // tile),
        in_specs=[
            pl.BlockSpec((half, width), lambda q, o, where: (0, 0)),
            pl.BlockSpec((half, width), lambda q, o, where: (0, 0)),
            pl.BlockSpec((1, 1, tile, width), lambda q, o, where: (q, 0, o, 0)),
        ],
        out_specs=pl.BlockSpec((1, tile, tokens), lambda q, o, where: (q, o, 0)),
        scratch_shapes=[pltpu.VMEM((tokens, width), mine.dtype)],
    )
    return pl.pallas_call(
        mix_kernel,
        grid_spec=spec,
        out_shape=jax.ShapeDtypeStruct((nq, depth, tokens), jnp.float32),
        compiler_params=pltpu.CompilerParams(vmem_limit_bytes=36 * 1024 * 1024),
        cost_estimate=pl.CostEstimate(
            flops=2 * nq * tokens * depth * width,
            bytes_accessed=2 * (nq * depth * width + tokens * width) + 4 * nq * depth * tokens,
            transcendentals=0,
        ),
    )(jnp.stack([core, 1 - core]).astype(jnp.int32), mine, other, queries)


def score_kernel(where, *refs):
    parts, (mix_ref, out_ref) = refs[:-2], refs[-2:]
    found = []
    for p in range(len(parts)):
        chosen = parts[0][...]
        for r in range(1, len(parts)):
            chosen = jnp.where(where[0] == p ^ r, parts[r][...], chosen)
        found.append(chosen.astype(jnp.float32))
    grads = found[0] if len(found) == 1 else jnp.concatenate(found, axis=1)
    for q in range(mix_ref.shape[0]):
        out_ref[q : q + 1, :] = jnp.sum(grads * mix_ref[q], axis=0, keepdims=True)


def piece_scores(parts, column, mix, piece, pieces):
    nq, depth, tokens = mix.shape
    rows = depth // pieces
    spec = pltpu.PrefetchScalarGridSpec(
        num_scalar_prefetch=1,
        grid=(1,),
        in_specs=[pl.BlockSpec(part.shape, lambda i, where: (0, 0)) for part in parts]
        + [pl.BlockSpec((nq, rows, tokens), lambda i, where: (0, piece, 0))],
        out_specs=pl.BlockSpec((nq, tokens), lambda i, where: (0, 0)),
    )
    return pl.pallas_call(
        score_kernel,
        grid_spec=spec,
        out_shape=jax.ShapeDtypeStruct((nq, tokens), jnp.float32),
        compiler_params=pltpu.CompilerParams(vmem_limit_bytes=36 * 1024 * 1024),
        cost_estimate=pl.CostEstimate(
            flops=2 * nq * rows * tokens,
            bytes_accessed=4 * nq * rows * tokens + 2 * rows * tokens,
            transcendentals=0,
        ),
    )(jnp.reshape(column, (1,)).astype(jnp.int32), *parts, mix)


def on_device(activations, out_grads, queries):
    count, spread = lax.axis_size("dp"), lax.axis_size("din")
    me, column, core = lax.axis_index("dp"), lax.axis_index("din"), lax.axis_index("dout")
    tokens, rows = activations.shape[0], queries.shape[2]
    part, half = tokens // spread, tokens // 2

    mine = lax.dynamic_slice_in_dim(activations, core * half, half, 0)
    hops = [(mine, mine)]
    hops.append(pass_on(hops[0], 1, count))

    turned = lax.dynamic_slice_in_dim(out_grads, column * part, part, 0).T

    def grads_for(d, piece=0, pieces=1):
        size = rows // pieces
        return lax.dynamic_slice_in_dim(turned, (me ^ d) * rows + piece * size, size, 0)

    def to_column(arrived):
        return [arrived] + [trade(arrived, {"din": r}) for r in range(1, spread)]

    def mixed_for(d):
        block = from_partner(hops, me, d, count)
        return mixed(block, trade(block, {"dout": 1}), core, queries)

    steps = list(range(count - 1, 0, -1))
    last = 2 if count > 2 else 1
    steps.remove(last)
    arrived = {steps[0]: trade(grads_for(steps[0]), {"dp": steps[0]})}

    own_mix = mixed(activations[:half], activations[half:], jnp.zeros_like(core), queries)
    own = lax.dynamic_slice_in_dim(out_grads, me * rows, rows, 1).T
    home = piece_scores([own], jnp.zeros_like(column), own_mix, 0, 1)

    pieces = 2
    tail = []
    for step in range(2, count):
        hops.append(pass_on(hops[-1], step, count))
        if step == 2:
            for piece in range(pieces):
                ready = after(grads_for(last, piece, pieces), *hops[1])
                tail.append(trade(ready, {"dp": last}))
        if step < count:
            for d in steps[step - 1 : step]:
                arrived[d] = trade(after(grads_for(d), *hops[step]), {"dp": d})
    if not tail:
        tail = [trade(grads_for(last, piece, pieces), {"dp": last}) for piece in range(pieces)]

    mixes = {d: mixed_for(d) for d in sorted(steps + [last])}
    for d in steps:
        home = home + trade(piece_scores(to_column(arrived[d]), column, mixes[d], 0, 1), {"dp": d})
    pairs = [(r, c) for r in range(spread) for c in range(2)]
    total = home
    for r, c in pairs[1:]:
        total = total + trade(home, {"din": r, "dout": c})
    final = None
    for piece, block in enumerate(tail):
        scores = piece_scores(to_column(block), column, mixes[last], piece, pieces)
        final = scores if final is None else final + scores
    for r, c in pairs:
        total = total + trade(final, {"dp": last, "din": r, "dout": c})
    return total


def solution(mesh):
    placed = (P(("groups", "dp"), "din"), P(("groups", "dp"), "dout"), P(None, "dout", "dp", "din"))
    return jax.shard_map(
        on_device, mesh=mesh, in_specs=placed, out_specs=P(None, ("groups", "dp")), check_vma=False
    )
```

time: 222 us -> 136 us (0.61)
  blocking collectives: 80.7 us -> 0 us
  waiting for transfers between devices: 92 us -> 48.8 us
  Pallas kernels: 0 us -> 36.7 us
  starting transfers between devices: 0.04 us -> 31.7 us
  matrix products: 18.4 us -> 0 us
  between operations: 13.5 us -> 0.28 us
    all_gather x2 -> x0, waiting for transfers between devices: 92 us -> none  [the longest x1 49.2 us: on_device(): grads = lax.all_gather(blocks, 'din', axis=1).reshape(count * tokens, rows)]
    all_to_all x1 -> x0, blocking collectives: 48.8 us -> none  [on_device(): blocks = lax.all_to_all(blocks, 'dp', 0, 0)]
    ppermute x0 -> x26, waiting for transfers between devices: none -> 48.8 us  [the longest x3 22.9 us: pass_on(): lax.ppermute(block[1], 'dp', [(i, i - 1) for i in range(1, count - step +...]
    pallas_call x0 -> x9, Pallas kernels: none -> 36.7 us  [the longest x4 33.7 us: mixed(): pl.pallas_call(mix_kernel, grid_spec=spec, out_shape=jax.ShapeDtypeStruct...]
    psum x1 -> x0, blocking collectives: 31.9 us -> none  [on_device(): total = lax.psum(total, ('dp', 'din', 'dout'))]
    ppermute x0 -> x26, starting transfers between devices: none -> 31.7 us  [the longest x20 19.9 us: trade(): lax.ppermute(block, axes, [(i, i ^ mask) for i in range(math.prod(sizes))])]
    dot_general x1 -> x0, matrix products: 18.4 us -> none  [on_device(): jnp.einsum('tc,qci->qti', grads, queries[:, 0], preferred_element_type=jn...]
    all_gather x1 -> x0, local copies, waits for them, and re-layouts: 6.03 us -> none  [on_device(): grads = lax.all_gather(blocks, 'din', axis=1).reshape(count * tokens, rows)]
  transfers between devices with their start and end apart: 2 -> 26, of which waited for: 2 -> 8; matrix products, arithmetic and copies ran while one was open for 3% -> 9% of each run, Pallas kernels for 0% -> 27%
where the time goes in v3:
time: 136 us; the launch traced here: 135 us
  waiting for transfers between devices  48.8 us (36%)
  Pallas kernels  36.7 us (27%)
  starting transfers between devices  31.7 us (23%)
  local copies, waits for them, and re-layouts  15.7 us (12%)
  other arithmetic  2.2 us (2%)
    pallas_call x4, Pallas kernels, mixed(): pl.pallas_call(mix_kernel, grid_spec=spec, out_shape=jax.ShapeDtypeStruct...  33.7 us
    ppermute x3, waiting for transfers between devices, pass_on(): lax.ppermute(block[1], 'dp', [(i, i - 1) for i in range(1, count - step +...  22.9 us
    ppermute x20, starting transfers between devices, trade(): lax.ppermute(block, axes, [(i, i ^ mask) for i in range(math.prod(sizes))])  19.9 us
    ppermute x20, waiting for transfers between devices, trade(): lax.ppermute(block, axes, [(i, i ^ mask) for i in range(math.prod(sizes))])  16.9 us
    ppermute x3, waiting for transfers between devices, pass_on(): lax.ppermute(block[0], 'dp', [(i, i + 1) for i in range(step - 1, count -...  9.04 us
    unnamed x21, local copies, waits for them, and re-layouts  8.99 us
    ppermute x3, starting transfers between devices, pass_on(): lax.ppermute(block[0], 'dp', [(i, i + 1) for i in range(step - 1, count -...  7.88 us
    ppermute x3, starting transfers between devices, pass_on(): lax.ppermute(block[1], 'dp', [(i, i - 1) for i in range(1, count - step +...  3.84 us
  transfers between devices with their start and end apart: 26, of which 8 were waited for; matrix products, arithmetic and copies ran while one was open for 9% of the time, Pallas kernels for 27%

profile of v3, /device:TPU:0, one launch (start us, length us, event | category | flops | bytes accessed | tf_op | source)
XLA Modules:
  0.0 135.3 jit_solution(8437303281330620369)
XLA Ops:
  0.0 1.5 %fusion.2 = (bf16[128,2048]{1,0:T(8,128)(2,1)S(1)}, bf16[128,2048]{1,0:T(8,128)(2,1)S(1)}, bf16[128,2048]{1,0:T(8,128)(2,1)S(1)}) fusion(bf16[256,2048]{1,0:T(8,128)(2,1)} %param.3, s32[]{:T(128)S(6)} %select_n.69), kind=kLoop, calls=%fused_computation.10 | loop fusion | bytes 3145732 | tf_op jit(solution)/shard_map/slice | solution.py:152
  1.5 5.7 %collective-permute-start.2 = (bf16[128,2048]{1,0:T(8,128)(2,1)S(1)}, bf16[128,2048]{1,0:T(8,128)(2,1)}, u32[]{:S(2)}, u32[]{:S(2)}) collective-permute-start(bf16[128,2048]{1,0:T(8,128)(2,1)S(1)} %get-tuple-element.19), channel_id=1, source_target_pairs={{0,4},{4,8},{8,12},{1,5},{5,9},{9,13},{2,6},{6,10},{10,14},{3,7},{... | collective-permute-start | bytes 1572872 | tf_op jit(solution)/shard_map/ppermute | solution.py:26
  7.3 1.3 collective-permute-start.5
  8.6 9.0 %collective-permute-done.2 = bf16[128,2048]{1,0:T(8,128)(2,1)} collective-permute-done((bf16[128,2048]{1,0:T(8,128)(2,1)S(1)}, bf16[128,2048]{1,0:T(8,128)(2,1)}, u32[]{:S(2)}, u32[]{:S(2)}) %collective-permute-start.2) | collective-permute-done | bytes 524320 | tf_op jit(solution)/shard_map/ppermute | solution.py:26
  18.3 4.3 %collective-permute-done.5 = bf16[128,2048]{1,0:T(8,128)(2,1)} collective-permute-done((bf16[128,2048]{1,0:T(8,128)(2,1)S(1)}, bf16[128,2048]{1,0:T(8,128)(2,1)}, u32[]{:S(2)}, u32[]{:S(2)}) %collective-permute-start.5) | collective-permute-done | bytes 524320 | tf_op jit(solution)/shard_map/ppermute | solution.py:27
  22.6 1.3 collective-permute-start.6
  23.9 1.7 %fusion = (bf16[128,1792]{1,0:T(8,128)(2,1)S(1)}, bf16[128,1792]{1,0:T(8,128)(2,1)S(1)}) fusion(bf16[256,7168]{1,0:T(8,128)(2,1)} %param.4, s32[]{:T(128)S(6)} %select_n.65, s32[]{:T(128)S(6)} %select_n.67, s32[]{:T(128)S(6)} %select_n.76), kind=kLoop, calls=%fused_computation.8 | loop fusion | bytes 1835020 | tf_op jit(solution)/shard_map/dynamic-slice
  25.6 1.0 copy.10
  27.0 1.5 %collective-permute-start.4 = (bf16[128,2048]{1,0:T(8,128)(2,1)S(1)}, bf16[128,2048]{1,0:T(8,128)(2,1)}, u32[]{:S(2)}, u32[]{:S(2)}) collective-permute-start(bf16[128,2048]{1,0:T(8,128)(2,1)S(1)} %collective-permute-done.3), channel_id=1, source_target_pairs={{8,12},{9,13},{10,14},{11,15},{24,28},{25,29},{26,30},{27,31}} | collective-permute-start | bytes 1572872 | tf_op jit(solution)/shard_map/ppermute | solution.py:26
  28.4 18.6 %collective-permute-done.6 = bf16[128,2048]{1,0:T(8,128)(2,1)S(1)} collective-permute-done((bf16[128,2048]{1,0:T(8,128)(2,1)}, bf16[128,2048]{1,0:T(8,128)(2,1)S(1)}, u32[]{:S(2)}, u32[]{:S(2)}) %collective-permute-start.6) | collective-permute-done | bytes 524320 | tf_op jit(solution)/shard_map/ppermute | solution.py:27
  47.0 1.3 collective-permute-start.7
  48.3 2.2 %constant_dynamic-slice_fusion.1 = bf16[256,1792]{1,0:T(8,128)(2,1)} fusion(bf16[256,7168]{1,0:T(8,128)(2,1)} %param.4, s32[]{:T(128)S(6)} %select_n.63), kind=kLoop, calls=%fused_computation.7 | loop fusion | bytes 1835012 | tf_op jit(solution)/shard_map/dynamic_slice | solution.py:153
  50.4 1.0 copy.11
  51.5 1.3 fusion.1
  52.8 8.4 %shard_map.37.refs_1_ = f32[2,1792,256]{2,1,0:T(8,128)S(1)} custom-call(s32[2]{0:T(128)S(1)} %iota.3.where, bf16[128,2048]{1,0:T(8,128)(2,1)S(1)} %get-tuple-element.18.mine_ref, bf16[128,2048]{1,0:T(8,128)(2,1)S(1)} %get-tuple-element.17.other_ref, bf16[2,1,1792,2048]{3,2,1,0:T(8,128)(2,1)} %query_ref.7), custom_call_target="tpu_custom_call" | custom-call | flops 3758096384 | bytes 19398656 | tf_op jit(solution)/shard_map/pallas_call | solution.py:75
  61.2 1.8 %copy-done = f32[2,1792,256]{2,1,0:T(8,128)} copy-done((f32[2,1792,256]{2,1,0:T(8,128)}, f32[2,1792,256]{2,1,0:T(8,128)S(1)}, u32[]{:S(2)}) %copy-start) | copy-done | bytes 3670040
  63.0 4.4 %collective-permute-start.10 = (bf16[1792,128]{1,0:T(8,128)(2,1)}, bf16[1792,128]{1,0:T(8,128)(2,1)S(1)}, u32[]{:S(2)}, u32[]{:S(2)}) collective-permute-start(bf16[1792,128]{1,0:T(8,128)(2,1)} %bitcast.5), channel_id=1, source_target_pairs={{0,4},{4,0},{8,12},{12,8},{1,5},{5,1},{9,13},{13,9},{2,6},{6,2},{1... | collective-permute-start | bytes 1376264 | tf_op jit(solution)/shard_map/ppermute | solution.py:18
  67.4 1.5 %select_select_fusion = (bf16[128,2048]{1,0:T(8,128)(2,1)S(1)}, bf16[128,2048]{1,0:T(8,128)(2,1)S(1)}) fusion(bf16[128,2048]{1,0:T(8,128)(2,1)} %collective-permute-done.4, bf16[128,2048]{1,0:T(8,128)(2,1)} %collective-permute-done.2, bf16[128,2048]{1,0:T(8,128)(2,1)} %collective-permute-done.5, bf16[128,2048]{1,0:T(8,128)(2,1)} %collective-permute-done.7, ...), kind=kLoop, calls=%fused_computation | loop fusion | flops 1048576 | bytes 3145732 | tf_op jit(solution)/shard_map/jit(_where)/select_n | solution.py:42
  70.7 1.5 %copy.9 = bf16[256,1792]{0,1:T(8,128)(2,1)S(1)} copy(bf16[256,1792]{1,0:T(8,128)(2,1)} %constant_dynamic-slice_fusion.1) | data formatting | bytes 1835008
  72.1 2.0 %copy-done.1 = f32[2,1792,256]{2,1,0:T(8,128)S(1)} copy-done((f32[2,1792,256]{2,1,0:T(8,128)S(1)}, f32[2,1792,256]{2,1,0:T(8,128)}, u32[]{:S(2)}) %copy-start.1) | copy-done | bytes 3670040
  74.6 1.5 %collective-permute-start.1 = (bf16[1792,128]{1,0:T(8,128)(2,1)S(1)}, bf16[1792,128]{1,0:T(8,128)(2,1)S(1)}, u32[]{:S(2)}, u32[]{:S(2)}) collective-permute-start(bf16[1792,128]{1,0:T(8,128)(2,1)S(1)} %collective-permute-done.refs_0_), channel_id=1, source_target_pairs={{0,2},{2,0},{1,3},{3,1},{4,6},{6,4},{5,7},{7,5},{8,10},{10,8},{9,1... | collective-permute-start | bytes 1376264 | tf_op jit(solution)/shard_map/ppermute | solution.py:18
  76.9 12.1 %collective-permute-done.17.refs_0_ = bf16[896,128]{1,0:T(8,128)(2,1)S(1)} collective-permute-done((bf16[896,128]{1,0:T(8,128)(2,1)S(1)}, bf16[896,128]{1,0:T(8,128)(2,1)S(1)}, u32[]{:S(2)}, u32[]{:S(2)}) %collective-permute-start.17) | collective-permute-done | bytes 229408 | tf_op jit(solution)/shard_map/ppermute | solution.py:18
  89.1 8.4 %shard_map.41.refs_2_ = f32[2,1792,256]{2,1,0:T(8,128)S(1)} custom-call(s32[2]{0:T(128)S(1)} %pad_add_fusion.where, bf16[128,2048]{1,0:T(8,128)(2,1)S(1)} %get-tuple-element.16.mine_ref, bf16[128,2048]{1,0:T(8,128)(2,1)S(1)} %collective-permute-done.12.other_ref, bf16[2,1,1792,2048]{3,2,1,0:T(8,128)(2,1)} %query_ref.7), custom_call_target="tpu_custom_call" | custom-call | flops 3758096384 | bytes 19398656 | tf_op jit(solution)/shard_map/pallas_call | solution.py:75
  97.6 2.9 %collective-permute-done.20.refs_0_ = bf16[896,128]{1,0:T(8,128)(2,1)S(1)} collective-permute-done((bf16[896,128]{1,0:T(8,128)(2,1)S(1)}, bf16[896,128]{1,0:T(8,128)(2,1)S(1)}, u32[]{:S(2)}, u32[]{:S(2)}) %collective-permute-start.20) | collective-permute-done | bytes 229408 | tf_op jit(solution)/shard_map/ppermute | solution.py:18
  101.3 1.3 collective-permute-start.21
  103.5 8.4 %shard_map.39.refs_2_ = f32[2,1792,256]{2,1,0:T(8,128)S(1)} custom-call(s32[2]{0:T(128)S(1)} %pad_add_fusion.where, bf16[128,2048]{1,0:T(8,128)(2,1)S(1)} %get-tuple-element.15.mine_ref, bf16[128,2048]{1,0:T(8,128)(2,1)S(1)} %collective-permute-done.8.other_ref, bf16[2,1,1792,2048]{3,2,1,0:T(8,128)(2,1)} %query_ref.7), custom_call_target="tpu_custom_call" | custom-call | flops 3758096384 | bytes 19398656 | tf_op jit(solution)/shard_map/pallas_call | solution.py:75
  112.8 2.7 %collective-permute-start.9 = (f32[2,256]{1,0:T(2,128)S(1)}, f32[2,256]{1,0:T(2,128)S(1)}, u32[]{:S(2)}, u32[]{:S(2)}) collective-permute-start(f32[2,256]{1,0:T(2,128)S(1)} %shard_map.40), channel_id=1, source_target_pairs={{0,12},{4,8},{8,4},{12,0},{1,13},{5,9},{9,5},{13,1},{2,14},{6,10},... | collective-permute-start | bytes 6152 | tf_op jit(solution)/shard_map/ppermute | solution.py:18
  115.5 8.4 %shard_map.43.refs_2_ = f32[2,1792,256]{2,1,0:T(8,128)S(1)} custom-call(s32[2]{0:T(128)S(1)} %pad_add_fusion.where, bf16[128,2048]{1,0:T(8,128)(2,1)S(1)} %broadcast_select_fusion.mine_ref, bf16[128,2048]{1,0:T(8,128)(2,1)S(1)} %collective-permute-done.19.other_ref, bf16[2,1,1792,2048]{3,2,1,0:T(8,128)(2,1)} %query_ref.7), custom_call_target="tpu_custom_call" | custom-call | flops 3758096384 | bytes 19398656 | tf_op jit(solution)/shard_map/pallas_call | solution.py:75
  124.8 2.1 %collective-permute-start.24 = (f32[2,256]{1,0:T(2,128)S(1)}, f32[2,256]{1,0:T(2,128)S(1)}, u32[]{:S(2)}, u32[]{:S(2)}) collective-permute-start(f32[2,256]{1,0:T(2,128)S(1)} %add.77), channel_id=1, source_target_pairs={{0,10},{1,11},{2,8},{3,9},{4,14},{5,15},{6,12},{7,13},{8,2},{9,3},... | collective-permute-start | bytes 6152 | tf_op jit(solution)/shard_map/ppermute | solution.py:18
  126.9 2.0 %collective-permute-start.23 = (f32[2,256]{1,0:T(2,128)S(1)}, f32[2,256]{1,0:T(2,128)S(1)}, u32[]{:S(2)}, u32[]{:S(2)}) collective-permute-start(f32[2,256]{1,0:T(2,128)S(1)} %add.77), channel_id=1, source_target_pairs={{0,9},{1,8},{2,11},{3,10},{4,13},{5,12},{6,15},{7,14},{8,1},{9,0},... | collective-permute-start | bytes 6152 | tf_op jit(solution)/shard_map/ppermute | solution.py:18
  128.9 2.1 %collective-permute-start.22 = (f32[2,256]{1,0:T(2,128)S(1)}, f32[2,256]{1,0:T(2,128)S(1)}, u32[]{:S(2)}, u32[]{:S(2)}) collective-permute-start(f32[2,256]{1,0:T(2,128)S(1)} %add.77), channel_id=1, source_target_pairs={{0,8},{1,9},{2,10},{3,11},{4,12},{5,13},{6,14},{7,15},{8,0},{9,1},... | collective-permute-start | bytes 6152 | tf_op jit(solution)/shard_map/ppermute | solution.py:18
  131.9 1.0 collective-permute-start.14
  (61 shorter events, 10.8 us)
Async XLA Ops:
  1.5 16.1 %collective-permute-start.2 = (bf16[128,2048]{1,0:T(8,128)(2,1)S(1)}, bf16[128,2048]{1,0:T(8,128)(2,1)}, u32[]{:S(2)}, u32[]{:S(2)}) collective-permute-start(bf16[128,2048]{1,0:T(8,128)(2,1)S(1)} %get-tuple-element.19), channel_id=1, source_target_pairs={{0,4},{4,8},{8,12},{1,5},{5,9},{9,13},{2,6},{6,10},{10,14},{3,7},{... | collective-permute-start | bytes 1572872 | tf_op jit(solution)/shard_map/ppermute | solution.py:26
  7.3 15.3 %collective-permute-start.5 = (bf16[128,2048]{1,0:T(8,128)(2,1)S(1)}, bf16[128,2048]{1,0:T(8,128)(2,1)}, u32[]{:S(2)}, u32[]{:S(2)}) collective-permute-start(bf16[128,2048]{1,0:T(8,128)(2,1)S(1)} %get-tuple-element.19), channel_id=1, source_target_pairs={{4,0},{8,4},{12,8},{5,1},{9,5},{13,9},{6,2},{10,6},{14,10},{7,3},{... | collective-permute-start | bytes 1572872 | tf_op jit(solution)/shard_map/ppermute | solution.py:27
  17.6 9.4 %collective-permute-start.3 = (bf16[128,2048]{1,0:T(8,128)(2,1)}, bf16[128,2048]{1,0:T(8,128)(2,1)S(1)}, u32[]{:S(2)}, u32[]{:S(2)}) collective-permute-start(bf16[128,2048]{1,0:T(8,128)(2,1)} %collective-permute-done.2), channel_id=1, source_target_pairs={{4,8},{8,12},{5,9},{9,13},{6,10},{10,14},{7,11},{11,15},{20,24},{2... | collective-permute-start | bytes 1572872 | tf_op jit(solution)/shard_map/ppermute | solution.py:26
  22.6 24.4 %collective-permute-start.6 = (bf16[128,2048]{1,0:T(8,128)(2,1)}, bf16[128,2048]{1,0:T(8,128)(2,1)S(1)}, u32[]{:S(2)}, u32[]{:S(2)}) collective-permute-start(bf16[128,2048]{1,0:T(8,128)(2,1)} %collective-permute-done.5), channel_id=1, source_target_pairs={{4,0},{8,4},{5,1},{9,5},{6,2},{10,6},{7,3},{11,7},{20,16},{24,20},... | collective-permute-start | bytes 1572872 | tf_op jit(solution)/shard_map/ppermute | solution.py:27
  26.6 48.0 %collective-permute-start = (bf16[1792,128]{1,0:T(8,128)(2,1)}, bf16[1792,128]{1,0:T(8,128)(2,1)S(1)}, u32[]{:S(2)}, u32[]{:S(2)}) collective-permute-start(bf16[1792,128]{1,0:T(8,128)(2,1)} %bitcast.2), channel_id=1, source_target_pairs={{0,12},{4,8},{8,4},{12,0},{1,13},{5,9},{9,5},{13,1},{2,14},{6,10},... | collective-permute-start | bytes 1376264 | tf_op jit(solution)/shard_map/ppermute | solution.py:18
  27.0 34.2 %copy-start.2 = (bf16[128,2048]{1,0:T(8,128)(2,1)}, bf16[128,2048]{1,0:T(8,128)(2,1)S(1)}, u32[]{:S(2)}) copy-start(bf16[128,2048]{1,0:T(8,128)(2,1)S(1)} %collective-permute-done.3) | copy-start | bytes 1572868
  27.0 40.4 %collective-permute-start.4 = (bf16[128,2048]{1,0:T(8,128)(2,1)S(1)}, bf16[128,2048]{1,0:T(8,128)(2,1)}, u32[]{:S(2)}, u32[]{:S(2)}) collective-permute-start(bf16[128,2048]{1,0:T(8,128)(2,1)S(1)} %collective-permute-done.3), channel_id=1, source_target_pairs={{8,12},{9,13},{10,14},{11,15},{24,28},{25,29},{26,30},{27,31}} | collective-permute-start | bytes 1572872 | tf_op jit(solution)/shard_map/ppermute | solution.py:26
  47.0 14.2 %copy-start.4 = (bf16[128,2048]{1,0:T(8,128)(2,1)}, bf16[128,2048]{1,0:T(8,128)(2,1)S(1)}, u32[]{:S(2)}) copy-start(bf16[128,2048]{1,0:T(8,128)(2,1)S(1)} %collective-permute-done.6) | copy-start | bytes 1572868
  47.0 20.4 %collective-permute-start.7 = (bf16[128,2048]{1,0:T(8,128)(2,1)S(1)}, bf16[128,2048]{1,0:T(8,128)(2,1)}, u32[]{:S(2)}, u32[]{:S(2)}) collective-permute-start(bf16[128,2048]{1,0:T(8,128)(2,1)S(1)} %collective-permute-done.6), channel_id=1, source_target_pairs={{4,0},{5,1},{6,2},{7,3},{20,16},{21,17},{22,18},{23,19}} | collective-permute-start | bytes 1572872 | tf_op jit(solution)/shard_map/ppermute | solution.py:27
  63.0 13.2 %collective-permute-start.10 = (bf16[1792,128]{1,0:T(8,128)(2,1)}, bf16[1792,128]{1,0:T(8,128)(2,1)S(1)}, u32[]{:S(2)}, u32[]{:S(2)}) collective-permute-start(bf16[1792,128]{1,0:T(8,128)(2,1)} %bitcast.5), channel_id=1, source_target_pairs={{0,4},{4,0},{8,12},{12,8},{1,5},{5,1},{9,13},{13,9},{2,6},{6,2},{1... | collective-permute-start | bytes 1376264 | tf_op jit(solution)/shard_map/ppermute | solution.py:18
  68.8 20.2 %collective-permute-start.12 = (bf16[128,2048]{1,0:T(8,128)(2,1)S(1)}, bf16[128,2048]{1,0:T(8,128)(2,1)S(1)}, u32[]{:S(2)}, u32[]{:S(2)}) collective-permute-start(bf16[128,2048]{1,0:T(8,128)(2,1)S(1)} %get-tuple-element.16.mine_ref), channel_id=1, source_target_pairs={{0,1},{1,0},{2,3},{3,2},{4,5},{5,4},{6,7},{7,6},{8,9},{9,8},{10,11... | collective-permute-start | bytes 1572872 | tf_op jit(solution)/shard_map/ppermute | solution.py:18
  72.1 2.0 %copy-start.1 = (f32[2,1792,256]{2,1,0:T(8,128)S(1)}, f32[2,1792,256]{2,1,0:T(8,128)}, u32[]{:S(2)}) copy-start(f32[2,1792,256]{2,1,0:T(8,128)} %copy-done) | copy-start | bytes 11010052
  74.2 2.6 %copy-start.3 = (bf16[128,2048]{1,0:T(8,128)(2,1)S(1)}, bf16[128,2048]{1,0:T(8,128)(2,1)}, u32[]{:S(2)}) copy-start(bf16[128,2048]{1,0:T(8,128)(2,1)} %copy-done.2) | copy-start | bytes 1572868
  74.2 2.6 %copy-start.5 = (bf16[128,2048]{1,0:T(8,128)(2,1)S(1)}, bf16[128,2048]{1,0:T(8,128)(2,1)}, u32[]{:S(2)}) copy-start(bf16[128,2048]{1,0:T(8,128)(2,1)} %copy-done.4) | copy-start | bytes 1572868
  74.2 14.8 %copy-start.6 = (bf16[128,896]{0,1:T(8,128)(2,1)S(1)}, bf16[128,896]{0,1:T(8,128)(2,1)}, u32[]{:S(2)}) copy-start(bf16[128,896]{0,1:T(8,128)(2,1)} %copy.13) | copy-start | bytes 688132
  74.6 37.3 %collective-permute-start.1 = (bf16[1792,128]{1,0:T(8,128)(2,1)S(1)}, bf16[1792,128]{1,0:T(8,128)(2,1)S(1)}, u32[]{:S(2)}, u32[]{:S(2)}) collective-permute-start(bf16[1792,128]{1,0:T(8,128)(2,1)S(1)} %collective-permute-done.refs_0_), channel_id=1, source_target_pairs={{0,2},{2,0},{1,3},{3,1},{4,6},{6,4},{5,7},{7,5},{8,10},{10,8},{9,1... | collective-permute-start | bytes 1376264 | tf_op jit(solution)/shard_map/ppermute | solution.py:18
  76.2 12.8 %collective-permute-start.17 = (bf16[896,128]{1,0:T(8,128)(2,1)S(1)}, bf16[896,128]{1,0:T(8,128)(2,1)S(1)}, u32[]{:S(2)}, u32[]{:S(2)}) collective-permute-start(bf16[896,128]{1,0:T(8,128)(2,1)S(1)} %bitcast.10), channel_id=1, source_target_pairs={{0,8},{4,12},{8,0},{12,4},{1,9},{5,13},{9,1},{13,5},{2,10},{6,14},... | collective-permute-start | bytes 688136 | tf_op jit(solution)/shard_map/ppermute | solution.py:18
  76.2 25.1 %collective-permute-start.11 = (bf16[1792,128]{1,0:T(8,128)(2,1)S(1)}, bf16[1792,128]{1,0:T(8,128)(2,1)S(1)}, u32[]{:S(2)}, u32[]{:S(2)}) collective-permute-start(bf16[1792,128]{1,0:T(8,128)(2,1)S(1)} %collective-permute-done.10.refs_0_), channel_id=1, source_target_pairs={{0,2},{2,0},{1,3},{3,1},{4,6},{6,4},{5,7},{7,5},{8,10},{10,8},{9,1... | collective-permute-start | bytes 1376264 | tf_op jit(solution)/shard_map/ppermute | solution.py:18
  76.8 26.6 %collective-permute-start.8 = (bf16[128,2048]{1,0:T(8,128)(2,1)S(1)}, bf16[128,2048]{1,0:T(8,128)(2,1)S(1)}, u32[]{:S(2)}, u32[]{:S(2)}) collective-permute-start(bf16[128,2048]{1,0:T(8,128)(2,1)S(1)} %get-tuple-element.15.mine_ref), channel_id=1, source_target_pairs={{0,1},{1,0},{2,3},{3,2},{4,5},{5,4},{6,7},{7,6},{8,9},{9,8},{10,11... | collective-permute-start | bytes 1572872 | tf_op jit(solution)/shard_map/ppermute | solution.py:18
  89.0 11.5 %collective-permute-start.20 = (bf16[896,128]{1,0:T(8,128)(2,1)S(1)}, bf16[896,128]{1,0:T(8,128)(2,1)S(1)}, u32[]{:S(2)}, u32[]{:S(2)}) collective-permute-start(bf16[896,128]{1,0:T(8,128)(2,1)S(1)} %bitcast.9), channel_id=1, source_target_pairs={{0,8},{4,12},{8,0},{12,4},{1,9},{5,13},{9,1},{13,5},{2,10},{6,14},... | collective-permute-start | bytes 688136 | tf_op jit(solution)/shard_map/ppermute | solution.py:18
  89.0 26.5 %collective-permute-start.19 = (bf16[128,2048]{1,0:T(8,128)(2,1)S(1)}, bf16[128,2048]{1,0:T(8,128)(2,1)S(1)}, u32[]{:S(2)}, u32[]{:S(2)}) collective-permute-start(bf16[128,2048]{1,0:T(8,128)(2,1)S(1)} %broadcast_select_fusion.mine_ref), channel_id=1, source_target_pairs={{0,1},{1,0},{2,3},{3,2},{4,5},{5,4},{6,7},{7,6},{8,9},{9,8},{10,11... | collective-permute-start | bytes 1572872 | tf_op jit(solution)/shard_map/ppermute | solution.py:18
  100.5 23.5 %collective-permute-start.18 = (bf16[896,128]{1,0:T(8,128)(2,1)S(1)}, bf16[896,128]{1,0:T(8,128)(2,1)S(1)}, u32[]{:S(2)}, u32[]{:S(2)}) collective-permute-start(bf16[896,128]{1,0:T(8,128)(2,1)S(1)} %collective-permute-done.17.refs_0_), channel_id=1, source_target_pairs={{0,2},{2,0},{1,3},{3,1},{4,6},{6,4},{5,7},{7,5},{8,10},{10,8},{9,1... | collective-permute-start | bytes 688136 | tf_op jit(solution)/shard_map/ppermute | solution.py:18
  101.3 23.1 %collective-permute-start.21 = (bf16[896,128]{1,0:T(8,128)(2,1)S(1)}, bf16[896,128]{1,0:T(8,128)(2,1)S(1)}, u32[]{:S(2)}, u32[]{:S(2)}) collective-permute-start(bf16[896,128]{1,0:T(8,128)(2,1)S(1)} %collective-permute-done.20.refs_0_), channel_id=1, source_target_pairs={{0,2},{2,0},{1,3},{3,1},{4,6},{6,4},{5,7},{7,5},{8,10},{10,8},{9,1... | collective-permute-start | bytes 688136 | tf_op jit(solution)/shard_map/ppermute | solution.py:18
  103.4 25.5 %collective-permute-start.13 = (f32[2,256]{1,0:T(2,128)S(1)}, f32[2,256]{1,0:T(2,128)S(1)}, u32[]{:S(2)}, u32[]{:S(2)}) collective-permute-start(f32[2,256]{1,0:T(2,128)S(1)} %shard_map.42), channel_id=1, source_target_pairs={{0,4},{4,0},{8,12},{12,8},{1,5},{5,1},{9,13},{13,9},{2,6},{6,2},{1... | collective-permute-start | bytes 6152 | tf_op jit(solution)/shard_map/ppermute | solution.py:18
  112.8 18.2 %collective-permute-start.9 = (f32[2,256]{1,0:T(2,128)S(1)}, f32[2,256]{1,0:T(2,128)S(1)}, u32[]{:S(2)}, u32[]{:S(2)}) collective-permute-start(f32[2,256]{1,0:T(2,128)S(1)} %shard_map.40), channel_id=1, source_target_pairs={{0,12},{4,8},{8,4},{12,0},{1,13},{5,9},{9,5},{13,1},{2,14},{6,10},... | collective-permute-start | bytes 6152 | tf_op jit(solution)/shard_map/ppermute | solution.py:18
  124.8 6.3 %collective-permute-start.25 = (f32[2,256]{1,0:T(2,128)S(1)}, f32[2,256]{1,0:T(2,128)S(1)}, u32[]{:S(2)}, u32[]{:S(2)}) collective-permute-start(f32[2,256]{1,0:T(2,128)S(1)} %add.77), channel_id=1, source_target_pairs={{0,11},{1,10},{2,9},{3,8},{4,15},{5,14},{6,13},{7,12},{8,3},{9,2},... | collective-permute-start | bytes 6152 | tf_op jit(solution)/shard_map/ppermute | solution.py:18
  124.8 7.0 %collective-permute-start.24 = (f32[2,256]{1,0:T(2,128)S(1)}, f32[2,256]{1,0:T(2,128)S(1)}, u32[]{:S(2)}, u32[]{:S(2)}) collective-permute-start(f32[2,256]{1,0:T(2,128)S(1)} %add.77), channel_id=1, source_target_pairs={{0,10},{1,11},{2,8},{3,9},{4,14},{5,15},{6,12},{7,13},{8,2},{9,3},... | collective-permute-start | bytes 6152 | tf_op jit(solution)/shard_map/ppermute | solution.py:18
  126.9 6.0 %collective-permute-start.23 = (f32[2,256]{1,0:T(2,128)S(1)}, f32[2,256]{1,0:T(2,128)S(1)}, u32[]{:S(2)}, u32[]{:S(2)}) collective-permute-start(f32[2,256]{1,0:T(2,128)S(1)} %add.77), channel_id=1, source_target_pairs={{0,9},{1,8},{2,11},{3,10},{4,13},{5,12},{6,15},{7,14},{8,1},{9,0},... | collective-permute-start | bytes 6152 | tf_op jit(solution)/shard_map/ppermute | solution.py:18
  128.9 4.5 %collective-permute-start.22 = (f32[2,256]{1,0:T(2,128)S(1)}, f32[2,256]{1,0:T(2,128)S(1)}, u32[]{:S(2)}, u32[]{:S(2)}) collective-permute-start(f32[2,256]{1,0:T(2,128)S(1)} %add.77), channel_id=1, source_target_pairs={{0,8},{1,9},{2,10},{3,11},{4,12},{5,13},{6,14},{7,15},{8,0},{9,1},... | collective-permute-start | bytes 6152 | tf_op jit(solution)/shard_map/ppermute | solution.py:18
  131.0 3.0 %collective-permute-start.16 = (f32[2,256]{1,0:T(2,128)S(1)}, f32[2,256]{1,0:T(2,128)S(1)}, u32[]{:S(2)}, u32[]{:S(2)}) collective-permute-start(f32[2,256]{1,0:T(2,128)S(1)} %add_add_fusion.1), channel_id=1, source_target_pairs={{0,3},{1,2},{2,1},{3,0},{4,7},{5,6},{6,5},{7,4},{8,11},{9,10},{10,... | collective-permute-start | bytes 6152 | tf_op jit(solution)/shard_map/ppermute | solution.py:18
  131.1 3.7 %collective-permute-start.15 = (f32[2,256]{1,0:T(2,128)S(1)}, f32[2,256]{1,0:T(2,128)S(1)}, u32[]{:S(2)}, u32[]{:S(2)}) collective-permute-start(f32[2,256]{1,0:T(2,128)S(1)} %add_add_fusion.1), channel_id=1, source_target_pairs={{0,2},{1,3},{2,0},{3,1},{4,6},{5,7},{6,4},{7,5},{8,10},{9,11},{10,... | collective-permute-start | bytes 6152 | tf_op jit(solution)/shard_map/ppermute | solution.py:18
  131.9 2.8 %collective-permute-start.14 = (f32[2,256]{1,0:T(2,128)S(1)}, f32[2,256]{1,0:T(2,128)S(1)}, u32[]{:S(2)}, u32[]{:S(2)}) collective-permute-start(f32[2,256]{1,0:T(2,128)S(1)} %add_add_fusion.1), channel_id=1, source_target_pairs={{0,1},{1,0},{2,3},{3,2},{4,5},{5,4},{6,7},{7,6},{8,9},{9,8},{10,11... | collective-permute-start | bytes 6152 | tf_op jit(solution)/shard_map/ppermute | solution.py:18
  (2 other events, 3.8 us)

commit v4 on v1

v4 whole, which is shorter than its diff:
```python
import functools
import math

import jax
import jax.numpy as jnp
from jax import lax
from jax.experimental import pallas as pl
from jax.experimental.pallas import tpu as pltpu
from jax.sharding import PartitionSpec as P


MATMUL_FLOPS = 5_000_000_000


def trade(block, steps):
    axes = tuple(steps)
    sizes = [lax.axis_size(axis) for axis in axes]
    mask = 0
    for axis, size in zip(axes, sizes):
        mask = mask * size + steps[axis]
    return lax.ppermute(block, axes, [(i, i ^ mask) for i in range(math.prod(sizes))])


def pass_on(block, step, count):
    up = lax.ppermute(block[0], "dp", [(i, i + 1) for i in range(step - 1, count - 1)])
    down = lax.ppermute(block[1], "dp", [(i, i - 1) for i in range(1, count - step + 1)])
    return up, down


ANYWHERE = pl.BlockSpec(memory_space=pl.ANY)


def call(kernel, grid, where, inputs, shape, out_spec, scratch, flops, tokens):
    arrays = [array for array, _ in inputs]
    skip = len(tokens)

    def body(where, *refs):
        kernel(where, *refs[: len(arrays)], *refs[len(arrays) + skip :])

    return pl.pallas_call(
        body,
        grid_spec=pltpu.PrefetchScalarGridSpec(
            num_scalar_prefetch=1,
            grid=grid,
            in_specs=[spec for _, spec in inputs] + [ANYWHERE] * skip,
            out_specs=out_spec,
            scratch_shapes=scratch,
        ),
        out_shape=shape,
        compiler_params=pltpu.CompilerParams(vmem_limit_bytes=36 * 1024 * 1024),
        cost_estimate=pl.CostEstimate(flops=flops, bytes_accessed=1024, transcendentals=0),
    )(jnp.stack([jnp.asarray(w, jnp.int32) for w in where]), *arrays, *tokens)


def hold(blocks, tokens):
    count = len(blocks)
    return pl.pallas_call(
        lambda *refs: None,
        in_specs=[ANYWHERE] * (count + len(tokens)),
        out_specs=[ANYWHERE] * count,
        out_shape=[jax.ShapeDtypeStruct(block.shape, block.dtype) for block in blocks],
        input_output_aliases={i: i for i in range(count)},
        cost_estimate=pl.CostEstimate(flops=1024, bytes_accessed=1024, transcendentals=0),
    )(*blocks, *tokens)


def cut_kernel(turn, where, block_ref, out_ref):
    block = block_ref[...]
    out_ref[...] = block.astype(jnp.float32).T.astype(block.dtype) if turn else block


def cut(out_grads, shape, at, turn, tokens=()):
    out = shape[::-1] if turn else shape
    if shape[0] % 128 or shape[1] % 128:
        block = lax.dynamic_slice(out_grads, [i * size for i, size in zip(at, shape)], shape)
        return block.T if turn else block
    return call(
        functools.partial(cut_kernel, turn), (1,), at,
        [(out_grads, pl.BlockSpec(shape, lambda i, where: (where[0], where[1])))],
        jax.ShapeDtypeStruct(out, out_grads.dtype), pl.BlockSpec(out, lambda i, where: (0, 0)), [], 1024, tokens,
    )


def pick_kernel(where, *refs):
    *blocks, out_ref = refs
    for k, block in enumerate(blocks):

        @pl.when(where[0] == k)
        def _():
            out_ref[...] = block[...]


def from_partner(hops, me, d, count, tokens=()):
    sources, choice = [], []
    for z in range(count):
        away = z - (z ^ d)
        source = (abs(away), int(away < 0))
        if source not in sources:
            sources.append(source)
        choice.append(sources.index(source))
    where = functools.reduce(lambda found, z: jnp.where(me == z, choice[z], found), range(count), 0)
    blocks = [hops[step][way] for step, way in sources]
    spec = pl.BlockSpec(blocks[0].shape, lambda i, where: (0, 0))
    return call(
        pick_kernel, (1,), [where], [(block, spec) for block in blocks],
        jax.ShapeDtypeStruct(blocks[0].shape, blocks[0].dtype), spec, [], 1024, tokens,
    )


def joined(parts, where, axis):
    found = []
    for p in range(len(parts)):
        chosen = parts[0][...]
        for r in range(1, len(parts)):
            chosen = jnp.where(where[0] == p ^ r, parts[r][...], chosen)
        found.append(chosen)
    return found[0] if len(found) == 1 else jnp.concatenate(found, axis=axis)


def mix_kernel(where, mine_ref, other_ref, query_ref, out_ref, acts):
    half = mine_ref.shape[0]

    @pl.when((pl.program_id(0) == 0) & (pl.program_id(1) == 0))
    def _():
        acts[pl.ds(pl.multiple_of(where[0] * half, half), half), :] = mine_ref[...]
        acts[pl.ds(pl.multiple_of((1 - where[0]) * half, half), half), :] = other_ref[...]

    out_ref[0] = lax.dot_general(
        query_ref[0, 0], acts[...], (((1,), (1,)), ((), ())), preferred_element_type=jnp.float32
    )


def mixed(mine, other, core, queries, tokens=()):
    nq, _, depth, width = queries.shape
    pairs = [block if isinstance(block, tuple) else (block, 0) for block in (mine, other)]
    half = pairs[1][0].shape[0] // (2 if isinstance(other, tuple) else 1)
    tile = depth // 2
    inputs = [(array, pl.BlockSpec((half, width), lambda q, o, where, k=k: (k, 0))) for array, k in pairs]
    inputs.append((queries, pl.BlockSpec((1, 1, tile, width), lambda q, o, where: (q, 0, o, 0))))
    return call(
        mix_kernel, (nq, depth // tile), [core], inputs,
        jax.ShapeDtypeStruct((nq, depth, 2 * half), jnp.float32),
        pl.BlockSpec((1, tile, 2 * half), lambda q, o, where: (q, o, 0)),
        [pltpu.VMEM((2 * half, width), queries.dtype)], MATMUL_FLOPS, tokens,
    )


def score_kernel(where, *refs):
    parts, (mix_ref, out_ref) = refs[:-2], refs[-2:]
    grads = joined(parts, where, 1).astype(jnp.float32)
    for q in range(mix_ref.shape[0]):
        out_ref[q : q + 1, :] = jnp.sum(grads * mix_ref[q], axis=0, keepdims=True)


def scores_of_grads(parts, column, mix, piece, pieces, tokens=()):
    nq, depth, count = mix.shape
    inputs = [(part, pl.BlockSpec(part.shape, lambda i, where: (0, 0))) for part in parts]
    inputs.append((mix, pl.BlockSpec((nq, depth // pieces, count), lambda i, where: (0, piece, 0))))
    return call(
        score_kernel, (1,), [column], inputs, jax.ShapeDtypeStruct((nq, count), jnp.float32),
        pl.BlockSpec((nq, count), lambda i, where: (0, 0)), [], 1024, tokens,
    )


def deliver_kernel(number, copies, where, *refs):
    (*parts, mix_ref), terms, out_ref = refs[: -number - 2], refs[-number - 2 : -1], refs[-1]
    grads = joined(parts, where, 1).astype(jnp.float32)
    last = [jnp.sum(grads * mix_ref[q], axis=0, keepdims=True) for q in range(mix_ref.shape[0])]
    last = jnp.concatenate(last, axis=0) + terms[0][...]
    for k in range(number + 1):
        value = last if k == 0 else terms[k][...]
        for c in range(copies):
            out_ref[where[1 + k] * copies + c] = value


def delivered(parts, column, mix, piece, pieces, terms, targets, copies):
    nq, depth, count = mix.shape
    inputs = [(part, pl.BlockSpec(part.shape, lambda i, where: (0, 0))) for part in parts]
    inputs.append((mix, pl.BlockSpec((nq, depth // pieces, count), lambda i, where: (0, piece, 0))))
    inputs += [(term, pl.BlockSpec(term.shape, lambda i, where: (0, 0))) for term in terms]
    shape = (len(terms) * copies, nq, count)
    return call(
        functools.partial(deliver_kernel, len(terms) - 1, copies), (1,), [column] + list(targets), inputs,
        jax.ShapeDtypeStruct(shape, jnp.float32), pl.BlockSpec(shape, lambda i, where: (0, 0, 0)), [], 1024, (),
    )


def project_kernel(where, *refs):
    parts, (query_ref, out_ref, grads) = refs[:-3], refs[-3:]

    @pl.when((pl.program_id(0) == 0) & (pl.program_id(1) == 0))
    def _():
        grads[...] = joined(parts, where, 0)

    out_ref[0] = jnp.dot(grads[...], query_ref[0, 0], preferred_element_type=jnp.float32)


def projected(parts, column, queries, tokens=()):
    nq, _, depth, width = queries.shape
    count = sum(part.shape[0] for part in parts)
    tile = width // 2
    inputs = [(part, pl.BlockSpec(part.shape, lambda q, i, where: (0, 0))) for part in parts]
    inputs.append((queries, pl.BlockSpec((1, 1, depth, tile), lambda q, i, where: (q, 0, 0, i))))
    return call(
        project_kernel, (nq, width // tile), [column], inputs,
        jax.ShapeDtypeStruct((nq, count, width), jnp.float32),
        pl.BlockSpec((1, count, tile), lambda q, i, where: (q, 0, i)),
        [pltpu.VMEM((count, depth), queries.dtype)], MATMUL_FLOPS, tokens,
    )


def finish_kernel(where, mine_ref, other_ref, proj_ref, out_ref):
    half, width = mine_ref.shape
    swapped = where[0] == 1
    for h, (first, second) in enumerate(((mine_ref, other_ref), (other_ref, mine_ref))):
        acts = jnp.where(swapped, second[...], first[...]).astype(jnp.float32)
        for q in range(proj_ref.shape[0]):
            terms = acts * proj_ref[q, h * half : (h + 1) * half, :]
            lanes = terms[:, :128]
            for at in range(128, width, 128):
                lanes = lanes + terms[:, at : at + 128]
            out_ref[q : q + 1, h * half : (h + 1) * half] = jnp.sum(lanes.T, axis=0, keepdims=True)


def scores_of_acts(mine, other, core, proj, tokens=()):
    nq, count, _ = proj.shape
    inputs = [(block, pl.BlockSpec(block.shape, lambda i, where: (0, 0))) for block in (mine, other)]
    inputs.append((proj, pl.BlockSpec(proj.shape, lambda i, where: (0, 0, 0))))
    return call(
        finish_kernel, (1,), [core], inputs, jax.ShapeDtypeStruct((nq, count), jnp.float32),
        pl.BlockSpec((nq, count), lambda i, where: (0, 0)), [], 1024, tokens,
    )


def on_device(activations, out_grads, queries):
    count, spread = lax.axis_size("dp"), lax.axis_size("din")
    me, column, core = lax.axis_index("dp"), lax.axis_index("din"), lax.axis_index("dout")
    tokens, rows = activations.shape[0], queries.shape[2]
    part, half = tokens // spread, tokens // 2
    pieces = 2

    def grads_for(d, turn, piece=0, pieces=1, tokens=()):
        size = rows // pieces
        return cut(out_grads, (part, size), (column, (me ^ d) * pieces + piece), turn, tokens)

    def to_columns(arrived):
        return [arrived] + [trade(arrived, {"din": r}) for r in range(1, spread)]

    def acts_of(d, tokens=()):
        block = from_partner(hops, me, d, count, tokens)
        return block, trade(block, {"dout": 1})

    far, late = count - 1, count // 2
    early = [d for d in range(1, count) if d not in (far, late)]

    mine = lax.dynamic_slice_in_dim(activations, core * half, half, 0)
    hops = [(mine, mine)]
    hops.append(pass_on(hops[0], 1, count))

    sent = {far: grads_for(far, False)}
    for d in early:
        sent[d] = grads_for(d, True)
    arrived = {d: trade(block, {"dp": d}) for d, block in sent.items()}

    zero = jnp.zeros((), jnp.int32)
    own_mix = mixed((activations, 0), (activations, 1), zero, queries, list(sent.values()))
    own = cut(out_grads, (tokens, rows), (zero, me), True)
    scores = {0: scores_of_grads([own], zero, own_mix, 0, 1)}

    mixes, token = {}, own_mix
    tail = []
    for step in range(1, count):
        if step > 1:
            hops.append(pass_on(hops[-1], step, count))
        if step == late:
            hops[step] = hold(hops[step], list(arrived.values()) + [token])
        if step in early:
            mixes[step] = token = mixed(*acts_of(step), core, queries, [token])
        if step <= pieces:
            waits = [token] if step == 1 else list(hops[step])
            tail.append(trade(grads_for(late, True, step - 1, pieces, waits), {"dp": late}))
    mixes[late] = token = mixed(*acts_of(late), core, queries, [token])
    proj = projected(to_columns(arrived[far]), column, queries, [token, tail[0], scores[0]])

    for d in early:
        scores[d] = scores_of_grads(to_columns(arrived[d]), column, mixes[d], 0, 1, [proj])
    scores[far] = scores_of_acts(*acts_of(far, [mixes[late]]), core, proj, [scores[d] for d in early])
    for piece, block in enumerate(tail[:-1]):
        term = scores_of_grads(to_columns(block), column, mixes[late], piece, pieces, [scores[far]])
        scores[late] = scores[late] + term if piece else term
    order = [late] + [d for d in range(count) if d != late]
    last, = hold(tail[-1:], [proj])
    blocks = delivered(
        to_columns(last), column, mixes[late], pieces - 1, pieces,
        [scores[d] for d in order], [me ^ d for d in order], spread * lax.axis_size("dout"),
    )
    return jnp.sum(lax.all_to_all(blocks, ("dp", "din", "dout"), 0, 0), axis=0)


def solution(mesh):
    placed = (P(("groups", "dp"), "din"), P(("groups", "dp"), "dout"), P(None, "dout", "dp", "din"))
    return jax.shard_map(
        on_device, mesh=mesh, in_specs=placed, out_specs=P(None, ("groups", "dp")), check_vma=False
    )
```

time: 222 us -> 130 us (0.59)
  waiting for transfers between devices: 92 us -> 20.4 us
  blocking collectives: 80.7 us -> 11.6 us
  Pallas kernels: 0 us -> 42.5 us
  starting transfers between devices: 0.04 us -> 25.5 us
  matrix products: 18.4 us -> 0 us
  local copies, waits for them, and re-layouts: 13.7 us -> 27.5 us
  between operations: 13.5 us -> 0.33 us
  other arithmetic: 3.41 us -> 0.99 us
    all_gather x2 -> x0, waiting for transfers between devices: 92 us -> none  [the longest x1 49.2 us: on_device(): grads = lax.all_gather(blocks, 'din', axis=1).reshape(count * tokens, rows)]
    pallas_call x0 -> x19, Pallas kernels: none -> 42.5 us  [the longest x17 42.5 us: call(): pl.pallas_call(body, grid_spec=pltpu.PrefetchScalarGridSpec(num_scalar_pr...]
    all_to_all x1, blocking collectives: 48.8 us -> 11.6 us  [on_device(): return jnp.sum(lax.all_to_all(blocks, ('dp', 'din', 'dout'), 0, 0), axis=0)]
    psum x1 -> x0, blocking collectives: 31.9 us -> none  [on_device(): total = lax.psum(total, ('dp', 'din', 'dout'))]
    ppermute x0 -> x17, starting transfers between devices: none -> 25.5 us  [the longest x11 13.9 us: trade(): lax.ppermute(block, axes, [(i, i ^ mask) for i in range(math.prod(sizes))])]
    unnamed x5 -> x48, local copies, waits for them, and re-layouts: 3.29 us -> 26.3 us
    ppermute x0 -> x17, waiting for transfers between devices: none -> 20.4 us  [the longest x3 17 us: pass_on(): lax.ppermute(block[1], 'dp', [(i, i - 1) for i in range(1, count - step +...]
    dot_general x1 -> x0, matrix products: 18.4 us -> none  [on_device(): jnp.einsum('tc,qci->qti', grads, queries[:, 0], preferred_element_type=jn...]
  transfers between devices with their start and end apart: 2 -> 17, of which waited for: 2 -> 4; matrix products, arithmetic and copies ran while one was open for 3% -> 0% of each run, Pallas kernels for 0% -> 32%
where the time goes in v4:
time: 130 us; the launch traced here: 129 us
  Pallas kernels  42.5 us (33%)
  local copies, waits for them, and re-layouts  27.5 us (21%)
  starting transfers between devices  25.5 us (20%)
  waiting for transfers between devices  20.4 us (16%)
  blocking collectives  11.6 us (9%)
    pallas_call x17, Pallas kernels, call(): pl.pallas_call(body, grid_spec=pltpu.PrefetchScalarGridSpec(num_scalar_pr...  42.5 us
    unnamed x48, local copies, waits for them, and re-layouts  26.3 us
    ppermute x3, waiting for transfers between devices, pass_on(): lax.ppermute(block[1], 'dp', [(i, i - 1) for i in range(1, count - step +...  17 us
    ppermute x11, starting transfers between devices, trade(): lax.ppermute(block, axes, [(i, i ^ mask) for i in range(math.prod(sizes))])  13.9 us
    all_to_all x1, blocking collectives, on_device(): return jnp.sum(lax.all_to_all(blocks, ('dp', 'din', 'dout'), 0, 0), axis=0)  11.6 us
    ppermute x3, starting transfers between devices, pass_on(): lax.ppermute(block[0], 'dp', [(i, i + 1) for i in range(step - 1, count -...  7.72 us
    ppermute x3, starting transfers between devices, pass_on(): lax.ppermute(block[1], 'dp', [(i, i - 1) for i in range(1, count - step +...  3.85 us
  transfers between devices with their start and end apart: 17, of which 4 were waited for; matrix products, arithmetic and copies ran while one was open for 0% of the time, Pallas kernels for 32%

profile of v4, /device:TPU:0, one launch (start us, length us, event | category | flops | bytes accessed | tf_op | source)
XLA Modules:
  0.0 128.8 jit_solution(11039795803428368594)
XLA Ops:
  1.1 1.3 %collective-permute-start.2 = (bf16[128,2048]{1,0:T(8,128)(2,1)S(1)}, bf16[128,2048]{1,0:T(8,128)(2,1)S(1)}, u32[]{:S(2)}, u32[]{:S(2)}) collective-permute-start(bf16[128,2048]{1,0:T(8,128)(2,1)S(1)} %constant_dynamic-slice_fusion), channel_id=1, source_target_pairs={{4,0},{8,4},{12,8},{5,1},{9,5},{13,9},{6,2},{10,6},{14,10},{7,3},{... | collective-permute-start | bytes 1572872 | tf_op jit(solution)/shard_map/ppermute | solution.py:26
  2.4 5.6 %collective-permute-start = (bf16[128,2048]{1,0:T(8,128)(2,1)S(1)}, bf16[128,2048]{1,0:T(8,128)(2,1)S(1)}, u32[]{:S(2)}, u32[]{:S(2)}) collective-permute-start(bf16[128,2048]{1,0:T(8,128)(2,1)S(1)} %constant_dynamic-slice_fusion), channel_id=1, source_target_pairs={{0,4},{4,8},{8,12},{1,5},{5,9},{9,13},{2,6},{6,10},{10,14},{3,7},{... | collective-permute-start | bytes 1572872 | tf_op jit(solution)/shard_map/ppermute | solution.py:25
  8.1 9.9 %collective-permute-done.2.refs_0_.refs_1_ = bf16[128,2048]{1,0:T(8,128)(2,1)S(1)} collective-permute-done((bf16[128,2048]{1,0:T(8,128)(2,1)S(1)}, bf16[128,2048]{1,0:T(8,128)(2,1)S(1)}, u32[]{:S(2)}, u32[]{:S(2)}) %collective-permute-start.2) | collective-permute-done | bytes 524320 | tf_op jit(solution)/shard_map/ppermute | solution.py:26
  19.3 2.0 %copy-done.5 = bf16[256,7168]{1,0:T(8,128)(2,1)S(1)} copy-done((bf16[256,7168]{1,0:T(8,128)(2,1)S(1)}, bf16[256,7168]{1,0:T(8,128)(2,1)}, u32[]{:S(2)}) %copy-start.5) | copy-done | bytes 3670040
  21.9 4.8 %collective-permute-start.4 = (bf16[128,1792]{1,0:T(8,128)(2,1)S(1)}, bf16[128,1792]{1,0:T(8,128)(2,1)}, u32[]{:S(2)}, u32[]{:S(2)}) collective-permute-start(bf16[128,1792]{1,0:T(8,128)(2,1)S(1)} %shard_map.37.refs_3_), channel_id=1, source_target_pairs={{0,12},{4,8},{8,4},{12,0},{1,13},{5,9},{9,5},{13,1},{2,14},{6,10},... | collective-permute-start | bytes 1376264 | tf_op jit(solution)/shard_map/ppermute | solution.py:21
  26.7 1.6 %shard_map.38.refs_4_ = bf16[1792,128]{1,0:T(8,128)(2,1)} custom-call(s32[2]{0:T(128)S(1)} %pad_add_fusion.2.where, bf16[256,7168]{1,0:T(8,128)(2,1)S(1)} %copy-done.6), custom_call_target="tpu_custom_call" | custom-call | flops 1024 | bytes 1024 | tf_op jit(solution)/shard_map/pallas_call | solution.py:40
  28.3 1.3 collective-permute-start.3
  30.3 7.9 %shard_map.40.refs_3_.refs_1_ = f32[2,1792,256]{2,1,0:T(8,128)S(1)} custom-call(s32[1]{0:T(128)} %constant.25.clone.1.where, bf16[256,2048]{1,0:T(8,128)(2,1)S(1)} %copy-done.15, bf16[256,2048]{1,0:T(8,128)(2,1)S(1)} %copy-done.15, bf16[2,1,1792,2048]{3,2,1,0:T(8,128)(2,1)} %refs_2_.7, bf16[128,1792]{1,0:T(8,128)(2,1)S(1)} %shard_map.37.refs_3_, ...), custom_call_target="tpu_custom_call" | custom-call | flops 5000000000 | bytes 1024 | tf_op jit(solution)/shard_map/pallas_call | solution.py:40
  38.2 1.9 %copy-done.12 = f32[2,1792,256]{2,1,0:T(8,128)} copy-done((f32[2,1792,256]{2,1,0:T(8,128)}, f32[2,1792,256]{2,1,0:T(8,128)S(1)}, u32[]{:S(2)}) %copy-start.12) | copy-done | bytes 3670040
  40.0 2.0 %copy-done.13 = f32[2,1792,256]{2,1,0:T(8,128)S(1)} copy-done((f32[2,1792,256]{2,1,0:T(8,128)S(1)}, f32[2,1792,256]{2,1,0:T(8,128)}, u32[]{:S(2)}) %copy-start.13) | copy-done | bytes 3670040
  42.1 8.0 %shard_map.41.refs_4_.refs_3_.refs_1_.refs_2_ = f32[2,1792,256]{2,1,0:T(8,128)S(1)} custom-call(s32[1]{0:T(128)} %bitcast.6.where, bf16[128,2048]{1,0:T(8,128)(2,1)S(1)} %shard_map.39.refs_0_, bf16[128,2048]{1,0:T(8,128)(2,1)} %collective-permute-done.6.refs_1_, bf16[2,1,1792,2048]{3,2,1,0:T(8,128)(2,1)} %refs_2_.7, f32[2,1792,256]{2,1,0:T(8,128)S(1)} %copy-done.13), custom_call_target="tpu_custom_call" | custom-call | flops 5000000000 | bytes 1024 | tf_op jit(solution)/shard_map/pallas_call | solution.py:40
  50.1 1.8 %copy-done = f32[2,1792,256]{2,1,0:T(8,128)} copy-done((f32[2,1792,256]{2,1,0:T(8,128)}, f32[2,1792,256]{2,1,0:T(8,128)S(1)}, u32[]{:S(2)}) %copy-start) | copy-done | bytes 3670040
  51.9 7.1 %collective-permute-done.3.refs_1_ = bf16[128,2048]{1,0:T(8,128)(2,1)S(1)} collective-permute-done((bf16[128,2048]{1,0:T(8,128)(2,1)S(1)}, bf16[128,2048]{1,0:T(8,128)(2,1)S(1)}, u32[]{:S(2)}, u32[]{:S(2)}) %collective-permute-start.3) | collective-permute-done | bytes 524320 | tf_op jit(solution)/shard_map/ppermute | solution.py:26
  63.0 2.1 %copy-done.7 = bf16[256,7168]{1,0:T(8,128)(2,1)S(1)} copy-done((bf16[256,7168]{1,0:T(8,128)(2,1)S(1)}, bf16[256,7168]{1,0:T(8,128)(2,1)}, u32[]{:S(2)}) %copy-start.7) | copy-done | bytes 3670040
  66.0 1.4 %collective-permute-start.14 = (bf16[128,2048]{1,0:T(8,128)(2,1)S(1)}, bf16[128,2048]{1,0:T(8,128)(2,1)}, u32[]{:S(2)}, u32[]{:S(2)}) collective-permute-start(bf16[128,2048]{1,0:T(8,128)(2,1)S(1)} %copy-done.21), channel_id=1, source_target_pairs={{8,12},{9,13},{10,14},{11,15},{24,28},{25,29},{26,30},{27,31}} | collective-permute-start | bytes 1572872 | tf_op jit(solution)/shard_map/ppermute | solution.py:25
  67.5 1.3 collective-permute-start.13
  68.8 2.0 %copy-done.14 = f32[2,1792,256]{2,1,0:T(8,128)S(1)} copy-done((f32[2,1792,256]{2,1,0:T(8,128)S(1)}, f32[2,1792,256]{2,1,0:T(8,128)}, u32[]{:S(2)}) %copy-start.14) | copy-done | bytes 3670040
  71.3 1.6 %collective-permute-start.8 = (bf16[128,1792]{1,0:T(8,128)(2,1)}, bf16[128,1792]{1,0:T(8,128)(2,1)S(1)}, u32[]{:S(2)}, u32[]{:S(2)}) collective-permute-start(bf16[128,1792]{1,0:T(8,128)(2,1)} %collective-permute-done.4.refs_2_.refs_0_), channel_id=1, source_target_pairs={{0,2},{2,0},{1,3},{3,1},{4,6},{6,4},{5,7},{7,5},{8,10},{10,8},{9,1... | collective-permute-start | bytes 1376264 | tf_op jit(solution)/shard_map/ppermute | solution.py:21
  73.4 2.0 %copy-done.8 = bf16[256,7168]{1,0:T(8,128)(2,1)S(1)} copy-done((bf16[256,7168]{1,0:T(8,128)(2,1)S(1)}, bf16[256,7168]{1,0:T(8,128)(2,1)}, u32[]{:S(2)}) %copy-start.8) | copy-done | bytes 3670040
  76.9 4.7 %collective-permute-start.10 = (bf16[896,128]{1,0:T(8,128)(2,1)S(1)}, bf16[896,128]{1,0:T(8,128)(2,1)S(1)}, u32[]{:S(2)}, u32[]{:S(2)}) collective-permute-start(bf16[896,128]{1,0:T(8,128)(2,1)S(1)} %shard_map.46), channel_id=1, source_target_pairs={{0,8},{4,12},{8,0},{12,4},{1,9},{5,13},{9,1},{13,5},{2,10},{6,14},... | collective-permute-start | bytes 688136 | tf_op jit(solution)/shard_map/ppermute | solution.py:21
  81.6 8.0 %shard_map.45.refs_3_.refs_4_.refs_2_ = f32[2,1792,256]{2,1,0:T(8,128)S(1)} custom-call(s32[1]{0:T(128)} %bitcast.6.where, bf16[128,2048]{1,0:T(8,128)(2,1)S(1)} %shard_map.44.refs_0_, bf16[128,2048]{1,0:T(8,128)(2,1)} %collective-permute-done.9.refs_1_, bf16[2,1,1792,2048]{3,2,1,0:T(8,128)(2,1)} %refs_2_.7, f32[2,1792,256]{2,1,0:T(8,128)S(1)} %copy-done.1), custom_call_target="tpu_custom_call" | custom-call | flops 5000000000 | bytes 1024 | tf_op jit(solution)/shard_map/pallas_call | solution.py:40
  89.6 2.2 %collective-permute-done.10.refs_4_.refs_0_ = bf16[896,128]{1,0:T(8,128)(2,1)S(1)} collective-permute-done((bf16[896,128]{1,0:T(8,128)(2,1)S(1)}, bf16[896,128]{1,0:T(8,128)(2,1)S(1)}, u32[]{:S(2)}, u32[]{:S(2)}) %collective-permute-start.10) | collective-permute-done | bytes 229408 | tf_op jit(solution)/shard_map/ppermute | solution.py:21
  91.8 1.5 %collective-permute-start.12 = (bf16[896,128]{1,0:T(8,128)(2,1)S(1)}, bf16[896,128]{1,0:T(8,128)(2,1)}, u32[]{:S(2)}, u32[]{:S(2)}) collective-permute-start(bf16[896,128]{1,0:T(8,128)(2,1)S(1)} %collective-permute-done.10.refs_4_.refs_0_), channel_id=1, source_target_pairs={{0,2},{2,0},{1,3},{3,1},{4,6},{6,4},{5,7},{7,5},{8,10},{10,8},{9,1... | collective-permute-start | bytes 688136 | tf_op jit(solution)/shard_map/ppermute | solution.py:21
  93.3 1.3 shard_map.51.refs_0_
  94.7 8.0 %shard_map.49.refs_1_.refs_3_.refs_2_ = f32[2,256,2048]{2,1,0:T(8,128)S(1)} custom-call(s32[1]{0:T(128)} %bitcast.where, bf16[128,1792]{1,0:T(8,128)(2,1)} %collective-permute-done.4.refs_2_.refs_0_, bf16[128,1792]{1,0:T(8,128)(2,1)S(1)} %collective-permute-done.8.refs_1_, bf16[2,1,1792,2048]{3,2,1,0:T(8,128)(2,1)} %refs_2_.7, ...), custom_call_target="tpu_custom_call" | custom-call | flops 5000000000 | bytes 1024 | tf_op jit(solution)/shard_map/pallas_call | solution.py:40
  102.7 2.1 %copy-done.9 = f32[2,256,2048]{2,1,0:T(8,128)} copy-done((f32[2,256,2048]{2,1,0:T(8,128)}, f32[2,256,2048]{2,1,0:T(8,128)S(1)}, u32[]{:S(2)}) %copy-start.9) | copy-done | bytes 4194328
  106.1 2.0 %copy-done.2 = f32[2,1792,256]{2,1,0:T(8,128)S(1)} copy-done((f32[2,1792,256]{2,1,0:T(8,128)S(1)}, f32[2,1792,256]{2,1,0:T(8,128)}, u32[]{:S(2)}) %copy-start.2) | copy-done | bytes 3670040
  108.2 2.2 %copy-done.10 = f32[2,256,2048]{2,1,0:T(8,128)S(1)} copy-done((f32[2,256,2048]{2,1,0:T(8,128)S(1)}, f32[2,256,2048]{2,1,0:T(8,128)}, u32[]{:S(2)}) %copy-start.10) | copy-done | bytes 4194328
  110.3 1.8 %shard_map.52.refs_3_.refs_5_ = f32[2,256]{1,0:T(2,128)S(1)} custom-call(s32[1]{0:T(128)} %bitcast.where, bf16[1792,128]{1,0:T(8,128)(2,1)} %collective-permute-done.5.refs_3_.refs_0_, bf16[1792,128]{1,0:T(8,128)(2,1)S(1)} %collective-permute-done.16.refs_1_, f32[2,1792,256]{2,1,0:T(8,128)S(1)} %copy-done.2, f32[2,256,2048]{2,1,0:T(8,128)S(1)} %copy-done.10), custom_call_target="tpu_custom_call" | custom-call | flops 1024 | bytes 1024 | tf_op jit(solution)/shard_map/pallas_call | solution.py:40
  113.1 1.2 copy-done.4
  114.3 1.3 shard_map.54.refs_3_
  116.5 11.6 %all_to_all.5 = f32[16,2,256]{2,1,0:T(2,128)S(1)} all-to-all(f32[16,2,256]{2,1,0:T(2,128)S(1)} %shard_map.55), channel_id=1, replica_groups=mesh['groups'=2,'dp'=4,'din'=2,'dout'=2] {'dp','din','dout'}, dimensions={0} | all-to-all | bytes 65536 | tf_op jit(solution)/shard_map/all_to_all | solution.py:297
  (78 shorter events, 14.9 us)
Async XLA Ops:
  1.1 16.8 %collective-permute-start.2 = (bf16[128,2048]{1,0:T(8,128)(2,1)S(1)}, bf16[128,2048]{1,0:T(8,128)(2,1)S(1)}, u32[]{:S(2)}, u32[]{:S(2)}) collective-permute-start(bf16[128,2048]{1,0:T(8,128)(2,1)S(1)} %constant_dynamic-slice_fusion), channel_id=1, source_target_pairs={{4,0},{8,4},{12,8},{5,1},{9,5},{13,9},{6,2},{10,6},{14,10},{7,3},{... | collective-permute-start | bytes 1572872 | tf_op jit(solution)/shard_map/ppermute | solution.py:26
  2.4 16.7 %collective-permute-start = (bf16[128,2048]{1,0:T(8,128)(2,1)S(1)}, bf16[128,2048]{1,0:T(8,128)(2,1)S(1)}, u32[]{:S(2)}, u32[]{:S(2)}) collective-permute-start(bf16[128,2048]{1,0:T(8,128)(2,1)S(1)} %constant_dynamic-slice_fusion), channel_id=1, source_target_pairs={{0,4},{4,8},{8,12},{1,5},{5,9},{9,13},{2,6},{6,10},{10,14},{3,7},{... | collective-permute-start | bytes 1572872 | tf_op jit(solution)/shard_map/ppermute | solution.py:25
  19.2 20.9 %collective-permute-start.6 = (bf16[128,2048]{1,0:T(8,128)(2,1)S(1)}, bf16[128,2048]{1,0:T(8,128)(2,1)}, u32[]{:S(2)}, u32[]{:S(2)}) collective-permute-start(bf16[128,2048]{1,0:T(8,128)(2,1)S(1)} %shard_map.39.refs_0_), channel_id=1, source_target_pairs={{0,1},{1,0},{2,3},{3,2},{4,5},{5,4},{6,7},{7,6},{8,9},{9,8},{10,11... | collective-permute-start | bytes 1572872 | tf_op jit(solution)/shard_map/ppermute | solution.py:21
  19.3 2.0 %copy-start.5 = (bf16[256,7168]{1,0:T(8,128)(2,1)S(1)}, bf16[256,7168]{1,0:T(8,128)(2,1)}, u32[]{:S(2)}) copy-start(bf16[256,7168]{1,0:T(8,128)(2,1)} %refs_0_.11) | copy-start | bytes 11010052
  21.4 5.3 %copy-start.6 = (bf16[256,7168]{1,0:T(8,128)(2,1)S(1)}, bf16[256,7168]{1,0:T(8,128)(2,1)}, u32[]{:S(2)}) copy-start(bf16[256,7168]{1,0:T(8,128)(2,1)} %refs_0_.11) | copy-start | bytes 11010052
  21.4 8.9 %copy-start.15 = (bf16[256,2048]{1,0:T(8,128)(2,1)S(1)}, bf16[256,2048]{1,0:T(8,128)(2,1)}, u32[]{:S(2)}) copy-start(bf16[256,2048]{1,0:T(8,128)(2,1)} %refs_1_.1) | copy-start | bytes 3145732
  21.9 29.9 %collective-permute-start.4 = (bf16[128,1792]{1,0:T(8,128)(2,1)S(1)}, bf16[128,1792]{1,0:T(8,128)(2,1)}, u32[]{:S(2)}, u32[]{:S(2)}) collective-permute-start(bf16[128,1792]{1,0:T(8,128)(2,1)S(1)} %shard_map.37.refs_3_), channel_id=1, source_target_pairs={{0,12},{4,8},{8,4},{12,0},{1,13},{5,9},{9,5},{13,1},{2,14},{6,10},... | collective-permute-start | bytes 1376264 | tf_op jit(solution)/shard_map/ppermute | solution.py:21
  28.3 23.6 %collective-permute-start.5 = (bf16[1792,128]{1,0:T(8,128)(2,1)}, bf16[1792,128]{1,0:T(8,128)(2,1)}, u32[]{:S(2)}, u32[]{:S(2)}) collective-permute-start(bf16[1792,128]{1,0:T(8,128)(2,1)} %shard_map.38.refs_4_), channel_id=1, source_target_pairs={{0,4},{4,0},{8,12},{12,8},{1,5},{5,1},{9,13},{13,9},{2,6},{6,2},{1... | collective-permute-start | bytes 1376264 | tf_op jit(solution)/shard_map/ppermute | solution.py:21
  28.3 30.8 %collective-permute-start.3 = (bf16[128,2048]{1,0:T(8,128)(2,1)S(1)}, bf16[128,2048]{1,0:T(8,128)(2,1)S(1)}, u32[]{:S(2)}, u32[]{:S(2)}) collective-permute-start(bf16[128,2048]{1,0:T(8,128)(2,1)S(1)} %collective-permute-done.2.refs_0_.refs_1_), channel_id=1, source_target_pairs={{4,0},{8,4},{5,1},{9,5},{6,2},{10,6},{7,3},{11,7},{20,16},{24,20},... | collective-permute-start | bytes 1572872 | tf_op jit(solution)/shard_map/ppermute | solution.py:26
  29.5 29.5 %collective-permute-start.1 = (bf16[128,2048]{1,0:T(8,128)(2,1)S(1)}, bf16[128,2048]{1,0:T(8,128)(2,1)S(1)}, u32[]{:S(2)}, u32[]{:S(2)}) collective-permute-start(bf16[128,2048]{1,0:T(8,128)(2,1)S(1)} %collective-permute-done.refs_1_.refs_2_), channel_id=1, source_target_pairs={{4,8},{8,12},{5,9},{9,13},{6,10},{10,14},{7,11},{11,15},{20,24},{2... | collective-permute-start | bytes 1572872 | tf_op jit(solution)/shard_map/ppermute | solution.py:25
  40.0 2.0 %copy-start.13 = (f32[2,1792,256]{2,1,0:T(8,128)S(1)}, f32[2,1792,256]{2,1,0:T(8,128)}, u32[]{:S(2)}) copy-start(f32[2,1792,256]{2,1,0:T(8,128)} %copy-done.12) | copy-start | bytes 11010052
  62.7 3.3 %copy-start.21 = (bf16[128,2048]{1,0:T(8,128)(2,1)S(1)}, bf16[128,2048]{1,0:T(8,128)(2,1)}, u32[]{:S(2)}) copy-start(bf16[128,2048]{1,0:T(8,128)(2,1)} %get-tuple-element.7.refs_1_) | copy-start | bytes 1572868
  62.7 4.7 %copy-start.18 = (bf16[128,2048]{1,0:T(8,128)(2,1)S(1)}, bf16[128,2048]{1,0:T(8,128)(2,1)}, u32[]{:S(2)}) copy-start(bf16[128,2048]{1,0:T(8,128)(2,1)} %get-tuple-element.8.refs_2_.refs_0_) | copy-start | bytes 1572868
  62.8 14.1 %collective-permute-start.9 = (bf16[128,2048]{1,0:T(8,128)(2,1)S(1)}, bf16[128,2048]{1,0:T(8,128)(2,1)}, u32[]{:S(2)}, u32[]{:S(2)}) collective-permute-start(bf16[128,2048]{1,0:T(8,128)(2,1)S(1)} %shard_map.44.refs_0_), channel_id=1, source_target_pairs={{0,1},{1,0},{2,3},{3,2},{4,5},{5,4},{6,7},{7,6},{8,9},{9,8},{10,11... | collective-permute-start | bytes 1572872 | tf_op jit(solution)/shard_map/ppermute | solution.py:21
  63.0 2.1 %copy-start.7 = (bf16[256,7168]{1,0:T(8,128)(2,1)S(1)}, bf16[256,7168]{1,0:T(8,128)(2,1)}, u32[]{:S(2)}) copy-start(bf16[256,7168]{1,0:T(8,128)(2,1)} %refs_0_.11) | copy-start | bytes 11010052
  66.0 25.8 %collective-permute-start.14 = (bf16[128,2048]{1,0:T(8,128)(2,1)S(1)}, bf16[128,2048]{1,0:T(8,128)(2,1)}, u32[]{:S(2)}, u32[]{:S(2)}) collective-permute-start(bf16[128,2048]{1,0:T(8,128)(2,1)S(1)} %copy-done.21), channel_id=1, source_target_pairs={{8,12},{9,13},{10,14},{11,15},{24,28},{25,29},{26,30},{27,31}} | collective-permute-start | bytes 1572872 | tf_op jit(solution)/shard_map/ppermute | solution.py:25
  67.5 25.8 %collective-permute-start.13 = (bf16[128,2048]{1,0:T(8,128)(2,1)S(1)}, bf16[128,2048]{1,0:T(8,128)(2,1)}, u32[]{:S(2)}, u32[]{:S(2)}) collective-permute-start(bf16[128,2048]{1,0:T(8,128)(2,1)S(1)} %copy-done.18), channel_id=1, source_target_pairs={{4,0},{5,1},{6,2},{7,3},{20,16},{21,17},{22,18},{23,19}} | collective-permute-start | bytes 1572872 | tf_op jit(solution)/shard_map/ppermute | solution.py:26
  71.3 4.8 %copy-start.1 = (f32[2,1792,256]{2,1,0:T(8,128)S(1)}, f32[2,1792,256]{2,1,0:T(8,128)}, u32[]{:S(2)}) copy-start(f32[2,1792,256]{2,1,0:T(8,128)} %copy-done) | copy-start | bytes 11010052
  71.3 23.3 %collective-permute-start.8 = (bf16[128,1792]{1,0:T(8,128)(2,1)}, bf16[128,1792]{1,0:T(8,128)(2,1)S(1)}, u32[]{:S(2)}, u32[]{:S(2)}) collective-permute-start(bf16[128,1792]{1,0:T(8,128)(2,1)} %collective-permute-done.4.refs_2_.refs_0_), channel_id=1, source_target_pairs={{0,2},{2,0},{1,3},{3,1},{4,6},{6,4},{5,7},{7,5},{8,10},{10,8},{9,1... | collective-permute-start | bytes 1376264 | tf_op jit(solution)/shard_map/ppermute | solution.py:21
  72.9 33.2 %collective-permute-start.16 = (bf16[1792,128]{1,0:T(8,128)(2,1)}, bf16[1792,128]{1,0:T(8,128)(2,1)S(1)}, u32[]{:S(2)}, u32[]{:S(2)}) collective-permute-start(bf16[1792,128]{1,0:T(8,128)(2,1)} %collective-permute-done.5.refs_3_.refs_0_), channel_id=1, source_target_pairs={{0,2},{2,0},{1,3},{3,1},{4,6},{6,4},{5,7},{7,5},{8,10},{10,8},{9,1... | collective-permute-start | bytes 1376264 | tf_op jit(solution)/shard_map/ppermute | solution.py:21
  76.9 14.9 %collective-permute-start.10 = (bf16[896,128]{1,0:T(8,128)(2,1)S(1)}, bf16[896,128]{1,0:T(8,128)(2,1)S(1)}, u32[]{:S(2)}, u32[]{:S(2)}) collective-permute-start(bf16[896,128]{1,0:T(8,128)(2,1)S(1)} %shard_map.46), channel_id=1, source_target_pairs={{0,8},{4,12},{8,0},{12,4},{1,9},{5,13},{9,1},{13,5},{2,10},{6,14},... | collective-permute-start | bytes 688136 | tf_op jit(solution)/shard_map/ppermute | solution.py:21
  89.6 13.1 %copy-start.3 = (f32[2,1792,256]{2,1,0:T(8,128)}, f32[2,1792,256]{2,1,0:T(8,128)S(1)}, u32[]{:S(2)}) copy-start(f32[2,1792,256]{2,1,0:T(8,128)S(1)} %shard_map.45.refs_3_.refs_4_.refs_2_) | copy-start | bytes 11010052
  91.8 13.0 %collective-permute-start.7 = (bf16[896,128]{1,0:T(8,128)(2,1)S(1)}, bf16[896,128]{1,0:T(8,128)(2,1)S(1)}, u32[]{:S(2)}, u32[]{:S(2)}) collective-permute-start(bf16[896,128]{1,0:T(8,128)(2,1)S(1)} %shard_map.43), channel_id=1, source_target_pairs={{0,8},{4,12},{8,0},{12,4},{1,9},{5,13},{9,1},{13,5},{2,10},{6,14},... | collective-permute-start | bytes 688136 | tf_op jit(solution)/shard_map/ppermute | solution.py:21
  91.8 21.3 %collective-permute-start.12 = (bf16[896,128]{1,0:T(8,128)(2,1)S(1)}, bf16[896,128]{1,0:T(8,128)(2,1)}, u32[]{:S(2)}, u32[]{:S(2)}) collective-permute-start(bf16[896,128]{1,0:T(8,128)(2,1)S(1)} %collective-permute-done.10.refs_4_.refs_0_), channel_id=1, source_target_pairs={{0,2},{2,0},{1,3},{3,1},{4,6},{6,4},{5,7},{7,5},{8,10},{10,8},{9,1... | collective-permute-start | bytes 688136 | tf_op jit(solution)/shard_map/ppermute | solution.py:21
  94.6 17.6 %collective-permute-start.15 = (bf16[128,2048]{1,0:T(8,128)(2,1)S(1)}, bf16[128,2048]{1,0:T(8,128)(2,1)S(1)}, u32[]{:S(2)}, u32[]{:S(2)}) collective-permute-start(bf16[128,2048]{1,0:T(8,128)(2,1)S(1)} %shard_map.51.refs_0_), channel_id=1, source_target_pairs={{0,1},{1,0},{2,3},{3,2},{4,5},{5,4},{6,7},{7,6},{8,9},{9,8},{10,11... | collective-permute-start | bytes 1572872 | tf_op jit(solution)/shard_map/ppermute | solution.py:21
  102.7 2.1 %copy-start.9 = (f32[2,256,2048]{2,1,0:T(8,128)}, f32[2,256,2048]{2,1,0:T(8,128)S(1)}, u32[]{:S(2)}) copy-start(f32[2,256,2048]{2,1,0:T(8,128)S(1)} %shard_map.49.refs_1_.refs_3_.refs_2_) | copy-start | bytes 12582916
  105.5 10.1 %collective-permute-start.11 = (bf16[896,128]{1,0:T(8,128)(2,1)}, bf16[896,128]{1,0:T(8,128)(2,1)S(1)}, u32[]{:S(2)}, u32[]{:S(2)}) collective-permute-start(bf16[896,128]{1,0:T(8,128)(2,1)} %shard_map.50.refs_0_), channel_id=1, source_target_pairs={{0,2},{2,0},{1,3},{3,1},{4,6},{6,4},{5,7},{7,5},{8,10},{10,8},{9,1... | collective-permute-start | bytes 688136 | tf_op jit(solution)/shard_map/ppermute | solution.py:21
  106.1 2.0 %copy-start.2 = (f32[2,1792,256]{2,1,0:T(8,128)S(1)}, f32[2,1792,256]{2,1,0:T(8,128)}, u32[]{:S(2)}) copy-start(f32[2,1792,256]{2,1,0:T(8,128)} %copy-done) | copy-start | bytes 11010052
  108.2 2.2 %copy-start.10 = (f32[2,256,2048]{2,1,0:T(8,128)S(1)}, f32[2,256,2048]{2,1,0:T(8,128)}, u32[]{:S(2)}) copy-start(f32[2,256,2048]{2,1,0:T(8,128)} %copy-done.9) | copy-start | bytes 12582916
  110.3 2.3 %copy-start.11 = (f32[2,256,2048]{2,1,0:T(8,128)S(1)}, f32[2,256,2048]{2,1,0:T(8,128)}, u32[]{:S(2)}) copy-start(f32[2,256,2048]{2,1,0:T(8,128)} %copy-done.9) | copy-start | bytes 12582916
  112.2 2.2 %copy-start.4 = (f32[2,1792,256]{2,1,0:T(8,128)S(1)}, f32[2,1792,256]{2,1,0:T(8,128)}, u32[]{:S(2)}) copy-start(f32[2,1792,256]{2,1,0:T(8,128)} %copy-done.3) | copy-start | bytes 11010052
  112.2 3.4 %copy-start.23 = (bf16[896,128]{1,0:T(8,128)(2,1)S(1)}, bf16[896,128]{1,0:T(8,128)(2,1)}, u32[]{:S(2)}) copy-start(bf16[896,128]{1,0:T(8,128)(2,1)} %shard_map.50.refs_0_) | copy-start | bytes 688132
  (9 other events, 12.2 us)

commit v5 on v4

--- a/solution.py
+++ b/solution.py
@@ -9,16 +9,18 @@
 from jax.sharding import PartitionSpec as P
 
 
-MATMUL_FLOPS = 5_000_000_000
-
-
-def trade(block, steps):
+MATMUL_FLOPS = 500_000_000
+LATE_FLOPS = 20_000_000_000
+
+
+def trade(block, steps, backwards=False):
     axes = tuple(steps)
     sizes = [lax.axis_size(axis) for axis in axes]
     mask = 0
     for axis, size in zip(axes, sizes):
         mask = mask * size + steps[axis]
-    return lax.ppermute(block, axes, [(i, i ^ mask) for i in range(math.prod(sizes))])
+    route = [(i, i ^ mask) for i in range(math.prod(sizes))]
+    return lax.ppermute(block, axes, route[::-1] if backwards else route)
 
 
 def pass_on(block, step, count):
@@ -30,7 +32,7 @@
 ANYWHERE = pl.BlockSpec(memory_space=pl.ANY)
 
 
-def call(kernel, grid, where, inputs, shape, out_spec, scratch, flops, tokens):
+def call(kernel, grid, where, inputs, shape, out_spec, scratch, flops, tokens, vmem=36):
     arrays = [array for array, _ in inputs]
     skip = len(tokens)
 
@@ -47,7 +49,7 @@
             scratch_shapes=scratch,
         ),
         out_shape=shape,
-        compiler_params=pltpu.CompilerParams(vmem_limit_bytes=36 * 1024 * 1024),
+        compiler_params=pltpu.CompilerParams(vmem_limit_bytes=vmem * 1024 * 1024),
         cost_estimate=pl.CostEstimate(flops=flops, bytes_accessed=1024, transcendentals=0),
     )(jnp.stack([jnp.asarray(w, jnp.int32) for w in where]), *arrays, *tokens)
 
@@ -64,20 +66,25 @@
     )(*blocks, *tokens)
 
 
-def cut_kernel(turn, where, block_ref, out_ref):
-    block = block_ref[...]
-    out_ref[...] = block.astype(jnp.float32).T.astype(block.dtype) if turn else block
-
-
-def cut(out_grads, shape, at, turn, tokens=()):
-    out = shape[::-1] if turn else shape
-    if shape[0] % 128 or shape[1] % 128:
-        block = lax.dynamic_slice(out_grads, [i * size for i, size in zip(at, shape)], shape)
-        return block.T if turn else block
-    return call(
-        functools.partial(cut_kernel, turn), (1,), at,
-        [(out_grads, pl.BlockSpec(shape, lambda i, where: (where[0], where[1])))],
-        jax.ShapeDtypeStruct(out, out_grads.dtype), pl.BlockSpec(out, lambda i, where: (0, 0)), [], 1024, tokens,
+def turn_kernel(pieces, where, *refs):
+    blocks, outs = refs[: len(pieces)], list(refs[len(pieces) :])
+    for block, number in zip(blocks, pieces):
+        turned = block[...].astype(jnp.float32).T.astype(block.dtype)
+        size = turned.shape[0] // number
+        for p in range(number):
+            outs.pop(0)[...] = turned[p * size : (p + 1) * size]
+
+
+def turned(blocks, pieces, tokens=()):
+    rows, width = blocks[0].shape
+    if rows % 128 or width % 128:
+        return [piece for block, number in zip(blocks, pieces) for piece in jnp.split(block.T, number)]
+    sizes = [width // number for number in pieces for _ in range(number)]
+    return call(
+        functools.partial(turn_kernel, pieces), (1,), [jnp.zeros((), jnp.int32)],
+        [(block, pl.BlockSpec(block.shape, lambda i, where: (0, 0))) for block in blocks],
+        [jax.ShapeDtypeStruct((size, rows), blocks[0].dtype) for size in sizes],
+        [pl.BlockSpec((size, rows), lambda i, where: (0, 0)) for size in sizes], [], 1024, tokens,
     )
 
 
@@ -152,36 +159,13 @@
         out_ref[q : q + 1, :] = jnp.sum(grads * mix_ref[q], axis=0, keepdims=True)
 
 
-def scores_of_grads(parts, column, mix, piece, pieces, tokens=()):
+def scores_of_grads(parts, column, mix, piece, pieces, tokens=(), flops=1024):
     nq, depth, count = mix.shape
     inputs = [(part, pl.BlockSpec(part.shape, lambda i, where: (0, 0))) for part in parts]
     inputs.append((mix, pl.BlockSpec((nq, depth // pieces, count), lambda i, where: (0, piece, 0))))
     return call(
         score_kernel, (1,), [column], inputs, jax.ShapeDtypeStruct((nq, count), jnp.float32),
-        pl.BlockSpec((nq, count), lambda i, where: (0, 0)), [], 1024, tokens,
-    )
-
-
-def deliver_kernel(number, copies, where, *refs):
-    (*parts, mix_ref), terms, out_ref = refs[: -number - 2], refs[-number - 2 : -1], refs[-1]
-    grads = joined(parts, where, 1).astype(jnp.float32)
-    last = [jnp.sum(grads * mix_ref[q], axis=0, keepdims=True) for q in range(mix_ref.shape[0])]
-    last = jnp.concatenate(last, axis=0) + terms[0][...]
-    for k in range(number + 1):
-        value = last if k == 0 else terms[k][...]
-        for c in range(copies):
-            out_ref[where[1 + k] * copies + c] = value
-
-
-def delivered(parts, column, mix, piece, pieces, terms, targets, copies):
-    nq, depth, count = mix.shape
-    inputs = [(part, pl.BlockSpec(part.shape, lambda i, where: (0, 0))) for part in parts]
-    inputs.append((mix, pl.BlockSpec((nq, depth // pieces, count), lambda i, where: (0, piece, 0))))
-    inputs += [(term, pl.BlockSpec(term.shape, lambda i, where: (0, 0))) for term in terms]
-    shape = (len(terms) * copies, nq, count)
-    return call(
-        functools.partial(deliver_kernel, len(terms) - 1, copies), (1,), [column] + list(targets), inputs,
-        jax.ShapeDtypeStruct(shape, jnp.float32), pl.BlockSpec(shape, lambda i, where: (0, 0, 0)), [], 1024, (),
+        pl.BlockSpec((nq, count), lambda i, where: (0, 0)), [], flops, tokens,
     )
 
 
@@ -237,64 +221,64 @@
     me, column, core = lax.axis_index("dp"), lax.axis_index("din"), lax.axis_index("dout")
     tokens, rows = activations.shape[0], queries.shape[2]
     part, half = tokens // spread, tokens // 2
-    pieces = 2
-
-    def grads_for(d, turn, piece=0, pieces=1, tokens=()):
-        size = rows // pieces
-        return cut(out_grads, (part, size), (column, (me ^ d) * pieces + piece), turn, tokens)
+    pieces = 1
 
     def to_columns(arrived):
         return [arrived] + [trade(arrived, {"din": r}) for r in range(1, spread)]
 
-    def acts_of(d, tokens=()):
-        block = from_partner(hops, me, d, count, tokens)
+    def acts_of(block):
         return block, trade(block, {"dout": 1})
 
-    far, late = count - 1, count // 2
+    far, late = count - 1, count - 2
     early = [d for d in range(1, count) if d not in (far, late)]
 
     mine = lax.dynamic_slice_in_dim(activations, core * half, half, 0)
     hops = [(mine, mine)]
     hops.append(pass_on(hops[0], 1, count))
 
-    sent = {far: grads_for(far, False)}
+    def grads_for(device, first, size):
+        return lax.dynamic_slice(out_grads, (first, device * rows), (size, rows))
+
+    arrived = {far: trade(grads_for(me ^ far, column * part, part), {"dp": far})}
+    others = early + [late]
+    sent = turned([grads_for(me ^ d, column * part, part) for d in others], [1] * len(early) + [pieces])
+    for d, block in zip(early, sent):
+        arrived[d] = trade(block, {"dp": d})
+    for step in range(2, count - 1):
+        hops.append(pass_on(hops[-1], step, count))
+
+    zero = jnp.zeros((), jnp.int32)
+    token = own_mix = mixed((activations, 0), (activations, 1), zero, queries, list(sent) + list(hops[1]))
+    tail = [trade(hold([block], [own_mix])[0], {"dp": late}) for block in sent[len(early) :]]
+    own, = turned([grads_for(me, 0, tokens)], [1])
+    scores = scores_of_grads([own], zero, own_mix, 0, 1)
+
+    mixes = {}
+    for d in others:
+        block = from_partner(hops, me, d, count, [token] + [arrived[e] for e in early] if d == late else [])
+        if d == late:
+            end = lax.ppermute(block, "dp", [(1, 0), (count - 2, count - 1)])
+            hops.append((end, end))
+        mixes[d] = token = mixed(*acts_of(block), core, queries, [token])
+    proj = projected(to_columns(arrived[far]), column, queries, [token, scores])
+
+    token = proj
     for d in early:
-        sent[d] = grads_for(d, True)
-    arrived = {d: trade(block, {"dp": d}) for d, block in sent.items()}
-
-    zero = jnp.zeros((), jnp.int32)
-    own_mix = mixed((activations, 0), (activations, 1), zero, queries, list(sent.values()))
-    own = cut(out_grads, (tokens, rows), (zero, me), True)
-    scores = {0: scores_of_grads([own], zero, own_mix, 0, 1)}
-
-    mixes, token = {}, own_mix
-    tail = []
-    for step in range(1, count):
-        if step > 1:
-            hops.append(pass_on(hops[-1], step, count))
-        if step == late:
-            hops[step] = hold(hops[step], list(arrived.values()) + [token])
-        if step in early:
-            mixes[step] = token = mixed(*acts_of(step), core, queries, [token])
-        if step <= pieces:
-            waits = [token] if step == 1 else list(hops[step])
-            tail.append(trade(grads_for(late, True, step - 1, pieces, waits), {"dp": late}))
-    mixes[late] = token = mixed(*acts_of(late), core, queries, [token])
-    proj = projected(to_columns(arrived[far]), column, queries, [token, tail[0], scores[0]])
-
-    for d in early:
-        scores[d] = scores_of_grads(to_columns(arrived[d]), column, mixes[d], 0, 1, [proj])
-    scores[far] = scores_of_acts(*acts_of(far, [mixes[late]]), core, proj, [scores[d] for d in early])
-    for piece, block in enumerate(tail[:-1]):
-        term = scores_of_grads(to_columns(block), column, mixes[late], piece, pieces, [scores[far]])
-        scores[late] = scores[late] + term if piece else term
-    order = [late] + [d for d in range(count) if d != late]
-    last, = hold(tail[-1:], [proj])
-    blocks = delivered(
-        to_columns(last), column, mixes[late], pieces - 1, pieces,
-        [scores[d] for d in order], [me ^ d for d in order], spread * lax.axis_size("dout"),
-    )
-    return jnp.sum(lax.all_to_all(blocks, ("dp", "din", "dout"), 0, 0), axis=0)
+        token = scores_of_grads(to_columns(arrived[d]), column, mixes[d], 0, 1, [token])
+        scores = scores + trade(token, {"dp": d})
+    total = None
+    for piece, block in enumerate(tail):
+        block = hold([block], [proj])[0]
+        term = scores_of_grads(
+            to_columns(block), column, mixes[late], piece, pieces, [token], LATE_FLOPS
+        )
+        total = term if total is None else total + term
+    block = from_partner(hops, me, far, count, [mixes[late]])
+    term = scores_of_acts(*acts_of(block), core, proj)
+    scores = scores + trade(term, {"dp": far})
+    total = scores + trade(total, {"dp": late})
+    total = total + trade(total, {"dout": 1})
+    return total + sum(trade(total, {"din": r}) for r in range(1, spread))
 
 
 def solution(mesh):

time: 130 us -> 116 us (0.89)
  local copies, waits for them, and re-layouts: 27.5 us -> 14 us
  blocking collectives: 11.6 us -> 0 us
  starting transfers between devices: 25.5 us -> 34.4 us
  waiting for transfers between devices: 20.4 us -> 26.2 us
  Pallas kernels: 42.5 us -> 40.6 us
    unnamed x48 -> x28, local copies, waits for them, and re-layouts: 26.3 us -> 9.23 us
    ppermute x11 -> x15, waiting for transfers between devices: 2.23 us -> 15.1 us  [the longest x14 14.5 us: trade(): return lax.ppermute(block, axes, route[::-1] if backwards else route)]
    all_to_all x1 -> x0, blocking collectives: 11.6 us -> none  [on_device(): return jnp.sum(lax.all_to_all(blocks, ('dp', 'din', 'dout'), 0, 0), axis=0)]
    ppermute x11 -> x15, starting transfers between devices: 13.9 us -> 24.7 us  [the longest x14 23.4 us: trade(): return lax.ppermute(block, axes, route[::-1] if backwards else route)]
    ppermute x3 -> x2, waiting for transfers between devices: 17 us -> 9.91 us  [pass_on(): lax.ppermute(block[1], 'dp', [(i, i - 1) for i in range(1, count - step +...]
    dynamic_slice x0 -> x2, local copies, waits for them, and re-layouts: none -> 3.56 us  [grads_for(): return lax.dynamic_slice(out_grads, (first, device * rows), (size, rows))]
    pallas_call x17 -> x13, Pallas kernels: 42.5 us -> 40.6 us  [call(): pl.pallas_call(body, grid_spec=pltpu.PrefetchScalarGridSpec(num_scalar_pr...]
    ppermute x3 -> x2, starting transfers between devices: 3.85 us -> 2.58 us  [pass_on(): lax.ppermute(block[1], 'dp', [(i, i - 1) for i in range(1, count - step +...]
  transfers between devices with their start and end apart: 17 -> 19, of which waited for: 4 -> 8; matrix products, arithmetic and copies ran while one was open for 0% -> 3% of each run, Pallas kernels for 32% -> 35%
where the time goes in v5:
time: 116 us
  Pallas kernels  40.6 us (35%)
  starting transfers between devices  34.4 us (30%)
  waiting for transfers between devices  26.2 us (23%)
  local copies, waits for them, and re-layouts  14 us (12%)
    pallas_call x13, Pallas kernels, call(): pl.pallas_call(body, grid_spec=pltpu.PrefetchScalarGridSpec(num_scalar_pr...  40.6 us
    ppermute x14, starting transfers between devices, trade(): return lax.ppermute(block, axes, route[::-1] if backwards else route)  23.4 us
    ppermute x14, waiting for transfers between devices, trade(): return lax.ppermute(block, axes, route[::-1] if backwards else route)  14.5 us
    ppermute x2, waiting for transfers between devices, pass_on(): lax.ppermute(block[1], 'dp', [(i, i - 1) for i in range(1, count - step +...  9.91 us
    unnamed x28, local copies, waits for them, and re-layouts  9.23 us
    ppermute x2, starting transfers between devices, pass_on(): lax.ppermute(block[0], 'dp', [(i, i + 1) for i in range(step - 1, count -...  7.08 us
    dynamic_slice x2, local copies, waits for them, and re-layouts, grads_for(): return lax.dynamic_slice(out_grads, (first, device * rows), (size, rows))  3.56 us
    ppermute x2, starting transfers between devices, pass_on(): lax.ppermute(block[1], 'dp', [(i, i - 1) for i in range(1, count - step +...  2.58 us
  transfers between devices with their start and end apart: 19, of which 8 were waited for; matrix products, arithmetic and copies ran while one was open for 3% of the time, Pallas kernels for 35%

profile of v5, /device:TPU:0, one launch (start us, length us, event | category | flops | bytes accessed | tf_op | source)
XLA Modules:
  0.0 116.0 jit_solution(18039515971457880012)
XLA Ops:
  0.0 1.2 %constant_dynamic-slice_fusion = bf16[128,2048]{1,0:T(8,128)(2,1)S(1)} fusion(bf16[256,2048]{1,0:T(8,128)(2,1)} %refs_1_.1, s32[]{:T(128)S(6)} %select_n.52), kind=kLoop, calls=%fused_computation.1 | loop fusion | bytes 1048580 | tf_op jit(solution)/shard_map/dynamic_slice | solution.py:235
  1.2 1.3 %collective-permute-start.1 = (bf16[128,2048]{1,0:T(8,128)(2,1)S(1)}, bf16[128,2048]{1,0:T(8,128)(2,1)S(1)}, u32[]{:S(2)}, u32[]{:S(2)}) collective-permute-start(bf16[128,2048]{1,0:T(8,128)(2,1)S(1)} %constant_dynamic-slice_fusion), channel_id=1, source_target_pairs={{4,0},{8,4},{12,8},{5,1},{9,5},{13,9},{6,2},{10,6},{14,10},{7,3},{... | collective-permute-start | bytes 1572872 | tf_op jit(solution)/shard_map/ppermute | solution.py:28
  2.5 5.6 %collective-permute-start = (bf16[128,2048]{1,0:T(8,128)(2,1)S(1)}, bf16[128,2048]{1,0:T(8,128)(2,1)S(1)}, u32[]{:S(2)}, u32[]{:S(2)}) collective-permute-start(bf16[128,2048]{1,0:T(8,128)(2,1)S(1)} %constant_dynamic-slice_fusion), channel_id=1, source_target_pairs={{0,4},{4,8},{8,12},{1,5},{5,9},{9,13},{2,6},{6,10},{10,14},{3,7},{... | collective-permute-start | bytes 1572872 | tf_op jit(solution)/shard_map/ppermute | solution.py:27
  8.1 9.9 %collective-permute-done.1.refs_6_.refs_0_.refs_1_ = bf16[128,2048]{1,0:T(8,128)(2,1)S(1)} collective-permute-done((bf16[128,2048]{1,0:T(8,128)(2,1)S(1)}, bf16[128,2048]{1,0:T(8,128)(2,1)S(1)}, u32[]{:S(2)}, u32[]{:S(2)}) %collective-permute-start.1) | collective-permute-done | bytes 524320 | tf_op jit(solution)/shard_map/ppermute | solution.py:28
  18.0 1.2 %collective-permute-done.refs_5_.refs_1_.refs_2_ = bf16[128,2048]{1,0:T(8,128)(2,1)S(1)} collective-permute-done((bf16[128,2048]{1,0:T(8,128)(2,1)S(1)}, bf16[128,2048]{1,0:T(8,128)(2,1)S(1)}, u32[]{:S(2)}, u32[]{:S(2)}) %collective-permute-start) | collective-permute-done | bytes 524320 | tf_op jit(solution)/shard_map/ppermute | solution.py:27
  19.3 1.3 %collective-permute-start.7 = (bf16[128,2048]{1,0:T(8,128)(2,1)S(1)}, bf16[128,2048]{1,0:T(8,128)(2,1)}, u32[]{:S(2)}, u32[]{:S(2)}) collective-permute-start(bf16[128,2048]{1,0:T(8,128)(2,1)S(1)} %collective-permute-done.1.refs_6_.refs_0_.refs_1_), channel_id=1, source_target_pairs={{4,0},{8,4},{5,1},{9,5},{6,2},{10,6},{7,3},{11,7},{20,16},{24,20},... | collective-permute-start | bytes 1572872 | tf_op jit(solution)/shard_map/ppermute | solution.py:28
  20.6 1.5 %collective-permute-start.8 = (bf16[128,2048]{1,0:T(8,128)(2,1)S(1)}, bf16[128,2048]{1,0:T(8,128)(2,1)}, u32[]{:S(2)}, u32[]{:S(2)}) collective-permute-start(bf16[128,2048]{1,0:T(8,128)(2,1)S(1)} %collective-permute-done.refs_5_.refs_1_.refs_2_), channel_id=1, source_target_pairs={{4,8},{8,12},{5,9},{9,13},{6,10},{10,14},{7,11},{11,15},{20,24},{2... | collective-permute-start | bytes 1572872 | tf_op jit(solution)/shard_map/ppermute | solution.py:27
  22.1 2.2 %fusion = (bf16[128,1792]{1,0:T(8,128)(2,1)}, bf16[128,1792]{1,0:T(8,128)(2,1)S(1)}, bf16[128,1792]{1,0:T(8,128)(2,1)S(1)}) fusion(bf16[256,7168]{1,0:T(8,128)(2,1)} %param.4, s32[]{:T(128)S(6)} %select_n.49, s32[]{:T(128)S(6)} %select_n.56, s32[]{:T(128)S(6)} %select_n.50, s32[]{:T(128)S(6)} %select_n.51), kind=kLoop, calls=%fused_computation.3 | loop fusion | bytes 2752528 | tf_op jit(solution)/shard_map/dynamic_slice | solution.py:240
  25.3 7.1 %collective-permute-start.2 = (bf16[1792,128]{1,0:T(8,128)(2,1)}, bf16[1792,128]{1,0:T(8,128)(2,1)S(1)}, u32[]{:S(2)}, u32[]{:S(2)}) collective-permute-start(bf16[1792,128]{1,0:T(8,128)(2,1)} %get-tuple-element.7.refs_3_), channel_id=1, source_target_pairs={{0,4},{4,0},{8,12},{12,8},{1,5},{5,1},{9,13},{13,9},{2,6},{6,2},{1... | collective-permute-start | bytes 1376264 | tf_op jit(solution)/shard_map/ppermute | solution.py:23
  32.6 7.9 %shard_map.39.refs_1_.refs_3_ = f32[2,1792,256]{2,1,0:T(8,128)S(1)} custom-call(s32[1]{0:T(128)} %constant.5.clone.1.where, bf16[256,2048]{1,0:T(8,128)(2,1)S(1)} %copy-done.10, bf16[256,2048]{1,0:T(8,128)(2,1)S(1)} %copy-done.10, bf16[2,1,1792,2048]{3,2,1,0:T(8,128)(2,1)} %refs_2_.7, bf16[1792,128]{1,0:T(8,128)(2,1)} %get-tuple-element.7.refs_3_, ...), custom_call_target="tpu_custom_call" | custom-call | flops 500000000 | bytes 1024 | tf_op jit(solution)/shard_map/pallas_call | solution.py:42
  40.5 9.3 %shard_map.42.refs_2_.refs_3_ = f32[2,1792,256]{2,1,0:T(8,128)S(1)} custom-call(s32[1]{0:T(128)} %bitcast.1.where, bf16[128,2048]{1,0:T(8,128)(2,1)S(1)} %shard_map.41.refs_0_, bf16[128,2048]{1,0:T(8,128)(2,1)} %collective-permute-done.4.refs_1_, bf16[2,1,1792,2048]{3,2,1,0:T(8,128)(2,1)} %refs_2_.7, f32[2,1792,256]{2,1,0:T(8,128)S(1)} %shard_map.39.refs_1_.refs_3_), custom_call_target="tpu_custom_call" | custom-call | flops 500000000 | bytes 1024 | tf_op jit(solution)/shard_map/pallas_call | solution.py:42
  49.8 6.1 %collective-permute-done.2.refs_3_.refs_0_ = bf16[1792,128]{1,0:T(8,128)(2,1)S(1)} collective-permute-done((bf16[1792,128]{1,0:T(8,128)(2,1)}, bf16[1792,128]{1,0:T(8,128)(2,1)S(1)}, u32[]{:S(2)}, u32[]{:S(2)}) %collective-permute-start.2) | collective-permute-done | bytes 458784 | tf_op jit(solution)/shard_map/ppermute | solution.py:23
  55.9 1.2 %shard_map.43.refs_0_ = bf16[128,2048]{1,0:T(8,128)(2,1)S(1)} custom-call(s32[1]{0:T(128)} %bitcast.3.where, bf16[128,2048]{1,0:T(8,128)(2,1)} %collective-permute-done.7.refs_0_, bf16[128,2048]{1,0:T(8,128)(2,1)} %collective-permute-done.8.refs_1_, f32[2,1792,256]{2,1,0:T(8,128)S(1)} %shard_map.42.refs_2_.refs_3_, ...), custom_call_target="tpu_custom_call" | custom-call | flops 1024 | bytes 1024 | tf_op jit(solution)/shard_map/pallas_call | solution.py:42
  57.2 1.8 %copy-done.2 = f32[2,1792,256]{2,1,0:T(8,128)} copy-done((f32[2,1792,256]{2,1,0:T(8,128)}, f32[2,1792,256]{2,1,0:T(8,128)S(1)}, u32[]{:S(2)}) %copy-start.2) | copy-done | bytes 3670040
  59.0 1.6 %collective-permute-start.6 = (bf16[128,1792]{1,0:T(8,128)(2,1)}, bf16[128,1792]{1,0:T(8,128)(2,1)}, u32[]{:S(2)}, u32[]{:S(2)}) collective-permute-start(bf16[128,1792]{1,0:T(8,128)(2,1)} %collective-permute-done.5.refs_0_), channel_id=1, source_target_pairs={{0,2},{2,0},{1,3},{3,1},{4,6},{6,4},{5,7},{7,5},{8,10},{10,8},{9,1... | collective-permute-start | bytes 1376264 | tf_op jit(solution)/shard_map/ppermute | solution.py:23
  60.7 3.5 %collective-permute-start.14 = (bf16[1792,128]{1,0:T(8,128)(2,1)}, bf16[1792,128]{1,0:T(8,128)(2,1)S(1)}, u32[]{:S(2)}, u32[]{:S(2)}) collective-permute-start(bf16[1792,128]{1,0:T(8,128)(2,1)} %shard_map.49), channel_id=1, source_target_pairs={{0,8},{4,12},{8,0},{12,4},{1,9},{5,13},{9,1},{13,5},{2,10},{6,14},... | collective-permute-start | bytes 1376264 | tf_op jit(solution)/shard_map/ppermute | solution.py:23
  64.2 1.4 %constant_dynamic-slice_fusion.1.refs_0_ = bf16[256,1792]{1,0:T(8,128)(2,1)S(1)} fusion(bf16[256,7168]{1,0:T(8,128)(2,1)} %param.4, s32[]{:T(128)S(6)} %select_n.48), kind=kLoop, calls=%fused_computation.2 | loop fusion | bytes 1835012 | tf_op jit(solution)/shard_map/dynamic_slice | solution.py:240
  66.9 1.3 %collective-permute-start.11 = (bf16[128,2048]{1,0:T(8,128)(2,1)S(1)}, bf16[128,2048]{1,0:T(8,128)(2,1)S(1)}, u32[]{:S(2)}, u32[]{:S(2)}) collective-permute-start(bf16[128,2048]{1,0:T(8,128)(2,1)S(1)} %shard_map.43.refs_0_), channel_id=1, source_target_pairs={{4,0},{8,12},{5,1},{9,13},{6,2},{10,14},{7,3},{11,15},{20,16},{24,... | collective-permute-start | bytes 1572872 | tf_op jit(solution)/shard_map/ppermute | solution.py:260
  68.2 7.9 %shard_map.44.refs_3_.refs_4_.refs_2_ = f32[2,1792,256]{2,1,0:T(8,128)S(1)} custom-call(s32[1]{0:T(128)} %bitcast.1.where, bf16[128,2048]{1,0:T(8,128)(2,1)S(1)} %shard_map.43.refs_0_, bf16[128,2048]{1,0:T(8,128)(2,1)S(1)} %collective-permute-done.9.refs_1_, bf16[2,1,1792,2048]{3,2,1,0:T(8,128)(2,1)} %refs_2_.7, f32[2,1792,256]{2,1,0:T(8,128)S(1)} %copy-done.3), custom_call_target="tpu_custom_call" | custom-call | flops 500000000 | bytes 1024 | tf_op jit(solution)/shard_map/pallas_call | solution.py:42
  76.1 9.5 %shard_map.45.refs_3_.refs_2_.refs_1_ = f32[2,256,2048]{2,1,0:T(8,128)S(1)} custom-call(s32[1]{0:T(128)} %bitcast.where, bf16[128,1792]{1,0:T(8,128)(2,1)} %collective-permute-done.5.refs_0_, bf16[128,1792]{1,0:T(8,128)(2,1)} %collective-permute-done.6.refs_1_, bf16[2,1,1792,2048]{3,2,1,0:T(8,128)(2,1)} %refs_2_.7, ...), custom_call_target="tpu_custom_call" | custom-call | flops 500000000 | bytes 1024 | tf_op jit(solution)/shard_map/pallas_call | solution.py:42
  85.7 1.9 %copy-done = f32[2,256,2048]{2,1,0:T(8,128)} copy-done((f32[2,256,2048]{2,1,0:T(8,128)}, f32[2,256,2048]{2,1,0:T(8,128)S(1)}, u32[]{:S(2)}) %copy-start) | copy-done | bytes 4194328
  88.4 1.5 %collective-permute-start.15 = (bf16[1792,128]{1,0:T(8,128)(2,1)}, bf16[1792,128]{1,0:T(8,128)(2,1)S(1)}, u32[]{:S(2)}, u32[]{:S(2)}) collective-permute-start(bf16[1792,128]{1,0:T(8,128)(2,1)} %shard_map.50.refs_0_), channel_id=1, source_target_pairs={{0,2},{2,0},{1,3},{3,1},{4,6},{6,4},{5,7},{7,5},{8,10},{10,8},{9,1... | collective-permute-start | bytes 1376264 | tf_op jit(solution)/shard_map/ppermute | solution.py:23
  90.5 2.3 %copy-done.8 = f32[2,1792,256]{2,1,0:T(8,128)S(1)} copy-done((f32[2,1792,256]{2,1,0:T(8,128)S(1)}, f32[2,1792,256]{2,1,0:T(8,128)}, u32[]{:S(2)}) %copy-start.8) | copy-done | bytes 3670040
  93.2 2.0 %copy-done.4 = f32[2,1792,256]{2,1,0:T(8,128)S(1)} copy-done((f32[2,1792,256]{2,1,0:T(8,128)S(1)}, f32[2,1792,256]{2,1,0:T(8,128)}, u32[]{:S(2)}) %copy-start.4) | copy-done | bytes 3670040
  95.2 1.8 %shard_map.46.refs_3_ = f32[2,256]{1,0:T(2,128)S(1)} custom-call(s32[1]{0:T(128)} %bitcast.where, bf16[1792,128]{1,0:T(8,128)(2,1)S(1)} %collective-permute-done.2.refs_3_.refs_0_, bf16[1792,128]{1,0:T(8,128)(2,1)} %collective-permute-done.3.refs_1_, f32[2,1792,256]{2,1,0:T(8,128)S(1)} %copy-done.4, f32[2,256,2048]{2,1,0:T(8,128)S(1)} %copy-done.1), custom_call_target="tpu_custom_call" | custom-call | flops 1024 | bytes 1024 | tf_op jit(solution)/shard_map/pallas_call | solution.py:42
  97.1 2.7 %collective-permute-start.10 = (f32[2,256]{1,0:T(2,128)S(1)}, f32[2,256]{1,0:T(2,128)S(1)}, u32[]{:S(2)}, u32[]{:S(2)}) collective-permute-start(f32[2,256]{1,0:T(2,128)S(1)} %shard_map.46.refs_3_), channel_id=1, source_target_pairs={{0,4},{4,0},{8,12},{12,8},{1,5},{5,1},{9,13},{13,9},{2,6},{6,2},{1... | collective-permute-start | bytes 6152 | tf_op jit(solution)/shard_map/ppermute | solution.py:23
  99.8 1.2 %collective-permute-done.15.refs_1_ = bf16[1792,128]{1,0:T(8,128)(2,1)S(1)} collective-permute-done((bf16[1792,128]{1,0:T(8,128)(2,1)}, bf16[1792,128]{1,0:T(8,128)(2,1)S(1)}, u32[]{:S(2)}, u32[]{:S(2)}) %collective-permute-start.15) | collective-permute-done | bytes 458784 | tf_op jit(solution)/shard_map/ppermute | solution.py:23
  101.7 3.1 %collective-permute-start.16 = (f32[2,256]{1,0:T(2,128)S(1)}, f32[2,256]{1,0:T(2,128)S(1)}, u32[]{:S(2)}, u32[]{:S(2)}) collective-permute-start(f32[2,256]{1,0:T(2,128)S(1)} %shard_map.51), channel_id=1, source_target_pairs={{0,8},{4,12},{8,0},{12,4},{1,9},{5,13},{9,1},{13,5},{2,10},{6,14},... | collective-permute-start | bytes 6152 | tf_op jit(solution)/shard_map/ppermute | solution.py:23
  105.2 1.8 %collective-permute-start.13 = (f32[2,256]{1,0:T(2,128)S(1)}, f32[2,256]{1,0:T(2,128)S(1)}, u32[]{:S(2)}, u32[]{:S(2)}) collective-permute-start(f32[2,256]{1,0:T(2,128)S(1)} %shard_map.48), channel_id=1, source_target_pairs={{0,12},{4,8},{8,4},{12,0},{1,13},{5,9},{9,5},{13,1},{2,14},{6,10},... | collective-permute-start | bytes 6152 | tf_op jit(solution)/shard_map/ppermute | solution.py:23
  107.1 3.6 %collective-permute-done.13 = f32[2,256]{1,0:T(2,128)S(1)} collective-permute-done((f32[2,256]{1,0:T(2,128)S(1)}, f32[2,256]{1,0:T(2,128)S(1)}, u32[]{:S(2)}, u32[]{:S(2)}) %collective-permute-start.13) | collective-permute-done | bytes 2080 | tf_op jit(solution)/shard_map/ppermute | solution.py:23
  111.9 1.2 %collective-permute-start.18 = (f32[2,256]{1,0:T(2,128)S(1)}, f32[2,256]{1,0:T(2,128)S(1)}, u32[]{:S(2)}, u32[]{:S(2)}) collective-permute-start(f32[2,256]{1,0:T(2,128)S(1)} %add.44), channel_id=1, source_target_pairs={{0,2},{2,0},{1,3},{3,1},{4,6},{6,4},{5,7},{7,5},{8,10},{10,8},{9,1... | collective-permute-start | bytes 6152 | tf_op jit(solution)/shard_map/ppermute | solution.py:23
  113.1 2.4 %collective-permute-done.18 = f32[2,256]{1,0:T(2,128)S(1)} collective-permute-done((f32[2,256]{1,0:T(2,128)S(1)}, f32[2,256]{1,0:T(2,128)S(1)}, u32[]{:S(2)}, u32[]{:S(2)}) %collective-permute-start.18) | collective-permute-done | bytes 2080 | tf_op jit(solution)/shard_map/ppermute | solution.py:23
  (55 shorter events, 7.3 us)
Async XLA Ops:
  0.0 32.6 %copy-start.10 = (bf16[256,2048]{1,0:T(8,128)(2,1)S(1)}, bf16[256,2048]{1,0:T(8,128)(2,1)}, u32[]{:S(2)}) copy-start(bf16[256,2048]{1,0:T(8,128)(2,1)} %refs_1_.1) | copy-start | bytes 3145732
  1.2 16.8 %collective-permute-start.1 = (bf16[128,2048]{1,0:T(8,128)(2,1)S(1)}, bf16[128,2048]{1,0:T(8,128)(2,1)S(1)}, u32[]{:S(2)}, u32[]{:S(2)}) collective-permute-start(bf16[128,2048]{1,0:T(8,128)(2,1)S(1)} %constant_dynamic-slice_fusion), channel_id=1, source_target_pairs={{4,0},{8,4},{12,8},{5,1},{9,5},{13,9},{6,2},{10,6},{14,10},{7,3},{... | collective-permute-start | bytes 1572872 | tf_op jit(solution)/shard_map/ppermute | solution.py:28
  2.5 16.7 %collective-permute-start = (bf16[128,2048]{1,0:T(8,128)(2,1)S(1)}, bf16[128,2048]{1,0:T(8,128)(2,1)S(1)}, u32[]{:S(2)}, u32[]{:S(2)}) collective-permute-start(bf16[128,2048]{1,0:T(8,128)(2,1)S(1)} %constant_dynamic-slice_fusion), channel_id=1, source_target_pairs={{0,4},{4,8},{8,12},{1,5},{5,9},{9,13},{2,6},{6,10},{10,14},{3,7},{... | collective-permute-start | bytes 1572872 | tf_op jit(solution)/shard_map/ppermute | solution.py:27
  19.2 21.2 %collective-permute-start.4 = (bf16[128,2048]{1,0:T(8,128)(2,1)S(1)}, bf16[128,2048]{1,0:T(8,128)(2,1)}, u32[]{:S(2)}, u32[]{:S(2)}) collective-permute-start(bf16[128,2048]{1,0:T(8,128)(2,1)S(1)} %shard_map.41.refs_0_), channel_id=1, source_target_pairs={{0,1},{1,0},{2,3},{3,2},{4,5},{5,4},{6,7},{7,6},{8,9},{9,8},{10,11... | collective-permute-start | bytes 1572872 | tf_op jit(solution)/shard_map/ppermute | solution.py:23
  19.3 36.6 %collective-permute-start.7 = (bf16[128,2048]{1,0:T(8,128)(2,1)S(1)}, bf16[128,2048]{1,0:T(8,128)(2,1)}, u32[]{:S(2)}, u32[]{:S(2)}) collective-permute-start(bf16[128,2048]{1,0:T(8,128)(2,1)S(1)} %collective-permute-done.1.refs_6_.refs_0_.refs_1_), channel_id=1, source_target_pairs={{4,0},{8,4},{5,1},{9,5},{6,2},{10,6},{7,3},{11,7},{20,16},{24,20},... | collective-permute-start | bytes 1572872 | tf_op jit(solution)/shard_map/ppermute | solution.py:28
  20.6 35.3 %collective-permute-start.8 = (bf16[128,2048]{1,0:T(8,128)(2,1)S(1)}, bf16[128,2048]{1,0:T(8,128)(2,1)}, u32[]{:S(2)}, u32[]{:S(2)}) collective-permute-start(bf16[128,2048]{1,0:T(8,128)(2,1)S(1)} %collective-permute-done.refs_5_.refs_1_.refs_2_), channel_id=1, source_target_pairs={{4,8},{8,12},{5,9},{9,13},{6,10},{10,14},{7,11},{11,15},{20,24},{2... | collective-permute-start | bytes 1572872 | tf_op jit(solution)/shard_map/ppermute | solution.py:27
  25.3 15.2 %copy-start.11 = (bf16[1792,128]{1,0:T(8,128)(2,1)}, bf16[1792,128]{1,0:T(8,128)(2,1)S(1)}, u32[]{:S(2)}) copy-start(bf16[1792,128]{1,0:T(8,128)(2,1)S(1)} %get-tuple-element.8.refs_4_.refs_0_) | copy-start | bytes 1376260
  25.3 30.7 %collective-permute-start.2 = (bf16[1792,128]{1,0:T(8,128)(2,1)}, bf16[1792,128]{1,0:T(8,128)(2,1)S(1)}, u32[]{:S(2)}, u32[]{:S(2)}) collective-permute-start(bf16[1792,128]{1,0:T(8,128)(2,1)} %get-tuple-element.7.refs_3_), channel_id=1, source_target_pairs={{0,4},{4,0},{8,12},{12,8},{1,5},{5,1},{9,13},{13,9},{2,6},{6,2},{1... | collective-permute-start | bytes 1376264 | tf_op jit(solution)/shard_map/ppermute | solution.py:23
  32.4 26.6 %collective-permute-start.5 = (bf16[128,1792]{1,0:T(8,128)(2,1)}, bf16[128,1792]{1,0:T(8,128)(2,1)}, u32[]{:S(2)}, u32[]{:S(2)}) collective-permute-start(bf16[128,1792]{1,0:T(8,128)(2,1)} %get-tuple-element.9), channel_id=1, source_target_pairs={{0,12},{4,8},{8,4},{12,0},{1,13},{5,9},{9,5},{13,1},{2,14},{6,10},... | collective-permute-start | bytes 1376264 | tf_op jit(solution)/shard_map/ppermute | solution.py:23
  40.5 9.3 %copy-start.5 = (f32[2,1792,256]{2,1,0:T(8,128)}, f32[2,1792,256]{2,1,0:T(8,128)S(1)}, u32[]{:S(2)}) copy-start(f32[2,1792,256]{2,1,0:T(8,128)S(1)} %shard_map.39.refs_1_.refs_3_) | copy-start | bytes 11010052
  57.2 1.8 %copy-start.2 = (f32[2,1792,256]{2,1,0:T(8,128)}, f32[2,1792,256]{2,1,0:T(8,128)S(1)}, u32[]{:S(2)}) copy-start(f32[2,1792,256]{2,1,0:T(8,128)S(1)} %shard_map.42.refs_2_.refs_3_) | copy-start | bytes 11010052
  59.0 9.2 %collective-permute-start.9 = (bf16[128,2048]{1,0:T(8,128)(2,1)S(1)}, bf16[128,2048]{1,0:T(8,128)(2,1)S(1)}, u32[]{:S(2)}, u32[]{:S(2)}) collective-permute-start(bf16[128,2048]{1,0:T(8,128)(2,1)S(1)} %shard_map.43.refs_0_), channel_id=1, source_target_pairs={{0,1},{1,0},{2,3},{3,2},{4,5},{5,4},{6,7},{7,6},{8,9},{9,8},{10,11... | collective-permute-start | bytes 1572872 | tf_op jit(solution)/shard_map/ppermute | solution.py:23
  59.0 17.1 %collective-permute-start.6 = (bf16[128,1792]{1,0:T(8,128)(2,1)}, bf16[128,1792]{1,0:T(8,128)(2,1)}, u32[]{:S(2)}, u32[]{:S(2)}) collective-permute-start(bf16[128,1792]{1,0:T(8,128)(2,1)} %collective-permute-done.5.refs_0_), channel_id=1, source_target_pairs={{0,2},{2,0},{1,3},{3,1},{4,6},{6,4},{5,7},{7,5},{8,10},{10,8},{9,1... | collective-permute-start | bytes 1376264 | tf_op jit(solution)/shard_map/ppermute | solution.py:23
  60.7 26.9 %collective-permute-start.14 = (bf16[1792,128]{1,0:T(8,128)(2,1)}, bf16[1792,128]{1,0:T(8,128)(2,1)S(1)}, u32[]{:S(2)}, u32[]{:S(2)}) collective-permute-start(bf16[1792,128]{1,0:T(8,128)(2,1)} %shard_map.49), channel_id=1, source_target_pairs={{0,8},{4,12},{8,0},{12,4},{1,9},{5,13},{9,1},{13,5},{2,10},{6,14},... | collective-permute-start | bytes 1376264 | tf_op jit(solution)/shard_map/ppermute | solution.py:23
  64.2 2.3 %copy-start.6 = (f32[2,1792,256]{2,1,0:T(8,128)S(1)}, f32[2,1792,256]{2,1,0:T(8,128)}, u32[]{:S(2)}) copy-start(f32[2,1792,256]{2,1,0:T(8,128)} %copy-done.5) | copy-start | bytes 11010052
  65.6 2.7 %copy-start.3 = (f32[2,1792,256]{2,1,0:T(8,128)S(1)}, f32[2,1792,256]{2,1,0:T(8,128)}, u32[]{:S(2)}) copy-start(f32[2,1792,256]{2,1,0:T(8,128)} %copy-done.2) | copy-start | bytes 11010052
  65.9 27.1 %collective-permute-start.3 = (bf16[1792,128]{1,0:T(8,128)(2,1)S(1)}, bf16[1792,128]{1,0:T(8,128)(2,1)}, u32[]{:S(2)}, u32[]{:S(2)}) collective-permute-start(bf16[1792,128]{1,0:T(8,128)(2,1)S(1)} %collective-permute-done.2.refs_3_.refs_0_), channel_id=1, source_target_pairs={{0,2},{2,0},{1,3},{3,1},{4,6},{6,4},{5,7},{7,5},{8,10},{10,8},{9,1... | collective-permute-start | bytes 1376264 | tf_op jit(solution)/shard_map/ppermute | solution.py:23
  66.9 23.6 %collective-permute-start.11 = (bf16[128,2048]{1,0:T(8,128)(2,1)S(1)}, bf16[128,2048]{1,0:T(8,128)(2,1)S(1)}, u32[]{:S(2)}, u32[]{:S(2)}) collective-permute-start(bf16[128,2048]{1,0:T(8,128)(2,1)S(1)} %shard_map.43.refs_0_), channel_id=1, source_target_pairs={{4,0},{8,12},{5,1},{9,13},{6,2},{10,14},{7,3},{11,15},{20,16},{24,... | collective-permute-start | bytes 1572872 | tf_op jit(solution)/shard_map/ppermute | solution.py:260
  76.1 9.5 %copy-start.7 = (f32[2,1792,256]{2,1,0:T(8,128)}, f32[2,1792,256]{2,1,0:T(8,128)S(1)}, u32[]{:S(2)}) copy-start(f32[2,1792,256]{2,1,0:T(8,128)S(1)} %shard_map.44.refs_3_.refs_4_.refs_2_) | copy-start | bytes 11010052
  85.6 2.0 %copy-start = (f32[2,256,2048]{2,1,0:T(8,128)}, f32[2,256,2048]{2,1,0:T(8,128)S(1)}, u32[]{:S(2)}) copy-start(f32[2,256,2048]{2,1,0:T(8,128)S(1)} %shard_map.45.refs_3_.refs_2_.refs_1_) | copy-start | bytes 12582916
  88.4 12.6 %collective-permute-start.15 = (bf16[1792,128]{1,0:T(8,128)(2,1)}, bf16[1792,128]{1,0:T(8,128)(2,1)S(1)}, u32[]{:S(2)}, u32[]{:S(2)}) collective-permute-start(bf16[1792,128]{1,0:T(8,128)(2,1)} %shard_map.50.refs_0_), channel_id=1, source_target_pairs={{0,2},{2,0},{1,3},{3,1},{4,6},{6,4},{5,7},{7,5},{8,10},{10,8},{9,1... | collective-permute-start | bytes 1376264 | tf_op jit(solution)/shard_map/ppermute | solution.py:23
  89.9 3.3 %copy-start.1 = (f32[2,256,2048]{2,1,0:T(8,128)S(1)}, f32[2,256,2048]{2,1,0:T(8,128)}, u32[]{:S(2)}) copy-start(f32[2,256,2048]{2,1,0:T(8,128)} %copy-done) | copy-start | bytes 12582916
  90.5 2.3 %copy-start.8 = (f32[2,1792,256]{2,1,0:T(8,128)S(1)}, f32[2,1792,256]{2,1,0:T(8,128)}, u32[]{:S(2)}) copy-start(f32[2,1792,256]{2,1,0:T(8,128)} %copy-done.7) | copy-start | bytes 11010052
  92.9 8.1 %copy-start.13 = (bf16[1792,128]{1,0:T(8,128)(2,1)S(1)}, bf16[1792,128]{1,0:T(8,128)(2,1)}, u32[]{:S(2)}) copy-start(bf16[1792,128]{1,0:T(8,128)(2,1)} %shard_map.50.refs_0_) | copy-start | bytes 1376260
  92.9 11.9 %collective-permute-start.12 = (bf16[128,2048]{1,0:T(8,128)(2,1)S(1)}, bf16[128,2048]{1,0:T(8,128)(2,1)S(1)}, u32[]{:S(2)}, u32[]{:S(2)}) collective-permute-start(bf16[128,2048]{1,0:T(8,128)(2,1)S(1)} %shard_map.47.refs_0_), channel_id=1, source_target_pairs={{0,1},{1,0},{2,3},{3,2},{4,5},{5,4},{6,7},{7,6},{8,9},{9,8},{10,11... | collective-permute-start | bytes 1572872 | tf_op jit(solution)/shard_map/ppermute | solution.py:23
  93.2 2.0 %copy-start.4 = (f32[2,1792,256]{2,1,0:T(8,128)S(1)}, f32[2,1792,256]{2,1,0:T(8,128)}, u32[]{:S(2)}) copy-start(f32[2,1792,256]{2,1,0:T(8,128)} %copy-done.2) | copy-start | bytes 11010052
  95.2 5.8 %copy-start.9 = (f32[2,1792,256]{2,1,0:T(8,128)S(1)}, f32[2,1792,256]{2,1,0:T(8,128)}, u32[]{:S(2)}) copy-start(f32[2,1792,256]{2,1,0:T(8,128)} %copy-done.7) | copy-start | bytes 11010052
  97.1 10.0 %collective-permute-start.10 = (f32[2,256]{1,0:T(2,128)S(1)}, f32[2,256]{1,0:T(2,128)S(1)}, u32[]{:S(2)}, u32[]{:S(2)}) collective-permute-start(f32[2,256]{1,0:T(2,128)S(1)} %shard_map.46.refs_3_), channel_id=1, source_target_pairs={{0,4},{4,0},{8,12},{12,8},{1,5},{5,1},{9,13},{13,9},{2,6},{6,2},{1... | collective-permute-start | bytes 6152 | tf_op jit(solution)/shard_map/ppermute | solution.py:23
  101.7 5.4 %collective-permute-start.16 = (f32[2,256]{1,0:T(2,128)S(1)}, f32[2,256]{1,0:T(2,128)S(1)}, u32[]{:S(2)}, u32[]{:S(2)}) collective-permute-start(f32[2,256]{1,0:T(2,128)S(1)} %shard_map.51), channel_id=1, source_target_pairs={{0,8},{4,12},{8,0},{12,4},{1,9},{5,13},{9,1},{13,5},{2,10},{6,14},... | collective-permute-start | bytes 6152 | tf_op jit(solution)/shard_map/ppermute | solution.py:23
  105.2 5.4 %collective-permute-start.13 = (f32[2,256]{1,0:T(2,128)S(1)}, f32[2,256]{1,0:T(2,128)S(1)}, u32[]{:S(2)}, u32[]{:S(2)}) collective-permute-start(f32[2,256]{1,0:T(2,128)S(1)} %shard_map.48), channel_id=1, source_target_pairs={{0,12},{4,8},{8,4},{12,0},{1,13},{5,9},{9,5},{13,1},{2,14},{6,10},... | collective-permute-start | bytes 6152 | tf_op jit(solution)/shard_map/ppermute | solution.py:23
  110.7 1.2 collective-permute-start.17
  111.9 3.6 %collective-permute-start.18 = (f32[2,256]{1,0:T(2,128)S(1)}, f32[2,256]{1,0:T(2,128)S(1)}, u32[]{:S(2)}, u32[]{:S(2)}) collective-permute-start(f32[2,256]{1,0:T(2,128)S(1)} %add.44), channel_id=1, source_target_pairs={{0,2},{2,0},{1,3},{3,1},{4,6},{6,4},{5,7},{7,5},{8,10},{10,8},{9,1... | collective-permute-start | bytes 6152 | tf_op jit(solution)/shard_map/ppermute | solution.py:23
  (1 other events, 0.8 us)

commit v6 on v5

--- a/solution.py
+++ b/solution.py
@@ -9,8 +9,7 @@
 from jax.sharding import PartitionSpec as P
 
 
-MATMUL_FLOPS = 500_000_000
-LATE_FLOPS = 20_000_000_000
+LONG, SHORT = 40_000_000_000, 1_000_000
 
 
 def trade(block, steps, backwards=False):
@@ -137,7 +136,7 @@
     )
 
 
-def mixed(mine, other, core, queries, tokens=()):
+def mixed(mine, other, core, queries, flops, tokens=()):
     nq, _, depth, width = queries.shape
     pairs = [block if isinstance(block, tuple) else (block, 0) for block in (mine, other)]
     half = pairs[1][0].shape[0] // (2 if isinstance(other, tuple) else 1)
@@ -148,7 +147,7 @@
         mix_kernel, (nq, depth // tile), [core], inputs,
         jax.ShapeDtypeStruct((nq, depth, 2 * half), jnp.float32),
         pl.BlockSpec((1, tile, 2 * half), lambda q, o, where: (q, o, 0)),
-        [pltpu.VMEM((2 * half, width), queries.dtype)], MATMUL_FLOPS, tokens,
+        [pltpu.VMEM((2 * half, width), queries.dtype)], flops, tokens,
     )
 
 
@@ -179,7 +178,7 @@
     out_ref[0] = jnp.dot(grads[...], query_ref[0, 0], preferred_element_type=jnp.float32)
 
 
-def projected(parts, column, queries, tokens=()):
+def projected(parts, column, queries, flops, tokens=()):
     nq, _, depth, width = queries.shape
     count = sum(part.shape[0] for part in parts)
     tile = width // 2
@@ -189,7 +188,7 @@
         project_kernel, (nq, width // tile), [column], inputs,
         jax.ShapeDtypeStruct((nq, count, width), jnp.float32),
         pl.BlockSpec((1, count, tile), lambda q, i, where: (q, 0, i)),
-        [pltpu.VMEM((count, depth), queries.dtype)], MATMUL_FLOPS, tokens,
+        [pltpu.VMEM((count, depth), queries.dtype)], flops, tokens,
     )
 
 
@@ -244,41 +243,43 @@
     sent = turned([grads_for(me ^ d, column * part, part) for d in others], [1] * len(early) + [pieces])
     for d, block in zip(early, sent):
         arrived[d] = trade(block, {"dp": d})
+
+    zero = jnp.zeros((), jnp.int32)
+    token = own_mix = mixed((activations, 0), (activations, 1), zero, queries, LONG, list(sent))
+    own, = turned([grads_for(me, 0, tokens)], [1])
+    token = scores = scores_of_grads([own], zero, own_mix, 0, 1)
+    hops[1] = hold(list(hops[1]), [own_mix])
     for step in range(2, count - 1):
         hops.append(pass_on(hops[-1], step, count))
 
-    zero = jnp.zeros((), jnp.int32)
-    token = own_mix = mixed((activations, 0), (activations, 1), zero, queries, list(sent) + list(hops[1]))
-    tail = [trade(hold([block], [own_mix])[0], {"dp": late}) for block in sent[len(early) :]]
-    own, = turned([grads_for(me, 0, tokens)], [1])
-    scores = scores_of_grads([own], zero, own_mix, 0, 1)
-
     mixes = {}
     for d in others:
-        block = from_partner(hops, me, d, count, [token] + [arrived[e] for e in early] if d == late else [])
+        block = from_partner(hops, me, d, count, [token] + list(arrived.values()) if d == late else [])
         if d == late:
             end = lax.ppermute(block, "dp", [(1, 0), (count - 2, count - 1)])
             hops.append((end, end))
-        mixes[d] = token = mixed(*acts_of(block), core, queries, [token])
-    proj = projected(to_columns(arrived[far]), column, queries, [token, scores])
+        mixes[d] = mixed(*acts_of(block), core, queries, LONG if d == late else SHORT, [token])
+        token = mixes[d]
+    tail = [trade(hold([block], [mixes[early[-1]]])[0], {"dp": late}) for block in sent[len(early) :]]
+    tail = [hold([block], [token])[0] for block in tail]
+    proj = projected(to_columns(arrived[far]), column, queries, LONG, [token, scores] + tail)
 
     token = proj
     for d in early:
         token = scores_of_grads(to_columns(arrived[d]), column, mixes[d], 0, 1, [token])
         scores = scores + trade(token, {"dp": d})
-    total = None
+    token = scores_of_acts(*acts_of(from_partner(hops, me, far, count, [mixes[late]])), core, proj, [token])
+    scores = over_chips(scores + trade(token, {"dp": far}), spread)
     for piece, block in enumerate(tail):
-        block = hold([block], [proj])[0]
-        term = scores_of_grads(
-            to_columns(block), column, mixes[late], piece, pieces, [token], LATE_FLOPS
-        )
-        total = term if total is None else total + term
-    block = from_partner(hops, me, far, count, [mixes[late]])
-    term = scores_of_acts(*acts_of(block), core, proj)
-    scores = scores + trade(term, {"dp": far})
-    total = scores + trade(total, {"dp": late})
-    total = total + trade(total, {"dout": 1})
-    return total + sum(trade(total, {"din": r}) for r in range(1, spread))
+        term = scores_of_grads(to_columns(block), column, mixes[late], piece, pieces, [token])
+        term = term + trade(term, {"dout": 1})
+        scores = scores + sum(trade(term, {"dp": late, "din": r}) for r in range(spread))
+    return scores
+
+
+def over_chips(scores, spread):
+    scores = scores + trade(scores, {"dout": 1})
+    return scores + sum(trade(scores, {"din": r}) for r in range(1, spread))
 
 
 def solution(mesh):

time: 116 us -> 120 us (1.034)
  waiting for transfers between devices: 26.2 us -> 33.2 us
  starting transfers between devices: 34.4 us -> 30.7 us
  Pallas kernels: 40.6 us -> 37.6 us
  local copies, waits for them, and re-layouts: 14 us -> 16.6 us
    ppermute x14 -> x16, waiting for transfers between devices: 14.5 us -> 31.5 us  [trade(): return lax.ppermute(block, axes, route[::-1] if backwards else route)]
    ppermute x2, waiting for transfers between devices: 9.91 us -> 1.72 us  [pass_on(): lax.ppermute(block[1], 'dp', [(i, i - 1) for i in range(1, count - step +...]
    ppermute x14 -> x16, starting transfers between devices: 23.4 us -> 20.4 us  [trade(): return lax.ppermute(block, axes, route[::-1] if backwards else route)]
    pallas_call x13, Pallas kernels: 40.6 us -> 37.6 us  [call(): pl.pallas_call(body, grid_spec=pltpu.PrefetchScalarGridSpec(num_scalar_pr...]
    unnamed x28 -> x24, local copies, waits for them, and re-layouts: 9.23 us -> 11.8 us
  transfers between devices with their start and end apart: 19 -> 21, of which waited for: 8 -> 8; matrix products, arithmetic and copies ran while one was open for 3% -> 3% of each run, Pallas kernels for 35% -> 31%
where the time goes in v6:
time: 120 us; the launch traced here: 119 us
  Pallas kernels  37.6 us (31%)
  waiting for transfers between devices  33.2 us (28%)
  starting transfers between devices  30.7 us (26%)
  local copies, waits for them, and re-layouts  16.6 us (14%)
    pallas_call x13, Pallas kernels, call(): pl.pallas_call(body, grid_spec=pltpu.PrefetchScalarGridSpec(num_scalar_pr...  37.6 us
    ppermute x16, waiting for transfers between devices, trade(): return lax.ppermute(block, axes, route[::-1] if backwards else route)  31.5 us
    ppermute x16, starting transfers between devices, trade(): return lax.ppermute(block, axes, route[::-1] if backwards else route)  20.4 us
    unnamed x24, local copies, waits for them, and re-layouts  11.8 us
    ppermute x2, starting transfers between devices, pass_on(): lax.ppermute(block[0], 'dp', [(i, i + 1) for i in range(step - 1, count -...  6.47 us
    dynamic_slice x2, local copies, waits for them, and re-layouts, grads_for(): return lax.dynamic_slice(out_grads, (first, device * rows), (size, rows))  3.55 us
    ppermute x2, starting transfers between devices, pass_on(): lax.ppermute(block[1], 'dp', [(i, i - 1) for i in range(1, count - step +...  2.57 us
  transfers between devices with their start and end apart: 21, of which 8 were waited for; matrix products, arithmetic and copies ran while one was open for 3% of the time, Pallas kernels for 31%

profile of v6, /device:TPU:0, one launch (start us, length us, event | category | flops | bytes accessed | tf_op | source)
XLA Modules:
  0.0 119.0 jit_solution(4003965188435860146)
XLA Ops:
  0.0 1.2 constant_dynamic-slice_fusion
  1.2 5.8 %collective-permute-start.2 = (bf16[128,2048]{1,0:T(8,128)(2,1)S(1)}, bf16[128,2048]{1,0:T(8,128)(2,1)}, u32[]{:S(2)}, u32[]{:S(2)}) collective-permute-start(bf16[128,2048]{1,0:T(8,128)(2,1)S(1)} %constant_dynamic-slice_fusion), channel_id=1, source_target_pairs={{0,4},{4,8},{8,12},{1,5},{5,9},{9,13},{2,6},{6,10},{10,14},{3,7},{... | collective-permute-start | bytes 1572872 | tf_op jit(solution)/shard_map/ppermute | solution.py:26
  6.9 1.3 %collective-permute-start.3 = (bf16[128,2048]{1,0:T(8,128)(2,1)S(1)}, bf16[128,2048]{1,0:T(8,128)(2,1)}, u32[]{:S(2)}, u32[]{:S(2)}) collective-permute-start(bf16[128,2048]{1,0:T(8,128)(2,1)S(1)} %constant_dynamic-slice_fusion), channel_id=1, source_target_pairs={{4,0},{8,4},{12,8},{5,1},{9,5},{13,9},{6,2},{10,6},{14,10},{7,3},{... | collective-permute-start | bytes 1572872 | tf_op jit(solution)/shard_map/ppermute | solution.py:27
  8.3 2.2 %fusion = (bf16[128,1792]{1,0:T(8,128)(2,1)}, bf16[128,1792]{1,0:T(8,128)(2,1)S(1)}, bf16[128,1792]{1,0:T(8,128)(2,1)S(1)}) fusion(bf16[256,7168]{1,0:T(8,128)(2,1)} %param.4, s32[]{:T(128)S(6)} %select_n.49, s32[]{:T(128)S(6)} %select_n.56, s32[]{:T(128)S(6)} %select_n.50, s32[]{:T(128)S(6)} %select_n.51), kind=kLoop, calls=%fused_computation.4 | loop fusion | bytes 2752528 | tf_op jit(solution)/shard_map/dynamic_slice | solution.py:239
  10.8 8.0 %shard_map.39.refs_1_.refs_2_ = f32[2,1792,256]{2,1,0:T(8,128)S(1)} custom-call(s32[1]{0:T(128)} %constant.5.clone.1.where, bf16[256,2048]{1,0:T(8,128)(2,1)S(1)} %copy-done.11, bf16[256,2048]{1,0:T(8,128)(2,1)S(1)} %copy-done.11, bf16[2,1,1792,2048]{3,2,1,0:T(8,128)(2,1)} %refs_2_.7, bf16[1792,128]{1,0:T(8,128)(2,1)S(1)} %get-tuple-element.9.refs_3_, ...), custom_call_target="tpu_custom_call" | custom-call | flops 40000000000 | bytes 1024 | tf_op jit(solution)/shard_map/pallas_call | solution.py:41
  18.8 1.8 %copy-done.6 = f32[2,1792,256]{2,1,0:T(8,128)} copy-done((f32[2,1792,256]{2,1,0:T(8,128)}, f32[2,1792,256]{2,1,0:T(8,128)S(1)}, u32[]{:S(2)}) %copy-start.6) | copy-done | bytes 3670040
  20.6 1.7 %collective-permute-done.3.refs_1_ = bf16[128,2048]{1,0:T(8,128)(2,1)} collective-permute-done((bf16[128,2048]{1,0:T(8,128)(2,1)S(1)}, bf16[128,2048]{1,0:T(8,128)(2,1)}, u32[]{:S(2)}, u32[]{:S(2)}) %collective-permute-start.3) | collective-permute-done | bytes 524320 | tf_op jit(solution)/shard_map/ppermute | solution.py:27
  22.3 1.2 %shard_map.42.refs_0_ = bf16[128,2048]{1,0:T(8,128)(2,1)S(1)} custom-call(s32[1]{0:T(128)} %bitcast.2.where, bf16[128,2048]{1,0:T(8,128)(2,1)} %get-tuple-element.11.refs_0_.refs_1_, bf16[128,2048]{1,0:T(8,128)(2,1)} %get-tuple-element.12.refs_1_.refs_2_), custom_call_target="tpu_custom_call" | custom-call | flops 1024 | bytes 1024 | tf_op jit(solution)/shard_map/pallas_call | solution.py:41
  23.6 1.3 %collective-permute-start.7 = (bf16[128,2048]{1,0:T(8,128)(2,1)}, bf16[128,2048]{1,0:T(8,128)(2,1)S(1)}, u32[]{:S(2)}, u32[]{:S(2)}) collective-permute-start(bf16[128,2048]{1,0:T(8,128)(2,1)} %get-tuple-element.11.refs_0_.refs_1_), channel_id=1, source_target_pairs={{4,0},{8,4},{5,1},{9,5},{6,2},{10,6},{7,3},{11,7},{20,16},{24,20},... | collective-permute-start | bytes 1572872 | tf_op jit(solution)/shard_map/ppermute | solution.py:27
  25.6 3.0 %collective-permute-start.5 = (bf16[128,1792]{1,0:T(8,128)(2,1)}, bf16[128,1792]{1,0:T(8,128)(2,1)S(1)}, u32[]{:S(2)}, u32[]{:S(2)}) collective-permute-start(bf16[128,1792]{1,0:T(8,128)(2,1)} %get-tuple-element.13), channel_id=1, source_target_pairs={{0,12},{4,8},{8,4},{12,0},{1,13},{5,9},{9,5},{13,1},{2,14},{6,10},... | collective-permute-start | bytes 1376264 | tf_op jit(solution)/shard_map/ppermute | solution.py:22
  28.6 2.0 %collective-permute-start = (bf16[1792,128]{1,0:T(8,128)(2,1)S(1)}, bf16[1792,128]{1,0:T(8,128)(2,1)S(1)}, u32[]{:S(2)}, u32[]{:S(2)}) collective-permute-start(bf16[1792,128]{1,0:T(8,128)(2,1)S(1)} %get-tuple-element.9.refs_3_), channel_id=1, source_target_pairs={{0,4},{4,0},{8,12},{12,8},{1,5},{5,1},{9,13},{13,9},{2,6},{6,2},{1... | collective-permute-start | bytes 1376264 | tf_op jit(solution)/shard_map/ppermute | solution.py:22
  30.6 1.4 %constant_dynamic-slice_fusion.1.refs_0_ = bf16[256,1792]{1,0:T(8,128)(2,1)S(1)} fusion(bf16[256,7168]{1,0:T(8,128)(2,1)} %param.4, s32[]{:T(128)S(6)} %select_n.48), kind=kLoop, calls=%fused_computation.3 | loop fusion | bytes 1835012 | tf_op jit(solution)/shard_map/dynamic_slice | solution.py:239
  33.4 7.9 %shard_map.43.refs_2_.refs_3_.refs_1_ = f32[2,1792,256]{2,1,0:T(8,128)S(1)} custom-call(s32[1]{0:T(128)} %bitcast.1.where, bf16[128,2048]{1,0:T(8,128)(2,1)S(1)} %shard_map.42.refs_0_, bf16[128,2048]{1,0:T(8,128)(2,1)S(1)} %collective-permute-done.4.refs_1_, bf16[2,1,1792,2048]{3,2,1,0:T(8,128)(2,1)} %refs_2_.7, f32[2,256]{1,0:T(2,128)S(1)} %shard_map.40.refs_3_.refs_4_), custom_call_target="tpu_custom_call" | custom-call | flops 1000000 | bytes 1024 | tf_op jit(solution)/shard_map/pallas_call | solution.py:41
  41.3 18.4 %collective-permute-done.refs_4_.refs_0_ = bf16[1792,128]{1,0:T(8,128)(2,1)S(1)} collective-permute-done((bf16[1792,128]{1,0:T(8,128)(2,1)S(1)}, bf16[1792,128]{1,0:T(8,128)(2,1)S(1)}, u32[]{:S(2)}, u32[]{:S(2)}) %collective-permute-start) | collective-permute-done | bytes 458784 | tf_op jit(solution)/shard_map/ppermute | solution.py:22
  59.8 1.8 %copy-done = f32[2,1792,256]{2,1,0:T(8,128)} copy-done((f32[2,1792,256]{2,1,0:T(8,128)}, f32[2,1792,256]{2,1,0:T(8,128)S(1)}, u32[]{:S(2)}) %copy-start) | copy-done | bytes 3670040
  61.6 1.5 %collective-permute-start.6 = (bf16[128,1792]{1,0:T(8,128)(2,1)S(1)}, bf16[128,1792]{1,0:T(8,128)(2,1)}, u32[]{:S(2)}, u32[]{:S(2)}) collective-permute-start(bf16[128,1792]{1,0:T(8,128)(2,1)S(1)} %collective-permute-done.5.refs_3_.refs_0_), channel_id=1, source_target_pairs={{0,2},{2,0},{1,3},{3,1},{4,6},{6,4},{5,7},{7,5},{8,10},{10,8},{9,1... | collective-permute-start | bytes 1376264 | tf_op jit(solution)/shard_map/ppermute | solution.py:22
  63.6 1.3 %collective-permute-start.12 = (bf16[128,2048]{1,0:T(8,128)(2,1)S(1)}, bf16[128,2048]{1,0:T(8,128)(2,1)S(1)}, u32[]{:S(2)}, u32[]{:S(2)}) collective-permute-start(bf16[128,2048]{1,0:T(8,128)(2,1)S(1)} %shard_map.44.refs_0_), channel_id=1, source_target_pairs={{4,0},{8,12},{5,1},{9,13},{6,2},{10,14},{7,3},{11,15},{20,16},{24,... | collective-permute-start | bytes 1572872 | tf_op jit(solution)/shard_map/ppermute | solution.py:259
  64.9 5.0 %collective-permute-start.10 = (bf16[1792,128]{1,0:T(8,128)(2,1)}, bf16[1792,128]{1,0:T(8,128)(2,1)S(1)}, u32[]{:S(2)}, u32[]{:S(2)}) collective-permute-start(bf16[1792,128]{1,0:T(8,128)(2,1)} %shard_map.46), channel_id=1, source_target_pairs={{0,8},{4,12},{8,0},{12,4},{1,9},{5,13},{9,1},{13,5},{2,10},{6,14},... | collective-permute-start | bytes 1376264 | tf_op jit(solution)/shard_map/ppermute | solution.py:22
  69.9 2.0 %copy-done.1 = f32[2,1792,256]{2,1,0:T(8,128)S(1)} copy-done((f32[2,1792,256]{2,1,0:T(8,128)S(1)}, f32[2,1792,256]{2,1,0:T(8,128)}, u32[]{:S(2)}) %copy-start.1) | copy-done | bytes 3670040
  72.0 7.9 %shard_map.45.refs_1_.refs_3_.refs_4_.refs_2_ = f32[2,1792,256]{2,1,0:T(8,128)S(1)} custom-call(s32[1]{0:T(128)} %bitcast.1.where, bf16[128,2048]{1,0:T(8,128)(2,1)S(1)} %shard_map.44.refs_0_, bf16[128,2048]{1,0:T(8,128)(2,1)S(1)} %collective-permute-done.9.refs_1_, bf16[2,1,1792,2048]{3,2,1,0:T(8,128)(2,1)} %refs_2_.7, f32[2,1792,256]{2,1,0:T(8,128)S(1)} %copy-done.1), custom_call_target="tpu_custom_call" | custom-call | flops 40000000000 | bytes 1024 | tf_op jit(solution)/shard_map/pallas_call | solution.py:41
  79.9 1.8 %copy-done.3 = f32[2,1792,256]{2,1,0:T(8,128)} copy-done((f32[2,1792,256]{2,1,0:T(8,128)}, f32[2,1792,256]{2,1,0:T(8,128)S(1)}, u32[]{:S(2)}) %copy-start.3) | copy-done | bytes 3670040
  81.7 8.4 %collective-permute-done.10.refs_0_ = bf16[1792,128]{1,0:T(8,128)(2,1)S(1)} collective-permute-done((bf16[1792,128]{1,0:T(8,128)(2,1)}, bf16[1792,128]{1,0:T(8,128)(2,1)S(1)}, u32[]{:S(2)}, u32[]{:S(2)}) %collective-permute-start.10) | collective-permute-done | bytes 458784 | tf_op jit(solution)/shard_map/ppermute | solution.py:22
  90.9 1.5 %collective-permute-start.17 = (bf16[1792,128]{1,0:T(8,128)(2,1)}, bf16[1792,128]{1,0:T(8,128)(2,1)S(1)}, u32[]{:S(2)}, u32[]{:S(2)}) collective-permute-start(bf16[1792,128]{1,0:T(8,128)(2,1)} %shard_map.47.refs_5_.refs_0_), channel_id=1, source_target_pairs={{0,2},{2,0},{1,3},{3,1},{4,6},{6,4},{5,7},{7,5},{8,10},{10,8},{9,1... | collective-permute-start | bytes 1376264 | tf_op jit(solution)/shard_map/ppermute | solution.py:22
  92.4 2.0 %copy-done.4 = f32[2,1792,256]{2,1,0:T(8,128)S(1)} copy-done((f32[2,1792,256]{2,1,0:T(8,128)S(1)}, f32[2,1792,256]{2,1,0:T(8,128)}, u32[]{:S(2)}) %copy-start.4) | copy-done | bytes 3670040
  94.5 1.4 %shard_map.50.refs_0_ = bf16[128,2048]{1,0:T(8,128)(2,1)S(1)} custom-call(s32[1]{0:T(128)} %bitcast.4.where, bf16[128,2048]{1,0:T(8,128)(2,1)S(1)} %collective-permute-done.12.refs_0_.refs_3_, bf16[128,2048]{1,0:T(8,128)(2,1)} %get-tuple-element.11.refs_0_.refs_1_, bf16[128,2048]{1,0:T(8,128)(2,1)} %get-tuple-element.12.refs_1_.refs_2_, ...), custom_call_target="tpu_custom_call" | custom-call | flops 1024 | bytes 1024 | tf_op jit(solution)/shard_map/pallas_call | solution.py:41
  96.9 8.2 %shard_map.48.refs_3_.refs_2_ = f32[2,256,2048]{2,1,0:T(8,128)S(1)} custom-call(s32[1]{0:T(128)} %bitcast.where, bf16[128,1792]{1,0:T(8,128)(2,1)S(1)} %collective-permute-done.5.refs_3_.refs_0_, bf16[128,1792]{1,0:T(8,128)(2,1)} %collective-permute-done.6.refs_1_, bf16[2,1,1792,2048]{3,2,1,0:T(8,128)(2,1)} %refs_2_.7, f32[2,1792,256]{2,1,0:T(8,128)S(1)} %copy-done.5, ...), custom_call_target="tpu_custom_call" | custom-call | flops 40000000000 | bytes 1024 | tf_op jit(solution)/shard_map/pallas_call | solution.py:41
  106.4 2.2 %collective-permute-start.14 = (f32[2,256]{1,0:T(2,128)S(1)}, f32[2,256]{1,0:T(2,128)S(1)}, u32[]{:S(2)}, u32[]{:S(2)}) collective-permute-start(f32[2,256]{1,0:T(2,128)S(1)} %shard_map.51.refs_3_), channel_id=1, source_target_pairs={{0,12},{4,8},{8,4},{12,0},{1,13},{5,9},{9,5},{13,1},{2,14},{6,10},... | collective-permute-start | bytes 6152 | tf_op jit(solution)/shard_map/ppermute | solution.py:22
  109.4 2.4 %collective-permute-done.14 = f32[2,256]{1,0:T(2,128)S(1)} collective-permute-done((f32[2,256]{1,0:T(2,128)S(1)}, f32[2,256]{1,0:T(2,128)S(1)}, u32[]{:S(2)}, u32[]{:S(2)}) %collective-permute-start.14) | collective-permute-done | bytes 2080 | tf_op jit(solution)/shard_map/ppermute | solution.py:22
  111.9 0.9 collective-permute-start.19
  112.8 2.1 %collective-permute-start.20 = (f32[2,256]{1,0:T(2,128)S(1)}, f32[2,256]{1,0:T(2,128)S(1)}, u32[]{:S(2)}, u32[]{:S(2)}) collective-permute-start(f32[2,256]{1,0:T(2,128)S(1)} %add.51), channel_id=1, source_target_pairs={{0,10},{2,8},{4,14},{6,12},{8,2},{10,0},{12,6},{14,4},{1,11},{3,9}... | collective-permute-start | bytes 6152 | tf_op jit(solution)/shard_map/ppermute | solution.py:22
  114.9 1.5 %collective-permute-start.16 = (f32[2,256]{1,0:T(2,128)S(1)}, f32[2,256]{1,0:T(2,128)S(1)}, u32[]{:S(2)}, u32[]{:S(2)}) collective-permute-start(f32[2,256]{1,0:T(2,128)S(1)} %add.49), channel_id=1, source_target_pairs={{0,2},{2,0},{1,3},{3,1},{4,6},{6,4},{5,7},{7,5},{8,10},{10,8},{9,1... | collective-permute-start | bytes 6152 | tf_op jit(solution)/shard_map/ppermute | solution.py:22
  116.5 1.7 %collective-permute-done.20 = f32[2,256]{1,0:T(2,128)S(1)} collective-permute-done((f32[2,256]{1,0:T(2,128)S(1)}, f32[2,256]{1,0:T(2,128)S(1)}, u32[]{:S(2)}, u32[]{:S(2)}) %collective-permute-start.20) | collective-permute-done | bytes 2080 | tf_op jit(solution)/shard_map/ppermute | solution.py:22
  (57 shorter events, 8.0 us)
Async XLA Ops:
  0.0 10.7 %copy-start.11 = (bf16[256,2048]{1,0:T(8,128)(2,1)S(1)}, bf16[256,2048]{1,0:T(8,128)(2,1)}, u32[]{:S(2)}) copy-start(bf16[256,2048]{1,0:T(8,128)(2,1)} %refs_1_.1) | copy-start | bytes 3145732
  1.2 19.4 %collective-permute-start.2 = (bf16[128,2048]{1,0:T(8,128)(2,1)S(1)}, bf16[128,2048]{1,0:T(8,128)(2,1)}, u32[]{:S(2)}, u32[]{:S(2)}) collective-permute-start(bf16[128,2048]{1,0:T(8,128)(2,1)S(1)} %constant_dynamic-slice_fusion), channel_id=1, source_target_pairs={{0,4},{4,8},{8,12},{1,5},{5,9},{9,13},{2,6},{6,10},{10,14},{3,7},{... | collective-permute-start | bytes 1572872 | tf_op jit(solution)/shard_map/ppermute | solution.py:26
  6.9 15.4 %collective-permute-start.3 = (bf16[128,2048]{1,0:T(8,128)(2,1)S(1)}, bf16[128,2048]{1,0:T(8,128)(2,1)}, u32[]{:S(2)}, u32[]{:S(2)}) collective-permute-start(bf16[128,2048]{1,0:T(8,128)(2,1)S(1)} %constant_dynamic-slice_fusion), channel_id=1, source_target_pairs={{4,0},{8,4},{12,8},{5,1},{9,5},{13,9},{6,2},{10,6},{14,10},{7,3},{... | collective-permute-start | bytes 1572872 | tf_op jit(solution)/shard_map/ppermute | solution.py:27
  10.7 8.1 %copy-start.10 = (bf16[1792,128]{1,0:T(8,128)(2,1)}, bf16[1792,128]{1,0:T(8,128)(2,1)S(1)}, u32[]{:S(2)}) copy-start(bf16[1792,128]{1,0:T(8,128)(2,1)S(1)} %get-tuple-element.10.refs_4_.refs_0_) | copy-start | bytes 1376260
  18.8 1.8 %copy-start.6 = (f32[2,1792,256]{2,1,0:T(8,128)}, f32[2,1792,256]{2,1,0:T(8,128)S(1)}, u32[]{:S(2)}) copy-start(f32[2,1792,256]{2,1,0:T(8,128)S(1)} %shard_map.39.refs_1_.refs_2_) | copy-start | bytes 11010052
  23.6 9.8 %collective-permute-start.4 = (bf16[128,2048]{1,0:T(8,128)(2,1)S(1)}, bf16[128,2048]{1,0:T(8,128)(2,1)S(1)}, u32[]{:S(2)}, u32[]{:S(2)}) collective-permute-start(bf16[128,2048]{1,0:T(8,128)(2,1)S(1)} %shard_map.42.refs_0_), channel_id=1, source_target_pairs={{0,1},{1,0},{2,3},{3,2},{4,5},{5,4},{6,7},{7,6},{8,9},{9,8},{10,11... | collective-permute-start | bytes 1572872 | tf_op jit(solution)/shard_map/ppermute | solution.py:22
  23.6 36.1 %collective-permute-start.7 = (bf16[128,2048]{1,0:T(8,128)(2,1)}, bf16[128,2048]{1,0:T(8,128)(2,1)S(1)}, u32[]{:S(2)}, u32[]{:S(2)}) collective-permute-start(bf16[128,2048]{1,0:T(8,128)(2,1)} %get-tuple-element.11.refs_0_.refs_1_), channel_id=1, source_target_pairs={{4,0},{8,4},{5,1},{9,5},{6,2},{10,6},{7,3},{11,7},{20,16},{24,20},... | collective-permute-start | bytes 1572872 | tf_op jit(solution)/shard_map/ppermute | solution.py:27
  24.9 34.8 %collective-permute-start.8 = (bf16[128,2048]{1,0:T(8,128)(2,1)}, bf16[128,2048]{1,0:T(8,128)(2,1)S(1)}, u32[]{:S(2)}, u32[]{:S(2)}) collective-permute-start(bf16[128,2048]{1,0:T(8,128)(2,1)} %get-tuple-element.12.refs_1_.refs_2_), channel_id=1, source_target_pairs={{4,8},{8,12},{5,9},{9,13},{6,10},{10,14},{7,11},{11,15},{20,24},{2... | collective-permute-start | bytes 1572872 | tf_op jit(solution)/shard_map/ppermute | solution.py:26
  25.6 15.6 %collective-permute-start.5 = (bf16[128,1792]{1,0:T(8,128)(2,1)}, bf16[128,1792]{1,0:T(8,128)(2,1)S(1)}, u32[]{:S(2)}, u32[]{:S(2)}) collective-permute-start(bf16[128,1792]{1,0:T(8,128)(2,1)} %get-tuple-element.13), channel_id=1, source_target_pairs={{0,12},{4,8},{8,4},{12,0},{1,13},{5,9},{9,5},{13,1},{2,14},{6,10},... | collective-permute-start | bytes 1376264 | tf_op jit(solution)/shard_map/ppermute | solution.py:22
  28.6 31.1 %collective-permute-start = (bf16[1792,128]{1,0:T(8,128)(2,1)S(1)}, bf16[1792,128]{1,0:T(8,128)(2,1)S(1)}, u32[]{:S(2)}, u32[]{:S(2)}) collective-permute-start(bf16[1792,128]{1,0:T(8,128)(2,1)S(1)} %get-tuple-element.9.refs_3_), channel_id=1, source_target_pairs={{0,4},{4,0},{8,12},{12,8},{1,5},{5,1},{9,13},{13,9},{2,6},{6,2},{1... | collective-permute-start | bytes 1376264 | tf_op jit(solution)/shard_map/ppermute | solution.py:22
  30.6 2.3 %copy-start.7 = (f32[2,1792,256]{2,1,0:T(8,128)S(1)}, f32[2,1792,256]{2,1,0:T(8,128)}, u32[]{:S(2)}) copy-start(f32[2,1792,256]{2,1,0:T(8,128)} %copy-done.6) | copy-start | bytes 11010052
  59.8 1.8 %copy-start = (f32[2,1792,256]{2,1,0:T(8,128)}, f32[2,1792,256]{2,1,0:T(8,128)S(1)}, u32[]{:S(2)}) copy-start(f32[2,1792,256]{2,1,0:T(8,128)S(1)} %shard_map.43.refs_2_.refs_3_.refs_1_) | copy-start | bytes 11010052
  61.6 8.4 %collective-permute-start.9 = (bf16[128,2048]{1,0:T(8,128)(2,1)S(1)}, bf16[128,2048]{1,0:T(8,128)(2,1)S(1)}, u32[]{:S(2)}, u32[]{:S(2)}) collective-permute-start(bf16[128,2048]{1,0:T(8,128)(2,1)S(1)} %shard_map.44.refs_0_), channel_id=1, source_target_pairs={{0,1},{1,0},{2,3},{3,2},{4,5},{5,4},{6,7},{7,6},{8,9},{9,8},{10,11... | collective-permute-start | bytes 1572872 | tf_op jit(solution)/shard_map/ppermute | solution.py:22
  61.6 34.4 %collective-permute-start.6 = (bf16[128,1792]{1,0:T(8,128)(2,1)S(1)}, bf16[128,1792]{1,0:T(8,128)(2,1)}, u32[]{:S(2)}, u32[]{:S(2)}) collective-permute-start(bf16[128,1792]{1,0:T(8,128)(2,1)S(1)} %collective-permute-done.5.refs_3_.refs_0_), channel_id=1, source_target_pairs={{0,2},{2,0},{1,3},{3,1},{4,6},{6,4},{5,7},{7,5},{8,10},{10,8},{9,1... | collective-permute-start | bytes 1376264 | tf_op jit(solution)/shard_map/ppermute | solution.py:22
  63.1 42.0 %collective-permute-start.1 = (bf16[1792,128]{1,0:T(8,128)(2,1)S(1)}, bf16[1792,128]{1,0:T(8,128)(2,1)S(1)}, u32[]{:S(2)}, u32[]{:S(2)}) collective-permute-start(bf16[1792,128]{1,0:T(8,128)(2,1)S(1)} %collective-permute-done.refs_4_.refs_0_), channel_id=1, source_target_pairs={{0,2},{2,0},{1,3},{3,1},{4,6},{6,4},{5,7},{7,5},{8,10},{10,8},{9,1... | collective-permute-start | bytes 1376264 | tf_op jit(solution)/shard_map/ppermute | solution.py:22
  63.6 28.8 %collective-permute-start.12 = (bf16[128,2048]{1,0:T(8,128)(2,1)S(1)}, bf16[128,2048]{1,0:T(8,128)(2,1)S(1)}, u32[]{:S(2)}, u32[]{:S(2)}) collective-permute-start(bf16[128,2048]{1,0:T(8,128)(2,1)S(1)} %shard_map.44.refs_0_), channel_id=1, source_target_pairs={{4,0},{8,12},{5,1},{9,13},{6,2},{10,14},{7,3},{11,15},{20,16},{24,... | collective-permute-start | bytes 1572872 | tf_op jit(solution)/shard_map/ppermute | solution.py:259
  64.9 25.2 %collective-permute-start.10 = (bf16[1792,128]{1,0:T(8,128)(2,1)}, bf16[1792,128]{1,0:T(8,128)(2,1)S(1)}, u32[]{:S(2)}, u32[]{:S(2)}) collective-permute-start(bf16[1792,128]{1,0:T(8,128)(2,1)} %shard_map.46), channel_id=1, source_target_pairs={{0,8},{4,12},{8,0},{12,4},{1,9},{5,13},{9,1},{13,5},{2,10},{6,14},... | collective-permute-start | bytes 1376264 | tf_op jit(solution)/shard_map/ppermute | solution.py:22
  69.9 2.0 %copy-start.1 = (f32[2,1792,256]{2,1,0:T(8,128)S(1)}, f32[2,1792,256]{2,1,0:T(8,128)}, u32[]{:S(2)}) copy-start(f32[2,1792,256]{2,1,0:T(8,128)} %copy-done) | copy-start | bytes 11010052
  79.8 1.8 %copy-start.3 = (f32[2,1792,256]{2,1,0:T(8,128)}, f32[2,1792,256]{2,1,0:T(8,128)S(1)}, u32[]{:S(2)}) copy-start(f32[2,1792,256]{2,1,0:T(8,128)S(1)} %shard_map.45.refs_1_.refs_3_.refs_4_.refs_2_) | copy-start | bytes 11010052
  90.9 17.7 %collective-permute-start.17 = (bf16[1792,128]{1,0:T(8,128)(2,1)}, bf16[1792,128]{1,0:T(8,128)(2,1)S(1)}, u32[]{:S(2)}, u32[]{:S(2)}) collective-permute-start(bf16[1792,128]{1,0:T(8,128)(2,1)} %shard_map.47.refs_5_.refs_0_), channel_id=1, source_target_pairs={{0,2},{2,0},{1,3},{3,1},{4,6},{6,4},{5,7},{7,5},{8,10},{10,8},{9,1... | collective-permute-start | bytes 1376264 | tf_op jit(solution)/shard_map/ppermute | solution.py:22
  92.4 2.0 %copy-start.4 = (f32[2,1792,256]{2,1,0:T(8,128)S(1)}, f32[2,1792,256]{2,1,0:T(8,128)}, u32[]{:S(2)}) copy-start(f32[2,1792,256]{2,1,0:T(8,128)} %copy-done.3) | copy-start | bytes 11010052
  94.5 2.4 %copy-start.5 = (f32[2,1792,256]{2,1,0:T(8,128)S(1)}, f32[2,1792,256]{2,1,0:T(8,128)}, u32[]{:S(2)}) copy-start(f32[2,1792,256]{2,1,0:T(8,128)} %copy-done.3) | copy-start | bytes 11010052
  94.5 2.4 %copy-start.9 = (bf16[1792,128]{1,0:T(8,128)(2,1)S(1)}, bf16[1792,128]{1,0:T(8,128)(2,1)}, u32[]{:S(2)}) copy-start(bf16[1792,128]{1,0:T(8,128)(2,1)} %shard_map.47.refs_5_.refs_0_) | copy-start | bytes 1376260
  95.9 10.0 %collective-permute-start.13 = (bf16[128,2048]{1,0:T(8,128)(2,1)S(1)}, bf16[128,2048]{1,0:T(8,128)(2,1)S(1)}, u32[]{:S(2)}, u32[]{:S(2)}) collective-permute-start(bf16[128,2048]{1,0:T(8,128)(2,1)S(1)} %shard_map.50.refs_0_), channel_id=1, source_target_pairs={{0,1},{1,0},{2,3},{3,2},{4,5},{5,4},{6,7},{7,6},{8,9},{9,8},{10,11... | collective-permute-start | bytes 1572872 | tf_op jit(solution)/shard_map/ppermute | solution.py:22
  96.9 8.2 %copy-start.2 = (f32[2,1792,256]{2,1,0:T(8,128)S(1)}, f32[2,1792,256]{2,1,0:T(8,128)}, u32[]{:S(2)}) copy-start(f32[2,1792,256]{2,1,0:T(8,128)} %copy-done) | copy-start | bytes 11010052
  105.8 3.6 %collective-permute-start.11 = (f32[2,256]{1,0:T(2,128)S(1)}, f32[2,256]{1,0:T(2,128)S(1)}, u32[]{:S(2)}, u32[]{:S(2)}) collective-permute-start(f32[2,256]{1,0:T(2,128)S(1)} %shard_map.49.refs_3_), channel_id=1, source_target_pairs={{0,4},{4,0},{8,12},{12,8},{1,5},{5,1},{9,13},{13,9},{2,6},{6,2},{1... | collective-permute-start | bytes 6152 | tf_op jit(solution)/shard_map/ppermute | solution.py:22
  106.4 5.4 %collective-permute-start.14 = (f32[2,256]{1,0:T(2,128)S(1)}, f32[2,256]{1,0:T(2,128)S(1)}, u32[]{:S(2)}, u32[]{:S(2)}) collective-permute-start(f32[2,256]{1,0:T(2,128)S(1)} %shard_map.51.refs_3_), channel_id=1, source_target_pairs={{0,12},{4,8},{8,4},{12,0},{1,13},{5,9},{9,5},{13,1},{2,14},{6,10},... | collective-permute-start | bytes 6152 | tf_op jit(solution)/shard_map/ppermute | solution.py:22
  109.3 2.6 %collective-permute-start.18 = (f32[2,256]{1,0:T(2,128)S(1)}, f32[2,256]{1,0:T(2,128)S(1)}, u32[]{:S(2)}, u32[]{:S(2)}) collective-permute-start(f32[2,256]{1,0:T(2,128)S(1)} %shard_map.52), channel_id=1, source_target_pairs={{0,1},{1,0},{2,3},{3,2},{4,5},{5,4},{6,7},{7,6},{8,9},{9,8},{10,11... | collective-permute-start | bytes 6152 | tf_op jit(solution)/shard_map/ppermute | solution.py:22
  111.9 3.0 %collective-permute-start.15 = (f32[2,256]{1,0:T(2,128)S(1)}, f32[2,256]{1,0:T(2,128)S(1)}, u32[]{:S(2)}, u32[]{:S(2)}) collective-permute-start(f32[2,256]{1,0:T(2,128)S(1)} %add_add_fusion.1), channel_id=1, source_target_pairs={{0,1},{1,0},{2,3},{3,2},{4,5},{5,4},{6,7},{7,6},{8,9},{9,8},{10,11... | collective-permute-start | bytes 6152 | tf_op jit(solution)/shard_map/ppermute | solution.py:22
  111.9 4.6 %collective-permute-start.19 = (f32[2,256]{1,0:T(2,128)S(1)}, f32[2,256]{1,0:T(2,128)S(1)}, u32[]{:S(2)}, u32[]{:S(2)}) collective-permute-start(f32[2,256]{1,0:T(2,128)S(1)} %add.51), channel_id=1, source_target_pairs={{0,8},{2,10},{4,12},{6,14},{8,0},{10,2},{12,4},{14,6},{1,9},{3,11}... | collective-permute-start | bytes 6152 | tf_op jit(solution)/shard_map/ppermute | solution.py:22
  112.8 5.4 %collective-permute-start.20 = (f32[2,256]{1,0:T(2,128)S(1)}, f32[2,256]{1,0:T(2,128)S(1)}, u32[]{:S(2)}, u32[]{:S(2)}) collective-permute-start(f32[2,256]{1,0:T(2,128)S(1)} %add.51), channel_id=1, source_target_pairs={{0,10},{2,8},{4,14},{6,12},{8,2},{10,0},{12,6},{14,4},{1,11},{3,9}... | collective-permute-start | bytes 6152 | tf_op jit(solution)/shard_map/ppermute | solution.py:22
  114.9 3.6 %collective-permute-start.16 = (f32[2,256]{1,0:T(2,128)S(1)}, f32[2,256]{1,0:T(2,128)S(1)}, u32[]{:S(2)}, u32[]{:S(2)}) collective-permute-start(f32[2,256]{1,0:T(2,128)S(1)} %add.49), channel_id=1, source_target_pairs={{0,2},{2,0},{1,3},{3,1},{4,6},{6,4},{5,7},{7,5},{8,10},{10,8},{9,1... | collective-permute-start | bytes 6152 | tf_op jit(solution)/shard_map/ppermute | solution.py:22
  (1 other events, 0.8 us)

commit v7 on v1

v7 whole, which is shorter than its diff:
```python
import functools
import math

import jax
import jax.numpy as jnp
from jax import lax
from jax.experimental import pallas as pl
from jax.experimental.pallas import tpu as pltpu
from jax.sharding import PartitionSpec as P


LONG = 8_000_000_000


def trade(block, steps, backwards=False):
    axes = tuple(steps)
    sizes = [lax.axis_size(axis) for axis in axes]
    mask = 0
    for axis, size in zip(axes, sizes):
        mask = mask * size + steps[axis]
    route = [(i, i ^ mask) for i in range(math.prod(sizes))]
    return lax.ppermute(block, axes, route[::-1] if backwards else route)


ANYWHERE = pl.BlockSpec(memory_space=pl.ANY)


def call(kernel, grid, where, inputs, shape, out_spec, scratch, flops, tokens, vmem=36):
    arrays = [array for array, _ in inputs]
    skip = len(tokens)

    def body(where, *refs):
        kernel(where, *refs[: len(arrays)], *refs[len(arrays) + skip :])

    return pl.pallas_call(
        body,
        grid_spec=pltpu.PrefetchScalarGridSpec(
            num_scalar_prefetch=1,
            grid=grid,
            in_specs=[spec for _, spec in inputs] + [ANYWHERE] * skip,
            out_specs=out_spec,
            scratch_shapes=scratch,
        ),
        out_shape=shape,
        compiler_params=pltpu.CompilerParams(vmem_limit_bytes=vmem * 1024 * 1024),
        cost_estimate=pl.CostEstimate(flops=flops, bytes_accessed=1024, transcendentals=0),
    )(jnp.stack([jnp.asarray(w, jnp.int32) for w in where]), *arrays, *tokens)


def hold(blocks, tokens):
    count = len(blocks)
    return pl.pallas_call(
        lambda *refs: None,
        in_specs=[ANYWHERE] * (count + len(tokens)),
        out_specs=[ANYWHERE] * count,
        out_shape=[jax.ShapeDtypeStruct(block.shape, block.dtype) for block in blocks],
        input_output_aliases={i: i for i in range(count)},
        cost_estimate=pl.CostEstimate(flops=1024, bytes_accessed=1024, transcendentals=0),
    )(*blocks, *tokens)


def joined(parts, where, axis):
    found = []
    for p in range(len(parts)):
        chosen = parts[0][...]
        for r in range(1, len(parts)):
            chosen = jnp.where(where[0] == p ^ r, parts[r][...], chosen)
        found.append(chosen)
    return found[0] if len(found) == 1 else jnp.concatenate(found, axis=axis)


def project_kernel(where, *refs):
    parts, (query_ref, out_ref, grads) = refs[:-3], refs[-3:]

    @pl.when((pl.program_id(0) == 0) & (pl.program_id(1) == 0))
    def _():
        grads[...] = joined(parts, where, 0)

    out_ref[0] = jnp.dot(grads[...], query_ref[0, 0], preferred_element_type=jnp.float32)


def projected(parts, column, queries, flops, tokens=()):
    nq, _, depth, width = queries.shape
    count = sum(part.shape[0] for part in parts)
    tile = width // 2
    inputs = [(part, pl.BlockSpec(part.shape, lambda q, i, where: (0, 0))) for part in parts]
    inputs.append((queries, pl.BlockSpec((1, 1, depth, tile), lambda q, i, where: (q, 0, 0, i))))
    return call(
        project_kernel, (nq, width // tile), [column], inputs,
        jax.ShapeDtypeStruct((nq, count, width), jnp.float32),
        pl.BlockSpec((1, count, tile), lambda q, i, where: (q, 0, i)),
        [pltpu.VMEM((count, depth), queries.dtype)], flops, tokens,
    )


def finish_kernel(where, mine_ref, other_ref, proj_ref, out_ref):
    half, width = mine_ref.shape
    swapped = where[0] == 1
    for h, (first, second) in enumerate(((mine_ref, other_ref), (other_ref, mine_ref))):
        acts = jnp.where(swapped, second[...], first[...]).astype(jnp.float32)
        for q in range(proj_ref.shape[0]):
            terms = acts * proj_ref[q, h * half : (h + 1) * half, :]
            lanes = terms[:, :128]
            for at in range(128, width, 128):
                lanes = lanes + terms[:, at : at + 128]
            out_ref[q : q + 1, h * half : (h + 1) * half] = jnp.sum(lanes.T, axis=0, keepdims=True)


def scores_of_acts(mine, other, core, proj, tokens=()):
    nq, count, _ = proj.shape
    inputs = [(block, pl.BlockSpec(block.shape, lambda i, where: (0, 0))) for block in (mine, other)]
    inputs.append((proj, pl.BlockSpec(proj.shape, lambda i, where: (0, 0, 0))))
    return call(
        finish_kernel, (1,), [core], inputs, jax.ShapeDtypeStruct((nq, count), jnp.float32),
        pl.BlockSpec((nq, count), lambda i, where: (0, 0)), [], 1024, tokens,
    )


def on_device(activations, out_grads, queries):
    count, spread = lax.axis_size("dp"), lax.axis_size("din")
    me, column, core = lax.axis_index("dp"), lax.axis_index("din"), lax.axis_index("dout")
    tokens, rows = activations.shape[0], queries.shape[2]
    part, half = tokens // spread, tokens // 2

    def grads_for(device, first, size):
        return lax.dynamic_slice(out_grads, (first, device * rows), (size, rows))

    steps = list(range(count - 1, 0, -1))
    mine = lax.dynamic_slice_in_dim(activations, core * half, half, 0)
    grads = {d: trade(grads_for(me ^ d, column * part, part), {"dp": d}) for d in steps}
    acts = {d: trade(mine, {"dp": d}) for d in steps}

    zero = jnp.zeros((), jnp.int32)
    proj = {0: projected([grads_for(me, 0, tokens)], zero, queries, LONG)}
    scores = scores_of_acts(activations[:half], activations[half:], zero, proj[0])
    token = proj[0]
    for d in steps:
        sides = [grads[d]] + [trade(grads[d], {"din": r}) for r in range(1, spread)]
        proj[d] = token = projected(sides, column, queries, LONG, [token])

    last = 2 if count > 2 else 1
    for d in sorted(steps, key=lambda d: d == last):
        if d == last:
            scores = over_chips(scores, spread)
            token = scores
        block, = hold([acts[d]], [proj[steps[-1]]])
        term = scores_of_acts(block, trade(block, {"dout": 1}), core, proj[d], [token])
        if d != last:
            scores = scores + trade(term, {"dp": d})
    term = term + trade(term, {"dout": 1})
    return scores + sum(trade(term, {"dp": last, "din": r}) for r in range(spread))


def over_chips(scores, spread):
    scores = scores + trade(scores, {"dout": 1})
    return scores + sum(trade(scores, {"din": r}) for r in range(1, spread))


def solution(mesh):
    placed = (P(("groups", "dp"), "din"), P(("groups", "dp"), "dout"), P(None, "dout", "dp", "din"))
    return jax.shard_map(
        on_device, mesh=mesh, in_specs=placed, out_specs=P(None, ("groups", "dp")), check_vma=False
    )
```

time: 222 us -> 149 us (0.67)
  blocking collectives: 80.7 us -> 0 us
  Pallas kernels: 0 us -> 35.1 us
  starting transfers between devices: 0.04 us -> 26.7 us
  waiting for transfers between devices: 92 us -> 71 us
  matrix products: 18.4 us -> 0 us
  between operations: 13.5 us -> 0.22 us
  other arithmetic: 3.41 us -> 0.6 us
    all_gather x2 -> x0, waiting for transfers between devices: 92 us -> none  [the longest x1 49.2 us: on_device(): grads = lax.all_gather(blocks, 'din', axis=1).reshape(count * tokens, rows)]
    ppermute x0 -> x19, waiting for transfers between devices: none -> 71 us  [trade(): return lax.ppermute(block, axes, route[::-1] if backwards else route)]
    all_to_all x1 -> x0, blocking collectives: 48.8 us -> none  [on_device(): blocks = lax.all_to_all(blocks, 'dp', 0, 0)]
    pallas_call x0 -> x11, Pallas kernels: none -> 35.1 us  [the longest x8 35.1 us: call(): pl.pallas_call(body, grid_spec=pltpu.PrefetchScalarGridSpec(num_scalar_pr...]
    psum x1 -> x0, blocking collectives: 31.9 us -> none  [on_device(): total = lax.psum(total, ('dp', 'din', 'dout'))]
    ppermute x0 -> x19, starting transfers between devices: none -> 26.7 us  [trade(): return lax.ppermute(block, axes, route[::-1] if backwards else route)]
    dot_general x1 -> x0, matrix products: 18.4 us -> none  [on_device(): jnp.einsum('tc,qci->qti', grads, queries[:, 0], preferred_element_type=jn...]
    all_gather x1 -> x0, local copies, waits for them, and re-layouts: 6.03 us -> none  [on_device(): grads = lax.all_gather(blocks, 'din', axis=1).reshape(count * tokens, rows)]
  transfers between devices with their start and end apart: 2 -> 19, of which waited for: 2 -> 11; matrix products, arithmetic and copies ran while one was open for 3% -> 2% of each run, Pallas kernels for 0% -> 23%
where the time goes in v7:
time: 149 us; the launch traced here: 148 us
  waiting for transfers between devices  71 us (48%)
  Pallas kernels  35.1 us (24%)
  starting transfers between devices  26.7 us (18%)
  local copies, waits for them, and re-layouts  14.9 us (10%)
    ppermute x19, waiting for transfers between devices, trade(): return lax.ppermute(block, axes, route[::-1] if backwards else route)  71 us
    pallas_call x8, Pallas kernels, call(): pl.pallas_call(body, grid_spec=pltpu.PrefetchScalarGridSpec(num_scalar_pr...  35.1 us
    ppermute x19, starting transfers between devices, trade(): return lax.ppermute(block, axes, route[::-1] if backwards else route)  26.7 us
    unnamed x30, local copies, waits for them, and re-layouts  9.05 us
    dynamic_slice x2, local copies, waits for them, and re-layouts, grads_for(): return lax.dynamic_slice(out_grads, (first, device * rows), (size, rows))  3.56 us
  transfers between devices with their start and end apart: 19, of which 11 were waited for; matrix products, arithmetic and copies ran while one was open for 2% of the time, Pallas kernels for 23%

profile of v7, /device:TPU:0, one launch (start us, length us, event | category | flops | bytes accessed | tf_op | source)
XLA Modules:
  0.0 148.5 jit_solution(6494101726824518762)
XLA Ops:
  0.0 2.3 %fusion = (bf16[128,1792]{1,0:T(8,128)(2,1)}, bf16[128,1792]{1,0:T(8,128)(2,1)S(1)}, bf16[128,1792]{1,0:T(8,128)(2,1)}) fusion(bf16[256,7168]{1,0:T(8,128)(2,1)} %param.4, s32[]{:T(128)S(6)} %select_n.22, s32[]{:T(128)S(6)} %select_n.25, s32[]{:T(128)S(6)} %select_n.23, s32[]{:T(128)S(6)} %select_n.24), kind=kLoop, calls=%fused_computation.4 | loop fusion | bytes 2752528 | tf_op jit(solution)/shard_map/dynamic_slice | solution.py:126
  2.3 5.0 %collective-permute-start.5 = (bf16[128,1792]{1,0:T(8,128)(2,1)}, bf16[128,1792]{1,0:T(8,128)(2,1)S(1)}, u32[]{:S(2)}, u32[]{:S(2)}) collective-permute-start(bf16[128,1792]{1,0:T(8,128)(2,1)} %get-tuple-element.5), channel_id=1, source_target_pairs={{0,12},{4,8},{8,4},{12,0},{1,13},{5,9},{9,5},{13,1},{2,14},{6,10},... | collective-permute-start | bytes 1376264 | tf_op jit(solution)/shard_map/ppermute | solution.py:22
  7.4 2.3 %fusion.1 = (bf16[128,2048]{1,0:T(8,128)(2,1)S(1)}, bf16[128,2048]{1,0:T(8,128)(2,1)S(1)}, bf16[128,2048]{1,0:T(8,128)(2,1)}) fusion(bf16[256,2048]{1,0:T(8,128)(2,1)} %param.3, s32[]{:T(128)S(6)} %select_n.21), kind=kLoop, calls=%fused_computation.5 | loop fusion | bytes 3145732 | tf_op jit(solution)/shard_map/slice | solution.py:135
  10.2 1.5 collective-permute-start.1
  11.7 2.9 %collective-permute-start.3 = (bf16[128,1792]{1,0:T(8,128)(2,1)}, bf16[128,1792]{1,0:T(8,128)(2,1)}, u32[]{:S(2)}, u32[]{:S(2)}) collective-permute-start(bf16[128,1792]{1,0:T(8,128)(2,1)} %get-tuple-element.7), channel_id=1, source_target_pairs={{0,8},{4,12},{8,0},{12,4},{1,9},{5,13},{9,1},{13,5},{2,10},{6,14},... | collective-permute-start | bytes 1376264 | tf_op jit(solution)/shard_map/ppermute | solution.py:22
  14.6 1.2 constant_dynamic-slice_fusion.1.refs_0_
  15.8 3.2 %collective-permute-done.5.refs_0_ = bf16[128,1792]{1,0:T(8,128)(2,1)S(1)} collective-permute-done((bf16[128,1792]{1,0:T(8,128)(2,1)}, bf16[128,1792]{1,0:T(8,128)(2,1)S(1)}, u32[]{:S(2)}, u32[]{:S(2)}) %collective-permute-start.5) | collective-permute-done | bytes 458784 | tf_op jit(solution)/shard_map/ppermute | solution.py:22
  19.1 1.7 %collective-permute-start.6 = (bf16[128,1792]{1,0:T(8,128)(2,1)S(1)}, bf16[128,1792]{1,0:T(8,128)(2,1)S(1)}, u32[]{:S(2)}, u32[]{:S(2)}) collective-permute-start(bf16[128,1792]{1,0:T(8,128)(2,1)S(1)} %collective-permute-done.5.refs_0_), channel_id=1, source_target_pairs={{0,2},{2,0},{1,3},{3,1},{4,6},{6,4},{5,7},{7,5},{8,10},{10,8},{9,1... | collective-permute-start | bytes 1376264 | tf_op jit(solution)/shard_map/ppermute | solution.py:22
  20.8 7.9 %shard_map.37.refs_2_.refs_3_ = f32[2,256,2048]{2,1,0:T(8,128)S(1)} custom-call(s32[1]{0:T(128)} %constant.5.clone.1.where, bf16[256,1792]{1,0:T(8,128)(2,1)S(1)} %constant_dynamic-slice_fusion.1.refs_0_, bf16[2,1,1792,2048]{3,2,1,0:T(8,128)(2,1)} %refs_2_.5), custom_call_target="tpu_custom_call" | custom-call | flops 8000000000 | bytes 1024 | tf_op jit(solution)/shard_map/pallas_call | solution.py:35
  28.7 22.8 %collective-permute-done.1.refs_0_ = bf16[128,1792]{1,0:T(8,128)(2,1)S(1)} collective-permute-done((bf16[128,1792]{1,0:T(8,128)(2,1)S(1)}, bf16[128,1792]{1,0:T(8,128)(2,1)S(1)}, u32[]{:S(2)}, u32[]{:S(2)}) %collective-permute-start.1) | collective-permute-done | bytes 458784 | tf_op jit(solution)/shard_map/ppermute | solution.py:22
  51.5 4.6 %collective-permute-start = (bf16[128,2048]{1,0:T(8,128)(2,1)}, bf16[128,2048]{1,0:T(8,128)(2,1)S(1)}, u32[]{:S(2)}, u32[]{:S(2)}) collective-permute-start(bf16[128,2048]{1,0:T(8,128)(2,1)} %get-tuple-element.10), channel_id=1, source_target_pairs={{0,12},{4,8},{8,4},{12,0},{1,13},{5,9},{9,5},{13,1},{2,14},{6,10},... | collective-permute-start | bytes 1572872 | tf_op jit(solution)/shard_map/ppermute | solution.py:22
  56.1 25.5 %collective-permute-done.3.refs_0_ = bf16[128,1792]{1,0:T(8,128)(2,1)} collective-permute-done((bf16[128,1792]{1,0:T(8,128)(2,1)}, bf16[128,1792]{1,0:T(8,128)(2,1)}, u32[]{:S(2)}, u32[]{:S(2)}) %collective-permute-start.3) | collective-permute-done | bytes 458784 | tf_op jit(solution)/shard_map/ppermute | solution.py:22
  81.6 1.5 %collective-permute-start.2 = (bf16[128,1792]{1,0:T(8,128)(2,1)S(1)}, bf16[128,1792]{1,0:T(8,128)(2,1)S(1)}, u32[]{:S(2)}, u32[]{:S(2)}) collective-permute-start(bf16[128,1792]{1,0:T(8,128)(2,1)S(1)} %collective-permute-done.1.refs_0_), channel_id=1, source_target_pairs={{0,2},{2,0},{1,3},{3,1},{4,6},{6,4},{5,7},{7,5},{8,10},{10,8},{9,1... | collective-permute-start | bytes 1376264 | tf_op jit(solution)/shard_map/ppermute | solution.py:22
  83.6 7.9 %shard_map.39.refs_3_.refs_2_ = f32[2,256,2048]{2,1,0:T(8,128)S(1)} custom-call(s32[1]{0:T(128)} %bitcast.1.where, bf16[128,1792]{1,0:T(8,128)(2,1)S(1)} %collective-permute-done.5.refs_0_, bf16[128,1792]{1,0:T(8,128)(2,1)S(1)} %collective-permute-done.6.refs_1_, bf16[2,1,1792,2048]{3,2,1,0:T(8,128)(2,1)} %refs_2_.5, ...), custom_call_target="tpu_custom_call" | custom-call | flops 8000000000 | bytes 1024 | tf_op jit(solution)/shard_map/pallas_call | solution.py:35
  91.5 10.5 %collective-permute-done.4.refs_1_ = bf16[128,1792]{1,0:T(8,128)(2,1)S(1)} collective-permute-done((bf16[128,1792]{1,0:T(8,128)(2,1)}, bf16[128,1792]{1,0:T(8,128)(2,1)S(1)}, u32[]{:S(2)}, u32[]{:S(2)}) %collective-permute-start.4) | collective-permute-done | bytes 458784 | tf_op jit(solution)/shard_map/ppermute | solution.py:22
  102.0 8.0 %shard_map.40.refs_3_.refs_2_ = f32[2,256,2048]{2,1,0:T(8,128)S(1)} custom-call(s32[1]{0:T(128)} %bitcast.1.where, bf16[128,1792]{1,0:T(8,128)(2,1)} %collective-permute-done.3.refs_0_, bf16[128,1792]{1,0:T(8,128)(2,1)S(1)} %collective-permute-done.4.refs_1_, bf16[2,1,1792,2048]{3,2,1,0:T(8,128)(2,1)} %refs_2_.5, f32[2,256,2048]{2,1,0:T(8,128)S(1)} %shard_map.39.refs_3_.refs_2_), custom_call_target="tpu_custom_call" | custom-call | flops 8000000000 | bytes 1024 | tf_op jit(solution)/shard_map/pallas_call | solution.py:35
  110.1 9.4 %shard_map.41.refs_1_.refs_3_.refs_2_ = f32[2,256,2048]{2,1,0:T(8,128)S(1)} custom-call(s32[1]{0:T(128)} %bitcast.1.where, bf16[128,1792]{1,0:T(8,128)(2,1)S(1)} %collective-permute-done.1.refs_0_, bf16[128,1792]{1,0:T(8,128)(2,1)S(1)} %collective-permute-done.2.refs_1_, bf16[2,1,1792,2048]{3,2,1,0:T(8,128)(2,1)} %refs_2_.5, ...), custom_call_target="tpu_custom_call" | custom-call | flops 8000000000 | bytes 1024 | tf_op jit(solution)/shard_map/pallas_call | solution.py:35
  119.5 1.9 %copy-done = f32[2,256,2048]{2,1,0:T(8,128)} copy-done((f32[2,256,2048]{2,1,0:T(8,128)}, f32[2,256,2048]{2,1,0:T(8,128)S(1)}, u32[]{:S(2)}) %copy-start) | copy-done | bytes 4194328
  121.5 0.8 copy-done.13
  122.3 0.8 copy-done.11
  124.4 2.2 %copy-done.1 = f32[2,256,2048]{2,1,0:T(8,128)S(1)} copy-done((f32[2,256,2048]{2,1,0:T(8,128)S(1)}, f32[2,256,2048]{2,1,0:T(8,128)}, u32[]{:S(2)}) %copy-start.1) | copy-done | bytes 4194328
  126.6 2.2 %copy-done.8 = f32[2,256,2048]{2,1,0:T(8,128)S(1)} copy-done((f32[2,256,2048]{2,1,0:T(8,128)S(1)}, f32[2,256,2048]{2,1,0:T(8,128)}, u32[]{:S(2)}) %copy-start.8) | copy-done | bytes 4194328
  129.2 2.4 %collective-permute-start.8 = (f32[2,256]{1,0:T(2,128)S(1)}, f32[2,256]{1,0:T(2,128)S(1)}, u32[]{:S(2)}, u32[]{:S(2)}) collective-permute-start(f32[2,256]{1,0:T(2,128)S(1)} %shard_map.43), channel_id=1, source_target_pairs={{0,12},{4,8},{8,4},{12,0},{1,13},{5,9},{9,5},{13,1},{2,14},{6,10},... | collective-permute-start | bytes 6152 | tf_op jit(solution)/shard_map/ppermute | solution.py:22
  132.9 1.7 %collective-permute-done.8 = f32[2,256]{1,0:T(2,128)S(1)} collective-permute-done((f32[2,256]{1,0:T(2,128)S(1)}, f32[2,256]{1,0:T(2,128)S(1)}, u32[]{:S(2)}, u32[]{:S(2)}) %collective-permute-start.8) | collective-permute-done | bytes 2080 | tf_op jit(solution)/shard_map/ppermute | solution.py:22
  134.7 1.0 collective-permute-done.11
  135.7 1.2 collective-permute-done.12
  136.9 1.5 %collective-permute-start.13 = (f32[2,256]{1,0:T(2,128)S(1)}, f32[2,256]{1,0:T(2,128)S(1)}, u32[]{:S(2)}, u32[]{:S(2)}) collective-permute-start(f32[2,256]{1,0:T(2,128)S(1)} %add.49), channel_id=1, source_target_pairs={{0,2},{2,0},{1,3},{3,1},{4,6},{6,4},{5,7},{7,5},{8,10},{10,8},{9,1... | collective-permute-start | bytes 6152 | tf_op jit(solution)/shard_map/ppermute | solution.py:22
  138.4 2.1 %collective-permute-done.13 = f32[2,256]{1,0:T(2,128)S(1)} collective-permute-done((f32[2,256]{1,0:T(2,128)S(1)}, f32[2,256]{1,0:T(2,128)S(1)}, u32[]{:S(2)}, u32[]{:S(2)}) %collective-permute-start.13) | collective-permute-done | bytes 2080 | tf_op jit(solution)/shard_map/ppermute | solution.py:22
  141.0 1.1 collective-permute-done.16
  142.2 1.2 collective-permute-start.18
  143.4 2.6 %collective-permute-start.17 = (f32[2,256]{1,0:T(2,128)S(1)}, f32[2,256]{1,0:T(2,128)S(1)}, u32[]{:S(2)}, u32[]{:S(2)}) collective-permute-start(f32[2,256]{1,0:T(2,128)S(1)} %add.51), channel_id=1, source_target_pairs={{0,8},{2,10},{4,12},{6,14},{8,0},{10,2},{12,4},{14,6},{1,9},{3,11}... | collective-permute-start | bytes 6152 | tf_op jit(solution)/shard_map/ppermute | solution.py:22
  146.0 1.5 %collective-permute-done.18 = f32[2,256]{1,0:T(2,128)S(1)} collective-permute-done((f32[2,256]{1,0:T(2,128)S(1)}, f32[2,256]{1,0:T(2,128)S(1)}, u32[]{:S(2)}, u32[]{:S(2)}) %collective-permute-start.18) | collective-permute-done | bytes 2080 | tf_op jit(solution)/shard_map/ppermute | solution.py:22
  (55 shorter events, 5.7 us)
Async XLA Ops:
  2.3 16.8 %collective-permute-start.5 = (bf16[128,1792]{1,0:T(8,128)(2,1)}, bf16[128,1792]{1,0:T(8,128)(2,1)S(1)}, u32[]{:S(2)}, u32[]{:S(2)}) collective-permute-start(bf16[128,1792]{1,0:T(8,128)(2,1)} %get-tuple-element.5), channel_id=1, source_target_pairs={{0,12},{4,8},{8,4},{12,0},{1,13},{5,9},{9,5},{13,1},{2,14},{6,10},... | collective-permute-start | bytes 1376264 | tf_op jit(solution)/shard_map/ppermute | solution.py:22
  9.6 113.9 %collective-permute-start.14 = (bf16[128,2048]{1,0:T(8,128)(2,1)}, bf16[128,2048]{1,0:T(8,128)(2,1)S(1)}, u32[]{:S(2)}, u32[]{:S(2)}) collective-permute-start(bf16[128,2048]{1,0:T(8,128)(2,1)} %get-tuple-element.10), channel_id=1, source_target_pairs={{0,8},{4,12},{8,0},{12,4},{1,9},{5,13},{9,1},{13,5},{2,10},{6,14},... | collective-permute-start | bytes 1572872 | tf_op jit(solution)/shard_map/ppermute | solution.py:22
  9.6 112.6 %collective-permute-start.9 = (bf16[128,2048]{1,0:T(8,128)(2,1)}, bf16[128,2048]{1,0:T(8,128)(2,1)S(1)}, u32[]{:S(2)}, u32[]{:S(2)}) collective-permute-start(bf16[128,2048]{1,0:T(8,128)(2,1)} %get-tuple-element.10), channel_id=1, source_target_pairs={{0,4},{4,0},{8,12},{12,8},{1,5},{5,1},{9,13},{13,9},{2,6},{6,2},{1... | collective-permute-start | bytes 1572872 | tf_op jit(solution)/shard_map/ppermute | solution.py:22
  10.2 41.3 %collective-permute-start.1 = (bf16[128,1792]{1,0:T(8,128)(2,1)S(1)}, bf16[128,1792]{1,0:T(8,128)(2,1)S(1)}, u32[]{:S(2)}, u32[]{:S(2)}) collective-permute-start(bf16[128,1792]{1,0:T(8,128)(2,1)S(1)} %get-tuple-element.6), channel_id=1, source_target_pairs={{0,4},{4,0},{8,12},{12,8},{1,5},{5,1},{9,13},{13,9},{2,6},{6,2},{1... | collective-permute-start | bytes 1376264 | tf_op jit(solution)/shard_map/ppermute | solution.py:22
  11.7 69.9 %collective-permute-start.3 = (bf16[128,1792]{1,0:T(8,128)(2,1)}, bf16[128,1792]{1,0:T(8,128)(2,1)}, u32[]{:S(2)}, u32[]{:S(2)}) collective-permute-start(bf16[128,1792]{1,0:T(8,128)(2,1)} %get-tuple-element.7), channel_id=1, source_target_pairs={{0,8},{4,12},{8,0},{12,4},{1,9},{5,13},{9,1},{13,5},{2,10},{6,14},... | collective-permute-start | bytes 1376264 | tf_op jit(solution)/shard_map/ppermute | solution.py:22
  19.1 64.0 %collective-permute-start.6 = (bf16[128,1792]{1,0:T(8,128)(2,1)S(1)}, bf16[128,1792]{1,0:T(8,128)(2,1)S(1)}, u32[]{:S(2)}, u32[]{:S(2)}) collective-permute-start(bf16[128,1792]{1,0:T(8,128)(2,1)S(1)} %collective-permute-done.5.refs_0_), channel_id=1, source_target_pairs={{0,2},{2,0},{1,3},{3,1},{4,6},{6,4},{5,7},{7,5},{8,10},{10,8},{9,1... | collective-permute-start | bytes 1376264 | tf_op jit(solution)/shard_map/ppermute | solution.py:22
  28.7 62.8 %copy-start.3 = (f32[2,256,2048]{2,1,0:T(8,128)}, f32[2,256,2048]{2,1,0:T(8,128)S(1)}, u32[]{:S(2)}) copy-start(f32[2,256,2048]{2,1,0:T(8,128)S(1)} %shard_map.37.refs_2_.refs_3_) | copy-start | bytes 12582916
  51.5 70.0 %collective-permute-start = (bf16[128,2048]{1,0:T(8,128)(2,1)}, bf16[128,2048]{1,0:T(8,128)(2,1)S(1)}, u32[]{:S(2)}, u32[]{:S(2)}) collective-permute-start(bf16[128,2048]{1,0:T(8,128)(2,1)} %get-tuple-element.10), channel_id=1, source_target_pairs={{0,12},{4,8},{8,4},{12,0},{1,13},{5,9},{9,5},{13,1},{2,14},{6,10},... | collective-permute-start | bytes 1572872 | tf_op jit(solution)/shard_map/ppermute | solution.py:22
  81.6 28.5 %collective-permute-start.2 = (bf16[128,1792]{1,0:T(8,128)(2,1)S(1)}, bf16[128,1792]{1,0:T(8,128)(2,1)S(1)}, u32[]{:S(2)}, u32[]{:S(2)}) collective-permute-start(bf16[128,1792]{1,0:T(8,128)(2,1)S(1)} %collective-permute-done.1.refs_0_), channel_id=1, source_target_pairs={{0,2},{2,0},{1,3},{3,1},{4,6},{6,4},{5,7},{7,5},{8,10},{10,8},{9,1... | collective-permute-start | bytes 1376264 | tf_op jit(solution)/shard_map/ppermute | solution.py:22
  83.1 18.9 %collective-permute-start.4 = (bf16[128,1792]{1,0:T(8,128)(2,1)}, bf16[128,1792]{1,0:T(8,128)(2,1)S(1)}, u32[]{:S(2)}, u32[]{:S(2)}) collective-permute-start(bf16[128,1792]{1,0:T(8,128)(2,1)} %collective-permute-done.3.refs_0_), channel_id=1, source_target_pairs={{0,2},{2,0},{1,3},{3,1},{4,6},{6,4},{5,7},{7,5},{8,10},{10,8},{9,1... | collective-permute-start | bytes 1376264 | tf_op jit(solution)/shard_map/ppermute | solution.py:22
  91.5 18.5 %copy-start.7 = (f32[2,256,2048]{2,1,0:T(8,128)}, f32[2,256,2048]{2,1,0:T(8,128)S(1)}, u32[]{:S(2)}) copy-start(f32[2,256,2048]{2,1,0:T(8,128)S(1)} %shard_map.39.refs_3_.refs_2_) | copy-start | bytes 12582916
  110.0 9.5 %copy-start.5 = (f32[2,256,2048]{2,1,0:T(8,128)}, f32[2,256,2048]{2,1,0:T(8,128)S(1)}, u32[]{:S(2)}) copy-start(f32[2,256,2048]{2,1,0:T(8,128)S(1)} %shard_map.40.refs_3_.refs_2_) | copy-start | bytes 12582916
  119.5 1.9 %copy-start = (f32[2,256,2048]{2,1,0:T(8,128)}, f32[2,256,2048]{2,1,0:T(8,128)S(1)}, u32[]{:S(2)}) copy-start(f32[2,256,2048]{2,1,0:T(8,128)S(1)} %shard_map.41.refs_1_.refs_3_.refs_2_) | copy-start | bytes 12582916
  122.2 2.1 %copy-start.14 = (bf16[128,2048]{1,0:T(8,128)(2,1)S(1)}, bf16[128,2048]{1,0:T(8,128)(2,1)}, u32[]{:S(2)}) copy-start(bf16[128,2048]{1,0:T(8,128)(2,1)} %shard_map.42.refs_0_) | copy-start | bytes 1572868
  122.2 2.1 %collective-permute-start.7 = (bf16[128,2048]{1,0:T(8,128)(2,1)}, bf16[128,2048]{1,0:T(8,128)(2,1)S(1)}, u32[]{:S(2)}, u32[]{:S(2)}) collective-permute-start(bf16[128,2048]{1,0:T(8,128)(2,1)} %shard_map.42.refs_0_), channel_id=1, source_target_pairs={{0,1},{1,0},{2,3},{3,2},{4,5},{5,4},{6,7},{7,6},{8,9},{9,8},{10,11... | collective-permute-start | bytes 1572872 | tf_op jit(solution)/shard_map/ppermute | solution.py:22
  122.3 0.8 copy-start.11
  123.1 8.5 %collective-permute-start.10 = (bf16[128,2048]{1,0:T(8,128)(2,1)}, bf16[128,2048]{1,0:T(8,128)(2,1)S(1)}, u32[]{:S(2)}, u32[]{:S(2)}) collective-permute-start(bf16[128,2048]{1,0:T(8,128)(2,1)} %shard_map.44.refs_0_), channel_id=1, source_target_pairs={{0,1},{1,0},{2,3},{3,2},{4,5},{5,4},{6,7},{7,6},{8,9},{9,8},{10,11... | collective-permute-start | bytes 1572872 | tf_op jit(solution)/shard_map/ppermute | solution.py:22
  124.4 16.1 %collective-permute-start.15 = (bf16[128,2048]{1,0:T(8,128)(2,1)}, bf16[128,2048]{1,0:T(8,128)(2,1)S(1)}, u32[]{:S(2)}, u32[]{:S(2)}) collective-permute-start(bf16[128,2048]{1,0:T(8,128)(2,1)} %shard_map.46.refs_0_), channel_id=1, source_target_pairs={{0,1},{1,0},{2,3},{3,2},{4,5},{5,4},{6,7},{7,6},{8,9},{9,8},{10,11... | collective-permute-start | bytes 1572872 | tf_op jit(solution)/shard_map/ppermute | solution.py:22
  124.4 2.2 %copy-start.1 = (f32[2,256,2048]{2,1,0:T(8,128)S(1)}, f32[2,256,2048]{2,1,0:T(8,128)}, u32[]{:S(2)}) copy-start(f32[2,256,2048]{2,1,0:T(8,128)} %copy-done) | copy-start | bytes 12582916
  126.6 2.2 %copy-start.8 = (f32[2,256,2048]{2,1,0:T(8,128)S(1)}, f32[2,256,2048]{2,1,0:T(8,128)}, u32[]{:S(2)}) copy-start(f32[2,256,2048]{2,1,0:T(8,128)} %copy-done.7) | copy-start | bytes 12582916
  128.7 2.8 %copy-start.2 = (f32[2,256,2048]{2,1,0:T(8,128)S(1)}, f32[2,256,2048]{2,1,0:T(8,128)}, u32[]{:S(2)}) copy-start(f32[2,256,2048]{2,1,0:T(8,128)} %copy-done) | copy-start | bytes 12582916
  128.8 2.8 %copy-start.12 = (bf16[128,2048]{1,0:T(8,128)(2,1)S(1)}, bf16[128,2048]{1,0:T(8,128)(2,1)}, u32[]{:S(2)}) copy-start(bf16[128,2048]{1,0:T(8,128)(2,1)} %shard_map.44.refs_0_) | copy-start | bytes 1572868
  129.2 3.3 %copy-start.4 = (f32[2,256,2048]{2,1,0:T(8,128)S(1)}, f32[2,256,2048]{2,1,0:T(8,128)}, u32[]{:S(2)}) copy-start(f32[2,256,2048]{2,1,0:T(8,128)} %copy-done.3) | copy-start | bytes 12582916
  129.2 5.4 %collective-permute-start.8 = (f32[2,256]{1,0:T(2,128)S(1)}, f32[2,256]{1,0:T(2,128)S(1)}, u32[]{:S(2)}, u32[]{:S(2)}) collective-permute-start(f32[2,256]{1,0:T(2,128)S(1)} %shard_map.43), channel_id=1, source_target_pairs={{0,12},{4,8},{8,4},{12,0},{1,13},{5,9},{9,5},{13,1},{2,14},{6,10},... | collective-permute-start | bytes 6152 | tf_op jit(solution)/shard_map/ppermute | solution.py:22
  132.0 8.4 %copy-start.6 = (f32[2,256,2048]{2,1,0:T(8,128)S(1)}, f32[2,256,2048]{2,1,0:T(8,128)}, u32[]{:S(2)}) copy-start(f32[2,256,2048]{2,1,0:T(8,128)} %copy-done.5) | copy-start | bytes 12582916
  132.0 8.4 %copy-start.10 = (bf16[128,2048]{1,0:T(8,128)(2,1)S(1)}, bf16[128,2048]{1,0:T(8,128)(2,1)}, u32[]{:S(2)}) copy-start(bf16[128,2048]{1,0:T(8,128)(2,1)} %shard_map.46.refs_0_) | copy-start | bytes 1572868
  132.1 3.7 %collective-permute-start.11 = (f32[2,256]{1,0:T(2,128)S(1)}, f32[2,256]{1,0:T(2,128)S(1)}, u32[]{:S(2)}, u32[]{:S(2)}) collective-permute-start(f32[2,256]{1,0:T(2,128)S(1)} %shard_map.45), channel_id=1, source_target_pairs={{0,4},{4,0},{8,12},{12,8},{1,5},{5,1},{9,13},{13,9},{2,6},{6,2},{1... | collective-permute-start | bytes 6152 | tf_op jit(solution)/shard_map/ppermute | solution.py:22
  135.7 1.2 collective-permute-start.12
  136.9 3.6 %collective-permute-start.13 = (f32[2,256]{1,0:T(2,128)S(1)}, f32[2,256]{1,0:T(2,128)S(1)}, u32[]{:S(2)}, u32[]{:S(2)}) collective-permute-start(f32[2,256]{1,0:T(2,128)S(1)} %add.49), channel_id=1, source_target_pairs={{0,2},{2,0},{1,3},{3,1},{4,6},{6,4},{5,7},{7,5},{8,10},{10,8},{9,1... | collective-permute-start | bytes 6152 | tf_op jit(solution)/shard_map/ppermute | solution.py:22
  140.9 1.2 collective-permute-start.16
  142.2 5.4 %collective-permute-start.18 = (f32[2,256]{1,0:T(2,128)S(1)}, f32[2,256]{1,0:T(2,128)S(1)}, u32[]{:S(2)}, u32[]{:S(2)}) collective-permute-start(f32[2,256]{1,0:T(2,128)S(1)} %add.51), channel_id=1, source_target_pairs={{0,10},{2,8},{4,14},{6,12},{8,2},{10,0},{12,6},{14,4},{1,11},{3,9}... | collective-permute-start | bytes 6152 | tf_op jit(solution)/shard_map/ppermute | solution.py:22
  143.4 4.5 %collective-permute-start.17 = (f32[2,256]{1,0:T(2,128)S(1)}, f32[2,256]{1,0:T(2,128)S(1)}, u32[]{:S(2)}, u32[]{:S(2)}) collective-permute-start(f32[2,256]{1,0:T(2,128)S(1)} %add.51), channel_id=1, source_target_pairs={{0,8},{2,10},{4,12},{6,14},{8,0},{10,2},{12,4},{14,6},{1,9},{3,11}... | collective-permute-start | bytes 6152 | tf_op jit(solution)/shard_map/ppermute | solution.py:22
  (2 other events, 1.6 us)

commit v8 on v6

--- a/solution.py
+++ b/solution.py
@@ -9,7 +9,7 @@
 from jax.sharding import PartitionSpec as P
 
 
-LONG, SHORT = 40_000_000_000, 1_000_000
+LONG, SHORT = 14_000_000_000, 1_000_000
 
 
 def trade(block, steps, backwards=False):
@@ -220,7 +220,6 @@
     me, column, core = lax.axis_index("dp"), lax.axis_index("din"), lax.axis_index("dout")
     tokens, rows = activations.shape[0], queries.shape[2]
     part, half = tokens // spread, tokens // 2
-    pieces = 1
 
     def to_columns(arrived):
         return [arrived] + [trade(arrived, {"din": r}) for r in range(1, spread)]
@@ -229,7 +228,7 @@
         return block, trade(block, {"dout": 1})
 
     far, late = count - 1, count - 2
-    early = [d for d in range(1, count) if d not in (far, late)]
+    early = list(range(1, late))
 
     mine = lax.dynamic_slice_in_dim(activations, core * half, half, 0)
     hops = [(mine, mine)]
@@ -238,43 +237,40 @@
     def grads_for(device, first, size):
         return lax.dynamic_slice(out_grads, (first, device * rows), (size, rows))
 
-    arrived = {far: trade(grads_for(me ^ far, column * part, part), {"dp": far})}
-    others = early + [late]
-    sent = turned([grads_for(me ^ d, column * part, part) for d in others], [1] * len(early) + [pieces])
-    for d, block in zip(early, sent):
-        arrived[d] = trade(block, {"dp": d})
+    sent = turned([grads_for(me ^ d, column * part, part) for d in early + [late]], [1] * (len(early) + 1))
+    sent = [*sent, grads_for(me ^ far, column * part, part)]
+    arrived = {d: trade(block, {"dp": d}) for d, block in zip(early + [late, far], sent)}
 
     zero = jnp.zeros((), jnp.int32)
-    token = own_mix = mixed((activations, 0), (activations, 1), zero, queries, LONG, list(sent))
+    mix = mixed((activations, 0), (activations, 1), zero, queries, SHORT, sent)
     own, = turned([grads_for(me, 0, tokens)], [1])
-    token = scores = scores_of_grads([own], zero, own_mix, 0, 1)
-    hops[1] = hold(list(hops[1]), [own_mix])
+    token = scores = scores_of_grads([own], zero, mix, 0, 1)
+    hops[1] = hold(list(hops[1]), [mix])
     for step in range(2, count - 1):
         hops.append(pass_on(hops[-1], step, count))
 
     mixes = {}
-    for d in others:
-        block = from_partner(hops, me, d, count, [token] + list(arrived.values()) if d == late else [])
-        if d == late:
-            end = lax.ppermute(block, "dp", [(1, 0), (count - 2, count - 1)])
-            hops.append((end, end))
-        mixes[d] = mixed(*acts_of(block), core, queries, LONG if d == late else SHORT, [token])
-        token = mixes[d]
-    tail = [trade(hold([block], [mixes[early[-1]]])[0], {"dp": late}) for block in sent[len(early) :]]
-    tail = [hold([block], [token])[0] for block in tail]
-    proj = projected(to_columns(arrived[far]), column, queries, LONG, [token, scores] + tail)
-
+    for d in early:
+        mixes[d] = token = mixed(*acts_of(from_partner(hops, me, d, count)), core, queries, SHORT, [token])
+    sides = to_columns(hold([arrived[far]], list(hops[1]))[0])
+    proj = projected(sides, column, queries, SHORT, [token])
     token = proj
     for d in early:
-        token = scores_of_grads(to_columns(arrived[d]), column, mixes[d], 0, 1, [token])
+        sides = to_columns(hold([arrived[d]], list(hops[1]))[0])
+        token = scores_of_grads(sides, column, mixes[d], 0, 1, [token])
         scores = scores + trade(token, {"dp": d})
-    token = scores_of_acts(*acts_of(from_partner(hops, me, far, count, [mixes[late]])), core, proj, [token])
-    scores = over_chips(scores + trade(token, {"dp": far}), spread)
-    for piece, block in enumerate(tail):
-        term = scores_of_grads(to_columns(block), column, mixes[late], piece, pieces, [token])
-        term = term + trade(term, {"dout": 1})
-        scores = scores + sum(trade(term, {"dp": late, "din": r}) for r in range(spread))
-    return scores
+    scores = over_chips(scores, spread)
+
+    block = from_partner(hops, me, late, count, [token])
+    end = lax.ppermute(block, "dp", [(1, 0), (count - 2, count - 1)])
+    hops.append((end, end))
+    sides = to_columns(hold([arrived[late]], [proj])[0])
+    mix = mixed(*acts_of(block), core, queries, SHORT, [scores])
+    sides = sides[:1] + list(hold(sides[1:], [mix]))
+    near = trade(scores_of_grads(sides, column, mix, 0, 1, (), LONG), {"dp": late})
+    block = from_partner(hops, me, far, count, [mix])
+    total = near + trade(scores_of_acts(*acts_of(block), core, proj), {"dp": far})
+    return scores + over_chips(total, spread)
 
 
 def over_chips(scores, spread):

time: 120 us -> 119 us (level)
  starting transfers between devices: 30.7 us -> 27.3 us
  local copies, waits for them, and re-layouts: 16.6 us -> 13.6 us
  Pallas kernels: 37.6 us -> 40.5 us
  waiting for transfers between devices: 33.2 us -> 35.9 us
    ppermute x2, waiting for transfers between devices: 1.72 us -> 7.13 us  [pass_on(): lax.ppermute(block[1], 'dp', [(i, i - 1) for i in range(1, count - step +...]
    ppermute x16, starting transfers between devices: 20.4 us -> 17 us  [trade(): return lax.ppermute(block, axes, route[::-1] if backwards else route)]
    pallas_call x13, Pallas kernels: 37.6 us -> 40.5 us  [call(): pl.pallas_call(body, grid_spec=pltpu.PrefetchScalarGridSpec(num_scalar_pr...]
    ppermute x16, waiting for transfers between devices: 31.5 us -> 28.7 us  [trade(): return lax.ppermute(block, axes, route[::-1] if backwards else route)]
    unnamed x24 -> x28, local copies, waits for them, and re-layouts: 11.8 us -> 9.64 us
  transfers between devices with their start and end apart: 21 -> 21, of which waited for: 8 -> 10; matrix products, arithmetic and copies ran while one was open for 3% -> 2% of each run, Pallas kernels for 31% -> 34%
where the time goes in v8:
time: 119 us; the launch traced here: 118 us
  Pallas kernels  40.5 us (34%)
  waiting for transfers between devices  35.9 us (30%)
  starting transfers between devices  27.3 us (23%)
  local copies, waits for them, and re-layouts  13.6 us (11%)
    pallas_call x13, Pallas kernels, call(): pl.pallas_call(body, grid_spec=pltpu.PrefetchScalarGridSpec(num_scalar_pr...  40.5 us
    ppermute x16, waiting for transfers between devices, trade(): return lax.ppermute(block, axes, route[::-1] if backwards else route)  28.7 us
    ppermute x16, starting transfers between devices, trade(): return lax.ppermute(block, axes, route[::-1] if backwards else route)  17 us
    unnamed x28, local copies, waits for them, and re-layouts  9.64 us
    ppermute x2, waiting for transfers between devices, pass_on(): lax.ppermute(block[1], 'dp', [(i, i - 1) for i in range(1, count - step +...  7.13 us
    ppermute x2, starting transfers between devices, pass_on(): lax.ppermute(block[0], 'dp', [(i, i + 1) for i in range(step - 1, count -...  6.44 us
    dynamic_slice x2, local copies, waits for them, and re-layouts, grads_for(): return lax.dynamic_slice(out_grads, (first, device * rows), (size, rows))  2.79 us
    ppermute x2, starting transfers between devices, pass_on(): lax.ppermute(block[1], 'dp', [(i, i - 1) for i in range(1, count - step +...  2.57 us
  transfers between devices with their start and end apart: 21, of which 10 were waited for; matrix products, arithmetic and copies ran while one was open for 2% of the time, Pallas kernels for 34%

profile of v8, /device:TPU:0, one launch (start us, length us, event | category | flops | bytes accessed | tf_op | source)
XLA Modules:
  0.0 118.2 jit_solution(1803723522311466968)
XLA Ops:
  1.2 5.7 %collective-permute-start.1 = (bf16[128,2048]{1,0:T(8,128)(2,1)S(1)}, bf16[128,2048]{1,0:T(8,128)(2,1)}, u32[]{:S(2)}, u32[]{:S(2)}) collective-permute-start(bf16[128,2048]{1,0:T(8,128)(2,1)S(1)} %constant_dynamic-slice_fusion), channel_id=1, source_target_pairs={{0,4},{4,8},{8,12},{1,5},{5,9},{9,13},{2,6},{6,10},{10,14},{3,7},{... | collective-permute-start | bytes 1572872 | tf_op jit(solution)/shard_map/ppermute | solution.py:26
  6.9 1.3 %collective-permute-start.2 = (bf16[128,2048]{1,0:T(8,128)(2,1)S(1)}, bf16[128,2048]{1,0:T(8,128)(2,1)}, u32[]{:S(2)}, u32[]{:S(2)}) collective-permute-start(bf16[128,2048]{1,0:T(8,128)(2,1)S(1)} %constant_dynamic-slice_fusion), channel_id=1, source_target_pairs={{4,0},{8,4},{12,8},{5,1},{9,5},{13,9},{6,2},{10,6},{14,10},{7,3},{... | collective-permute-start | bytes 1572872 | tf_op jit(solution)/shard_map/ppermute | solution.py:27
  8.2 1.4 %fusion = (bf16[128,1792]{1,0:T(8,128)(2,1)S(1)}, bf16[128,1792]{1,0:T(8,128)(2,1)S(1)}, bf16[128,1792]{1,0:T(8,128)(2,1)S(1)}) fusion(bf16[256,7168]{1,0:T(8,128)(2,1)} %param.4, s32[]{:T(128)S(6)} %select_n.49, s32[]{:T(128)S(6)} %select_n.52, s32[]{:T(128)S(6)} %select_n.50, s32[]{:T(128)S(6)} %select_n.51), kind=kLoop, calls=%fused_computation.3 | loop fusion | bytes 2752528 | tf_op jit(solution)/shard_map/dynamic_slice | solution.py:238
  9.6 4.7 %collective-permute-start.5 = (bf16[128,1792]{1,0:T(8,128)(2,1)S(1)}, bf16[128,1792]{1,0:T(8,128)(2,1)S(1)}, u32[]{:S(2)}, u32[]{:S(2)}) collective-permute-start(bf16[128,1792]{1,0:T(8,128)(2,1)S(1)} %get-tuple-element.13.refs_5_), channel_id=1, source_target_pairs={{0,12},{4,8},{8,4},{12,0},{1,13},{5,9},{9,5},{13,1},{2,14},{6,10},... | collective-permute-start | bytes 1376264 | tf_op jit(solution)/shard_map/ppermute | solution.py:22
  15.3 8.0 %shard_map.39.refs_1_.refs_2_ = f32[2,1792,256]{2,1,0:T(8,128)S(1)} custom-call(s32[1]{0:T(128)} %constant.5.clone.1.where, bf16[256,2048]{1,0:T(8,128)(2,1)S(1)} %copy-done.6, bf16[256,2048]{1,0:T(8,128)(2,1)S(1)} %copy-done.6, bf16[2,1,1792,2048]{3,2,1,0:T(8,128)(2,1)} %refs_2_.7, bf16[1792,128]{1,0:T(8,128)(2,1)} %get-tuple-element.9.refs_3_, ...), custom_call_target="tpu_custom_call" | custom-call | flops 1000000 | bytes 1024 | tf_op jit(solution)/shard_map/pallas_call | solution.py:41
  23.4 1.8 %copy-done.2 = f32[2,1792,256]{2,1,0:T(8,128)} copy-done((f32[2,1792,256]{2,1,0:T(8,128)}, f32[2,1792,256]{2,1,0:T(8,128)S(1)}, u32[]{:S(2)}) %copy-start.2) | copy-done | bytes 3670040
  25.2 7.1 %collective-permute-done.2.refs_1_ = bf16[128,2048]{1,0:T(8,128)(2,1)} collective-permute-done((bf16[128,2048]{1,0:T(8,128)(2,1)S(1)}, bf16[128,2048]{1,0:T(8,128)(2,1)}, u32[]{:S(2)}, u32[]{:S(2)}) %collective-permute-start.2) | collective-permute-done | bytes 524320 | tf_op jit(solution)/shard_map/ppermute | solution.py:27
  32.3 1.2 %shard_map.43.refs_0_ = bf16[128,2048]{1,0:T(8,128)(2,1)S(1)} custom-call(s32[1]{0:T(128)} %bitcast.2.where, bf16[128,2048]{1,0:T(8,128)(2,1)} %get-tuple-element.12.refs_2_.refs_0_.refs_1_, bf16[128,2048]{1,0:T(8,128)(2,1)} %get-tuple-element.11.refs_1_.refs_2_), custom_call_target="tpu_custom_call" | custom-call | flops 1024 | bytes 1024 | tf_op jit(solution)/shard_map/pallas_call | solution.py:41
  33.6 1.3 %collective-permute-start.12 = (bf16[128,2048]{1,0:T(8,128)(2,1)}, bf16[128,2048]{1,0:T(8,128)(2,1)S(1)}, u32[]{:S(2)}, u32[]{:S(2)}) collective-permute-start(bf16[128,2048]{1,0:T(8,128)(2,1)} %get-tuple-element.12.refs_2_.refs_0_.refs_1_), channel_id=1, source_target_pairs={{4,0},{8,4},{5,1},{9,5},{6,2},{10,6},{7,3},{11,7},{20,16},{24,20},... | collective-permute-start | bytes 1572872 | tf_op jit(solution)/shard_map/ppermute | solution.py:27
  36.4 1.5 %collective-permute-start.6 = (bf16[128,1792]{1,0:T(8,128)(2,1)}, bf16[128,1792]{1,0:T(8,128)(2,1)}, u32[]{:S(2)}, u32[]{:S(2)}) collective-permute-start(bf16[128,1792]{1,0:T(8,128)(2,1)} %shard_map.45.refs_0_), channel_id=1, source_target_pairs={{0,2},{2,0},{1,3},{3,1},{4,6},{6,4},{5,7},{7,5},{8,10},{10,8},{9,1... | collective-permute-start | bytes 1376264 | tf_op jit(solution)/shard_map/ppermute | solution.py:22
  37.9 5.4 %collective-permute-done.refs_0_ = bf16[1792,128]{1,0:T(8,128)(2,1)S(1)} collective-permute-done((bf16[1792,128]{1,0:T(8,128)(2,1)}, bf16[1792,128]{1,0:T(8,128)(2,1)S(1)}, u32[]{:S(2)}, u32[]{:S(2)}) %collective-permute-start) | collective-permute-done | bytes 458784 | tf_op jit(solution)/shard_map/ppermute | solution.py:22
  44.1 1.5 %collective-permute-start.3 = (bf16[1792,128]{1,0:T(8,128)(2,1)}, bf16[1792,128]{1,0:T(8,128)(2,1)}, u32[]{:S(2)}, u32[]{:S(2)}) collective-permute-start(bf16[1792,128]{1,0:T(8,128)(2,1)} %shard_map.42.refs_0_), channel_id=1, source_target_pairs={{0,2},{2,0},{1,3},{3,1},{4,6},{6,4},{5,7},{7,5},{8,10},{10,8},{9,1... | collective-permute-start | bytes 1376264 | tf_op jit(solution)/shard_map/ppermute | solution.py:22
  46.7 1.4 %constant_dynamic-slice_fusion.1.refs_0_ = bf16[256,1792]{1,0:T(8,128)(2,1)S(1)} fusion(bf16[256,7168]{1,0:T(8,128)(2,1)} %param.4, s32[]{:T(128)S(6)} %select_n.48), kind=kLoop, calls=%fused_computation.2 | loop fusion | bytes 1835012 | tf_op jit(solution)/shard_map/dynamic_slice | solution.py:238
  49.4 7.9 %shard_map.44.refs_3_.refs_2_ = f32[2,1792,256]{2,1,0:T(8,128)S(1)} custom-call(s32[1]{0:T(128)} %bitcast.1.where, bf16[128,2048]{1,0:T(8,128)(2,1)S(1)} %shard_map.43.refs_0_, bf16[128,2048]{1,0:T(8,128)(2,1)S(1)} %collective-permute-done.4.refs_1_, bf16[2,1,1792,2048]{3,2,1,0:T(8,128)(2,1)} %refs_2_.7, f32[2,256]{1,0:T(2,128)S(1)} %shard_map.40.refs_3_), custom_call_target="tpu_custom_call" | custom-call | flops 1000000 | bytes 1024 | tf_op jit(solution)/shard_map/pallas_call | solution.py:41
  57.4 8.1 %shard_map.46.refs_3_.refs_1_.refs_2_ = f32[2,256,2048]{2,1,0:T(8,128)S(1)} custom-call(s32[1]{0:T(128)} %bitcast.where, bf16[128,1792]{1,0:T(8,128)(2,1)S(1)} %copy-done.8, bf16[128,1792]{1,0:T(8,128)(2,1)} %collective-permute-done.6.refs_1_, bf16[2,1,1792,2048]{3,2,1,0:T(8,128)(2,1)} %refs_2_.7, f32[2,1792,256]{2,1,0:T(8,128)S(1)} %shard_map.44.refs_3_.refs_2_), custom_call_target="tpu_custom_call" | custom-call | flops 1000000 | bytes 1024 | tf_op jit(solution)/shard_map/pallas_call | solution.py:41
  65.5 2.0 %shard_map.47.refs_2_ = f32[2,256]{1,0:T(2,128)S(1)} custom-call(s32[1]{0:T(128)} %bitcast.where, bf16[1792,128]{1,0:T(8,128)(2,1)S(1)} %copy-done.10, bf16[1792,128]{1,0:T(8,128)(2,1)} %collective-permute-done.3.refs_1_, f32[2,1792,256]{2,1,0:T(8,128)S(1)} %shard_map.44.refs_3_.refs_2_, f32[2,256,2048]{2,1,0:T(8,128)S(1)} %shard_map.46.refs_3_.refs_1_.refs_2_), custom_call_target="tpu_custom_call" | custom-call | flops 1024 | bytes 1024 | tf_op jit(solution)/shard_map/pallas_call | solution.py:41
  67.7 1.3 %collective-permute-start.16 = (bf16[128,2048]{1,0:T(8,128)(2,1)S(1)}, bf16[128,2048]{1,0:T(8,128)(2,1)S(1)}, u32[]{:S(2)}, u32[]{:S(2)}) collective-permute-start(bf16[128,2048]{1,0:T(8,128)(2,1)S(1)} %shard_map.49.refs_0_), channel_id=1, source_target_pairs={{4,0},{8,12},{5,1},{9,13},{6,2},{10,14},{7,3},{11,15},{20,16},{24,... | collective-permute-start | bytes 1572872 | tf_op jit(solution)/shard_map/ppermute | solution.py:265
  69.0 4.1 %collective-permute-done.10.refs_0_ = bf16[1792,128]{1,0:T(8,128)(2,1)} collective-permute-done((bf16[1792,128]{1,0:T(8,128)(2,1)}, bf16[1792,128]{1,0:T(8,128)(2,1)}, u32[]{:S(2)}, u32[]{:S(2)}) %collective-permute-start.10) | collective-permute-done | bytes 458784 | tf_op jit(solution)/shard_map/ppermute | solution.py:22
  73.1 1.5 %collective-permute-start.11 = (bf16[1792,128]{1,0:T(8,128)(2,1)}, bf16[1792,128]{1,0:T(8,128)(2,1)S(1)}, u32[]{:S(2)}, u32[]{:S(2)}) collective-permute-start(bf16[1792,128]{1,0:T(8,128)(2,1)} %shard_map.48.refs_0_), channel_id=1, source_target_pairs={{0,2},{2,0},{1,3},{3,1},{4,6},{6,4},{5,7},{7,5},{8,10},{10,8},{9,1... | collective-permute-start | bytes 1376264 | tf_op jit(solution)/shard_map/ppermute | solution.py:22
  74.6 9.7 %collective-permute-done.7 = f32[2,256]{1,0:T(2,128)S(1)} collective-permute-done((f32[2,256]{1,0:T(2,128)S(1)}, f32[2,256]{1,0:T(2,128)S(1)}, u32[]{:S(2)}, u32[]{:S(2)}) %collective-permute-start.7) | collective-permute-done | bytes 2080 | tf_op jit(solution)/shard_map/ppermute | solution.py:22
  85.4 1.5 %collective-permute-start.9 = (f32[2,256]{1,0:T(2,128)S(1)}, f32[2,256]{1,0:T(2,128)S(1)}, u32[]{:S(2)}, u32[]{:S(2)}) collective-permute-start(f32[2,256]{1,0:T(2,128)S(1)} %add.48), channel_id=1, source_target_pairs={{0,2},{2,0},{1,3},{3,1},{4,6},{6,4},{5,7},{7,5},{8,10},{10,8},{9,1... | collective-permute-start | bytes 6152 | tf_op jit(solution)/shard_map/ppermute | solution.py:22
  86.9 2.1 %collective-permute-done.9 = f32[2,256]{1,0:T(2,128)S(1)} collective-permute-done((f32[2,256]{1,0:T(2,128)S(1)}, f32[2,256]{1,0:T(2,128)S(1)}, u32[]{:S(2)}, u32[]{:S(2)}) %collective-permute-start.9) | collective-permute-done | bytes 2080 | tf_op jit(solution)/shard_map/ppermute | solution.py:22
  89.0 7.9 %shard_map.50.refs_1_.refs_2_.refs_4_ = f32[2,1792,256]{2,1,0:T(8,128)S(1)} custom-call(s32[1]{0:T(128)} %bitcast.1.where, bf16[128,2048]{1,0:T(8,128)(2,1)S(1)} %shard_map.49.refs_0_, bf16[128,2048]{1,0:T(8,128)(2,1)S(1)} %collective-permute-done.14.refs_1_, bf16[2,1,1792,2048]{3,2,1,0:T(8,128)(2,1)} %refs_2_.7, f32[2,256]{1,0:T(2,128)S(1)} %add.49.refs_3_), custom_call_target="tpu_custom_call" | custom-call | flops 1000000 | bytes 1024 | tf_op jit(solution)/shard_map/pallas_call | solution.py:41
  96.9 1.3 %shard_map.53.refs_0_ = bf16[128,2048]{1,0:T(8,128)(2,1)S(1)} custom-call(s32[1]{0:T(128)} %bitcast.4.where, bf16[128,2048]{1,0:T(8,128)(2,1)S(1)} %collective-permute-done.16.refs_0_.refs_3_, bf16[128,2048]{1,0:T(8,128)(2,1)} %get-tuple-element.12.refs_2_.refs_0_.refs_1_, bf16[128,2048]{1,0:T(8,128)(2,1)} %get-tuple-element.11.refs_1_.refs_2_, ...), custom_call_target="tpu_custom_call" | custom-call | flops 1024 | bytes 1024 | tf_op jit(solution)/shard_map/pallas_call | solution.py:41
  98.2 1.8 %copy-done.4 = f32[2,1792,256]{2,1,0:T(8,128)} copy-done((f32[2,1792,256]{2,1,0:T(8,128)}, f32[2,1792,256]{2,1,0:T(8,128)S(1)}, u32[]{:S(2)}) %copy-start.4) | copy-done | bytes 3670040
  100.8 2.0 %copy-done.5 = f32[2,1792,256]{2,1,0:T(8,128)S(1)} copy-done((f32[2,1792,256]{2,1,0:T(8,128)S(1)}, f32[2,1792,256]{2,1,0:T(8,128)}, u32[]{:S(2)}) %copy-start.5) | copy-done | bytes 3670040
  103.9 1.8 %shard_map.52 = f32[2,256]{1,0:T(2,128)S(1)} custom-call(s32[1]{0:T(128)} %bitcast.where, bf16[1792,128]{1,0:T(8,128)(2,1)} %shard_map.48.refs_0_, bf16[1792,128]{1,0:T(8,128)(2,1)S(1)} %copy-done.12, f32[2,1792,256]{2,1,0:T(8,128)S(1)} %copy-done.5), custom_call_target="tpu_custom_call" | custom-call | flops 14000000000 | bytes 1024 | tf_op jit(solution)/shard_map/pallas_call | solution.py:41
  105.7 1.2 %collective-permute-start.15 = (f32[2,256]{1,0:T(2,128)S(1)}, f32[2,256]{1,0:T(2,128)S(1)}, u32[]{:S(2)}, u32[]{:S(2)}) collective-permute-start(f32[2,256]{1,0:T(2,128)S(1)} %shard_map.52), channel_id=1, source_target_pairs={{0,8},{4,12},{8,0},{12,4},{1,9},{5,13},{9,1},{13,5},{2,10},{6,14},... | collective-permute-start | bytes 6152 | tf_op jit(solution)/shard_map/ppermute | solution.py:22
  107.4 2.4 %collective-permute-start.18 = (f32[2,256]{1,0:T(2,128)S(1)}, f32[2,256]{1,0:T(2,128)S(1)}, u32[]{:S(2)}, u32[]{:S(2)}) collective-permute-start(f32[2,256]{1,0:T(2,128)S(1)} %shard_map.54), channel_id=1, source_target_pairs={{0,12},{4,8},{8,4},{12,0},{1,13},{5,9},{9,5},{13,1},{2,14},{6,10},... | collective-permute-start | bytes 6152 | tf_op jit(solution)/shard_map/ppermute | solution.py:22
  110.3 2.6 %collective-permute-done.18 = f32[2,256]{1,0:T(2,128)S(1)} collective-permute-done((f32[2,256]{1,0:T(2,128)S(1)}, f32[2,256]{1,0:T(2,128)S(1)}, u32[]{:S(2)}, u32[]{:S(2)}) %collective-permute-start.18) | collective-permute-done | bytes 2080 | tf_op jit(solution)/shard_map/ppermute | solution.py:22
  114.0 1.5 %collective-permute-start.20 = (f32[2,256]{1,0:T(2,128)S(1)}, f32[2,256]{1,0:T(2,128)S(1)}, u32[]{:S(2)}, u32[]{:S(2)}) collective-permute-start(f32[2,256]{1,0:T(2,128)S(1)} %add.51), channel_id=1, source_target_pairs={{0,2},{2,0},{1,3},{3,1},{4,6},{6,4},{5,7},{7,5},{8,10},{10,8},{9,1... | collective-permute-start | bytes 6152 | tf_op jit(solution)/shard_map/ppermute | solution.py:22
  115.5 2.1 %collective-permute-done.20 = f32[2,256]{1,0:T(2,128)S(1)} collective-permute-done((f32[2,256]{1,0:T(2,128)S(1)}, f32[2,256]{1,0:T(2,128)S(1)}, u32[]{:S(2)}, u32[]{:S(2)}) %collective-permute-start.20) | collective-permute-done | bytes 2080 | tf_op jit(solution)/shard_map/ppermute | solution.py:22
  (65 shorter events, 12.7 us)
Async XLA Ops:
  0.0 15.3 %copy-start.6 = (bf16[256,2048]{1,0:T(8,128)(2,1)S(1)}, bf16[256,2048]{1,0:T(8,128)(2,1)}, u32[]{:S(2)}) copy-start(bf16[256,2048]{1,0:T(8,128)(2,1)} %refs_1_.1) | copy-start | bytes 3145732
  1.2 24.0 %collective-permute-start.1 = (bf16[128,2048]{1,0:T(8,128)(2,1)S(1)}, bf16[128,2048]{1,0:T(8,128)(2,1)}, u32[]{:S(2)}, u32[]{:S(2)}) collective-permute-start(bf16[128,2048]{1,0:T(8,128)(2,1)S(1)} %constant_dynamic-slice_fusion), channel_id=1, source_target_pairs={{0,4},{4,8},{8,12},{1,5},{5,9},{9,13},{2,6},{6,10},{10,14},{3,7},{... | collective-permute-start | bytes 1572872 | tf_op jit(solution)/shard_map/ppermute | solution.py:26
  6.9 25.4 %collective-permute-start.2 = (bf16[128,2048]{1,0:T(8,128)(2,1)S(1)}, bf16[128,2048]{1,0:T(8,128)(2,1)}, u32[]{:S(2)}, u32[]{:S(2)}) collective-permute-start(bf16[128,2048]{1,0:T(8,128)(2,1)S(1)} %constant_dynamic-slice_fusion), channel_id=1, source_target_pairs={{4,0},{8,4},{12,8},{5,1},{9,5},{13,9},{6,2},{10,6},{14,10},{7,3},{... | collective-permute-start | bytes 1572872 | tf_op jit(solution)/shard_map/ppermute | solution.py:27
  9.6 26.0 %collective-permute-start.5 = (bf16[128,1792]{1,0:T(8,128)(2,1)S(1)}, bf16[128,1792]{1,0:T(8,128)(2,1)S(1)}, u32[]{:S(2)}, u32[]{:S(2)}) collective-permute-start(bf16[128,1792]{1,0:T(8,128)(2,1)S(1)} %get-tuple-element.13.refs_5_), channel_id=1, source_target_pairs={{0,12},{4,8},{8,4},{12,0},{1,13},{5,9},{9,5},{13,1},{2,14},{6,10},... | collective-permute-start | bytes 1376264 | tf_op jit(solution)/shard_map/ppermute | solution.py:22
  15.3 8.1 %copy-start.13 = (bf16[1792,128]{1,0:T(8,128)(2,1)}, bf16[1792,128]{1,0:T(8,128)(2,1)S(1)}, u32[]{:S(2)}) copy-start(bf16[1792,128]{1,0:T(8,128)(2,1)S(1)} %get-tuple-element.10.refs_4_) | copy-start | bytes 1376260
  15.3 28.0 %collective-permute-start = (bf16[1792,128]{1,0:T(8,128)(2,1)}, bf16[1792,128]{1,0:T(8,128)(2,1)S(1)}, u32[]{:S(2)}, u32[]{:S(2)}) collective-permute-start(bf16[1792,128]{1,0:T(8,128)(2,1)} %get-tuple-element.9.refs_3_), channel_id=1, source_target_pairs={{0,4},{4,0},{8,12},{12,8},{1,5},{5,1},{9,13},{13,9},{2,6},{6,2},{1... | collective-permute-start | bytes 1376264 | tf_op jit(solution)/shard_map/ppermute | solution.py:22
  23.4 1.8 %copy-start.2 = (f32[2,1792,256]{2,1,0:T(8,128)}, f32[2,1792,256]{2,1,0:T(8,128)S(1)}, u32[]{:S(2)}) copy-start(f32[2,1792,256]{2,1,0:T(8,128)S(1)} %shard_map.39.refs_1_.refs_2_) | copy-start | bytes 11010052
  33.5 12.0 %collective-permute-start.4 = (bf16[128,2048]{1,0:T(8,128)(2,1)S(1)}, bf16[128,2048]{1,0:T(8,128)(2,1)S(1)}, u32[]{:S(2)}, u32[]{:S(2)}) collective-permute-start(bf16[128,2048]{1,0:T(8,128)(2,1)S(1)} %shard_map.43.refs_0_), channel_id=1, source_target_pairs={{0,1},{1,0},{2,3},{3,2},{4,5},{5,4},{6,7},{7,6},{8,9},{9,8},{10,11... | collective-permute-start | bytes 1572872 | tf_op jit(solution)/shard_map/ppermute | solution.py:22
  33.6 33.9 %collective-permute-start.12 = (bf16[128,2048]{1,0:T(8,128)(2,1)}, bf16[128,2048]{1,0:T(8,128)(2,1)S(1)}, u32[]{:S(2)}, u32[]{:S(2)}) collective-permute-start(bf16[128,2048]{1,0:T(8,128)(2,1)} %get-tuple-element.12.refs_2_.refs_0_.refs_1_), channel_id=1, source_target_pairs={{4,0},{8,4},{5,1},{9,5},{6,2},{10,6},{7,3},{11,7},{20,16},{24,20},... | collective-permute-start | bytes 1572872 | tf_op jit(solution)/shard_map/ppermute | solution.py:27
  34.9 32.7 %collective-permute-start.13 = (bf16[128,2048]{1,0:T(8,128)(2,1)}, bf16[128,2048]{1,0:T(8,128)(2,1)S(1)}, u32[]{:S(2)}, u32[]{:S(2)}) collective-permute-start(bf16[128,2048]{1,0:T(8,128)(2,1)} %get-tuple-element.11.refs_1_.refs_2_), channel_id=1, source_target_pairs={{4,8},{8,12},{5,9},{9,13},{6,10},{10,14},{7,11},{11,15},{20,24},{2... | collective-permute-start | bytes 1572872 | tf_op jit(solution)/shard_map/ppermute | solution.py:26
  36.4 21.0 %collective-permute-start.6 = (bf16[128,1792]{1,0:T(8,128)(2,1)}, bf16[128,1792]{1,0:T(8,128)(2,1)}, u32[]{:S(2)}, u32[]{:S(2)}) collective-permute-start(bf16[128,1792]{1,0:T(8,128)(2,1)} %shard_map.45.refs_0_), channel_id=1, source_target_pairs={{0,2},{2,0},{1,3},{3,1},{4,6},{6,4},{5,7},{7,5},{8,10},{10,8},{9,1... | collective-permute-start | bytes 1376264 | tf_op jit(solution)/shard_map/ppermute | solution.py:22
  44.1 21.4 %collective-permute-start.3 = (bf16[1792,128]{1,0:T(8,128)(2,1)}, bf16[1792,128]{1,0:T(8,128)(2,1)}, u32[]{:S(2)}, u32[]{:S(2)}) collective-permute-start(bf16[1792,128]{1,0:T(8,128)(2,1)} %shard_map.42.refs_0_), channel_id=1, source_target_pairs={{0,2},{2,0},{1,3},{3,1},{4,6},{6,4},{5,7},{7,5},{8,10},{10,8},{9,1... | collective-permute-start | bytes 1376264 | tf_op jit(solution)/shard_map/ppermute | solution.py:22
  45.6 27.5 %collective-permute-start.10 = (bf16[1792,128]{1,0:T(8,128)(2,1)}, bf16[1792,128]{1,0:T(8,128)(2,1)}, u32[]{:S(2)}, u32[]{:S(2)}) collective-permute-start(bf16[1792,128]{1,0:T(8,128)(2,1)} %copy-done.13), channel_id=1, source_target_pairs={{0,8},{4,12},{8,0},{12,4},{1,9},{5,13},{9,1},{13,5},{2,10},{6,14},... | collective-permute-start | bytes 1376264 | tf_op jit(solution)/shard_map/ppermute | solution.py:22
  46.7 2.3 %copy-start.3 = (f32[2,1792,256]{2,1,0:T(8,128)S(1)}, f32[2,1792,256]{2,1,0:T(8,128)}, u32[]{:S(2)}) copy-start(f32[2,1792,256]{2,1,0:T(8,128)} %copy-done.2) | copy-start | bytes 11010052
  49.4 8.0 %copy-start.8 = (bf16[128,1792]{1,0:T(8,128)(2,1)S(1)}, bf16[128,1792]{1,0:T(8,128)(2,1)}, u32[]{:S(2)}) copy-start(bf16[128,1792]{1,0:T(8,128)(2,1)} %shard_map.45.refs_0_) | copy-start | bytes 1376260
  57.4 8.1 %copy-start.10 = (bf16[1792,128]{1,0:T(8,128)(2,1)S(1)}, bf16[1792,128]{1,0:T(8,128)(2,1)}, u32[]{:S(2)}) copy-start(bf16[1792,128]{1,0:T(8,128)(2,1)} %shard_map.42.refs_0_) | copy-start | bytes 1376260
  65.5 2.1 %copy-start = (f32[2,256,2048]{2,1,0:T(8,128)}, f32[2,256,2048]{2,1,0:T(8,128)S(1)}, u32[]{:S(2)}) copy-start(f32[2,256,2048]{2,1,0:T(8,128)S(1)} %shard_map.46.refs_3_.refs_1_.refs_2_) | copy-start | bytes 12582916
  67.6 21.4 %collective-permute-start.14 = (bf16[128,2048]{1,0:T(8,128)(2,1)S(1)}, bf16[128,2048]{1,0:T(8,128)(2,1)S(1)}, u32[]{:S(2)}, u32[]{:S(2)}) collective-permute-start(bf16[128,2048]{1,0:T(8,128)(2,1)S(1)} %shard_map.49.refs_0_), channel_id=1, source_target_pairs={{0,1},{1,0},{2,3},{3,2},{4,5},{5,4},{6,7},{7,6},{8,9},{9,8},{10,11... | collective-permute-start | bytes 1572872 | tf_op jit(solution)/shard_map/ppermute | solution.py:22
  67.7 29.2 %collective-permute-start.16 = (bf16[128,2048]{1,0:T(8,128)(2,1)S(1)}, bf16[128,2048]{1,0:T(8,128)(2,1)S(1)}, u32[]{:S(2)}, u32[]{:S(2)}) collective-permute-start(bf16[128,2048]{1,0:T(8,128)(2,1)S(1)} %shard_map.49.refs_0_), channel_id=1, source_target_pairs={{4,0},{8,12},{5,1},{9,13},{6,2},{10,14},{7,3},{11,15},{20,16},{24,... | collective-permute-start | bytes 1572872 | tf_op jit(solution)/shard_map/ppermute | solution.py:265
  73.1 26.9 %collective-permute-start.11 = (bf16[1792,128]{1,0:T(8,128)(2,1)}, bf16[1792,128]{1,0:T(8,128)(2,1)S(1)}, u32[]{:S(2)}, u32[]{:S(2)}) collective-permute-start(bf16[1792,128]{1,0:T(8,128)(2,1)} %shard_map.48.refs_0_), channel_id=1, source_target_pairs={{0,2},{2,0},{1,3},{3,1},{4,6},{6,4},{5,7},{7,5},{8,10},{10,8},{9,1... | collective-permute-start | bytes 1376264 | tf_op jit(solution)/shard_map/ppermute | solution.py:22
  74.6 9.7 %collective-permute-start.7 = (f32[2,256]{1,0:T(2,128)S(1)}, f32[2,256]{1,0:T(2,128)S(1)}, u32[]{:S(2)}, u32[]{:S(2)}) collective-permute-start(f32[2,256]{1,0:T(2,128)S(1)} %shard_map.47.refs_2_), channel_id=1, source_target_pairs={{0,4},{4,0},{8,12},{12,8},{1,5},{5,1},{9,13},{13,9},{2,6},{6,2},{1... | collective-permute-start | bytes 6152 | tf_op jit(solution)/shard_map/ppermute | solution.py:22
  84.2 1.2 collective-permute-start.8
  85.4 3.6 %collective-permute-start.9 = (f32[2,256]{1,0:T(2,128)S(1)}, f32[2,256]{1,0:T(2,128)S(1)}, u32[]{:S(2)}, u32[]{:S(2)}) collective-permute-start(f32[2,256]{1,0:T(2,128)S(1)} %add.48), channel_id=1, source_target_pairs={{0,2},{2,0},{1,3},{3,1},{4,6},{6,4},{5,7},{7,5},{8,10},{10,8},{9,1... | collective-permute-start | bytes 6152 | tf_op jit(solution)/shard_map/ppermute | solution.py:22
  98.2 1.8 %copy-start.4 = (f32[2,1792,256]{2,1,0:T(8,128)}, f32[2,1792,256]{2,1,0:T(8,128)S(1)}, u32[]{:S(2)}) copy-start(f32[2,1792,256]{2,1,0:T(8,128)S(1)} %shard_map.50.refs_1_.refs_2_.refs_4_) | copy-start | bytes 11010052
  100.0 7.0 %collective-permute-start.17 = (bf16[128,2048]{1,0:T(8,128)(2,1)S(1)}, bf16[128,2048]{1,0:T(8,128)(2,1)S(1)}, u32[]{:S(2)}, u32[]{:S(2)}) collective-permute-start(bf16[128,2048]{1,0:T(8,128)(2,1)S(1)} %shard_map.53.refs_0_), channel_id=1, source_target_pairs={{0,1},{1,0},{2,3},{3,2},{4,5},{5,4},{6,7},{7,6},{8,9},{9,8},{10,11... | collective-permute-start | bytes 1572872 | tf_op jit(solution)/shard_map/ppermute | solution.py:22
  100.8 2.0 %copy-start.5 = (f32[2,1792,256]{2,1,0:T(8,128)S(1)}, f32[2,1792,256]{2,1,0:T(8,128)}, u32[]{:S(2)}) copy-start(f32[2,1792,256]{2,1,0:T(8,128)} %copy-done.4) | copy-start | bytes 11010052
  102.9 1.0 copy-start.12
  103.9 3.1 %copy-start.1 = (f32[2,256,2048]{2,1,0:T(8,128)S(1)}, f32[2,256,2048]{2,1,0:T(8,128)}, u32[]{:S(2)}) copy-start(f32[2,256,2048]{2,1,0:T(8,128)} %copy-done) | copy-start | bytes 12582916
  105.7 4.5 %collective-permute-start.15 = (f32[2,256]{1,0:T(2,128)S(1)}, f32[2,256]{1,0:T(2,128)S(1)}, u32[]{:S(2)}, u32[]{:S(2)}) collective-permute-start(f32[2,256]{1,0:T(2,128)S(1)} %shard_map.52), channel_id=1, source_target_pairs={{0,8},{4,12},{8,0},{12,4},{1,9},{5,13},{9,1},{13,5},{2,10},{6,14},... | collective-permute-start | bytes 6152 | tf_op jit(solution)/shard_map/ppermute | solution.py:22
  107.4 5.4 %collective-permute-start.18 = (f32[2,256]{1,0:T(2,128)S(1)}, f32[2,256]{1,0:T(2,128)S(1)}, u32[]{:S(2)}, u32[]{:S(2)}) collective-permute-start(f32[2,256]{1,0:T(2,128)S(1)} %shard_map.54), channel_id=1, source_target_pairs={{0,12},{4,8},{8,4},{12,0},{1,13},{5,9},{9,5},{13,1},{2,14},{6,10},... | collective-permute-start | bytes 6152 | tf_op jit(solution)/shard_map/ppermute | solution.py:22
  112.9 1.2 collective-permute-start.19
  114.0 3.6 %collective-permute-start.20 = (f32[2,256]{1,0:T(2,128)S(1)}, f32[2,256]{1,0:T(2,128)S(1)}, u32[]{:S(2)}, u32[]{:S(2)}) collective-permute-start(f32[2,256]{1,0:T(2,128)S(1)} %add.51), channel_id=1, source_target_pairs={{0,2},{2,0},{1,3},{3,1},{4,6},{6,4},{5,7},{7,5},{8,10},{10,8},{9,1... | collective-permute-start | bytes 6152 | tf_op jit(solution)/shard_map/ppermute | solution.py:22
  (3 other events, 2.4 us)

commit v9 on v8

--- a/solution.py
+++ b/solution.py
@@ -259,18 +259,17 @@
         sides = to_columns(hold([arrived[d]], list(hops[1]))[0])
         token = scores_of_grads(sides, column, mixes[d], 0, 1, [token])
         scores = scores + trade(token, {"dp": d})
-    scores = over_chips(scores, spread)
 
     block = from_partner(hops, me, late, count, [token])
     end = lax.ppermute(block, "dp", [(1, 0), (count - 2, count - 1)])
     hops.append((end, end))
     sides = to_columns(hold([arrived[late]], [proj])[0])
-    mix = mixed(*acts_of(block), core, queries, SHORT, [scores])
+    mix = mixed(*acts_of(block), core, queries, SHORT, [token])
     sides = sides[:1] + list(hold(sides[1:], [mix]))
     near = trade(scores_of_grads(sides, column, mix, 0, 1, (), LONG), {"dp": late})
     block = from_partner(hops, me, far, count, [mix])
-    total = near + trade(scores_of_acts(*acts_of(block), core, proj), {"dp": far})
-    return scores + over_chips(total, spread)
+    scores = scores + near + trade(scores_of_acts(*acts_of(block), core, proj), {"dp": far})
+    return over_chips(scores, spread)
 
 
 def over_chips(scores, spread):

time: 119 us -> 106 us (0.89)
  waiting for transfers between devices: 35.9 us -> 24.7 us
  starting transfers between devices: 27.3 us -> 25.8 us
    ppermute x16 -> x14, waiting for transfers between devices: 28.7 us -> 15.8 us  [trade(): return lax.ppermute(block, axes, route[::-1] if backwards else route)]
    ppermute x1, waiting for transfers between devices: 0.01 us -> 1.75 us  [on_device(): end = lax.ppermute(block, 'dp', [(1, 0), (count - 2, count - 1)])]
    ppermute x16 -> x14, starting transfers between devices: 17 us -> 15.5 us  [trade(): return lax.ppermute(block, axes, route[::-1] if backwards else route)]
  transfers between devices with their start and end apart: 21 -> 19, of which waited for: 10 -> 8; matrix products, arithmetic and copies ran while one was open for 2% -> 3% of each run, Pallas kernels for 34% -> 38%
where the time goes in v9:
time: 106 us
  Pallas kernels  40.5 us (38%)
  starting transfers between devices  25.8 us (24%)
  waiting for transfers between devices  24.7 us (23%)
  local copies, waits for them, and re-layouts  13.6 us (13%)
    pallas_call x13, Pallas kernels, call(): pl.pallas_call(body, grid_spec=pltpu.PrefetchScalarGridSpec(num_scalar_pr...  40.5 us
    ppermute x14, waiting for transfers between devices, trade(): return lax.ppermute(block, axes, route[::-1] if backwards else route)  15.8 us
    ppermute x14, starting transfers between devices, trade(): return lax.ppermute(block, axes, route[::-1] if backwards else route)  15.5 us
    unnamed x28, local copies, waits for them, and re-layouts  9.65 us
    ppermute x2, waiting for transfers between devices, pass_on(): lax.ppermute(block[1], 'dp', [(i, i - 1) for i in range(1, count - step +...  7.13 us
    ppermute x2, starting transfers between devices, pass_on(): lax.ppermute(block[0], 'dp', [(i, i + 1) for i in range(step - 1, count -...  6.45 us
    dynamic_slice x2, local copies, waits for them, and re-layouts, grads_for(): return lax.dynamic_slice(out_grads, (first, device * rows), (size, rows))  2.79 us
    ppermute x2, starting transfers between devices, pass_on(): lax.ppermute(block[1], 'dp', [(i, i - 1) for i in range(1, count - step +...  2.57 us
  transfers between devices with their start and end apart: 19, of which 8 were waited for; matrix products, arithmetic and copies ran while one was open for 3% of the time, Pallas kernels for 38%

profile of v9, /device:TPU:0, one launch (start us, length us, event | category | flops | bytes accessed | tf_op | source)
XLA Modules:
  0.0 105.5 jit_solution(17482678111084689831)
XLA Ops:
  0.0 1.2 %constant_dynamic-slice_fusion = bf16[128,2048]{1,0:T(8,128)(2,1)S(1)} fusion(bf16[256,2048]{1,0:T(8,128)(2,1)} %refs_1_.1, s32[]{:T(128)S(6)} %select_n.53), kind=kLoop, calls=%fused_computation.1 | loop fusion | bytes 1048580 | tf_op jit(solution)/shard_map/dynamic_slice | solution.py:233
  1.2 5.8 %collective-permute-start.1 = (bf16[128,2048]{1,0:T(8,128)(2,1)S(1)}, bf16[128,2048]{1,0:T(8,128)(2,1)}, u32[]{:S(2)}, u32[]{:S(2)}) collective-permute-start(bf16[128,2048]{1,0:T(8,128)(2,1)S(1)} %constant_dynamic-slice_fusion), channel_id=1, source_target_pairs={{0,4},{4,8},{8,12},{1,5},{5,9},{9,13},{2,6},{6,10},{10,14},{3,7},{... | collective-permute-start | bytes 1572872 | tf_op jit(solution)/shard_map/ppermute | solution.py:26
  6.9 1.3 %collective-permute-start.2 = (bf16[128,2048]{1,0:T(8,128)(2,1)S(1)}, bf16[128,2048]{1,0:T(8,128)(2,1)}, u32[]{:S(2)}, u32[]{:S(2)}) collective-permute-start(bf16[128,2048]{1,0:T(8,128)(2,1)S(1)} %constant_dynamic-slice_fusion), channel_id=1, source_target_pairs={{4,0},{8,4},{12,8},{5,1},{9,5},{13,9},{6,2},{10,6},{14,10},{7,3},{... | collective-permute-start | bytes 1572872 | tf_op jit(solution)/shard_map/ppermute | solution.py:27
  8.2 1.4 %fusion = (bf16[128,1792]{1,0:T(8,128)(2,1)S(1)}, bf16[128,1792]{1,0:T(8,128)(2,1)S(1)}, bf16[128,1792]{1,0:T(8,128)(2,1)S(1)}) fusion(bf16[256,7168]{1,0:T(8,128)(2,1)} %param.4, s32[]{:T(128)S(6)} %select_n.49, s32[]{:T(128)S(6)} %select_n.52, s32[]{:T(128)S(6)} %select_n.50, s32[]{:T(128)S(6)} %select_n.51), kind=kLoop, calls=%fused_computation.3 | loop fusion | bytes 2752528 | tf_op jit(solution)/shard_map/dynamic_slice | solution.py:238
  9.6 4.7 %collective-permute-start.5 = (bf16[128,1792]{1,0:T(8,128)(2,1)S(1)}, bf16[128,1792]{1,0:T(8,128)(2,1)S(1)}, u32[]{:S(2)}, u32[]{:S(2)}) collective-permute-start(bf16[128,1792]{1,0:T(8,128)(2,1)S(1)} %get-tuple-element.13.refs_5_), channel_id=1, source_target_pairs={{0,12},{4,8},{8,4},{12,0},{1,13},{5,9},{9,5},{13,1},{2,14},{6,10},... | collective-permute-start | bytes 1376264 | tf_op jit(solution)/shard_map/ppermute | solution.py:22
  15.3 8.0 %shard_map.39.refs_1_.refs_2_ = f32[2,1792,256]{2,1,0:T(8,128)S(1)} custom-call(s32[1]{0:T(128)} %constant.5.clone.1.where, bf16[256,2048]{1,0:T(8,128)(2,1)S(1)} %copy-done.6, bf16[256,2048]{1,0:T(8,128)(2,1)S(1)} %copy-done.6, bf16[2,1,1792,2048]{3,2,1,0:T(8,128)(2,1)} %refs_2_.7, bf16[1792,128]{1,0:T(8,128)(2,1)} %get-tuple-element.9.refs_3_, ...), custom_call_target="tpu_custom_call" | custom-call | flops 1000000 | bytes 1024 | tf_op jit(solution)/shard_map/pallas_call | solution.py:41
  23.4 1.8 %copy-done.2 = f32[2,1792,256]{2,1,0:T(8,128)} copy-done((f32[2,1792,256]{2,1,0:T(8,128)}, f32[2,1792,256]{2,1,0:T(8,128)S(1)}, u32[]{:S(2)}) %copy-start.2) | copy-done | bytes 3670040
  25.2 7.1 %collective-permute-done.2.refs_1_ = bf16[128,2048]{1,0:T(8,128)(2,1)} collective-permute-done((bf16[128,2048]{1,0:T(8,128)(2,1)S(1)}, bf16[128,2048]{1,0:T(8,128)(2,1)}, u32[]{:S(2)}, u32[]{:S(2)}) %collective-permute-start.2) | collective-permute-done | bytes 524320 | tf_op jit(solution)/shard_map/ppermute | solution.py:27
  32.3 1.2 %shard_map.43.refs_0_ = bf16[128,2048]{1,0:T(8,128)(2,1)S(1)} custom-call(s32[1]{0:T(128)} %bitcast.2.where, bf16[128,2048]{1,0:T(8,128)(2,1)} %get-tuple-element.12.refs_2_.refs_0_.refs_1_, bf16[128,2048]{1,0:T(8,128)(2,1)} %get-tuple-element.11.refs_1_.refs_2_), custom_call_target="tpu_custom_call" | custom-call | flops 1024 | bytes 1024 | tf_op jit(solution)/shard_map/pallas_call | solution.py:41
  33.6 1.3 %collective-permute-start.10 = (bf16[128,2048]{1,0:T(8,128)(2,1)}, bf16[128,2048]{1,0:T(8,128)(2,1)S(1)}, u32[]{:S(2)}, u32[]{:S(2)}) collective-permute-start(bf16[128,2048]{1,0:T(8,128)(2,1)} %get-tuple-element.12.refs_2_.refs_0_.refs_1_), channel_id=1, source_target_pairs={{4,0},{8,4},{5,1},{9,5},{6,2},{10,6},{7,3},{11,7},{20,16},{24,20},... | collective-permute-start | bytes 1572872 | tf_op jit(solution)/shard_map/ppermute | solution.py:27
  36.4 1.5 %collective-permute-start.6 = (bf16[128,1792]{1,0:T(8,128)(2,1)}, bf16[128,1792]{1,0:T(8,128)(2,1)}, u32[]{:S(2)}, u32[]{:S(2)}) collective-permute-start(bf16[128,1792]{1,0:T(8,128)(2,1)} %shard_map.45.refs_0_), channel_id=1, source_target_pairs={{0,2},{2,0},{1,3},{3,1},{4,6},{6,4},{5,7},{7,5},{8,10},{10,8},{9,1... | collective-permute-start | bytes 1376264 | tf_op jit(solution)/shard_map/ppermute | solution.py:22
  37.9 5.4 %collective-permute-done.refs_0_ = bf16[1792,128]{1,0:T(8,128)(2,1)S(1)} collective-permute-done((bf16[1792,128]{1,0:T(8,128)(2,1)}, bf16[1792,128]{1,0:T(8,128)(2,1)S(1)}, u32[]{:S(2)}, u32[]{:S(2)}) %collective-permute-start) | collective-permute-done | bytes 458784 | tf_op jit(solution)/shard_map/ppermute | solution.py:22
  44.1 1.5 %collective-permute-start.3 = (bf16[1792,128]{1,0:T(8,128)(2,1)}, bf16[1792,128]{1,0:T(8,128)(2,1)}, u32[]{:S(2)}, u32[]{:S(2)}) collective-permute-start(bf16[1792,128]{1,0:T(8,128)(2,1)} %shard_map.42.refs_0_), channel_id=1, source_target_pairs={{0,2},{2,0},{1,3},{3,1},{4,6},{6,4},{5,7},{7,5},{8,10},{10,8},{9,1... | collective-permute-start | bytes 1376264 | tf_op jit(solution)/shard_map/ppermute | solution.py:22
  46.7 1.4 %constant_dynamic-slice_fusion.1.refs_0_ = bf16[256,1792]{1,0:T(8,128)(2,1)S(1)} fusion(bf16[256,7168]{1,0:T(8,128)(2,1)} %param.4, s32[]{:T(128)S(6)} %select_n.48), kind=kLoop, calls=%fused_computation.2 | loop fusion | bytes 1835012 | tf_op jit(solution)/shard_map/dynamic_slice | solution.py:238
  49.4 7.9 %shard_map.44.refs_3_.refs_2_ = f32[2,1792,256]{2,1,0:T(8,128)S(1)} custom-call(s32[1]{0:T(128)} %bitcast.1.where, bf16[128,2048]{1,0:T(8,128)(2,1)S(1)} %shard_map.43.refs_0_, bf16[128,2048]{1,0:T(8,128)(2,1)S(1)} %collective-permute-done.4.refs_1_, bf16[2,1,1792,2048]{3,2,1,0:T(8,128)(2,1)} %refs_2_.7, f32[2,256]{1,0:T(2,128)S(1)} %shard_map.40.refs_3_), custom_call_target="tpu_custom_call" | custom-call | flops 1000000 | bytes 1024 | tf_op jit(solution)/shard_map/pallas_call | solution.py:41
  57.4 8.1 %shard_map.46.refs_3_.refs_1_.refs_2_ = f32[2,256,2048]{2,1,0:T(8,128)S(1)} custom-call(s32[1]{0:T(128)} %bitcast.where, bf16[128,1792]{1,0:T(8,128)(2,1)S(1)} %copy-done.8, bf16[128,1792]{1,0:T(8,128)(2,1)} %collective-permute-done.6.refs_1_, bf16[2,1,1792,2048]{3,2,1,0:T(8,128)(2,1)} %refs_2_.7, f32[2,1792,256]{2,1,0:T(8,128)S(1)} %shard_map.44.refs_3_.refs_2_), custom_call_target="tpu_custom_call" | custom-call | flops 1000000 | bytes 1024 | tf_op jit(solution)/shard_map/pallas_call | solution.py:41
  65.5 2.0 %shard_map.47.refs_2_.refs_3_ = f32[2,256]{1,0:T(2,128)S(1)} custom-call(s32[1]{0:T(128)} %bitcast.where, bf16[1792,128]{1,0:T(8,128)(2,1)S(1)} %copy-done.10, bf16[1792,128]{1,0:T(8,128)(2,1)} %collective-permute-done.3.refs_1_, f32[2,1792,256]{2,1,0:T(8,128)S(1)} %shard_map.44.refs_3_.refs_2_, f32[2,256,2048]{2,1,0:T(8,128)S(1)} %shard_map.46.refs_3_.refs_1_.refs_2_), custom_call_target="tpu_custom_call" | custom-call | flops 1024 | bytes 1024 | tf_op jit(solution)/shard_map/pallas_call | solution.py:41
  67.7 1.3 %collective-permute-start.14 = (bf16[128,2048]{1,0:T(8,128)(2,1)S(1)}, bf16[128,2048]{1,0:T(8,128)(2,1)S(1)}, u32[]{:S(2)}, u32[]{:S(2)}) collective-permute-start(bf16[128,2048]{1,0:T(8,128)(2,1)S(1)} %shard_map.49.refs_0_), channel_id=1, source_target_pairs={{4,0},{8,12},{5,1},{9,13},{6,2},{10,14},{7,3},{11,15},{20,16},{24,... | collective-permute-start | bytes 1572872 | tf_op jit(solution)/shard_map/ppermute | solution.py:264
  69.0 4.1 %collective-permute-done.8.refs_0_ = bf16[1792,128]{1,0:T(8,128)(2,1)} collective-permute-done((bf16[1792,128]{1,0:T(8,128)(2,1)}, bf16[1792,128]{1,0:T(8,128)(2,1)}, u32[]{:S(2)}, u32[]{:S(2)}) %collective-permute-start.8) | collective-permute-done | bytes 458784 | tf_op jit(solution)/shard_map/ppermute | solution.py:22
  73.1 1.5 %collective-permute-start.9 = (bf16[1792,128]{1,0:T(8,128)(2,1)}, bf16[1792,128]{1,0:T(8,128)(2,1)S(1)}, u32[]{:S(2)}, u32[]{:S(2)}) collective-permute-start(bf16[1792,128]{1,0:T(8,128)(2,1)} %shard_map.48.refs_0_), channel_id=1, source_target_pairs={{0,2},{2,0},{1,3},{3,1},{4,6},{6,4},{5,7},{7,5},{8,10},{10,8},{9,1... | collective-permute-start | bytes 1376264 | tf_op jit(solution)/shard_map/ppermute | solution.py:22
  74.6 7.9 %shard_map.50.refs_1_.refs_2_.refs_4_ = f32[2,1792,256]{2,1,0:T(8,128)S(1)} custom-call(s32[1]{0:T(128)} %bitcast.1.where, bf16[128,2048]{1,0:T(8,128)(2,1)S(1)} %shard_map.49.refs_0_, bf16[128,2048]{1,0:T(8,128)(2,1)S(1)} %collective-permute-done.12.refs_1_, bf16[2,1,1792,2048]{3,2,1,0:T(8,128)(2,1)} %refs_2_.7, f32[2,256]{1,0:T(2,128)S(1)} %shard_map.47.refs_2_.refs_3_), custom_call_target="tpu_custom_call" | custom-call | flops 1000000 | bytes 1024 | tf_op jit(solution)/shard_map/pallas_call | solution.py:41
  82.5 1.8 %collective-permute-done.14.refs_0_.refs_3_ = bf16[128,2048]{1,0:T(8,128)(2,1)S(1)} collective-permute-done((bf16[128,2048]{1,0:T(8,128)(2,1)S(1)}, bf16[128,2048]{1,0:T(8,128)(2,1)S(1)}, u32[]{:S(2)}, u32[]{:S(2)}) %collective-permute-start.14) | collective-permute-done | bytes 524320 | tf_op jit(solution)/shard_map/ppermute | solution.py:264
  84.2 1.3 %shard_map.53.refs_0_ = bf16[128,2048]{1,0:T(8,128)(2,1)S(1)} custom-call(s32[1]{0:T(128)} %bitcast.4.where, bf16[128,2048]{1,0:T(8,128)(2,1)S(1)} %collective-permute-done.14.refs_0_.refs_3_, bf16[128,2048]{1,0:T(8,128)(2,1)} %get-tuple-element.12.refs_2_.refs_0_.refs_1_, bf16[128,2048]{1,0:T(8,128)(2,1)} %get-tuple-element.11.refs_1_.refs_2_, ...), custom_call_target="tpu_custom_call" | custom-call | flops 1024 | bytes 1024 | tf_op jit(solution)/shard_map/pallas_call | solution.py:41
  85.5 1.8 %copy-done.4 = f32[2,1792,256]{2,1,0:T(8,128)} copy-done((f32[2,1792,256]{2,1,0:T(8,128)}, f32[2,1792,256]{2,1,0:T(8,128)S(1)}, u32[]{:S(2)}) %copy-start.4) | copy-done | bytes 3670040
  88.1 2.0 %copy-done.5 = f32[2,1792,256]{2,1,0:T(8,128)S(1)} copy-done((f32[2,1792,256]{2,1,0:T(8,128)S(1)}, f32[2,1792,256]{2,1,0:T(8,128)}, u32[]{:S(2)}) %copy-start.5) | copy-done | bytes 3670040
  91.2 1.8 %shard_map.52 = f32[2,256]{1,0:T(2,128)S(1)} custom-call(s32[1]{0:T(128)} %bitcast.where, bf16[1792,128]{1,0:T(8,128)(2,1)} %shard_map.48.refs_0_, bf16[1792,128]{1,0:T(8,128)(2,1)S(1)} %copy-done.12, f32[2,1792,256]{2,1,0:T(8,128)S(1)} %copy-done.5), custom_call_target="tpu_custom_call" | custom-call | flops 14000000000 | bytes 1024 | tf_op jit(solution)/shard_map/pallas_call | solution.py:41
  93.0 1.2 %collective-permute-start.13 = (f32[2,256]{1,0:T(2,128)S(1)}, f32[2,256]{1,0:T(2,128)S(1)}, u32[]{:S(2)}, u32[]{:S(2)}) collective-permute-start(f32[2,256]{1,0:T(2,128)S(1)} %shard_map.52), channel_id=1, source_target_pairs={{0,8},{4,12},{8,0},{12,4},{1,9},{5,13},{9,1},{13,5},{2,10},{6,14},... | collective-permute-start | bytes 6152 | tf_op jit(solution)/shard_map/ppermute | solution.py:22
  94.7 2.4 %collective-permute-start.16 = (f32[2,256]{1,0:T(2,128)S(1)}, f32[2,256]{1,0:T(2,128)S(1)}, u32[]{:S(2)}, u32[]{:S(2)}) collective-permute-start(f32[2,256]{1,0:T(2,128)S(1)} %shard_map.54), channel_id=1, source_target_pairs={{0,12},{4,8},{8,4},{12,0},{1,13},{5,9},{9,5},{13,1},{2,14},{6,10},... | collective-permute-start | bytes 6152 | tf_op jit(solution)/shard_map/ppermute | solution.py:22
  97.6 2.6 %collective-permute-done.16 = f32[2,256]{1,0:T(2,128)S(1)} collective-permute-done((f32[2,256]{1,0:T(2,128)S(1)}, f32[2,256]{1,0:T(2,128)S(1)}, u32[]{:S(2)}, u32[]{:S(2)}) %collective-permute-start.16) | collective-permute-done | bytes 2080 | tf_op jit(solution)/shard_map/ppermute | solution.py:22
  100.2 1.2 %collective-permute-done.17 = f32[2,256]{1,0:T(2,128)S(1)} collective-permute-done((f32[2,256]{1,0:T(2,128)S(1)}, f32[2,256]{1,0:T(2,128)S(1)}, u32[]{:S(2)}, u32[]{:S(2)}) %collective-permute-start.17) | collective-permute-done | bytes 2080 | tf_op jit(solution)/shard_map/ppermute | solution.py:22
  101.3 1.5 %collective-permute-start.18 = (f32[2,256]{1,0:T(2,128)S(1)}, f32[2,256]{1,0:T(2,128)S(1)}, u32[]{:S(2)}, u32[]{:S(2)}) collective-permute-start(f32[2,256]{1,0:T(2,128)S(1)} %add.44), channel_id=1, source_target_pairs={{0,2},{2,0},{1,3},{3,1},{4,6},{6,4},{5,7},{7,5},{8,10},{10,8},{9,1... | collective-permute-start | bytes 6152 | tf_op jit(solution)/shard_map/ppermute | solution.py:22
  102.8 2.1 %collective-permute-done.18 = f32[2,256]{1,0:T(2,128)S(1)} collective-permute-done((f32[2,256]{1,0:T(2,128)S(1)}, f32[2,256]{1,0:T(2,128)S(1)}, u32[]{:S(2)}, u32[]{:S(2)}) %collective-permute-start.18) | collective-permute-done | bytes 2080 | tf_op jit(solution)/shard_map/ppermute | solution.py:22
  (58 shorter events, 9.2 us)
Async XLA Ops:
  0.0 15.3 %copy-start.6 = (bf16[256,2048]{1,0:T(8,128)(2,1)S(1)}, bf16[256,2048]{1,0:T(8,128)(2,1)}, u32[]{:S(2)}) copy-start(bf16[256,2048]{1,0:T(8,128)(2,1)} %refs_1_.1) | copy-start | bytes 3145732
  1.2 24.0 %collective-permute-start.1 = (bf16[128,2048]{1,0:T(8,128)(2,1)S(1)}, bf16[128,2048]{1,0:T(8,128)(2,1)}, u32[]{:S(2)}, u32[]{:S(2)}) collective-permute-start(bf16[128,2048]{1,0:T(8,128)(2,1)S(1)} %constant_dynamic-slice_fusion), channel_id=1, source_target_pairs={{0,4},{4,8},{8,12},{1,5},{5,9},{9,13},{2,6},{6,10},{10,14},{3,7},{... | collective-permute-start | bytes 1572872 | tf_op jit(solution)/shard_map/ppermute | solution.py:26
  6.9 25.4 %collective-permute-start.2 = (bf16[128,2048]{1,0:T(8,128)(2,1)S(1)}, bf16[128,2048]{1,0:T(8,128)(2,1)}, u32[]{:S(2)}, u32[]{:S(2)}) collective-permute-start(bf16[128,2048]{1,0:T(8,128)(2,1)S(1)} %constant_dynamic-slice_fusion), channel_id=1, source_target_pairs={{4,0},{8,4},{12,8},{5,1},{9,5},{13,9},{6,2},{10,6},{14,10},{7,3},{... | collective-permute-start | bytes 1572872 | tf_op jit(solution)/shard_map/ppermute | solution.py:27
  9.6 26.0 %collective-permute-start.5 = (bf16[128,1792]{1,0:T(8,128)(2,1)S(1)}, bf16[128,1792]{1,0:T(8,128)(2,1)S(1)}, u32[]{:S(2)}, u32[]{:S(2)}) collective-permute-start(bf16[128,1792]{1,0:T(8,128)(2,1)S(1)} %get-tuple-element.13.refs_5_), channel_id=1, source_target_pairs={{0,12},{4,8},{8,4},{12,0},{1,13},{5,9},{9,5},{13,1},{2,14},{6,10},... | collective-permute-start | bytes 1376264 | tf_op jit(solution)/shard_map/ppermute | solution.py:22
  15.3 8.1 %copy-start.13 = (bf16[1792,128]{1,0:T(8,128)(2,1)}, bf16[1792,128]{1,0:T(8,128)(2,1)S(1)}, u32[]{:S(2)}) copy-start(bf16[1792,128]{1,0:T(8,128)(2,1)S(1)} %get-tuple-element.10.refs_4_) | copy-start | bytes 1376260
  15.3 28.0 %collective-permute-start = (bf16[1792,128]{1,0:T(8,128)(2,1)}, bf16[1792,128]{1,0:T(8,128)(2,1)S(1)}, u32[]{:S(2)}, u32[]{:S(2)}) collective-permute-start(bf16[1792,128]{1,0:T(8,128)(2,1)} %get-tuple-element.9.refs_3_), channel_id=1, source_target_pairs={{0,4},{4,0},{8,12},{12,8},{1,5},{5,1},{9,13},{13,9},{2,6},{6,2},{1... | collective-permute-start | bytes 1376264 | tf_op jit(solution)/shard_map/ppermute | solution.py:22
  23.4 1.8 %copy-start.2 = (f32[2,1792,256]{2,1,0:T(8,128)}, f32[2,1792,256]{2,1,0:T(8,128)S(1)}, u32[]{:S(2)}) copy-start(f32[2,1792,256]{2,1,0:T(8,128)S(1)} %shard_map.39.refs_1_.refs_2_) | copy-start | bytes 11010052
  33.6 12.0 %collective-permute-start.4 = (bf16[128,2048]{1,0:T(8,128)(2,1)S(1)}, bf16[128,2048]{1,0:T(8,128)(2,1)S(1)}, u32[]{:S(2)}, u32[]{:S(2)}) collective-permute-start(bf16[128,2048]{1,0:T(8,128)(2,1)S(1)} %shard_map.43.refs_0_), channel_id=1, source_target_pairs={{0,1},{1,0},{2,3},{3,2},{4,5},{5,4},{6,7},{7,6},{8,9},{9,8},{10,11... | collective-permute-start | bytes 1572872 | tf_op jit(solution)/shard_map/ppermute | solution.py:22
  33.6 33.9 %collective-permute-start.10 = (bf16[128,2048]{1,0:T(8,128)(2,1)}, bf16[128,2048]{1,0:T(8,128)(2,1)S(1)}, u32[]{:S(2)}, u32[]{:S(2)}) collective-permute-start(bf16[128,2048]{1,0:T(8,128)(2,1)} %get-tuple-element.12.refs_2_.refs_0_.refs_1_), channel_id=1, source_target_pairs={{4,0},{8,4},{5,1},{9,5},{6,2},{10,6},{7,3},{11,7},{20,16},{24,20},... | collective-permute-start | bytes 1572872 | tf_op jit(solution)/shard_map/ppermute | solution.py:27
  34.9 32.6 %collective-permute-start.11 = (bf16[128,2048]{1,0:T(8,128)(2,1)}, bf16[128,2048]{1,0:T(8,128)(2,1)S(1)}, u32[]{:S(2)}, u32[]{:S(2)}) collective-permute-start(bf16[128,2048]{1,0:T(8,128)(2,1)} %get-tuple-element.11.refs_1_.refs_2_), channel_id=1, source_target_pairs={{4,8},{8,12},{5,9},{9,13},{6,10},{10,14},{7,11},{11,15},{20,24},{2... | collective-permute-start | bytes 1572872 | tf_op jit(solution)/shard_map/ppermute | solution.py:26
  35.7 0.8 copy-start.7
  36.4 20.9 %collective-permute-start.6 = (bf16[128,1792]{1,0:T(8,128)(2,1)}, bf16[128,1792]{1,0:T(8,128)(2,1)}, u32[]{:S(2)}, u32[]{:S(2)}) collective-permute-start(bf16[128,1792]{1,0:T(8,128)(2,1)} %shard_map.45.refs_0_), channel_id=1, source_target_pairs={{0,2},{2,0},{1,3},{3,1},{4,6},{6,4},{5,7},{7,5},{8,10},{10,8},{9,1... | collective-permute-start | bytes 1376264 | tf_op jit(solution)/shard_map/ppermute | solution.py:22
  44.1 21.4 %collective-permute-start.3 = (bf16[1792,128]{1,0:T(8,128)(2,1)}, bf16[1792,128]{1,0:T(8,128)(2,1)}, u32[]{:S(2)}, u32[]{:S(2)}) collective-permute-start(bf16[1792,128]{1,0:T(8,128)(2,1)} %shard_map.42.refs_0_), channel_id=1, source_target_pairs={{0,2},{2,0},{1,3},{3,1},{4,6},{6,4},{5,7},{7,5},{8,10},{10,8},{9,1... | collective-permute-start | bytes 1376264 | tf_op jit(solution)/shard_map/ppermute | solution.py:22
  45.6 27.5 %collective-permute-start.8 = (bf16[1792,128]{1,0:T(8,128)(2,1)}, bf16[1792,128]{1,0:T(8,128)(2,1)}, u32[]{:S(2)}, u32[]{:S(2)}) collective-permute-start(bf16[1792,128]{1,0:T(8,128)(2,1)} %copy-done.13), channel_id=1, source_target_pairs={{0,8},{4,12},{8,0},{12,4},{1,9},{5,13},{9,1},{13,5},{2,10},{6,14},... | collective-permute-start | bytes 1376264 | tf_op jit(solution)/shard_map/ppermute | solution.py:22
  46.7 2.3 %copy-start.3 = (f32[2,1792,256]{2,1,0:T(8,128)S(1)}, f32[2,1792,256]{2,1,0:T(8,128)}, u32[]{:S(2)}) copy-start(f32[2,1792,256]{2,1,0:T(8,128)} %copy-done.2) | copy-start | bytes 11010052
  49.4 8.0 %copy-start.8 = (bf16[128,1792]{1,0:T(8,128)(2,1)S(1)}, bf16[128,1792]{1,0:T(8,128)(2,1)}, u32[]{:S(2)}) copy-start(bf16[128,1792]{1,0:T(8,128)(2,1)} %shard_map.45.refs_0_) | copy-start | bytes 1376260
  57.4 8.1 %copy-start.10 = (bf16[1792,128]{1,0:T(8,128)(2,1)S(1)}, bf16[1792,128]{1,0:T(8,128)(2,1)}, u32[]{:S(2)}) copy-start(bf16[1792,128]{1,0:T(8,128)(2,1)} %shard_map.42.refs_0_) | copy-start | bytes 1376260
  65.5 2.1 %copy-start = (f32[2,256,2048]{2,1,0:T(8,128)}, f32[2,256,2048]{2,1,0:T(8,128)S(1)}, u32[]{:S(2)}) copy-start(f32[2,256,2048]{2,1,0:T(8,128)S(1)} %shard_map.46.refs_3_.refs_1_.refs_2_) | copy-start | bytes 12582916
  67.6 7.0 %collective-permute-start.12 = (bf16[128,2048]{1,0:T(8,128)(2,1)S(1)}, bf16[128,2048]{1,0:T(8,128)(2,1)S(1)}, u32[]{:S(2)}, u32[]{:S(2)}) collective-permute-start(bf16[128,2048]{1,0:T(8,128)(2,1)S(1)} %shard_map.49.refs_0_), channel_id=1, source_target_pairs={{0,1},{1,0},{2,3},{3,2},{4,5},{5,4},{6,7},{7,6},{8,9},{9,8},{10,11... | collective-permute-start | bytes 1572872 | tf_op jit(solution)/shard_map/ppermute | solution.py:22
  67.7 16.5 %collective-permute-start.14 = (bf16[128,2048]{1,0:T(8,128)(2,1)S(1)}, bf16[128,2048]{1,0:T(8,128)(2,1)S(1)}, u32[]{:S(2)}, u32[]{:S(2)}) collective-permute-start(bf16[128,2048]{1,0:T(8,128)(2,1)S(1)} %shard_map.49.refs_0_), channel_id=1, source_target_pairs={{4,0},{8,12},{5,1},{9,13},{6,2},{10,14},{7,3},{11,15},{20,16},{24,... | collective-permute-start | bytes 1572872 | tf_op jit(solution)/shard_map/ppermute | solution.py:264
  73.1 14.2 %collective-permute-start.9 = (bf16[1792,128]{1,0:T(8,128)(2,1)}, bf16[1792,128]{1,0:T(8,128)(2,1)S(1)}, u32[]{:S(2)}, u32[]{:S(2)}) collective-permute-start(bf16[1792,128]{1,0:T(8,128)(2,1)} %shard_map.48.refs_0_), channel_id=1, source_target_pairs={{0,2},{2,0},{1,3},{3,1},{4,6},{6,4},{5,7},{7,5},{8,10},{10,8},{9,1... | collective-permute-start | bytes 1376264 | tf_op jit(solution)/shard_map/ppermute | solution.py:22
  74.6 22.5 %collective-permute-start.7 = (f32[2,256]{1,0:T(2,128)S(1)}, f32[2,256]{1,0:T(2,128)S(1)}, u32[]{:S(2)}, u32[]{:S(2)}) collective-permute-start(f32[2,256]{1,0:T(2,128)S(1)} %shard_map.47.refs_2_.refs_3_), channel_id=1, source_target_pairs={{0,4},{4,0},{8,12},{12,8},{1,5},{5,1},{9,13},{13,9},{2,6},{6,2},{1... | collective-permute-start | bytes 6152 | tf_op jit(solution)/shard_map/ppermute | solution.py:22
  85.5 1.8 %copy-start.4 = (f32[2,1792,256]{2,1,0:T(8,128)}, f32[2,1792,256]{2,1,0:T(8,128)S(1)}, u32[]{:S(2)}) copy-start(f32[2,1792,256]{2,1,0:T(8,128)S(1)} %shard_map.50.refs_1_.refs_2_.refs_4_) | copy-start | bytes 11010052
  87.3 7.0 %collective-permute-start.15 = (bf16[128,2048]{1,0:T(8,128)(2,1)S(1)}, bf16[128,2048]{1,0:T(8,128)(2,1)S(1)}, u32[]{:S(2)}, u32[]{:S(2)}) collective-permute-start(bf16[128,2048]{1,0:T(8,128)(2,1)S(1)} %shard_map.53.refs_0_), channel_id=1, source_target_pairs={{0,1},{1,0},{2,3},{3,2},{4,5},{5,4},{6,7},{7,6},{8,9},{9,8},{10,11... | collective-permute-start | bytes 1572872 | tf_op jit(solution)/shard_map/ppermute | solution.py:22
  87.3 0.8 copy-start.11
  88.1 2.0 %copy-start.5 = (f32[2,1792,256]{2,1,0:T(8,128)S(1)}, f32[2,1792,256]{2,1,0:T(8,128)}, u32[]{:S(2)}) copy-start(f32[2,1792,256]{2,1,0:T(8,128)} %copy-done.4) | copy-start | bytes 11010052
  90.2 1.0 copy-start.12
  91.2 3.1 %copy-start.1 = (f32[2,256,2048]{2,1,0:T(8,128)S(1)}, f32[2,256,2048]{2,1,0:T(8,128)}, u32[]{:S(2)}) copy-start(f32[2,256,2048]{2,1,0:T(8,128)} %copy-done) | copy-start | bytes 12582916
  93.0 4.5 %collective-permute-start.13 = (f32[2,256]{1,0:T(2,128)S(1)}, f32[2,256]{1,0:T(2,128)S(1)}, u32[]{:S(2)}, u32[]{:S(2)}) collective-permute-start(f32[2,256]{1,0:T(2,128)S(1)} %shard_map.52), channel_id=1, source_target_pairs={{0,8},{4,12},{8,0},{12,4},{1,9},{5,13},{9,1},{13,5},{2,10},{6,14},... | collective-permute-start | bytes 6152 | tf_op jit(solution)/shard_map/ppermute | solution.py:22
  94.7 5.4 %collective-permute-start.16 = (f32[2,256]{1,0:T(2,128)S(1)}, f32[2,256]{1,0:T(2,128)S(1)}, u32[]{:S(2)}, u32[]{:S(2)}) collective-permute-start(f32[2,256]{1,0:T(2,128)S(1)} %shard_map.54), channel_id=1, source_target_pairs={{0,12},{4,8},{8,4},{12,0},{1,13},{5,9},{9,5},{13,1},{2,14},{6,10},... | collective-permute-start | bytes 6152 | tf_op jit(solution)/shard_map/ppermute | solution.py:22
  100.2 1.2 %collective-permute-start.17 = (f32[2,256]{1,0:T(2,128)S(1)}, f32[2,256]{1,0:T(2,128)S(1)}, u32[]{:S(2)}, u32[]{:S(2)}) collective-permute-start(f32[2,256]{1,0:T(2,128)S(1)} %add_add_fusion), channel_id=1, source_target_pairs={{0,1},{1,0},{2,3},{3,2},{4,5},{5,4},{6,7},{7,6},{8,9},{9,8},{10,11... | collective-permute-start | bytes 6152 | tf_op jit(solution)/shard_map/ppermute | solution.py:22
  101.3 3.6 %collective-permute-start.18 = (f32[2,256]{1,0:T(2,128)S(1)}, f32[2,256]{1,0:T(2,128)S(1)}, u32[]{:S(2)}, u32[]{:S(2)}) collective-permute-start(f32[2,256]{1,0:T(2,128)S(1)} %add.44), channel_id=1, source_target_pairs={{0,2},{2,0},{1,3},{3,1},{4,6},{6,4},{5,7},{7,5},{8,10},{10,8},{9,1... | collective-permute-start | bytes 6152 | tf_op jit(solution)/shard_map/ppermute | solution.py:22
  (1 other events, 0.8 us)

commit v10 on v9

--- a/solution.py
+++ b/solution.py
@@ -31,7 +31,7 @@
 ANYWHERE = pl.BlockSpec(memory_space=pl.ANY)
 
 
-def call(kernel, grid, where, inputs, shape, out_spec, scratch, flops, tokens, vmem=36):
+def call(kernel, grid, where, inputs, shape, out_spec, scratch, flops, tokens, vmem=20):
     arrays = [array for array, _ in inputs]
     skip = len(tokens)
 
@@ -61,6 +61,7 @@
         out_specs=[ANYWHERE] * count,
         out_shape=[jax.ShapeDtypeStruct(block.shape, block.dtype) for block in blocks],
         input_output_aliases={i: i for i in range(count)},
+        compiler_params=pltpu.CompilerParams(vmem_limit_bytes=1024 * 1024),
         cost_estimate=pl.CostEstimate(flops=1024, bytes_accessed=1024, transcendentals=0),
     )(*blocks, *tokens)
 
@@ -123,8 +124,12 @@
     return found[0] if len(found) == 1 else jnp.concatenate(found, axis=axis)
 
 
-def mix_kernel(where, mine_ref, other_ref, query_ref, out_ref, acts):
+MARK = jax.ShapeDtypeStruct((8, 128), jnp.float32), pl.BlockSpec((8, 128), lambda *at: (0, 0))
+
+
+def mix_kernel(where, mine_ref, other_ref, query_ref, out_ref, mark_ref, acts):
     half = mine_ref.shape[0]
+    mark_ref[...] = jnp.zeros_like(mark_ref)
 
     @pl.when((pl.program_id(0) == 0) & (pl.program_id(1) == 0))
     def _():
@@ -145,8 +150,8 @@
     inputs.append((queries, pl.BlockSpec((1, 1, tile, width), lambda q, o, where: (q, 0, o, 0))))
     return call(
         mix_kernel, (nq, depth // tile), [core], inputs,
-        jax.ShapeDtypeStruct((nq, depth, 2 * half), jnp.float32),
-        pl.BlockSpec((1, tile, 2 * half), lambda q, o, where: (q, o, 0)),
+        [jax.ShapeDtypeStruct((nq, depth, 2 * half), jnp.float32), MARK[0]],
+        [pl.BlockSpec((1, tile, 2 * half), lambda q, o, where: (q, o, 0)), MARK[1]],
         [pltpu.VMEM((2 * half, width), queries.dtype)], flops, tokens,
     )
 
@@ -169,7 +174,8 @@
 
 
 def project_kernel(where, *refs):
-    parts, (query_ref, out_ref, grads) = refs[:-3], refs[-3:]
+    parts, (query_ref, out_ref, mark_ref, grads) = refs[:-4], refs[-4:]
+    mark_ref[...] = jnp.zeros_like(mark_ref)
 
     @pl.when((pl.program_id(0) == 0) & (pl.program_id(1) == 0))
     def _():
@@ -186,8 +192,8 @@
     inputs.append((queries, pl.BlockSpec((1, 1, depth, tile), lambda q, i, where: (q, 0, 0, i))))
     return call(
         project_kernel, (nq, width // tile), [column], inputs,
-        jax.ShapeDtypeStruct((nq, count, width), jnp.float32),
-        pl.BlockSpec((1, count, tile), lambda q, i, where: (q, 0, i)),
+        [jax.ShapeDtypeStruct((nq, count, width), jnp.float32), MARK[0]],
+        [pl.BlockSpec((1, count, tile), lambda q, i, where: (q, 0, i)), MARK[1]],
         [pltpu.VMEM((count, depth), queries.dtype)], flops, tokens,
     )
 
@@ -242,32 +248,32 @@
     arrived = {d: trade(block, {"dp": d}) for d, block in zip(early + [late, far], sent)}
 
     zero = jnp.zeros((), jnp.int32)
-    mix = mixed((activations, 0), (activations, 1), zero, queries, SHORT, sent)
+    mix, token = mixed((activations, 0), (activations, 1), zero, queries, SHORT, sent)
     own, = turned([grads_for(me, 0, tokens)], [1])
-    token = scores = scores_of_grads([own], zero, mix, 0, 1)
-    hops[1] = hold(list(hops[1]), [mix])
+    scores = scores_of_grads([own], zero, mix, 0, 1)
+    hops[1] = hold(list(hops[1]), [token])
     for step in range(2, count - 1):
         hops.append(pass_on(hops[-1], step, count))
 
-    mixes = {}
+    mixes, token = {}, scores
     for d in early:
-        mixes[d] = token = mixed(*acts_of(from_partner(hops, me, d, count)), core, queries, SHORT, [token])
-    sides = to_columns(hold([arrived[far]], list(hops[1]))[0])
-    proj = projected(sides, column, queries, SHORT, [token])
-    token = proj
+        mixes[d], token = mixed(*acts_of(from_partner(hops, me, d, count)), core, queries, SHORT, [token])
+    sides = to_columns(hold([arrived[far]], hops[1])[0])
+    block = from_partner(hops, me, late, count, [token] + sides)
+    end = lax.ppermute(block, "dp", [(1, 0), (count - 2, count - 1)])
+    hops.append((end, end))
+
+    proj, token = projected(sides, column, queries, SHORT, [token])
     for d in early:
-        sides = to_columns(hold([arrived[d]], list(hops[1]))[0])
+        sides = to_columns(hold([arrived[d]], hops[1])[0])
         token = scores_of_grads(sides, column, mixes[d], 0, 1, [token])
         scores = scores + trade(token, {"dp": d})
 
-    block = from_partner(hops, me, late, count, [token])
-    end = lax.ppermute(block, "dp", [(1, 0), (count - 2, count - 1)])
-    hops.append((end, end))
-    sides = to_columns(hold([arrived[late]], [proj])[0])
-    mix = mixed(*acts_of(block), core, queries, SHORT, [token])
-    sides = sides[:1] + list(hold(sides[1:], [mix]))
+    sides = to_columns(hold([arrived[late]], [token])[0])
+    mix, token = mixed(*acts_of(block), core, queries, SHORT, [token])
+    sides = sides[:1] + list(hold(sides[1:], [token]))
     near = trade(scores_of_grads(sides, column, mix, 0, 1, (), LONG), {"dp": late})
-    block = from_partner(hops, me, far, count, [mix])
+    block = from_partner(hops, me, far, count, [token])
     scores = scores + near + trade(scores_of_acts(*acts_of(block), core, proj), {"dp": far})
     return over_chips(scores, spread)
 

time: 106 us -> 112 us (1.057)
  local copies, waits for them, and re-layouts: 13.6 us -> 29.8 us
  Pallas kernels: 40.5 us -> 28.1 us
  starting transfers between devices: 25.8 us -> 36.5 us
  waiting for transfers between devices: 24.7 us -> 15.8 us
    unnamed x28 -> x22, local copies, waits for them, and re-layouts: 9.65 us -> 25.1 us
    pallas_call x13, Pallas kernels: 40.5 us -> 28.1 us  [call(): pl.pallas_call(body, grid_spec=pltpu.PrefetchScalarGridSpec(num_scalar_pr...]
    ppermute x14, starting transfers between devices: 15.5 us -> 26.2 us  [trade(): return lax.ppermute(block, axes, route[::-1] if backwards else route)]
    ppermute x2, waiting for transfers between devices: 7.13 us -> 0.01 us  [pass_on(): lax.ppermute(block[1], 'dp', [(i, i - 1) for i in range(1, count - step +...]
    ppermute x1, waiting for transfers between devices: 1.75 us -> 0.01 us  [on_device(): end = lax.ppermute(block, 'dp', [(1, 0), (count - 2, count - 1)])]
  transfers between devices with their start and end apart: 19 -> 19, of which waited for: 8 -> 5; matrix products, arithmetic and copies ran while one was open for 3% -> 3% of each run, Pallas kernels for 38% -> 25%
where the time goes in v10:
time: 112 us; the launch traced here: 111 us
  starting transfers between devices  36.5 us (33%)
  local copies, waits for them, and re-layouts  29.8 us (27%)
  Pallas kernels  28.1 us (25%)
  waiting for transfers between devices  15.8 us (14%)
    pallas_call x13, Pallas kernels, call(): pl.pallas_call(body, grid_spec=pltpu.PrefetchScalarGridSpec(num_scalar_pr...  28.1 us
    ppermute x14, starting transfers between devices, trade(): return lax.ppermute(block, axes, route[::-1] if backwards else route)  26.2 us
    unnamed x22, local copies, waits for them, and re-layouts  25.1 us
    ppermute x14, waiting for transfers between devices, trade(): return lax.ppermute(block, axes, route[::-1] if backwards else route)  15.8 us
    ppermute x2, starting transfers between devices, pass_on(): lax.ppermute(block[0], 'dp', [(i, i + 1) for i in range(step - 1, count -...  6.44 us
    dynamic_slice x2, local copies, waits for them, and re-layouts, grads_for(): return lax.dynamic_slice(out_grads, (first, device * rows), (size, rows))  3.56 us
    ppermute x2, starting transfers between devices, pass_on(): lax.ppermute(block[1], 'dp', [(i, i - 1) for i in range(1, count - step +...  2.57 us
  transfers between devices with their start and end apart: 19, of which 5 were waited for; matrix products, arithmetic and copies ran while one was open for 3% of the time, Pallas kernels for 25%

profile of v10, /device:TPU:0, one launch (start us, length us, event | category | flops | bytes accessed | tf_op | source)
XLA Modules:
  0.0 111.1 jit_solution(11661128269290895297)
XLA Ops:
  0.0 1.2 %constant_dynamic-slice_fusion = bf16[128,2048]{1,0:T(8,128)(2,1)S(1)} fusion(bf16[256,2048]{1,0:T(8,128)(2,1)} %refs_1_.1, s32[]{:T(128)S(6)} %select_n.53), kind=kLoop, calls=%fused_computation.1 | loop fusion | bytes 1048580 | tf_op jit(solution)/shard_map/dynamic_slice | solution.py:239
  1.2 5.0 %collective-permute-start.1 = (bf16[128,2048]{1,0:T(8,128)(2,1)S(1)}, bf16[128,2048]{1,0:T(8,128)(2,1)S(1)}, u32[]{:S(2)}, u32[]{:S(2)}) collective-permute-start(bf16[128,2048]{1,0:T(8,128)(2,1)S(1)} %constant_dynamic-slice_fusion), channel_id=1, source_target_pairs={{0,4},{4,8},{8,12},{1,5},{5,9},{9,13},{2,6},{6,10},{10,14},{3,7},{... | collective-permute-start | bytes 1572872 | tf_op jit(solution)/shard_map/ppermute | solution.py:26
  6.1 1.3 %collective-permute-start.2 = (bf16[128,2048]{1,0:T(8,128)(2,1)S(1)}, bf16[128,2048]{1,0:T(8,128)(2,1)S(1)}, u32[]{:S(2)}, u32[]{:S(2)}) collective-permute-start(bf16[128,2048]{1,0:T(8,128)(2,1)S(1)} %constant_dynamic-slice_fusion), channel_id=1, source_target_pairs={{4,0},{8,4},{12,8},{5,1},{9,5},{13,9},{6,2},{10,6},{14,10},{7,3},{... | collective-permute-start | bytes 1572872 | tf_op jit(solution)/shard_map/ppermute | solution.py:27
  7.5 2.2 %fusion = (bf16[128,1792]{1,0:T(8,128)(2,1)}, bf16[128,1792]{1,0:T(8,128)(2,1)S(1)}, bf16[128,1792]{1,0:T(8,128)(2,1)S(1)}) fusion(bf16[256,7168]{1,0:T(8,128)(2,1)} %param.4, s32[]{:T(128)S(6)} %select_n.49, s32[]{:T(128)S(6)} %select_n.52, s32[]{:T(128)S(6)} %select_n.50, s32[]{:T(128)S(6)} %select_n.51), kind=kLoop, calls=%fused_computation.3 | loop fusion | bytes 2752528 | tf_op jit(solution)/shard_map/dynamic_slice | solution.py:244
  9.6 4.7 %collective-permute-start.5 = (bf16[128,1792]{1,0:T(8,128)(2,1)}, bf16[128,1792]{1,0:T(8,128)(2,1)S(1)}, u32[]{:S(2)}, u32[]{:S(2)}) collective-permute-start(bf16[128,1792]{1,0:T(8,128)(2,1)} %get-tuple-element.29.refs_5_), channel_id=1, source_target_pairs={{0,12},{4,8},{8,4},{12,0},{1,13},{5,9},{9,5},{13,1},{2,14},{6,10},... | collective-permute-start | bytes 1376264 | tf_op jit(solution)/shard_map/ppermute | solution.py:22
  14.3 1.1 shard_map.38
  15.4 5.2 %copy-done = bf16[2,1,1792,2048]{3,2,1,0:T(8,128)(2,1)S(1)} copy-done((bf16[2,1,1792,2048]{3,2,1,0:T(8,128)(2,1)S(1)}, bf16[2,1,1792,2048]{3,2,1,0:T(8,128)(2,1)}, u32[]{:S(2)}) %copy-start) | copy-done | bytes 14680088
  20.6 4.8 %shard_map.39 = (f32[2,1792,256]{2,1,0:T(8,128)S(1)}, f32[8,128]{1,0:T(8,128)S(1)}) custom-call(s32[1]{0:T(128)} %constant.5.clone.1.where, bf16[256,2048]{1,0:T(8,128)(2,1)S(1)} %copy-done.4, bf16[256,2048]{1,0:T(8,128)(2,1)S(1)} %copy-done.4, bf16[2,1,1792,2048]{3,2,1,0:T(8,128)(2,1)S(1)} %copy-done, bf16[1792,128]{1,0:T(8,128)(2,1)S(1)} %get-tuple-element.17.refs_3_, ...), custom_call_target="tpu_custom_call" | custom-call | flops 1000000 | bytes 1024 | tf_op jit(solution)/shard_map/pallas_call | solution.py:41
  25.6 8.9 %collective-permute-start = (bf16[1792,128]{1,0:T(8,128)(2,1)S(1)}, bf16[1792,128]{1,0:T(8,128)(2,1)S(1)}, u32[]{:S(2)}, u32[]{:S(2)}) collective-permute-start(bf16[1792,128]{1,0:T(8,128)(2,1)S(1)} %get-tuple-element.17.refs_3_), channel_id=1, source_target_pairs={{0,4},{4,0},{8,12},{12,8},{1,5},{5,1},{9,13},{13,9},{2,6},{6,2},{1... | collective-permute-start | bytes 1376264 | tf_op jit(solution)/shard_map/ppermute | solution.py:22
  34.4 1.3 %collective-permute-start.10 = (bf16[128,2048]{1,0:T(8,128)(2,1)S(1)}, bf16[128,2048]{1,0:T(8,128)(2,1)}, u32[]{:S(2)}, u32[]{:S(2)}) collective-permute-start(bf16[128,2048]{1,0:T(8,128)(2,1)S(1)} %get-tuple-element.22.refs_2_.refs_0_.refs_1_), channel_id=1, source_target_pairs={{4,0},{8,4},{5,1},{9,5},{6,2},{10,6},{7,3},{11,7},{20,16},{24,20},... | collective-permute-start | bytes 1572872 | tf_op jit(solution)/shard_map/ppermute | solution.py:27
  35.7 1.5 %collective-permute-start.11 = (bf16[128,2048]{1,0:T(8,128)(2,1)S(1)}, bf16[128,2048]{1,0:T(8,128)(2,1)}, u32[]{:S(2)}, u32[]{:S(2)}) collective-permute-start(bf16[128,2048]{1,0:T(8,128)(2,1)S(1)} %get-tuple-element.21.refs_1_.refs_2_), channel_id=1, source_target_pairs={{4,8},{8,12},{5,9},{9,13},{6,10},{10,14},{7,11},{11,15},{20,24},{2... | collective-permute-start | bytes 1572872 | tf_op jit(solution)/shard_map/ppermute | solution.py:26
  37.2 1.5 %collective-permute-start.6 = (bf16[128,1792]{1,0:T(8,128)(2,1)S(1)}, bf16[128,1792]{1,0:T(8,128)(2,1)}, u32[]{:S(2)}, u32[]{:S(2)}) collective-permute-start(bf16[128,1792]{1,0:T(8,128)(2,1)S(1)} %shard_map.45.refs_0_.refs_3_), channel_id=1, source_target_pairs={{0,2},{2,0},{1,3},{3,1},{4,6},{6,4},{5,7},{7,5},{8,10},{10,8},{9,1... | collective-permute-start | bytes 1376264 | tf_op jit(solution)/shard_map/ppermute | solution.py:22
  38.7 7.1 %collective-permute-done.refs_0_ = bf16[1792,128]{1,0:T(8,128)(2,1)S(1)} collective-permute-done((bf16[1792,128]{1,0:T(8,128)(2,1)S(1)}, bf16[1792,128]{1,0:T(8,128)(2,1)S(1)}, u32[]{:S(2)}, u32[]{:S(2)}) %collective-permute-start) | collective-permute-done | bytes 458784 | tf_op jit(solution)/shard_map/ppermute | solution.py:22
  45.8 1.5 %collective-permute-start.3 = (bf16[1792,128]{1,0:T(8,128)(2,1)S(1)}, bf16[1792,128]{1,0:T(8,128)(2,1)}, u32[]{:S(2)}, u32[]{:S(2)}) collective-permute-start(bf16[1792,128]{1,0:T(8,128)(2,1)S(1)} %shard_map.42.refs_0_), channel_id=1, source_target_pairs={{0,2},{2,0},{1,3},{3,1},{4,6},{6,4},{5,7},{7,5},{8,10},{10,8},{9,1... | collective-permute-start | bytes 1376264 | tf_op jit(solution)/shard_map/ppermute | solution.py:22
  48.1 1.4 %constant_dynamic-slice_fusion.1.refs_0_ = bf16[256,1792]{1,0:T(8,128)(2,1)S(1)} fusion(bf16[256,7168]{1,0:T(8,128)(2,1)} %param.4, s32[]{:T(128)S(6)} %select_n.48), kind=kLoop, calls=%fused_computation.2 | loop fusion | bytes 1835012 | tf_op jit(solution)/shard_map/dynamic_slice | solution.py:244
  50.9 5.2 %copy-done.1 = bf16[2,1,1792,2048]{3,2,1,0:T(8,128)(2,1)S(1)} copy-done((bf16[2,1,1792,2048]{3,2,1,0:T(8,128)(2,1)S(1)}, bf16[2,1,1792,2048]{3,2,1,0:T(8,128)(2,1)}, u32[]{:S(2)}) %copy-start.1) | copy-done | bytes 14680088
  56.1 1.0 copy-done.10
  57.1 4.8 %shard_map.44 = (f32[2,1792,256]{2,1,0:T(8,128)S(1)}, f32[8,128]{1,0:T(8,128)S(1)}) custom-call(s32[1]{0:T(128)} %bitcast.1.where, bf16[128,2048]{1,0:T(8,128)(2,1)S(1)} %shard_map.43.refs_0_, bf16[128,2048]{1,0:T(8,128)(2,1)S(1)} %copy-done.10, bf16[2,1,1792,2048]{3,2,1,0:T(8,128)(2,1)S(1)} %copy-done.1, f32[2,256]{1,0:T(2,128)S(1)} %shard_map.40.refs_3_), custom_call_target="tpu_custom_call" | custom-call | flops 1000000 | bytes 1024 | tf_op jit(solution)/shard_map/pallas_call | solution.py:41
  61.9 1.2 %shard_map.49.refs_0_ = bf16[128,2048]{1,0:T(8,128)(2,1)S(1)} custom-call(s32[1]{0:T(128)} %bitcast.3.where, bf16[128,2048]{1,0:T(8,128)(2,1)} %collective-permute-done.10.refs_0_, bf16[128,2048]{1,0:T(8,128)(2,1)} %collective-permute-done.11.refs_1_, f32[8,128]{1,0:T(8,128)S(1)} %get-tuple-element.24.refs_3_.refs_2_, ...), custom_call_target="tpu_custom_call" | custom-call | flops 1024 | bytes 1024 | tf_op jit(solution)/shard_map/pallas_call | solution.py:41
  63.3 1.3 %collective-permute-start.14 = (bf16[128,2048]{1,0:T(8,128)(2,1)S(1)}, bf16[128,2048]{1,0:T(8,128)(2,1)S(1)}, u32[]{:S(2)}, u32[]{:S(2)}) collective-permute-start(bf16[128,2048]{1,0:T(8,128)(2,1)S(1)} %shard_map.49.refs_0_), channel_id=1, source_target_pairs={{4,0},{8,12},{5,1},{9,13},{6,2},{10,14},{7,3},{11,15},{20,16},{24,... | collective-permute-start | bytes 1572872 | tf_op jit(solution)/shard_map/ppermute | solution.py:263
  64.6 5.2 %copy-done.2 = bf16[2,1,1792,2048]{3,2,1,0:T(8,128)(2,1)S(1)} copy-done((bf16[2,1,1792,2048]{3,2,1,0:T(8,128)(2,1)S(1)}, bf16[2,1,1792,2048]{3,2,1,0:T(8,128)(2,1)}, u32[]{:S(2)}) %copy-start.2) | copy-done | bytes 14680088
  69.7 6.6 %shard_map.46 = (f32[2,256,2048]{2,1,0:T(8,128)S(1)}, f32[8,128]{1,0:T(8,128)S(1)}) custom-call(s32[1]{0:T(128)} %bitcast.where, bf16[128,1792]{1,0:T(8,128)(2,1)S(1)} %shard_map.45.refs_0_.refs_3_, bf16[128,1792]{1,0:T(8,128)(2,1)} %collective-permute-done.6.refs_1_.refs_4_, bf16[2,1,1792,2048]{3,2,1,0:T(8,128)(2,1)S(1)} %copy-done.2, ...), custom_call_target="tpu_custom_call" | custom-call | flops 1000000 | bytes 1024 | tf_op jit(solution)/shard_map/pallas_call | solution.py:41
  76.3 2.0 %copy-done.5 = f32[2,256,2048]{2,1,0:T(8,128)} copy-done((f32[2,256,2048]{2,1,0:T(8,128)}, f32[2,256,2048]{2,1,0:T(8,128)S(1)}, u32[]{:S(2)}) %copy-start.5) | copy-done | bytes 4194328
  78.3 1.7 %shard_map.47.refs_1_.refs_3_ = f32[2,256]{1,0:T(2,128)S(1)} custom-call(s32[1]{0:T(128)} %bitcast.where, bf16[1792,128]{1,0:T(8,128)(2,1)S(1)} %shard_map.42.refs_0_, bf16[1792,128]{1,0:T(8,128)(2,1)} %collective-permute-done.3.refs_1_, f32[2,1792,256]{2,1,0:T(8,128)S(1)} %get-tuple-element.23.refs_2_, f32[8,128]{1,0:T(8,128)S(1)} %get-tuple-element.25.refs_3_), custom_call_target="tpu_custom_call" | custom-call | flops 1024 | bytes 1024 | tf_op jit(solution)/shard_map/pallas_call | solution.py:41
  80.6 4.3 %collective-permute-start.7 = (f32[2,256]{1,0:T(2,128)S(1)}, f32[2,256]{1,0:T(2,128)S(1)}, u32[]{:S(2)}, u32[]{:S(2)}) collective-permute-start(f32[2,256]{1,0:T(2,128)S(1)} %shard_map.47.refs_1_.refs_3_), channel_id=1, source_target_pairs={{0,4},{4,0},{8,12},{12,8},{1,5},{5,1},{9,13},{13,9},{2,6},{6,2},{1... | collective-permute-start | bytes 6152 | tf_op jit(solution)/shard_map/ppermute | solution.py:22
  84.9 5.2 %copy-done.3 = bf16[2,1,1792,2048]{3,2,1,0:T(8,128)(2,1)S(1)} copy-done((bf16[2,1,1792,2048]{3,2,1,0:T(8,128)(2,1)S(1)}, bf16[2,1,1792,2048]{3,2,1,0:T(8,128)(2,1)}, u32[]{:S(2)}) %copy-start.3) | copy-done | bytes 14680088
  90.1 4.7 %shard_map.50 = (f32[2,1792,256]{2,1,0:T(8,128)S(1)}, f32[8,128]{1,0:T(8,128)S(1)}) custom-call(s32[1]{0:T(128)} %bitcast.1.where, bf16[128,2048]{1,0:T(8,128)(2,1)S(1)} %shard_map.49.refs_0_, bf16[128,2048]{1,0:T(8,128)(2,1)S(1)} %collective-permute-done.12.refs_1_, bf16[2,1,1792,2048]{3,2,1,0:T(8,128)(2,1)S(1)} %copy-done.3, ...), custom_call_target="tpu_custom_call" | custom-call | flops 1000000 | bytes 1024 | tf_op jit(solution)/shard_map/pallas_call | solution.py:41
  95.0 1.8 %shard_map.52 = f32[2,256]{1,0:T(2,128)S(1)} custom-call(s32[1]{0:T(128)} %bitcast.where, bf16[1792,128]{1,0:T(8,128)(2,1)} %shard_map.48.refs_0_, bf16[1792,128]{1,0:T(8,128)(2,1)S(1)} %shard_map.51.refs_1_, f32[2,1792,256]{2,1,0:T(8,128)S(1)} %get-tuple-element.27.refs_2_), custom_call_target="tpu_custom_call" | custom-call | flops 14000000000 | bytes 1024 | tf_op jit(solution)/shard_map/pallas_call | solution.py:41
  96.9 3.0 %collective-permute-start.13 = (f32[2,256]{1,0:T(2,128)S(1)}, f32[2,256]{1,0:T(2,128)S(1)}, u32[]{:S(2)}, u32[]{:S(2)}) collective-permute-start(f32[2,256]{1,0:T(2,128)S(1)} %shard_map.52), channel_id=1, source_target_pairs={{0,8},{4,12},{8,0},{12,4},{1,9},{5,13},{9,1},{13,5},{2,10},{6,14},... | collective-permute-start | bytes 6152 | tf_op jit(solution)/shard_map/ppermute | solution.py:22
  101.4 4.3 %collective-permute-done.16 = f32[2,256]{1,0:T(2,128)S(1)} collective-permute-done((f32[2,256]{1,0:T(2,128)S(1)}, f32[2,256]{1,0:T(2,128)S(1)}, u32[]{:S(2)}, u32[]{:S(2)}) %collective-permute-start.16) | collective-permute-done | bytes 2080 | tf_op jit(solution)/shard_map/ppermute | solution.py:22
  105.8 1.2 %collective-permute-done.17 = f32[2,256]{1,0:T(2,128)S(1)} collective-permute-done((f32[2,256]{1,0:T(2,128)S(1)}, f32[2,256]{1,0:T(2,128)S(1)}, u32[]{:S(2)}, u32[]{:S(2)}) %collective-permute-start.17) | collective-permute-done | bytes 2080 | tf_op jit(solution)/shard_map/ppermute | solution.py:22
  107.5 3.0 %collective-permute-done.18 = f32[2,256]{1,0:T(2,128)S(1)} collective-permute-done((f32[2,256]{1,0:T(2,128)S(1)}, f32[2,256]{1,0:T(2,128)S(1)}, u32[]{:S(2)}, u32[]{:S(2)}) %collective-permute-start.18) | collective-permute-done | bytes 2080 | tf_op jit(solution)/shard_map/ppermute | solution.py:22
  (52 shorter events, 5.9 us)
Async XLA Ops:
  0.0 15.4 %copy-start.4 = (bf16[256,2048]{1,0:T(8,128)(2,1)S(1)}, bf16[256,2048]{1,0:T(8,128)(2,1)}, u32[]{:S(2)}) copy-start(bf16[256,2048]{1,0:T(8,128)(2,1)} %refs_1_.1) | copy-start | bytes 3145732
  1.2 24.2 %collective-permute-start.1 = (bf16[128,2048]{1,0:T(8,128)(2,1)S(1)}, bf16[128,2048]{1,0:T(8,128)(2,1)S(1)}, u32[]{:S(2)}, u32[]{:S(2)}) collective-permute-start(bf16[128,2048]{1,0:T(8,128)(2,1)S(1)} %constant_dynamic-slice_fusion), channel_id=1, source_target_pairs={{0,4},{4,8},{8,12},{1,5},{5,9},{9,13},{2,6},{6,10},{10,14},{3,7},{... | collective-permute-start | bytes 1572872 | tf_op jit(solution)/shard_map/ppermute | solution.py:26
  6.1 19.3 %collective-permute-start.2 = (bf16[128,2048]{1,0:T(8,128)(2,1)S(1)}, bf16[128,2048]{1,0:T(8,128)(2,1)S(1)}, u32[]{:S(2)}, u32[]{:S(2)}) collective-permute-start(bf16[128,2048]{1,0:T(8,128)(2,1)S(1)} %constant_dynamic-slice_fusion), channel_id=1, source_target_pairs={{4,0},{8,4},{12,8},{5,1},{9,5},{13,9},{6,2},{10,6},{14,10},{7,3},{... | collective-permute-start | bytes 1572872 | tf_op jit(solution)/shard_map/ppermute | solution.py:27
  9.6 27.6 %collective-permute-start.5 = (bf16[128,1792]{1,0:T(8,128)(2,1)}, bf16[128,1792]{1,0:T(8,128)(2,1)S(1)}, u32[]{:S(2)}, u32[]{:S(2)}) collective-permute-start(bf16[128,1792]{1,0:T(8,128)(2,1)} %get-tuple-element.29.refs_5_), channel_id=1, source_target_pairs={{0,12},{4,8},{8,4},{12,0},{1,13},{5,9},{9,5},{13,1},{2,14},{6,10},... | collective-permute-start | bytes 1376264 | tf_op jit(solution)/shard_map/ppermute | solution.py:22
  15.4 5.2 %copy-start = (bf16[2,1,1792,2048]{3,2,1,0:T(8,128)(2,1)S(1)}, bf16[2,1,1792,2048]{3,2,1,0:T(8,128)(2,1)}, u32[]{:S(2)}) copy-start(bf16[2,1,1792,2048]{3,2,1,0:T(8,128)(2,1)} %refs_2_.7) | copy-start | bytes 44040196
  25.4 11.8 %copy-start.7 = (f32[2,1792,256]{2,1,0:T(8,128)}, f32[2,1792,256]{2,1,0:T(8,128)S(1)}, u32[]{:S(2)}) copy-start(f32[2,1792,256]{2,1,0:T(8,128)S(1)} %get-tuple-element.19.refs_1_) | copy-start | bytes 11010052
  25.5 21.8 %collective-permute-start.4 = (bf16[128,2048]{1,0:T(8,128)(2,1)S(1)}, bf16[128,2048]{1,0:T(8,128)(2,1)S(1)}, u32[]{:S(2)}, u32[]{:S(2)}) collective-permute-start(bf16[128,2048]{1,0:T(8,128)(2,1)S(1)} %shard_map.43.refs_0_), channel_id=1, source_target_pairs={{0,1},{1,0},{2,3},{3,2},{4,5},{5,4},{6,7},{7,6},{8,9},{9,8},{10,11... | collective-permute-start | bytes 1572872 | tf_op jit(solution)/shard_map/ppermute | solution.py:22
  25.6 20.3 %collective-permute-start = (bf16[1792,128]{1,0:T(8,128)(2,1)S(1)}, bf16[1792,128]{1,0:T(8,128)(2,1)S(1)}, u32[]{:S(2)}, u32[]{:S(2)}) collective-permute-start(bf16[1792,128]{1,0:T(8,128)(2,1)S(1)} %get-tuple-element.17.refs_3_), channel_id=1, source_target_pairs={{0,4},{4,0},{8,12},{12,8},{1,5},{5,1},{9,13},{13,9},{2,6},{6,2},{1... | collective-permute-start | bytes 1376264 | tf_op jit(solution)/shard_map/ppermute | solution.py:22
  34.4 27.5 %collective-permute-start.10 = (bf16[128,2048]{1,0:T(8,128)(2,1)S(1)}, bf16[128,2048]{1,0:T(8,128)(2,1)}, u32[]{:S(2)}, u32[]{:S(2)}) collective-permute-start(bf16[128,2048]{1,0:T(8,128)(2,1)S(1)} %get-tuple-element.22.refs_2_.refs_0_.refs_1_), channel_id=1, source_target_pairs={{4,0},{8,4},{5,1},{9,5},{6,2},{10,6},{7,3},{11,7},{20,16},{24,20},... | collective-permute-start | bytes 1572872 | tf_op jit(solution)/shard_map/ppermute | solution.py:27
  35.7 26.2 %collective-permute-start.11 = (bf16[128,2048]{1,0:T(8,128)(2,1)S(1)}, bf16[128,2048]{1,0:T(8,128)(2,1)}, u32[]{:S(2)}, u32[]{:S(2)}) collective-permute-start(bf16[128,2048]{1,0:T(8,128)(2,1)S(1)} %get-tuple-element.21.refs_1_.refs_2_), channel_id=1, source_target_pairs={{4,8},{8,12},{5,9},{9,13},{6,10},{10,14},{7,11},{11,15},{20,24},{2... | collective-permute-start | bytes 1572872 | tf_op jit(solution)/shard_map/ppermute | solution.py:26
  37.2 24.7 %collective-permute-start.6 = (bf16[128,1792]{1,0:T(8,128)(2,1)S(1)}, bf16[128,1792]{1,0:T(8,128)(2,1)}, u32[]{:S(2)}, u32[]{:S(2)}) collective-permute-start(bf16[128,1792]{1,0:T(8,128)(2,1)S(1)} %shard_map.45.refs_0_.refs_3_), channel_id=1, source_target_pairs={{0,2},{2,0},{1,3},{3,1},{4,6},{6,4},{5,7},{7,5},{8,10},{10,8},{9,1... | collective-permute-start | bytes 1376264 | tf_op jit(solution)/shard_map/ppermute | solution.py:22
  45.8 32.5 %collective-permute-start.3 = (bf16[1792,128]{1,0:T(8,128)(2,1)S(1)}, bf16[1792,128]{1,0:T(8,128)(2,1)}, u32[]{:S(2)}, u32[]{:S(2)}) collective-permute-start(bf16[1792,128]{1,0:T(8,128)(2,1)S(1)} %shard_map.42.refs_0_), channel_id=1, source_target_pairs={{0,2},{2,0},{1,3},{3,1},{4,6},{6,4},{5,7},{7,5},{8,10},{10,8},{9,1... | collective-permute-start | bytes 1376264 | tf_op jit(solution)/shard_map/ppermute | solution.py:22
  47.3 0.8 copy-start.9
  48.1 31.9 %collective-permute-start.8 = (bf16[1792,128]{1,0:T(8,128)(2,1)}, bf16[1792,128]{1,0:T(8,128)(2,1)}, u32[]{:S(2)}, u32[]{:S(2)}) collective-permute-start(bf16[1792,128]{1,0:T(8,128)(2,1)} %get-tuple-element.18.refs_4_), channel_id=1, source_target_pairs={{0,8},{4,12},{8,0},{12,4},{1,9},{5,13},{9,1},{13,5},{2,10},{6,14},... | collective-permute-start | bytes 1376264 | tf_op jit(solution)/shard_map/ppermute | solution.py:22
  48.1 2.3 %copy-start.8 = (f32[2,1792,256]{2,1,0:T(8,128)S(1)}, f32[2,1792,256]{2,1,0:T(8,128)}, u32[]{:S(2)}) copy-start(f32[2,1792,256]{2,1,0:T(8,128)} %copy-done.7) | copy-start | bytes 11010052
  50.9 5.2 %copy-start.1 = (bf16[2,1,1792,2048]{3,2,1,0:T(8,128)(2,1)S(1)}, bf16[2,1,1792,2048]{3,2,1,0:T(8,128)(2,1)}, u32[]{:S(2)}) copy-start(bf16[2,1,1792,2048]{3,2,1,0:T(8,128)(2,1)} %refs_2_.7) | copy-start | bytes 44040196
  56.0 1.0 copy-start.10
  63.2 21.7 %collective-permute-start.12 = (bf16[128,2048]{1,0:T(8,128)(2,1)S(1)}, bf16[128,2048]{1,0:T(8,128)(2,1)S(1)}, u32[]{:S(2)}, u32[]{:S(2)}) collective-permute-start(bf16[128,2048]{1,0:T(8,128)(2,1)S(1)} %shard_map.49.refs_0_), channel_id=1, source_target_pairs={{0,1},{1,0},{2,3},{3,2},{4,5},{5,4},{6,7},{7,6},{8,9},{9,8},{10,11... | collective-permute-start | bytes 1572872 | tf_op jit(solution)/shard_map/ppermute | solution.py:22
  63.3 31.6 %collective-permute-start.14 = (bf16[128,2048]{1,0:T(8,128)(2,1)S(1)}, bf16[128,2048]{1,0:T(8,128)(2,1)S(1)}, u32[]{:S(2)}, u32[]{:S(2)}) collective-permute-start(bf16[128,2048]{1,0:T(8,128)(2,1)S(1)} %shard_map.49.refs_0_), channel_id=1, source_target_pairs={{4,0},{8,12},{5,1},{9,13},{6,2},{10,14},{7,3},{11,15},{20,16},{24,... | collective-permute-start | bytes 1572872 | tf_op jit(solution)/shard_map/ppermute | solution.py:263
  64.6 5.2 %copy-start.2 = (bf16[2,1,1792,2048]{3,2,1,0:T(8,128)(2,1)S(1)}, bf16[2,1,1792,2048]{3,2,1,0:T(8,128)(2,1)}, u32[]{:S(2)}) copy-start(bf16[2,1,1792,2048]{3,2,1,0:T(8,128)(2,1)} %refs_2_.7) | copy-start | bytes 44040196
  76.3 2.0 %copy-start.5 = (f32[2,256,2048]{2,1,0:T(8,128)}, f32[2,256,2048]{2,1,0:T(8,128)S(1)}, u32[]{:S(2)}) copy-start(f32[2,256,2048]{2,1,0:T(8,128)S(1)} %get-tuple-element.28.refs_2_) | copy-start | bytes 12582916
  80.0 15.0 %collective-permute-start.9 = (bf16[1792,128]{1,0:T(8,128)(2,1)}, bf16[1792,128]{1,0:T(8,128)(2,1)S(1)}, u32[]{:S(2)}, u32[]{:S(2)}) collective-permute-start(bf16[1792,128]{1,0:T(8,128)(2,1)} %shard_map.48.refs_0_), channel_id=1, source_target_pairs={{0,2},{2,0},{1,3},{3,1},{4,6},{6,4},{5,7},{7,5},{8,10},{10,8},{9,1... | collective-permute-start | bytes 1376264 | tf_op jit(solution)/shard_map/ppermute | solution.py:22
  80.6 20.7 %collective-permute-start.7 = (f32[2,256]{1,0:T(2,128)S(1)}, f32[2,256]{1,0:T(2,128)S(1)}, u32[]{:S(2)}, u32[]{:S(2)}) collective-permute-start(f32[2,256]{1,0:T(2,128)S(1)} %shard_map.47.refs_1_.refs_3_), channel_id=1, source_target_pairs={{0,4},{4,0},{8,12},{12,8},{1,5},{5,1},{9,13},{13,9},{2,6},{6,2},{1... | collective-permute-start | bytes 6152 | tf_op jit(solution)/shard_map/ppermute | solution.py:22
  84.9 5.2 %copy-start.3 = (bf16[2,1,1792,2048]{3,2,1,0:T(8,128)(2,1)S(1)}, bf16[2,1,1792,2048]{3,2,1,0:T(8,128)(2,1)}, u32[]{:S(2)}) copy-start(bf16[2,1,1792,2048]{3,2,1,0:T(8,128)(2,1)} %refs_2_.7) | copy-start | bytes 44040196
  94.9 5.0 %collective-permute-start.15 = (bf16[128,2048]{1,0:T(8,128)(2,1)S(1)}, bf16[128,2048]{1,0:T(8,128)(2,1)S(1)}, u32[]{:S(2)}, u32[]{:S(2)}) collective-permute-start(bf16[128,2048]{1,0:T(8,128)(2,1)S(1)} %shard_map.53.refs_0_), channel_id=1, source_target_pairs={{0,1},{1,0},{2,3},{3,2},{4,5},{5,4},{6,7},{7,6},{8,9},{9,8},{10,11... | collective-permute-start | bytes 1572872 | tf_op jit(solution)/shard_map/ppermute | solution.py:22
  95.0 4.9 %copy-start.6 = (f32[2,256,2048]{2,1,0:T(8,128)S(1)}, f32[2,256,2048]{2,1,0:T(8,128)}, u32[]{:S(2)}) copy-start(f32[2,256,2048]{2,1,0:T(8,128)} %copy-done.5) | copy-start | bytes 12582916
  96.9 4.6 %collective-permute-start.13 = (f32[2,256]{1,0:T(2,128)S(1)}, f32[2,256]{1,0:T(2,128)S(1)}, u32[]{:S(2)}, u32[]{:S(2)}) collective-permute-start(f32[2,256]{1,0:T(2,128)S(1)} %shard_map.52), channel_id=1, source_target_pairs={{0,8},{4,12},{8,0},{12,4},{1,9},{5,13},{9,1},{13,5},{2,10},{6,14},... | collective-permute-start | bytes 6152 | tf_op jit(solution)/shard_map/ppermute | solution.py:22
  100.3 5.4 %collective-permute-start.16 = (f32[2,256]{1,0:T(2,128)S(1)}, f32[2,256]{1,0:T(2,128)S(1)}, u32[]{:S(2)}, u32[]{:S(2)}) collective-permute-start(f32[2,256]{1,0:T(2,128)S(1)} %shard_map.54), channel_id=1, source_target_pairs={{0,12},{4,8},{8,4},{12,0},{1,13},{5,9},{9,5},{13,1},{2,14},{6,10},... | collective-permute-start | bytes 6152 | tf_op jit(solution)/shard_map/ppermute | solution.py:22
  105.8 1.2 %collective-permute-start.17 = (f32[2,256]{1,0:T(2,128)S(1)}, f32[2,256]{1,0:T(2,128)S(1)}, u32[]{:S(2)}, u32[]{:S(2)}) collective-permute-start(f32[2,256]{1,0:T(2,128)S(1)} %add_add_fusion), channel_id=1, source_target_pairs={{0,1},{1,0},{2,3},{3,2},{4,5},{5,4},{6,7},{7,6},{8,9},{9,8},{10,11... | collective-permute-start | bytes 6152 | tf_op jit(solution)/shard_map/ppermute | solution.py:22
  106.9 3.6 %collective-permute-start.18 = (f32[2,256]{1,0:T(2,128)S(1)}, f32[2,256]{1,0:T(2,128)S(1)}, u32[]{:S(2)}, u32[]{:S(2)}) collective-permute-start(f32[2,256]{1,0:T(2,128)S(1)} %add.44), channel_id=1, source_target_pairs={{0,2},{2,0},{1,3},{3,1},{4,6},{6,4},{5,7},{7,5},{8,10},{10,8},{9,1... | collective-permute-start | bytes 6152 | tf_op jit(solution)/shard_map/ppermute | solution.py:22

commit v11 on v10

v11 whole, which is shorter than its diff:
```python
import functools
import math

import jax
import jax.numpy as jnp
from jax import lax
from jax.experimental import pallas as pl
from jax.experimental.pallas import tpu as pltpu
from jax.sharding import PartitionSpec as P


LONG, SHORT = 14_000_000_000, 1_000_000


def trade(block, steps, backwards=False):
    axes = tuple(steps)
    sizes = [lax.axis_size(axis) for axis in axes]
    mask = 0
    for axis, size in zip(axes, sizes):
        mask = mask * size + steps[axis]
    route = [(i, i ^ mask) for i in range(math.prod(sizes))]
    return lax.ppermute(block, axes, route[::-1] if backwards else route)


def pass_on(block, step, count):
    up = lax.ppermute(block[0], "dp", [(i, i + 1) for i in range(step - 1, count - 1)])
    down = lax.ppermute(block[1], "dp", [(i, i - 1) for i in range(1, count - step + 1)])
    return up, down


ANYWHERE = pl.BlockSpec(memory_space=pl.ANY)
SCALARS = pl.BlockSpec(memory_space=pltpu.SMEM)
NEAR = pl.BlockSpec(memory_space=pltpu.VMEM)


def call(kernel, where, arrays, outs, flops, tokens=(), scratch=()):
    skip = len(tokens)

    def body(where, *refs):
        kernel(where, *refs[: len(arrays)], *refs[len(arrays) + skip :])

    return pl.pallas_call(
        body,
        in_specs=[SCALARS] + [NEAR] * len(arrays) + [ANYWHERE] * skip,
        out_specs=[NEAR] * len(outs),
        out_shape=[pltpu.VMEM(shape, dtype) for shape, dtype in outs],
        scratch_shapes=list(scratch),
        compiler_params=pltpu.CompilerParams(vmem_limit_bytes=12 * 1024 * 1024),
        cost_estimate=pl.CostEstimate(flops=flops, bytes_accessed=1024, transcendentals=0),
    )(
        jnp.stack([jnp.asarray(w, jnp.int32) for w in where]),
        *[pltpu.with_memory_space_constraint(array, pltpu.VMEM) for array in arrays],
        *tokens,
    )


def load_kernel(far_ref, near_ref, arrived):
    copy = pltpu.make_async_copy(far_ref, near_ref, arrived)
    copy.start()
    copy.wait()


def loaded(array):
    return pl.pallas_call(
        load_kernel,
        in_specs=[ANYWHERE],
        out_specs=NEAR,
        out_shape=pltpu.VMEM(array.shape, array.dtype),
        scratch_shapes=[pltpu.SemaphoreType.DMA],
        compiler_params=pltpu.CompilerParams(vmem_limit_bytes=1024 * 1024),
        cost_estimate=pl.CostEstimate(flops=1024, bytes_accessed=1024, transcendentals=0),
    )(pltpu.with_memory_space_constraint(array, pltpu.HBM))


def hold(blocks, tokens):
    count = len(blocks)
    return pl.pallas_call(
        lambda *refs: None,
        in_specs=[ANYWHERE] * (count + len(tokens)),
        out_specs=[ANYWHERE] * count,
        out_shape=[jax.ShapeDtypeStruct(block.shape, block.dtype) for block in blocks],
        input_output_aliases={i: i for i in range(count)},
        compiler_params=pltpu.CompilerParams(vmem_limit_bytes=1024 * 1024),
        cost_estimate=pl.CostEstimate(flops=1024, bytes_accessed=1024, transcendentals=0),
    )(*blocks, *tokens)


def turn_kernel(where, *refs):
    count = len(refs) // 2
    for block, out in zip(refs[:count], refs[count:]):
        out[...] = block[...].astype(jnp.float32).T.astype(block.dtype)


def turned(blocks):
    rows, width = blocks[0].shape
    if rows % 128 or width % 128:
        return [block.T for block in blocks]
    return call(turn_kernel, [0], blocks, [((width, rows), block.dtype) for block in blocks], 1024)


def pick_kernel(where, *refs):
    *blocks, out_ref = refs
    for k, block in enumerate(blocks):

        @pl.when(where[0] == k)
        def _():
            out_ref[...] = block[...]


def from_partner(hops, me, d, count, tokens=()):
    sources, choice = [], []
    for z in range(count):
        away = z - (z ^ d)
        source = (abs(away), int(away < 0))
        if source not in sources:
            sources.append(source)
        choice.append(sources.index(source))
    where = functools.reduce(lambda found, z: jnp.where(me == z, choice[z], found), range(count), 0)
    blocks = [hops[step][way] for step, way in sources]
    return call(pick_kernel, [where], blocks, [(blocks[0].shape, blocks[0].dtype)], 1024, tokens)[0]


def joined(parts, where, axis):
    found = []
    for p in range(len(parts)):
        chosen = parts[0][...]
        for r in range(1, len(parts)):
            chosen = jnp.where(where[0] == p ^ r, parts[r][...], chosen)
        found.append(chosen)
    return found[0] if len(found) == 1 else jnp.concatenate(found, axis=axis)


MARK = (8, 128), jnp.float32


def mix_kernel(where, *refs):
    *parts, query_ref, out_ref, mark_ref, acts = refs
    mark_ref[...] = jnp.zeros_like(mark_ref)
    half = parts[0].shape[0]
    acts[pl.ds(pl.multiple_of(where[0] * half, half), half), :] = parts[0][...]
    if len(parts) > 1:
        acts[pl.ds(pl.multiple_of((1 - where[0]) * half, half), half), :] = parts[1][...]
    nq, _, depth, _ = query_ref.shape
    tile = depth // 2

    def step(at, _):
        q, rows = at // 2, pl.ds(pl.multiple_of(at % 2 * tile, tile), tile)
        out_ref[q, rows, :] = lax.dot_general(
            query_ref[q, 0, rows, :], acts[...], (((1,), (1,)), ((), ())), preferred_element_type=jnp.float32
        )
        return 0

    lax.fori_loop(0, 2 * nq, step, 0)


def mixed(parts, core, queries, flops, tokens=()):
    nq, _, depth, width = queries.shape
    tokens_here = sum(part.shape[0] for part in parts)
    outs = [((nq, depth, tokens_here), jnp.float32), MARK]
    scratch = [pltpu.VMEM((tokens_here, width), queries.dtype)]
    return call(mix_kernel, [core], [*parts, queries], outs, flops, tokens, scratch)


def score_kernel(where, *refs):
    *parts, mix_ref, out_ref = refs
    grads = joined(parts, where, 1).astype(jnp.float32)
    for q in range(mix_ref.shape[0]):
        out_ref[q : q + 1, :] = jnp.sum(grads * mix_ref[q], axis=0, keepdims=True)


def scores_of_grads(parts, column, mix, tokens=(), flops=1024):
    nq, _, count = mix.shape
    return call(score_kernel, [column], [*parts, mix], [((nq, count), jnp.float32)], flops, tokens)[0]


def project_kernel(where, *refs):
    *parts, query_ref, out_ref, mark_ref, grads = refs
    mark_ref[...] = jnp.zeros_like(mark_ref)
    grads[...] = joined(parts, where, 0)
    nq, _, _, width = query_ref.shape
    tile = width // 2

    def step(at, _):
        q, columns = at // 2, pl.ds(pl.multiple_of(at % 2 * tile, tile), tile)
        out_ref[q, :, columns] = jnp.dot(
            grads[...], query_ref[q, 0, :, columns], preferred_element_type=jnp.float32
        )
        return 0

    lax.fori_loop(0, 2 * nq, step, 0)


def projected(parts, column, queries, flops, tokens=()):
    nq, _, depth, width = queries.shape
    count = sum(part.shape[0] for part in parts)
    outs = [((nq, count, width), jnp.float32), MARK]
    scratch = [pltpu.VMEM((count, depth), queries.dtype)]
    return call(project_kernel, [column], [*parts, queries], outs, flops, tokens, scratch)


def finish_kernel(where, mine_ref, other_ref, proj_ref, out_ref):
    half, width = mine_ref.shape
    swapped = where[0] == 1
    for h, (first, second) in enumerate(((mine_ref, other_ref), (other_ref, mine_ref))):
        acts = jnp.where(swapped, second[...], first[...]).astype(jnp.float32)
        for q in range(proj_ref.shape[0]):
            terms = acts * proj_ref[q, h * half : (h + 1) * half, :]
            lanes = terms[:, :128]
            for at in range(128, width, 128):
                lanes = lanes + terms[:, at : at + 128]
            out_ref[q : q + 1, h * half : (h + 1) * half] = jnp.sum(lanes.T, axis=0, keepdims=True)


def scores_of_acts(mine, other, core, proj, tokens=()):
    nq, count, _ = proj.shape
    return call(finish_kernel, [core], [mine, other, proj], [((nq, count), jnp.float32)], 1024, tokens)[0]


def on_device(activations, out_grads, queries):
    count, spread = lax.axis_size("dp"), lax.axis_size("din")
    me, column, core = lax.axis_index("dp"), lax.axis_index("din"), lax.axis_index("dout")
    tokens, rows = activations.shape[0], queries.shape[2]
    part, half = tokens // spread, tokens // 2

    def to_columns(arrived):
        return [arrived] + [trade(arrived, {"din": r}) for r in range(1, spread)]

    def acts_of(block):
        return [block, trade(block, {"dout": 1})]

    far, late = count - 1, count - 2
    early = list(range(1, late))

    mine = lax.dynamic_slice_in_dim(activations, core * half, half, 0)
    hops = [(mine, mine)]
    hops.append(pass_on(hops[0], 1, count))

    def grads_for(device, first, size):
        return lax.dynamic_slice(out_grads, (first, device * rows), (size, rows))

    sent = turned([grads_for(me ^ d, column * part, part) for d in early + [late]])
    sent = [*sent, grads_for(me ^ far, column * part, part)]
    arrived = {d: trade(block, {"dp": d}) for d, block in zip(early + [late, far], sent)}

    queries = loaded(queries)
    zero = jnp.zeros((), jnp.int32)
    mix, token = mixed([activations], zero, queries, SHORT, sent)
    own, = turned([grads_for(me, 0, tokens)])
    scores = scores_of_grads([own], zero, mix)
    hops[1] = hold(list(hops[1]), [token])
    for step in range(2, count - 1):
        hops.append(pass_on(hops[-1], step, count))

    mixes, token = {}, scores
    for d in early:
        mixes[d], token = mixed(acts_of(from_partner(hops, me, d, count)), core, queries, SHORT, [token])
    sides = to_columns(hold([arrived[far]], hops[1])[0])
    block = from_partner(hops, me, late, count, [token] + sides)
    end = lax.ppermute(block, "dp", [(1, 0), (count - 2, count - 1)])
    hops.append((end, end))

    proj, token = projected(sides, column, queries, SHORT, [token])
    for d in early:
        sides = to_columns(hold([arrived[d]], hops[1])[0])
        token = scores_of_grads(sides, column, mixes[d], [token])
        scores = scores + trade(token, {"dp": d})

    sides = to_columns(hold([arrived[late]], [token])[0])
    mix, token = mixed(acts_of(block), core, queries, SHORT, [token])
    sides = sides[:1] + list(hold(sides[1:], [token]))
    near = trade(scores_of_grads(sides, column, mix, (), LONG), {"dp": late})
    block = from_partner(hops, me, far, count, [token])
    scores = scores + near + trade(scores_of_acts(*acts_of(block), core, proj), {"dp": far})
    return over_chips(scores, spread)


def over_chips(scores, spread):
    scores = scores + trade(scores, {"dout": 1})
    return scores + sum(trade(scores, {"din": r}) for r in range(1, spread))


def solution(mesh):
    placed = (P(("groups", "dp"), "din"), P(("groups", "dp"), "dout"), P(None, "dout", "dp", "din"))
    return jax.shard_map(
        on_device, mesh=mesh, in_specs=placed, out_specs=P(None, ("groups", "dp")), check_vma=False
    )
```

time: 112 us -> 113 us (level)
  starting transfers between devices: 36.5 us -> 28.6 us
  Pallas kernels: 28.1 us -> 32.3 us
  local copies, waits for them, and re-layouts: 29.8 us -> 33.9 us
    ppermute x14, starting transfers between devices: 26.2 us -> 18.3 us  [trade(): return lax.ppermute(block, axes, route[::-1] if backwards else route)]
    pallas_call x13 -> x14, Pallas kernels: 28.1 us -> 32.3 us  [the longest x13 27.1 us: call(): pl.pallas_call(body, in_specs=[SCALARS] + [NEAR] * len(arrays) + [ANYWHER...]
    unnamed x22 -> x20, local copies, waits for them, and re-layouts: 25.1 us -> 28.4 us
  transfers between devices with their start and end apart: 19 -> 19, of which waited for: 5 -> 5; matrix products, arithmetic and copies ran while one was open for 3% -> 3% of each run, Pallas kernels for 25% -> 29%
where the time goes in v11:
time: 113 us; the launch traced here: 112 us
  local copies, waits for them, and re-layouts  33.9 us (30%)
  Pallas kernels  32.3 us (29%)
  starting transfers between devices  28.6 us (25%)
  waiting for transfers between devices  16.3 us (14%)
    unnamed x20, local copies, waits for them, and re-layouts  28.4 us
    pallas_call x13, Pallas kernels, call(): pl.pallas_call(body, in_specs=[SCALARS] + [NEAR] * len(arrays) + [ANYWHER...  27.1 us
    ppermute x14, starting transfers between devices, trade(): return lax.ppermute(block, axes, route[::-1] if backwards else route)  18.3 us
    ppermute x14, waiting for transfers between devices, trade(): return lax.ppermute(block, axes, route[::-1] if backwards else route)  16.3 us
    ppermute x2, starting transfers between devices, pass_on(): lax.ppermute(block[0], 'dp', [(i, i + 1) for i in range(step - 1, count -...  6.44 us
    pallas_call x1, Pallas kernels, loaded(): pl.pallas_call(load_kernel, in_specs=[ANYWHERE], out_specs=NEAR, out_shap...  5.18 us
    dynamic_slice x2, local copies, waits for them, and re-layouts, grads_for(): return lax.dynamic_slice(out_grads, (first, device * rows), (size, rows))  3.57 us
    ppermute x2, starting transfers between devices, pass_on(): lax.ppermute(block[1], 'dp', [(i, i - 1) for i in range(1, count - step +...  2.58 us
  transfers between devices with their start and end apart: 19, of which 5 were waited for; matrix products, arithmetic and copies ran while one was open for 3% of the time, Pallas kernels for 29%

profile of v11, /device:TPU:0, one launch (start us, length us, event | category | flops | bytes accessed | tf_op | source)
XLA Modules:
  0.0 112.0 jit_solution(12898515400291157905)
XLA Ops:
  0.0 1.9 %constant_dynamic-slice_fusion = bf16[128,2048]{1,0:T(8,128)(2,1)} fusion(bf16[256,2048]{1,0:T(8,128)(2,1)} %refs_0_.1, s32[]{:T(128)S(6)} %select_n.53), kind=kLoop, calls=%fused_computation.1 | loop fusion | bytes 1048580 | tf_op jit(solution)/shard_map/dynamic_slice | solution.py:234
  1.9 4.9 %collective-permute-start.1 = (bf16[128,2048]{1,0:T(8,128)(2,1)}, bf16[128,2048]{1,0:T(8,128)(2,1)S(1)}, u32[]{:S(2)}, u32[]{:S(2)}) collective-permute-start(bf16[128,2048]{1,0:T(8,128)(2,1)} %constant_dynamic-slice_fusion), channel_id=1, source_target_pairs={{0,4},{4,8},{8,12},{1,5},{5,9},{9,13},{2,6},{6,10},{10,14},{3,7},{... | collective-permute-start | bytes 1572872 | tf_op jit(solution)/shard_map/ppermute | solution.py:26
  6.8 1.3 %collective-permute-start.2 = (bf16[128,2048]{1,0:T(8,128)(2,1)}, bf16[128,2048]{1,0:T(8,128)(2,1)S(1)}, u32[]{:S(2)}, u32[]{:S(2)}) collective-permute-start(bf16[128,2048]{1,0:T(8,128)(2,1)} %constant_dynamic-slice_fusion), channel_id=1, source_target_pairs={{4,0},{8,4},{12,8},{5,1},{9,5},{13,9},{6,2},{10,6},{14,10},{7,3},{... | collective-permute-start | bytes 1572872 | tf_op jit(solution)/shard_map/ppermute | solution.py:27
  8.2 2.2 %fusion = (bf16[128,1792]{1,0:T(8,128)(2,1)}, bf16[128,1792]{1,0:T(8,128)(2,1)S(1)}, bf16[128,1792]{1,0:T(8,128)(2,1)S(1)}) fusion(bf16[256,7168]{1,0:T(8,128)(2,1)} %param.4, s32[]{:T(128)S(6)} %select_n.49, s32[]{:T(128)S(6)} %select_n.52, s32[]{:T(128)S(6)} %select_n.50, s32[]{:T(128)S(6)} %select_n.51), kind=kLoop, calls=%fused_computation.3 | loop fusion | bytes 2752528 | tf_op jit(solution)/shard_map/dynamic_slice | solution.py:239
  10.3 4.7 %collective-permute-start.5 = (bf16[128,1792]{1,0:T(8,128)(2,1)}, bf16[128,1792]{1,0:T(8,128)(2,1)S(1)}, u32[]{:S(2)}, u32[]{:S(2)}) collective-permute-start(bf16[128,1792]{1,0:T(8,128)(2,1)} %get-tuple-element.29.refs_4_), channel_id=1, source_target_pairs={{0,12},{4,8},{8,4},{12,0},{1,13},{5,9},{9,5},{13,1},{2,14},{6,10},... | collective-permute-start | bytes 1376264 | tf_op jit(solution)/shard_map/ppermute | solution.py:22
  15.0 5.2 %shard_map.38.refs_1_.refs_2_ = bf16[2,1,1792,2048]{3,2,1,0:T(8,128)(2,1)S(1)} custom-call(bf16[2,1,1792,2048]{3,2,1,0:T(8,128)(2,1)} %far_ref.1), custom_call_target="tpu_custom_call" | custom-call | flops 1024 | bytes 1024 | tf_op jit(solution)/shard_map/pallas_call | solution.py:64
  20.2 5.2 %copy-done = bf16[2,1,1792,2048]{3,2,1,0:T(8,128)(2,1)} copy-done((bf16[2,1,1792,2048]{3,2,1,0:T(8,128)(2,1)}, bf16[2,1,1792,2048]{3,2,1,0:T(8,128)(2,1)S(1)}, u32[]{:S(2)}) %copy-start) | copy-done | bytes 14680088
  26.5 5.2 %copy-done.1 = bf16[2,1,1792,2048]{3,2,1,0:T(8,128)(2,1)S(1)} copy-done((bf16[2,1,1792,2048]{3,2,1,0:T(8,128)(2,1)S(1)}, bf16[2,1,1792,2048]{3,2,1,0:T(8,128)(2,1)}, u32[]{:S(2)}) %copy-start.1) | copy-done | bytes 14680088
  31.6 4.7 %shard_map.40 = (f32[2,1792,256]{2,1,0:T(8,128)S(1)}, f32[8,128]{1,0:T(8,128)S(1)}) custom-call(s32[1]{0:T(128)} %constant.5.clone.1.where, bf16[256,2048]{1,0:T(8,128)(2,1)S(1)} %copy-done.9, bf16[2,1,1792,2048]{3,2,1,0:T(8,128)(2,1)S(1)} %copy-done.1, bf16[1792,128]{1,0:T(8,128)(2,1)S(1)} %get-tuple-element.17.refs_2_, ...), custom_call_target="tpu_custom_call" | custom-call | flops 1000000 | bytes 1024 | tf_op jit(solution)/shard_map/pallas_call | solution.py:42
  36.6 1.3 %collective-permute-start.10 = (bf16[128,2048]{1,0:T(8,128)(2,1)S(1)}, bf16[128,2048]{1,0:T(8,128)(2,1)}, u32[]{:S(2)}, u32[]{:S(2)}) collective-permute-start(bf16[128,2048]{1,0:T(8,128)(2,1)S(1)} %get-tuple-element.22.refs_2_.refs_0_.refs_1_), channel_id=1, source_target_pairs={{4,0},{8,4},{5,1},{9,5},{6,2},{10,6},{7,3},{11,7},{20,16},{24,20},... | collective-permute-start | bytes 1572872 | tf_op jit(solution)/shard_map/ppermute | solution.py:27
  37.9 1.5 %collective-permute-start.11 = (bf16[128,2048]{1,0:T(8,128)(2,1)S(1)}, bf16[128,2048]{1,0:T(8,128)(2,1)}, u32[]{:S(2)}, u32[]{:S(2)}) collective-permute-start(bf16[128,2048]{1,0:T(8,128)(2,1)S(1)} %get-tuple-element.21.refs_1_.refs_2_), channel_id=1, source_target_pairs={{4,8},{8,12},{5,9},{9,13},{6,10},{10,14},{7,11},{11,15},{20,24},{2... | collective-permute-start | bytes 1572872 | tf_op jit(solution)/shard_map/ppermute | solution.py:26
  39.4 1.5 %collective-permute-start.6 = (bf16[128,1792]{1,0:T(8,128)(2,1)S(1)}, bf16[128,1792]{1,0:T(8,128)(2,1)S(1)}, u32[]{:S(2)}, u32[]{:S(2)}) collective-permute-start(bf16[128,1792]{1,0:T(8,128)(2,1)S(1)} %shard_map.46.refs_0_.refs_3_), channel_id=1, source_target_pairs={{0,2},{2,0},{1,3},{3,1},{4,6},{6,4},{5,7},{7,5},{8,10},{10,8},{9,1... | collective-permute-start | bytes 1376264 | tf_op jit(solution)/shard_map/ppermute | solution.py:22
  40.9 9.0 %collective-permute-done.refs_0_ = bf16[1792,128]{1,0:T(8,128)(2,1)S(1)} collective-permute-done((bf16[1792,128]{1,0:T(8,128)(2,1)S(1)}, bf16[1792,128]{1,0:T(8,128)(2,1)S(1)}, u32[]{:S(2)}, u32[]{:S(2)}) %collective-permute-start) | collective-permute-done | bytes 458784 | tf_op jit(solution)/shard_map/ppermute | solution.py:22
  49.9 1.5 %collective-permute-start.3 = (bf16[1792,128]{1,0:T(8,128)(2,1)S(1)}, bf16[1792,128]{1,0:T(8,128)(2,1)}, u32[]{:S(2)}, u32[]{:S(2)}) collective-permute-start(bf16[1792,128]{1,0:T(8,128)(2,1)S(1)} %shard_map.43.refs_0_), channel_id=1, source_target_pairs={{0,2},{2,0},{1,3},{3,1},{4,6},{6,4},{5,7},{7,5},{8,10},{10,8},{9,1... | collective-permute-start | bytes 1376264 | tf_op jit(solution)/shard_map/ppermute | solution.py:22
  51.5 1.4 %constant_dynamic-slice_fusion.1.refs_0_ = bf16[256,1792]{1,0:T(8,128)(2,1)S(1)} fusion(bf16[256,7168]{1,0:T(8,128)(2,1)} %param.4, s32[]{:T(128)S(6)} %select_n.48), kind=kLoop, calls=%fused_computation.2 | loop fusion | bytes 1835012 | tf_op jit(solution)/shard_map/dynamic_slice | solution.py:239
  54.2 5.2 %copy-done.2 = bf16[2,1,1792,2048]{3,2,1,0:T(8,128)(2,1)S(1)} copy-done((bf16[2,1,1792,2048]{3,2,1,0:T(8,128)(2,1)S(1)}, bf16[2,1,1792,2048]{3,2,1,0:T(8,128)(2,1)}, u32[]{:S(2)}) %copy-start.2) | copy-done | bytes 14680088
  59.4 4.7 %shard_map.45 = (f32[2,1792,256]{2,1,0:T(8,128)S(1)}, f32[8,128]{1,0:T(8,128)S(1)}) custom-call(s32[1]{0:T(128)} %bitcast.1.where, bf16[128,2048]{1,0:T(8,128)(2,1)S(1)} %shard_map.44.refs_0_, bf16[128,2048]{1,0:T(8,128)(2,1)S(1)} %collective-permute-done.4.refs_1_, bf16[2,1,1792,2048]{3,2,1,0:T(8,128)(2,1)S(1)} %copy-done.2, f32[2,256]{1,0:T(2,128)S(1)} %shard_map.41.refs_3_), custom_call_target="tpu_custom_call" | custom-call | flops 1000000 | bytes 1024 | tf_op jit(solution)/shard_map/pallas_call | solution.py:42
  64.1 1.2 %shard_map.50.refs_0_ = bf16[128,2048]{1,0:T(8,128)(2,1)S(1)} custom-call(s32[1]{0:T(128)} %bitcast.3.where, bf16[128,2048]{1,0:T(8,128)(2,1)} %collective-permute-done.10.refs_0_, bf16[128,2048]{1,0:T(8,128)(2,1)} %collective-permute-done.11.refs_1_, f32[8,128]{1,0:T(8,128)S(1)} %get-tuple-element.24.refs_3_.refs_2_, ...), custom_call_target="tpu_custom_call" | custom-call | flops 1024 | bytes 1024 | tf_op jit(solution)/shard_map/pallas_call | solution.py:42
  65.5 1.3 %collective-permute-start.14 = (bf16[128,2048]{1,0:T(8,128)(2,1)S(1)}, bf16[128,2048]{1,0:T(8,128)(2,1)S(1)}, u32[]{:S(2)}, u32[]{:S(2)}) collective-permute-start(bf16[128,2048]{1,0:T(8,128)(2,1)S(1)} %shard_map.50.refs_0_), channel_id=1, source_target_pairs={{4,0},{8,12},{5,1},{9,13},{6,2},{10,14},{7,3},{11,15},{20,16},{24,... | collective-permute-start | bytes 1572872 | tf_op jit(solution)/shard_map/ppermute | solution.py:259
  66.8 5.2 %copy-done.3 = bf16[2,1,1792,2048]{3,2,1,0:T(8,128)(2,1)S(1)} copy-done((bf16[2,1,1792,2048]{3,2,1,0:T(8,128)(2,1)S(1)}, bf16[2,1,1792,2048]{3,2,1,0:T(8,128)(2,1)}, u32[]{:S(2)}) %copy-start.3) | copy-done | bytes 14680088
  72.0 4.8 %shard_map.47 = (f32[2,256,2048]{2,1,0:T(8,128)S(1)}, f32[8,128]{1,0:T(8,128)S(1)}) custom-call(s32[1]{0:T(128)} %bitcast.where, bf16[128,1792]{1,0:T(8,128)(2,1)S(1)} %shard_map.46.refs_0_.refs_3_, bf16[128,1792]{1,0:T(8,128)(2,1)S(1)} %collective-permute-done.6.refs_1_.refs_4_, bf16[2,1,1792,2048]{3,2,1,0:T(8,128)(2,1)S(1)} %copy-done.3, ...), custom_call_target="tpu_custom_call" | custom-call | flops 1000000 | bytes 1024 | tf_op jit(solution)/shard_map/pallas_call | solution.py:42
  76.7 2.0 %copy-done.5 = f32[2,256,2048]{2,1,0:T(8,128)} copy-done((f32[2,256,2048]{2,1,0:T(8,128)}, f32[2,256,2048]{2,1,0:T(8,128)S(1)}, u32[]{:S(2)}) %copy-start.5) | copy-done | bytes 4194328
  78.7 1.7 %shard_map.48.refs_1_.refs_3_ = f32[2,256]{1,0:T(2,128)S(1)} custom-call(s32[1]{0:T(128)} %bitcast.where, bf16[1792,128]{1,0:T(8,128)(2,1)S(1)} %shard_map.43.refs_0_, bf16[1792,128]{1,0:T(8,128)(2,1)} %collective-permute-done.3.refs_1_, f32[2,1792,256]{2,1,0:T(8,128)S(1)} %get-tuple-element.23.refs_2_, f32[8,128]{1,0:T(8,128)S(1)} %get-tuple-element.25.refs_3_), custom_call_target="tpu_custom_call" | custom-call | flops 1024 | bytes 1024 | tf_op jit(solution)/shard_map/pallas_call | solution.py:42
  81.0 4.3 %collective-permute-start.7 = (f32[2,256]{1,0:T(2,128)S(1)}, f32[2,256]{1,0:T(2,128)S(1)}, u32[]{:S(2)}, u32[]{:S(2)}) collective-permute-start(f32[2,256]{1,0:T(2,128)S(1)} %shard_map.48.refs_1_.refs_3_), channel_id=1, source_target_pairs={{0,4},{4,0},{8,12},{12,8},{1,5},{5,1},{9,13},{13,9},{2,6},{6,2},{1... | collective-permute-start | bytes 6152 | tf_op jit(solution)/shard_map/ppermute | solution.py:22
  85.3 5.2 %copy-done.4 = bf16[2,1,1792,2048]{3,2,1,0:T(8,128)(2,1)S(1)} copy-done((bf16[2,1,1792,2048]{3,2,1,0:T(8,128)(2,1)S(1)}, bf16[2,1,1792,2048]{3,2,1,0:T(8,128)(2,1)}, u32[]{:S(2)}) %copy-start.4) | copy-done | bytes 14680088
  90.4 5.7 %shard_map.51 = (f32[2,1792,256]{2,1,0:T(8,128)S(1)}, f32[8,128]{1,0:T(8,128)S(1)}) custom-call(s32[1]{0:T(128)} %bitcast.1.where, bf16[128,2048]{1,0:T(8,128)(2,1)S(1)} %shard_map.50.refs_0_, bf16[128,2048]{1,0:T(8,128)(2,1)} %collective-permute-done.12.refs_1_, bf16[2,1,1792,2048]{3,2,1,0:T(8,128)(2,1)S(1)} %copy-done.4, ...), custom_call_target="tpu_custom_call" | custom-call | flops 1000000 | bytes 1024 | tf_op jit(solution)/shard_map/pallas_call | solution.py:42
  96.3 1.8 %shard_map.53 = f32[2,256]{1,0:T(2,128)S(1)} custom-call(s32[1]{0:T(128)} %bitcast.where, bf16[1792,128]{1,0:T(8,128)(2,1)} %shard_map.49.refs_0_, bf16[1792,128]{1,0:T(8,128)(2,1)S(1)} %shard_map.52.refs_1_, f32[2,1792,256]{2,1,0:T(8,128)S(1)} %get-tuple-element.27.refs_2_), custom_call_target="tpu_custom_call" | custom-call | flops 14000000000 | bytes 1024 | tf_op jit(solution)/shard_map/pallas_call | solution.py:42
  98.2 2.6 %collective-permute-start.13 = (f32[2,256]{1,0:T(2,128)S(1)}, f32[2,256]{1,0:T(2,128)S(1)}, u32[]{:S(2)}, u32[]{:S(2)}) collective-permute-start(f32[2,256]{1,0:T(2,128)S(1)} %shard_map.53), channel_id=1, source_target_pairs={{0,8},{4,12},{8,0},{12,4},{1,9},{5,13},{9,1},{13,5},{2,10},{6,14},... | collective-permute-start | bytes 6152 | tf_op jit(solution)/shard_map/ppermute | solution.py:22
  101.3 1.4 %collective-permute-start.16 = (f32[2,256]{1,0:T(2,128)S(1)}, f32[2,256]{1,0:T(2,128)S(1)}, u32[]{:S(2)}, u32[]{:S(2)}) collective-permute-start(f32[2,256]{1,0:T(2,128)S(1)} %shard_map.55), channel_id=1, source_target_pairs={{0,12},{4,8},{8,4},{12,0},{1,13},{5,9},{9,5},{13,1},{2,14},{6,10},... | collective-permute-start | bytes 6152 | tf_op jit(solution)/shard_map/ppermute | solution.py:22
  102.7 4.0 %collective-permute-done.16 = f32[2,256]{1,0:T(2,128)S(1)} collective-permute-done((f32[2,256]{1,0:T(2,128)S(1)}, f32[2,256]{1,0:T(2,128)S(1)}, u32[]{:S(2)}, u32[]{:S(2)}) %collective-permute-start.16) | collective-permute-done | bytes 2080 | tf_op jit(solution)/shard_map/ppermute | solution.py:22
  107.9 1.5 %collective-permute-start.18 = (f32[2,256]{1,0:T(2,128)S(1)}, f32[2,256]{1,0:T(2,128)S(1)}, u32[]{:S(2)}, u32[]{:S(2)}) collective-permute-start(f32[2,256]{1,0:T(2,128)S(1)} %add.44), channel_id=1, source_target_pairs={{0,2},{2,0},{1,3},{3,1},{4,6},{6,4},{5,7},{7,5},{8,10},{10,8},{9,1... | collective-permute-start | bytes 6152 | tf_op jit(solution)/shard_map/ppermute | solution.py:22
  109.4 2.1 %collective-permute-done.18 = f32[2,256]{1,0:T(2,128)S(1)} collective-permute-done((f32[2,256]{1,0:T(2,128)S(1)}, f32[2,256]{1,0:T(2,128)S(1)}, u32[]{:S(2)}, u32[]{:S(2)}) %collective-permute-start.18) | collective-permute-done | bytes 2080 | tf_op jit(solution)/shard_map/ppermute | solution.py:22
  (51 shorter events, 5.7 us)
Async XLA Ops:
  1.9 34.5 %collective-permute-start.1 = (bf16[128,2048]{1,0:T(8,128)(2,1)}, bf16[128,2048]{1,0:T(8,128)(2,1)S(1)}, u32[]{:S(2)}, u32[]{:S(2)}) collective-permute-start(bf16[128,2048]{1,0:T(8,128)(2,1)} %constant_dynamic-slice_fusion), channel_id=1, source_target_pairs={{0,4},{4,8},{8,12},{1,5},{5,9},{9,13},{2,6},{6,10},{10,14},{3,7},{... | collective-permute-start | bytes 1572872 | tf_op jit(solution)/shard_map/ppermute | solution.py:26
  6.8 29.6 %collective-permute-start.2 = (bf16[128,2048]{1,0:T(8,128)(2,1)}, bf16[128,2048]{1,0:T(8,128)(2,1)S(1)}, u32[]{:S(2)}, u32[]{:S(2)}) collective-permute-start(bf16[128,2048]{1,0:T(8,128)(2,1)} %constant_dynamic-slice_fusion), channel_id=1, source_target_pairs={{4,0},{8,4},{12,8},{5,1},{9,5},{13,9},{6,2},{10,6},{14,10},{7,3},{... | collective-permute-start | bytes 1572872 | tf_op jit(solution)/shard_map/ppermute | solution.py:27
  10.3 16.1 %copy-start.9 = (bf16[256,2048]{1,0:T(8,128)(2,1)S(1)}, bf16[256,2048]{1,0:T(8,128)(2,1)}, u32[]{:S(2)}) copy-start(bf16[256,2048]{1,0:T(8,128)(2,1)} %refs_0_.1) | copy-start | bytes 3145732
  10.3 29.1 %collective-permute-start.5 = (bf16[128,1792]{1,0:T(8,128)(2,1)}, bf16[128,1792]{1,0:T(8,128)(2,1)S(1)}, u32[]{:S(2)}, u32[]{:S(2)}) collective-permute-start(bf16[128,1792]{1,0:T(8,128)(2,1)} %get-tuple-element.29.refs_4_), channel_id=1, source_target_pairs={{0,12},{4,8},{8,4},{12,0},{1,13},{5,9},{9,5},{13,1},{2,14},{6,10},... | collective-permute-start | bytes 1376264 | tf_op jit(solution)/shard_map/ppermute | solution.py:22
  20.2 5.2 %copy-start = (bf16[2,1,1792,2048]{3,2,1,0:T(8,128)(2,1)}, bf16[2,1,1792,2048]{3,2,1,0:T(8,128)(2,1)S(1)}, u32[]{:S(2)}) copy-start(bf16[2,1,1792,2048]{3,2,1,0:T(8,128)(2,1)S(1)} %shard_map.38.refs_1_.refs_2_) | copy-start | bytes 44040196
  26.5 5.2 %copy-start.1 = (bf16[2,1,1792,2048]{3,2,1,0:T(8,128)(2,1)S(1)}, bf16[2,1,1792,2048]{3,2,1,0:T(8,128)(2,1)}, u32[]{:S(2)}) copy-start(bf16[2,1,1792,2048]{3,2,1,0:T(8,128)(2,1)} %copy-done) | copy-start | bytes 44040196
  36.4 3.1 %copy-start.7 = (f32[2,1792,256]{2,1,0:T(8,128)}, f32[2,1792,256]{2,1,0:T(8,128)S(1)}, u32[]{:S(2)}) copy-start(f32[2,1792,256]{2,1,0:T(8,128)S(1)} %get-tuple-element.19.refs_1_) | copy-start | bytes 11010052
  36.5 15.0 %collective-permute-start.4 = (bf16[128,2048]{1,0:T(8,128)(2,1)S(1)}, bf16[128,2048]{1,0:T(8,128)(2,1)S(1)}, u32[]{:S(2)}, u32[]{:S(2)}) collective-permute-start(bf16[128,2048]{1,0:T(8,128)(2,1)S(1)} %shard_map.44.refs_0_), channel_id=1, source_target_pairs={{0,1},{1,0},{2,3},{3,2},{4,5},{5,4},{6,7},{7,6},{8,9},{9,8},{10,11... | collective-permute-start | bytes 1572872 | tf_op jit(solution)/shard_map/ppermute | solution.py:22
  36.6 13.4 %collective-permute-start = (bf16[1792,128]{1,0:T(8,128)(2,1)S(1)}, bf16[1792,128]{1,0:T(8,128)(2,1)S(1)}, u32[]{:S(2)}, u32[]{:S(2)}) collective-permute-start(bf16[1792,128]{1,0:T(8,128)(2,1)S(1)} %get-tuple-element.17.refs_2_), channel_id=1, source_target_pairs={{0,4},{4,0},{8,12},{12,8},{1,5},{5,1},{9,13},{13,9},{2,6},{6,2},{1... | collective-permute-start | bytes 1376264 | tf_op jit(solution)/shard_map/ppermute | solution.py:22
  36.6 27.5 %collective-permute-start.10 = (bf16[128,2048]{1,0:T(8,128)(2,1)S(1)}, bf16[128,2048]{1,0:T(8,128)(2,1)}, u32[]{:S(2)}, u32[]{:S(2)}) collective-permute-start(bf16[128,2048]{1,0:T(8,128)(2,1)S(1)} %get-tuple-element.22.refs_2_.refs_0_.refs_1_), channel_id=1, source_target_pairs={{4,0},{8,4},{5,1},{9,5},{6,2},{10,6},{7,3},{11,7},{20,16},{24,20},... | collective-permute-start | bytes 1572872 | tf_op jit(solution)/shard_map/ppermute | solution.py:27
  37.9 26.2 %collective-permute-start.11 = (bf16[128,2048]{1,0:T(8,128)(2,1)S(1)}, bf16[128,2048]{1,0:T(8,128)(2,1)}, u32[]{:S(2)}, u32[]{:S(2)}) collective-permute-start(bf16[128,2048]{1,0:T(8,128)(2,1)S(1)} %get-tuple-element.21.refs_1_.refs_2_), channel_id=1, source_target_pairs={{4,8},{8,12},{5,9},{9,13},{6,10},{10,14},{7,11},{11,15},{20,24},{2... | collective-permute-start | bytes 1572872 | tf_op jit(solution)/shard_map/ppermute | solution.py:26
  39.4 24.7 %collective-permute-start.6 = (bf16[128,1792]{1,0:T(8,128)(2,1)S(1)}, bf16[128,1792]{1,0:T(8,128)(2,1)S(1)}, u32[]{:S(2)}, u32[]{:S(2)}) collective-permute-start(bf16[128,1792]{1,0:T(8,128)(2,1)S(1)} %shard_map.46.refs_0_.refs_3_), channel_id=1, source_target_pairs={{0,2},{2,0},{1,3},{3,1},{4,6},{6,4},{5,7},{7,5},{8,10},{10,8},{9,1... | collective-permute-start | bytes 1376264 | tf_op jit(solution)/shard_map/ppermute | solution.py:22
  49.9 28.8 %collective-permute-start.3 = (bf16[1792,128]{1,0:T(8,128)(2,1)S(1)}, bf16[1792,128]{1,0:T(8,128)(2,1)}, u32[]{:S(2)}, u32[]{:S(2)}) collective-permute-start(bf16[1792,128]{1,0:T(8,128)(2,1)S(1)} %shard_map.43.refs_0_), channel_id=1, source_target_pairs={{0,2},{2,0},{1,3},{3,1},{4,6},{6,4},{5,7},{7,5},{8,10},{10,8},{9,1... | collective-permute-start | bytes 1376264 | tf_op jit(solution)/shard_map/ppermute | solution.py:22
  51.4 29.0 %collective-permute-start.8 = (bf16[1792,128]{1,0:T(8,128)(2,1)}, bf16[1792,128]{1,0:T(8,128)(2,1)}, u32[]{:S(2)}, u32[]{:S(2)}) collective-permute-start(bf16[1792,128]{1,0:T(8,128)(2,1)} %get-tuple-element.18.refs_3_), channel_id=1, source_target_pairs={{0,8},{4,12},{8,0},{12,4},{1,9},{5,13},{9,1},{13,5},{2,10},{6,14},... | collective-permute-start | bytes 1376264 | tf_op jit(solution)/shard_map/ppermute | solution.py:22
  51.4 2.3 %copy-start.8 = (f32[2,1792,256]{2,1,0:T(8,128)S(1)}, f32[2,1792,256]{2,1,0:T(8,128)}, u32[]{:S(2)}) copy-start(f32[2,1792,256]{2,1,0:T(8,128)} %copy-done.7) | copy-start | bytes 11010052
  54.2 5.2 %copy-start.2 = (bf16[2,1,1792,2048]{3,2,1,0:T(8,128)(2,1)S(1)}, bf16[2,1,1792,2048]{3,2,1,0:T(8,128)(2,1)}, u32[]{:S(2)}) copy-start(bf16[2,1,1792,2048]{3,2,1,0:T(8,128)(2,1)} %copy-done) | copy-start | bytes 44040196
  65.4 19.9 %collective-permute-start.12 = (bf16[128,2048]{1,0:T(8,128)(2,1)S(1)}, bf16[128,2048]{1,0:T(8,128)(2,1)}, u32[]{:S(2)}, u32[]{:S(2)}) collective-permute-start(bf16[128,2048]{1,0:T(8,128)(2,1)S(1)} %shard_map.50.refs_0_), channel_id=1, source_target_pairs={{0,1},{1,0},{2,3},{3,2},{4,5},{5,4},{6,7},{7,6},{8,9},{9,8},{10,11... | collective-permute-start | bytes 1572872 | tf_op jit(solution)/shard_map/ppermute | solution.py:22
  65.5 30.7 %collective-permute-start.14 = (bf16[128,2048]{1,0:T(8,128)(2,1)S(1)}, bf16[128,2048]{1,0:T(8,128)(2,1)S(1)}, u32[]{:S(2)}, u32[]{:S(2)}) collective-permute-start(bf16[128,2048]{1,0:T(8,128)(2,1)S(1)} %shard_map.50.refs_0_), channel_id=1, source_target_pairs={{4,0},{8,12},{5,1},{9,13},{6,2},{10,14},{7,3},{11,15},{20,16},{24,... | collective-permute-start | bytes 1572872 | tf_op jit(solution)/shard_map/ppermute | solution.py:259
  66.8 5.2 %copy-start.3 = (bf16[2,1,1792,2048]{3,2,1,0:T(8,128)(2,1)S(1)}, bf16[2,1,1792,2048]{3,2,1,0:T(8,128)(2,1)}, u32[]{:S(2)}) copy-start(bf16[2,1,1792,2048]{3,2,1,0:T(8,128)(2,1)} %copy-done) | copy-start | bytes 44040196
  76.7 2.0 %copy-start.5 = (f32[2,256,2048]{2,1,0:T(8,128)}, f32[2,256,2048]{2,1,0:T(8,128)S(1)}, u32[]{:S(2)}) copy-start(f32[2,256,2048]{2,1,0:T(8,128)S(1)} %get-tuple-element.28.refs_2_) | copy-start | bytes 12582916
  80.4 15.9 %collective-permute-start.9 = (bf16[1792,128]{1,0:T(8,128)(2,1)}, bf16[1792,128]{1,0:T(8,128)(2,1)S(1)}, u32[]{:S(2)}, u32[]{:S(2)}) collective-permute-start(bf16[1792,128]{1,0:T(8,128)(2,1)} %shard_map.49.refs_0_), channel_id=1, source_target_pairs={{0,2},{2,0},{1,3},{3,1},{4,6},{6,4},{5,7},{7,5},{8,10},{10,8},{9,1... | collective-permute-start | bytes 1376264 | tf_op jit(solution)/shard_map/ppermute | solution.py:22
  81.0 21.6 %collective-permute-start.7 = (f32[2,256]{1,0:T(2,128)S(1)}, f32[2,256]{1,0:T(2,128)S(1)}, u32[]{:S(2)}, u32[]{:S(2)}) collective-permute-start(f32[2,256]{1,0:T(2,128)S(1)} %shard_map.48.refs_1_.refs_3_), channel_id=1, source_target_pairs={{0,4},{4,0},{8,12},{12,8},{1,5},{5,1},{9,13},{13,9},{2,6},{6,2},{1... | collective-permute-start | bytes 6152 | tf_op jit(solution)/shard_map/ppermute | solution.py:22
  85.3 5.2 %copy-start.4 = (bf16[2,1,1792,2048]{3,2,1,0:T(8,128)(2,1)S(1)}, bf16[2,1,1792,2048]{3,2,1,0:T(8,128)(2,1)}, u32[]{:S(2)}) copy-start(bf16[2,1,1792,2048]{3,2,1,0:T(8,128)(2,1)} %copy-done) | copy-start | bytes 44040196
  96.2 4.6 %collective-permute-start.15 = (bf16[128,2048]{1,0:T(8,128)(2,1)S(1)}, bf16[128,2048]{1,0:T(8,128)(2,1)S(1)}, u32[]{:S(2)}, u32[]{:S(2)}) collective-permute-start(bf16[128,2048]{1,0:T(8,128)(2,1)S(1)} %shard_map.54.refs_0_), channel_id=1, source_target_pairs={{0,1},{1,0},{2,3},{3,2},{4,5},{5,4},{6,7},{7,6},{8,9},{9,8},{10,11... | collective-permute-start | bytes 1572872 | tf_op jit(solution)/shard_map/ppermute | solution.py:22
  96.3 4.5 %copy-start.6 = (f32[2,256,2048]{2,1,0:T(8,128)S(1)}, f32[2,256,2048]{2,1,0:T(8,128)}, u32[]{:S(2)}) copy-start(f32[2,256,2048]{2,1,0:T(8,128)} %copy-done.5) | copy-start | bytes 12582916
  98.2 4.5 %collective-permute-start.13 = (f32[2,256]{1,0:T(2,128)S(1)}, f32[2,256]{1,0:T(2,128)S(1)}, u32[]{:S(2)}, u32[]{:S(2)}) collective-permute-start(f32[2,256]{1,0:T(2,128)S(1)} %shard_map.53), channel_id=1, source_target_pairs={{0,8},{4,12},{8,0},{12,4},{1,9},{5,13},{9,1},{13,5},{2,10},{6,14},... | collective-permute-start | bytes 6152 | tf_op jit(solution)/shard_map/ppermute | solution.py:22
  101.3 5.4 %collective-permute-start.16 = (f32[2,256]{1,0:T(2,128)S(1)}, f32[2,256]{1,0:T(2,128)S(1)}, u32[]{:S(2)}, u32[]{:S(2)}) collective-permute-start(f32[2,256]{1,0:T(2,128)S(1)} %shard_map.55), channel_id=1, source_target_pairs={{0,12},{4,8},{8,4},{12,0},{1,13},{5,9},{9,5},{13,1},{2,14},{6,10},... | collective-permute-start | bytes 6152 | tf_op jit(solution)/shard_map/ppermute | solution.py:22
  106.7 1.2 %collective-permute-start.17 = (f32[2,256]{1,0:T(2,128)S(1)}, f32[2,256]{1,0:T(2,128)S(1)}, u32[]{:S(2)}, u32[]{:S(2)}) collective-permute-start(f32[2,256]{1,0:T(2,128)S(1)} %add_add_fusion), channel_id=1, source_target_pairs={{0,1},{1,0},{2,3},{3,2},{4,5},{5,4},{6,7},{7,6},{8,9},{9,8},{10,11... | collective-permute-start | bytes 6152 | tf_op jit(solution)/shard_map/ppermute | solution.py:22
  107.9 3.6 %collective-permute-start.18 = (f32[2,256]{1,0:T(2,128)S(1)}, f32[2,256]{1,0:T(2,128)S(1)}, u32[]{:S(2)}, u32[]{:S(2)}) collective-permute-start(f32[2,256]{1,0:T(2,128)S(1)} %add.44), channel_id=1, source_target_pairs={{0,2},{2,0},{1,3},{3,1},{4,6},{6,4},{5,7},{7,5},{8,10},{10,8},{9,1... | collective-permute-start | bytes 6152 | tf_op jit(solution)/shard_map/ppermute | solution.py:22

commit v12 on v11

v12 whole, which is shorter than its diff:
```python
import functools
import math

import jax
import jax.numpy as jnp
from jax import lax
from jax.experimental import pallas as pl
from jax.experimental.pallas import tpu as pltpu
from jax.sharding import PartitionSpec as P


LONG, SHORT = 14_000_000_000, 1_000_000


def trade(block, steps, backwards=False):
    axes = tuple(steps)
    sizes = [lax.axis_size(axis) for axis in axes]
    mask = 0
    for axis, size in zip(axes, sizes):
        mask = mask * size + steps[axis]
    route = [(i, i ^ mask) for i in range(math.prod(sizes))]
    return lax.ppermute(block, axes, route[::-1] if backwards else route)


def pass_on(block, step, count):
    up = lax.ppermute(block[0], "dp", [(i, i + 1) for i in range(step - 1, count - 1)])
    down = lax.ppermute(block[1], "dp", [(i, i - 1) for i in range(1, count - step + 1)])
    return up, down


ANYWHERE = pl.BlockSpec(memory_space=pl.ANY)
NEAR = pl.BlockSpec(memory_space=pltpu.VMEM)


def call(kernel, arrays, outs, flops=1024, tokens=(), scratch=()):
    skip = len(tokens)

    def body(*refs):
        kernel(*refs[: len(arrays)], *refs[len(arrays) + skip :])

    return pl.pallas_call(
        body,
        in_specs=[NEAR] * len(arrays) + [ANYWHERE] * skip,
        out_specs=[NEAR] * len(outs),
        out_shape=[pltpu.VMEM(shape, dtype) for shape, dtype in outs],
        scratch_shapes=list(scratch),
        compiler_params=pltpu.CompilerParams(vmem_limit_bytes=12 * 1024 * 1024),
        cost_estimate=pl.CostEstimate(flops=flops, bytes_accessed=1024, transcendentals=0),
    )(*[pltpu.with_memory_space_constraint(array, pltpu.VMEM) for array in arrays], *tokens)


def fetch(kernel, arrays, outs, scratch, copies):
    return pl.pallas_call(
        kernel,
        in_specs=[ANYWHERE] * len(arrays),
        out_specs=[NEAR] * len(outs),
        out_shape=[pltpu.VMEM(shape, dtype) for shape, dtype in outs],
        scratch_shapes=[*scratch, pltpu.SemaphoreType.DMA((copies,))],
        compiler_params=pltpu.CompilerParams(vmem_limit_bytes=12 * 1024 * 1024),
        cost_estimate=pl.CostEstimate(flops=1024, bytes_accessed=1024, transcendentals=0),
    )(*[pltpu.with_memory_space_constraint(array, pltpu.HBM) for array in arrays])


def grads_block(grads_ref, device, part, rows):
    first = pl.multiple_of(lax.axis_index("din") * part, part)
    return grads_ref.at[pl.ds(first, part), pl.ds(pl.multiple_of(device * rows, rows), rows)]


def first_kernel(far, acts_ref, grads_ref, mine_ref, far_ref, arrived):
    half = mine_ref.shape[0]
    rows = pl.ds(pl.multiple_of(lax.axis_index("dout") * half, half), half)
    block = grads_block(grads_ref, lax.axis_index("dp") ^ far, *far_ref.shape)
    copies = [
        pltpu.make_async_copy(acts_ref.at[rows, :], mine_ref, arrived.at[0]),
        pltpu.make_async_copy(block, far_ref, arrived.at[1]),
    ]
    for copy in copies:
        copy.start()
    for copy in copies:
        copy.wait()


def rest_kernel(steps, acts_ref, grads_ref, query_ref, near_query, near_acts, own_out, *refs):
    outs, own, blocks, arrived = refs[: len(steps)], refs[-3], refs[-2], refs[-1]
    me = lax.axis_index("dp")
    tokens, rows = own.shape
    copies = [pltpu.make_async_copy(grads_ref.at[:, pl.ds(pl.multiple_of(me * rows, rows), rows)], own, arrived.at[0])]
    for k, d in enumerate(steps):
        block = grads_block(grads_ref, me ^ d, *blocks.shape[1:])
        copies.append(pltpu.make_async_copy(block, blocks.at[k], arrived.at[1 + k]))
    copies.append(pltpu.make_async_copy(acts_ref, near_acts, arrived.at[len(steps) + 1]))
    copies.append(pltpu.make_async_copy(query_ref, near_query, arrived.at[len(steps) + 2]))
    for copy in copies:
        copy.start()
    for k, out in enumerate(outs):
        copies[1 + k].wait()
        out[...] = blocks[k].astype(jnp.float32).T.astype(out.dtype)
    copies[0].wait()
    own_out[...] = own[...].astype(jnp.float32).T.astype(own_out.dtype)
    for copy in copies[-2:]:
        copy.wait()


def hold(blocks, tokens):
    count = len(blocks)
    return pl.pallas_call(
        lambda *refs: None,
        in_specs=[ANYWHERE] * (count + len(tokens)),
        out_specs=[ANYWHERE] * count,
        out_shape=[jax.ShapeDtypeStruct(block.shape, block.dtype) for block in blocks],
        input_output_aliases={i: i for i in range(count)},
        compiler_params=pltpu.CompilerParams(vmem_limit_bytes=1024 * 1024),
        cost_estimate=pl.CostEstimate(flops=1024, bytes_accessed=1024, transcendentals=0),
    )(*blocks, *tokens)


def pick_kernel(choice, *refs):
    *blocks, out_ref = refs
    me = lax.axis_index("dp")
    where = functools.reduce(lambda found, z: jnp.where(me == z, choice[z], found), range(len(choice)), 0)
    for k, block in enumerate(blocks):

        @pl.when(where == k)
        def _():
            out_ref[...] = block[...]


def from_partner(hops, d, count, tokens=()):
    sources, choice = [], []
    for z in range(count):
        away = z - (z ^ d)
        source = (abs(away), int(away < 0 and abs(away) < count - 1))
        if source not in sources:
            sources.append(source)
        choice.append(sources.index(source))
    blocks = [hops[step][way] for step, way in sources]
    outs = [(blocks[0].shape, blocks[0].dtype)]
    return call(functools.partial(pick_kernel, choice), blocks, outs, tokens=tokens)[0]


def joined(parts, axis):
    if len(parts) == 1:
        return parts[0][...]
    column, found = lax.axis_index("din"), []
    for p in range(len(parts)):
        chosen = parts[0][...]
        for r in range(1, len(parts)):
            chosen = jnp.where(column == p ^ r, parts[r][...], chosen)
        found.append(chosen)
    return jnp.concatenate(found, axis=axis)


MARK = (8, 128), jnp.float32


def mix_kernel(*refs):
    *parts, query_ref, out_ref, mark_ref, acts = refs
    mark_ref[...] = jnp.zeros_like(mark_ref)
    half = parts[0].shape[0]
    first = lax.axis_index("dout") * half if len(parts) > 1 else 0
    for part, at in zip(parts, (first, half - first)):
        acts[pl.ds(pl.multiple_of(at, half), half), :] = part[...]
    nq, _, depth, _ = query_ref.shape
    tile = depth // 2

    def step(at, _):
        q, rows = at // 2, pl.ds(pl.multiple_of(at % 2 * tile, tile), tile)
        out_ref[q, rows, :] = lax.dot_general(
            query_ref[q, 0, rows, :], acts[...], (((1,), (1,)), ((), ())), preferred_element_type=jnp.float32
        )
        return 0

    lax.fori_loop(0, 2 * nq, step, 0)


def mixed(parts, queries, flops, tokens=()):
    nq, _, depth, width = queries.shape
    tokens_here = sum(part.shape[0] for part in parts)
    outs = [((nq, depth, tokens_here), jnp.float32), MARK]
    scratch = [pltpu.VMEM((tokens_here, width), queries.dtype)]
    return call(mix_kernel, [*parts, queries], outs, flops, tokens, scratch)


def score_kernel(*refs):
    *parts, mix_ref, out_ref = refs
    grads = joined(parts, 1).astype(jnp.float32)
    for q in range(mix_ref.shape[0]):
        out_ref[q : q + 1, :] = jnp.sum(grads * mix_ref[q], axis=0, keepdims=True)


def scores_of_grads(parts, mix, tokens=(), flops=1024):
    nq, _, count = mix.shape
    return call(score_kernel, [*parts, mix], [((nq, count), jnp.float32)], flops, tokens)[0]


def project_kernel(*refs):
    *parts, query_ref, out_ref, mark_ref, grads = refs
    mark_ref[...] = jnp.zeros_like(mark_ref)
    grads[...] = joined(parts, 0)
    nq, _, _, width = query_ref.shape
    tile = width // 2

    def step(at, _):
        q, columns = at // 2, pl.ds(pl.multiple_of(at % 2 * tile, tile), tile)
        out_ref[q, :, columns] = jnp.dot(
            grads[...], query_ref[q, 0, :, columns], preferred_element_type=jnp.float32
        )
        return 0

    lax.fori_loop(0, 2 * nq, step, 0)


def projected(parts, queries, flops, tokens=()):
    nq, _, depth, width = queries.shape
    count = sum(part.shape[0] for part in parts)
    outs = [((nq, count, width), jnp.float32), MARK]
    scratch = [pltpu.VMEM((count, depth), queries.dtype)]
    return call(project_kernel, [*parts, queries], outs, flops, tokens, scratch)


def finish_kernel(mine_ref, other_ref, proj_ref, out_ref):
    half, width = mine_ref.shape
    swapped = lax.axis_index("dout") == 1
    for h, (first, second) in enumerate(((mine_ref, other_ref), (other_ref, mine_ref))):
        acts = jnp.where(swapped, second[...], first[...]).astype(jnp.float32)
        for q in range(proj_ref.shape[0]):
            terms = acts * proj_ref[q, h * half : (h + 1) * half, :]
            lanes = terms[:, :128]
            for at in range(128, width, 128):
                lanes = lanes + terms[:, at : at + 128]
            out_ref[q : q + 1, h * half : (h + 1) * half] = jnp.sum(lanes.T, axis=0, keepdims=True)


def scores_of_acts(mine, other, proj, tokens=()):
    nq, count, _ = proj.shape
    return call(finish_kernel, [mine, other, proj], [((nq, count), jnp.float32)], tokens=tokens)[0]


def cut(activations, out_grads, queries, far, others):
    count, part = lax.axis_size("dp"), out_grads.shape[0] // lax.axis_size("din")
    rows, (tokens, width), dtype = queries.shape[2], activations.shape, out_grads.dtype
    half = tokens // 2
    if part % 128 or rows % 128:
        me, column = lax.axis_index("dp"), lax.axis_index("din")
        mine = lax.dynamic_slice_in_dim(activations, lax.axis_index("dout") * half, half, 0)
        share = lax.dynamic_slice_in_dim(out_grads, column * part, part, 0)
        away = [lax.dynamic_slice_in_dim(share, (me ^ d) * rows, rows, 1) for d in [far, *others]]
        own = lax.dynamic_slice_in_dim(out_grads, me * rows, rows, 1).T
        return (mine, away[0]), (queries, activations, own, *[block.T for block in away[1:]])
    outs = [((half, width), activations.dtype), ((part, rows), dtype)]
    first = fetch(functools.partial(first_kernel, far), [activations, out_grads], outs, [], 2)
    outs = [(queries.shape, queries.dtype), (activations.shape, activations.dtype), ((rows, tokens), dtype)]
    outs += [((rows, part), dtype)] * len(others)
    scratch = [pltpu.VMEM((tokens, rows), dtype), pltpu.VMEM((len(others), part, rows), dtype)]
    arrays = [activations, out_grads, queries]
    return first, fetch(functools.partial(rest_kernel, others), arrays, outs, scratch, len(others) + 3)


def on_device(activations, out_grads, queries):
    count, spread = lax.axis_size("dp"), lax.axis_size("din")

    def to_columns(arrived):
        return [arrived] + [trade(arrived, {"din": r}) for r in range(1, spread)]

    def acts_of(block):
        return [block, trade(block, {"dout": 1})]

    far, late = count - 1, count - 2
    early = list(range(1, late))
    (mine, far_grads), (queries, own_acts, own, *sent) = cut(activations, out_grads, queries, far, early + [late])
    hops = [(mine, mine)]
    hops.append(pass_on(hops[0], 1, count))
    arrived = {d: trade(block, {"dp": d}) for d, block in zip([far, *early, late], [far_grads, *sent])}

    mix, token = mixed([own_acts], queries, SHORT)
    scores = scores_of_grads([own], mix)
    hops[1] = hold(list(hops[1]), [token])
    for step in range(2, count - 1):
        hops.append(pass_on(hops[-1], step, count))

    mixes, token = {}, scores
    for d in early:
        mixes[d], token = mixed(acts_of(from_partner(hops, d, count)), queries, SHORT, [token])
    sides = to_columns(hold([arrived[far]], hops[1])[0])
    block = from_partner(hops, late, count, [token] + sides)
    end = lax.ppermute(block, "dp", [(1, 0), (count - 2, count - 1)])
    hops.append((end, end))

    proj, token = projected(sides, queries, SHORT, [token])
    terms = []
    for d in early:
        sides = to_columns(hold([arrived[d]], hops[1])[0])
        token = scores_of_grads(sides, mixes[d], [token])
        terms.append(trade(token, {"dp": d}))

    sides = to_columns(hold([arrived[late]], [token])[0])
    mix, token = mixed(acts_of(block), queries, SHORT, [token])
    sides = sides[:1] + list(hold(sides[1:], [token]))
    terms.append(trade(scores_of_grads(sides, mix, (), LONG), {"dp": late}))
    block = from_partner(hops, far, count, [token])
    terms.append(trade(scores_of_acts(*acts_of(block), proj), {"dp": far}))
    return over_chips(sum(terms, scores), spread)


def over_chips(scores, spread):
    scores = scores + trade(scores, {"dout": 1})
    return scores + sum(trade(scores, {"din": r}) for r in range(1, spread))


def solution(mesh):
    placed = (P(("groups", "dp"), "din"), P(("groups", "dp"), "dout"), P(None, "dout", "dp", "din"))
    return jax.shard_map(
        on_device, mesh=mesh, in_specs=placed, out_specs=P(None, ("groups", "dp")), check_vma=False
    )
```

time: 113 us -> 97.7 us (0.86)
  local copies, waits for them, and re-layouts: 33.9 us -> 0 us
  waiting for transfers between devices: 16.3 us -> 34 us
  starting transfers between devices: 28.6 us -> 34.1 us
  Pallas kernels: 32.3 us -> 28.6 us
    unnamed x20 -> x0, local copies, waits for them, and re-layouts: 28.4 us -> none
    ppermute x14, waiting for transfers between devices: 16.3 us -> 24.7 us  [trade(): return lax.ppermute(block, axes, route[::-1] if backwards else route)]
    ppermute x14, starting transfers between devices: 18.3 us -> 24.6 us  [trade(): return lax.ppermute(block, axes, route[::-1] if backwards else route)]
    dynamic_slice x3 -> x0, local copies, waits for them, and re-layouts: 5.45 us -> none  [the longest x2 3.57 us: grads_for(): return lax.dynamic_slice(out_grads, (first, device * rows), (size, rows))]
    ppermute x1, waiting for transfers between devices: 0.01 us -> 4.97 us  [on_device(): end = lax.ppermute(block, 'dp', [(1, 0), (count - 2, count - 1)])]
    ppermute x2, waiting for transfers between devices: 0.01 us -> 4.37 us  [pass_on(): lax.ppermute(block[1], 'dp', [(i, i - 1) for i in range(1, count - step +...]
    pallas_call x14 -> x13, Pallas kernels: 32.3 us -> 28.6 us  [the longest x11 21.3 us: call(): pl.pallas_call(body, in_specs=[NEAR] * len(arrays) + [ANYWHERE] * skip, o...]
  transfers between devices with their start and end apart: 19 -> 19, of which waited for: 5 -> 9; matrix products, arithmetic and copies ran while one was open for 3% -> 0% of each run, Pallas kernels for 29% -> 28%
where the time goes in v12:
time: 97.7 us; the launch traced here: 97.5 us
  starting transfers between devices  34.1 us (35%)
  waiting for transfers between devices  34 us (35%)
  Pallas kernels  28.6 us (29%)
    ppermute x14, waiting for transfers between devices, trade(): return lax.ppermute(block, axes, route[::-1] if backwards else route)  24.7 us
    ppermute x14, starting transfers between devices, trade(): return lax.ppermute(block, axes, route[::-1] if backwards else route)  24.6 us
    pallas_call x11, Pallas kernels, call(): pl.pallas_call(body, in_specs=[NEAR] * len(arrays) + [ANYWHERE] * skip, o...  21.3 us
    pallas_call x2, Pallas kernels, fetch(): pl.pallas_call(kernel, in_specs=[ANYWHERE] * len(arrays), out_specs=[NEAR...  7.3 us
    ppermute x2, starting transfers between devices, pass_on(): lax.ppermute(block[0], 'dp', [(i, i + 1) for i in range(step - 1, count -...  5.65 us
    ppermute x1, waiting for transfers between devices, on_device(): end = lax.ppermute(block, 'dp', [(1, 0), (count - 2, count - 1)])  4.97 us
    ppermute x2, waiting for transfers between devices, pass_on(): lax.ppermute(block[1], 'dp', [(i, i - 1) for i in range(1, count - step +...  4.37 us
    ppermute x2, starting transfers between devices, pass_on(): lax.ppermute(block[1], 'dp', [(i, i - 1) for i in range(1, count - step +...  2.57 us
  transfers between devices with their start and end apart: 19, of which 9 were waited for; matrix products, arithmetic and copies ran while one was open for 0% of the time, Pallas kernels for 28%

profile of v12, /device:TPU:0, one launch (start us, length us, event | category | flops | bytes accessed | tf_op | source)
XLA Modules:
  0.0 97.5 jit_solution(3081968330845147405)
XLA Ops:
  0.0 1.2 %shard_map.40 = (bf16[128,2048]{1,0:T(8,128)(2,1)S(1)}, bf16[128,1792]{1,0:T(8,128)(2,1)S(1)}) custom-call(bf16[256,2048]{1,0:T(8,128)(2,1)} %acts_ref.3, bf16[256,7168]{1,0:T(8,128)(2,1)} %grads_ref.3), custom_call_target="tpu_custom_call" | custom-call | flops 1024 | bytes 1024 | tf_op jit(solution)/shard_map/pallas_call | solution.py:53
  1.2 5.0 %collective-permute-start.1 = (bf16[128,2048]{1,0:T(8,128)(2,1)S(1)}, bf16[128,2048]{1,0:T(8,128)(2,1)S(1)}, u32[]{:S(2)}, u32[]{:S(2)}) collective-permute-start(bf16[128,2048]{1,0:T(8,128)(2,1)S(1)} %get-tuple-element.27), channel_id=1, source_target_pairs={{0,4},{4,8},{8,12},{1,5},{5,9},{9,13},{2,6},{6,10},{10,14},{3,7},{... | collective-permute-start | bytes 1572872 | tf_op jit(solution)/shard_map/ppermute | solution.py:26
  6.2 1.3 %collective-permute-start.2 = (bf16[128,2048]{1,0:T(8,128)(2,1)S(1)}, bf16[128,2048]{1,0:T(8,128)(2,1)S(1)}, u32[]{:S(2)}, u32[]{:S(2)}) collective-permute-start(bf16[128,2048]{1,0:T(8,128)(2,1)S(1)} %get-tuple-element.27), channel_id=1, source_target_pairs={{4,0},{8,4},{12,8},{5,1},{9,5},{13,9},{6,2},{10,6},{14,10},{7,3},{... | collective-permute-start | bytes 1572872 | tf_op jit(solution)/shard_map/ppermute | solution.py:27
  7.5 4.7 %collective-permute-start.5 = (bf16[128,1792]{1,0:T(8,128)(2,1)S(1)}, bf16[128,1792]{1,0:T(8,128)(2,1)S(1)}, u32[]{:S(2)}, u32[]{:S(2)}) collective-permute-start(bf16[128,1792]{1,0:T(8,128)(2,1)S(1)} %get-tuple-element.32), channel_id=1, source_target_pairs={{0,12},{4,8},{8,4},{12,0},{1,13},{5,9},{9,5},{13,1},{2,14},{6,10},... | collective-permute-start | bytes 1376264 | tf_op jit(solution)/shard_map/ppermute | solution.py:22
  12.2 6.1 %shard_map.37 = (bf16[2,1,1792,2048]{3,2,1,0:T(8,128)(2,1)S(1)}, bf16[256,2048]{1,0:T(8,128)(2,1)S(1)}, bf16[1792,256]{1,0:T(8,128)(2,1)S(1)}, bf16[1792,128]{1,0:T(8,128)(2,1)S(1)}, bf16[1792,128]{1,0:T(8,128)(2,1)S(1)}) custom-call(bf16[256,2048]{1,0:T(8,128)(2,1)} %acts_ref.3, bf16[256,7168]{1,0:T(8,128)(2,1)} %grads_ref.3, ...), custom_call_target="tpu_custom_call" | custom-call | flops 1024 | bytes 1024 | tf_op jit(solution)/shard_map/pallas_call | solution.py:53
  18.3 4.7 %shard_map.38 = (f32[2,1792,256]{2,1,0:T(8,128)S(1)}, f32[8,128]{1,0:T(8,128)S(1)}) custom-call(bf16[256,2048]{1,0:T(8,128)(2,1)S(1)} %get-tuple-element.23.refs_0_, bf16[2,1,1792,2048]{3,2,1,0:T(8,128)(2,1)S(1)} %get-tuple-element.24.refs_1_.refs_2_), custom_call_target="tpu_custom_call" | custom-call | flops 1000000 | bytes 1024 | tf_op jit(solution)/shard_map/pallas_call | solution.py:41
  23.2 11.3 %collective-permute-start = (bf16[1792,128]{1,0:T(8,128)(2,1)S(1)}, bf16[1792,128]{1,0:T(8,128)(2,1)S(1)}, u32[]{:S(2)}, u32[]{:S(2)}) collective-permute-start(bf16[1792,128]{1,0:T(8,128)(2,1)S(1)} %get-tuple-element.26), channel_id=1, source_target_pairs={{0,4},{4,0},{8,12},{12,8},{1,5},{5,1},{9,13},{13,9},{2,6},{6,2},{1... | collective-permute-start | bytes 1376264 | tf_op jit(solution)/shard_map/ppermute | solution.py:22
  34.5 1.3 %collective-permute-start.10 = (bf16[128,2048]{1,0:T(8,128)(2,1)S(1)}, bf16[128,2048]{1,0:T(8,128)(2,1)S(1)}, u32[]{:S(2)}, u32[]{:S(2)}) collective-permute-start(bf16[128,2048]{1,0:T(8,128)(2,1)S(1)} %get-tuple-element.30.refs_2_.refs_0_.refs_1_), channel_id=1, source_target_pairs={{4,0},{8,4},{5,1},{9,5},{6,2},{10,6},{7,3},{11,7},{20,16},{24,20},... | collective-permute-start | bytes 1572872 | tf_op jit(solution)/shard_map/ppermute | solution.py:27
  35.8 0.7 collective-permute-start.11
  36.5 1.6 %collective-permute-start.6 = (bf16[128,1792]{1,0:T(8,128)(2,1)S(1)}, bf16[128,1792]{1,0:T(8,128)(2,1)S(1)}, u32[]{:S(2)}, u32[]{:S(2)}) collective-permute-start(bf16[128,1792]{1,0:T(8,128)(2,1)S(1)} %shard_map.45.refs_0_.refs_3_), channel_id=1, source_target_pairs={{0,2},{2,0},{1,3},{3,1},{4,6},{6,4},{5,7},{7,5},{8,10},{10,8},{9,1... | collective-permute-start | bytes 1376264 | tf_op jit(solution)/shard_map/ppermute | solution.py:22
  38.0 7.8 %collective-permute-done.refs_0_ = bf16[1792,128]{1,0:T(8,128)(2,1)S(1)} collective-permute-done((bf16[1792,128]{1,0:T(8,128)(2,1)S(1)}, bf16[1792,128]{1,0:T(8,128)(2,1)S(1)}, u32[]{:S(2)}, u32[]{:S(2)}) %collective-permute-start) | collective-permute-done | bytes 458784 | tf_op jit(solution)/shard_map/ppermute | solution.py:22
  45.8 1.5 %collective-permute-start.3 = (bf16[1792,128]{1,0:T(8,128)(2,1)S(1)}, bf16[1792,128]{1,0:T(8,128)(2,1)S(1)}, u32[]{:S(2)}, u32[]{:S(2)}) collective-permute-start(bf16[1792,128]{1,0:T(8,128)(2,1)S(1)} %shard_map.42.refs_0_), channel_id=1, source_target_pairs={{0,2},{2,0},{1,3},{3,1},{4,6},{6,4},{5,7},{7,5},{8,10},{10,8},{9,1... | collective-permute-start | bytes 1376264 | tf_op jit(solution)/shard_map/ppermute | solution.py:22
  47.3 0.4 shard_map.39.refs_3_
  47.8 4.7 %shard_map.44 = (f32[2,1792,256]{2,1,0:T(8,128)S(1)}, f32[8,128]{1,0:T(8,128)S(1)}) custom-call(bf16[128,2048]{1,0:T(8,128)(2,1)S(1)} %shard_map.43.refs_0_, bf16[128,2048]{1,0:T(8,128)(2,1)S(1)} %collective-permute-done.4.refs_1_, bf16[2,1,1792,2048]{3,2,1,0:T(8,128)(2,1)S(1)} %get-tuple-element.24.refs_1_.refs_2_, f32[2,256]{1,0:T(2,128)S(1)} %shard_map.39.refs_3_), custom_call_target="tpu_custom_call" | custom-call | flops 1000000 | bytes 1024 | tf_op jit(solution)/shard_map/pallas_call | solution.py:41
  52.5 4.4 %collective-permute-done.10.refs_0_ = bf16[128,2048]{1,0:T(8,128)(2,1)S(1)} collective-permute-done((bf16[128,2048]{1,0:T(8,128)(2,1)S(1)}, bf16[128,2048]{1,0:T(8,128)(2,1)S(1)}, u32[]{:S(2)}, u32[]{:S(2)}) %collective-permute-start.10) | collective-permute-done | bytes 524320 | tf_op jit(solution)/shard_map/ppermute | solution.py:27
  57.0 1.3 %collective-permute-start.14 = (bf16[128,2048]{1,0:T(8,128)(2,1)S(1)}, bf16[128,2048]{1,0:T(8,128)(2,1)S(1)}, u32[]{:S(2)}, u32[]{:S(2)}) collective-permute-start(bf16[128,2048]{1,0:T(8,128)(2,1)S(1)} %shard_map.49.refs_0_), channel_id=1, source_target_pairs={{4,0},{8,12},{5,1},{9,13},{6,2},{10,14},{7,3},{11,15},{20,16},{24,... | collective-permute-start | bytes 1572872 | tf_op jit(solution)/shard_map/ppermute | solution.py:286
  58.3 4.7 %shard_map.46 = (f32[2,256,2048]{2,1,0:T(8,128)S(1)}, f32[8,128]{1,0:T(8,128)S(1)}) custom-call(bf16[128,1792]{1,0:T(8,128)(2,1)S(1)} %shard_map.45.refs_0_.refs_3_, bf16[128,1792]{1,0:T(8,128)(2,1)S(1)} %collective-permute-done.6.refs_1_.refs_4_, bf16[2,1,1792,2048]{3,2,1,0:T(8,128)(2,1)S(1)} %get-tuple-element.24.refs_1_.refs_2_, ...), custom_call_target="tpu_custom_call" | custom-call | flops 1000000 | bytes 1024 | tf_op jit(solution)/shard_map/pallas_call | solution.py:41
  63.0 0.8 shard_map.47.refs_1_.refs_3_
  63.8 9.3 %collective-permute-done.8.refs_0_ = bf16[1792,128]{1,0:T(8,128)(2,1)S(1)} collective-permute-done((bf16[1792,128]{1,0:T(8,128)(2,1)S(1)}, bf16[1792,128]{1,0:T(8,128)(2,1)S(1)}, u32[]{:S(2)}, u32[]{:S(2)}) %collective-permute-start.8) | collective-permute-done | bytes 458784 | tf_op jit(solution)/shard_map/ppermute | solution.py:22
  73.1 1.5 %collective-permute-start.9 = (bf16[1792,128]{1,0:T(8,128)(2,1)S(1)}, bf16[1792,128]{1,0:T(8,128)(2,1)S(1)}, u32[]{:S(2)}, u32[]{:S(2)}) collective-permute-start(bf16[1792,128]{1,0:T(8,128)(2,1)S(1)} %shard_map.48.refs_0_), channel_id=1, source_target_pairs={{0,2},{2,0},{1,3},{3,1},{4,6},{6,4},{5,7},{7,5},{8,10},{10,8},{9,1... | collective-permute-start | bytes 1376264 | tf_op jit(solution)/shard_map/ppermute | solution.py:22
  74.6 4.7 %shard_map.50 = (f32[2,1792,256]{2,1,0:T(8,128)S(1)}, f32[8,128]{1,0:T(8,128)S(1)}) custom-call(bf16[128,2048]{1,0:T(8,128)(2,1)S(1)} %shard_map.49.refs_0_, bf16[128,2048]{1,0:T(8,128)(2,1)S(1)} %collective-permute-done.12.refs_1_, bf16[2,1,1792,2048]{3,2,1,0:T(8,128)(2,1)S(1)} %get-tuple-element.24.refs_1_.refs_2_, f32[2,256]{1,0:T(2,128)S(1)} %shard_map.47.refs_1_.refs_3_), custom_call_target="tpu_custom_call" | custom-call | flops 1000000 | bytes 1024 | tf_op jit(solution)/shard_map/pallas_call | solution.py:41
  79.3 5.0 %collective-permute-done.14.refs_0_ = bf16[128,2048]{1,0:T(8,128)(2,1)S(1)} collective-permute-done((bf16[128,2048]{1,0:T(8,128)(2,1)S(1)}, bf16[128,2048]{1,0:T(8,128)(2,1)S(1)}, u32[]{:S(2)}, u32[]{:S(2)}) %collective-permute-start.14) | collective-permute-done | bytes 524320 | tf_op jit(solution)/shard_map/ppermute | solution.py:286
  84.4 0.8 shard_map.52
  85.3 1.0 %collective-permute-done.15.refs_1_ = bf16[128,2048]{1,0:T(8,128)(2,1)S(1)} collective-permute-done((bf16[128,2048]{1,0:T(8,128)(2,1)S(1)}, bf16[128,2048]{1,0:T(8,128)(2,1)S(1)}, u32[]{:S(2)}, u32[]{:S(2)}) %collective-permute-start.15) | collective-permute-done | bytes 524320 | tf_op jit(solution)/shard_map/ppermute | solution.py:22
  86.3 0.5 shard_map.54
  86.7 2.1 %collective-permute-start.16 = (f32[2,256]{1,0:T(2,128)S(1)}, f32[2,256]{1,0:T(2,128)S(1)}, u32[]{:S(2)}, u32[]{:S(2)}) collective-permute-start(f32[2,256]{1,0:T(2,128)S(1)} %shard_map.54), channel_id=1, source_target_pairs={{0,12},{4,8},{8,4},{12,0},{1,13},{5,9},{9,5},{13,1},{2,14},{6,10},... | collective-permute-start | bytes 6152 | tf_op jit(solution)/shard_map/ppermute | solution.py:22
  88.9 0.9 collective-permute-done.13
  89.7 2.4 %collective-permute-done.16 = f32[2,256]{1,0:T(2,128)S(1)} collective-permute-done((f32[2,256]{1,0:T(2,128)S(1)}, f32[2,256]{1,0:T(2,128)S(1)}, u32[]{:S(2)}, u32[]{:S(2)}) %collective-permute-start.16) | collective-permute-done | bytes 2080 | tf_op jit(solution)/shard_map/ppermute | solution.py:22
  92.2 1.2 %collective-permute-done.17 = f32[2,256]{1,0:T(2,128)S(1)} collective-permute-done((f32[2,256]{1,0:T(2,128)S(1)}, f32[2,256]{1,0:T(2,128)S(1)}, u32[]{:S(2)}, u32[]{:S(2)}) %collective-permute-start.17) | collective-permute-done | bytes 2080 | tf_op jit(solution)/shard_map/ppermute | solution.py:22
  93.3 1.5 %collective-permute-start.18 = (f32[2,256]{1,0:T(2,128)S(1)}, f32[2,256]{1,0:T(2,128)S(1)}, u32[]{:S(2)}, u32[]{:S(2)}) collective-permute-start(f32[2,256]{1,0:T(2,128)S(1)} %add.18), channel_id=1, source_target_pairs={{0,2},{2,0},{1,3},{3,1},{4,6},{6,4},{5,7},{7,5},{8,10},{10,8},{9,1... | collective-permute-start | bytes 6152 | tf_op jit(solution)/shard_map/ppermute | solution.py:22
  94.8 2.1 %collective-permute-done.18 = f32[2,256]{1,0:T(2,128)S(1)} collective-permute-done((f32[2,256]{1,0:T(2,128)S(1)}, f32[2,256]{1,0:T(2,128)S(1)}, u32[]{:S(2)}, u32[]{:S(2)}) %collective-permute-start.18) | collective-permute-done | bytes 2080 | tf_op jit(solution)/shard_map/ppermute | solution.py:22
  96.9 0.6 add.19
  (27 shorter events, 0.5 us)
Async XLA Ops:
  1.2 21.8 %collective-permute-start.1 = (bf16[128,2048]{1,0:T(8,128)(2,1)S(1)}, bf16[128,2048]{1,0:T(8,128)(2,1)S(1)}, u32[]{:S(2)}, u32[]{:S(2)}) collective-permute-start(bf16[128,2048]{1,0:T(8,128)(2,1)S(1)} %get-tuple-element.27), channel_id=1, source_target_pairs={{0,4},{4,8},{8,12},{1,5},{5,9},{9,13},{2,6},{6,10},{10,14},{3,7},{... | collective-permute-start | bytes 1572872 | tf_op jit(solution)/shard_map/ppermute | solution.py:26
  6.2 16.8 %collective-permute-start.2 = (bf16[128,2048]{1,0:T(8,128)(2,1)S(1)}, bf16[128,2048]{1,0:T(8,128)(2,1)S(1)}, u32[]{:S(2)}, u32[]{:S(2)}) collective-permute-start(bf16[128,2048]{1,0:T(8,128)(2,1)S(1)} %get-tuple-element.27), channel_id=1, source_target_pairs={{4,0},{8,4},{12,8},{5,1},{9,5},{13,9},{6,2},{10,6},{14,10},{7,3},{... | collective-permute-start | bytes 1572872 | tf_op jit(solution)/shard_map/ppermute | solution.py:27
  7.5 29.0 %collective-permute-start.5 = (bf16[128,1792]{1,0:T(8,128)(2,1)S(1)}, bf16[128,1792]{1,0:T(8,128)(2,1)S(1)}, u32[]{:S(2)}, u32[]{:S(2)}) collective-permute-start(bf16[128,1792]{1,0:T(8,128)(2,1)S(1)} %get-tuple-element.32), channel_id=1, source_target_pairs={{0,12},{4,8},{8,4},{12,0},{1,13},{5,9},{9,5},{13,1},{2,14},{6,10},... | collective-permute-start | bytes 1376264 | tf_op jit(solution)/shard_map/ppermute | solution.py:22
  23.1 24.3 %collective-permute-start.4 = (bf16[128,2048]{1,0:T(8,128)(2,1)S(1)}, bf16[128,2048]{1,0:T(8,128)(2,1)S(1)}, u32[]{:S(2)}, u32[]{:S(2)}) collective-permute-start(bf16[128,2048]{1,0:T(8,128)(2,1)S(1)} %shard_map.43.refs_0_), channel_id=1, source_target_pairs={{0,1},{1,0},{2,3},{3,2},{4,5},{5,4},{6,7},{7,6},{8,9},{9,8},{10,11... | collective-permute-start | bytes 1572872 | tf_op jit(solution)/shard_map/ppermute | solution.py:22
  23.2 22.7 %collective-permute-start = (bf16[1792,128]{1,0:T(8,128)(2,1)S(1)}, bf16[1792,128]{1,0:T(8,128)(2,1)S(1)}, u32[]{:S(2)}, u32[]{:S(2)}) collective-permute-start(bf16[1792,128]{1,0:T(8,128)(2,1)S(1)} %get-tuple-element.26), channel_id=1, source_target_pairs={{0,4},{4,0},{8,12},{12,8},{1,5},{5,1},{9,13},{13,9},{2,6},{6,2},{1... | collective-permute-start | bytes 1376264 | tf_op jit(solution)/shard_map/ppermute | solution.py:22
  34.5 22.3 %collective-permute-start.10 = (bf16[128,2048]{1,0:T(8,128)(2,1)S(1)}, bf16[128,2048]{1,0:T(8,128)(2,1)S(1)}, u32[]{:S(2)}, u32[]{:S(2)}) collective-permute-start(bf16[128,2048]{1,0:T(8,128)(2,1)S(1)} %get-tuple-element.30.refs_2_.refs_0_.refs_1_), channel_id=1, source_target_pairs={{4,0},{8,4},{5,1},{9,5},{6,2},{10,6},{7,3},{11,7},{20,16},{24,20},... | collective-permute-start | bytes 1572872 | tf_op jit(solution)/shard_map/ppermute | solution.py:27
  35.8 21.1 %collective-permute-start.11 = (bf16[128,2048]{1,0:T(8,128)(2,1)S(1)}, bf16[128,2048]{1,0:T(8,128)(2,1)S(1)}, u32[]{:S(2)}, u32[]{:S(2)}) collective-permute-start(bf16[128,2048]{1,0:T(8,128)(2,1)S(1)} %get-tuple-element.29.refs_1_.refs_2_), channel_id=1, source_target_pairs={{4,8},{8,12},{5,9},{9,13},{6,10},{10,14},{7,11},{11,15},{20,24},{2... | collective-permute-start | bytes 1572872 | tf_op jit(solution)/shard_map/ppermute | solution.py:26
  36.5 16.0 %collective-permute-start.6 = (bf16[128,1792]{1,0:T(8,128)(2,1)S(1)}, bf16[128,1792]{1,0:T(8,128)(2,1)S(1)}, u32[]{:S(2)}, u32[]{:S(2)}) collective-permute-start(bf16[128,1792]{1,0:T(8,128)(2,1)S(1)} %shard_map.45.refs_0_.refs_3_), channel_id=1, source_target_pairs={{0,2},{2,0},{1,3},{3,1},{4,6},{6,4},{5,7},{7,5},{8,10},{10,8},{9,1... | collective-permute-start | bytes 1376264 | tf_op jit(solution)/shard_map/ppermute | solution.py:22
  45.8 17.2 %collective-permute-start.3 = (bf16[1792,128]{1,0:T(8,128)(2,1)S(1)}, bf16[1792,128]{1,0:T(8,128)(2,1)S(1)}, u32[]{:S(2)}, u32[]{:S(2)}) collective-permute-start(bf16[1792,128]{1,0:T(8,128)(2,1)S(1)} %shard_map.42.refs_0_), channel_id=1, source_target_pairs={{0,2},{2,0},{1,3},{3,1},{4,6},{6,4},{5,7},{7,5},{8,10},{10,8},{9,1... | collective-permute-start | bytes 1376264 | tf_op jit(solution)/shard_map/ppermute | solution.py:22
  47.3 25.8 %collective-permute-start.8 = (bf16[1792,128]{1,0:T(8,128)(2,1)S(1)}, bf16[1792,128]{1,0:T(8,128)(2,1)S(1)}, u32[]{:S(2)}, u32[]{:S(2)}) collective-permute-start(bf16[1792,128]{1,0:T(8,128)(2,1)S(1)} %get-tuple-element.35), channel_id=1, source_target_pairs={{0,8},{4,12},{8,0},{12,4},{1,9},{5,13},{9,1},{13,5},{2,10},{6,14},... | collective-permute-start | bytes 1376264 | tf_op jit(solution)/shard_map/ppermute | solution.py:22
  56.9 17.7 %collective-permute-start.12 = (bf16[128,2048]{1,0:T(8,128)(2,1)S(1)}, bf16[128,2048]{1,0:T(8,128)(2,1)S(1)}, u32[]{:S(2)}, u32[]{:S(2)}) collective-permute-start(bf16[128,2048]{1,0:T(8,128)(2,1)S(1)} %shard_map.49.refs_0_), channel_id=1, source_target_pairs={{0,1},{1,0},{2,3},{3,2},{4,5},{5,4},{6,7},{7,6},{8,9},{9,8},{10,11... | collective-permute-start | bytes 1572872 | tf_op jit(solution)/shard_map/ppermute | solution.py:22
  57.0 27.3 %collective-permute-start.14 = (bf16[128,2048]{1,0:T(8,128)(2,1)S(1)}, bf16[128,2048]{1,0:T(8,128)(2,1)S(1)}, u32[]{:S(2)}, u32[]{:S(2)}) collective-permute-start(bf16[128,2048]{1,0:T(8,128)(2,1)S(1)} %shard_map.49.refs_0_), channel_id=1, source_target_pairs={{4,0},{8,12},{5,1},{9,13},{6,2},{10,14},{7,3},{11,15},{20,16},{24,... | collective-permute-start | bytes 1572872 | tf_op jit(solution)/shard_map/ppermute | solution.py:286
  73.1 11.3 %collective-permute-start.9 = (bf16[1792,128]{1,0:T(8,128)(2,1)S(1)}, bf16[1792,128]{1,0:T(8,128)(2,1)S(1)}, u32[]{:S(2)}, u32[]{:S(2)}) collective-permute-start(bf16[1792,128]{1,0:T(8,128)(2,1)S(1)} %shard_map.48.refs_0_), channel_id=1, source_target_pairs={{0,2},{2,0},{1,3},{3,1},{4,6},{6,4},{5,7},{7,5},{8,10},{10,8},{9,1... | collective-permute-start | bytes 1376264 | tf_op jit(solution)/shard_map/ppermute | solution.py:22
  74.6 14.3 %collective-permute-start.7 = (f32[2,256]{1,0:T(2,128)S(1)}, f32[2,256]{1,0:T(2,128)S(1)}, u32[]{:S(2)}, u32[]{:S(2)}) collective-permute-start(f32[2,256]{1,0:T(2,128)S(1)} %shard_map.47.refs_1_.refs_3_), channel_id=1, source_target_pairs={{0,4},{4,0},{8,12},{12,8},{1,5},{5,1},{9,13},{13,9},{2,6},{6,2},{1... | collective-permute-start | bytes 6152 | tf_op jit(solution)/shard_map/ppermute | solution.py:22
  84.3 2.0 %collective-permute-start.15 = (bf16[128,2048]{1,0:T(8,128)(2,1)S(1)}, bf16[128,2048]{1,0:T(8,128)(2,1)S(1)}, u32[]{:S(2)}, u32[]{:S(2)}) collective-permute-start(bf16[128,2048]{1,0:T(8,128)(2,1)S(1)} %shard_map.53.refs_0_), channel_id=1, source_target_pairs={{0,1},{1,0},{2,3},{3,2},{4,5},{5,4},{6,7},{7,6},{8,9},{9,8},{10,11... | collective-permute-start | bytes 1572872 | tf_op jit(solution)/shard_map/ppermute | solution.py:22
  85.2 4.5 %collective-permute-start.13 = (f32[2,256]{1,0:T(2,128)S(1)}, f32[2,256]{1,0:T(2,128)S(1)}, u32[]{:S(2)}, u32[]{:S(2)}) collective-permute-start(f32[2,256]{1,0:T(2,128)S(1)} %shard_map.52), channel_id=1, source_target_pairs={{0,8},{4,12},{8,0},{12,4},{1,9},{5,13},{9,1},{13,5},{2,10},{6,14},... | collective-permute-start | bytes 6152 | tf_op jit(solution)/shard_map/ppermute | solution.py:22
  86.7 5.4 %collective-permute-start.16 = (f32[2,256]{1,0:T(2,128)S(1)}, f32[2,256]{1,0:T(2,128)S(1)}, u32[]{:S(2)}, u32[]{:S(2)}) collective-permute-start(f32[2,256]{1,0:T(2,128)S(1)} %shard_map.54), channel_id=1, source_target_pairs={{0,12},{4,8},{8,4},{12,0},{1,13},{5,9},{9,5},{13,1},{2,14},{6,10},... | collective-permute-start | bytes 6152 | tf_op jit(solution)/shard_map/ppermute | solution.py:22
  92.2 1.2 %collective-permute-start.17 = (f32[2,256]{1,0:T(2,128)S(1)}, f32[2,256]{1,0:T(2,128)S(1)}, u32[]{:S(2)}, u32[]{:S(2)}) collective-permute-start(f32[2,256]{1,0:T(2,128)S(1)} %add_add_fusion), channel_id=1, source_target_pairs={{0,1},{1,0},{2,3},{3,2},{4,5},{5,4},{6,7},{7,6},{8,9},{9,8},{10,11... | collective-permute-start | bytes 6152 | tf_op jit(solution)/shard_map/ppermute | solution.py:22
  93.3 3.6 %collective-permute-start.18 = (f32[2,256]{1,0:T(2,128)S(1)}, f32[2,256]{1,0:T(2,128)S(1)}, u32[]{:S(2)}, u32[]{:S(2)}) collective-permute-start(f32[2,256]{1,0:T(2,128)S(1)} %add.18), channel_id=1, source_target_pairs={{0,2},{2,0},{1,3},{3,1},{4,6},{6,4},{5,7},{7,5},{8,10},{10,8},{9,1... | collective-permute-start | bytes 6152 | tf_op jit(solution)/shard_map/ppermute | solution.py:22

commit v13 on v12

--- a/solution.py
+++ b/solution.py
@@ -81,7 +81,7 @@
 
 
 def rest_kernel(steps, acts_ref, grads_ref, query_ref, near_query, near_acts, own_out, *refs):
-    outs, own, blocks, arrived = refs[: len(steps)], refs[-3], refs[-2], refs[-1]
+    outs, own, blocks, arrived = list(refs[:-3]), refs[-3], refs[-2], refs[-1]
     me = lax.axis_index("dp")
     tokens, rows = own.shape
     copies = [pltpu.make_async_copy(grads_ref.at[:, pl.ds(pl.multiple_of(me * rows, rows), rows)], own, arrived.at[0])]
@@ -92,16 +92,20 @@
     copies.append(pltpu.make_async_copy(query_ref, near_query, arrived.at[len(steps) + 2]))
     for copy in copies:
         copy.start()
-    for k, out in enumerate(outs):
+    for k in range(len(steps)):
         copies[1 + k].wait()
-        out[...] = blocks[k].astype(jnp.float32).T.astype(out.dtype)
+        turned, at = blocks[k].astype(jnp.float32).T.astype(blocks.dtype), 0
+        while at < rows:
+            out = outs.pop(0)
+            out[...] = turned[at : at + out.shape[0]]
+            at += out.shape[0]
     copies[0].wait()
     own_out[...] = own[...].astype(jnp.float32).T.astype(own_out.dtype)
     for copy in copies[-2:]:
         copy.wait()
 
 
-def hold(blocks, tokens):
+def hold(blocks, tokens, flops=1024):
     count = len(blocks)
     return pl.pallas_call(
         lambda *refs: None,
@@ -110,7 +114,7 @@
         out_shape=[jax.ShapeDtypeStruct(block.shape, block.dtype) for block in blocks],
         input_output_aliases={i: i for i in range(count)},
         compiler_params=pltpu.CompilerParams(vmem_limit_bytes=1024 * 1024),
-        cost_estimate=pl.CostEstimate(flops=1024, bytes_accessed=1024, transcendentals=0),
+        cost_estimate=pl.CostEstimate(flops=flops, bytes_accessed=1024, transcendentals=0),
     )(*blocks, *tokens)
 
 
@@ -139,13 +143,14 @@
 
 
 def joined(parts, axis):
+    parts = [part[...] for part in parts]
     if len(parts) == 1:
-        return parts[0][...]
+        return parts[0]
     column, found = lax.axis_index("din"), []
     for p in range(len(parts)):
-        chosen = parts[0][...]
+        chosen = parts[0]
         for r in range(1, len(parts)):
-            chosen = jnp.where(column == p ^ r, parts[r][...], chosen)
+            chosen = jnp.where(column == p ^ r, parts[r], chosen)
         found.append(chosen)
     return jnp.concatenate(found, axis=axis)
 
@@ -181,16 +186,21 @@
     return call(mix_kernel, [*parts, queries], outs, flops, tokens, scratch)
 
 
-def score_kernel(*refs):
+def score_kernel(pieces, *refs):
     *parts, mix_ref, out_ref = refs
-    grads = joined(parts, 1).astype(jnp.float32)
-    for q in range(mix_ref.shape[0]):
-        out_ref[q : q + 1, :] = jnp.sum(grads * mix_ref[q], axis=0, keepdims=True)
+    size = mix_ref.shape[1] // pieces
+    for p in range(pieces):
+        grads = joined(parts[p::pieces], 1).astype(jnp.float32)
+        for q in range(mix_ref.shape[0]):
+            term = jnp.sum(grads * mix_ref[q, p * size : (p + 1) * size], axis=0, keepdims=True)
+            out_ref[q : q + 1, :] = term if p == 0 else out_ref[q : q + 1, :] + term
 
 
 def scores_of_grads(parts, mix, tokens=(), flops=1024):
     nq, _, count = mix.shape
-    return call(score_kernel, [*parts, mix], [((nq, count), jnp.float32)], flops, tokens)[0]
+    parts = [part if isinstance(part, list) else [part] for part in parts]
+    kernel = functools.partial(score_kernel, len(parts[0]))
+    return call(kernel, [*sum(parts, []), mix], [((nq, count), jnp.float32)], flops, tokens)[0]
 
 
 def project_kernel(*refs):
@@ -236,7 +246,7 @@
     return call(finish_kernel, [mine, other, proj], [((nq, count), jnp.float32)], tokens=tokens)[0]
 
 
-def cut(activations, out_grads, queries, far, others):
+def cut(activations, out_grads, queries, far, others, pieces):
     count, part = lax.axis_size("dp"), out_grads.shape[0] // lax.axis_size("din")
     rows, (tokens, width), dtype = queries.shape[2], activations.shape, out_grads.dtype
     half = tokens // 2
@@ -246,11 +256,12 @@
         share = lax.dynamic_slice_in_dim(out_grads, column * part, part, 0)
         away = [lax.dynamic_slice_in_dim(share, (me ^ d) * rows, rows, 1) for d in [far, *others]]
         own = lax.dynamic_slice_in_dim(out_grads, me * rows, rows, 1).T
-        return (mine, away[0]), (queries, activations, own, *[block.T for block in away[1:]])
+        turned = [block.T for block in away[1:]]
+        return (mine, away[0]), (queries, activations, own, *turned[:-1], *jnp.split(turned[-1], pieces))
     outs = [((half, width), activations.dtype), ((part, rows), dtype)]
     first = fetch(functools.partial(first_kernel, far), [activations, out_grads], outs, [], 2)
     outs = [(queries.shape, queries.dtype), (activations.shape, activations.dtype), ((rows, tokens), dtype)]
-    outs += [((rows, part), dtype)] * len(others)
+    outs += [((rows, part), dtype)] * (len(others) - 1) + [((rows // pieces, part), dtype)] * pieces
     scratch = [pltpu.VMEM((tokens, rows), dtype), pltpu.VMEM((len(others), part, rows), dtype)]
     arrays = [activations, out_grads, queries]
     return first, fetch(functools.partial(rest_kernel, others), arrays, outs, scratch, len(others) + 3)
@@ -267,10 +278,14 @@
 
     far, late = count - 1, count - 2
     early = list(range(1, late))
-    (mine, far_grads), (queries, own_acts, own, *sent) = cut(activations, out_grads, queries, far, early + [late])
+    pieces = 2
+    (mine, far_grads), (queries, own_acts, own, *sent) = cut(
+        activations, out_grads, queries, far, early + [late], pieces
+    )
     hops = [(mine, mine)]
     hops.append(pass_on(hops[0], 1, count))
-    arrived = {d: trade(block, {"dp": d}) for d, block in zip([far, *early, late], [far_grads, *sent])}
+    arrived = {d: trade(block, {"dp": d}) for d, block in zip([far, *early], [far_grads, *sent])}
+    tail = [trade(block, {"dp": late}) for block in sent[len(early) :]]
 
     mix, token = mixed([own_acts], queries, SHORT)
     scores = scores_of_grads([own], mix)
@@ -281,7 +296,7 @@
     mixes, token = {}, scores
     for d in early:
         mixes[d], token = mixed(acts_of(from_partner(hops, d, count)), queries, SHORT, [token])
-    sides = to_columns(hold([arrived[far]], hops[1])[0])
+    sides = to_columns(hold([arrived[far]], [*hops[1], *[arrived[d] for d in early]])[0])
     block = from_partner(hops, late, count, [token] + sides)
     end = lax.ppermute(block, "dp", [(1, 0), (count - 2, count - 1)])
     hops.append((end, end))
@@ -293,12 +308,12 @@
         token = scores_of_grads(sides, mixes[d], [token])
         terms.append(trade(token, {"dp": d}))
 
-    sides = to_columns(hold([arrived[late]], [token])[0])
-    mix, token = mixed(acts_of(block), queries, SHORT, [token])
-    sides = sides[:1] + list(hold(sides[1:], [token]))
+    tail = [to_columns(hold([piece], [token], LONG)[0]) for piece in tail]
+    mix, done = mixed(acts_of(block), queries, SHORT, [token])
+    block = from_partner(hops, far, count, [done])
+    terms.append(trade(scores_of_acts(*acts_of(block), proj), {"dp": far}))
+    sides = [list(hold(sides, [done])) for sides in zip(*tail)]
     terms.append(trade(scores_of_grads(sides, mix, (), LONG), {"dp": late}))
-    block = from_partner(hops, far, count, [token])
-    terms.append(trade(scores_of_acts(*acts_of(block), proj), {"dp": far}))
     return over_chips(sum(terms, scores), spread)
 
 

time: 97.7 us -> 97.7 us (level)
  waiting for transfers between devices: 34 us -> 42.6 us
  starting transfers between devices: 34.1 us -> 25.6 us
    ppermute x14 -> x16, waiting for transfers between devices: 24.7 us -> 36.9 us  [trade(): return lax.ppermute(block, axes, route[::-1] if backwards else route)]
    ppermute x14 -> x16, starting transfers between devices: 24.6 us -> 16.1 us  [trade(): return lax.ppermute(block, axes, route[::-1] if backwards else route)]
    ppermute x2, waiting for transfers between devices: 4.37 us -> 0.76 us  [pass_on(): lax.ppermute(block[1], 'dp', [(i, i - 1) for i in range(1, count - step +...]
  transfers between devices with their start and end apart: 19 -> 21, of which waited for: 9 -> 12; matrix products, arithmetic and copies ran while one was open for 0% -> 0% of each run, Pallas kernels for 28% -> 28%
where the time goes in v13:
time: 97.7 us; the launch traced here: 97.5 us
  waiting for transfers between devices  42.6 us (44%)
  Pallas kernels  28.5 us (29%)
  starting transfers between devices  25.6 us (26%)
    ppermute x16, waiting for transfers between devices, trade(): return lax.ppermute(block, axes, route[::-1] if backwards else route)  36.9 us
    pallas_call x11, Pallas kernels, call(): pl.pallas_call(body, in_specs=[NEAR] * len(arrays) + [ANYWHERE] * skip, o...  21.2 us
    ppermute x16, starting transfers between devices, trade(): return lax.ppermute(block, axes, route[::-1] if backwards else route)  16.1 us
    pallas_call x2, Pallas kernels, fetch(): pl.pallas_call(kernel, in_specs=[ANYWHERE] * len(arrays), out_specs=[NEAR...  7.3 us
    ppermute x2, starting transfers between devices, pass_on(): lax.ppermute(block[0], 'dp', [(i, i + 1) for i in range(step - 1, count -...  5.65 us
    ppermute x1, waiting for transfers between devices, on_device(): end = lax.ppermute(block, 'dp', [(1, 0), (count - 2, count - 1)])  4.97 us
    ppermute x2, starting transfers between devices, pass_on(): lax.ppermute(block[1], 'dp', [(i, i - 1) for i in range(1, count - step +...  2.58 us
  transfers between devices with their start and end apart: 21, of which 12 were waited for; matrix products, arithmetic and copies ran while one was open for 0% of the time, Pallas kernels for 28%

profile of v13, /device:TPU:0, one launch (start us, length us, event | category | flops | bytes accessed | tf_op | source)
XLA Modules:
  0.0 97.5 jit_solution(14999280800035724986)
XLA Ops:
  0.0 1.2 %shard_map.40 = (bf16[128,2048]{1,0:T(8,128)(2,1)S(1)}, bf16[128,1792]{1,0:T(8,128)(2,1)S(1)}) custom-call(bf16[256,2048]{1,0:T(8,128)(2,1)} %acts_ref.3, bf16[256,7168]{1,0:T(8,128)(2,1)} %grads_ref.3), custom_call_target="tpu_custom_call" | custom-call | flops 1024 | bytes 1024 | tf_op jit(solution)/shard_map/pallas_call | solution.py:53
  1.2 5.0 %collective-permute-start.1 = (bf16[128,2048]{1,0:T(8,128)(2,1)S(1)}, bf16[128,2048]{1,0:T(8,128)(2,1)S(1)}, u32[]{:S(2)}, u32[]{:S(2)}) collective-permute-start(bf16[128,2048]{1,0:T(8,128)(2,1)S(1)} %get-tuple-element.32), channel_id=1, source_target_pairs={{0,4},{4,8},{8,12},{1,5},{5,9},{9,13},{2,6},{6,10},{10,14},{3,7},{... | collective-permute-start | bytes 1572872 | tf_op jit(solution)/shard_map/ppermute | solution.py:26
  6.2 1.3 %collective-permute-start.2 = (bf16[128,2048]{1,0:T(8,128)(2,1)S(1)}, bf16[128,2048]{1,0:T(8,128)(2,1)S(1)}, u32[]{:S(2)}, u32[]{:S(2)}) collective-permute-start(bf16[128,2048]{1,0:T(8,128)(2,1)S(1)} %get-tuple-element.32), channel_id=1, source_target_pairs={{4,0},{8,4},{12,8},{5,1},{9,5},{13,9},{6,2},{10,6},{14,10},{7,3},{... | collective-permute-start | bytes 1572872 | tf_op jit(solution)/shard_map/ppermute | solution.py:27
  7.5 4.7 %collective-permute-start.5 = (bf16[128,1792]{1,0:T(8,128)(2,1)S(1)}, bf16[128,1792]{1,0:T(8,128)(2,1)S(1)}, u32[]{:S(2)}, u32[]{:S(2)}) collective-permute-start(bf16[128,1792]{1,0:T(8,128)(2,1)S(1)} %get-tuple-element.37), channel_id=1, source_target_pairs={{0,12},{4,8},{8,4},{12,0},{1,13},{5,9},{9,5},{13,1},{2,14},{6,10},... | collective-permute-start | bytes 1376264 | tf_op jit(solution)/shard_map/ppermute | solution.py:22
  12.2 6.1 %shard_map.37 = (bf16[2,1,1792,2048]{3,2,1,0:T(8,128)(2,1)S(1)}, bf16[256,2048]{1,0:T(8,128)(2,1)S(1)}, bf16[1792,256]{1,0:T(8,128)(2,1)S(1)}, bf16[1792,128]{1,...) custom-call(bf16[256,2048]{1,0:T(8,128)(2,1)} %acts_ref.3, bf16[256,7168]{1,0:T(8,128)(2,1)} %grads_ref.3, ...), custom_call_target="tpu_custom_call" | custom-call | flops 1024 | bytes 1024 | tf_op jit(solution)/shard_map/pallas_call | solution.py:53
  18.4 4.7 %shard_map.38 = (f32[2,1792,256]{2,1,0:T(8,128)S(1)}, f32[8,128]{1,0:T(8,128)S(1)}) custom-call(bf16[256,2048]{1,0:T(8,128)(2,1)S(1)} %get-tuple-element.28.refs_0_, bf16[2,1,1792,2048]{3,2,1,0:T(8,128)(2,1)S(1)} %get-tuple-element.29.refs_1_.refs_2_), custom_call_target="tpu_custom_call" | custom-call | flops 1000000 | bytes 1024 | tf_op jit(solution)/shard_map/pallas_call | solution.py:41
  23.1 0.8 collective-permute-done.2.refs_1_
  24.0 1.3 %collective-permute-start.8 = (bf16[128,2048]{1,0:T(8,128)(2,1)S(1)}, bf16[128,2048]{1,0:T(8,128)(2,1)S(1)}, u32[]{:S(2)}, u32[]{:S(2)}) collective-permute-start(bf16[128,2048]{1,0:T(8,128)(2,1)S(1)} %get-tuple-element.35.refs_2_.refs_0_.refs_1_), channel_id=1, source_target_pairs={{4,0},{8,4},{5,1},{9,5},{6,2},{10,6},{7,3},{11,7},{20,16},{24,20},... | collective-permute-start | bytes 1572872 | tf_op jit(solution)/shard_map/ppermute | solution.py:27
  26.0 8.8 %collective-permute-done.5.refs_0_ = bf16[128,1792]{1,0:T(8,128)(2,1)S(1)} collective-permute-done((bf16[128,1792]{1,0:T(8,128)(2,1)S(1)}, bf16[128,1792]{1,0:T(8,128)(2,1)S(1)}, u32[]{:S(2)}, u32[]{:S(2)}) %collective-permute-start.5) | collective-permute-done | bytes 458784 | tf_op jit(solution)/shard_map/ppermute | solution.py:22
  34.8 7.8 %collective-permute-done.refs_0_.refs_3_ = bf16[1792,128]{1,0:T(8,128)(2,1)S(1)} collective-permute-done((bf16[1792,128]{1,0:T(8,128)(2,1)S(1)}, bf16[1792,128]{1,0:T(8,128)(2,1)S(1)}, u32[]{:S(2)}, u32[]{:S(2)}) %collective-permute-start) | collective-permute-done | bytes 458784 | tf_op jit(solution)/shard_map/ppermute | solution.py:22
  42.6 1.5 %collective-permute-start.6 = (bf16[128,1792]{1,0:T(8,128)(2,1)S(1)}, bf16[128,1792]{1,0:T(8,128)(2,1)S(1)}, u32[]{:S(2)}, u32[]{:S(2)}) collective-permute-start(bf16[128,1792]{1,0:T(8,128)(2,1)S(1)} %shard_map.45.refs_0_.refs_3_), channel_id=1, source_target_pairs={{0,2},{2,0},{1,3},{3,1},{4,6},{6,4},{5,7},{7,5},{8,10},{10,8},{9,1... | collective-permute-start | bytes 1376264 | tf_op jit(solution)/shard_map/ppermute | solution.py:22
  44.6 1.1 %collective-permute-start.15 = (bf16[896,128]{1,0:T(8,128)(2,1)S(1)}, bf16[896,128]{1,0:T(8,128)(2,1)S(1)}, u32[]{:S(2)}, u32[]{:S(2)}) collective-permute-start(bf16[896,128]{1,0:T(8,128)(2,1)S(1)} %get-tuple-element.43), channel_id=1, source_target_pairs={{0,8},{4,12},{8,0},{12,4},{1,9},{5,13},{9,1},{13,5},{2,10},{6,14},... | collective-permute-start | bytes 688136 | tf_op jit(solution)/shard_map/ppermute | solution.py:22
  46.2 4.7 %shard_map.44 = (f32[2,1792,256]{2,1,0:T(8,128)S(1)}, f32[8,128]{1,0:T(8,128)S(1)}) custom-call(bf16[128,2048]{1,0:T(8,128)(2,1)S(1)} %shard_map.43.refs_0_, bf16[128,2048]{1,0:T(8,128)(2,1)S(1)} %collective-permute-done.4.refs_1_, bf16[2,1,1792,2048]{3,2,1,0:T(8,128)(2,1)S(1)} %get-tuple-element.29.refs_1_.refs_2_, f32[2,256]{1,0:T(2,128)S(1)} %shard_map.39.refs_3_), custom_call_target="tpu_custom_call" | custom-call | flops 1000000 | bytes 1024 | tf_op jit(solution)/shard_map/pallas_call | solution.py:41
  50.8 5.2 %collective-permute-done.6.refs_1_.refs_4_ = bf16[128,1792]{1,0:T(8,128)(2,1)S(1)} collective-permute-done((bf16[128,1792]{1,0:T(8,128)(2,1)S(1)}, bf16[128,1792]{1,0:T(8,128)(2,1)S(1)}, u32[]{:S(2)}, u32[]{:S(2)}) %collective-permute-start.6) | collective-permute-done | bytes 458784 | tf_op jit(solution)/shard_map/ppermute | solution.py:22
  56.0 1.1 %collective-permute-start.14 = (bf16[896,128]{1,0:T(8,128)(2,1)S(1)}, bf16[896,128]{1,0:T(8,128)(2,1)S(1)}, u32[]{:S(2)}, u32[]{:S(2)}) collective-permute-start(bf16[896,128]{1,0:T(8,128)(2,1)S(1)} %get-tuple-element.42), channel_id=1, source_target_pairs={{0,8},{4,12},{8,0},{12,4},{1,9},{5,13},{9,1},{13,5},{2,10},{6,14},... | collective-permute-start | bytes 688136 | tf_op jit(solution)/shard_map/ppermute | solution.py:22
  57.3 1.3 %collective-permute-start.10 = (bf16[128,2048]{1,0:T(8,128)(2,1)S(1)}, bf16[128,2048]{1,0:T(8,128)(2,1)S(1)}, u32[]{:S(2)}, u32[]{:S(2)}) collective-permute-start(bf16[128,2048]{1,0:T(8,128)(2,1)S(1)} %shard_map.48.refs_0_), channel_id=1, source_target_pairs={{4,0},{8,12},{5,1},{9,13},{6,2},{10,14},{7,3},{11,15},{20,16},{24,... | collective-permute-start | bytes 1572872 | tf_op jit(solution)/shard_map/ppermute | solution.py:301
  58.6 4.7 %shard_map.46 = (f32[2,256,2048]{2,1,0:T(8,128)S(1)}, f32[8,128]{1,0:T(8,128)S(1)}) custom-call(bf16[128,1792]{1,0:T(8,128)(2,1)S(1)} %shard_map.45.refs_0_.refs_3_, bf16[128,1792]{1,0:T(8,128)(2,1)S(1)} %collective-permute-done.6.refs_1_.refs_4_, bf16[2,1,1792,2048]{3,2,1,0:T(8,128)(2,1)S(1)} %get-tuple-element.29.refs_1_.refs_2_, ...), custom_call_target="tpu_custom_call" | custom-call | flops 1000000 | bytes 1024 | tf_op jit(solution)/shard_map/pallas_call | solution.py:41
  63.4 0.8 shard_map.47.refs_3_.refs_1_
  64.1 5.5 %collective-permute-done.15.refs_0_ = bf16[896,128]{1,0:T(8,128)(2,1)S(1)} collective-permute-done((bf16[896,128]{1,0:T(8,128)(2,1)S(1)}, bf16[896,128]{1,0:T(8,128)(2,1)S(1)}, u32[]{:S(2)}, u32[]{:S(2)}) %collective-permute-start.15) | collective-permute-done | bytes 229408 | tf_op jit(solution)/shard_map/ppermute | solution.py:22
  69.6 1.5 %collective-permute-start.17 = (bf16[896,128]{1,0:T(8,128)(2,1)S(1)}, bf16[896,128]{1,0:T(8,128)(2,1)S(1)}, u32[]{:S(2)}, u32[]{:S(2)}) collective-permute-start(bf16[896,128]{1,0:T(8,128)(2,1)S(1)} %shard_map.53.refs_1_), channel_id=1, source_target_pairs={{0,2},{2,0},{1,3},{3,1},{4,6},{6,4},{5,7},{7,5},{8,10},{10,8},{9,1... | collective-permute-start | bytes 688136 | tf_op jit(solution)/shard_map/ppermute | solution.py:22
  71.1 2.0 %collective-permute-done.14.refs_0_ = bf16[896,128]{1,0:T(8,128)(2,1)S(1)} collective-permute-done((bf16[896,128]{1,0:T(8,128)(2,1)S(1)}, bf16[896,128]{1,0:T(8,128)(2,1)S(1)}, u32[]{:S(2)}, u32[]{:S(2)}) %collective-permute-start.14) | collective-permute-done | bytes 229408 | tf_op jit(solution)/shard_map/ppermute | solution.py:22
  73.1 1.5 %collective-permute-start.16 = (bf16[896,128]{1,0:T(8,128)(2,1)S(1)}, bf16[896,128]{1,0:T(8,128)(2,1)S(1)}, u32[]{:S(2)}, u32[]{:S(2)}) collective-permute-start(bf16[896,128]{1,0:T(8,128)(2,1)S(1)} %shard_map.52.refs_0_), channel_id=1, source_target_pairs={{0,2},{2,0},{1,3},{3,1},{4,6},{6,4},{5,7},{7,5},{8,10},{10,8},{9,1... | collective-permute-start | bytes 688136 | tf_op jit(solution)/shard_map/ppermute | solution.py:22
  74.6 4.7 %shard_map.49 = (f32[2,1792,256]{2,1,0:T(8,128)S(1)}, f32[8,128]{1,0:T(8,128)S(1)}) custom-call(bf16[128,2048]{1,0:T(8,128)(2,1)S(1)} %shard_map.48.refs_0_, bf16[128,2048]{1,0:T(8,128)(2,1)S(1)} %collective-permute-done.11.refs_1_, bf16[2,1,1792,2048]{3,2,1,0:T(8,128)(2,1)S(1)} %get-tuple-element.29.refs_1_.refs_2_, f32[2,256]{1,0:T(2,128)S(1)} %shard_map.47.refs_3_.refs_1_), custom_call_target="tpu_custom_call" | custom-call | flops 1000000 | bytes 1024 | tf_op jit(solution)/shard_map/pallas_call | solution.py:41
  79.3 5.0 %collective-permute-done.10.refs_0_ = bf16[128,2048]{1,0:T(8,128)(2,1)S(1)} collective-permute-done((bf16[128,2048]{1,0:T(8,128)(2,1)S(1)}, bf16[128,2048]{1,0:T(8,128)(2,1)S(1)}, u32[]{:S(2)}, u32[]{:S(2)}) %collective-permute-start.10) | collective-permute-done | bytes 524320 | tf_op jit(solution)/shard_map/ppermute | solution.py:301
  84.4 0.7 shard_map.56
  85.2 1.0 %collective-permute-done.12.refs_1_ = bf16[128,2048]{1,0:T(8,128)(2,1)S(1)} collective-permute-done((bf16[128,2048]{1,0:T(8,128)(2,1)S(1)}, bf16[128,2048]{1,0:T(8,128)(2,1)S(1)}, u32[]{:S(2)}, u32[]{:S(2)}) %collective-permute-start.12) | collective-permute-done | bytes 524320 | tf_op jit(solution)/shard_map/ppermute | solution.py:22
  86.7 2.1 %collective-permute-start.13 = (f32[2,256]{1,0:T(2,128)S(1)}, f32[2,256]{1,0:T(2,128)S(1)}, u32[]{:S(2)}, u32[]{:S(2)}) collective-permute-start(f32[2,256]{1,0:T(2,128)S(1)} %shard_map.51), channel_id=1, source_target_pairs={{0,12},{4,8},{8,4},{12,0},{1,13},{5,9},{9,5},{13,1},{2,14},{6,10},... | collective-permute-start | bytes 6152 | tf_op jit(solution)/shard_map/ppermute | solution.py:22
  88.8 0.9 collective-permute-done.18
  89.7 2.4 %collective-permute-done.13 = f32[2,256]{1,0:T(2,128)S(1)} collective-permute-done((f32[2,256]{1,0:T(2,128)S(1)}, f32[2,256]{1,0:T(2,128)S(1)}, u32[]{:S(2)}, u32[]{:S(2)}) %collective-permute-start.13) | collective-permute-done | bytes 2080 | tf_op jit(solution)/shard_map/ppermute | solution.py:22
  92.2 1.2 %collective-permute-done.19 = f32[2,256]{1,0:T(2,128)S(1)} collective-permute-done((f32[2,256]{1,0:T(2,128)S(1)}, f32[2,256]{1,0:T(2,128)S(1)}, u32[]{:S(2)}, u32[]{:S(2)}) %collective-permute-start.19) | collective-permute-done | bytes 2080 | tf_op jit(solution)/shard_map/ppermute | solution.py:22
  93.3 1.5 %collective-permute-start.20 = (f32[2,256]{1,0:T(2,128)S(1)}, f32[2,256]{1,0:T(2,128)S(1)}, u32[]{:S(2)}, u32[]{:S(2)}) collective-permute-start(f32[2,256]{1,0:T(2,128)S(1)} %add.18), channel_id=1, source_target_pairs={{0,2},{2,0},{1,3},{3,1},{4,6},{6,4},{5,7},{7,5},{8,10},{10,8},{9,1... | collective-permute-start | bytes 6152 | tf_op jit(solution)/shard_map/ppermute | solution.py:22
  94.8 2.1 %collective-permute-done.20 = f32[2,256]{1,0:T(2,128)S(1)} collective-permute-done((f32[2,256]{1,0:T(2,128)S(1)}, f32[2,256]{1,0:T(2,128)S(1)}, u32[]{:S(2)}, u32[]{:S(2)}) %collective-permute-start.20) | collective-permute-done | bytes 2080 | tf_op jit(solution)/shard_map/ppermute | solution.py:22
  (33 shorter events, 3.3 us)
Async XLA Ops:
  1.2 21.9 %collective-permute-start.1 = (bf16[128,2048]{1,0:T(8,128)(2,1)S(1)}, bf16[128,2048]{1,0:T(8,128)(2,1)S(1)}, u32[]{:S(2)}, u32[]{:S(2)}) collective-permute-start(bf16[128,2048]{1,0:T(8,128)(2,1)S(1)} %get-tuple-element.32), channel_id=1, source_target_pairs={{0,4},{4,8},{8,12},{1,5},{5,9},{9,13},{2,6},{6,10},{10,14},{3,7},{... | collective-permute-start | bytes 1572872 | tf_op jit(solution)/shard_map/ppermute | solution.py:26
  6.2 17.7 %collective-permute-start.2 = (bf16[128,2048]{1,0:T(8,128)(2,1)S(1)}, bf16[128,2048]{1,0:T(8,128)(2,1)S(1)}, u32[]{:S(2)}, u32[]{:S(2)}) collective-permute-start(bf16[128,2048]{1,0:T(8,128)(2,1)S(1)} %get-tuple-element.32), channel_id=1, source_target_pairs={{4,0},{8,4},{12,8},{5,1},{9,5},{13,9},{6,2},{10,6},{14,10},{7,3},{... | collective-permute-start | bytes 1572872 | tf_op jit(solution)/shard_map/ppermute | solution.py:27
  7.5 27.3 %collective-permute-start.5 = (bf16[128,1792]{1,0:T(8,128)(2,1)S(1)}, bf16[128,1792]{1,0:T(8,128)(2,1)S(1)}, u32[]{:S(2)}, u32[]{:S(2)}) collective-permute-start(bf16[128,1792]{1,0:T(8,128)(2,1)S(1)} %get-tuple-element.37), channel_id=1, source_target_pairs={{0,12},{4,8},{8,4},{12,0},{1,13},{5,9},{9,5},{13,1},{2,14},{6,10},... | collective-permute-start | bytes 1376264 | tf_op jit(solution)/shard_map/ppermute | solution.py:22
  18.3 24.3 %collective-permute-start = (bf16[1792,128]{1,0:T(8,128)(2,1)S(1)}, bf16[1792,128]{1,0:T(8,128)(2,1)S(1)}, u32[]{:S(2)}, u32[]{:S(2)}) collective-permute-start(bf16[1792,128]{1,0:T(8,128)(2,1)S(1)} %get-tuple-element.31), channel_id=1, source_target_pairs={{0,4},{4,0},{8,12},{12,8},{1,5},{5,1},{9,13},{13,9},{2,6},{6,2},{1... | collective-permute-start | bytes 1376264 | tf_op jit(solution)/shard_map/ppermute | solution.py:22
  23.9 20.7 %collective-permute-start.4 = (bf16[128,2048]{1,0:T(8,128)(2,1)S(1)}, bf16[128,2048]{1,0:T(8,128)(2,1)S(1)}, u32[]{:S(2)}, u32[]{:S(2)}) collective-permute-start(bf16[128,2048]{1,0:T(8,128)(2,1)S(1)} %shard_map.43.refs_0_), channel_id=1, source_target_pairs={{0,1},{1,0},{2,3},{3,2},{4,5},{5,4},{6,7},{7,6},{8,9},{9,8},{10,11... | collective-permute-start | bytes 1572872 | tf_op jit(solution)/shard_map/ppermute | solution.py:22
  24.0 33.2 %collective-permute-start.8 = (bf16[128,2048]{1,0:T(8,128)(2,1)S(1)}, bf16[128,2048]{1,0:T(8,128)(2,1)S(1)}, u32[]{:S(2)}, u32[]{:S(2)}) collective-permute-start(bf16[128,2048]{1,0:T(8,128)(2,1)S(1)} %get-tuple-element.35.refs_2_.refs_0_.refs_1_), channel_id=1, source_target_pairs={{4,0},{8,4},{5,1},{9,5},{6,2},{10,6},{7,3},{11,7},{20,16},{24,20},... | collective-permute-start | bytes 1572872 | tf_op jit(solution)/shard_map/ppermute | solution.py:27
  25.3 31.9 %collective-permute-start.9 = (bf16[128,2048]{1,0:T(8,128)(2,1)S(1)}, bf16[128,2048]{1,0:T(8,128)(2,1)S(1)}, u32[]{:S(2)}, u32[]{:S(2)}) collective-permute-start(bf16[128,2048]{1,0:T(8,128)(2,1)S(1)} %get-tuple-element.34.refs_1_.refs_2_), channel_id=1, source_target_pairs={{4,8},{8,12},{5,9},{9,13},{6,10},{10,14},{7,11},{11,15},{20,24},{2... | collective-permute-start | bytes 1572872 | tf_op jit(solution)/shard_map/ppermute | solution.py:26
  42.6 13.5 %collective-permute-start.6 = (bf16[128,1792]{1,0:T(8,128)(2,1)S(1)}, bf16[128,1792]{1,0:T(8,128)(2,1)S(1)}, u32[]{:S(2)}, u32[]{:S(2)}) collective-permute-start(bf16[128,1792]{1,0:T(8,128)(2,1)S(1)} %shard_map.45.refs_0_.refs_3_), channel_id=1, source_target_pairs={{0,2},{2,0},{1,3},{3,1},{4,6},{6,4},{5,7},{7,5},{8,10},{10,8},{9,1... | collective-permute-start | bytes 1376264 | tf_op jit(solution)/shard_map/ppermute | solution.py:22
  44.1 19.3 %collective-permute-start.3 = (bf16[1792,128]{1,0:T(8,128)(2,1)S(1)}, bf16[1792,128]{1,0:T(8,128)(2,1)S(1)}, u32[]{:S(2)}, u32[]{:S(2)}) collective-permute-start(bf16[1792,128]{1,0:T(8,128)(2,1)S(1)} %shard_map.42.refs_0_), channel_id=1, source_target_pairs={{0,2},{2,0},{1,3},{3,1},{4,6},{6,4},{5,7},{7,5},{8,10},{10,8},{9,1... | collective-permute-start | bytes 1376264 | tf_op jit(solution)/shard_map/ppermute | solution.py:22
  44.6 25.0 %collective-permute-start.15 = (bf16[896,128]{1,0:T(8,128)(2,1)S(1)}, bf16[896,128]{1,0:T(8,128)(2,1)S(1)}, u32[]{:S(2)}, u32[]{:S(2)}) collective-permute-start(bf16[896,128]{1,0:T(8,128)(2,1)S(1)} %get-tuple-element.43), channel_id=1, source_target_pairs={{0,8},{4,12},{8,0},{12,4},{1,9},{5,13},{9,1},{13,5},{2,10},{6,14},... | collective-permute-start | bytes 688136 | tf_op jit(solution)/shard_map/ppermute | solution.py:22
  56.0 17.1 %collective-permute-start.14 = (bf16[896,128]{1,0:T(8,128)(2,1)S(1)}, bf16[896,128]{1,0:T(8,128)(2,1)S(1)}, u32[]{:S(2)}, u32[]{:S(2)}) collective-permute-start(bf16[896,128]{1,0:T(8,128)(2,1)S(1)} %get-tuple-element.42), channel_id=1, source_target_pairs={{0,8},{4,12},{8,0},{12,4},{1,9},{5,13},{9,1},{13,5},{2,10},{6,14},... | collective-permute-start | bytes 688136 | tf_op jit(solution)/shard_map/ppermute | solution.py:22
  57.2 17.4 %collective-permute-start.11 = (bf16[128,2048]{1,0:T(8,128)(2,1)S(1)}, bf16[128,2048]{1,0:T(8,128)(2,1)S(1)}, u32[]{:S(2)}, u32[]{:S(2)}) collective-permute-start(bf16[128,2048]{1,0:T(8,128)(2,1)S(1)} %shard_map.48.refs_0_), channel_id=1, source_target_pairs={{0,1},{1,0},{2,3},{3,2},{4,5},{5,4},{6,7},{7,6},{8,9},{9,8},{10,11... | collective-permute-start | bytes 1572872 | tf_op jit(solution)/shard_map/ppermute | solution.py:22
  57.3 26.9 %collective-permute-start.10 = (bf16[128,2048]{1,0:T(8,128)(2,1)S(1)}, bf16[128,2048]{1,0:T(8,128)(2,1)S(1)}, u32[]{:S(2)}, u32[]{:S(2)}) collective-permute-start(bf16[128,2048]{1,0:T(8,128)(2,1)S(1)} %shard_map.48.refs_0_), channel_id=1, source_target_pairs={{4,0},{8,12},{5,1},{9,13},{6,2},{10,14},{7,3},{11,15},{20,16},{24,... | collective-permute-start | bytes 1572872 | tf_op jit(solution)/shard_map/ppermute | solution.py:301
  69.6 14.8 %collective-permute-start.17 = (bf16[896,128]{1,0:T(8,128)(2,1)S(1)}, bf16[896,128]{1,0:T(8,128)(2,1)S(1)}, u32[]{:S(2)}, u32[]{:S(2)}) collective-permute-start(bf16[896,128]{1,0:T(8,128)(2,1)S(1)} %shard_map.53.refs_1_), channel_id=1, source_target_pairs={{0,2},{2,0},{1,3},{3,1},{4,6},{6,4},{5,7},{7,5},{8,10},{10,8},{9,1... | collective-permute-start | bytes 688136 | tf_op jit(solution)/shard_map/ppermute | solution.py:22
  73.1 11.3 %collective-permute-start.16 = (bf16[896,128]{1,0:T(8,128)(2,1)S(1)}, bf16[896,128]{1,0:T(8,128)(2,1)S(1)}, u32[]{:S(2)}, u32[]{:S(2)}) collective-permute-start(bf16[896,128]{1,0:T(8,128)(2,1)S(1)} %shard_map.52.refs_0_), channel_id=1, source_target_pairs={{0,2},{2,0},{1,3},{3,1},{4,6},{6,4},{5,7},{7,5},{8,10},{10,8},{9,1... | collective-permute-start | bytes 688136 | tf_op jit(solution)/shard_map/ppermute | solution.py:22
  74.6 14.2 %collective-permute-start.7 = (f32[2,256]{1,0:T(2,128)S(1)}, f32[2,256]{1,0:T(2,128)S(1)}, u32[]{:S(2)}, u32[]{:S(2)}) collective-permute-start(f32[2,256]{1,0:T(2,128)S(1)} %shard_map.47.refs_3_.refs_1_), channel_id=1, source_target_pairs={{0,4},{4,0},{8,12},{12,8},{1,5},{5,1},{9,13},{13,9},{2,6},{6,2},{1... | collective-permute-start | bytes 6152 | tf_op jit(solution)/shard_map/ppermute | solution.py:22
  84.3 2.0 %collective-permute-start.12 = (bf16[128,2048]{1,0:T(8,128)(2,1)S(1)}, bf16[128,2048]{1,0:T(8,128)(2,1)S(1)}, u32[]{:S(2)}, u32[]{:S(2)}) collective-permute-start(bf16[128,2048]{1,0:T(8,128)(2,1)S(1)} %shard_map.50.refs_0_), channel_id=1, source_target_pairs={{0,1},{1,0},{2,3},{3,2},{4,5},{5,4},{6,7},{7,6},{8,9},{9,8},{10,11... | collective-permute-start | bytes 1572872 | tf_op jit(solution)/shard_map/ppermute | solution.py:22
  85.2 4.6 %collective-permute-start.18 = (f32[2,256]{1,0:T(2,128)S(1)}, f32[2,256]{1,0:T(2,128)S(1)}, u32[]{:S(2)}, u32[]{:S(2)}) collective-permute-start(f32[2,256]{1,0:T(2,128)S(1)} %shard_map.56), channel_id=1, source_target_pairs={{0,8},{4,12},{8,0},{12,4},{1,9},{5,13},{9,1},{13,5},{2,10},{6,14},... | collective-permute-start | bytes 6152 | tf_op jit(solution)/shard_map/ppermute | solution.py:22
  86.7 5.4 %collective-permute-start.13 = (f32[2,256]{1,0:T(2,128)S(1)}, f32[2,256]{1,0:T(2,128)S(1)}, u32[]{:S(2)}, u32[]{:S(2)}) collective-permute-start(f32[2,256]{1,0:T(2,128)S(1)} %shard_map.51), channel_id=1, source_target_pairs={{0,12},{4,8},{8,4},{12,0},{1,13},{5,9},{9,5},{13,1},{2,14},{6,10},... | collective-permute-start | bytes 6152 | tf_op jit(solution)/shard_map/ppermute | solution.py:22
  92.2 1.2 %collective-permute-start.19 = (f32[2,256]{1,0:T(2,128)S(1)}, f32[2,256]{1,0:T(2,128)S(1)}, u32[]{:S(2)}, u32[]{:S(2)}) collective-permute-start(f32[2,256]{1,0:T(2,128)S(1)} %add_add_fusion), channel_id=1, source_target_pairs={{0,1},{1,0},{2,3},{3,2},{4,5},{5,4},{6,7},{7,6},{8,9},{9,8},{10,11... | collective-permute-start | bytes 6152 | tf_op jit(solution)/shard_map/ppermute | solution.py:22
  93.3 3.6 %collective-permute-start.20 = (f32[2,256]{1,0:T(2,128)S(1)}, f32[2,256]{1,0:T(2,128)S(1)}, u32[]{:S(2)}, u32[]{:S(2)}) collective-permute-start(f32[2,256]{1,0:T(2,128)S(1)} %add.18), channel_id=1, source_target_pairs={{0,2},{2,0},{1,3},{3,1},{4,6},{6,4},{5,7},{7,5},{8,10},{10,8},{9,1... | collective-permute-start | bytes 6152 | tf_op jit(solution)/shard_map/ppermute | solution.py:22

commit v14 on v13

--- a/solution.py
+++ b/solution.py
@@ -285,7 +285,6 @@
     hops = [(mine, mine)]
     hops.append(pass_on(hops[0], 1, count))
     arrived = {d: trade(block, {"dp": d}) for d, block in zip([far, *early], [far_grads, *sent])}
-    tail = [trade(block, {"dp": late}) for block in sent[len(early) :]]
 
     mix, token = mixed([own_acts], queries, SHORT)
     scores = scores_of_grads([own], mix)
@@ -296,6 +295,7 @@
     mixes, token = {}, scores
     for d in early:
         mixes[d], token = mixed(acts_of(from_partner(hops, d, count)), queries, SHORT, [token])
+    tail = [trade(hold([block], [token])[0], {"dp": late}) for block in sent[len(early) :]]
     sides = to_columns(hold([arrived[far]], [*hops[1], *[arrived[d] for d in early]])[0])
     block = from_partner(hops, late, count, [token] + sides)
     end = lax.ppermute(block, "dp", [(1, 0), (count - 2, count - 1)])

time: 97.7 us -> 94.6 us (0.968)
  waiting for transfers between devices: 42.6 us -> 36 us
  starting transfers between devices: 25.6 us -> 29 us
    ppermute x1, waiting for transfers between devices: 4.97 us -> 0.01 us  [on_device(): end = lax.ppermute(block, 'dp', [(1, 0), (count - 2, count - 1)])]
    ppermute x16, starting transfers between devices: 16.1 us -> 19.5 us  [trade(): return lax.ppermute(block, axes, route[::-1] if backwards else route)]
    ppermute x16, waiting for transfers between devices: 36.9 us -> 35.2 us  [trade(): return lax.ppermute(block, axes, route[::-1] if backwards else route)]
  transfers between devices with their start and end apart: 21 -> 21, of which waited for: 12 -> 9; matrix products, arithmetic and copies ran while one was open for 0% -> 0% of each run, Pallas kernels for 28% -> 29%
where the time goes in v14:
time: 94.6 us; the launch traced here: 94.4 us
  waiting for transfers between devices  36 us (38%)
  starting transfers between devices  29 us (31%)
  Pallas kernels  28.5 us (30%)
    ppermute x16, waiting for transfers between devices, trade(): return lax.ppermute(block, axes, route[::-1] if backwards else route)  35.2 us
    pallas_call x11, Pallas kernels, call(): pl.pallas_call(body, in_specs=[NEAR] * len(arrays) + [ANYWHERE] * skip, o...  21.2 us
    ppermute x16, starting transfers between devices, trade(): return lax.ppermute(block, axes, route[::-1] if backwards else route)  19.5 us
    pallas_call x2, Pallas kernels, fetch(): pl.pallas_call(kernel, in_specs=[ANYWHERE] * len(arrays), out_specs=[NEAR...  7.3 us
    ppermute x2, starting transfers between devices, pass_on(): lax.ppermute(block[0], 'dp', [(i, i + 1) for i in range(step - 1, count -...  5.65 us
    ppermute x2, starting transfers between devices, pass_on(): lax.ppermute(block[1], 'dp', [(i, i - 1) for i in range(1, count - step +...  2.58 us
  transfers between devices with their start and end apart: 21, of which 9 were waited for; matrix products, arithmetic and copies ran while one was open for 0% of the time, Pallas kernels for 29%

profile of v14, /device:TPU:0, one launch (start us, length us, event | category | flops | bytes accessed | tf_op | source)
XLA Modules:
  0.0 94.4 jit_solution(9466542134315069824)
XLA Ops:
  0.0 1.2 %shard_map.40 = (bf16[128,2048]{1,0:T(8,128)(2,1)S(1)}, bf16[128,1792]{1,0:T(8,128)(2,1)S(1)}) custom-call(bf16[256,2048]{1,0:T(8,128)(2,1)} %acts_ref.3, bf16[256,7168]{1,0:T(8,128)(2,1)} %grads_ref.3), custom_call_target="tpu_custom_call" | custom-call | flops 1024 | bytes 1024 | tf_op jit(solution)/shard_map/pallas_call | solution.py:53
  1.2 5.0 %collective-permute-start.1 = (bf16[128,2048]{1,0:T(8,128)(2,1)S(1)}, bf16[128,2048]{1,0:T(8,128)(2,1)S(1)}, u32[]{:S(2)}, u32[]{:S(2)}) collective-permute-start(bf16[128,2048]{1,0:T(8,128)(2,1)S(1)} %get-tuple-element.32), channel_id=1, source_target_pairs={{0,4},{4,8},{8,12},{1,5},{5,9},{9,13},{2,6},{6,10},{10,14},{3,7},{... | collective-permute-start | bytes 1572872 | tf_op jit(solution)/shard_map/ppermute | solution.py:26
  6.2 1.3 %collective-permute-start.2 = (bf16[128,2048]{1,0:T(8,128)(2,1)S(1)}, bf16[128,2048]{1,0:T(8,128)(2,1)S(1)}, u32[]{:S(2)}, u32[]{:S(2)}) collective-permute-start(bf16[128,2048]{1,0:T(8,128)(2,1)S(1)} %get-tuple-element.32), channel_id=1, source_target_pairs={{4,0},{8,4},{12,8},{5,1},{9,5},{13,9},{6,2},{10,6},{14,10},{7,3},{... | collective-permute-start | bytes 1572872 | tf_op jit(solution)/shard_map/ppermute | solution.py:27
  7.5 4.7 %collective-permute-start.5 = (bf16[128,1792]{1,0:T(8,128)(2,1)S(1)}, bf16[128,1792]{1,0:T(8,128)(2,1)S(1)}, u32[]{:S(2)}, u32[]{:S(2)}) collective-permute-start(bf16[128,1792]{1,0:T(8,128)(2,1)S(1)} %get-tuple-element.37), channel_id=1, source_target_pairs={{0,12},{4,8},{8,4},{12,0},{1,13},{5,9},{9,5},{13,1},{2,14},{6,10},... | collective-permute-start | bytes 1376264 | tf_op jit(solution)/shard_map/ppermute | solution.py:22
  12.2 6.1 %shard_map.37 = (bf16[2,1,1792,2048]{3,2,1,0:T(8,128)(2,1)S(1)}, bf16[256,2048]{1,0:T(8,128)(2,1)S(1)}, bf16[1792,256]{1,0:T(8,128)(2,1)S(1)}, bf16[1792,128]{1,...) custom-call(bf16[256,2048]{1,0:T(8,128)(2,1)} %acts_ref.3, bf16[256,7168]{1,0:T(8,128)(2,1)} %grads_ref.3, ...), custom_call_target="tpu_custom_call" | custom-call | flops 1024 | bytes 1024 | tf_op jit(solution)/shard_map/pallas_call | solution.py:53
  18.4 4.7 %shard_map.38 = (f32[2,1792,256]{2,1,0:T(8,128)S(1)}, f32[8,128]{1,0:T(8,128)S(1)}) custom-call(bf16[256,2048]{1,0:T(8,128)(2,1)S(1)} %get-tuple-element.28.refs_0_, bf16[2,1,1792,2048]{3,2,1,0:T(8,128)(2,1)S(1)} %get-tuple-element.29.refs_1_.refs_2_), custom_call_target="tpu_custom_call" | custom-call | flops 1000000 | bytes 1024 | tf_op jit(solution)/shard_map/pallas_call | solution.py:41
  23.1 0.8 collective-permute-done.2.refs_1_
  24.0 1.3 %collective-permute-start.8 = (bf16[128,2048]{1,0:T(8,128)(2,1)S(1)}, bf16[128,2048]{1,0:T(8,128)(2,1)S(1)}, u32[]{:S(2)}, u32[]{:S(2)}) collective-permute-start(bf16[128,2048]{1,0:T(8,128)(2,1)S(1)} %get-tuple-element.35.refs_2_.refs_0_.refs_1_), channel_id=1, source_target_pairs={{4,0},{8,4},{5,1},{9,5},{6,2},{10,6},{7,3},{11,7},{20,16},{24,20},... | collective-permute-start | bytes 1572872 | tf_op jit(solution)/shard_map/ppermute | solution.py:27
  25.3 0.7 collective-permute-start.9
  26.0 8.8 %collective-permute-done.5.refs_0_ = bf16[128,1792]{1,0:T(8,128)(2,1)S(1)} collective-permute-done((bf16[128,1792]{1,0:T(8,128)(2,1)S(1)}, bf16[128,1792]{1,0:T(8,128)(2,1)S(1)}, u32[]{:S(2)}, u32[]{:S(2)}) %collective-permute-start.5) | collective-permute-done | bytes 458784 | tf_op jit(solution)/shard_map/ppermute | solution.py:22
  34.8 7.8 %collective-permute-done.refs_0_.refs_3_ = bf16[1792,128]{1,0:T(8,128)(2,1)S(1)} collective-permute-done((bf16[1792,128]{1,0:T(8,128)(2,1)S(1)}, bf16[1792,128]{1,0:T(8,128)(2,1)S(1)}, u32[]{:S(2)}, u32[]{:S(2)}) %collective-permute-start) | collective-permute-done | bytes 458784 | tf_op jit(solution)/shard_map/ppermute | solution.py:22
  42.6 1.5 %collective-permute-start.6 = (bf16[128,1792]{1,0:T(8,128)(2,1)S(1)}, bf16[128,1792]{1,0:T(8,128)(2,1)S(1)}, u32[]{:S(2)}, u32[]{:S(2)}) collective-permute-start(bf16[128,1792]{1,0:T(8,128)(2,1)S(1)} %shard_map.45.refs_0_.refs_3_), channel_id=1, source_target_pairs={{0,2},{2,0},{1,3},{3,1},{4,6},{6,4},{5,7},{7,5},{8,10},{10,8},{9,1... | collective-permute-start | bytes 1376264 | tf_op jit(solution)/shard_map/ppermute | solution.py:22
  44.1 0.5 collective-permute-start.3
  45.0 4.7 %shard_map.44 = (f32[2,1792,256]{2,1,0:T(8,128)S(1)}, f32[8,128]{1,0:T(8,128)S(1)}) custom-call(bf16[128,2048]{1,0:T(8,128)(2,1)S(1)} %shard_map.43.refs_0_, bf16[128,2048]{1,0:T(8,128)(2,1)S(1)} %collective-permute-done.4.refs_1_, bf16[2,1,1792,2048]{3,2,1,0:T(8,128)(2,1)S(1)} %get-tuple-element.29.refs_1_.refs_2_, f32[2,256]{1,0:T(2,128)S(1)} %shard_map.39.refs_3_), custom_call_target="tpu_custom_call" | custom-call | flops 1000000 | bytes 1024 | tf_op jit(solution)/shard_map/pallas_call | solution.py:41
  49.7 1.2 %collective-permute-start.15 = (bf16[896,128]{1,0:T(8,128)(2,1)S(1)}, bf16[896,128]{1,0:T(8,128)(2,1)S(1)}, u32[]{:S(2)}, u32[]{:S(2)}) collective-permute-start(bf16[896,128]{1,0:T(8,128)(2,1)S(1)} %shard_map.54), channel_id=1, source_target_pairs={{0,8},{4,12},{8,0},{12,4},{1,9},{5,13},{9,1},{13,5},{2,10},{6,14},... | collective-permute-start | bytes 688136 | tf_op jit(solution)/shard_map/ppermute | solution.py:22
  50.9 5.1 %collective-permute-done.6.refs_1_.refs_4_ = bf16[128,1792]{1,0:T(8,128)(2,1)S(1)} collective-permute-done((bf16[128,1792]{1,0:T(8,128)(2,1)S(1)}, bf16[128,1792]{1,0:T(8,128)(2,1)S(1)}, u32[]{:S(2)}, u32[]{:S(2)}) %collective-permute-start.6) | collective-permute-done | bytes 458784 | tf_op jit(solution)/shard_map/ppermute | solution.py:22
  56.2 1.3 %collective-permute-start.10 = (bf16[128,2048]{1,0:T(8,128)(2,1)S(1)}, bf16[128,2048]{1,0:T(8,128)(2,1)S(1)}, u32[]{:S(2)}, u32[]{:S(2)}) collective-permute-start(bf16[128,2048]{1,0:T(8,128)(2,1)S(1)} %shard_map.48.refs_0_), channel_id=1, source_target_pairs={{4,0},{8,12},{5,1},{9,13},{6,2},{10,14},{7,3},{11,15},{20,16},{24,... | collective-permute-start | bytes 1572872 | tf_op jit(solution)/shard_map/ppermute | solution.py:301
  57.5 3.3 %collective-permute-start.14 = (bf16[896,128]{1,0:T(8,128)(2,1)S(1)}, bf16[896,128]{1,0:T(8,128)(2,1)S(1)}, u32[]{:S(2)}, u32[]{:S(2)}) collective-permute-start(bf16[896,128]{1,0:T(8,128)(2,1)S(1)} %shard_map.52), channel_id=1, source_target_pairs={{0,8},{4,12},{8,0},{12,4},{1,9},{5,13},{9,1},{13,5},{2,10},{6,14},... | collective-permute-start | bytes 688136 | tf_op jit(solution)/shard_map/ppermute | solution.py:22
  60.8 4.8 %shard_map.46 = (f32[2,256,2048]{2,1,0:T(8,128)S(1)}, f32[8,128]{1,0:T(8,128)S(1)}) custom-call(bf16[128,1792]{1,0:T(8,128)(2,1)S(1)} %shard_map.45.refs_0_.refs_3_, bf16[128,1792]{1,0:T(8,128)(2,1)S(1)} %collective-permute-done.6.refs_1_.refs_4_, bf16[2,1,1792,2048]{3,2,1,0:T(8,128)(2,1)S(1)} %get-tuple-element.29.refs_1_.refs_2_, ...), custom_call_target="tpu_custom_call" | custom-call | flops 1000000 | bytes 1024 | tf_op jit(solution)/shard_map/pallas_call | solution.py:41
  65.6 0.8 shard_map.47.refs_3_.refs_1_
  66.3 1.6 %collective-permute-start.17 = (bf16[896,128]{1,0:T(8,128)(2,1)S(1)}, bf16[896,128]{1,0:T(8,128)(2,1)S(1)}, u32[]{:S(2)}, u32[]{:S(2)}) collective-permute-start(bf16[896,128]{1,0:T(8,128)(2,1)S(1)} %shard_map.55.refs_1_), channel_id=1, source_target_pairs={{0,2},{2,0},{1,3},{3,1},{4,6},{6,4},{5,7},{7,5},{8,10},{10,8},{9,1... | collective-permute-start | bytes 688136 | tf_op jit(solution)/shard_map/ppermute | solution.py:22
  67.9 5.3 %collective-permute-done.14.refs_0_ = bf16[896,128]{1,0:T(8,128)(2,1)S(1)} collective-permute-done((bf16[896,128]{1,0:T(8,128)(2,1)S(1)}, bf16[896,128]{1,0:T(8,128)(2,1)S(1)}, u32[]{:S(2)}, u32[]{:S(2)}) %collective-permute-start.14) | collective-permute-done | bytes 229408 | tf_op jit(solution)/shard_map/ppermute | solution.py:22
  73.1 1.5 %collective-permute-start.16 = (bf16[896,128]{1,0:T(8,128)(2,1)S(1)}, bf16[896,128]{1,0:T(8,128)(2,1)S(1)}, u32[]{:S(2)}, u32[]{:S(2)}) collective-permute-start(bf16[896,128]{1,0:T(8,128)(2,1)S(1)} %shard_map.53.refs_0_), channel_id=1, source_target_pairs={{0,2},{2,0},{1,3},{3,1},{4,6},{6,4},{5,7},{7,5},{8,10},{10,8},{9,1... | collective-permute-start | bytes 688136 | tf_op jit(solution)/shard_map/ppermute | solution.py:22
  74.6 4.7 %shard_map.49 = (f32[2,1792,256]{2,1,0:T(8,128)S(1)}, f32[8,128]{1,0:T(8,128)S(1)}) custom-call(bf16[128,2048]{1,0:T(8,128)(2,1)S(1)} %shard_map.48.refs_0_, bf16[128,2048]{1,0:T(8,128)(2,1)S(1)} %collective-permute-done.11.refs_1_, bf16[2,1,1792,2048]{3,2,1,0:T(8,128)(2,1)S(1)} %get-tuple-element.29.refs_1_.refs_2_, f32[2,256]{1,0:T(2,128)S(1)} %shard_map.47.refs_3_.refs_1_), custom_call_target="tpu_custom_call" | custom-call | flops 1000000 | bytes 1024 | tf_op jit(solution)/shard_map/pallas_call | solution.py:41
  79.7 0.7 shard_map.58
  80.4 2.7 %collective-permute-start.18 = (f32[2,256]{1,0:T(2,128)S(1)}, f32[2,256]{1,0:T(2,128)S(1)}, u32[]{:S(2)}, u32[]{:S(2)}) collective-permute-start(f32[2,256]{1,0:T(2,128)S(1)} %shard_map.58), channel_id=1, source_target_pairs={{0,8},{4,12},{8,0},{12,4},{1,9},{5,13},{9,1},{13,5},{2,10},{6,14},... | collective-permute-start | bytes 6152 | tf_op jit(solution)/shard_map/ppermute | solution.py:22
  83.6 1.6 %collective-permute-start.13 = (f32[2,256]{1,0:T(2,128)S(1)}, f32[2,256]{1,0:T(2,128)S(1)}, u32[]{:S(2)}, u32[]{:S(2)}) collective-permute-start(f32[2,256]{1,0:T(2,128)S(1)} %shard_map.51), channel_id=1, source_target_pairs={{0,12},{4,8},{8,4},{12,0},{1,13},{5,9},{9,5},{13,1},{2,14},{6,10},... | collective-permute-start | bytes 6152 | tf_op jit(solution)/shard_map/ppermute | solution.py:22
  85.2 3.9 %collective-permute-done.13 = f32[2,256]{1,0:T(2,128)S(1)} collective-permute-done((f32[2,256]{1,0:T(2,128)S(1)}, f32[2,256]{1,0:T(2,128)S(1)}, u32[]{:S(2)}, u32[]{:S(2)}) %collective-permute-start.13) | collective-permute-done | bytes 2080 | tf_op jit(solution)/shard_map/ppermute | solution.py:22
  89.1 1.2 %collective-permute-done.19 = f32[2,256]{1,0:T(2,128)S(1)} collective-permute-done((f32[2,256]{1,0:T(2,128)S(1)}, f32[2,256]{1,0:T(2,128)S(1)}, u32[]{:S(2)}, u32[]{:S(2)}) %collective-permute-start.19) | collective-permute-done | bytes 2080 | tf_op jit(solution)/shard_map/ppermute | solution.py:22
  90.2 0.5 collective-permute-start.20
  90.8 3.0 %collective-permute-done.20 = f32[2,256]{1,0:T(2,128)S(1)} collective-permute-done((f32[2,256]{1,0:T(2,128)S(1)}, f32[2,256]{1,0:T(2,128)S(1)}, u32[]{:S(2)}, u32[]{:S(2)}) %collective-permute-start.20) | collective-permute-done | bytes 2080 | tf_op jit(solution)/shard_map/ppermute | solution.py:22
  93.8 0.6 add.19
  (35 shorter events, 1.6 us)
Async XLA Ops:
  1.2 21.9 %collective-permute-start.1 = (bf16[128,2048]{1,0:T(8,128)(2,1)S(1)}, bf16[128,2048]{1,0:T(8,128)(2,1)S(1)}, u32[]{:S(2)}, u32[]{:S(2)}) collective-permute-start(bf16[128,2048]{1,0:T(8,128)(2,1)S(1)} %get-tuple-element.32), channel_id=1, source_target_pairs={{0,4},{4,8},{8,12},{1,5},{5,9},{9,13},{2,6},{6,10},{10,14},{3,7},{... | collective-permute-start | bytes 1572872 | tf_op jit(solution)/shard_map/ppermute | solution.py:26
  6.2 17.7 %collective-permute-start.2 = (bf16[128,2048]{1,0:T(8,128)(2,1)S(1)}, bf16[128,2048]{1,0:T(8,128)(2,1)S(1)}, u32[]{:S(2)}, u32[]{:S(2)}) collective-permute-start(bf16[128,2048]{1,0:T(8,128)(2,1)S(1)} %get-tuple-element.32), channel_id=1, source_target_pairs={{4,0},{8,4},{12,8},{5,1},{9,5},{13,9},{6,2},{10,6},{14,10},{7,3},{... | collective-permute-start | bytes 1572872 | tf_op jit(solution)/shard_map/ppermute | solution.py:27
  7.5 27.3 %collective-permute-start.5 = (bf16[128,1792]{1,0:T(8,128)(2,1)S(1)}, bf16[128,1792]{1,0:T(8,128)(2,1)S(1)}, u32[]{:S(2)}, u32[]{:S(2)}) collective-permute-start(bf16[128,1792]{1,0:T(8,128)(2,1)S(1)} %get-tuple-element.37), channel_id=1, source_target_pairs={{0,12},{4,8},{8,4},{12,0},{1,13},{5,9},{9,5},{13,1},{2,14},{6,10},... | collective-permute-start | bytes 1376264 | tf_op jit(solution)/shard_map/ppermute | solution.py:22
  18.3 24.3 %collective-permute-start = (bf16[1792,128]{1,0:T(8,128)(2,1)S(1)}, bf16[1792,128]{1,0:T(8,128)(2,1)S(1)}, u32[]{:S(2)}, u32[]{:S(2)}) collective-permute-start(bf16[1792,128]{1,0:T(8,128)(2,1)S(1)} %get-tuple-element.31), channel_id=1, source_target_pairs={{0,4},{4,0},{8,12},{12,8},{1,5},{5,1},{9,13},{13,9},{2,6},{6,2},{1... | collective-permute-start | bytes 1376264 | tf_op jit(solution)/shard_map/ppermute | solution.py:22
  23.9 21.1 %collective-permute-start.4 = (bf16[128,2048]{1,0:T(8,128)(2,1)S(1)}, bf16[128,2048]{1,0:T(8,128)(2,1)S(1)}, u32[]{:S(2)}, u32[]{:S(2)}) collective-permute-start(bf16[128,2048]{1,0:T(8,128)(2,1)S(1)} %shard_map.43.refs_0_), channel_id=1, source_target_pairs={{0,1},{1,0},{2,3},{3,2},{4,5},{5,4},{6,7},{7,6},{8,9},{9,8},{10,11... | collective-permute-start | bytes 1572872 | tf_op jit(solution)/shard_map/ppermute | solution.py:22
  24.0 32.1 %collective-permute-start.8 = (bf16[128,2048]{1,0:T(8,128)(2,1)S(1)}, bf16[128,2048]{1,0:T(8,128)(2,1)S(1)}, u32[]{:S(2)}, u32[]{:S(2)}) collective-permute-start(bf16[128,2048]{1,0:T(8,128)(2,1)S(1)} %get-tuple-element.35.refs_2_.refs_0_.refs_1_), channel_id=1, source_target_pairs={{4,0},{8,4},{5,1},{9,5},{6,2},{10,6},{7,3},{11,7},{20,16},{24,20},... | collective-permute-start | bytes 1572872 | tf_op jit(solution)/shard_map/ppermute | solution.py:27
  25.3 30.8 %collective-permute-start.9 = (bf16[128,2048]{1,0:T(8,128)(2,1)S(1)}, bf16[128,2048]{1,0:T(8,128)(2,1)S(1)}, u32[]{:S(2)}, u32[]{:S(2)}) collective-permute-start(bf16[128,2048]{1,0:T(8,128)(2,1)S(1)} %get-tuple-element.34.refs_1_.refs_2_), channel_id=1, source_target_pairs={{4,8},{8,12},{5,9},{9,13},{6,10},{10,14},{7,11},{11,15},{20,24},{2... | collective-permute-start | bytes 1572872 | tf_op jit(solution)/shard_map/ppermute | solution.py:26
  42.6 13.5 %collective-permute-start.6 = (bf16[128,1792]{1,0:T(8,128)(2,1)S(1)}, bf16[128,1792]{1,0:T(8,128)(2,1)S(1)}, u32[]{:S(2)}, u32[]{:S(2)}) collective-permute-start(bf16[128,1792]{1,0:T(8,128)(2,1)S(1)} %shard_map.45.refs_0_.refs_3_), channel_id=1, source_target_pairs={{0,2},{2,0},{1,3},{3,1},{4,6},{6,4},{5,7},{7,5},{8,10},{10,8},{9,1... | collective-permute-start | bytes 1376264 | tf_op jit(solution)/shard_map/ppermute | solution.py:22
  44.1 21.5 %collective-permute-start.3 = (bf16[1792,128]{1,0:T(8,128)(2,1)S(1)}, bf16[1792,128]{1,0:T(8,128)(2,1)S(1)}, u32[]{:S(2)}, u32[]{:S(2)}) collective-permute-start(bf16[1792,128]{1,0:T(8,128)(2,1)S(1)} %shard_map.42.refs_0_), channel_id=1, source_target_pairs={{0,2},{2,0},{1,3},{3,1},{4,6},{6,4},{5,7},{7,5},{8,10},{10,8},{9,1... | collective-permute-start | bytes 1376264 | tf_op jit(solution)/shard_map/ppermute | solution.py:22
  49.7 16.6 %collective-permute-start.15 = (bf16[896,128]{1,0:T(8,128)(2,1)S(1)}, bf16[896,128]{1,0:T(8,128)(2,1)S(1)}, u32[]{:S(2)}, u32[]{:S(2)}) collective-permute-start(bf16[896,128]{1,0:T(8,128)(2,1)S(1)} %shard_map.54), channel_id=1, source_target_pairs={{0,8},{4,12},{8,0},{12,4},{1,9},{5,13},{9,1},{13,5},{2,10},{6,14},... | collective-permute-start | bytes 688136 | tf_op jit(solution)/shard_map/ppermute | solution.py:22
  56.1 18.6 %collective-permute-start.11 = (bf16[128,2048]{1,0:T(8,128)(2,1)S(1)}, bf16[128,2048]{1,0:T(8,128)(2,1)S(1)}, u32[]{:S(2)}, u32[]{:S(2)}) collective-permute-start(bf16[128,2048]{1,0:T(8,128)(2,1)S(1)} %shard_map.48.refs_0_), channel_id=1, source_target_pairs={{0,1},{1,0},{2,3},{3,2},{4,5},{5,4},{6,7},{7,6},{8,9},{9,8},{10,11... | collective-permute-start | bytes 1572872 | tf_op jit(solution)/shard_map/ppermute | solution.py:22
  56.2 23.2 %collective-permute-start.10 = (bf16[128,2048]{1,0:T(8,128)(2,1)S(1)}, bf16[128,2048]{1,0:T(8,128)(2,1)S(1)}, u32[]{:S(2)}, u32[]{:S(2)}) collective-permute-start(bf16[128,2048]{1,0:T(8,128)(2,1)S(1)} %shard_map.48.refs_0_), channel_id=1, source_target_pairs={{4,0},{8,12},{5,1},{9,13},{6,2},{10,14},{7,3},{11,15},{20,16},{24,... | collective-permute-start | bytes 1572872 | tf_op jit(solution)/shard_map/ppermute | solution.py:301
  57.5 15.7 %collective-permute-start.14 = (bf16[896,128]{1,0:T(8,128)(2,1)S(1)}, bf16[896,128]{1,0:T(8,128)(2,1)S(1)}, u32[]{:S(2)}, u32[]{:S(2)}) collective-permute-start(bf16[896,128]{1,0:T(8,128)(2,1)S(1)} %shard_map.52), channel_id=1, source_target_pairs={{0,8},{4,12},{8,0},{12,4},{1,9},{5,13},{9,1},{13,5},{2,10},{6,14},... | collective-permute-start | bytes 688136 | tf_op jit(solution)/shard_map/ppermute | solution.py:22
  66.3 13.2 %collective-permute-start.17 = (bf16[896,128]{1,0:T(8,128)(2,1)S(1)}, bf16[896,128]{1,0:T(8,128)(2,1)S(1)}, u32[]{:S(2)}, u32[]{:S(2)}) collective-permute-start(bf16[896,128]{1,0:T(8,128)(2,1)S(1)} %shard_map.55.refs_1_), channel_id=1, source_target_pairs={{0,2},{2,0},{1,3},{3,1},{4,6},{6,4},{5,7},{7,5},{8,10},{10,8},{9,1... | collective-permute-start | bytes 688136 | tf_op jit(solution)/shard_map/ppermute | solution.py:22
  73.1 6.6 %collective-permute-start.16 = (bf16[896,128]{1,0:T(8,128)(2,1)S(1)}, bf16[896,128]{1,0:T(8,128)(2,1)S(1)}, u32[]{:S(2)}, u32[]{:S(2)}) collective-permute-start(bf16[896,128]{1,0:T(8,128)(2,1)S(1)} %shard_map.53.refs_0_), channel_id=1, source_target_pairs={{0,2},{2,0},{1,3},{3,1},{4,6},{6,4},{5,7},{7,5},{8,10},{10,8},{9,1... | collective-permute-start | bytes 688136 | tf_op jit(solution)/shard_map/ppermute | solution.py:22
  74.6 10.6 %collective-permute-start.7 = (f32[2,256]{1,0:T(2,128)S(1)}, f32[2,256]{1,0:T(2,128)S(1)}, u32[]{:S(2)}, u32[]{:S(2)}) collective-permute-start(f32[2,256]{1,0:T(2,128)S(1)} %shard_map.47.refs_3_.refs_1_), channel_id=1, source_target_pairs={{0,4},{4,0},{8,12},{12,8},{1,5},{5,1},{9,13},{13,9},{2,6},{6,2},{1... | collective-permute-start | bytes 6152 | tf_op jit(solution)/shard_map/ppermute | solution.py:22
  79.4 3.8 %collective-permute-start.12 = (bf16[128,2048]{1,0:T(8,128)(2,1)S(1)}, bf16[128,2048]{1,0:T(8,128)(2,1)S(1)}, u32[]{:S(2)}, u32[]{:S(2)}) collective-permute-start(bf16[128,2048]{1,0:T(8,128)(2,1)S(1)} %shard_map.50.refs_0_), channel_id=1, source_target_pairs={{0,1},{1,0},{2,3},{3,2},{4,5},{5,4},{6,7},{7,6},{8,9},{9,8},{10,11... | collective-permute-start | bytes 1572872 | tf_op jit(solution)/shard_map/ppermute | solution.py:22
  80.4 4.8 %collective-permute-start.18 = (f32[2,256]{1,0:T(2,128)S(1)}, f32[2,256]{1,0:T(2,128)S(1)}, u32[]{:S(2)}, u32[]{:S(2)}) collective-permute-start(f32[2,256]{1,0:T(2,128)S(1)} %shard_map.58), channel_id=1, source_target_pairs={{0,8},{4,12},{8,0},{12,4},{1,9},{5,13},{9,1},{13,5},{2,10},{6,14},... | collective-permute-start | bytes 6152 | tf_op jit(solution)/shard_map/ppermute | solution.py:22
  83.6 5.4 %collective-permute-start.13 = (f32[2,256]{1,0:T(2,128)S(1)}, f32[2,256]{1,0:T(2,128)S(1)}, u32[]{:S(2)}, u32[]{:S(2)}) collective-permute-start(f32[2,256]{1,0:T(2,128)S(1)} %shard_map.51), channel_id=1, source_target_pairs={{0,12},{4,8},{8,4},{12,0},{1,13},{5,9},{9,5},{13,1},{2,14},{6,10},... | collective-permute-start | bytes 6152 | tf_op jit(solution)/shard_map/ppermute | solution.py:22
  89.1 1.2 %collective-permute-start.19 = (f32[2,256]{1,0:T(2,128)S(1)}, f32[2,256]{1,0:T(2,128)S(1)}, u32[]{:S(2)}, u32[]{:S(2)}) collective-permute-start(f32[2,256]{1,0:T(2,128)S(1)} %add_add_fusion), channel_id=1, source_target_pairs={{0,1},{1,0},{2,3},{3,2},{4,5},{5,4},{6,7},{7,6},{8,9},{9,8},{10,11... | collective-permute-start | bytes 6152 | tf_op jit(solution)/shard_map/ppermute | solution.py:22
  90.2 3.6 %collective-permute-start.20 = (f32[2,256]{1,0:T(2,128)S(1)}, f32[2,256]{1,0:T(2,128)S(1)}, u32[]{:S(2)}, u32[]{:S(2)}) collective-permute-start(f32[2,256]{1,0:T(2,128)S(1)} %add.18), channel_id=1, source_target_pairs={{0,2},{2,0},{1,3},{3,1},{4,6},{6,4},{5,7},{7,5},{8,10},{10,8},{9,1... | collective-permute-start | bytes 6152 | tf_op jit(solution)/shard_map/ppermute | solution.py:22

commit v15 on v14

--- a/solution.py
+++ b/solution.py
@@ -66,21 +66,15 @@
     return grads_ref.at[pl.ds(first, part), pl.ds(pl.multiple_of(device * rows, rows), rows)]
 
 
-def first_kernel(far, acts_ref, grads_ref, mine_ref, far_ref, arrived):
+def first_kernel(acts_ref, mine_ref, arrived):
     half = mine_ref.shape[0]
     rows = pl.ds(pl.multiple_of(lax.axis_index("dout") * half, half), half)
-    block = grads_block(grads_ref, lax.axis_index("dp") ^ far, *far_ref.shape)
-    copies = [
-        pltpu.make_async_copy(acts_ref.at[rows, :], mine_ref, arrived.at[0]),
-        pltpu.make_async_copy(block, far_ref, arrived.at[1]),
-    ]
-    for copy in copies:
-        copy.start()
-    for copy in copies:
-        copy.wait()
-
-
-def rest_kernel(steps, acts_ref, grads_ref, query_ref, near_query, near_acts, own_out, *refs):
+    copy = pltpu.make_async_copy(acts_ref.at[rows, :], mine_ref, arrived.at[0])
+    copy.start()
+    copy.wait()
+
+
+def rest_kernel(far, steps, acts_ref, grads_ref, query_ref, near_query, near_acts, far_out, own_out, *refs):
     outs, own, blocks, arrived = list(refs[:-3]), refs[-3], refs[-2], refs[-1]
     me = lax.axis_index("dp")
     tokens, rows = own.shape
@@ -88,8 +82,10 @@
     for k, d in enumerate(steps):
         block = grads_block(grads_ref, me ^ d, *blocks.shape[1:])
         copies.append(pltpu.make_async_copy(block, blocks.at[k], arrived.at[1 + k]))
-    copies.append(pltpu.make_async_copy(acts_ref, near_acts, arrived.at[len(steps) + 1]))
-    copies.append(pltpu.make_async_copy(query_ref, near_query, arrived.at[len(steps) + 2]))
+    block = grads_block(grads_ref, me ^ far, *far_out.shape)
+    copies.append(pltpu.make_async_copy(block, far_out, arrived.at[len(steps) + 1]))
+    copies.append(pltpu.make_async_copy(acts_ref, near_acts, arrived.at[len(steps) + 2]))
+    copies.append(pltpu.make_async_copy(query_ref, near_query, arrived.at[len(steps) + 3]))
     for copy in copies:
         copy.start()
     for k in range(len(steps)):
@@ -101,7 +97,7 @@
             at += out.shape[0]
     copies[0].wait()
     own_out[...] = own[...].astype(jnp.float32).T.astype(own_out.dtype)
-    for copy in copies[-2:]:
+    for copy in copies[-3:]:
         copy.wait()
 
 
@@ -257,14 +253,14 @@
         away = [lax.dynamic_slice_in_dim(share, (me ^ d) * rows, rows, 1) for d in [far, *others]]
         own = lax.dynamic_slice_in_dim(out_grads, me * rows, rows, 1).T
         turned = [block.T for block in away[1:]]
-        return (mine, away[0]), (queries, activations, own, *turned[:-1], *jnp.split(turned[-1], pieces))
-    outs = [((half, width), activations.dtype), ((part, rows), dtype)]
-    first = fetch(functools.partial(first_kernel, far), [activations, out_grads], outs, [], 2)
-    outs = [(queries.shape, queries.dtype), (activations.shape, activations.dtype), ((rows, tokens), dtype)]
+        return mine, (queries, activations, away[0], own, *turned[:-1], *jnp.split(turned[-1], pieces))
+    first, = fetch(first_kernel, [activations], [((half, width), activations.dtype)], [], 1)
+    outs = [(queries.shape, queries.dtype), (activations.shape, activations.dtype)]
+    outs += [((part, rows), dtype), ((rows, tokens), dtype)]
     outs += [((rows, part), dtype)] * (len(others) - 1) + [((rows // pieces, part), dtype)] * pieces
     scratch = [pltpu.VMEM((tokens, rows), dtype), pltpu.VMEM((len(others), part, rows), dtype)]
     arrays = [activations, out_grads, queries]
-    return first, fetch(functools.partial(rest_kernel, others), arrays, outs, scratch, len(others) + 3)
+    return first, fetch(functools.partial(rest_kernel, far, others), arrays, outs, scratch, len(others) + 4)
 
 
 def on_device(activations, out_grads, queries):
@@ -279,7 +275,7 @@
     far, late = count - 1, count - 2
     early = list(range(1, late))
     pieces = 2
-    (mine, far_grads), (queries, own_acts, own, *sent) = cut(
+    mine, (queries, own_acts, far_grads, own, *sent) = cut(
         activations, out_grads, queries, far, early + [late], pieces
     )
     hops = [(mine, mine)]
@@ -308,12 +304,11 @@
         token = scores_of_grads(sides, mixes[d], [token])
         terms.append(trade(token, {"dp": d}))
 
-    tail = [to_columns(hold([piece], [token], LONG)[0]) for piece in tail]
     mix, done = mixed(acts_of(block), queries, SHORT, [token])
-    block = from_partner(hops, far, count, [done])
-    terms.append(trade(scores_of_acts(*acts_of(block), proj), {"dp": far}))
-    sides = [list(hold(sides, [done])) for sides in zip(*tail)]
-    terms.append(trade(scores_of_grads(sides, mix, (), LONG), {"dp": late}))
+    tail = [to_columns(hold([piece], [done if p else token], LONG)[0]) for p, piece in enumerate(tail)]
+    token = scores_of_acts(*acts_of(from_partner(hops, far, count, [done])), proj)
+    terms.append(trade(token, {"dp": far}))
+    terms.append(trade(scores_of_grads([list(sides) for sides in zip(*tail)], mix, [token], LONG), {"dp": late}))
     return over_chips(sum(terms, scores), spread)
 
 

time: 94.6 us -> 99.1 us (1.048)
  waiting for transfers between devices: 36 us -> 41.5 us
  starting transfers between devices: 29 us -> 27.9 us
    ppermute x1, waiting for transfers between devices: 0.01 us -> 6.75 us  [on_device(): end = lax.ppermute(block, 'dp', [(1, 0), (count - 2, count - 1)])]
    ppermute x16, starting transfers between devices: 19.5 us -> 18.4 us  [trade(): return lax.ppermute(block, axes, route[::-1] if backwards else route)]
  transfers between devices with their start and end apart: 21 -> 21, of which waited for: 9 -> 11; matrix products, arithmetic and copies ran while one was open for 0% -> 0% of each run, Pallas kernels for 29% -> 28%
where the time goes in v15:
time: 99.1 us; the launch traced here: 98.9 us
  waiting for transfers between devices  41.5 us (42%)
  Pallas kernels  28.7 us (29%)
  starting transfers between devices  27.9 us (28%)
    ppermute x16, waiting for transfers between devices, trade(): return lax.ppermute(block, axes, route[::-1] if backwards else route)  34.4 us
    pallas_call x11, Pallas kernels, call(): pl.pallas_call(body, in_specs=[NEAR] * len(arrays) + [ANYWHERE] * skip, o...  21.4 us
    ppermute x16, starting transfers between devices, trade(): return lax.ppermute(block, axes, route[::-1] if backwards else route)  18.4 us
    pallas_call x2, Pallas kernels, fetch(): pl.pallas_call(kernel, in_specs=[ANYWHERE] * len(arrays), out_specs=[NEAR...  7.33 us
    ppermute x1, waiting for transfers between devices, on_device(): end = lax.ppermute(block, 'dp', [(1, 0), (count - 2, count - 1)])  6.75 us
    ppermute x2, starting transfers between devices, pass_on(): lax.ppermute(block[0], 'dp', [(i, i + 1) for i in range(step - 1, count -...  5.65 us
    ppermute x2, starting transfers between devices, pass_on(): lax.ppermute(block[1], 'dp', [(i, i - 1) for i in range(1, count - step +...  2.58 us
  transfers between devices with their start and end apart: 21, of which 11 were waited for; matrix products, arithmetic and copies ran while one was open for 0% of the time, Pallas kernels for 28%

profile of v15, /device:TPU:0, one launch (start us, length us, event | category | flops | bytes accessed | tf_op | source)
XLA Modules:
  0.0 98.9 jit_solution(13321436899347753660)
XLA Ops:
  0.0 1.0 %shard_map.40 = bf16[128,2048]{1,0:T(8,128)(2,1)S(1)} custom-call(bf16[256,2048]{1,0:T(8,128)(2,1)} %acts_ref.3), custom_call_target="tpu_custom_call" | custom-call | flops 1024 | bytes 1024 | tf_op jit(solution)/shard_map/pallas_call | solution.py:53
  1.1 5.0 %collective-permute-start.1 = (bf16[128,2048]{1,0:T(8,128)(2,1)S(1)}, bf16[128,2048]{1,0:T(8,128)(2,1)S(1)}, u32[]{:S(2)}, u32[]{:S(2)}) collective-permute-start(bf16[128,2048]{1,0:T(8,128)(2,1)S(1)} %shard_map.40), channel_id=1, source_target_pairs={{0,4},{4,8},{8,12},{1,5},{5,9},{9,13},{2,6},{6,10},{10,14},{3,7},{... | collective-permute-start | bytes 1572872 | tf_op jit(solution)/shard_map/ppermute | solution.py:26
  6.0 1.3 %collective-permute-start.2 = (bf16[128,2048]{1,0:T(8,128)(2,1)S(1)}, bf16[128,2048]{1,0:T(8,128)(2,1)S(1)}, u32[]{:S(2)}, u32[]{:S(2)}) collective-permute-start(bf16[128,2048]{1,0:T(8,128)(2,1)S(1)} %shard_map.40), channel_id=1, source_target_pairs={{4,0},{8,4},{12,8},{5,1},{9,5},{13,9},{6,2},{10,6},{14,10},{7,3},{... | collective-permute-start | bytes 1572872 | tf_op jit(solution)/shard_map/ppermute | solution.py:27
  7.3 6.3 %shard_map.37 = (bf16[2,1,1792,2048]{3,2,1,0:T(8,128)(2,1)S(1)}, bf16[256,2048]{1,0:T(8,128)(2,1)S(1)}, bf16[128,1792]{1,0:T(8,128)(2,1)S(1)}, bf16[1792,256]{1,...) custom-call(bf16[256,2048]{1,0:T(8,128)(2,1)} %acts_ref.3, ...), custom_call_target="tpu_custom_call" | custom-call | flops 1024 | bytes 1024 | tf_op jit(solution)/shard_map/pallas_call | solution.py:53
  13.6 4.7 %collective-permute-start.5 = (bf16[128,1792]{1,0:T(8,128)(2,1)S(1)}, bf16[128,1792]{1,0:T(8,128)(2,1)S(1)}, u32[]{:S(2)}, u32[]{:S(2)}) collective-permute-start(bf16[128,1792]{1,0:T(8,128)(2,1)S(1)} %get-tuple-element.31), channel_id=1, source_target_pairs={{0,12},{4,8},{8,4},{12,0},{1,13},{5,9},{9,5},{13,1},{2,14},{6,10},... | collective-permute-start | bytes 1376264 | tf_op jit(solution)/shard_map/ppermute | solution.py:22
  18.3 4.7 %shard_map.38 = (f32[2,1792,256]{2,1,0:T(8,128)S(1)}, f32[8,128]{1,0:T(8,128)S(1)}) custom-call(bf16[256,2048]{1,0:T(8,128)(2,1)S(1)} %get-tuple-element.23.refs_0_, bf16[2,1,1792,2048]{3,2,1,0:T(8,128)(2,1)S(1)} %get-tuple-element.24.refs_1_.refs_2_), custom_call_target="tpu_custom_call" | custom-call | flops 1000000 | bytes 1024 | tf_op jit(solution)/shard_map/pallas_call | solution.py:41
  23.5 1.3 %collective-permute-start.8 = (bf16[128,2048]{1,0:T(8,128)(2,1)S(1)}, bf16[128,2048]{1,0:T(8,128)(2,1)S(1)}, u32[]{:S(2)}, u32[]{:S(2)}) collective-permute-start(bf16[128,2048]{1,0:T(8,128)(2,1)S(1)} %get-tuple-element.29.refs_2_.refs_0_.refs_1_), channel_id=1, source_target_pairs={{4,0},{8,4},{5,1},{9,5},{6,2},{10,6},{7,3},{11,7},{20,16},{24,20},... | collective-permute-start | bytes 1572872 | tf_op jit(solution)/shard_map/ppermute | solution.py:27
  24.8 0.7 collective-permute-start.9
  25.5 9.2 %collective-permute-done.5.refs_0_ = bf16[128,1792]{1,0:T(8,128)(2,1)S(1)} collective-permute-done((bf16[128,1792]{1,0:T(8,128)(2,1)S(1)}, bf16[128,1792]{1,0:T(8,128)(2,1)S(1)}, u32[]{:S(2)}, u32[]{:S(2)}) %collective-permute-start.5) | collective-permute-done | bytes 458784 | tf_op jit(solution)/shard_map/ppermute | solution.py:22
  34.6 7.6 %collective-permute-done.refs_0_.refs_3_ = bf16[1792,128]{1,0:T(8,128)(2,1)S(1)} collective-permute-done((bf16[1792,128]{1,0:T(8,128)(2,1)S(1)}, bf16[1792,128]{1,0:T(8,128)(2,1)S(1)}, u32[]{:S(2)}, u32[]{:S(2)}) %collective-permute-start) | collective-permute-done | bytes 458784 | tf_op jit(solution)/shard_map/ppermute | solution.py:22
  42.3 1.5 %collective-permute-start.6 = (bf16[128,1792]{1,0:T(8,128)(2,1)S(1)}, bf16[128,1792]{1,0:T(8,128)(2,1)S(1)}, u32[]{:S(2)}, u32[]{:S(2)}) collective-permute-start(bf16[128,1792]{1,0:T(8,128)(2,1)S(1)} %shard_map.45.refs_0_.refs_3_), channel_id=1, source_target_pairs={{0,2},{2,0},{1,3},{3,1},{4,6},{6,4},{5,7},{7,5},{8,10},{10,8},{9,1... | collective-permute-start | bytes 1376264 | tf_op jit(solution)/shard_map/ppermute | solution.py:22
  44.7 4.7 %shard_map.44 = (f32[2,1792,256]{2,1,0:T(8,128)S(1)}, f32[8,128]{1,0:T(8,128)S(1)}) custom-call(bf16[128,2048]{1,0:T(8,128)(2,1)S(1)} %shard_map.43.refs_0_, bf16[128,2048]{1,0:T(8,128)(2,1)S(1)} %collective-permute-done.4.refs_1_, bf16[2,1,1792,2048]{3,2,1,0:T(8,128)(2,1)S(1)} %get-tuple-element.24.refs_1_.refs_2_, f32[2,256]{1,0:T(2,128)S(1)} %shard_map.39.refs_3_), custom_call_target="tpu_custom_call" | custom-call | flops 1000000 | bytes 1024 | tf_op jit(solution)/shard_map/pallas_call | solution.py:41
  49.4 1.4 %collective-permute-start.14 = (bf16[896,128]{1,0:T(8,128)(2,1)S(1)}, bf16[896,128]{1,0:T(8,128)(2,1)S(1)}, u32[]{:S(2)}, u32[]{:S(2)}) collective-permute-start(bf16[896,128]{1,0:T(8,128)(2,1)S(1)} %shard_map.52), channel_id=1, source_target_pairs={{0,8},{4,12},{8,0},{12,4},{1,9},{5,13},{9,1},{13,5},{2,10},{6,14},... | collective-permute-start | bytes 688136 | tf_op jit(solution)/shard_map/ppermute | solution.py:22
  50.8 4.9 %collective-permute-done.6.refs_1_.refs_4_ = bf16[128,1792]{1,0:T(8,128)(2,1)S(1)} collective-permute-done((bf16[128,1792]{1,0:T(8,128)(2,1)S(1)}, bf16[128,1792]{1,0:T(8,128)(2,1)S(1)}, u32[]{:S(2)}, u32[]{:S(2)}) %collective-permute-start.6) | collective-permute-done | bytes 458784 | tf_op jit(solution)/shard_map/ppermute | solution.py:22
  55.9 1.3 %collective-permute-start.10 = (bf16[128,2048]{1,0:T(8,128)(2,1)S(1)}, bf16[128,2048]{1,0:T(8,128)(2,1)S(1)}, u32[]{:S(2)}, u32[]{:S(2)}) collective-permute-start(bf16[128,2048]{1,0:T(8,128)(2,1)S(1)} %shard_map.48.refs_0_), channel_id=1, source_target_pairs={{4,0},{8,12},{5,1},{9,13},{6,2},{10,14},{7,3},{11,15},{20,16},{24,... | collective-permute-start | bytes 1572872 | tf_op jit(solution)/shard_map/ppermute | solution.py:297
  57.2 3.5 %collective-permute-start.15 = (bf16[896,128]{1,0:T(8,128)(2,1)S(1)}, bf16[896,128]{1,0:T(8,128)(2,1)S(1)}, u32[]{:S(2)}, u32[]{:S(2)}) collective-permute-start(bf16[896,128]{1,0:T(8,128)(2,1)S(1)} %shard_map.54), channel_id=1, source_target_pairs={{0,8},{4,12},{8,0},{12,4},{1,9},{5,13},{9,1},{13,5},{2,10},{6,14},... | collective-permute-start | bytes 688136 | tf_op jit(solution)/shard_map/ppermute | solution.py:22
  60.6 4.8 %shard_map.46 = (f32[2,256,2048]{2,1,0:T(8,128)S(1)}, f32[8,128]{1,0:T(8,128)S(1)}) custom-call(bf16[128,1792]{1,0:T(8,128)(2,1)S(1)} %shard_map.45.refs_0_.refs_3_, bf16[128,1792]{1,0:T(8,128)(2,1)S(1)} %collective-permute-done.6.refs_1_.refs_4_, bf16[2,1,1792,2048]{3,2,1,0:T(8,128)(2,1)S(1)} %get-tuple-element.24.refs_1_.refs_2_, ...), custom_call_target="tpu_custom_call" | custom-call | flops 1000000 | bytes 1024 | tf_op jit(solution)/shard_map/pallas_call | solution.py:41
  65.4 0.8 shard_map.47.refs_3_.refs_1_
  66.2 1.6 %collective-permute-start.16 = (bf16[896,128]{1,0:T(8,128)(2,1)S(1)}, bf16[896,128]{1,0:T(8,128)(2,1)S(1)}, u32[]{:S(2)}, u32[]{:S(2)}) collective-permute-start(bf16[896,128]{1,0:T(8,128)(2,1)S(1)} %shard_map.53.refs_0_), channel_id=1, source_target_pairs={{0,2},{2,0},{1,3},{3,1},{4,6},{6,4},{5,7},{7,5},{8,10},{10,8},{9,1... | collective-permute-start | bytes 688136 | tf_op jit(solution)/shard_map/ppermute | solution.py:22
  67.7 4.7 %shard_map.49 = (f32[2,1792,256]{2,1,0:T(8,128)S(1)}, f32[8,128]{1,0:T(8,128)S(1)}) custom-call(bf16[128,2048]{1,0:T(8,128)(2,1)S(1)} %shard_map.48.refs_0_, bf16[128,2048]{1,0:T(8,128)(2,1)S(1)} %collective-permute-done.11.refs_1_, bf16[2,1,1792,2048]{3,2,1,0:T(8,128)(2,1)S(1)} %get-tuple-element.24.refs_1_.refs_2_, f32[2,256]{1,0:T(2,128)S(1)} %shard_map.47.refs_3_.refs_1_), custom_call_target="tpu_custom_call" | custom-call | flops 1000000 | bytes 1024 | tf_op jit(solution)/shard_map/pallas_call | solution.py:41
  72.4 6.7 %collective-permute-done.10.refs_0_ = bf16[128,2048]{1,0:T(8,128)(2,1)S(1)} collective-permute-done((bf16[128,2048]{1,0:T(8,128)(2,1)S(1)}, bf16[128,2048]{1,0:T(8,128)(2,1)S(1)}, u32[]{:S(2)}, u32[]{:S(2)}) %collective-permute-start.10) | collective-permute-done | bytes 524320 | tf_op jit(solution)/shard_map/ppermute | solution.py:297
  79.4 1.5 %collective-permute-start.17 = (bf16[896,128]{1,0:T(8,128)(2,1)S(1)}, bf16[896,128]{1,0:T(8,128)(2,1)S(1)}, u32[]{:S(2)}, u32[]{:S(2)}) collective-permute-start(bf16[896,128]{1,0:T(8,128)(2,1)S(1)} %shard_map.55.refs_1_), channel_id=1, source_target_pairs={{0,2},{2,0},{1,3},{3,1},{4,6},{6,4},{5,7},{7,5},{8,10},{10,8},{9,1... | collective-permute-start | bytes 688136 | tf_op jit(solution)/shard_map/ppermute | solution.py:22
  81.2 0.6 shard_map.51.refs_5_
  81.8 5.5 %collective-permute-done.17.refs_3_ = bf16[896,128]{1,0:T(8,128)(2,1)S(1)} collective-permute-done((bf16[896,128]{1,0:T(8,128)(2,1)S(1)}, bf16[896,128]{1,0:T(8,128)(2,1)S(1)}, u32[]{:S(2)}, u32[]{:S(2)}) %collective-permute-start.17) | collective-permute-done | bytes 229408 | tf_op jit(solution)/shard_map/ppermute | solution.py:22
  87.3 0.7 shard_map.56
  88.1 1.9 %collective-permute-start.13 = (f32[2,256]{1,0:T(2,128)S(1)}, f32[2,256]{1,0:T(2,128)S(1)}, u32[]{:S(2)}, u32[]{:S(2)}) collective-permute-start(f32[2,256]{1,0:T(2,128)S(1)} %shard_map.51.refs_5_), channel_id=1, source_target_pairs={{0,12},{4,8},{8,4},{12,0},{1,13},{5,9},{9,5},{13,1},{2,14},{6,10},... | collective-permute-start | bytes 6152 | tf_op jit(solution)/shard_map/ppermute | solution.py:22
  90.0 2.6 %collective-permute-done.18 = f32[2,256]{1,0:T(2,128)S(1)} collective-permute-done((f32[2,256]{1,0:T(2,128)S(1)}, f32[2,256]{1,0:T(2,128)S(1)}, u32[]{:S(2)}, u32[]{:S(2)}) %collective-permute-start.18) | collective-permute-done | bytes 2080 | tf_op jit(solution)/shard_map/ppermute | solution.py:22
  92.6 1.0 collective-permute-done.13
  93.6 1.2 %collective-permute-done.19 = f32[2,256]{1,0:T(2,128)S(1)} collective-permute-done((f32[2,256]{1,0:T(2,128)S(1)}, f32[2,256]{1,0:T(2,128)S(1)}, u32[]{:S(2)}, u32[]{:S(2)}) %collective-permute-start.19) | collective-permute-done | bytes 2080 | tf_op jit(solution)/shard_map/ppermute | solution.py:22
  94.7 1.5 %collective-permute-start.20 = (f32[2,256]{1,0:T(2,128)S(1)}, f32[2,256]{1,0:T(2,128)S(1)}, u32[]{:S(2)}, u32[]{:S(2)}) collective-permute-start(f32[2,256]{1,0:T(2,128)S(1)} %add.18), channel_id=1, source_target_pairs={{0,2},{2,0},{1,3},{3,1},{4,6},{6,4},{5,7},{7,5},{8,10},{10,8},{9,1... | collective-permute-start | bytes 6152 | tf_op jit(solution)/shard_map/ppermute | solution.py:22
  96.2 2.1 %collective-permute-done.20 = f32[2,256]{1,0:T(2,128)S(1)} collective-permute-done((f32[2,256]{1,0:T(2,128)S(1)}, f32[2,256]{1,0:T(2,128)S(1)}, u32[]{:S(2)}, u32[]{:S(2)}) %collective-permute-start.20) | collective-permute-done | bytes 2080 | tf_op jit(solution)/shard_map/ppermute | solution.py:22
  98.3 0.6 add.19
  (33 shorter events, 2.1 us)
Async XLA Ops:
  1.1 22.0 %collective-permute-start.1 = (bf16[128,2048]{1,0:T(8,128)(2,1)S(1)}, bf16[128,2048]{1,0:T(8,128)(2,1)S(1)}, u32[]{:S(2)}, u32[]{:S(2)}) collective-permute-start(bf16[128,2048]{1,0:T(8,128)(2,1)S(1)} %shard_map.40), channel_id=1, source_target_pairs={{0,4},{4,8},{8,12},{1,5},{5,9},{9,13},{2,6},{6,10},{10,14},{3,7},{... | collective-permute-start | bytes 1572872 | tf_op jit(solution)/shard_map/ppermute | solution.py:26
  6.0 17.3 %collective-permute-start.2 = (bf16[128,2048]{1,0:T(8,128)(2,1)S(1)}, bf16[128,2048]{1,0:T(8,128)(2,1)S(1)}, u32[]{:S(2)}, u32[]{:S(2)}) collective-permute-start(bf16[128,2048]{1,0:T(8,128)(2,1)S(1)} %shard_map.40), channel_id=1, source_target_pairs={{4,0},{8,4},{12,8},{5,1},{9,5},{13,9},{6,2},{10,6},{14,10},{7,3},{... | collective-permute-start | bytes 1572872 | tf_op jit(solution)/shard_map/ppermute | solution.py:27
  13.6 21.0 %collective-permute-start.5 = (bf16[128,1792]{1,0:T(8,128)(2,1)S(1)}, bf16[128,1792]{1,0:T(8,128)(2,1)S(1)}, u32[]{:S(2)}, u32[]{:S(2)}) collective-permute-start(bf16[128,1792]{1,0:T(8,128)(2,1)S(1)} %get-tuple-element.31), channel_id=1, source_target_pairs={{0,12},{4,8},{8,4},{12,0},{1,13},{5,9},{9,5},{13,1},{2,14},{6,10},... | collective-permute-start | bytes 1376264 | tf_op jit(solution)/shard_map/ppermute | solution.py:22
  18.3 23.9 %collective-permute-start = (bf16[1792,128]{1,0:T(8,128)(2,1)S(1)}, bf16[1792,128]{1,0:T(8,128)(2,1)S(1)}, u32[]{:S(2)}, u32[]{:S(2)}) collective-permute-start(bf16[1792,128]{1,0:T(8,128)(2,1)S(1)} %get-tuple-element.26), channel_id=1, source_target_pairs={{0,4},{4,0},{8,12},{12,8},{1,5},{5,1},{9,13},{13,9},{2,6},{6,2},{1... | collective-permute-start | bytes 1376264 | tf_op jit(solution)/shard_map/ppermute | solution.py:22
  23.4 21.3 %collective-permute-start.4 = (bf16[128,2048]{1,0:T(8,128)(2,1)S(1)}, bf16[128,2048]{1,0:T(8,128)(2,1)S(1)}, u32[]{:S(2)}, u32[]{:S(2)}) collective-permute-start(bf16[128,2048]{1,0:T(8,128)(2,1)S(1)} %shard_map.43.refs_0_), channel_id=1, source_target_pairs={{0,1},{1,0},{2,3},{3,2},{4,5},{5,4},{6,7},{7,6},{8,9},{9,8},{10,11... | collective-permute-start | bytes 1572872 | tf_op jit(solution)/shard_map/ppermute | solution.py:22
  23.5 32.2 %collective-permute-start.8 = (bf16[128,2048]{1,0:T(8,128)(2,1)S(1)}, bf16[128,2048]{1,0:T(8,128)(2,1)S(1)}, u32[]{:S(2)}, u32[]{:S(2)}) collective-permute-start(bf16[128,2048]{1,0:T(8,128)(2,1)S(1)} %get-tuple-element.29.refs_2_.refs_0_.refs_1_), channel_id=1, source_target_pairs={{4,0},{8,4},{5,1},{9,5},{6,2},{10,6},{7,3},{11,7},{20,16},{24,20},... | collective-permute-start | bytes 1572872 | tf_op jit(solution)/shard_map/ppermute | solution.py:27
  24.8 30.9 %collective-permute-start.9 = (bf16[128,2048]{1,0:T(8,128)(2,1)S(1)}, bf16[128,2048]{1,0:T(8,128)(2,1)S(1)}, u32[]{:S(2)}, u32[]{:S(2)}) collective-permute-start(bf16[128,2048]{1,0:T(8,128)(2,1)S(1)} %get-tuple-element.28.refs_1_.refs_2_), channel_id=1, source_target_pairs={{4,8},{8,12},{5,9},{9,13},{6,10},{10,14},{7,11},{11,15},{20,24},{2... | collective-permute-start | bytes 1572872 | tf_op jit(solution)/shard_map/ppermute | solution.py:26
  42.3 13.5 %collective-permute-start.6 = (bf16[128,1792]{1,0:T(8,128)(2,1)S(1)}, bf16[128,1792]{1,0:T(8,128)(2,1)S(1)}, u32[]{:S(2)}, u32[]{:S(2)}) collective-permute-start(bf16[128,1792]{1,0:T(8,128)(2,1)S(1)} %shard_map.45.refs_0_.refs_3_), channel_id=1, source_target_pairs={{0,2},{2,0},{1,3},{3,1},{4,6},{6,4},{5,7},{7,5},{8,10},{10,8},{9,1... | collective-permute-start | bytes 1376264 | tf_op jit(solution)/shard_map/ppermute | solution.py:22
  43.8 21.6 %collective-permute-start.3 = (bf16[1792,128]{1,0:T(8,128)(2,1)S(1)}, bf16[1792,128]{1,0:T(8,128)(2,1)S(1)}, u32[]{:S(2)}, u32[]{:S(2)}) collective-permute-start(bf16[1792,128]{1,0:T(8,128)(2,1)S(1)} %shard_map.42.refs_0_), channel_id=1, source_target_pairs={{0,2},{2,0},{1,3},{3,1},{4,6},{6,4},{5,7},{7,5},{8,10},{10,8},{9,1... | collective-permute-start | bytes 1376264 | tf_op jit(solution)/shard_map/ppermute | solution.py:22
  49.4 16.8 %collective-permute-start.14 = (bf16[896,128]{1,0:T(8,128)(2,1)S(1)}, bf16[896,128]{1,0:T(8,128)(2,1)S(1)}, u32[]{:S(2)}, u32[]{:S(2)}) collective-permute-start(bf16[896,128]{1,0:T(8,128)(2,1)S(1)} %shard_map.52), channel_id=1, source_target_pairs={{0,8},{4,12},{8,0},{12,4},{1,9},{5,13},{9,1},{13,5},{2,10},{6,14},... | collective-permute-start | bytes 688136 | tf_op jit(solution)/shard_map/ppermute | solution.py:22
  55.8 12.0 %collective-permute-start.11 = (bf16[128,2048]{1,0:T(8,128)(2,1)S(1)}, bf16[128,2048]{1,0:T(8,128)(2,1)S(1)}, u32[]{:S(2)}, u32[]{:S(2)}) collective-permute-start(bf16[128,2048]{1,0:T(8,128)(2,1)S(1)} %shard_map.48.refs_0_), channel_id=1, source_target_pairs={{0,1},{1,0},{2,3},{3,2},{4,5},{5,4},{6,7},{7,6},{8,9},{9,8},{10,11... | collective-permute-start | bytes 1572872 | tf_op jit(solution)/shard_map/ppermute | solution.py:22
  55.9 23.3 %collective-permute-start.10 = (bf16[128,2048]{1,0:T(8,128)(2,1)S(1)}, bf16[128,2048]{1,0:T(8,128)(2,1)S(1)}, u32[]{:S(2)}, u32[]{:S(2)}) collective-permute-start(bf16[128,2048]{1,0:T(8,128)(2,1)S(1)} %shard_map.48.refs_0_), channel_id=1, source_target_pairs={{4,0},{8,12},{5,1},{9,13},{6,2},{10,14},{7,3},{11,15},{20,16},{24,... | collective-permute-start | bytes 1572872 | tf_op jit(solution)/shard_map/ppermute | solution.py:297
  57.2 22.2 %collective-permute-start.15 = (bf16[896,128]{1,0:T(8,128)(2,1)S(1)}, bf16[896,128]{1,0:T(8,128)(2,1)S(1)}, u32[]{:S(2)}, u32[]{:S(2)}) collective-permute-start(bf16[896,128]{1,0:T(8,128)(2,1)S(1)} %shard_map.54), channel_id=1, source_target_pairs={{0,8},{4,12},{8,0},{12,4},{1,9},{5,13},{9,1},{13,5},{2,10},{6,14},... | collective-permute-start | bytes 688136 | tf_op jit(solution)/shard_map/ppermute | solution.py:22
  66.2 15.6 %collective-permute-start.16 = (bf16[896,128]{1,0:T(8,128)(2,1)S(1)}, bf16[896,128]{1,0:T(8,128)(2,1)S(1)}, u32[]{:S(2)}, u32[]{:S(2)}) collective-permute-start(bf16[896,128]{1,0:T(8,128)(2,1)S(1)} %shard_map.53.refs_0_), channel_id=1, source_target_pairs={{0,2},{2,0},{1,3},{3,1},{4,6},{6,4},{5,7},{7,5},{8,10},{10,8},{9,1... | collective-permute-start | bytes 688136 | tf_op jit(solution)/shard_map/ppermute | solution.py:22
  79.2 2.0 %collective-permute-start.12 = (bf16[128,2048]{1,0:T(8,128)(2,1)S(1)}, bf16[128,2048]{1,0:T(8,128)(2,1)S(1)}, u32[]{:S(2)}, u32[]{:S(2)}) collective-permute-start(bf16[128,2048]{1,0:T(8,128)(2,1)S(1)} %shard_map.50.refs_0_), channel_id=1, source_target_pairs={{0,1},{1,0},{2,3},{3,2},{4,5},{5,4},{6,7},{7,6},{8,9},{9,8},{10,11... | collective-permute-start | bytes 1572872 | tf_op jit(solution)/shard_map/ppermute | solution.py:22
  79.4 7.9 %collective-permute-start.17 = (bf16[896,128]{1,0:T(8,128)(2,1)S(1)}, bf16[896,128]{1,0:T(8,128)(2,1)S(1)}, u32[]{:S(2)}, u32[]{:S(2)}) collective-permute-start(bf16[896,128]{1,0:T(8,128)(2,1)S(1)} %shard_map.55.refs_1_), channel_id=1, source_target_pairs={{0,2},{2,0},{1,3},{3,1},{4,6},{6,4},{5,7},{7,5},{8,10},{10,8},{9,1... | collective-permute-start | bytes 688136 | tf_op jit(solution)/shard_map/ppermute | solution.py:22
  80.9 9.1 %collective-permute-start.7 = (f32[2,256]{1,0:T(2,128)S(1)}, f32[2,256]{1,0:T(2,128)S(1)}, u32[]{:S(2)}, u32[]{:S(2)}) collective-permute-start(f32[2,256]{1,0:T(2,128)S(1)} %shard_map.47.refs_3_.refs_1_), channel_id=1, source_target_pairs={{0,4},{4,0},{8,12},{12,8},{1,5},{5,1},{9,13},{13,9},{2,6},{6,2},{1... | collective-permute-start | bytes 6152 | tf_op jit(solution)/shard_map/ppermute | solution.py:22
  88.0 4.5 %collective-permute-start.18 = (f32[2,256]{1,0:T(2,128)S(1)}, f32[2,256]{1,0:T(2,128)S(1)}, u32[]{:S(2)}, u32[]{:S(2)}) collective-permute-start(f32[2,256]{1,0:T(2,128)S(1)} %shard_map.56), channel_id=1, source_target_pairs={{0,8},{4,12},{8,0},{12,4},{1,9},{5,13},{9,1},{13,5},{2,10},{6,14},... | collective-permute-start | bytes 6152 | tf_op jit(solution)/shard_map/ppermute | solution.py:22
  88.1 5.4 %collective-permute-start.13 = (f32[2,256]{1,0:T(2,128)S(1)}, f32[2,256]{1,0:T(2,128)S(1)}, u32[]{:S(2)}, u32[]{:S(2)}) collective-permute-start(f32[2,256]{1,0:T(2,128)S(1)} %shard_map.51.refs_5_), channel_id=1, source_target_pairs={{0,12},{4,8},{8,4},{12,0},{1,13},{5,9},{9,5},{13,1},{2,14},{6,10},... | collective-permute-start | bytes 6152 | tf_op jit(solution)/shard_map/ppermute | solution.py:22
  93.6 1.2 %collective-permute-start.19 = (f32[2,256]{1,0:T(2,128)S(1)}, f32[2,256]{1,0:T(2,128)S(1)}, u32[]{:S(2)}, u32[]{:S(2)}) collective-permute-start(f32[2,256]{1,0:T(2,128)S(1)} %add_add_fusion), channel_id=1, source_target_pairs={{0,1},{1,0},{2,3},{3,2},{4,5},{5,4},{6,7},{7,6},{8,9},{9,8},{10,11... | collective-permute-start | bytes 6152 | tf_op jit(solution)/shard_map/ppermute | solution.py:22
  94.7 3.6 %collective-permute-start.20 = (f32[2,256]{1,0:T(2,128)S(1)}, f32[2,256]{1,0:T(2,128)S(1)}, u32[]{:S(2)}, u32[]{:S(2)}) collective-permute-start(f32[2,256]{1,0:T(2,128)S(1)} %add.18), channel_id=1, source_target_pairs={{0,2},{2,0},{1,3},{3,1},{4,6},{6,4},{5,7},{7,5},{8,10},{10,8},{9,1... | collective-permute-start | bytes 6152 | tf_op jit(solution)/shard_map/ppermute | solution.py:22

commit v16 on v15

--- a/solution.py
+++ b/solution.py
@@ -280,9 +280,10 @@
     )
     hops = [(mine, mine)]
     hops.append(pass_on(hops[0], 1, count))
-    arrived = {d: trade(block, {"dp": d}) for d, block in zip([far, *early], [far_grads, *sent])}
+    arrived = {d: trade(block, {"dp": d}) for d, block in zip(early, sent)}
 
     mix, token = mixed([own_acts], queries, SHORT)
+    arrived[far] = trade(hold([far_grads], [token])[0], {"dp": far})
     scores = scores_of_grads([own], mix)
     hops[1] = hold(list(hops[1]), [token])
     for step in range(2, count - 1):
@@ -292,8 +293,8 @@
     for d in early:
         mixes[d], token = mixed(acts_of(from_partner(hops, d, count)), queries, SHORT, [token])
     tail = [trade(hold([block], [token])[0], {"dp": late}) for block in sent[len(early) :]]
-    sides = to_columns(hold([arrived[far]], [*hops[1], *[arrived[d] for d in early]])[0])
-    block = from_partner(hops, late, count, [token] + sides)
+    sides = to_columns(hold([arrived[far]], [token])[0])
+    block = from_partner(hops, late, count, [token])
     end = lax.ppermute(block, "dp", [(1, 0), (count - 2, count - 1)])
     hops.append((end, end))
 
@@ -306,9 +307,9 @@
 
     mix, done = mixed(acts_of(block), queries, SHORT, [token])
     tail = [to_columns(hold([piece], [done if p else token], LONG)[0]) for p, piece in enumerate(tail)]
-    token = scores_of_acts(*acts_of(from_partner(hops, far, count, [done])), proj)
-    terms.append(trade(token, {"dp": far}))
-    terms.append(trade(scores_of_grads([list(sides) for sides in zip(*tail)], mix, [token], LONG), {"dp": late}))
+    block = from_partner(hops, far, count, [done])
+    terms.append(trade(scores_of_acts(*acts_of(block), proj), {"dp": far}))
+    terms.append(trade(scores_of_grads([list(sides) for sides in zip(*tail)], mix, (), LONG), {"dp": late}))
     return over_chips(sum(terms, scores), spread)
 
 

time: 99.1 us -> 96.4 us (0.973)
  waiting for transfers between devices: 41.5 us -> 36.9 us
  starting transfers between devices: 27.9 us -> 29.9 us
    ppermute x16, waiting for transfers between devices: 34.4 us -> 21.3 us  [trade(): return lax.ppermute(block, axes, route[::-1] if backwards else route)]
    ppermute x2, waiting for transfers between devices: 0.34 us -> 10.9 us  [pass_on(): lax.ppermute(block[1], 'dp', [(i, i - 1) for i in range(1, count - step +...]
    ppermute x1, waiting for transfers between devices: 6.75 us -> 4.69 us  [on_device(): end = lax.ppermute(block, 'dp', [(1, 0), (count - 2, count - 1)])]
    ppermute x16, starting transfers between devices: 18.4 us -> 20.3 us  [trade(): return lax.ppermute(block, axes, route[::-1] if backwards else route)]
  transfers between devices with their start and end apart: 21 -> 21, of which waited for: 11 -> 10; matrix products, arithmetic and copies ran while one was open for 0% -> 0% of each run, Pallas kernels for 28% -> 29%
where the time goes in v16:
time: 96.4 us; the launch traced here: 96.2 us
  waiting for transfers between devices  36.9 us (38%)
  starting transfers between devices  29.9 us (31%)
  Pallas kernels  28.6 us (30%)
    ppermute x16, waiting for transfers between devices, trade(): return lax.ppermute(block, axes, route[::-1] if backwards else route)  21.3 us
    pallas_call x11, Pallas kernels, call(): pl.pallas_call(body, in_specs=[NEAR] * len(arrays) + [ANYWHERE] * skip, o...  21.2 us
    ppermute x16, starting transfers between devices, trade(): return lax.ppermute(block, axes, route[::-1] if backwards else route)  20.3 us
    ppermute x2, waiting for transfers between devices, pass_on(): lax.ppermute(block[1], 'dp', [(i, i - 1) for i in range(1, count - step +...  10.9 us
    pallas_call x2, Pallas kernels, fetch(): pl.pallas_call(kernel, in_specs=[ANYWHERE] * len(arrays), out_specs=[NEAR...  7.33 us
    ppermute x2, starting transfers between devices, pass_on(): lax.ppermute(block[0], 'dp', [(i, i + 1) for i in range(step - 1, count -...  5.65 us
    ppermute x1, waiting for transfers between devices, on_device(): end = lax.ppermute(block, 'dp', [(1, 0), (count - 2, count - 1)])  4.69 us
    ppermute x2, starting transfers between devices, pass_on(): lax.ppermute(block[1], 'dp', [(i, i - 1) for i in range(1, count - step +...  2.57 us
  transfers between devices with their start and end apart: 21, of which 10 were waited for; matrix products, arithmetic and copies ran while one was open for 0% of the time, Pallas kernels for 29%

profile of v16, /device:TPU:0, one launch (start us, length us, event | category | flops | bytes accessed | tf_op | source)
XLA Modules:
  0.0 96.2 jit_solution(18089269440903322424)
XLA Ops:
  0.0 1.0 %shard_map.40 = bf16[128,2048]{1,0:T(8,128)(2,1)S(1)} custom-call(bf16[256,2048]{1,0:T(8,128)(2,1)} %acts_ref.3), custom_call_target="tpu_custom_call" | custom-call | flops 1024 | bytes 1024 | tf_op jit(solution)/shard_map/pallas_call | solution.py:53
  1.1 5.0 %collective-permute-start.1 = (bf16[128,2048]{1,0:T(8,128)(2,1)S(1)}, bf16[128,2048]{1,0:T(8,128)(2,1)S(1)}, u32[]{:S(2)}, u32[]{:S(2)}) collective-permute-start(bf16[128,2048]{1,0:T(8,128)(2,1)S(1)} %shard_map.40), channel_id=1, source_target_pairs={{0,4},{4,8},{8,12},{1,5},{5,9},{9,13},{2,6},{6,10},{10,14},{3,7},{... | collective-permute-start | bytes 1572872 | tf_op jit(solution)/shard_map/ppermute | solution.py:26
  6.0 1.3 %collective-permute-start.2 = (bf16[128,2048]{1,0:T(8,128)(2,1)S(1)}, bf16[128,2048]{1,0:T(8,128)(2,1)S(1)}, u32[]{:S(2)}, u32[]{:S(2)}) collective-permute-start(bf16[128,2048]{1,0:T(8,128)(2,1)S(1)} %shard_map.40), channel_id=1, source_target_pairs={{4,0},{8,4},{12,8},{5,1},{9,5},{13,9},{6,2},{10,6},{14,10},{7,3},{... | collective-permute-start | bytes 1572872 | tf_op jit(solution)/shard_map/ppermute | solution.py:27
  7.3 6.3 %shard_map.37 = (bf16[2,1,1792,2048]{3,2,1,0:T(8,128)(2,1)S(1)}, bf16[256,2048]{1,0:T(8,128)(2,1)S(1)}, bf16[128,1792]{1,0:T(8,128)(2,1)S(1)}, bf16[1792,256]{1,...) custom-call(bf16[256,2048]{1,0:T(8,128)(2,1)} %acts_ref.3, ...), custom_call_target="tpu_custom_call" | custom-call | flops 1024 | bytes 1024 | tf_op jit(solution)/shard_map/pallas_call | solution.py:53
  13.6 4.7 %shard_map.38 = (f32[2,1792,256]{2,1,0:T(8,128)S(1)}, f32[8,128]{1,0:T(8,128)S(1)}) custom-call(bf16[256,2048]{1,0:T(8,128)(2,1)S(1)} %get-tuple-element.23.refs_0_, bf16[2,1,1792,2048]{3,2,1,0:T(8,128)(2,1)S(1)} %get-tuple-element.24.refs_1_.refs_2_), custom_call_target="tpu_custom_call" | custom-call | flops 1000000 | bytes 1024 | tf_op jit(solution)/shard_map/pallas_call | solution.py:41
  18.3 3.0 %collective-permute-done.2.refs_1_ = bf16[128,2048]{1,0:T(8,128)(2,1)S(1)} collective-permute-done((bf16[128,2048]{1,0:T(8,128)(2,1)S(1)}, bf16[128,2048]{1,0:T(8,128)(2,1)S(1)}, u32[]{:S(2)}, u32[]{:S(2)}) %collective-permute-start.2) | collective-permute-done | bytes 524320 | tf_op jit(solution)/shard_map/ppermute | solution.py:27
  21.4 1.8 %collective-permute-start.5 = (bf16[128,1792]{1,0:T(8,128)(2,1)S(1)}, bf16[128,1792]{1,0:T(8,128)(2,1)S(1)}, u32[]{:S(2)}, u32[]{:S(2)}) collective-permute-start(bf16[128,1792]{1,0:T(8,128)(2,1)S(1)} %shard_map.45), channel_id=1, source_target_pairs={{0,12},{4,8},{8,4},{12,0},{1,13},{5,9},{9,5},{13,1},{2,14},{6,10},... | collective-permute-start | bytes 1376264 | tf_op jit(solution)/shard_map/ppermute | solution.py:22
  23.2 1.4 %collective-permute-start = (bf16[1792,128]{1,0:T(8,128)(2,1)S(1)}, bf16[1792,128]{1,0:T(8,128)(2,1)S(1)}, u32[]{:S(2)}, u32[]{:S(2)}) collective-permute-start(bf16[1792,128]{1,0:T(8,128)(2,1)S(1)} %get-tuple-element.26), channel_id=1, source_target_pairs={{0,4},{4,0},{8,12},{12,8},{1,5},{5,1},{9,13},{13,9},{2,6},{6,2},{1... | collective-permute-start | bytes 1376264 | tf_op jit(solution)/shard_map/ppermute | solution.py:22
  24.6 1.3 %collective-permute-start.8 = (bf16[128,2048]{1,0:T(8,128)(2,1)S(1)}, bf16[128,2048]{1,0:T(8,128)(2,1)S(1)}, u32[]{:S(2)}, u32[]{:S(2)}) collective-permute-start(bf16[128,2048]{1,0:T(8,128)(2,1)S(1)} %get-tuple-element.29.refs_2_.refs_0_.refs_1_), channel_id=1, source_target_pairs={{4,0},{8,4},{5,1},{9,5},{6,2},{10,6},{7,3},{11,7},{20,16},{24,20},... | collective-permute-start | bytes 1572872 | tf_op jit(solution)/shard_map/ppermute | solution.py:27
  27.1 4.7 %shard_map.44 = (f32[2,1792,256]{2,1,0:T(8,128)S(1)}, f32[8,128]{1,0:T(8,128)S(1)}) custom-call(bf16[128,2048]{1,0:T(8,128)(2,1)S(1)} %shard_map.43.refs_0_, bf16[128,2048]{1,0:T(8,128)(2,1)S(1)} %collective-permute-done.4.refs_1_, bf16[2,1,1792,2048]{3,2,1,0:T(8,128)(2,1)S(1)} %get-tuple-element.24.refs_1_.refs_2_, f32[2,256]{1,0:T(2,128)S(1)} %shard_map.39.refs_3_), custom_call_target="tpu_custom_call" | custom-call | flops 1000000 | bytes 1024 | tf_op jit(solution)/shard_map/pallas_call | solution.py:41
  31.7 5.0 %collective-permute-done.5.refs_0_ = bf16[128,1792]{1,0:T(8,128)(2,1)S(1)} collective-permute-done((bf16[128,1792]{1,0:T(8,128)(2,1)S(1)}, bf16[128,1792]{1,0:T(8,128)(2,1)S(1)}, u32[]{:S(2)}, u32[]{:S(2)}) %collective-permute-start.5) | collective-permute-done | bytes 458784 | tf_op jit(solution)/shard_map/ppermute | solution.py:22
  36.7 1.5 %collective-permute-start.6 = (bf16[128,1792]{1,0:T(8,128)(2,1)S(1)}, bf16[128,1792]{1,0:T(8,128)(2,1)S(1)}, u32[]{:S(2)}, u32[]{:S(2)}) collective-permute-start(bf16[128,1792]{1,0:T(8,128)(2,1)S(1)} %shard_map.46.refs_0_), channel_id=1, source_target_pairs={{0,2},{2,0},{1,3},{3,1},{4,6},{6,4},{5,7},{7,5},{8,10},{10,8},{9,1... | collective-permute-start | bytes 1376264 | tf_op jit(solution)/shard_map/ppermute | solution.py:22
  38.2 7.9 %collective-permute-done.refs_0_ = bf16[1792,128]{1,0:T(8,128)(2,1)S(1)} collective-permute-done((bf16[1792,128]{1,0:T(8,128)(2,1)S(1)}, bf16[1792,128]{1,0:T(8,128)(2,1)S(1)}, u32[]{:S(2)}, u32[]{:S(2)}) %collective-permute-start) | collective-permute-done | bytes 458784 | tf_op jit(solution)/shard_map/ppermute | solution.py:22
  46.1 1.5 %collective-permute-start.3 = (bf16[1792,128]{1,0:T(8,128)(2,1)S(1)}, bf16[1792,128]{1,0:T(8,128)(2,1)S(1)}, u32[]{:S(2)}, u32[]{:S(2)}) collective-permute-start(bf16[1792,128]{1,0:T(8,128)(2,1)S(1)} %shard_map.42.refs_0_), channel_id=1, source_target_pairs={{0,2},{2,0},{1,3},{3,1},{4,6},{6,4},{5,7},{7,5},{8,10},{10,8},{9,1... | collective-permute-start | bytes 1376264 | tf_op jit(solution)/shard_map/ppermute | solution.py:22
  47.6 1.3 %collective-permute-start.14 = (bf16[896,128]{1,0:T(8,128)(2,1)S(1)}, bf16[896,128]{1,0:T(8,128)(2,1)S(1)}, u32[]{:S(2)}, u32[]{:S(2)}) collective-permute-start(bf16[896,128]{1,0:T(8,128)(2,1)S(1)} %shard_map.53), channel_id=1, source_target_pairs={{0,8},{4,12},{8,0},{12,4},{1,9},{5,13},{9,1},{13,5},{2,10},{6,14},... | collective-permute-start | bytes 688136 | tf_op jit(solution)/shard_map/ppermute | solution.py:22
  48.9 7.9 %collective-permute-done.8.refs_0_ = bf16[128,2048]{1,0:T(8,128)(2,1)S(1)} collective-permute-done((bf16[128,2048]{1,0:T(8,128)(2,1)S(1)}, bf16[128,2048]{1,0:T(8,128)(2,1)S(1)}, u32[]{:S(2)}, u32[]{:S(2)}) %collective-permute-start.8) | collective-permute-done | bytes 524320 | tf_op jit(solution)/shard_map/ppermute | solution.py:27
  57.0 1.3 %collective-permute-start.10 = (bf16[128,2048]{1,0:T(8,128)(2,1)S(1)}, bf16[128,2048]{1,0:T(8,128)(2,1)S(1)}, u32[]{:S(2)}, u32[]{:S(2)}) collective-permute-start(bf16[128,2048]{1,0:T(8,128)(2,1)S(1)} %shard_map.49.refs_0_), channel_id=1, source_target_pairs={{4,0},{8,12},{5,1},{9,13},{6,2},{10,14},{7,3},{11,15},{20,16},{24,... | collective-permute-start | bytes 1572872 | tf_op jit(solution)/shard_map/ppermute | solution.py:298
  58.3 6.3 %collective-permute-start.15 = (bf16[896,128]{1,0:T(8,128)(2,1)S(1)}, bf16[896,128]{1,0:T(8,128)(2,1)S(1)}, u32[]{:S(2)}, u32[]{:S(2)}) collective-permute-start(bf16[896,128]{1,0:T(8,128)(2,1)S(1)} %shard_map.55), channel_id=1, source_target_pairs={{0,8},{4,12},{8,0},{12,4},{1,9},{5,13},{9,1},{13,5},{2,10},{6,14},... | collective-permute-start | bytes 688136 | tf_op jit(solution)/shard_map/ppermute | solution.py:22
  64.6 4.8 %shard_map.47 = (f32[2,256,2048]{2,1,0:T(8,128)S(1)}, f32[8,128]{1,0:T(8,128)S(1)}) custom-call(bf16[128,1792]{1,0:T(8,128)(2,1)S(1)} %shard_map.46.refs_0_, bf16[128,1792]{1,0:T(8,128)(2,1)S(1)} %collective-permute-done.6.refs_1_, bf16[2,1,1792,2048]{3,2,1,0:T(8,128)(2,1)S(1)} %get-tuple-element.24.refs_1_.refs_2_, ...), custom_call_target="tpu_custom_call" | custom-call | flops 1000000 | bytes 1024 | tf_op jit(solution)/shard_map/pallas_call | solution.py:41
  69.4 0.8 shard_map.48.refs_3_.refs_1_
  70.1 1.5 %collective-permute-start.16 = (bf16[896,128]{1,0:T(8,128)(2,1)S(1)}, bf16[896,128]{1,0:T(8,128)(2,1)S(1)}, u32[]{:S(2)}, u32[]{:S(2)}) collective-permute-start(bf16[896,128]{1,0:T(8,128)(2,1)S(1)} %shard_map.54.refs_0_), channel_id=1, source_target_pairs={{0,2},{2,0},{1,3},{3,1},{4,6},{6,4},{5,7},{7,5},{8,10},{10,8},{9,1... | collective-permute-start | bytes 688136 | tf_op jit(solution)/shard_map/ppermute | solution.py:22
  71.7 4.7 %shard_map.50 = (f32[2,1792,256]{2,1,0:T(8,128)S(1)}, f32[8,128]{1,0:T(8,128)S(1)}) custom-call(bf16[128,2048]{1,0:T(8,128)(2,1)S(1)} %shard_map.49.refs_0_, bf16[128,2048]{1,0:T(8,128)(2,1)S(1)} %collective-permute-done.11.refs_1_, bf16[2,1,1792,2048]{3,2,1,0:T(8,128)(2,1)S(1)} %get-tuple-element.24.refs_1_.refs_2_, f32[2,256]{1,0:T(2,128)S(1)} %shard_map.48.refs_3_.refs_1_), custom_call_target="tpu_custom_call" | custom-call | flops 1000000 | bytes 1024 | tf_op jit(solution)/shard_map/pallas_call | solution.py:41
  76.4 1.3 %collective-permute-start.17 = (bf16[896,128]{1,0:T(8,128)(2,1)S(1)}, bf16[896,128]{1,0:T(8,128)(2,1)S(1)}, u32[]{:S(2)}, u32[]{:S(2)}) collective-permute-start(bf16[896,128]{1,0:T(8,128)(2,1)S(1)} %shard_map.56.refs_1_), channel_id=1, source_target_pairs={{0,2},{2,0},{1,3},{3,1},{4,6},{6,4},{5,7},{7,5},{8,10},{10,8},{9,1... | collective-permute-start | bytes 688136 | tf_op jit(solution)/shard_map/ppermute | solution.py:22
  77.7 4.7 %collective-permute-done.10.refs_0_ = bf16[128,2048]{1,0:T(8,128)(2,1)S(1)} collective-permute-done((bf16[128,2048]{1,0:T(8,128)(2,1)S(1)}, bf16[128,2048]{1,0:T(8,128)(2,1)S(1)}, u32[]{:S(2)}, u32[]{:S(2)}) %collective-permute-start.10) | collective-permute-done | bytes 524320 | tf_op jit(solution)/shard_map/ppermute | solution.py:298
  82.6 1.3 %collective-permute-done.17.refs_3_ = bf16[896,128]{1,0:T(8,128)(2,1)S(1)} collective-permute-done((bf16[896,128]{1,0:T(8,128)(2,1)S(1)}, bf16[896,128]{1,0:T(8,128)(2,1)S(1)}, u32[]{:S(2)}, u32[]{:S(2)}) %collective-permute-start.17) | collective-permute-done | bytes 229408 | tf_op jit(solution)/shard_map/ppermute | solution.py:22
  83.9 0.7 shard_map.57
  85.4 2.1 %collective-permute-start.13 = (f32[2,256]{1,0:T(2,128)S(1)}, f32[2,256]{1,0:T(2,128)S(1)}, u32[]{:S(2)}, u32[]{:S(2)}) collective-permute-start(f32[2,256]{1,0:T(2,128)S(1)} %shard_map.52), channel_id=1, source_target_pairs={{0,12},{4,8},{8,4},{12,0},{1,13},{5,9},{9,5},{13,1},{2,14},{6,10},... | collective-permute-start | bytes 6152 | tf_op jit(solution)/shard_map/ppermute | solution.py:22
  87.5 1.7 %collective-permute-done.18 = f32[2,256]{1,0:T(2,128)S(1)} collective-permute-done((f32[2,256]{1,0:T(2,128)S(1)}, f32[2,256]{1,0:T(2,128)S(1)}, u32[]{:S(2)}, u32[]{:S(2)}) %collective-permute-start.18) | collective-permute-done | bytes 2080 | tf_op jit(solution)/shard_map/ppermute | solution.py:22
  89.2 1.7 %collective-permute-done.13 = f32[2,256]{1,0:T(2,128)S(1)} collective-permute-done((f32[2,256]{1,0:T(2,128)S(1)}, f32[2,256]{1,0:T(2,128)S(1)}, u32[]{:S(2)}, u32[]{:S(2)}) %collective-permute-start.13) | collective-permute-done | bytes 2080 | tf_op jit(solution)/shard_map/ppermute | solution.py:22
  90.9 1.2 %collective-permute-done.19 = f32[2,256]{1,0:T(2,128)S(1)} collective-permute-done((f32[2,256]{1,0:T(2,128)S(1)}, f32[2,256]{1,0:T(2,128)S(1)}, u32[]{:S(2)}, u32[]{:S(2)}) %collective-permute-start.19) | collective-permute-done | bytes 2080 | tf_op jit(solution)/shard_map/ppermute | solution.py:22
  92.0 1.0 %collective-permute-start.20 = (f32[2,256]{1,0:T(2,128)S(1)}, f32[2,256]{1,0:T(2,128)S(1)}, u32[]{:S(2)}, u32[]{:S(2)}) collective-permute-start(f32[2,256]{1,0:T(2,128)S(1)} %add.18), channel_id=1, source_target_pairs={{0,2},{2,0},{1,3},{3,1},{4,6},{6,4},{5,7},{7,5},{8,10},{10,8},{9,1... | collective-permute-start | bytes 6152 | tf_op jit(solution)/shard_map/ppermute | solution.py:22
  93.0 2.6 %collective-permute-done.20 = f32[2,256]{1,0:T(2,128)S(1)} collective-permute-done((f32[2,256]{1,0:T(2,128)S(1)}, f32[2,256]{1,0:T(2,128)S(1)}, u32[]{:S(2)}, u32[]{:S(2)}) %collective-permute-start.20) | collective-permute-done | bytes 2080 | tf_op jit(solution)/shard_map/ppermute | solution.py:22
  (34 shorter events, 3.0 us)
Async XLA Ops:
  1.1 17.2 %collective-permute-start.1 = (bf16[128,2048]{1,0:T(8,128)(2,1)S(1)}, bf16[128,2048]{1,0:T(8,128)(2,1)S(1)}, u32[]{:S(2)}, u32[]{:S(2)}) collective-permute-start(bf16[128,2048]{1,0:T(8,128)(2,1)S(1)} %shard_map.40), channel_id=1, source_target_pairs={{0,4},{4,8},{8,12},{1,5},{5,9},{9,13},{2,6},{6,10},{10,14},{3,7},{... | collective-permute-start | bytes 1572872 | tf_op jit(solution)/shard_map/ppermute | solution.py:26
  6.0 15.3 %collective-permute-start.2 = (bf16[128,2048]{1,0:T(8,128)(2,1)S(1)}, bf16[128,2048]{1,0:T(8,128)(2,1)S(1)}, u32[]{:S(2)}, u32[]{:S(2)}) collective-permute-start(bf16[128,2048]{1,0:T(8,128)(2,1)S(1)} %shard_map.40), channel_id=1, source_target_pairs={{4,0},{8,4},{12,8},{5,1},{9,5},{13,9},{6,2},{10,6},{14,10},{7,3},{... | collective-permute-start | bytes 1572872 | tf_op jit(solution)/shard_map/ppermute | solution.py:27
  21.3 5.7 %collective-permute-start.4 = (bf16[128,2048]{1,0:T(8,128)(2,1)S(1)}, bf16[128,2048]{1,0:T(8,128)(2,1)S(1)}, u32[]{:S(2)}, u32[]{:S(2)}) collective-permute-start(bf16[128,2048]{1,0:T(8,128)(2,1)S(1)} %shard_map.43.refs_0_), channel_id=1, source_target_pairs={{0,1},{1,0},{2,3},{3,2},{4,5},{5,4},{6,7},{7,6},{8,9},{9,8},{10,11... | collective-permute-start | bytes 1572872 | tf_op jit(solution)/shard_map/ppermute | solution.py:22
  21.4 15.2 %collective-permute-start.5 = (bf16[128,1792]{1,0:T(8,128)(2,1)S(1)}, bf16[128,1792]{1,0:T(8,128)(2,1)S(1)}, u32[]{:S(2)}, u32[]{:S(2)}) collective-permute-start(bf16[128,1792]{1,0:T(8,128)(2,1)S(1)} %shard_map.45), channel_id=1, source_target_pairs={{0,12},{4,8},{8,4},{12,0},{1,13},{5,9},{9,5},{13,1},{2,14},{6,10},... | collective-permute-start | bytes 1376264 | tf_op jit(solution)/shard_map/ppermute | solution.py:22
  23.2 22.9 %collective-permute-start = (bf16[1792,128]{1,0:T(8,128)(2,1)S(1)}, bf16[1792,128]{1,0:T(8,128)(2,1)S(1)}, u32[]{:S(2)}, u32[]{:S(2)}) collective-permute-start(bf16[1792,128]{1,0:T(8,128)(2,1)S(1)} %get-tuple-element.26), channel_id=1, source_target_pairs={{0,4},{4,0},{8,12},{12,8},{1,5},{5,1},{9,13},{13,9},{2,6},{6,2},{1... | collective-permute-start | bytes 1376264 | tf_op jit(solution)/shard_map/ppermute | solution.py:22
  24.6 32.2 %collective-permute-start.8 = (bf16[128,2048]{1,0:T(8,128)(2,1)S(1)}, bf16[128,2048]{1,0:T(8,128)(2,1)S(1)}, u32[]{:S(2)}, u32[]{:S(2)}) collective-permute-start(bf16[128,2048]{1,0:T(8,128)(2,1)S(1)} %get-tuple-element.29.refs_2_.refs_0_.refs_1_), channel_id=1, source_target_pairs={{4,0},{8,4},{5,1},{9,5},{6,2},{10,6},{7,3},{11,7},{20,16},{24,20},... | collective-permute-start | bytes 1572872 | tf_op jit(solution)/shard_map/ppermute | solution.py:27
  25.9 30.9 %collective-permute-start.9 = (bf16[128,2048]{1,0:T(8,128)(2,1)S(1)}, bf16[128,2048]{1,0:T(8,128)(2,1)S(1)}, u32[]{:S(2)}, u32[]{:S(2)}) collective-permute-start(bf16[128,2048]{1,0:T(8,128)(2,1)S(1)} %get-tuple-element.28.refs_1_.refs_2_), channel_id=1, source_target_pairs={{4,8},{8,12},{5,9},{9,13},{6,10},{10,14},{7,11},{11,15},{20,24},{2... | collective-permute-start | bytes 1572872 | tf_op jit(solution)/shard_map/ppermute | solution.py:26
  36.7 21.6 %collective-permute-start.6 = (bf16[128,1792]{1,0:T(8,128)(2,1)S(1)}, bf16[128,1792]{1,0:T(8,128)(2,1)S(1)}, u32[]{:S(2)}, u32[]{:S(2)}) collective-permute-start(bf16[128,1792]{1,0:T(8,128)(2,1)S(1)} %shard_map.46.refs_0_), channel_id=1, source_target_pairs={{0,2},{2,0},{1,3},{3,1},{4,6},{6,4},{5,7},{7,5},{8,10},{10,8},{9,1... | collective-permute-start | bytes 1376264 | tf_op jit(solution)/shard_map/ppermute | solution.py:22
  46.1 23.3 %collective-permute-start.3 = (bf16[1792,128]{1,0:T(8,128)(2,1)S(1)}, bf16[1792,128]{1,0:T(8,128)(2,1)S(1)}, u32[]{:S(2)}, u32[]{:S(2)}) collective-permute-start(bf16[1792,128]{1,0:T(8,128)(2,1)S(1)} %shard_map.42.refs_0_), channel_id=1, source_target_pairs={{0,2},{2,0},{1,3},{3,1},{4,6},{6,4},{5,7},{7,5},{8,10},{10,8},{9,1... | collective-permute-start | bytes 1376264 | tf_op jit(solution)/shard_map/ppermute | solution.py:22
  47.6 22.5 %collective-permute-start.14 = (bf16[896,128]{1,0:T(8,128)(2,1)S(1)}, bf16[896,128]{1,0:T(8,128)(2,1)S(1)}, u32[]{:S(2)}, u32[]{:S(2)}) collective-permute-start(bf16[896,128]{1,0:T(8,128)(2,1)S(1)} %shard_map.53), channel_id=1, source_target_pairs={{0,8},{4,12},{8,0},{12,4},{1,9},{5,13},{9,1},{13,5},{2,10},{6,14},... | collective-permute-start | bytes 688136 | tf_op jit(solution)/shard_map/ppermute | solution.py:22
  56.9 14.8 %collective-permute-start.11 = (bf16[128,2048]{1,0:T(8,128)(2,1)S(1)}, bf16[128,2048]{1,0:T(8,128)(2,1)S(1)}, u32[]{:S(2)}, u32[]{:S(2)}) collective-permute-start(bf16[128,2048]{1,0:T(8,128)(2,1)S(1)} %shard_map.49.refs_0_), channel_id=1, source_target_pairs={{0,1},{1,0},{2,3},{3,2},{4,5},{5,4},{6,7},{7,6},{8,9},{9,8},{10,11... | collective-permute-start | bytes 1572872 | tf_op jit(solution)/shard_map/ppermute | solution.py:22
  57.0 25.4 %collective-permute-start.10 = (bf16[128,2048]{1,0:T(8,128)(2,1)S(1)}, bf16[128,2048]{1,0:T(8,128)(2,1)S(1)}, u32[]{:S(2)}, u32[]{:S(2)}) collective-permute-start(bf16[128,2048]{1,0:T(8,128)(2,1)S(1)} %shard_map.49.refs_0_), channel_id=1, source_target_pairs={{4,0},{8,12},{5,1},{9,13},{6,2},{10,14},{7,3},{11,15},{20,16},{24,... | collective-permute-start | bytes 1572872 | tf_op jit(solution)/shard_map/ppermute | solution.py:298
  58.3 18.1 %collective-permute-start.15 = (bf16[896,128]{1,0:T(8,128)(2,1)S(1)}, bf16[896,128]{1,0:T(8,128)(2,1)S(1)}, u32[]{:S(2)}, u32[]{:S(2)}) collective-permute-start(bf16[896,128]{1,0:T(8,128)(2,1)S(1)} %shard_map.55), channel_id=1, source_target_pairs={{0,8},{4,12},{8,0},{12,4},{1,9},{5,13},{9,1},{13,5},{2,10},{6,14},... | collective-permute-start | bytes 688136 | tf_op jit(solution)/shard_map/ppermute | solution.py:22
  70.1 12.5 %collective-permute-start.16 = (bf16[896,128]{1,0:T(8,128)(2,1)S(1)}, bf16[896,128]{1,0:T(8,128)(2,1)S(1)}, u32[]{:S(2)}, u32[]{:S(2)}) collective-permute-start(bf16[896,128]{1,0:T(8,128)(2,1)S(1)} %shard_map.54.refs_0_), channel_id=1, source_target_pairs={{0,2},{2,0},{1,3},{3,1},{4,6},{6,4},{5,7},{7,5},{8,10},{10,8},{9,1... | collective-permute-start | bytes 688136 | tf_op jit(solution)/shard_map/ppermute | solution.py:22
  76.4 7.5 %collective-permute-start.17 = (bf16[896,128]{1,0:T(8,128)(2,1)S(1)}, bf16[896,128]{1,0:T(8,128)(2,1)S(1)}, u32[]{:S(2)}, u32[]{:S(2)}) collective-permute-start(bf16[896,128]{1,0:T(8,128)(2,1)S(1)} %shard_map.56.refs_1_), channel_id=1, source_target_pairs={{0,2},{2,0},{1,3},{3,1},{4,6},{6,4},{5,7},{7,5},{8,10},{10,8},{9,1... | collective-permute-start | bytes 688136 | tf_op jit(solution)/shard_map/ppermute | solution.py:22
  77.7 9.7 %collective-permute-start.7 = (f32[2,256]{1,0:T(2,128)S(1)}, f32[2,256]{1,0:T(2,128)S(1)}, u32[]{:S(2)}, u32[]{:S(2)}) collective-permute-start(f32[2,256]{1,0:T(2,128)S(1)} %shard_map.48.refs_3_.refs_1_), channel_id=1, source_target_pairs={{0,4},{4,0},{8,12},{12,8},{1,5},{5,1},{9,13},{13,9},{2,6},{6,2},{1... | collective-permute-start | bytes 6152 | tf_op jit(solution)/shard_map/ppermute | solution.py:22
  82.5 2.5 %collective-permute-start.12 = (bf16[128,2048]{1,0:T(8,128)(2,1)S(1)}, bf16[128,2048]{1,0:T(8,128)(2,1)S(1)}, u32[]{:S(2)}, u32[]{:S(2)}) collective-permute-start(bf16[128,2048]{1,0:T(8,128)(2,1)S(1)} %shard_map.51.refs_0_), channel_id=1, source_target_pairs={{0,1},{1,0},{2,3},{3,2},{4,5},{5,4},{6,7},{7,6},{8,9},{9,8},{10,11... | collective-permute-start | bytes 1572872 | tf_op jit(solution)/shard_map/ppermute | solution.py:22
  84.6 4.6 %collective-permute-start.18 = (f32[2,256]{1,0:T(2,128)S(1)}, f32[2,256]{1,0:T(2,128)S(1)}, u32[]{:S(2)}, u32[]{:S(2)}) collective-permute-start(f32[2,256]{1,0:T(2,128)S(1)} %shard_map.57), channel_id=1, source_target_pairs={{0,8},{4,12},{8,0},{12,4},{1,9},{5,13},{9,1},{13,5},{2,10},{6,14},... | collective-permute-start | bytes 6152 | tf_op jit(solution)/shard_map/ppermute | solution.py:22
  85.4 5.4 %collective-permute-start.13 = (f32[2,256]{1,0:T(2,128)S(1)}, f32[2,256]{1,0:T(2,128)S(1)}, u32[]{:S(2)}, u32[]{:S(2)}) collective-permute-start(f32[2,256]{1,0:T(2,128)S(1)} %shard_map.52), channel_id=1, source_target_pairs={{0,12},{4,8},{8,4},{12,0},{1,13},{5,9},{9,5},{13,1},{2,14},{6,10},... | collective-permute-start | bytes 6152 | tf_op jit(solution)/shard_map/ppermute | solution.py:22
  90.8 1.2 %collective-permute-start.19 = (f32[2,256]{1,0:T(2,128)S(1)}, f32[2,256]{1,0:T(2,128)S(1)}, u32[]{:S(2)}, u32[]{:S(2)}) collective-permute-start(f32[2,256]{1,0:T(2,128)S(1)} %add_add_fusion), channel_id=1, source_target_pairs={{0,1},{1,0},{2,3},{3,2},{4,5},{5,4},{6,7},{7,6},{8,9},{9,8},{10,11... | collective-permute-start | bytes 6152 | tf_op jit(solution)/shard_map/ppermute | solution.py:22
  92.0 3.6 %collective-permute-start.20 = (f32[2,256]{1,0:T(2,128)S(1)}, f32[2,256]{1,0:T(2,128)S(1)}, u32[]{:S(2)}, u32[]{:S(2)}) collective-permute-start(f32[2,256]{1,0:T(2,128)S(1)} %add.18), channel_id=1, source_target_pairs={{0,2},{2,0},{1,3},{3,1},{4,6},{6,4},{5,7},{7,5},{8,10},{10,8},{9,1... | collective-permute-start | bytes 6152 | tf_op jit(solution)/shard_map/ppermute | solution.py:22

commit v17 on v16

--- a/solution.py
+++ b/solution.py
@@ -9,7 +9,7 @@
 from jax.sharding import PartitionSpec as P
 
 
-LONG, SHORT = 14_000_000_000, 1_000_000
+LONG, MIDDLE, SHORT = 14_000_000_000, 8_000_000_000, 1_000_000
 
 
 def trade(block, steps, backwards=False):
@@ -125,7 +125,7 @@
             out_ref[...] = block[...]
 
 
-def from_partner(hops, d, count, tokens=()):
+def from_partner(hops, d, count, tokens=(), flops=1024):
     sources, choice = [], []
     for z in range(count):
         away = z - (z ^ d)
@@ -135,7 +135,7 @@
         choice.append(sources.index(source))
     blocks = [hops[step][way] for step, way in sources]
     outs = [(blocks[0].shape, blocks[0].dtype)]
-    return call(functools.partial(pick_kernel, choice), blocks, outs, tokens=tokens)[0]
+    return call(functools.partial(pick_kernel, choice), blocks, outs, flops, tokens)[0]
 
 
 def joined(parts, axis):
@@ -283,18 +283,18 @@
     arrived = {d: trade(block, {"dp": d}) for d, block in zip(early, sent)}
 
     mix, token = mixed([own_acts], queries, SHORT)
-    arrived[far] = trade(hold([far_grads], [token])[0], {"dp": far})
     scores = scores_of_grads([own], mix)
     hops[1] = hold(list(hops[1]), [token])
     for step in range(2, count - 1):
         hops.append(pass_on(hops[-1], step, count))
+    arrived[far] = trade(hold([far_grads], hops[1])[0], {"dp": far})
 
     mixes, token = {}, scores
     for d in early:
         mixes[d], token = mixed(acts_of(from_partner(hops, d, count)), queries, SHORT, [token])
     tail = [trade(hold([block], [token])[0], {"dp": late}) for block in sent[len(early) :]]
     sides = to_columns(hold([arrived[far]], [token])[0])
-    block = from_partner(hops, late, count, [token])
+    block = from_partner(hops, late, count, [token], MIDDLE)
     end = lax.ppermute(block, "dp", [(1, 0), (count - 2, count - 1)])
     hops.append((end, end))
 
@@ -307,7 +307,7 @@
 
     mix, done = mixed(acts_of(block), queries, SHORT, [token])
     tail = [to_columns(hold([piece], [done if p else token], LONG)[0]) for p, piece in enumerate(tail)]
-    block = from_partner(hops, far, count, [done])
+    block = from_partner(hops, far, count, [done], MIDDLE)
     terms.append(trade(scores_of_acts(*acts_of(block), proj), {"dp": far}))
     terms.append(trade(scores_of_grads([list(sides) for sides in zip(*tail)], mix, (), LONG), {"dp": late}))
     return over_chips(sum(terms, scores), spread)

time: 96.4 us -> 114 us (1.18)
  waiting for transfers between devices: 36.9 us -> 53.8 us
    ppermute x16, waiting for transfers between devices: 21.3 us -> 50.8 us  [trade(): return lax.ppermute(block, axes, route[::-1] if backwards else route)]
    ppermute x2, waiting for transfers between devices: 10.9 us -> 3.02 us  [pass_on(): lax.ppermute(block[1], 'dp', [(i, i - 1) for i in range(1, count - step +...]
    ppermute x1, waiting for transfers between devices: 4.69 us -> 0.01 us  [on_device(): end = lax.ppermute(block, 'dp', [(1, 0), (count - 2, count - 1)])]
  transfers between devices with their start and end apart: 21 -> 21, of which waited for: 10 -> 8; matrix products, arithmetic and copies ran while one was open for 0% -> 0% of each run, Pallas kernels for 29% -> 24%
where the time goes in v17:
time: 114 us
  waiting for transfers between devices  53.8 us (47%)
  starting transfers between devices  30.9 us (27%)
  Pallas kernels  28.6 us (25%)
    ppermute x16, waiting for transfers between devices, trade(): return lax.ppermute(block, axes, route[::-1] if backwards else route)  50.8 us
    ppermute x16, starting transfers between devices, trade(): return lax.ppermute(block, axes, route[::-1] if backwards else route)  21.4 us
    pallas_call x11, Pallas kernels, call(): pl.pallas_call(body, in_specs=[NEAR] * len(arrays) + [ANYWHERE] * skip, o...  21.2 us
    pallas_call x2, Pallas kernels, fetch(): pl.pallas_call(kernel, in_specs=[ANYWHERE] * len(arrays), out_specs=[NEAR...  7.33 us
    ppermute x2, starting transfers between devices, pass_on(): lax.ppermute(block[0], 'dp', [(i, i + 1) for i in range(step - 1, count -...  5.65 us
    ppermute x2, waiting for transfers between devices, pass_on(): lax.ppermute(block[1], 'dp', [(i, i - 1) for i in range(1, count - step +...  3.02 us
    ppermute x2, starting transfers between devices, pass_on(): lax.ppermute(block[1], 'dp', [(i, i - 1) for i in range(1, count - step +...  2.58 us
  transfers between devices with their start and end apart: 21, of which 8 were waited for; matrix products, arithmetic and copies ran while one was open for 0% of the time, Pallas kernels for 24%

profile of v17, /device:TPU:0, one launch (start us, length us, event | category | flops | bytes accessed | tf_op | source)
XLA Modules:
  0.0 114.1 jit_solution(5148402776232664726)
XLA Ops:
  0.0 1.0 shard_map.40
  1.1 5.0 %collective-permute-start.1 = (bf16[128,2048]{1,0:T(8,128)(2,1)S(1)}, bf16[128,2048]{1,0:T(8,128)(2,1)S(1)}, u32[]{:S(2)}, u32[]{:S(2)}) collective-permute-start(bf16[128,2048]{1,0:T(8,128)(2,1)S(1)} %shard_map.40), channel_id=1, source_target_pairs={{0,4},{4,8},{8,12},{1,5},{5,9},{9,13},{2,6},{6,10},{10,14},{3,7},{... | collective-permute-start | bytes 1572872 | tf_op jit(solution)/shard_map/ppermute | solution.py:26
  6.0 1.3 %collective-permute-start.2 = (bf16[128,2048]{1,0:T(8,128)(2,1)S(1)}, bf16[128,2048]{1,0:T(8,128)(2,1)S(1)}, u32[]{:S(2)}, u32[]{:S(2)}) collective-permute-start(bf16[128,2048]{1,0:T(8,128)(2,1)S(1)} %shard_map.40), channel_id=1, source_target_pairs={{4,0},{8,4},{12,8},{5,1},{9,5},{13,9},{6,2},{10,6},{14,10},{7,3},{... | collective-permute-start | bytes 1572872 | tf_op jit(solution)/shard_map/ppermute | solution.py:27
  7.3 6.3 %shard_map.37 = (bf16[2,1,1792,2048]{3,2,1,0:T(8,128)(2,1)S(1)}, bf16[256,2048]{1,0:T(8,128)(2,1)S(1)}, bf16[128,1792]{1,0:T(8,128)(2,1)S(1)}, bf16[1792,256]{1,...) custom-call(bf16[256,2048]{1,0:T(8,128)(2,1)} %acts_ref.3, ...), custom_call_target="tpu_custom_call" | custom-call | flops 1024 | bytes 1024 | tf_op jit(solution)/shard_map/pallas_call | solution.py:53
  13.6 4.7 %shard_map.38 = (f32[2,1792,256]{2,1,0:T(8,128)S(1)}, f32[8,128]{1,0:T(8,128)S(1)}) custom-call(bf16[256,2048]{1,0:T(8,128)(2,1)S(1)} %get-tuple-element.23.refs_0_, bf16[2,1,1792,2048]{3,2,1,0:T(8,128)(2,1)S(1)} %get-tuple-element.24.refs_1_.refs_2_), custom_call_target="tpu_custom_call" | custom-call | flops 1000000 | bytes 1024 | tf_op jit(solution)/shard_map/pallas_call | solution.py:41
  18.3 3.0 %collective-permute-done.2.refs_1_ = bf16[128,2048]{1,0:T(8,128)(2,1)S(1)} collective-permute-done((bf16[128,2048]{1,0:T(8,128)(2,1)S(1)}, bf16[128,2048]{1,0:T(8,128)(2,1)S(1)}, u32[]{:S(2)}, u32[]{:S(2)}) %collective-permute-start.2) | collective-permute-done | bytes 524320 | tf_op jit(solution)/shard_map/ppermute | solution.py:27
  21.4 1.3 %collective-permute-start.8 = (bf16[128,2048]{1,0:T(8,128)(2,1)S(1)}, bf16[128,2048]{1,0:T(8,128)(2,1)S(1)}, u32[]{:S(2)}, u32[]{:S(2)}) collective-permute-start(bf16[128,2048]{1,0:T(8,128)(2,1)S(1)} %get-tuple-element.29.refs_2_.refs_0_.refs_1_), channel_id=1, source_target_pairs={{4,0},{8,4},{5,1},{9,5},{6,2},{10,6},{7,3},{11,7},{20,16},{24,20},... | collective-permute-start | bytes 1572872 | tf_op jit(solution)/shard_map/ppermute | solution.py:27
  22.7 0.7 collective-permute-start.9
  23.4 5.5 %collective-permute-start = (bf16[1792,128]{1,0:T(8,128)(2,1)S(1)}, bf16[1792,128]{1,0:T(8,128)(2,1)S(1)}, u32[]{:S(2)}, u32[]{:S(2)}) collective-permute-start(bf16[1792,128]{1,0:T(8,128)(2,1)S(1)} %get-tuple-element.26), channel_id=1, source_target_pairs={{0,4},{4,0},{8,12},{12,8},{1,5},{5,1},{9,13},{13,9},{2,6},{6,2},{1... | collective-permute-start | bytes 1376264 | tf_op jit(solution)/shard_map/ppermute | solution.py:22
  29.0 0.9 collective-permute-start.5
  30.3 27.0 %collective-permute-done.refs_0_ = bf16[1792,128]{1,0:T(8,128)(2,1)S(1)} collective-permute-done((bf16[1792,128]{1,0:T(8,128)(2,1)S(1)}, bf16[1792,128]{1,0:T(8,128)(2,1)S(1)}, u32[]{:S(2)}, u32[]{:S(2)}) %collective-permute-start) | collective-permute-done | bytes 458784 | tf_op jit(solution)/shard_map/ppermute | solution.py:22
  57.3 1.5 %collective-permute-start.3 = (bf16[1792,128]{1,0:T(8,128)(2,1)S(1)}, bf16[1792,128]{1,0:T(8,128)(2,1)S(1)}, u32[]{:S(2)}, u32[]{:S(2)}) collective-permute-start(bf16[1792,128]{1,0:T(8,128)(2,1)S(1)} %shard_map.42.refs_0_), channel_id=1, source_target_pairs={{0,2},{2,0},{1,3},{3,1},{4,6},{6,4},{5,7},{7,5},{8,10},{10,8},{9,1... | collective-permute-start | bytes 1376264 | tf_op jit(solution)/shard_map/ppermute | solution.py:22
  58.8 4.7 %shard_map.44 = (f32[2,1792,256]{2,1,0:T(8,128)S(1)}, f32[8,128]{1,0:T(8,128)S(1)}) custom-call(bf16[128,2048]{1,0:T(8,128)(2,1)S(1)} %shard_map.43.refs_0_, bf16[128,2048]{1,0:T(8,128)(2,1)S(1)} %collective-permute-done.4.refs_1_, bf16[2,1,1792,2048]{3,2,1,0:T(8,128)(2,1)S(1)} %get-tuple-element.24.refs_1_.refs_2_, f32[2,256]{1,0:T(2,128)S(1)} %shard_map.39.refs_3_), custom_call_target="tpu_custom_call" | custom-call | flops 1000000 | bytes 1024 | tf_op jit(solution)/shard_map/pallas_call | solution.py:41
  63.5 2.5 %collective-permute-start.14 = (bf16[896,128]{1,0:T(8,128)(2,1)S(1)}, bf16[896,128]{1,0:T(8,128)(2,1)S(1)}, u32[]{:S(2)}, u32[]{:S(2)}) collective-permute-start(bf16[896,128]{1,0:T(8,128)(2,1)S(1)} %shard_map.53), channel_id=1, source_target_pairs={{0,8},{4,12},{8,0},{12,4},{1,9},{5,13},{9,1},{13,5},{2,10},{6,14},... | collective-permute-start | bytes 688136 | tf_op jit(solution)/shard_map/ppermute | solution.py:22
  66.0 0.5 collective-permute-start.6
  66.7 1.3 %collective-permute-start.10 = (bf16[128,2048]{1,0:T(8,128)(2,1)S(1)}, bf16[128,2048]{1,0:T(8,128)(2,1)S(1)}, u32[]{:S(2)}, u32[]{:S(2)}) collective-permute-start(bf16[128,2048]{1,0:T(8,128)(2,1)S(1)} %shard_map.49.refs_0_), channel_id=1, source_target_pairs={{4,0},{8,12},{5,1},{9,13},{6,2},{10,14},{7,3},{11,15},{20,16},{24,... | collective-permute-start | bytes 1572872 | tf_op jit(solution)/shard_map/ppermute | solution.py:298
  68.0 11.2 %collective-permute-done.6.refs_1_ = bf16[128,1792]{1,0:T(8,128)(2,1)S(1)} collective-permute-done((bf16[128,1792]{1,0:T(8,128)(2,1)S(1)}, bf16[128,1792]{1,0:T(8,128)(2,1)S(1)}, u32[]{:S(2)}, u32[]{:S(2)}) %collective-permute-start.6) | collective-permute-done | bytes 458784 | tf_op jit(solution)/shard_map/ppermute | solution.py:22
  79.3 2.5 %collective-permute-start.15 = (bf16[896,128]{1,0:T(8,128)(2,1)S(1)}, bf16[896,128]{1,0:T(8,128)(2,1)S(1)}, u32[]{:S(2)}, u32[]{:S(2)}) collective-permute-start(bf16[896,128]{1,0:T(8,128)(2,1)S(1)} %shard_map.55), channel_id=1, source_target_pairs={{0,8},{4,12},{8,0},{12,4},{1,9},{5,13},{9,1},{13,5},{2,10},{6,14},... | collective-permute-start | bytes 688136 | tf_op jit(solution)/shard_map/ppermute | solution.py:22
  81.7 4.8 %shard_map.47 = (f32[2,256,2048]{2,1,0:T(8,128)S(1)}, f32[8,128]{1,0:T(8,128)S(1)}) custom-call(bf16[128,1792]{1,0:T(8,128)(2,1)S(1)} %shard_map.46.refs_0_, bf16[128,1792]{1,0:T(8,128)(2,1)S(1)} %collective-permute-done.6.refs_1_, bf16[2,1,1792,2048]{3,2,1,0:T(8,128)(2,1)S(1)} %get-tuple-element.24.refs_1_.refs_2_, ...), custom_call_target="tpu_custom_call" | custom-call | flops 1000000 | bytes 1024 | tf_op jit(solution)/shard_map/pallas_call | solution.py:41
  86.5 0.8 shard_map.48.refs_3_.refs_1_
  87.3 2.5 %collective-permute-start.7 = (f32[2,256]{1,0:T(2,128)S(1)}, f32[2,256]{1,0:T(2,128)S(1)}, u32[]{:S(2)}, u32[]{:S(2)}) collective-permute-start(f32[2,256]{1,0:T(2,128)S(1)} %shard_map.48.refs_3_.refs_1_), channel_id=1, source_target_pairs={{0,4},{4,0},{8,12},{12,8},{1,5},{5,1},{9,13},{13,9},{2,6},{6,2},{1... | collective-permute-start | bytes 6152 | tf_op jit(solution)/shard_map/ppermute | solution.py:22
  89.8 1.5 %collective-permute-start.16 = (bf16[896,128]{1,0:T(8,128)(2,1)S(1)}, bf16[896,128]{1,0:T(8,128)(2,1)S(1)}, u32[]{:S(2)}, u32[]{:S(2)}) collective-permute-start(bf16[896,128]{1,0:T(8,128)(2,1)S(1)} %shard_map.54.refs_0_), channel_id=1, source_target_pairs={{0,2},{2,0},{1,3},{3,1},{4,6},{6,4},{5,7},{7,5},{8,10},{10,8},{9,1... | collective-permute-start | bytes 688136 | tf_op jit(solution)/shard_map/ppermute | solution.py:22
  91.3 4.7 %shard_map.50 = (f32[2,1792,256]{2,1,0:T(8,128)S(1)}, f32[8,128]{1,0:T(8,128)S(1)}) custom-call(bf16[128,2048]{1,0:T(8,128)(2,1)S(1)} %shard_map.49.refs_0_, bf16[128,2048]{1,0:T(8,128)(2,1)S(1)} %collective-permute-done.11.refs_1_, bf16[2,1,1792,2048]{3,2,1,0:T(8,128)(2,1)S(1)} %get-tuple-element.24.refs_1_.refs_2_, f32[2,256]{1,0:T(2,128)S(1)} %shard_map.48.refs_3_.refs_1_), custom_call_target="tpu_custom_call" | custom-call | flops 1000000 | bytes 1024 | tf_op jit(solution)/shard_map/pallas_call | solution.py:41
  96.0 0.6 collective-permute-start.17
  96.7 5.3 %collective-permute-done.17.refs_3_ = bf16[896,128]{1,0:T(8,128)(2,1)S(1)} collective-permute-done((bf16[896,128]{1,0:T(8,128)(2,1)S(1)}, bf16[896,128]{1,0:T(8,128)(2,1)S(1)}, u32[]{:S(2)}, u32[]{:S(2)}) %collective-permute-start.17) | collective-permute-done | bytes 229408 | tf_op jit(solution)/shard_map/ppermute | solution.py:22
  102.1 0.7 shard_map.57
  103.3 2.5 %collective-permute-start.13 = (f32[2,256]{1,0:T(2,128)S(1)}, f32[2,256]{1,0:T(2,128)S(1)}, u32[]{:S(2)}, u32[]{:S(2)}) collective-permute-start(f32[2,256]{1,0:T(2,128)S(1)} %shard_map.52), channel_id=1, source_target_pairs={{0,12},{4,8},{8,4},{12,0},{1,13},{5,9},{9,5},{13,1},{2,14},{6,10},... | collective-permute-start | bytes 6152 | tf_op jit(solution)/shard_map/ppermute | solution.py:22
  105.8 1.5 %collective-permute-done.18 = f32[2,256]{1,0:T(2,128)S(1)} collective-permute-done((f32[2,256]{1,0:T(2,128)S(1)}, f32[2,256]{1,0:T(2,128)S(1)}, u32[]{:S(2)}, u32[]{:S(2)}) %collective-permute-start.18) | collective-permute-done | bytes 2080 | tf_op jit(solution)/shard_map/ppermute | solution.py:22
  107.4 1.4 %collective-permute-done.13 = f32[2,256]{1,0:T(2,128)S(1)} collective-permute-done((f32[2,256]{1,0:T(2,128)S(1)}, f32[2,256]{1,0:T(2,128)S(1)}, u32[]{:S(2)}, u32[]{:S(2)}) %collective-permute-start.13) | collective-permute-done | bytes 2080 | tf_op jit(solution)/shard_map/ppermute | solution.py:22
  108.8 1.2 %collective-permute-done.19 = f32[2,256]{1,0:T(2,128)S(1)} collective-permute-done((f32[2,256]{1,0:T(2,128)S(1)}, f32[2,256]{1,0:T(2,128)S(1)}, u32[]{:S(2)}, u32[]{:S(2)}) %collective-permute-start.19) | collective-permute-done | bytes 2080 | tf_op jit(solution)/shard_map/ppermute | solution.py:22
  110.5 3.0 %collective-permute-done.20 = f32[2,256]{1,0:T(2,128)S(1)} collective-permute-done((f32[2,256]{1,0:T(2,128)S(1)}, f32[2,256]{1,0:T(2,128)S(1)}, u32[]{:S(2)}, u32[]{:S(2)}) %collective-permute-start.20) | collective-permute-done | bytes 2080 | tf_op jit(solution)/shard_map/ppermute | solution.py:22
  113.5 0.6 add.19
  (34 shorter events, 1.9 us)
Async XLA Ops:
  1.1 17.2 %collective-permute-start.1 = (bf16[128,2048]{1,0:T(8,128)(2,1)S(1)}, bf16[128,2048]{1,0:T(8,128)(2,1)S(1)}, u32[]{:S(2)}, u32[]{:S(2)}) collective-permute-start(bf16[128,2048]{1,0:T(8,128)(2,1)S(1)} %shard_map.40), channel_id=1, source_target_pairs={{0,4},{4,8},{8,12},{1,5},{5,9},{9,13},{2,6},{6,10},{10,14},{3,7},{... | collective-permute-start | bytes 1572872 | tf_op jit(solution)/shard_map/ppermute | solution.py:26
  6.0 15.3 %collective-permute-start.2 = (bf16[128,2048]{1,0:T(8,128)(2,1)S(1)}, bf16[128,2048]{1,0:T(8,128)(2,1)S(1)}, u32[]{:S(2)}, u32[]{:S(2)}) collective-permute-start(bf16[128,2048]{1,0:T(8,128)(2,1)S(1)} %shard_map.40), channel_id=1, source_target_pairs={{4,0},{8,4},{12,8},{5,1},{9,5},{13,9},{6,2},{10,6},{14,10},{7,3},{... | collective-permute-start | bytes 1572872 | tf_op jit(solution)/shard_map/ppermute | solution.py:27
  21.3 37.4 %collective-permute-start.4 = (bf16[128,2048]{1,0:T(8,128)(2,1)S(1)}, bf16[128,2048]{1,0:T(8,128)(2,1)S(1)}, u32[]{:S(2)}, u32[]{:S(2)}) collective-permute-start(bf16[128,2048]{1,0:T(8,128)(2,1)S(1)} %shard_map.43.refs_0_), channel_id=1, source_target_pairs={{0,1},{1,0},{2,3},{3,2},{4,5},{5,4},{6,7},{7,6},{8,9},{9,8},{10,11... | collective-permute-start | bytes 1572872 | tf_op jit(solution)/shard_map/ppermute | solution.py:22
  21.4 45.1 %collective-permute-start.8 = (bf16[128,2048]{1,0:T(8,128)(2,1)S(1)}, bf16[128,2048]{1,0:T(8,128)(2,1)S(1)}, u32[]{:S(2)}, u32[]{:S(2)}) collective-permute-start(bf16[128,2048]{1,0:T(8,128)(2,1)S(1)} %get-tuple-element.29.refs_2_.refs_0_.refs_1_), channel_id=1, source_target_pairs={{4,0},{8,4},{5,1},{9,5},{6,2},{10,6},{7,3},{11,7},{20,16},{24,20},... | collective-permute-start | bytes 1572872 | tf_op jit(solution)/shard_map/ppermute | solution.py:27
  22.7 43.8 %collective-permute-start.9 = (bf16[128,2048]{1,0:T(8,128)(2,1)S(1)}, bf16[128,2048]{1,0:T(8,128)(2,1)S(1)}, u32[]{:S(2)}, u32[]{:S(2)}) collective-permute-start(bf16[128,2048]{1,0:T(8,128)(2,1)S(1)} %get-tuple-element.28.refs_1_.refs_2_), channel_id=1, source_target_pairs={{4,8},{8,12},{5,9},{9,13},{6,10},{10,14},{7,11},{11,15},{20,24},{2... | collective-permute-start | bytes 1572872 | tf_op jit(solution)/shard_map/ppermute | solution.py:26
  23.4 33.9 %collective-permute-start = (bf16[1792,128]{1,0:T(8,128)(2,1)S(1)}, bf16[1792,128]{1,0:T(8,128)(2,1)S(1)}, u32[]{:S(2)}, u32[]{:S(2)}) collective-permute-start(bf16[1792,128]{1,0:T(8,128)(2,1)S(1)} %get-tuple-element.26), channel_id=1, source_target_pairs={{0,4},{4,0},{8,12},{12,8},{1,5},{5,1},{9,13},{13,9},{2,6},{6,2},{1... | collective-permute-start | bytes 1376264 | tf_op jit(solution)/shard_map/ppermute | solution.py:22
  29.0 37.1 %collective-permute-start.5 = (bf16[128,1792]{1,0:T(8,128)(2,1)S(1)}, bf16[128,1792]{1,0:T(8,128)(2,1)S(1)}, u32[]{:S(2)}, u32[]{:S(2)}) collective-permute-start(bf16[128,1792]{1,0:T(8,128)(2,1)S(1)} %shard_map.45), channel_id=1, source_target_pairs={{0,12},{4,8},{8,4},{12,0},{1,13},{5,9},{9,5},{13,1},{2,14},{6,10},... | collective-permute-start | bytes 1376264 | tf_op jit(solution)/shard_map/ppermute | solution.py:22
  57.3 29.2 %collective-permute-start.3 = (bf16[1792,128]{1,0:T(8,128)(2,1)S(1)}, bf16[1792,128]{1,0:T(8,128)(2,1)S(1)}, u32[]{:S(2)}, u32[]{:S(2)}) collective-permute-start(bf16[1792,128]{1,0:T(8,128)(2,1)S(1)} %shard_map.42.refs_0_), channel_id=1, source_target_pairs={{0,2},{2,0},{1,3},{3,1},{4,6},{6,4},{5,7},{7,5},{8,10},{10,8},{9,1... | collective-permute-start | bytes 1376264 | tf_op jit(solution)/shard_map/ppermute | solution.py:22
  63.5 26.3 %collective-permute-start.14 = (bf16[896,128]{1,0:T(8,128)(2,1)S(1)}, bf16[896,128]{1,0:T(8,128)(2,1)S(1)}, u32[]{:S(2)}, u32[]{:S(2)}) collective-permute-start(bf16[896,128]{1,0:T(8,128)(2,1)S(1)} %shard_map.53), channel_id=1, source_target_pairs={{0,8},{4,12},{8,0},{12,4},{1,9},{5,13},{9,1},{13,5},{2,10},{6,14},... | collective-permute-start | bytes 688136 | tf_op jit(solution)/shard_map/ppermute | solution.py:22
  66.0 13.2 %collective-permute-start.6 = (bf16[128,1792]{1,0:T(8,128)(2,1)S(1)}, bf16[128,1792]{1,0:T(8,128)(2,1)S(1)}, u32[]{:S(2)}, u32[]{:S(2)}) collective-permute-start(bf16[128,1792]{1,0:T(8,128)(2,1)S(1)} %shard_map.46.refs_0_), channel_id=1, source_target_pairs={{0,2},{2,0},{1,3},{3,1},{4,6},{6,4},{5,7},{7,5},{8,10},{10,8},{9,1... | collective-permute-start | bytes 1376264 | tf_op jit(solution)/shard_map/ppermute | solution.py:22
  66.6 24.7 %collective-permute-start.11 = (bf16[128,2048]{1,0:T(8,128)(2,1)S(1)}, bf16[128,2048]{1,0:T(8,128)(2,1)S(1)}, u32[]{:S(2)}, u32[]{:S(2)}) collective-permute-start(bf16[128,2048]{1,0:T(8,128)(2,1)S(1)} %shard_map.49.refs_0_), channel_id=1, source_target_pairs={{0,1},{1,0},{2,3},{3,2},{4,5},{5,4},{6,7},{7,6},{8,9},{9,8},{10,11... | collective-permute-start | bytes 1572872 | tf_op jit(solution)/shard_map/ppermute | solution.py:22
  66.7 29.9 %collective-permute-start.10 = (bf16[128,2048]{1,0:T(8,128)(2,1)S(1)}, bf16[128,2048]{1,0:T(8,128)(2,1)S(1)}, u32[]{:S(2)}, u32[]{:S(2)}) collective-permute-start(bf16[128,2048]{1,0:T(8,128)(2,1)S(1)} %shard_map.49.refs_0_), channel_id=1, source_target_pairs={{4,0},{8,12},{5,1},{9,13},{6,2},{10,14},{7,3},{11,15},{20,16},{24,... | collective-permute-start | bytes 1572872 | tf_op jit(solution)/shard_map/ppermute | solution.py:298
  79.3 16.7 %collective-permute-start.15 = (bf16[896,128]{1,0:T(8,128)(2,1)S(1)}, bf16[896,128]{1,0:T(8,128)(2,1)S(1)}, u32[]{:S(2)}, u32[]{:S(2)}) collective-permute-start(bf16[896,128]{1,0:T(8,128)(2,1)S(1)} %shard_map.55), channel_id=1, source_target_pairs={{0,8},{4,12},{8,0},{12,4},{1,9},{5,13},{9,1},{13,5},{2,10},{6,14},... | collective-permute-start | bytes 688136 | tf_op jit(solution)/shard_map/ppermute | solution.py:22
  87.3 18.6 %collective-permute-start.7 = (f32[2,256]{1,0:T(2,128)S(1)}, f32[2,256]{1,0:T(2,128)S(1)}, u32[]{:S(2)}, u32[]{:S(2)}) collective-permute-start(f32[2,256]{1,0:T(2,128)S(1)} %shard_map.48.refs_3_.refs_1_), channel_id=1, source_target_pairs={{0,4},{4,0},{8,12},{12,8},{1,5},{5,1},{9,13},{13,9},{2,6},{6,2},{1... | collective-permute-start | bytes 6152 | tf_op jit(solution)/shard_map/ppermute | solution.py:22
  89.8 6.9 %collective-permute-start.16 = (bf16[896,128]{1,0:T(8,128)(2,1)S(1)}, bf16[896,128]{1,0:T(8,128)(2,1)S(1)}, u32[]{:S(2)}, u32[]{:S(2)}) collective-permute-start(bf16[896,128]{1,0:T(8,128)(2,1)S(1)} %shard_map.54.refs_0_), channel_id=1, source_target_pairs={{0,2},{2,0},{1,3},{3,1},{4,6},{6,4},{5,7},{7,5},{8,10},{10,8},{9,1... | collective-permute-start | bytes 688136 | tf_op jit(solution)/shard_map/ppermute | solution.py:22
  96.0 6.1 %collective-permute-start.17 = (bf16[896,128]{1,0:T(8,128)(2,1)S(1)}, bf16[896,128]{1,0:T(8,128)(2,1)S(1)}, u32[]{:S(2)}, u32[]{:S(2)}) collective-permute-start(bf16[896,128]{1,0:T(8,128)(2,1)S(1)} %shard_map.56.refs_1_), channel_id=1, source_target_pairs={{0,2},{2,0},{1,3},{3,1},{4,6},{6,4},{5,7},{7,5},{8,10},{10,8},{9,1... | collective-permute-start | bytes 688136 | tf_op jit(solution)/shard_map/ppermute | solution.py:22
  96.7 6.2 %collective-permute-start.12 = (bf16[128,2048]{1,0:T(8,128)(2,1)S(1)}, bf16[128,2048]{1,0:T(8,128)(2,1)S(1)}, u32[]{:S(2)}, u32[]{:S(2)}) collective-permute-start(bf16[128,2048]{1,0:T(8,128)(2,1)S(1)} %shard_map.51.refs_0_), channel_id=1, source_target_pairs={{0,1},{1,0},{2,3},{3,2},{4,5},{5,4},{6,7},{7,6},{8,9},{9,8},{10,11... | collective-permute-start | bytes 1572872 | tf_op jit(solution)/shard_map/ppermute | solution.py:22
  102.8 4.5 %collective-permute-start.18 = (f32[2,256]{1,0:T(2,128)S(1)}, f32[2,256]{1,0:T(2,128)S(1)}, u32[]{:S(2)}, u32[]{:S(2)}) collective-permute-start(f32[2,256]{1,0:T(2,128)S(1)} %shard_map.57), channel_id=1, source_target_pairs={{0,8},{4,12},{8,0},{12,4},{1,9},{5,13},{9,1},{13,5},{2,10},{6,14},... | collective-permute-start | bytes 6152 | tf_op jit(solution)/shard_map/ppermute | solution.py:22
  103.3 5.4 %collective-permute-start.13 = (f32[2,256]{1,0:T(2,128)S(1)}, f32[2,256]{1,0:T(2,128)S(1)}, u32[]{:S(2)}, u32[]{:S(2)}) collective-permute-start(f32[2,256]{1,0:T(2,128)S(1)} %shard_map.52), channel_id=1, source_target_pairs={{0,12},{4,8},{8,4},{12,0},{1,13},{5,9},{9,5},{13,1},{2,14},{6,10},... | collective-permute-start | bytes 6152 | tf_op jit(solution)/shard_map/ppermute | solution.py:22
  108.8 1.2 %collective-permute-start.19 = (f32[2,256]{1,0:T(2,128)S(1)}, f32[2,256]{1,0:T(2,128)S(1)}, u32[]{:S(2)}, u32[]{:S(2)}) collective-permute-start(f32[2,256]{1,0:T(2,128)S(1)} %add_add_fusion), channel_id=1, source_target_pairs={{0,1},{1,0},{2,3},{3,2},{4,5},{5,4},{6,7},{7,6},{8,9},{9,8},{10,11... | collective-permute-start | bytes 6152 | tf_op jit(solution)/shard_map/ppermute | solution.py:22
  110.0 3.6 %collective-permute-start.20 = (f32[2,256]{1,0:T(2,128)S(1)}, f32[2,256]{1,0:T(2,128)S(1)}, u32[]{:S(2)}, u32[]{:S(2)}) collective-permute-start(f32[2,256]{1,0:T(2,128)S(1)} %add.18), channel_id=1, source_target_pairs={{0,2},{2,0},{1,3},{3,1},{4,6},{6,4},{5,7},{7,5},{8,10},{10,8},{9,1... | collective-permute-start | bytes 6152 | tf_op jit(solution)/shard_map/ppermute | solution.py:22

commit v18 on v14

--- a/solution.py
+++ b/solution.py
@@ -308,12 +308,11 @@
         token = scores_of_grads(sides, mixes[d], [token])
         terms.append(trade(token, {"dp": d}))
 
-    tail = [to_columns(hold([piece], [token], LONG)[0]) for piece in tail]
     mix, done = mixed(acts_of(block), queries, SHORT, [token])
+    tail = [to_columns(hold([piece], [done if p else token], LONG)[0]) for p, piece in enumerate(tail)]
     block = from_partner(hops, far, count, [done])
     terms.append(trade(scores_of_acts(*acts_of(block), proj), {"dp": far}))
-    sides = [list(hold(sides, [done])) for sides in zip(*tail)]
-    terms.append(trade(scores_of_grads(sides, mix, (), LONG), {"dp": late}))
+    terms.append(trade(scores_of_grads([list(sides) for sides in zip(*tail)], mix, (), LONG), {"dp": late}))
     return over_chips(sum(terms, scores), spread)
 
 

time: 94.6 us -> 92.8 us (0.981)
  waiting for transfers between devices: 36 us -> 33.9 us
    ppermute x16, waiting for transfers between devices: 35.2 us -> 28.5 us  [trade(): return lax.ppermute(block, axes, route[::-1] if backwards else route)]
    ppermute x1, waiting for transfers between devices: 0.01 us -> 4.69 us  [on_device(): end = lax.ppermute(block, 'dp', [(1, 0), (count - 2, count - 1)])]
  transfers between devices with their start and end apart: 21 -> 21, of which waited for: 9 -> 12; matrix products, arithmetic and copies ran while one was open for 0% -> 0% of each run, Pallas kernels for 29% -> 30%
where the time goes in v18:
time: 92.8 us; the launch traced here: 92.6 us
  waiting for transfers between devices  33.9 us (37%)
  starting transfers between devices  29.3 us (32%)
  Pallas kernels  28.5 us (31%)
    ppermute x16, waiting for transfers between devices, trade(): return lax.ppermute(block, axes, route[::-1] if backwards else route)  28.5 us
    pallas_call x11, Pallas kernels, call(): pl.pallas_call(body, in_specs=[NEAR] * len(arrays) + [ANYWHERE] * skip, o...  21.2 us
    ppermute x16, starting transfers between devices, trade(): return lax.ppermute(block, axes, route[::-1] if backwards else route)  19.8 us
    pallas_call x2, Pallas kernels, fetch(): pl.pallas_call(kernel, in_specs=[ANYWHERE] * len(arrays), out_specs=[NEAR...  7.3 us
    ppermute x2, starting transfers between devices, pass_on(): lax.ppermute(block[0], 'dp', [(i, i + 1) for i in range(step - 1, count -...  5.65 us
    ppermute x1, waiting for transfers between devices, on_device(): end = lax.ppermute(block, 'dp', [(1, 0), (count - 2, count - 1)])  4.69 us
    ppermute x2, starting transfers between devices, pass_on(): lax.ppermute(block[1], 'dp', [(i, i - 1) for i in range(1, count - step +...  2.58 us
  transfers between devices with their start and end apart: 21, of which 12 were waited for; matrix products, arithmetic and copies ran while one was open for 0% of the time, Pallas kernels for 30%

profile of v18, /device:TPU:0, one launch (start us, length us, event | category | flops | bytes accessed | tf_op | source)
XLA Modules:
  0.0 92.6 jit_solution(9221588121889407718)
XLA Ops:
  0.0 1.2 %shard_map.40 = (bf16[128,2048]{1,0:T(8,128)(2,1)S(1)}, bf16[128,1792]{1,0:T(8,128)(2,1)S(1)}) custom-call(bf16[256,2048]{1,0:T(8,128)(2,1)} %acts_ref.3, bf16[256,7168]{1,0:T(8,128)(2,1)} %grads_ref.3), custom_call_target="tpu_custom_call" | custom-call | flops 1024 | bytes 1024 | tf_op jit(solution)/shard_map/pallas_call | solution.py:53
  1.2 5.0 %collective-permute-start.1 = (bf16[128,2048]{1,0:T(8,128)(2,1)S(1)}, bf16[128,2048]{1,0:T(8,128)(2,1)S(1)}, u32[]{:S(2)}, u32[]{:S(2)}) collective-permute-start(bf16[128,2048]{1,0:T(8,128)(2,1)S(1)} %get-tuple-element.28), channel_id=1, source_target_pairs={{0,4},{4,8},{8,12},{1,5},{5,9},{9,13},{2,6},{6,10},{10,14},{3,7},{... | collective-permute-start | bytes 1572872 | tf_op jit(solution)/shard_map/ppermute | solution.py:26
  6.2 1.3 %collective-permute-start.2 = (bf16[128,2048]{1,0:T(8,128)(2,1)S(1)}, bf16[128,2048]{1,0:T(8,128)(2,1)S(1)}, u32[]{:S(2)}, u32[]{:S(2)}) collective-permute-start(bf16[128,2048]{1,0:T(8,128)(2,1)S(1)} %get-tuple-element.28), channel_id=1, source_target_pairs={{4,0},{8,4},{12,8},{5,1},{9,5},{13,9},{6,2},{10,6},{14,10},{7,3},{... | collective-permute-start | bytes 1572872 | tf_op jit(solution)/shard_map/ppermute | solution.py:27
  7.5 4.7 %collective-permute-start.5 = (bf16[128,1792]{1,0:T(8,128)(2,1)S(1)}, bf16[128,1792]{1,0:T(8,128)(2,1)S(1)}, u32[]{:S(2)}, u32[]{:S(2)}) collective-permute-start(bf16[128,1792]{1,0:T(8,128)(2,1)S(1)} %get-tuple-element.33), channel_id=1, source_target_pairs={{0,12},{4,8},{8,4},{12,0},{1,13},{5,9},{9,5},{13,1},{2,14},{6,10},... | collective-permute-start | bytes 1376264 | tf_op jit(solution)/shard_map/ppermute | solution.py:22
  12.2 6.1 %shard_map.37 = (bf16[2,1,1792,2048]{3,2,1,0:T(8,128)(2,1)S(1)}, bf16[256,2048]{1,0:T(8,128)(2,1)S(1)}, bf16[1792,256]{1,0:T(8,128)(2,1)S(1)}, bf16[1792,128]{1,...) custom-call(bf16[256,2048]{1,0:T(8,128)(2,1)} %acts_ref.3, bf16[256,7168]{1,0:T(8,128)(2,1)} %grads_ref.3, ...), custom_call_target="tpu_custom_call" | custom-call | flops 1024 | bytes 1024 | tf_op jit(solution)/shard_map/pallas_call | solution.py:53
  18.4 4.7 %shard_map.38 = (f32[2,1792,256]{2,1,0:T(8,128)S(1)}, f32[8,128]{1,0:T(8,128)S(1)}) custom-call(bf16[256,2048]{1,0:T(8,128)(2,1)S(1)} %get-tuple-element.24.refs_0_, bf16[2,1,1792,2048]{3,2,1,0:T(8,128)(2,1)S(1)} %get-tuple-element.25.refs_1_.refs_2_), custom_call_target="tpu_custom_call" | custom-call | flops 1000000 | bytes 1024 | tf_op jit(solution)/shard_map/pallas_call | solution.py:41
  23.1 0.8 collective-permute-done.2.refs_1_
  24.0 1.3 %collective-permute-start.8 = (bf16[128,2048]{1,0:T(8,128)(2,1)S(1)}, bf16[128,2048]{1,0:T(8,128)(2,1)S(1)}, u32[]{:S(2)}, u32[]{:S(2)}) collective-permute-start(bf16[128,2048]{1,0:T(8,128)(2,1)S(1)} %get-tuple-element.31.refs_2_.refs_0_.refs_1_), channel_id=1, source_target_pairs={{4,0},{8,4},{5,1},{9,5},{6,2},{10,6},{7,3},{11,7},{20,16},{24,20},... | collective-permute-start | bytes 1572872 | tf_op jit(solution)/shard_map/ppermute | solution.py:27
  25.3 0.7 collective-permute-start.9
  26.0 8.8 %collective-permute-done.5.refs_0_ = bf16[128,1792]{1,0:T(8,128)(2,1)S(1)} collective-permute-done((bf16[128,1792]{1,0:T(8,128)(2,1)S(1)}, bf16[128,1792]{1,0:T(8,128)(2,1)S(1)}, u32[]{:S(2)}, u32[]{:S(2)}) %collective-permute-start.5) | collective-permute-done | bytes 458784 | tf_op jit(solution)/shard_map/ppermute | solution.py:22
  34.8 7.8 %collective-permute-done.refs_0_.refs_3_ = bf16[1792,128]{1,0:T(8,128)(2,1)S(1)} collective-permute-done((bf16[1792,128]{1,0:T(8,128)(2,1)S(1)}, bf16[1792,128]{1,0:T(8,128)(2,1)S(1)}, u32[]{:S(2)}, u32[]{:S(2)}) %collective-permute-start) | collective-permute-done | bytes 458784 | tf_op jit(solution)/shard_map/ppermute | solution.py:22
  42.6 1.5 %collective-permute-start.6 = (bf16[128,1792]{1,0:T(8,128)(2,1)S(1)}, bf16[128,1792]{1,0:T(8,128)(2,1)S(1)}, u32[]{:S(2)}, u32[]{:S(2)}) collective-permute-start(bf16[128,1792]{1,0:T(8,128)(2,1)S(1)} %shard_map.45.refs_0_.refs_3_), channel_id=1, source_target_pairs={{0,2},{2,0},{1,3},{3,1},{4,6},{6,4},{5,7},{7,5},{8,10},{10,8},{9,1... | collective-permute-start | bytes 1376264 | tf_op jit(solution)/shard_map/ppermute | solution.py:22
  45.0 4.7 %shard_map.44 = (f32[2,1792,256]{2,1,0:T(8,128)S(1)}, f32[8,128]{1,0:T(8,128)S(1)}) custom-call(bf16[128,2048]{1,0:T(8,128)(2,1)S(1)} %shard_map.43.refs_0_, bf16[128,2048]{1,0:T(8,128)(2,1)S(1)} %collective-permute-done.4.refs_1_, bf16[2,1,1792,2048]{3,2,1,0:T(8,128)(2,1)S(1)} %get-tuple-element.25.refs_1_.refs_2_, f32[2,256]{1,0:T(2,128)S(1)} %shard_map.39.refs_3_), custom_call_target="tpu_custom_call" | custom-call | flops 1000000 | bytes 1024 | tf_op jit(solution)/shard_map/pallas_call | solution.py:41
  49.7 1.2 %collective-permute-start.14 = (bf16[896,128]{1,0:T(8,128)(2,1)S(1)}, bf16[896,128]{1,0:T(8,128)(2,1)S(1)}, u32[]{:S(2)}, u32[]{:S(2)}) collective-permute-start(bf16[896,128]{1,0:T(8,128)(2,1)S(1)} %shard_map.52), channel_id=1, source_target_pairs={{0,8},{4,12},{8,0},{12,4},{1,9},{5,13},{9,1},{13,5},{2,10},{6,14},... | collective-permute-start | bytes 688136 | tf_op jit(solution)/shard_map/ppermute | solution.py:22
  50.9 5.1 %collective-permute-done.6.refs_1_.refs_4_ = bf16[128,1792]{1,0:T(8,128)(2,1)S(1)} collective-permute-done((bf16[128,1792]{1,0:T(8,128)(2,1)S(1)}, bf16[128,1792]{1,0:T(8,128)(2,1)S(1)}, u32[]{:S(2)}, u32[]{:S(2)}) %collective-permute-start.6) | collective-permute-done | bytes 458784 | tf_op jit(solution)/shard_map/ppermute | solution.py:22
  56.2 1.3 %collective-permute-start.10 = (bf16[128,2048]{1,0:T(8,128)(2,1)S(1)}, bf16[128,2048]{1,0:T(8,128)(2,1)S(1)}, u32[]{:S(2)}, u32[]{:S(2)}) collective-permute-start(bf16[128,2048]{1,0:T(8,128)(2,1)S(1)} %shard_map.48.refs_0_), channel_id=1, source_target_pairs={{4,0},{8,12},{5,1},{9,13},{6,2},{10,14},{7,3},{11,15},{20,16},{24,... | collective-permute-start | bytes 1572872 | tf_op jit(solution)/shard_map/ppermute | solution.py:301
  57.5 3.3 %collective-permute-start.15 = (bf16[896,128]{1,0:T(8,128)(2,1)S(1)}, bf16[896,128]{1,0:T(8,128)(2,1)S(1)}, u32[]{:S(2)}, u32[]{:S(2)}) collective-permute-start(bf16[896,128]{1,0:T(8,128)(2,1)S(1)} %shard_map.54), channel_id=1, source_target_pairs={{0,8},{4,12},{8,0},{12,4},{1,9},{5,13},{9,1},{13,5},{2,10},{6,14},... | collective-permute-start | bytes 688136 | tf_op jit(solution)/shard_map/ppermute | solution.py:22
  60.8 4.8 %shard_map.46 = (f32[2,256,2048]{2,1,0:T(8,128)S(1)}, f32[8,128]{1,0:T(8,128)S(1)}) custom-call(bf16[128,1792]{1,0:T(8,128)(2,1)S(1)} %shard_map.45.refs_0_.refs_3_, bf16[128,1792]{1,0:T(8,128)(2,1)S(1)} %collective-permute-done.6.refs_1_.refs_4_, bf16[2,1,1792,2048]{3,2,1,0:T(8,128)(2,1)S(1)} %get-tuple-element.25.refs_1_.refs_2_, ...), custom_call_target="tpu_custom_call" | custom-call | flops 1000000 | bytes 1024 | tf_op jit(solution)/shard_map/pallas_call | solution.py:41
  65.6 0.8 shard_map.47.refs_3_.refs_1_
  66.3 1.6 %collective-permute-start.16 = (bf16[896,128]{1,0:T(8,128)(2,1)S(1)}, bf16[896,128]{1,0:T(8,128)(2,1)S(1)}, u32[]{:S(2)}, u32[]{:S(2)}) collective-permute-start(bf16[896,128]{1,0:T(8,128)(2,1)S(1)} %shard_map.53.refs_0_), channel_id=1, source_target_pairs={{0,2},{2,0},{1,3},{3,1},{4,6},{6,4},{5,7},{7,5},{8,10},{10,8},{9,1... | collective-permute-start | bytes 688136 | tf_op jit(solution)/shard_map/ppermute | solution.py:22
  67.9 4.7 %shard_map.49 = (f32[2,1792,256]{2,1,0:T(8,128)S(1)}, f32[8,128]{1,0:T(8,128)S(1)}) custom-call(bf16[128,2048]{1,0:T(8,128)(2,1)S(1)} %shard_map.48.refs_0_, bf16[128,2048]{1,0:T(8,128)(2,1)S(1)} %collective-permute-done.11.refs_1_, bf16[2,1,1792,2048]{3,2,1,0:T(8,128)(2,1)S(1)} %get-tuple-element.25.refs_1_.refs_2_, f32[2,256]{1,0:T(2,128)S(1)} %shard_map.47.refs_3_.refs_1_), custom_call_target="tpu_custom_call" | custom-call | flops 1000000 | bytes 1024 | tf_op jit(solution)/shard_map/pallas_call | solution.py:41
  72.6 0.6 collective-permute-done.15.refs_0_
  73.1 1.5 %collective-permute-start.17 = (bf16[896,128]{1,0:T(8,128)(2,1)S(1)}, bf16[896,128]{1,0:T(8,128)(2,1)S(1)}, u32[]{:S(2)}, u32[]{:S(2)}) collective-permute-start(bf16[896,128]{1,0:T(8,128)(2,1)S(1)} %shard_map.55.refs_1_), channel_id=1, source_target_pairs={{0,2},{2,0},{1,3},{3,1},{4,6},{6,4},{5,7},{7,5},{8,10},{10,8},{9,1... | collective-permute-start | bytes 688136 | tf_op jit(solution)/shard_map/ppermute | solution.py:22
  74.6 4.7 %collective-permute-done.10.refs_0_ = bf16[128,2048]{1,0:T(8,128)(2,1)S(1)} collective-permute-done((bf16[128,2048]{1,0:T(8,128)(2,1)S(1)}, bf16[128,2048]{1,0:T(8,128)(2,1)S(1)}, u32[]{:S(2)}, u32[]{:S(2)}) %collective-permute-start.10) | collective-permute-done | bytes 524320 | tf_op jit(solution)/shard_map/ppermute | solution.py:301
  79.5 0.6 collective-permute-done.17.refs_3_
  80.1 0.7 shard_map.56
  81.8 3.3 %collective-permute-start.13 = (f32[2,256]{1,0:T(2,128)S(1)}, f32[2,256]{1,0:T(2,128)S(1)}, u32[]{:S(2)}, u32[]{:S(2)}) collective-permute-start(f32[2,256]{1,0:T(2,128)S(1)} %shard_map.51), channel_id=1, source_target_pairs={{0,12},{4,8},{8,4},{12,0},{1,13},{5,9},{9,5},{13,1},{2,14},{6,10},... | collective-permute-start | bytes 6152 | tf_op jit(solution)/shard_map/ppermute | solution.py:22
  85.3 1.9 %collective-permute-done.13 = f32[2,256]{1,0:T(2,128)S(1)} collective-permute-done((f32[2,256]{1,0:T(2,128)S(1)}, f32[2,256]{1,0:T(2,128)S(1)}, u32[]{:S(2)}, u32[]{:S(2)}) %collective-permute-start.13) | collective-permute-done | bytes 2080 | tf_op jit(solution)/shard_map/ppermute | solution.py:22
  87.3 1.2 %collective-permute-done.19 = f32[2,256]{1,0:T(2,128)S(1)} collective-permute-done((f32[2,256]{1,0:T(2,128)S(1)}, f32[2,256]{1,0:T(2,128)S(1)}, u32[]{:S(2)}, u32[]{:S(2)}) %collective-permute-start.19) | collective-permute-done | bytes 2080 | tf_op jit(solution)/shard_map/ppermute | solution.py:22
  88.4 1.5 %collective-permute-start.20 = (f32[2,256]{1,0:T(2,128)S(1)}, f32[2,256]{1,0:T(2,128)S(1)}, u32[]{:S(2)}, u32[]{:S(2)}) collective-permute-start(f32[2,256]{1,0:T(2,128)S(1)} %add.18), channel_id=1, source_target_pairs={{0,2},{2,0},{1,3},{3,1},{4,6},{6,4},{5,7},{7,5},{8,10},{10,8},{9,1... | collective-permute-start | bytes 6152 | tf_op jit(solution)/shard_map/ppermute | solution.py:22
  89.9 2.1 %collective-permute-done.20 = f32[2,256]{1,0:T(2,128)S(1)} collective-permute-done((f32[2,256]{1,0:T(2,128)S(1)}, f32[2,256]{1,0:T(2,128)S(1)}, u32[]{:S(2)}, u32[]{:S(2)}) %collective-permute-start.20) | collective-permute-done | bytes 2080 | tf_op jit(solution)/shard_map/ppermute | solution.py:22
  92.0 0.6 add.19
  (33 shorter events, 2.7 us)
Async XLA Ops:
  1.2 21.9 %collective-permute-start.1 = (bf16[128,2048]{1,0:T(8,128)(2,1)S(1)}, bf16[128,2048]{1,0:T(8,128)(2,1)S(1)}, u32[]{:S(2)}, u32[]{:S(2)}) collective-permute-start(bf16[128,2048]{1,0:T(8,128)(2,1)S(1)} %get-tuple-element.28), channel_id=1, source_target_pairs={{0,4},{4,8},{8,12},{1,5},{5,9},{9,13},{2,6},{6,10},{10,14},{3,7},{... | collective-permute-start | bytes 1572872 | tf_op jit(solution)/shard_map/ppermute | solution.py:26
  6.2 17.7 %collective-permute-start.2 = (bf16[128,2048]{1,0:T(8,128)(2,1)S(1)}, bf16[128,2048]{1,0:T(8,128)(2,1)S(1)}, u32[]{:S(2)}, u32[]{:S(2)}) collective-permute-start(bf16[128,2048]{1,0:T(8,128)(2,1)S(1)} %get-tuple-element.28), channel_id=1, source_target_pairs={{4,0},{8,4},{12,8},{5,1},{9,5},{13,9},{6,2},{10,6},{14,10},{7,3},{... | collective-permute-start | bytes 1572872 | tf_op jit(solution)/shard_map/ppermute | solution.py:27
  7.5 27.3 %collective-permute-start.5 = (bf16[128,1792]{1,0:T(8,128)(2,1)S(1)}, bf16[128,1792]{1,0:T(8,128)(2,1)S(1)}, u32[]{:S(2)}, u32[]{:S(2)}) collective-permute-start(bf16[128,1792]{1,0:T(8,128)(2,1)S(1)} %get-tuple-element.33), channel_id=1, source_target_pairs={{0,12},{4,8},{8,4},{12,0},{1,13},{5,9},{9,5},{13,1},{2,14},{6,10},... | collective-permute-start | bytes 1376264 | tf_op jit(solution)/shard_map/ppermute | solution.py:22
  18.3 24.3 %collective-permute-start = (bf16[1792,128]{1,0:T(8,128)(2,1)S(1)}, bf16[1792,128]{1,0:T(8,128)(2,1)S(1)}, u32[]{:S(2)}, u32[]{:S(2)}) collective-permute-start(bf16[1792,128]{1,0:T(8,128)(2,1)S(1)} %get-tuple-element.27), channel_id=1, source_target_pairs={{0,4},{4,0},{8,12},{12,8},{1,5},{5,1},{9,13},{13,9},{2,6},{6,2},{1... | collective-permute-start | bytes 1376264 | tf_op jit(solution)/shard_map/ppermute | solution.py:22
  23.9 21.1 %collective-permute-start.4 = (bf16[128,2048]{1,0:T(8,128)(2,1)S(1)}, bf16[128,2048]{1,0:T(8,128)(2,1)S(1)}, u32[]{:S(2)}, u32[]{:S(2)}) collective-permute-start(bf16[128,2048]{1,0:T(8,128)(2,1)S(1)} %shard_map.43.refs_0_), channel_id=1, source_target_pairs={{0,1},{1,0},{2,3},{3,2},{4,5},{5,4},{6,7},{7,6},{8,9},{9,8},{10,11... | collective-permute-start | bytes 1572872 | tf_op jit(solution)/shard_map/ppermute | solution.py:22
  24.0 32.1 %collective-permute-start.8 = (bf16[128,2048]{1,0:T(8,128)(2,1)S(1)}, bf16[128,2048]{1,0:T(8,128)(2,1)S(1)}, u32[]{:S(2)}, u32[]{:S(2)}) collective-permute-start(bf16[128,2048]{1,0:T(8,128)(2,1)S(1)} %get-tuple-element.31.refs_2_.refs_0_.refs_1_), channel_id=1, source_target_pairs={{4,0},{8,4},{5,1},{9,5},{6,2},{10,6},{7,3},{11,7},{20,16},{24,20},... | collective-permute-start | bytes 1572872 | tf_op jit(solution)/shard_map/ppermute | solution.py:27
  25.3 30.8 %collective-permute-start.9 = (bf16[128,2048]{1,0:T(8,128)(2,1)S(1)}, bf16[128,2048]{1,0:T(8,128)(2,1)S(1)}, u32[]{:S(2)}, u32[]{:S(2)}) collective-permute-start(bf16[128,2048]{1,0:T(8,128)(2,1)S(1)} %get-tuple-element.30.refs_1_.refs_2_), channel_id=1, source_target_pairs={{4,8},{8,12},{5,9},{9,13},{6,10},{10,14},{7,11},{11,15},{20,24},{2... | collective-permute-start | bytes 1572872 | tf_op jit(solution)/shard_map/ppermute | solution.py:26
  42.6 13.5 %collective-permute-start.6 = (bf16[128,1792]{1,0:T(8,128)(2,1)S(1)}, bf16[128,1792]{1,0:T(8,128)(2,1)S(1)}, u32[]{:S(2)}, u32[]{:S(2)}) collective-permute-start(bf16[128,1792]{1,0:T(8,128)(2,1)S(1)} %shard_map.45.refs_0_.refs_3_), channel_id=1, source_target_pairs={{0,2},{2,0},{1,3},{3,1},{4,6},{6,4},{5,7},{7,5},{8,10},{10,8},{9,1... | collective-permute-start | bytes 1376264 | tf_op jit(solution)/shard_map/ppermute | solution.py:22
  44.1 21.5 %collective-permute-start.3 = (bf16[1792,128]{1,0:T(8,128)(2,1)S(1)}, bf16[1792,128]{1,0:T(8,128)(2,1)S(1)}, u32[]{:S(2)}, u32[]{:S(2)}) collective-permute-start(bf16[1792,128]{1,0:T(8,128)(2,1)S(1)} %shard_map.42.refs_0_), channel_id=1, source_target_pairs={{0,2},{2,0},{1,3},{3,1},{4,6},{6,4},{5,7},{7,5},{8,10},{10,8},{9,1... | collective-permute-start | bytes 1376264 | tf_op jit(solution)/shard_map/ppermute | solution.py:22
  49.7 16.6 %collective-permute-start.14 = (bf16[896,128]{1,0:T(8,128)(2,1)S(1)}, bf16[896,128]{1,0:T(8,128)(2,1)S(1)}, u32[]{:S(2)}, u32[]{:S(2)}) collective-permute-start(bf16[896,128]{1,0:T(8,128)(2,1)S(1)} %shard_map.52), channel_id=1, source_target_pairs={{0,8},{4,12},{8,0},{12,4},{1,9},{5,13},{9,1},{13,5},{2,10},{6,14},... | collective-permute-start | bytes 688136 | tf_op jit(solution)/shard_map/ppermute | solution.py:22
  56.1 11.8 %collective-permute-start.11 = (bf16[128,2048]{1,0:T(8,128)(2,1)S(1)}, bf16[128,2048]{1,0:T(8,128)(2,1)S(1)}, u32[]{:S(2)}, u32[]{:S(2)}) collective-permute-start(bf16[128,2048]{1,0:T(8,128)(2,1)S(1)} %shard_map.48.refs_0_), channel_id=1, source_target_pairs={{0,1},{1,0},{2,3},{3,2},{4,5},{5,4},{6,7},{7,6},{8,9},{9,8},{10,11... | collective-permute-start | bytes 1572872 | tf_op jit(solution)/shard_map/ppermute | solution.py:22
  56.2 23.2 %collective-permute-start.10 = (bf16[128,2048]{1,0:T(8,128)(2,1)S(1)}, bf16[128,2048]{1,0:T(8,128)(2,1)S(1)}, u32[]{:S(2)}, u32[]{:S(2)}) collective-permute-start(bf16[128,2048]{1,0:T(8,128)(2,1)S(1)} %shard_map.48.refs_0_), channel_id=1, source_target_pairs={{4,0},{8,12},{5,1},{9,13},{6,2},{10,14},{7,3},{11,15},{20,16},{24,... | collective-permute-start | bytes 1572872 | tf_op jit(solution)/shard_map/ppermute | solution.py:301
  57.5 15.7 %collective-permute-start.15 = (bf16[896,128]{1,0:T(8,128)(2,1)S(1)}, bf16[896,128]{1,0:T(8,128)(2,1)S(1)}, u32[]{:S(2)}, u32[]{:S(2)}) collective-permute-start(bf16[896,128]{1,0:T(8,128)(2,1)S(1)} %shard_map.54), channel_id=1, source_target_pairs={{0,8},{4,12},{8,0},{12,4},{1,9},{5,13},{9,1},{13,5},{2,10},{6,14},... | collective-permute-start | bytes 688136 | tf_op jit(solution)/shard_map/ppermute | solution.py:22
  66.3 13.2 %collective-permute-start.16 = (bf16[896,128]{1,0:T(8,128)(2,1)S(1)}, bf16[896,128]{1,0:T(8,128)(2,1)S(1)}, u32[]{:S(2)}, u32[]{:S(2)}) collective-permute-start(bf16[896,128]{1,0:T(8,128)(2,1)S(1)} %shard_map.53.refs_0_), channel_id=1, source_target_pairs={{0,2},{2,0},{1,3},{3,1},{4,6},{6,4},{5,7},{7,5},{8,10},{10,8},{9,1... | collective-permute-start | bytes 688136 | tf_op jit(solution)/shard_map/ppermute | solution.py:22
  73.1 6.9 %collective-permute-start.17 = (bf16[896,128]{1,0:T(8,128)(2,1)S(1)}, bf16[896,128]{1,0:T(8,128)(2,1)S(1)}, u32[]{:S(2)}, u32[]{:S(2)}) collective-permute-start(bf16[896,128]{1,0:T(8,128)(2,1)S(1)} %shard_map.55.refs_1_), channel_id=1, source_target_pairs={{0,2},{2,0},{1,3},{3,1},{4,6},{6,4},{5,7},{7,5},{8,10},{10,8},{9,1... | collective-permute-start | bytes 688136 | tf_op jit(solution)/shard_map/ppermute | solution.py:22
  74.6 10.5 %collective-permute-start.7 = (f32[2,256]{1,0:T(2,128)S(1)}, f32[2,256]{1,0:T(2,128)S(1)}, u32[]{:S(2)}, u32[]{:S(2)}) collective-permute-start(f32[2,256]{1,0:T(2,128)S(1)} %shard_map.47.refs_3_.refs_1_), channel_id=1, source_target_pairs={{0,4},{4,0},{8,12},{12,8},{1,5},{5,1},{9,13},{13,9},{2,6},{6,2},{1... | collective-permute-start | bytes 6152 | tf_op jit(solution)/shard_map/ppermute | solution.py:22
  79.4 2.0 %collective-permute-start.12 = (bf16[128,2048]{1,0:T(8,128)(2,1)S(1)}, bf16[128,2048]{1,0:T(8,128)(2,1)S(1)}, u32[]{:S(2)}, u32[]{:S(2)}) collective-permute-start(bf16[128,2048]{1,0:T(8,128)(2,1)S(1)} %shard_map.50.refs_0_), channel_id=1, source_target_pairs={{0,1},{1,0},{2,3},{3,2},{4,5},{5,4},{6,7},{7,6},{8,9},{9,8},{10,11... | collective-permute-start | bytes 1572872 | tf_op jit(solution)/shard_map/ppermute | solution.py:22
  80.8 4.5 %collective-permute-start.18 = (f32[2,256]{1,0:T(2,128)S(1)}, f32[2,256]{1,0:T(2,128)S(1)}, u32[]{:S(2)}, u32[]{:S(2)}) collective-permute-start(f32[2,256]{1,0:T(2,128)S(1)} %shard_map.56), channel_id=1, source_target_pairs={{0,8},{4,12},{8,0},{12,4},{1,9},{5,13},{9,1},{13,5},{2,10},{6,14},... | collective-permute-start | bytes 6152 | tf_op jit(solution)/shard_map/ppermute | solution.py:22
  81.8 5.4 %collective-permute-start.13 = (f32[2,256]{1,0:T(2,128)S(1)}, f32[2,256]{1,0:T(2,128)S(1)}, u32[]{:S(2)}, u32[]{:S(2)}) collective-permute-start(f32[2,256]{1,0:T(2,128)S(1)} %shard_map.51), channel_id=1, source_target_pairs={{0,12},{4,8},{8,4},{12,0},{1,13},{5,9},{9,5},{13,1},{2,14},{6,10},... | collective-permute-start | bytes 6152 | tf_op jit(solution)/shard_map/ppermute | solution.py:22
  87.3 1.2 %collective-permute-start.19 = (f32[2,256]{1,0:T(2,128)S(1)}, f32[2,256]{1,0:T(2,128)S(1)}, u32[]{:S(2)}, u32[]{:S(2)}) collective-permute-start(f32[2,256]{1,0:T(2,128)S(1)} %add_add_fusion), channel_id=1, source_target_pairs={{0,1},{1,0},{2,3},{3,2},{4,5},{5,4},{6,7},{7,6},{8,9},{9,8},{10,11... | collective-permute-start | bytes 6152 | tf_op jit(solution)/shard_map/ppermute | solution.py:22
  88.4 3.6 %collective-permute-start.20 = (f32[2,256]{1,0:T(2,128)S(1)}, f32[2,256]{1,0:T(2,128)S(1)}, u32[]{:S(2)}, u32[]{:S(2)}) collective-permute-start(f32[2,256]{1,0:T(2,128)S(1)} %add.18), channel_id=1, source_target_pairs={{0,2},{2,0},{1,3},{3,1},{4,6},{6,4},{5,7},{7,5},{8,10},{10,8},{9,1... | collective-permute-start | bytes 6152 | tf_op jit(solution)/shard_map/ppermute | solution.py:22

commit v19 on v17

--- a/solution.py
+++ b/solution.py
@@ -9,7 +9,7 @@
 from jax.sharding import PartitionSpec as P
 
 
-LONG, MIDDLE, SHORT = 14_000_000_000, 8_000_000_000, 1_000_000
+LONG, MIDDLE, SHORT = 14_000_000_000, 14_000_000_000, 1_000_000
 
 
 def trade(block, steps, backwards=False):
@@ -292,22 +292,23 @@
     mixes, token = {}, scores
     for d in early:
         mixes[d], token = mixed(acts_of(from_partner(hops, d, count)), queries, SHORT, [token])
-    tail = [trade(hold([block], [token])[0], {"dp": late}) for block in sent[len(early) :]]
-    sides = to_columns(hold([arrived[far]], [token])[0])
+    near = {d: to_columns(hold([arrived[d]], hops[1], LONG)[0]) for d in early}
     block = from_partner(hops, late, count, [token], MIDDLE)
     end = lax.ppermute(block, "dp", [(1, 0), (count - 2, count - 1)])
     hops.append((end, end))
-
-    proj, token = projected(sides, queries, SHORT, [token])
+    tail = [trade(hold([piece], [block])[0], {"dp": late}) for piece in sent[len(early) :]]
+    sides = to_columns(hold([arrived[far]], [block])[0])
+
     terms = []
     for d in early:
-        sides = to_columns(hold([arrived[d]], hops[1])[0])
-        token = scores_of_grads(sides, mixes[d], [token])
+        token = scores_of_grads(near[d], mixes[d], [token], LONG)
         terms.append(trade(token, {"dp": d}))
-
     mix, done = mixed(acts_of(block), queries, SHORT, [token])
-    tail = [to_columns(hold([piece], [done if p else token], LONG)[0]) for p, piece in enumerate(tail)]
-    block = from_partner(hops, far, count, [done], MIDDLE)
+    proj, token = projected(sides, queries, SHORT, [done])
+    tail[0], = hold(tail[:1], [done], LONG)
+    tail = [to_columns(hold([piece], [token if p else done], LONG)[0]) for p, piece in enumerate(tail)]
+    block = from_partner(hops, far, count, [done], LONG)
+    block, = hold([block], [], LONG)
     terms.append(trade(scores_of_acts(*acts_of(block), proj), {"dp": far}))
     terms.append(trade(scores_of_grads([list(sides) for sides in zip(*tail)], mix, (), LONG), {"dp": late}))
     return over_chips(sum(terms, scores), spread)

time: 114 us -> 101 us (0.89)
  waiting for transfers between devices: 53.8 us -> 27.7 us
  starting transfers between devices: 30.9 us -> 43.7 us
    ppermute x16, waiting for transfers between devices: 50.8 us -> 15.6 us  [trade(): return lax.ppermute(block, axes, route[::-1] if backwards else route)]
    ppermute x16, starting transfers between devices: 21.4 us -> 33.5 us  [trade(): return lax.ppermute(block, axes, route[::-1] if backwards else route)]
    ppermute x2, waiting for transfers between devices: 3.02 us -> 12.1 us  [pass_on(): lax.ppermute(block[1], 'dp', [(i, i - 1) for i in range(1, count - step +...]
  transfers between devices with their start and end apart: 21 -> 21, of which waited for: 8 -> 9; matrix products, arithmetic and copies ran while one was open for 0% -> 0% of each run, Pallas kernels for 24% -> 27%
where the time goes in v19:
time: 101 us
  starting transfers between devices  43.7 us (43%)
  Pallas kernels  28.6 us (28%)
  waiting for transfers between devices  27.7 us (27%)
    ppermute x16, starting transfers between devices, trade(): return lax.ppermute(block, axes, route[::-1] if backwards else route)  33.5 us
    pallas_call x11, Pallas kernels, call(): pl.pallas_call(body, in_specs=[NEAR] * len(arrays) + [ANYWHERE] * skip, o...  21.3 us
    ppermute x16, waiting for transfers between devices, trade(): return lax.ppermute(block, axes, route[::-1] if backwards else route)  15.6 us
    ppermute x2, waiting for transfers between devices, pass_on(): lax.ppermute(block[1], 'dp', [(i, i - 1) for i in range(1, count - step +...  12.1 us
    pallas_call x2, Pallas kernels, fetch(): pl.pallas_call(kernel, in_specs=[ANYWHERE] * len(arrays), out_specs=[NEAR...  7.33 us
    ppermute x2, starting transfers between devices, pass_on(): lax.ppermute(block[0], 'dp', [(i, i + 1) for i in range(step - 1, count -...  6.28 us
    ppermute x2, starting transfers between devices, pass_on(): lax.ppermute(block[1], 'dp', [(i, i - 1) for i in range(1, count - step +...  2.58 us
  transfers between devices with their start and end apart: 21, of which 9 were waited for; matrix products, arithmetic and copies ran while one was open for 0% of the time, Pallas kernels for 27%

profile of v19, /device:TPU:0, one launch (start us, length us, event | category | flops | bytes accessed | tf_op | source)
XLA Modules:
  0.0 100.8 jit_solution(3873004586663832600)
XLA Ops:
  0.0 1.0 %shard_map.40 = bf16[128,2048]{1,0:T(8,128)(2,1)S(1)} custom-call(bf16[256,2048]{1,0:T(8,128)(2,1)} %acts_ref.3), custom_call_target="tpu_custom_call" | custom-call | flops 1024 | bytes 1024 | tf_op jit(solution)/shard_map/pallas_call | solution.py:53
  1.1 1.3 %collective-permute-start.2 = (bf16[128,2048]{1,0:T(8,128)(2,1)S(1)}, bf16[128,2048]{1,0:T(8,128)(2,1)S(1)}, u32[]{:S(2)}, u32[]{:S(2)}) collective-permute-start(bf16[128,2048]{1,0:T(8,128)(2,1)S(1)} %shard_map.40), channel_id=1, source_target_pairs={{4,0},{8,4},{12,8},{5,1},{9,5},{13,9},{6,2},{10,6},{14,10},{7,3},{... | collective-permute-start | bytes 1572872 | tf_op jit(solution)/shard_map/ppermute | solution.py:27
  2.4 5.6 %collective-permute-start.1 = (bf16[128,2048]{1,0:T(8,128)(2,1)S(1)}, bf16[128,2048]{1,0:T(8,128)(2,1)S(1)}, u32[]{:S(2)}, u32[]{:S(2)}) collective-permute-start(bf16[128,2048]{1,0:T(8,128)(2,1)S(1)} %shard_map.40), channel_id=1, source_target_pairs={{0,4},{4,8},{8,12},{1,5},{5,9},{9,13},{2,6},{6,10},{10,14},{3,7},{... | collective-permute-start | bytes 1572872 | tf_op jit(solution)/shard_map/ppermute | solution.py:26
  8.0 6.3 %shard_map.37 = (bf16[2,1,1792,2048]{3,2,1,0:T(8,128)(2,1)S(1)}, bf16[256,2048]{1,0:T(8,128)(2,1)S(1)}, bf16[128,1792]{1,0:T(8,128)(2,1)S(1)}, bf16[1792,256]{1,...) custom-call(bf16[256,2048]{1,0:T(8,128)(2,1)} %acts_ref.3, ...), custom_call_target="tpu_custom_call" | custom-call | flops 1024 | bytes 1024 | tf_op jit(solution)/shard_map/pallas_call | solution.py:53
  14.2 2.1 %collective-permute-start = (bf16[1792,128]{1,0:T(8,128)(2,1)S(1)}, bf16[1792,128]{1,0:T(8,128)(2,1)S(1)}, u32[]{:S(2)}, u32[]{:S(2)}) collective-permute-start(bf16[1792,128]{1,0:T(8,128)(2,1)S(1)} %get-tuple-element.26), channel_id=1, source_target_pairs={{0,4},{4,0},{8,12},{12,8},{1,5},{5,1},{9,13},{13,9},{2,6},{6,2},{1... | collective-permute-start | bytes 1376264 | tf_op jit(solution)/shard_map/ppermute | solution.py:22
  16.3 4.7 %shard_map.38 = (f32[2,1792,256]{2,1,0:T(8,128)S(1)}, f32[8,128]{1,0:T(8,128)S(1)}) custom-call(bf16[256,2048]{1,0:T(8,128)(2,1)S(1)} %get-tuple-element.23.refs_0_, bf16[2,1,1792,2048]{3,2,1,0:T(8,128)(2,1)S(1)} %get-tuple-element.24.refs_1_.refs_2_), custom_call_target="tpu_custom_call" | custom-call | flops 1000000 | bytes 1024 | tf_op jit(solution)/shard_map/pallas_call | solution.py:41
  21.4 0.7 collective-permute-start.7
  22.2 1.3 %collective-permute-start.6 = (bf16[128,2048]{1,0:T(8,128)(2,1)S(1)}, bf16[128,2048]{1,0:T(8,128)(2,1)S(1)}, u32[]{:S(2)}, u32[]{:S(2)}) collective-permute-start(bf16[128,2048]{1,0:T(8,128)(2,1)S(1)} %get-tuple-element.29.refs_2_.refs_0_.refs_1_), channel_id=1, source_target_pairs={{4,0},{8,4},{5,1},{9,5},{6,2},{10,6},{7,3},{11,7},{20,16},{24,20},... | collective-permute-start | bytes 1572872 | tf_op jit(solution)/shard_map/ppermute | solution.py:27
  23.5 3.9 %collective-permute-start.11 = (bf16[128,1792]{1,0:T(8,128)(2,1)S(1)}, bf16[128,1792]{1,0:T(8,128)(2,1)S(1)}, u32[]{:S(2)}, u32[]{:S(2)}) collective-permute-start(bf16[128,1792]{1,0:T(8,128)(2,1)S(1)} %shard_map.50), channel_id=1, source_target_pairs={{0,12},{4,8},{8,4},{12,0},{1,13},{5,9},{9,5},{13,1},{2,14},{6,10},... | collective-permute-start | bytes 1376264 | tf_op jit(solution)/shard_map/ppermute | solution.py:22
  27.4 2.7 %collective-permute-done.refs_0_ = bf16[1792,128]{1,0:T(8,128)(2,1)S(1)} collective-permute-done((bf16[1792,128]{1,0:T(8,128)(2,1)S(1)}, bf16[1792,128]{1,0:T(8,128)(2,1)S(1)}, u32[]{:S(2)}, u32[]{:S(2)}) %collective-permute-start) | collective-permute-done | bytes 458784 | tf_op jit(solution)/shard_map/ppermute | solution.py:22
  30.1 2.0 %collective-permute-start.3 = (bf16[1792,128]{1,0:T(8,128)(2,1)S(1)}, bf16[1792,128]{1,0:T(8,128)(2,1)S(1)}, u32[]{:S(2)}, u32[]{:S(2)}) collective-permute-start(bf16[1792,128]{1,0:T(8,128)(2,1)S(1)} %shard_map.42.refs_0_), channel_id=1, source_target_pairs={{0,2},{2,0},{1,3},{3,1},{4,6},{6,4},{5,7},{7,5},{8,10},{10,8},{9,1... | collective-permute-start | bytes 1376264 | tf_op jit(solution)/shard_map/ppermute | solution.py:22
  32.0 4.7 %shard_map.44 = (f32[2,1792,256]{2,1,0:T(8,128)S(1)}, f32[8,128]{1,0:T(8,128)S(1)}) custom-call(bf16[128,2048]{1,0:T(8,128)(2,1)S(1)} %shard_map.43.refs_0_, bf16[128,2048]{1,0:T(8,128)(2,1)S(1)} %collective-permute-done.4.refs_1_, bf16[2,1,1792,2048]{3,2,1,0:T(8,128)(2,1)S(1)} %get-tuple-element.24.refs_1_.refs_2_, f32[2,256]{1,0:T(2,128)S(1)} %shard_map.39.refs_3_), custom_call_target="tpu_custom_call" | custom-call | flops 1000000 | bytes 1024 | tf_op jit(solution)/shard_map/pallas_call | solution.py:41
  36.7 12.1 %collective-permute-done.6.refs_0_ = bf16[128,2048]{1,0:T(8,128)(2,1)S(1)} collective-permute-done((bf16[128,2048]{1,0:T(8,128)(2,1)S(1)}, bf16[128,2048]{1,0:T(8,128)(2,1)S(1)}, u32[]{:S(2)}, u32[]{:S(2)}) %collective-permute-start.6) | collective-permute-done | bytes 524320 | tf_op jit(solution)/shard_map/ppermute | solution.py:27
  48.9 1.3 %collective-permute-start.8 = (bf16[128,2048]{1,0:T(8,128)(2,1)S(1)}, bf16[128,2048]{1,0:T(8,128)(2,1)S(1)}, u32[]{:S(2)}, u32[]{:S(2)}) collective-permute-start(bf16[128,2048]{1,0:T(8,128)(2,1)S(1)} %shard_map.46.refs_0_.refs_1_), channel_id=1, source_target_pairs={{4,0},{8,12},{5,1},{9,13},{6,2},{10,14},{7,3},{11,15},{20,16},{24,... | collective-permute-start | bytes 1572872 | tf_op jit(solution)/shard_map/ppermute | solution.py:297
  50.2 7.1 %collective-permute-start.14 = (bf16[896,128]{1,0:T(8,128)(2,1)S(1)}, bf16[896,128]{1,0:T(8,128)(2,1)S(1)}, u32[]{:S(2)}, u32[]{:S(2)}) collective-permute-start(bf16[896,128]{1,0:T(8,128)(2,1)S(1)} %shard_map.54), channel_id=1, source_target_pairs={{0,8},{4,12},{8,0},{12,4},{1,9},{5,13},{9,1},{13,5},{2,10},{6,14},... | collective-permute-start | bytes 688136 | tf_op jit(solution)/shard_map/ppermute | solution.py:22
  57.4 0.7 shard_map.45.refs_3_
  58.2 8.7 %collective-permute-start.15 = (bf16[896,128]{1,0:T(8,128)(2,1)S(1)}, bf16[896,128]{1,0:T(8,128)(2,1)S(1)}, u32[]{:S(2)}, u32[]{:S(2)}) collective-permute-start(bf16[896,128]{1,0:T(8,128)(2,1)S(1)} %shard_map.57), channel_id=1, source_target_pairs={{0,8},{4,12},{8,0},{12,4},{1,9},{5,13},{9,1},{13,5},{2,10},{6,14},... | collective-permute-start | bytes 688136 | tf_op jit(solution)/shard_map/ppermute | solution.py:22
  66.9 1.5 %collective-permute-start.12 = (bf16[128,1792]{1,0:T(8,128)(2,1)S(1)}, bf16[128,1792]{1,0:T(8,128)(2,1)S(1)}, u32[]{:S(2)}, u32[]{:S(2)}) collective-permute-start(bf16[128,1792]{1,0:T(8,128)(2,1)S(1)} %shard_map.51.refs_0_), channel_id=1, source_target_pairs={{0,2},{2,0},{1,3},{3,1},{4,6},{6,4},{5,7},{7,5},{8,10},{10,8},{9,1... | collective-permute-start | bytes 1376264 | tf_op jit(solution)/shard_map/ppermute | solution.py:22
  68.4 4.7 %shard_map.47 = (f32[2,1792,256]{2,1,0:T(8,128)S(1)}, f32[8,128]{1,0:T(8,128)S(1)}) custom-call(bf16[128,2048]{1,0:T(8,128)(2,1)S(1)} %shard_map.46.refs_0_.refs_1_, bf16[128,2048]{1,0:T(8,128)(2,1)S(1)} %collective-permute-done.9.refs_1_, bf16[2,1,1792,2048]{3,2,1,0:T(8,128)(2,1)S(1)} %get-tuple-element.24.refs_1_.refs_2_, f32[2,256]{1,0:T(2,128)S(1)} %shard_map.45.refs_3_), custom_call_target="tpu_custom_call" | custom-call | flops 1000000 | bytes 1024 | tf_op jit(solution)/shard_map/pallas_call | solution.py:41
  73.1 1.7 %collective-permute-done.14.refs_0_ = bf16[896,128]{1,0:T(8,128)(2,1)S(1)} collective-permute-done((bf16[896,128]{1,0:T(8,128)(2,1)S(1)}, bf16[896,128]{1,0:T(8,128)(2,1)S(1)}, u32[]{:S(2)}, u32[]{:S(2)}) %collective-permute-start.14) | collective-permute-done | bytes 229408 | tf_op jit(solution)/shard_map/ppermute | solution.py:22
  74.8 1.5 %collective-permute-start.16 = (bf16[896,128]{1,0:T(8,128)(2,1)S(1)}, bf16[896,128]{1,0:T(8,128)(2,1)S(1)}, u32[]{:S(2)}, u32[]{:S(2)}) collective-permute-start(bf16[896,128]{1,0:T(8,128)(2,1)S(1)} %shard_map.56.refs_0_), channel_id=1, source_target_pairs={{0,2},{2,0},{1,3},{3,1},{4,6},{6,4},{5,7},{7,5},{8,10},{10,8},{9,1... | collective-permute-start | bytes 688136 | tf_op jit(solution)/shard_map/ppermute | solution.py:22
  76.3 1.6 %collective-permute-done.12.refs_1_ = bf16[128,1792]{1,0:T(8,128)(2,1)S(1)} collective-permute-done((bf16[128,1792]{1,0:T(8,128)(2,1)S(1)}, bf16[128,1792]{1,0:T(8,128)(2,1)S(1)}, u32[]{:S(2)}, u32[]{:S(2)}) %collective-permute-start.12) | collective-permute-done | bytes 458784 | tf_op jit(solution)/shard_map/ppermute | solution.py:22
  77.9 4.8 %shard_map.52 = (f32[2,256,2048]{2,1,0:T(8,128)S(1)}, f32[8,128]{1,0:T(8,128)S(1)}) custom-call(bf16[128,1792]{1,0:T(8,128)(2,1)S(1)} %shard_map.51.refs_0_, bf16[128,1792]{1,0:T(8,128)(2,1)S(1)} %collective-permute-done.12.refs_1_, bf16[2,1,1792,2048]{3,2,1,0:T(8,128)(2,1)S(1)} %get-tuple-element.24.refs_1_.refs_2_, ...), custom_call_target="tpu_custom_call" | custom-call | flops 1000000 | bytes 1024 | tf_op jit(solution)/shard_map/pallas_call | solution.py:41
  82.7 1.5 %collective-permute-start.17 = (bf16[896,128]{1,0:T(8,128)(2,1)S(1)}, bf16[896,128]{1,0:T(8,128)(2,1)S(1)}, u32[]{:S(2)}, u32[]{:S(2)}) collective-permute-start(bf16[896,128]{1,0:T(8,128)(2,1)S(1)} %shard_map.58.refs_1_), channel_id=1, source_target_pairs={{0,2},{2,0},{1,3},{3,1},{4,6},{6,4},{5,7},{7,5},{8,10},{10,8},{9,1... | collective-permute-start | bytes 688136 | tf_op jit(solution)/shard_map/ppermute | solution.py:22
  84.4 4.4 %collective-permute-done.17.refs_3_ = bf16[896,128]{1,0:T(8,128)(2,1)S(1)} collective-permute-done((bf16[896,128]{1,0:T(8,128)(2,1)S(1)}, bf16[896,128]{1,0:T(8,128)(2,1)S(1)}, u32[]{:S(2)}, u32[]{:S(2)}) %collective-permute-start.17) | collective-permute-done | bytes 229408 | tf_op jit(solution)/shard_map/ppermute | solution.py:22
  88.8 0.7 shard_map.59
  90.1 3.5 %collective-permute-start.13 = (f32[2,256]{1,0:T(2,128)S(1)}, f32[2,256]{1,0:T(2,128)S(1)}, u32[]{:S(2)}, u32[]{:S(2)}) collective-permute-start(f32[2,256]{1,0:T(2,128)S(1)} %shard_map.53), channel_id=1, source_target_pairs={{0,12},{4,8},{8,4},{12,0},{1,13},{5,9},{9,5},{13,1},{2,14},{6,10},... | collective-permute-start | bytes 6152 | tf_op jit(solution)/shard_map/ppermute | solution.py:22
  94.0 1.5 %collective-permute-done.13 = f32[2,256]{1,0:T(2,128)S(1)} collective-permute-done((f32[2,256]{1,0:T(2,128)S(1)}, f32[2,256]{1,0:T(2,128)S(1)}, u32[]{:S(2)}, u32[]{:S(2)}) %collective-permute-start.13) | collective-permute-done | bytes 2080 | tf_op jit(solution)/shard_map/ppermute | solution.py:22
  95.5 1.2 %collective-permute-done.19 = f32[2,256]{1,0:T(2,128)S(1)} collective-permute-done((f32[2,256]{1,0:T(2,128)S(1)}, f32[2,256]{1,0:T(2,128)S(1)}, u32[]{:S(2)}, u32[]{:S(2)}) %collective-permute-start.19) | collective-permute-done | bytes 2080 | tf_op jit(solution)/shard_map/ppermute | solution.py:22
  96.7 1.5 %collective-permute-start.20 = (f32[2,256]{1,0:T(2,128)S(1)}, f32[2,256]{1,0:T(2,128)S(1)}, u32[]{:S(2)}, u32[]{:S(2)}) collective-permute-start(f32[2,256]{1,0:T(2,128)S(1)} %add.18), channel_id=1, source_target_pairs={{0,2},{2,0},{1,3},{3,1},{4,6},{6,4},{5,7},{7,5},{8,10},{10,8},{9,1... | collective-permute-start | bytes 6152 | tf_op jit(solution)/shard_map/ppermute | solution.py:22
  98.2 2.1 %collective-permute-done.20 = f32[2,256]{1,0:T(2,128)S(1)} collective-permute-done((f32[2,256]{1,0:T(2,128)S(1)}, f32[2,256]{1,0:T(2,128)S(1)}, u32[]{:S(2)}, u32[]{:S(2)}) %collective-permute-start.20) | collective-permute-done | bytes 2080 | tf_op jit(solution)/shard_map/ppermute | solution.py:22
  100.3 0.6 add.19
  (36 shorter events, 1.9 us)
Async XLA Ops:
  1.1 20.3 %collective-permute-start.2 = (bf16[128,2048]{1,0:T(8,128)(2,1)S(1)}, bf16[128,2048]{1,0:T(8,128)(2,1)S(1)}, u32[]{:S(2)}, u32[]{:S(2)}) collective-permute-start(bf16[128,2048]{1,0:T(8,128)(2,1)S(1)} %shard_map.40), channel_id=1, source_target_pairs={{4,0},{8,4},{12,8},{5,1},{9,5},{13,9},{6,2},{10,6},{14,10},{7,3},{... | collective-permute-start | bytes 1572872 | tf_op jit(solution)/shard_map/ppermute | solution.py:27
  2.4 19.0 %collective-permute-start.1 = (bf16[128,2048]{1,0:T(8,128)(2,1)S(1)}, bf16[128,2048]{1,0:T(8,128)(2,1)S(1)}, u32[]{:S(2)}, u32[]{:S(2)}) collective-permute-start(bf16[128,2048]{1,0:T(8,128)(2,1)S(1)} %shard_map.40), channel_id=1, source_target_pairs={{0,4},{4,8},{8,12},{1,5},{5,9},{9,13},{2,6},{6,10},{10,14},{3,7},{... | collective-permute-start | bytes 1572872 | tf_op jit(solution)/shard_map/ppermute | solution.py:26
  14.2 15.8 %collective-permute-start = (bf16[1792,128]{1,0:T(8,128)(2,1)S(1)}, bf16[1792,128]{1,0:T(8,128)(2,1)S(1)}, u32[]{:S(2)}, u32[]{:S(2)}) collective-permute-start(bf16[1792,128]{1,0:T(8,128)(2,1)S(1)} %get-tuple-element.26), channel_id=1, source_target_pairs={{0,4},{4,0},{8,12},{12,8},{1,5},{5,1},{9,13},{13,9},{2,6},{6,2},{1... | collective-permute-start | bytes 1376264 | tf_op jit(solution)/shard_map/ppermute | solution.py:22
  21.4 15.3 %collective-permute-start.7 = (bf16[128,2048]{1,0:T(8,128)(2,1)S(1)}, bf16[128,2048]{1,0:T(8,128)(2,1)S(1)}, u32[]{:S(2)}, u32[]{:S(2)}) collective-permute-start(bf16[128,2048]{1,0:T(8,128)(2,1)S(1)} %get-tuple-element.28.refs_1_.refs_2_), channel_id=1, source_target_pairs={{4,8},{8,12},{5,9},{9,13},{6,10},{10,14},{7,11},{11,15},{20,24},{2... | collective-permute-start | bytes 1572872 | tf_op jit(solution)/shard_map/ppermute | solution.py:26
  22.2 26.6 %collective-permute-start.6 = (bf16[128,2048]{1,0:T(8,128)(2,1)S(1)}, bf16[128,2048]{1,0:T(8,128)(2,1)S(1)}, u32[]{:S(2)}, u32[]{:S(2)}) collective-permute-start(bf16[128,2048]{1,0:T(8,128)(2,1)S(1)} %get-tuple-element.29.refs_2_.refs_0_.refs_1_), channel_id=1, source_target_pairs={{4,0},{8,4},{5,1},{9,5},{6,2},{10,6},{7,3},{11,7},{20,16},{24,20},... | collective-permute-start | bytes 1572872 | tf_op jit(solution)/shard_map/ppermute | solution.py:27
  23.5 34.7 %collective-permute-start.11 = (bf16[128,1792]{1,0:T(8,128)(2,1)S(1)}, bf16[128,1792]{1,0:T(8,128)(2,1)S(1)}, u32[]{:S(2)}, u32[]{:S(2)}) collective-permute-start(bf16[128,1792]{1,0:T(8,128)(2,1)S(1)} %shard_map.50), channel_id=1, source_target_pairs={{0,12},{4,8},{8,4},{12,0},{1,13},{5,9},{9,5},{13,1},{2,14},{6,10},... | collective-permute-start | bytes 1376264 | tf_op jit(solution)/shard_map/ppermute | solution.py:22
  27.4 4.7 %collective-permute-start.4 = (bf16[128,2048]{1,0:T(8,128)(2,1)S(1)}, bf16[128,2048]{1,0:T(8,128)(2,1)S(1)}, u32[]{:S(2)}, u32[]{:S(2)}) collective-permute-start(bf16[128,2048]{1,0:T(8,128)(2,1)S(1)} %shard_map.43.refs_0_), channel_id=1, source_target_pairs={{0,1},{1,0},{2,3},{3,2},{4,5},{5,4},{6,7},{7,6},{8,9},{9,8},{10,11... | collective-permute-start | bytes 1572872 | tf_op jit(solution)/shard_map/ppermute | solution.py:22
  30.1 27.3 %collective-permute-start.3 = (bf16[1792,128]{1,0:T(8,128)(2,1)S(1)}, bf16[1792,128]{1,0:T(8,128)(2,1)S(1)}, u32[]{:S(2)}, u32[]{:S(2)}) collective-permute-start(bf16[1792,128]{1,0:T(8,128)(2,1)S(1)} %shard_map.42.refs_0_), channel_id=1, source_target_pairs={{0,2},{2,0},{1,3},{3,1},{4,6},{6,4},{5,7},{7,5},{8,10},{10,8},{9,1... | collective-permute-start | bytes 1376264 | tf_op jit(solution)/shard_map/ppermute | solution.py:22
  48.8 18.1 %collective-permute-start.9 = (bf16[128,2048]{1,0:T(8,128)(2,1)S(1)}, bf16[128,2048]{1,0:T(8,128)(2,1)S(1)}, u32[]{:S(2)}, u32[]{:S(2)}) collective-permute-start(bf16[128,2048]{1,0:T(8,128)(2,1)S(1)} %shard_map.46.refs_0_.refs_1_), channel_id=1, source_target_pairs={{0,1},{1,0},{2,3},{3,2},{4,5},{5,4},{6,7},{7,6},{8,9},{9,8},{10,11... | collective-permute-start | bytes 1572872 | tf_op jit(solution)/shard_map/ppermute | solution.py:22
  48.9 35.3 %collective-permute-start.8 = (bf16[128,2048]{1,0:T(8,128)(2,1)S(1)}, bf16[128,2048]{1,0:T(8,128)(2,1)S(1)}, u32[]{:S(2)}, u32[]{:S(2)}) collective-permute-start(bf16[128,2048]{1,0:T(8,128)(2,1)S(1)} %shard_map.46.refs_0_.refs_1_), channel_id=1, source_target_pairs={{4,0},{8,12},{5,1},{9,13},{6,2},{10,14},{7,3},{11,15},{20,16},{24,... | collective-permute-start | bytes 1572872 | tf_op jit(solution)/shard_map/ppermute | solution.py:297
  50.2 24.5 %collective-permute-start.14 = (bf16[896,128]{1,0:T(8,128)(2,1)S(1)}, bf16[896,128]{1,0:T(8,128)(2,1)S(1)}, u32[]{:S(2)}, u32[]{:S(2)}) collective-permute-start(bf16[896,128]{1,0:T(8,128)(2,1)S(1)} %shard_map.54), channel_id=1, source_target_pairs={{0,8},{4,12},{8,0},{12,4},{1,9},{5,13},{9,1},{13,5},{2,10},{6,14},... | collective-permute-start | bytes 688136 | tf_op jit(solution)/shard_map/ppermute | solution.py:22
  58.1 35.4 %collective-permute-start.5 = (f32[2,256]{1,0:T(2,128)S(1)}, f32[2,256]{1,0:T(2,128)S(1)}, u32[]{:S(2)}, u32[]{:S(2)}) collective-permute-start(f32[2,256]{1,0:T(2,128)S(1)} %shard_map.45.refs_3_), channel_id=1, source_target_pairs={{0,4},{4,0},{8,12},{12,8},{1,5},{5,1},{9,13},{13,9},{2,6},{6,2},{1... | collective-permute-start | bytes 6152 | tf_op jit(solution)/shard_map/ppermute | solution.py:22
  58.2 24.4 %collective-permute-start.15 = (bf16[896,128]{1,0:T(8,128)(2,1)S(1)}, bf16[896,128]{1,0:T(8,128)(2,1)S(1)}, u32[]{:S(2)}, u32[]{:S(2)}) collective-permute-start(bf16[896,128]{1,0:T(8,128)(2,1)S(1)} %shard_map.57), channel_id=1, source_target_pairs={{0,8},{4,12},{8,0},{12,4},{1,9},{5,13},{9,1},{13,5},{2,10},{6,14},... | collective-permute-start | bytes 688136 | tf_op jit(solution)/shard_map/ppermute | solution.py:22
  66.9 10.9 %collective-permute-start.12 = (bf16[128,1792]{1,0:T(8,128)(2,1)S(1)}, bf16[128,1792]{1,0:T(8,128)(2,1)S(1)}, u32[]{:S(2)}, u32[]{:S(2)}) collective-permute-start(bf16[128,1792]{1,0:T(8,128)(2,1)S(1)} %shard_map.51.refs_0_), channel_id=1, source_target_pairs={{0,2},{2,0},{1,3},{3,1},{4,6},{6,4},{5,7},{7,5},{8,10},{10,8},{9,1... | collective-permute-start | bytes 1376264 | tf_op jit(solution)/shard_map/ppermute | solution.py:22
  74.8 9.6 %collective-permute-start.16 = (bf16[896,128]{1,0:T(8,128)(2,1)S(1)}, bf16[896,128]{1,0:T(8,128)(2,1)S(1)}, u32[]{:S(2)}, u32[]{:S(2)}) collective-permute-start(bf16[896,128]{1,0:T(8,128)(2,1)S(1)} %shard_map.56.refs_0_), channel_id=1, source_target_pairs={{0,2},{2,0},{1,3},{3,1},{4,6},{6,4},{5,7},{7,5},{8,10},{10,8},{9,1... | collective-permute-start | bytes 688136 | tf_op jit(solution)/shard_map/ppermute | solution.py:22
  82.7 6.1 %collective-permute-start.17 = (bf16[896,128]{1,0:T(8,128)(2,1)S(1)}, bf16[896,128]{1,0:T(8,128)(2,1)S(1)}, u32[]{:S(2)}, u32[]{:S(2)}) collective-permute-start(bf16[896,128]{1,0:T(8,128)(2,1)S(1)} %shard_map.58.refs_1_), channel_id=1, source_target_pairs={{0,2},{2,0},{1,3},{3,1},{4,6},{6,4},{5,7},{7,5},{8,10},{10,8},{9,1... | collective-permute-start | bytes 688136 | tf_op jit(solution)/shard_map/ppermute | solution.py:22
  84.3 5.3 %collective-permute-start.10 = (bf16[128,2048]{1,0:T(8,128)(2,1)S(1)}, bf16[128,2048]{1,0:T(8,128)(2,1)S(1)}, u32[]{:S(2)}, u32[]{:S(2)}) collective-permute-start(bf16[128,2048]{1,0:T(8,128)(2,1)S(1)} %shard_map.49.refs_0_), channel_id=1, source_target_pairs={{0,1},{1,0},{2,3},{3,2},{4,5},{5,4},{6,7},{7,6},{8,9},{9,8},{10,11... | collective-permute-start | bytes 1572872 | tf_op jit(solution)/shard_map/ppermute | solution.py:22
  89.5 4.5 %collective-permute-start.18 = (f32[2,256]{1,0:T(2,128)S(1)}, f32[2,256]{1,0:T(2,128)S(1)}, u32[]{:S(2)}, u32[]{:S(2)}) collective-permute-start(f32[2,256]{1,0:T(2,128)S(1)} %shard_map.59), channel_id=1, source_target_pairs={{0,8},{4,12},{8,0},{12,4},{1,9},{5,13},{9,1},{13,5},{2,10},{6,14},... | collective-permute-start | bytes 6152 | tf_op jit(solution)/shard_map/ppermute | solution.py:22
  90.1 5.4 %collective-permute-start.13 = (f32[2,256]{1,0:T(2,128)S(1)}, f32[2,256]{1,0:T(2,128)S(1)}, u32[]{:S(2)}, u32[]{:S(2)}) collective-permute-start(f32[2,256]{1,0:T(2,128)S(1)} %shard_map.53), channel_id=1, source_target_pairs={{0,12},{4,8},{8,4},{12,0},{1,13},{5,9},{9,5},{13,1},{2,14},{6,10},... | collective-permute-start | bytes 6152 | tf_op jit(solution)/shard_map/ppermute | solution.py:22
  95.5 1.2 %collective-permute-start.19 = (f32[2,256]{1,0:T(2,128)S(1)}, f32[2,256]{1,0:T(2,128)S(1)}, u32[]{:S(2)}, u32[]{:S(2)}) collective-permute-start(f32[2,256]{1,0:T(2,128)S(1)} %add_add_fusion), channel_id=1, source_target_pairs={{0,1},{1,0},{2,3},{3,2},{4,5},{5,4},{6,7},{7,6},{8,9},{9,8},{10,11... | collective-permute-start | bytes 6152 | tf_op jit(solution)/shard_map/ppermute | solution.py:22
  96.7 3.6 %collective-permute-start.20 = (f32[2,256]{1,0:T(2,128)S(1)}, f32[2,256]{1,0:T(2,128)S(1)}, u32[]{:S(2)}, u32[]{:S(2)}) collective-permute-start(f32[2,256]{1,0:T(2,128)S(1)} %add.18), channel_id=1, source_target_pairs={{0,2},{2,0},{1,3},{3,1},{4,6},{6,4},{5,7},{7,5},{8,10},{10,8},{9,1... | collective-permute-start | bytes 6152 | tf_op jit(solution)/shard_map/ppermute | solution.py:22

commit v20 on v18

--- a/solution.py
+++ b/solution.py
@@ -186,21 +186,19 @@
     return call(mix_kernel, [*parts, queries], outs, flops, tokens, scratch)
 
 
-def score_kernel(pieces, *refs):
-    *parts, mix_ref, out_ref = refs
-    size = mix_ref.shape[1] // pieces
-    for p in range(pieces):
-        grads = joined(parts[p::pieces], 1).astype(jnp.float32)
-        for q in range(mix_ref.shape[0]):
-            term = jnp.sum(grads * mix_ref[q, p * size : (p + 1) * size], axis=0, keepdims=True)
-            out_ref[q : q + 1, :] = term if p == 0 else out_ref[q : q + 1, :] + term
-
-
-def scores_of_grads(parts, mix, tokens=(), flops=1024):
+def score_kernel(first, number, *refs):
+    parts, (mix_ref, *before, out_ref) = refs[:number], refs[number:]
+    grads = joined(parts, 1).astype(jnp.float32)
+    for q in range(mix_ref.shape[0]):
+        mix = mix_ref[q, first : first + grads.shape[0]]
+        term = jnp.sum(grads * mix, axis=0, keepdims=True)
+        out_ref[q : q + 1, :] = before[0][q : q + 1, :] + term if before else term
+
+
+def scores_of_grads(parts, mix, tokens=(), flops=1024, first=0, before=()):
     nq, _, count = mix.shape
-    parts = [part if isinstance(part, list) else [part] for part in parts]
-    kernel = functools.partial(score_kernel, len(parts[0]))
-    return call(kernel, [*sum(parts, []), mix], [((nq, count), jnp.float32)], flops, tokens)[0]
+    kernel = functools.partial(score_kernel, first, len(parts))
+    return call(kernel, [*parts, mix, *before], [((nq, count), jnp.float32)], flops, tokens)[0]
 
 
 def project_kernel(*refs):
@@ -246,7 +244,7 @@
     return call(finish_kernel, [mine, other, proj], [((nq, count), jnp.float32)], tokens=tokens)[0]
 
 
-def cut(activations, out_grads, queries, far, others, pieces):
+def cut(activations, out_grads, queries, far, others, sizes):
     count, part = lax.axis_size("dp"), out_grads.shape[0] // lax.axis_size("din")
     rows, (tokens, width), dtype = queries.shape[2], activations.shape, out_grads.dtype
     half = tokens // 2
@@ -257,11 +255,11 @@
         away = [lax.dynamic_slice_in_dim(share, (me ^ d) * rows, rows, 1) for d in [far, *others]]
         own = lax.dynamic_slice_in_dim(out_grads, me * rows, rows, 1).T
         turned = [block.T for block in away[1:]]
-        return (mine, away[0]), (queries, activations, own, *turned[:-1], *jnp.split(turned[-1], pieces))
+        return (mine, away[0]), (queries, activations, own, *turned[:-1], *jnp.split(turned[-1], [sizes[0]]))
     outs = [((half, width), activations.dtype), ((part, rows), dtype)]
     first = fetch(functools.partial(first_kernel, far), [activations, out_grads], outs, [], 2)
     outs = [(queries.shape, queries.dtype), (activations.shape, activations.dtype), ((rows, tokens), dtype)]
-    outs += [((rows, part), dtype)] * (len(others) - 1) + [((rows // pieces, part), dtype)] * pieces
+    outs += [((rows, part), dtype)] * (len(others) - 1) + [((size, part), dtype) for size in sizes]
     scratch = [pltpu.VMEM((tokens, rows), dtype), pltpu.VMEM((len(others), part, rows), dtype)]
     arrays = [activations, out_grads, queries]
     return first, fetch(functools.partial(rest_kernel, others), arrays, outs, scratch, len(others) + 3)
@@ -278,9 +276,10 @@
 
     far, late = count - 1, count - 2
     early = list(range(1, late))
-    pieces = 2
+    rows = queries.shape[2]
+    sizes = [rows // 7 * 5, rows - rows // 7 * 5]
     (mine, far_grads), (queries, own_acts, own, *sent) = cut(
-        activations, out_grads, queries, far, early + [late], pieces
+        activations, out_grads, queries, far, early + [late], sizes
     )
     hops = [(mine, mine)]
     hops.append(pass_on(hops[0], 1, count))
@@ -312,7 +311,9 @@
     tail = [to_columns(hold([piece], [done if p else token], LONG)[0]) for p, piece in enumerate(tail)]
     block = from_partner(hops, far, count, [done])
     terms.append(trade(scores_of_acts(*acts_of(block), proj), {"dp": far}))
-    terms.append(trade(scores_of_grads([list(sides) for sides in zip(*tail)], mix, (), LONG), {"dp": late}))
+    term = scores_of_grads(tail[0], mix)
+    term = scores_of_grads(tail[1], mix, (), LONG, sizes[0], [term])
+    terms.append(trade(term, {"dp": late}))
     return over_chips(sum(terms, scores), spread)
 
 

time: 92.8 us -> 95 us (1.024)
  waiting for transfers between devices: 33.9 us -> 38.2 us
  starting transfers between devices: 29.3 us -> 27.1 us
    ppermute x16, waiting for transfers between devices: 28.5 us -> 35.3 us  [trade(): return lax.ppermute(block, axes, route[::-1] if backwards else route)]
    ppermute x16, starting transfers between devices: 19.8 us -> 17.6 us  [trade(): return lax.ppermute(block, axes, route[::-1] if backwards else route)]
    ppermute x1, waiting for transfers between devices: 4.69 us -> 2.9 us  [on_device(): end = lax.ppermute(block, 'dp', [(1, 0), (count - 2, count - 1)])]
    pallas_call x11 -> x12, Pallas kernels: 21.2 us -> 21.4 us  [call(): pl.pallas_call(body, in_specs=[NEAR] * len(arrays) + [ANYWHERE] * skip, o...]
  transfers between devices with their start and end apart: 21 -> 21, of which waited for: 12 -> 11; matrix products, arithmetic and copies ran while one was open for 0% -> 0% of each run, Pallas kernels for 30% -> 29%
where the time goes in v20:
time: 95 us; the launch traced here: 94.8 us
  waiting for transfers between devices  38.2 us (40%)
  Pallas kernels  28.7 us (30%)
  starting transfers between devices  27.1 us (29%)
    ppermute x16, waiting for transfers between devices, trade(): return lax.ppermute(block, axes, route[::-1] if backwards else route)  35.3 us
    pallas_call x12, Pallas kernels, call(): pl.pallas_call(body, in_specs=[NEAR] * len(arrays) + [ANYWHERE] * skip, o...  21.4 us
    ppermute x16, starting transfers between devices, trade(): return lax.ppermute(block, axes, route[::-1] if backwards else route)  17.6 us
    pallas_call x2, Pallas kernels, fetch(): pl.pallas_call(kernel, in_specs=[ANYWHERE] * len(arrays), out_specs=[NEAR...  7.32 us
    ppermute x2, starting transfers between devices, pass_on(): lax.ppermute(block[0], 'dp', [(i, i + 1) for i in range(step - 1, count -...  5.65 us
    ppermute x1, waiting for transfers between devices, on_device(): end = lax.ppermute(block, 'dp', [(1, 0), (count - 2, count - 1)])  2.9 us
    ppermute x2, starting transfers between devices, pass_on(): lax.ppermute(block[1], 'dp', [(i, i - 1) for i in range(1, count - step +...  2.58 us
  transfers between devices with their start and end apart: 21, of which 11 were waited for; matrix products, arithmetic and copies ran while one was open for 0% of the time, Pallas kernels for 29%

profile of v20, /device:TPU:0, one launch (start us, length us, event | category | flops | bytes accessed | tf_op | source)
XLA Modules:
  0.0 94.8 jit_solution(12192981755325270375)
XLA Ops:
  0.0 1.2 %shard_map.40 = (bf16[128,2048]{1,0:T(8,128)(2,1)S(1)}, bf16[128,1792]{1,0:T(8,128)(2,1)S(1)}) custom-call(bf16[256,2048]{1,0:T(8,128)(2,1)} %acts_ref.3, bf16[256,7168]{1,0:T(8,128)(2,1)} %grads_ref.3), custom_call_target="tpu_custom_call" | custom-call | flops 1024 | bytes 1024 | tf_op jit(solution)/shard_map/pallas_call | solution.py:53
  1.2 5.0 %collective-permute-start.1 = (bf16[128,2048]{1,0:T(8,128)(2,1)S(1)}, bf16[128,2048]{1,0:T(8,128)(2,1)S(1)}, u32[]{:S(2)}, u32[]{:S(2)}) collective-permute-start(bf16[128,2048]{1,0:T(8,128)(2,1)S(1)} %get-tuple-element.28), channel_id=1, source_target_pairs={{0,4},{4,8},{8,12},{1,5},{5,9},{9,13},{2,6},{6,10},{10,14},{3,7},{... | collective-permute-start | bytes 1572872 | tf_op jit(solution)/shard_map/ppermute | solution.py:26
  6.2 1.3 %collective-permute-start.2 = (bf16[128,2048]{1,0:T(8,128)(2,1)S(1)}, bf16[128,2048]{1,0:T(8,128)(2,1)S(1)}, u32[]{:S(2)}, u32[]{:S(2)}) collective-permute-start(bf16[128,2048]{1,0:T(8,128)(2,1)S(1)} %get-tuple-element.28), channel_id=1, source_target_pairs={{4,0},{8,4},{12,8},{5,1},{9,5},{13,9},{6,2},{10,6},{14,10},{7,3},{... | collective-permute-start | bytes 1572872 | tf_op jit(solution)/shard_map/ppermute | solution.py:27
  7.5 6.1 %shard_map.37 = (bf16[2,1,1792,2048]{3,2,1,0:T(8,128)(2,1)S(1)}, bf16[256,2048]{1,0:T(8,128)(2,1)S(1)}, bf16[1792,256]{1,0:T(8,128)(2,1)S(1)}, bf16[1792,128]{1,...) custom-call(bf16[256,2048]{1,0:T(8,128)(2,1)} %acts_ref.3, bf16[256,7168]{1,0:T(8,128)(2,1)} %grads_ref.3, ...), custom_call_target="tpu_custom_call" | custom-call | flops 1024 | bytes 1024 | tf_op jit(solution)/shard_map/pallas_call | solution.py:53
  13.6 2.7 %collective-permute-start = (bf16[1792,128]{1,0:T(8,128)(2,1)S(1)}, bf16[1792,128]{1,0:T(8,128)(2,1)S(1)}, u32[]{:S(2)}, u32[]{:S(2)}) collective-permute-start(bf16[1792,128]{1,0:T(8,128)(2,1)S(1)} %get-tuple-element.27), channel_id=1, source_target_pairs={{0,4},{4,0},{8,12},{12,8},{1,5},{5,1},{9,13},{13,9},{2,6},{6,2},{1... | collective-permute-start | bytes 1376264 | tf_op jit(solution)/shard_map/ppermute | solution.py:22
  16.3 2.4 %collective-permute-start.5 = (bf16[128,1792]{1,0:T(8,128)(2,1)S(1)}, bf16[128,1792]{1,0:T(8,128)(2,1)S(1)}, u32[]{:S(2)}, u32[]{:S(2)}) collective-permute-start(bf16[128,1792]{1,0:T(8,128)(2,1)S(1)} %get-tuple-element.33), channel_id=1, source_target_pairs={{0,12},{4,8},{8,4},{12,0},{1,13},{5,9},{9,5},{13,1},{2,14},{6,10},... | collective-permute-start | bytes 1376264 | tf_op jit(solution)/shard_map/ppermute | solution.py:22
  18.8 4.7 %shard_map.38 = (f32[2,1792,256]{2,1,0:T(8,128)S(1)}, f32[8,128]{1,0:T(8,128)S(1)}) custom-call(bf16[256,2048]{1,0:T(8,128)(2,1)S(1)} %get-tuple-element.24.refs_0_, bf16[2,1,1792,2048]{3,2,1,0:T(8,128)(2,1)S(1)} %get-tuple-element.25.refs_1_.refs_2_), custom_call_target="tpu_custom_call" | custom-call | flops 1000000 | bytes 1024 | tf_op jit(solution)/shard_map/pallas_call | solution.py:41
  23.6 1.3 %collective-permute-start.8 = (bf16[128,2048]{1,0:T(8,128)(2,1)S(1)}, bf16[128,2048]{1,0:T(8,128)(2,1)S(1)}, u32[]{:S(2)}, u32[]{:S(2)}) collective-permute-start(bf16[128,2048]{1,0:T(8,128)(2,1)S(1)} %get-tuple-element.31.refs_2_.refs_0_.refs_1_), channel_id=1, source_target_pairs={{4,0},{8,4},{5,1},{9,5},{6,2},{10,6},{7,3},{11,7},{20,16},{24,20},... | collective-permute-start | bytes 1572872 | tf_op jit(solution)/shard_map/ppermute | solution.py:27
  24.9 0.7 collective-permute-start.9
  25.6 8.1 %collective-permute-done.refs_0_.refs_3_ = bf16[1792,128]{1,0:T(8,128)(2,1)S(1)} collective-permute-done((bf16[1792,128]{1,0:T(8,128)(2,1)S(1)}, bf16[1792,128]{1,0:T(8,128)(2,1)S(1)}, u32[]{:S(2)}, u32[]{:S(2)}) %collective-permute-start) | collective-permute-done | bytes 458784 | tf_op jit(solution)/shard_map/ppermute | solution.py:22
  33.7 9.6 %collective-permute-done.5.refs_0_ = bf16[128,1792]{1,0:T(8,128)(2,1)S(1)} collective-permute-done((bf16[128,1792]{1,0:T(8,128)(2,1)S(1)}, bf16[128,1792]{1,0:T(8,128)(2,1)S(1)}, u32[]{:S(2)}, u32[]{:S(2)}) %collective-permute-start.5) | collective-permute-done | bytes 458784 | tf_op jit(solution)/shard_map/ppermute | solution.py:22
  43.3 1.5 %collective-permute-start.6 = (bf16[128,1792]{1,0:T(8,128)(2,1)S(1)}, bf16[128,1792]{1,0:T(8,128)(2,1)S(1)}, u32[]{:S(2)}, u32[]{:S(2)}) collective-permute-start(bf16[128,1792]{1,0:T(8,128)(2,1)S(1)} %shard_map.45.refs_0_.refs_3_), channel_id=1, source_target_pairs={{0,2},{2,0},{1,3},{3,1},{4,6},{6,4},{5,7},{7,5},{8,10},{10,8},{9,1... | collective-permute-start | bytes 1376264 | tf_op jit(solution)/shard_map/ppermute | solution.py:22
  45.7 4.7 %shard_map.44 = (f32[2,1792,256]{2,1,0:T(8,128)S(1)}, f32[8,128]{1,0:T(8,128)S(1)}) custom-call(bf16[128,2048]{1,0:T(8,128)(2,1)S(1)} %shard_map.43.refs_0_, bf16[128,2048]{1,0:T(8,128)(2,1)S(1)} %collective-permute-done.4.refs_1_, bf16[2,1,1792,2048]{3,2,1,0:T(8,128)(2,1)S(1)} %get-tuple-element.25.refs_1_.refs_2_, f32[2,256]{1,0:T(2,128)S(1)} %shard_map.39.refs_3_), custom_call_target="tpu_custom_call" | custom-call | flops 1000000 | bytes 1024 | tf_op jit(solution)/shard_map/pallas_call | solution.py:41
  50.5 6.2 %collective-permute-done.6.refs_1_.refs_4_ = bf16[128,1792]{1,0:T(8,128)(2,1)S(1)} collective-permute-done((bf16[128,1792]{1,0:T(8,128)(2,1)S(1)}, bf16[128,1792]{1,0:T(8,128)(2,1)S(1)}, u32[]{:S(2)}, u32[]{:S(2)}) %collective-permute-start.6) | collective-permute-done | bytes 458784 | tf_op jit(solution)/shard_map/ppermute | solution.py:22
  56.9 1.3 %collective-permute-start.10 = (bf16[128,2048]{1,0:T(8,128)(2,1)S(1)}, bf16[128,2048]{1,0:T(8,128)(2,1)S(1)}, u32[]{:S(2)}, u32[]{:S(2)}) collective-permute-start(bf16[128,2048]{1,0:T(8,128)(2,1)S(1)} %shard_map.48.refs_0_), channel_id=1, source_target_pairs={{4,0},{8,12},{5,1},{9,13},{6,2},{10,14},{7,3},{11,15},{20,16},{24,... | collective-permute-start | bytes 1572872 | tf_op jit(solution)/shard_map/ppermute | solution.py:300
  58.2 4.7 %collective-permute-start.14 = (bf16[512,128]{1,0:T(8,128)(2,1)S(1)}, bf16[512,128]{1,0:T(8,128)(2,1)S(1)}, u32[]{:S(2)}, u32[]{:S(2)}) collective-permute-start(bf16[512,128]{1,0:T(8,128)(2,1)S(1)} %shard_map.52), channel_id=1, source_target_pairs={{0,8},{4,12},{8,0},{12,4},{1,9},{5,13},{9,1},{13,5},{2,10},{6,14},... | collective-permute-start | bytes 393224 | tf_op jit(solution)/shard_map/ppermute | solution.py:22
  62.9 4.8 %shard_map.46 = (f32[2,256,2048]{2,1,0:T(8,128)S(1)}, f32[8,128]{1,0:T(8,128)S(1)}) custom-call(bf16[128,1792]{1,0:T(8,128)(2,1)S(1)} %shard_map.45.refs_0_.refs_3_, bf16[128,1792]{1,0:T(8,128)(2,1)S(1)} %collective-permute-done.6.refs_1_.refs_4_, bf16[2,1,1792,2048]{3,2,1,0:T(8,128)(2,1)S(1)} %get-tuple-element.25.refs_1_.refs_2_, ...), custom_call_target="tpu_custom_call" | custom-call | flops 1000000 | bytes 1024 | tf_op jit(solution)/shard_map/pallas_call | solution.py:41
  67.7 0.8 shard_map.47.refs_3_.refs_1_
  68.4 3.3 %collective-permute-done.16.refs_0_ = bf16[1280,128]{1,0:T(8,128)(2,1)S(1)} collective-permute-done((bf16[1280,128]{1,0:T(8,128)(2,1)S(1)}, bf16[1280,128]{1,0:T(8,128)(2,1)S(1)}, u32[]{:S(2)}, u32[]{:S(2)}) %collective-permute-start.16) | collective-permute-done | bytes 327712 | tf_op jit(solution)/shard_map/ppermute | solution.py:22
  71.7 1.5 %collective-permute-start.17 = (bf16[1280,128]{1,0:T(8,128)(2,1)S(1)}, bf16[1280,128]{1,0:T(8,128)(2,1)S(1)}, u32[]{:S(2)}, u32[]{:S(2)}) collective-permute-start(bf16[1280,128]{1,0:T(8,128)(2,1)S(1)} %shard_map.55.refs_0_), channel_id=1, source_target_pairs={{0,2},{2,0},{1,3},{3,1},{4,6},{6,4},{5,7},{7,5},{8,10},{10,8},{9,1... | collective-permute-start | bytes 983048 | tf_op jit(solution)/shard_map/ppermute | solution.py:22
  73.2 4.7 %shard_map.49 = (f32[2,1792,256]{2,1,0:T(8,128)S(1)}, f32[8,128]{1,0:T(8,128)S(1)}) custom-call(bf16[128,2048]{1,0:T(8,128)(2,1)S(1)} %shard_map.48.refs_0_, bf16[128,2048]{1,0:T(8,128)(2,1)S(1)} %collective-permute-done.11.refs_1_, bf16[2,1,1792,2048]{3,2,1,0:T(8,128)(2,1)S(1)} %get-tuple-element.25.refs_1_.refs_2_, f32[2,256]{1,0:T(2,128)S(1)} %shard_map.47.refs_3_.refs_1_), custom_call_target="tpu_custom_call" | custom-call | flops 1000000 | bytes 1024 | tf_op jit(solution)/shard_map/pallas_call | solution.py:41
  77.9 0.6 collective-permute-start.15
  78.5 2.9 %collective-permute-done.10.refs_0_ = bf16[128,2048]{1,0:T(8,128)(2,1)S(1)} collective-permute-done((bf16[128,2048]{1,0:T(8,128)(2,1)S(1)}, bf16[128,2048]{1,0:T(8,128)(2,1)S(1)}, u32[]{:S(2)}, u32[]{:S(2)}) %collective-permute-start.10) | collective-permute-done | bytes 524320 | tf_op jit(solution)/shard_map/ppermute | solution.py:300
  82.1 0.8 collective-permute-done.15.refs_1_
  83.5 0.6 shard_map.51
  84.0 1.7 %collective-permute-start.13 = (f32[2,256]{1,0:T(2,128)S(1)}, f32[2,256]{1,0:T(2,128)S(1)}, u32[]{:S(2)}, u32[]{:S(2)}) collective-permute-start(f32[2,256]{1,0:T(2,128)S(1)} %shard_map.51), channel_id=1, source_target_pairs={{0,12},{4,8},{8,4},{12,0},{1,13},{5,9},{9,5},{13,1},{2,14},{6,10},... | collective-permute-start | bytes 6152 | tf_op jit(solution)/shard_map/ppermute | solution.py:22
  85.7 2.0 %collective-permute-done.18 = f32[2,256]{1,0:T(2,128)S(1)} collective-permute-done((f32[2,256]{1,0:T(2,128)S(1)}, f32[2,256]{1,0:T(2,128)S(1)}, u32[]{:S(2)}, u32[]{:S(2)}) %collective-permute-start.18) | collective-permute-done | bytes 2080 | tf_op jit(solution)/shard_map/ppermute | solution.py:22
  87.7 1.8 %collective-permute-done.13 = f32[2,256]{1,0:T(2,128)S(1)} collective-permute-done((f32[2,256]{1,0:T(2,128)S(1)}, f32[2,256]{1,0:T(2,128)S(1)}, u32[]{:S(2)}, u32[]{:S(2)}) %collective-permute-start.13) | collective-permute-done | bytes 2080 | tf_op jit(solution)/shard_map/ppermute | solution.py:22
  89.5 1.2 %collective-permute-done.19 = f32[2,256]{1,0:T(2,128)S(1)} collective-permute-done((f32[2,256]{1,0:T(2,128)S(1)}, f32[2,256]{1,0:T(2,128)S(1)}, u32[]{:S(2)}, u32[]{:S(2)}) %collective-permute-start.19) | collective-permute-done | bytes 2080 | tf_op jit(solution)/shard_map/ppermute | solution.py:22
  90.7 1.5 %collective-permute-start.20 = (f32[2,256]{1,0:T(2,128)S(1)}, f32[2,256]{1,0:T(2,128)S(1)}, u32[]{:S(2)}, u32[]{:S(2)}) collective-permute-start(f32[2,256]{1,0:T(2,128)S(1)} %add.18), channel_id=1, source_target_pairs={{0,2},{2,0},{1,3},{3,1},{4,6},{6,4},{5,7},{7,5},{8,10},{10,8},{9,1... | collective-permute-start | bytes 6152 | tf_op jit(solution)/shard_map/ppermute | solution.py:22
  92.2 2.1 %collective-permute-done.20 = f32[2,256]{1,0:T(2,128)S(1)} collective-permute-done((f32[2,256]{1,0:T(2,128)S(1)}, f32[2,256]{1,0:T(2,128)S(1)}, u32[]{:S(2)}, u32[]{:S(2)}) %collective-permute-start.20) | collective-permute-done | bytes 2080 | tf_op jit(solution)/shard_map/ppermute | solution.py:22
  94.2 0.6 add.19
  (34 shorter events, 2.5 us)
Async XLA Ops:
  1.2 22.2 %collective-permute-start.1 = (bf16[128,2048]{1,0:T(8,128)(2,1)S(1)}, bf16[128,2048]{1,0:T(8,128)(2,1)S(1)}, u32[]{:S(2)}, u32[]{:S(2)}) collective-permute-start(bf16[128,2048]{1,0:T(8,128)(2,1)S(1)} %get-tuple-element.28), channel_id=1, source_target_pairs={{0,4},{4,8},{8,12},{1,5},{5,9},{9,13},{2,6},{6,10},{10,14},{3,7},{... | collective-permute-start | bytes 1572872 | tf_op jit(solution)/shard_map/ppermute | solution.py:26
  6.2 17.3 %collective-permute-start.2 = (bf16[128,2048]{1,0:T(8,128)(2,1)S(1)}, bf16[128,2048]{1,0:T(8,128)(2,1)S(1)}, u32[]{:S(2)}, u32[]{:S(2)}) collective-permute-start(bf16[128,2048]{1,0:T(8,128)(2,1)S(1)} %get-tuple-element.28), channel_id=1, source_target_pairs={{4,0},{8,4},{12,8},{5,1},{9,5},{13,9},{6,2},{10,6},{14,10},{7,3},{... | collective-permute-start | bytes 1572872 | tf_op jit(solution)/shard_map/ppermute | solution.py:27
  13.6 20.1 %collective-permute-start = (bf16[1792,128]{1,0:T(8,128)(2,1)S(1)}, bf16[1792,128]{1,0:T(8,128)(2,1)S(1)}, u32[]{:S(2)}, u32[]{:S(2)}) collective-permute-start(bf16[1792,128]{1,0:T(8,128)(2,1)S(1)} %get-tuple-element.27), channel_id=1, source_target_pairs={{0,4},{4,0},{8,12},{12,8},{1,5},{5,1},{9,13},{13,9},{2,6},{6,2},{1... | collective-permute-start | bytes 1376264 | tf_op jit(solution)/shard_map/ppermute | solution.py:22
  16.3 27.0 %collective-permute-start.5 = (bf16[128,1792]{1,0:T(8,128)(2,1)S(1)}, bf16[128,1792]{1,0:T(8,128)(2,1)S(1)}, u32[]{:S(2)}, u32[]{:S(2)}) collective-permute-start(bf16[128,1792]{1,0:T(8,128)(2,1)S(1)} %get-tuple-element.33), channel_id=1, source_target_pairs={{0,12},{4,8},{8,4},{12,0},{1,13},{5,9},{9,5},{13,1},{2,14},{6,10},... | collective-permute-start | bytes 1376264 | tf_op jit(solution)/shard_map/ppermute | solution.py:22
  23.5 22.2 %collective-permute-start.4 = (bf16[128,2048]{1,0:T(8,128)(2,1)S(1)}, bf16[128,2048]{1,0:T(8,128)(2,1)S(1)}, u32[]{:S(2)}, u32[]{:S(2)}) collective-permute-start(bf16[128,2048]{1,0:T(8,128)(2,1)S(1)} %shard_map.43.refs_0_), channel_id=1, source_target_pairs={{0,1},{1,0},{2,3},{3,2},{4,5},{5,4},{6,7},{7,6},{8,9},{9,8},{10,11... | collective-permute-start | bytes 1572872 | tf_op jit(solution)/shard_map/ppermute | solution.py:22
  23.6 33.1 %collective-permute-start.8 = (bf16[128,2048]{1,0:T(8,128)(2,1)S(1)}, bf16[128,2048]{1,0:T(8,128)(2,1)S(1)}, u32[]{:S(2)}, u32[]{:S(2)}) collective-permute-start(bf16[128,2048]{1,0:T(8,128)(2,1)S(1)} %get-tuple-element.31.refs_2_.refs_0_.refs_1_), channel_id=1, source_target_pairs={{4,0},{8,4},{5,1},{9,5},{6,2},{10,6},{7,3},{11,7},{20,16},{24,20},... | collective-permute-start | bytes 1572872 | tf_op jit(solution)/shard_map/ppermute | solution.py:27
  24.9 31.8 %collective-permute-start.9 = (bf16[128,2048]{1,0:T(8,128)(2,1)S(1)}, bf16[128,2048]{1,0:T(8,128)(2,1)S(1)}, u32[]{:S(2)}, u32[]{:S(2)}) collective-permute-start(bf16[128,2048]{1,0:T(8,128)(2,1)S(1)} %get-tuple-element.30.refs_1_.refs_2_), channel_id=1, source_target_pairs={{4,8},{8,12},{5,9},{9,13},{6,10},{10,14},{7,11},{11,15},{20,24},{2... | collective-permute-start | bytes 1572872 | tf_op jit(solution)/shard_map/ppermute | solution.py:26
  43.3 13.5 %collective-permute-start.6 = (bf16[128,1792]{1,0:T(8,128)(2,1)S(1)}, bf16[128,1792]{1,0:T(8,128)(2,1)S(1)}, u32[]{:S(2)}, u32[]{:S(2)}) collective-permute-start(bf16[128,1792]{1,0:T(8,128)(2,1)S(1)} %shard_map.45.refs_0_.refs_3_), channel_id=1, source_target_pairs={{0,2},{2,0},{1,3},{3,1},{4,6},{6,4},{5,7},{7,5},{8,10},{10,8},{9,1... | collective-permute-start | bytes 1376264 | tf_op jit(solution)/shard_map/ppermute | solution.py:22
  44.8 22.9 %collective-permute-start.3 = (bf16[1792,128]{1,0:T(8,128)(2,1)S(1)}, bf16[1792,128]{1,0:T(8,128)(2,1)S(1)}, u32[]{:S(2)}, u32[]{:S(2)}) collective-permute-start(bf16[1792,128]{1,0:T(8,128)(2,1)S(1)} %shard_map.42.refs_0_), channel_id=1, source_target_pairs={{0,2},{2,0},{1,3},{3,1},{4,6},{6,4},{5,7},{7,5},{8,10},{10,8},{9,1... | collective-permute-start | bytes 1376264 | tf_op jit(solution)/shard_map/ppermute | solution.py:22
  50.4 21.3 %collective-permute-start.16 = (bf16[1280,128]{1,0:T(8,128)(2,1)S(1)}, bf16[1280,128]{1,0:T(8,128)(2,1)S(1)}, u32[]{:S(2)}, u32[]{:S(2)}) collective-permute-start(bf16[1280,128]{1,0:T(8,128)(2,1)S(1)} %shard_map.54), channel_id=1, source_target_pairs={{0,8},{4,12},{8,0},{12,4},{1,9},{5,13},{9,1},{13,5},{2,10},{6,14},... | collective-permute-start | bytes 983048 | tf_op jit(solution)/shard_map/ppermute | solution.py:22
  56.8 16.4 %collective-permute-start.11 = (bf16[128,2048]{1,0:T(8,128)(2,1)S(1)}, bf16[128,2048]{1,0:T(8,128)(2,1)S(1)}, u32[]{:S(2)}, u32[]{:S(2)}) collective-permute-start(bf16[128,2048]{1,0:T(8,128)(2,1)S(1)} %shard_map.48.refs_0_), channel_id=1, source_target_pairs={{0,1},{1,0},{2,3},{3,2},{4,5},{5,4},{6,7},{7,6},{8,9},{9,8},{10,11... | collective-permute-start | bytes 1572872 | tf_op jit(solution)/shard_map/ppermute | solution.py:22
  56.9 24.6 %collective-permute-start.10 = (bf16[128,2048]{1,0:T(8,128)(2,1)S(1)}, bf16[128,2048]{1,0:T(8,128)(2,1)S(1)}, u32[]{:S(2)}, u32[]{:S(2)}) collective-permute-start(bf16[128,2048]{1,0:T(8,128)(2,1)S(1)} %shard_map.48.refs_0_), channel_id=1, source_target_pairs={{4,0},{8,12},{5,1},{9,13},{6,2},{10,14},{7,3},{11,15},{20,16},{24,... | collective-permute-start | bytes 1572872 | tf_op jit(solution)/shard_map/ppermute | solution.py:300
  58.2 19.7 %collective-permute-start.14 = (bf16[512,128]{1,0:T(8,128)(2,1)S(1)}, bf16[512,128]{1,0:T(8,128)(2,1)S(1)}, u32[]{:S(2)}, u32[]{:S(2)}) collective-permute-start(bf16[512,128]{1,0:T(8,128)(2,1)S(1)} %shard_map.52), channel_id=1, source_target_pairs={{0,8},{4,12},{8,0},{12,4},{1,9},{5,13},{9,1},{13,5},{2,10},{6,14},... | collective-permute-start | bytes 393224 | tf_op jit(solution)/shard_map/ppermute | solution.py:22
  71.7 9.9 %collective-permute-start.17 = (bf16[1280,128]{1,0:T(8,128)(2,1)S(1)}, bf16[1280,128]{1,0:T(8,128)(2,1)S(1)}, u32[]{:S(2)}, u32[]{:S(2)}) collective-permute-start(bf16[1280,128]{1,0:T(8,128)(2,1)S(1)} %shard_map.55.refs_0_), channel_id=1, source_target_pairs={{0,2},{2,0},{1,3},{3,1},{4,6},{6,4},{5,7},{7,5},{8,10},{10,8},{9,1... | collective-permute-start | bytes 983048 | tf_op jit(solution)/shard_map/ppermute | solution.py:22
  77.9 5.0 %collective-permute-start.15 = (bf16[512,128]{1,0:T(8,128)(2,1)S(1)}, bf16[512,128]{1,0:T(8,128)(2,1)S(1)}, u32[]{:S(2)}, u32[]{:S(2)}) collective-permute-start(bf16[512,128]{1,0:T(8,128)(2,1)S(1)} %shard_map.53.refs_0_), channel_id=1, source_target_pairs={{0,2},{2,0},{1,3},{3,1},{4,6},{6,4},{5,7},{7,5},{8,10},{10,8},{9,1... | collective-permute-start | bytes 393224 | tf_op jit(solution)/shard_map/ppermute | solution.py:22
  78.5 7.2 %collective-permute-start.7 = (f32[2,256]{1,0:T(2,128)S(1)}, f32[2,256]{1,0:T(2,128)S(1)}, u32[]{:S(2)}, u32[]{:S(2)}) collective-permute-start(f32[2,256]{1,0:T(2,128)S(1)} %shard_map.47.refs_3_.refs_1_), channel_id=1, source_target_pairs={{0,4},{4,0},{8,12},{12,8},{1,5},{5,1},{9,13},{13,9},{2,6},{6,2},{1... | collective-permute-start | bytes 6152 | tf_op jit(solution)/shard_map/ppermute | solution.py:22
  81.5 2.0 %collective-permute-start.12 = (bf16[128,2048]{1,0:T(8,128)(2,1)S(1)}, bf16[128,2048]{1,0:T(8,128)(2,1)S(1)}, u32[]{:S(2)}, u32[]{:S(2)}) collective-permute-start(bf16[128,2048]{1,0:T(8,128)(2,1)S(1)} %shard_map.50.refs_0_), channel_id=1, source_target_pairs={{0,1},{1,0},{2,3},{3,2},{4,5},{5,4},{6,7},{7,6},{8,9},{9,8},{10,11... | collective-permute-start | bytes 1572872 | tf_op jit(solution)/shard_map/ppermute | solution.py:22
  83.1 4.5 %collective-permute-start.18 = (f32[2,256]{1,0:T(2,128)S(1)}, f32[2,256]{1,0:T(2,128)S(1)}, u32[]{:S(2)}, u32[]{:S(2)}) collective-permute-start(f32[2,256]{1,0:T(2,128)S(1)} %shard_map.57), channel_id=1, source_target_pairs={{0,8},{4,12},{8,0},{12,4},{1,9},{5,13},{9,1},{13,5},{2,10},{6,14},... | collective-permute-start | bytes 6152 | tf_op jit(solution)/shard_map/ppermute | solution.py:22
  84.0 5.4 %collective-permute-start.13 = (f32[2,256]{1,0:T(2,128)S(1)}, f32[2,256]{1,0:T(2,128)S(1)}, u32[]{:S(2)}, u32[]{:S(2)}) collective-permute-start(f32[2,256]{1,0:T(2,128)S(1)} %shard_map.51), channel_id=1, source_target_pairs={{0,12},{4,8},{8,4},{12,0},{1,13},{5,9},{9,5},{13,1},{2,14},{6,10},... | collective-permute-start | bytes 6152 | tf_op jit(solution)/shard_map/ppermute | solution.py:22
  89.5 1.2 %collective-permute-start.19 = (f32[2,256]{1,0:T(2,128)S(1)}, f32[2,256]{1,0:T(2,128)S(1)}, u32[]{:S(2)}, u32[]{:S(2)}) collective-permute-start(f32[2,256]{1,0:T(2,128)S(1)} %add_add_fusion), channel_id=1, source_target_pairs={{0,1},{1,0},{2,3},{3,2},{4,5},{5,4},{6,7},{7,6},{8,9},{9,8},{10,11... | collective-permute-start | bytes 6152 | tf_op jit(solution)/shard_map/ppermute | solution.py:22
  90.7 3.6 %collective-permute-start.20 = (f32[2,256]{1,0:T(2,128)S(1)}, f32[2,256]{1,0:T(2,128)S(1)}, u32[]{:S(2)}, u32[]{:S(2)}) collective-permute-start(f32[2,256]{1,0:T(2,128)S(1)} %add.18), channel_id=1, source_target_pairs={{0,2},{2,0},{1,3},{3,1},{4,6},{6,4},{5,7},{7,5},{8,10},{10,8},{9,1... | collective-permute-start | bytes 6152 | tf_op jit(solution)/shard_map/ppermute | solution.py:22

commit v21 on v18

--- a/solution.py
+++ b/solution.py
@@ -165,17 +165,14 @@
     first = lax.axis_index("dout") * half if len(parts) > 1 else 0
     for part, at in zip(parts, (first, half - first)):
         acts[pl.ds(pl.multiple_of(at, half), half), :] = part[...]
-    nq, _, depth, _ = query_ref.shape
-    tile = depth // 2
-
-    def step(at, _):
-        q, rows = at // 2, pl.ds(pl.multiple_of(at % 2 * tile, tile), tile)
-        out_ref[q, rows, :] = lax.dot_general(
-            query_ref[q, 0, rows, :], acts[...], (((1,), (1,)), ((), ())), preferred_element_type=jnp.float32
+
+    def step(q, _):
+        out_ref[q] = lax.dot_general(
+            query_ref[q, 0], acts[...], (((1,), (1,)), ((), ())), preferred_element_type=jnp.float32
         )
         return 0
 
-    lax.fori_loop(0, 2 * nq, step, 0)
+    lax.fori_loop(0, query_ref.shape[0], step, 0)
 
 
 def mixed(parts, queries, flops, tokens=()):
@@ -207,17 +204,12 @@
     *parts, query_ref, out_ref, mark_ref, grads = refs
     mark_ref[...] = jnp.zeros_like(mark_ref)
     grads[...] = joined(parts, 0)
-    nq, _, _, width = query_ref.shape
-    tile = width // 2
-
-    def step(at, _):
-        q, columns = at // 2, pl.ds(pl.multiple_of(at % 2 * tile, tile), tile)
-        out_ref[q, :, columns] = jnp.dot(
-            grads[...], query_ref[q, 0, :, columns], preferred_element_type=jnp.float32
-        )
+
+    def step(q, _):
+        out_ref[q] = jnp.dot(grads[...], query_ref[q, 0], preferred_element_type=jnp.float32)
         return 0
 
-    lax.fori_loop(0, 2 * nq, step, 0)
+    lax.fori_loop(0, query_ref.shape[0], step, 0)
 
 
 def projected(parts, queries, flops, tokens=()):

time: 92.8 us -> 92.8 us (level)
  waiting for transfers between devices: 33.9 us -> 36 us
  Pallas kernels: 28.5 us -> 27.3 us
    ppermute x16, waiting for transfers between devices: 28.5 us -> 30.2 us  [trade(): return lax.ppermute(block, axes, route[::-1] if backwards else route)]
    pallas_call x11, Pallas kernels: 21.2 us -> 20 us  [call(): pl.pallas_call(body, in_specs=[NEAR] * len(arrays) + [ANYWHERE] * skip, o...]
  transfers between devices with their start and end apart: 21 -> 21, of which waited for: 12 -> 12; matrix products, arithmetic and copies ran while one was open for 0% -> 0% of each run, Pallas kernels for 30% -> 28%
where the time goes in v21:
time: 92.8 us; the launch traced here: 92.6 us
  waiting for transfers between devices  36 us (39%)
  starting transfers between devices  28.5 us (31%)
  Pallas kernels  27.3 us (29%)
    ppermute x16, waiting for transfers between devices, trade(): return lax.ppermute(block, axes, route[::-1] if backwards else route)  30.2 us
    pallas_call x11, Pallas kernels, call(): pl.pallas_call(body, in_specs=[NEAR] * len(arrays) + [ANYWHERE] * skip, o...  20 us
    ppermute x16, starting transfers between devices, trade(): return lax.ppermute(block, axes, route[::-1] if backwards else route)  18.9 us
    pallas_call x2, Pallas kernels, fetch(): pl.pallas_call(kernel, in_specs=[ANYWHERE] * len(arrays), out_specs=[NEAR...  7.3 us
    ppermute x2, starting transfers between devices, pass_on(): lax.ppermute(block[0], 'dp', [(i, i + 1) for i in range(step - 1, count -...  5.65 us
    ppermute x1, waiting for transfers between devices, on_device(): end = lax.ppermute(block, 'dp', [(1, 0), (count - 2, count - 1)])  4.69 us
    ppermute x2, starting transfers between devices, pass_on(): lax.ppermute(block[1], 'dp', [(i, i - 1) for i in range(1, count - step +...  2.58 us
  transfers between devices with their start and end apart: 21, of which 12 were waited for; matrix products, arithmetic and copies ran while one was open for 0% of the time, Pallas kernels for 28%

profile of v21, /device:TPU:0, one launch (start us, length us, event | category | flops | bytes accessed | tf_op | source)
XLA Modules:
  0.0 92.6 jit_solution(1736609319795620532)
XLA Ops:
  0.0 1.2 %shard_map.40 = (bf16[128,2048]{1,0:T(8,128)(2,1)S(1)}, bf16[128,1792]{1,0:T(8,128)(2,1)S(1)}) custom-call(bf16[256,2048]{1,0:T(8,128)(2,1)} %acts_ref.3, bf16[256,7168]{1,0:T(8,128)(2,1)} %grads_ref.3), custom_call_target="tpu_custom_call" | custom-call | flops 1024 | bytes 1024 | tf_op jit(solution)/shard_map/pallas_call | solution.py:53
  1.2 5.0 %collective-permute-start.1 = (bf16[128,2048]{1,0:T(8,128)(2,1)S(1)}, bf16[128,2048]{1,0:T(8,128)(2,1)S(1)}, u32[]{:S(2)}, u32[]{:S(2)}) collective-permute-start(bf16[128,2048]{1,0:T(8,128)(2,1)S(1)} %get-tuple-element.28), channel_id=1, source_target_pairs={{0,4},{4,8},{8,12},{1,5},{5,9},{9,13},{2,6},{6,10},{10,14},{3,7},{... | collective-permute-start | bytes 1572872 | tf_op jit(solution)/shard_map/ppermute | solution.py:26
  6.2 1.3 %collective-permute-start.2 = (bf16[128,2048]{1,0:T(8,128)(2,1)S(1)}, bf16[128,2048]{1,0:T(8,128)(2,1)S(1)}, u32[]{:S(2)}, u32[]{:S(2)}) collective-permute-start(bf16[128,2048]{1,0:T(8,128)(2,1)S(1)} %get-tuple-element.28), channel_id=1, source_target_pairs={{4,0},{8,4},{12,8},{5,1},{9,5},{13,9},{6,2},{10,6},{14,10},{7,3},{... | collective-permute-start | bytes 1572872 | tf_op jit(solution)/shard_map/ppermute | solution.py:27
  7.5 4.7 %collective-permute-start.5 = (bf16[128,1792]{1,0:T(8,128)(2,1)S(1)}, bf16[128,1792]{1,0:T(8,128)(2,1)S(1)}, u32[]{:S(2)}, u32[]{:S(2)}) collective-permute-start(bf16[128,1792]{1,0:T(8,128)(2,1)S(1)} %get-tuple-element.33), channel_id=1, source_target_pairs={{0,12},{4,8},{8,4},{12,0},{1,13},{5,9},{9,5},{13,1},{2,14},{6,10},... | collective-permute-start | bytes 1376264 | tf_op jit(solution)/shard_map/ppermute | solution.py:22
  12.2 6.1 %shard_map.37 = (bf16[2,1,1792,2048]{3,2,1,0:T(8,128)(2,1)S(1)}, bf16[256,2048]{1,0:T(8,128)(2,1)S(1)}, bf16[1792,256]{1,0:T(8,128)(2,1)S(1)}, bf16[1792,128]{1,...) custom-call(bf16[256,2048]{1,0:T(8,128)(2,1)} %acts_ref.3, bf16[256,7168]{1,0:T(8,128)(2,1)} %grads_ref.3, ...), custom_call_target="tpu_custom_call" | custom-call | flops 1024 | bytes 1024 | tf_op jit(solution)/shard_map/pallas_call | solution.py:53
  18.4 4.4 %shard_map.38 = (f32[2,1792,256]{2,1,0:T(8,128)S(1)}, f32[8,128]{1,0:T(8,128)S(1)}) custom-call(bf16[256,2048]{1,0:T(8,128)(2,1)S(1)} %get-tuple-element.24.refs_0_, bf16[2,1,1792,2048]{3,2,1,0:T(8,128)(2,1)S(1)} %get-tuple-element.25.refs_1_.refs_2_), custom_call_target="tpu_custom_call" | custom-call | flops 1000000 | bytes 1024 | tf_op jit(solution)/shard_map/pallas_call | solution.py:41
  22.8 1.0 %collective-permute-done.2.refs_1_ = bf16[128,2048]{1,0:T(8,128)(2,1)S(1)} collective-permute-done((bf16[128,2048]{1,0:T(8,128)(2,1)S(1)}, bf16[128,2048]{1,0:T(8,128)(2,1)S(1)}, u32[]{:S(2)}, u32[]{:S(2)}) %collective-permute-start.2) | collective-permute-done | bytes 524320 | tf_op jit(solution)/shard_map/ppermute | solution.py:27
  24.0 1.3 %collective-permute-start.8 = (bf16[128,2048]{1,0:T(8,128)(2,1)S(1)}, bf16[128,2048]{1,0:T(8,128)(2,1)S(1)}, u32[]{:S(2)}, u32[]{:S(2)}) collective-permute-start(bf16[128,2048]{1,0:T(8,128)(2,1)S(1)} %get-tuple-element.31.refs_2_.refs_0_.refs_1_), channel_id=1, source_target_pairs={{4,0},{8,4},{5,1},{9,5},{6,2},{10,6},{7,3},{11,7},{20,16},{24,20},... | collective-permute-start | bytes 1572872 | tf_op jit(solution)/shard_map/ppermute | solution.py:27
  25.3 0.7 collective-permute-start.9
  26.0 8.8 %collective-permute-done.5.refs_0_ = bf16[128,1792]{1,0:T(8,128)(2,1)S(1)} collective-permute-done((bf16[128,1792]{1,0:T(8,128)(2,1)S(1)}, bf16[128,1792]{1,0:T(8,128)(2,1)S(1)}, u32[]{:S(2)}, u32[]{:S(2)}) %collective-permute-start.5) | collective-permute-done | bytes 458784 | tf_op jit(solution)/shard_map/ppermute | solution.py:22
  34.8 7.8 %collective-permute-done.refs_0_.refs_3_ = bf16[1792,128]{1,0:T(8,128)(2,1)S(1)} collective-permute-done((bf16[1792,128]{1,0:T(8,128)(2,1)S(1)}, bf16[1792,128]{1,0:T(8,128)(2,1)S(1)}, u32[]{:S(2)}, u32[]{:S(2)}) %collective-permute-start) | collective-permute-done | bytes 458784 | tf_op jit(solution)/shard_map/ppermute | solution.py:22
  42.6 1.5 %collective-permute-start.6 = (bf16[128,1792]{1,0:T(8,128)(2,1)S(1)}, bf16[128,1792]{1,0:T(8,128)(2,1)S(1)}, u32[]{:S(2)}, u32[]{:S(2)}) collective-permute-start(bf16[128,1792]{1,0:T(8,128)(2,1)S(1)} %shard_map.45.refs_0_.refs_3_), channel_id=1, source_target_pairs={{0,2},{2,0},{1,3},{3,1},{4,6},{6,4},{5,7},{7,5},{8,10},{10,8},{9,1... | collective-permute-start | bytes 1376264 | tf_op jit(solution)/shard_map/ppermute | solution.py:22
  45.0 4.4 %shard_map.44 = (f32[2,1792,256]{2,1,0:T(8,128)S(1)}, f32[8,128]{1,0:T(8,128)S(1)}) custom-call(bf16[128,2048]{1,0:T(8,128)(2,1)S(1)} %shard_map.43.refs_0_, bf16[128,2048]{1,0:T(8,128)(2,1)S(1)} %collective-permute-done.4.refs_1_, bf16[2,1,1792,2048]{3,2,1,0:T(8,128)(2,1)S(1)} %get-tuple-element.25.refs_1_.refs_2_, f32[2,256]{1,0:T(2,128)S(1)} %shard_map.39.refs_3_), custom_call_target="tpu_custom_call" | custom-call | flops 1000000 | bytes 1024 | tf_op jit(solution)/shard_map/pallas_call | solution.py:41
  49.4 1.2 %collective-permute-start.14 = (bf16[896,128]{1,0:T(8,128)(2,1)S(1)}, bf16[896,128]{1,0:T(8,128)(2,1)S(1)}, u32[]{:S(2)}, u32[]{:S(2)}) collective-permute-start(bf16[896,128]{1,0:T(8,128)(2,1)S(1)} %shard_map.52), channel_id=1, source_target_pairs={{0,8},{4,12},{8,0},{12,4},{1,9},{5,13},{9,1},{13,5},{2,10},{6,14},... | collective-permute-start | bytes 688136 | tf_op jit(solution)/shard_map/ppermute | solution.py:22
  50.6 5.4 %collective-permute-done.6.refs_1_.refs_4_ = bf16[128,1792]{1,0:T(8,128)(2,1)S(1)} collective-permute-done((bf16[128,1792]{1,0:T(8,128)(2,1)S(1)}, bf16[128,1792]{1,0:T(8,128)(2,1)S(1)}, u32[]{:S(2)}, u32[]{:S(2)}) %collective-permute-start.6) | collective-permute-done | bytes 458784 | tf_op jit(solution)/shard_map/ppermute | solution.py:22
  56.2 1.3 %collective-permute-start.10 = (bf16[128,2048]{1,0:T(8,128)(2,1)S(1)}, bf16[128,2048]{1,0:T(8,128)(2,1)S(1)}, u32[]{:S(2)}, u32[]{:S(2)}) collective-permute-start(bf16[128,2048]{1,0:T(8,128)(2,1)S(1)} %shard_map.48.refs_0_), channel_id=1, source_target_pairs={{4,0},{8,12},{5,1},{9,13},{6,2},{10,14},{7,3},{11,15},{20,16},{24,... | collective-permute-start | bytes 1572872 | tf_op jit(solution)/shard_map/ppermute | solution.py:293
  57.5 3.3 %collective-permute-start.15 = (bf16[896,128]{1,0:T(8,128)(2,1)S(1)}, bf16[896,128]{1,0:T(8,128)(2,1)S(1)}, u32[]{:S(2)}, u32[]{:S(2)}) collective-permute-start(bf16[896,128]{1,0:T(8,128)(2,1)S(1)} %shard_map.54), channel_id=1, source_target_pairs={{0,8},{4,12},{8,0},{12,4},{1,9},{5,13},{9,1},{13,5},{2,10},{6,14},... | collective-permute-start | bytes 688136 | tf_op jit(solution)/shard_map/ppermute | solution.py:22
  60.8 4.4 %shard_map.46 = (f32[2,256,2048]{2,1,0:T(8,128)S(1)}, f32[8,128]{1,0:T(8,128)S(1)}) custom-call(bf16[128,1792]{1,0:T(8,128)(2,1)S(1)} %shard_map.45.refs_0_.refs_3_, bf16[128,1792]{1,0:T(8,128)(2,1)S(1)} %collective-permute-done.6.refs_1_.refs_4_, bf16[2,1,1792,2048]{3,2,1,0:T(8,128)(2,1)S(1)} %get-tuple-element.25.refs_1_.refs_2_, ...), custom_call_target="tpu_custom_call" | custom-call | flops 1000000 | bytes 1024 | tf_op jit(solution)/shard_map/pallas_call | solution.py:41
  65.2 0.8 shard_map.47.refs_3_.refs_1_
  66.0 1.6 %collective-permute-start.16 = (bf16[896,128]{1,0:T(8,128)(2,1)S(1)}, bf16[896,128]{1,0:T(8,128)(2,1)S(1)}, u32[]{:S(2)}, u32[]{:S(2)}) collective-permute-start(bf16[896,128]{1,0:T(8,128)(2,1)S(1)} %shard_map.53.refs_0_), channel_id=1, source_target_pairs={{0,2},{2,0},{1,3},{3,1},{4,6},{6,4},{5,7},{7,5},{8,10},{10,8},{9,1... | collective-permute-start | bytes 688136 | tf_op jit(solution)/shard_map/ppermute | solution.py:22
  67.5 4.4 %shard_map.49 = (f32[2,1792,256]{2,1,0:T(8,128)S(1)}, f32[8,128]{1,0:T(8,128)S(1)}) custom-call(bf16[128,2048]{1,0:T(8,128)(2,1)S(1)} %shard_map.48.refs_0_, bf16[128,2048]{1,0:T(8,128)(2,1)S(1)} %collective-permute-done.11.refs_1_, bf16[2,1,1792,2048]{3,2,1,0:T(8,128)(2,1)S(1)} %get-tuple-element.25.refs_1_.refs_2_, f32[2,256]{1,0:T(2,128)S(1)} %shard_map.47.refs_3_.refs_1_), custom_call_target="tpu_custom_call" | custom-call | flops 1000000 | bytes 1024 | tf_op jit(solution)/shard_map/pallas_call | solution.py:41
  71.9 1.2 %collective-permute-done.15.refs_0_ = bf16[896,128]{1,0:T(8,128)(2,1)S(1)} collective-permute-done((bf16[896,128]{1,0:T(8,128)(2,1)S(1)}, bf16[896,128]{1,0:T(8,128)(2,1)S(1)}, u32[]{:S(2)}, u32[]{:S(2)}) %collective-permute-start.15) | collective-permute-done | bytes 229408 | tf_op jit(solution)/shard_map/ppermute | solution.py:22
  73.1 1.5 %collective-permute-start.17 = (bf16[896,128]{1,0:T(8,128)(2,1)S(1)}, bf16[896,128]{1,0:T(8,128)(2,1)S(1)}, u32[]{:S(2)}, u32[]{:S(2)}) collective-permute-start(bf16[896,128]{1,0:T(8,128)(2,1)S(1)} %shard_map.55.refs_1_), channel_id=1, source_target_pairs={{0,2},{2,0},{1,3},{3,1},{4,6},{6,4},{5,7},{7,5},{8,10},{10,8},{9,1... | collective-permute-start | bytes 688136 | tf_op jit(solution)/shard_map/ppermute | solution.py:22
  74.6 4.7 %collective-permute-done.10.refs_0_ = bf16[128,2048]{1,0:T(8,128)(2,1)S(1)} collective-permute-done((bf16[128,2048]{1,0:T(8,128)(2,1)S(1)}, bf16[128,2048]{1,0:T(8,128)(2,1)S(1)}, u32[]{:S(2)}, u32[]{:S(2)}) %collective-permute-start.10) | collective-permute-done | bytes 524320 | tf_op jit(solution)/shard_map/ppermute | solution.py:293
  79.7 0.7 shard_map.56
  80.5 0.8 collective-permute-done.12.refs_1_
  81.8 2.7 %collective-permute-start.13 = (f32[2,256]{1,0:T(2,128)S(1)}, f32[2,256]{1,0:T(2,128)S(1)}, u32[]{:S(2)}, u32[]{:S(2)}) collective-permute-start(f32[2,256]{1,0:T(2,128)S(1)} %shard_map.51), channel_id=1, source_target_pairs={{0,12},{4,8},{8,4},{12,0},{1,13},{5,9},{9,5},{13,1},{2,14},{6,10},... | collective-permute-start | bytes 6152 | tf_op jit(solution)/shard_map/ppermute | solution.py:22
  85.0 2.3 %collective-permute-done.13 = f32[2,256]{1,0:T(2,128)S(1)} collective-permute-done((f32[2,256]{1,0:T(2,128)S(1)}, f32[2,256]{1,0:T(2,128)S(1)}, u32[]{:S(2)}, u32[]{:S(2)}) %collective-permute-start.13) | collective-permute-done | bytes 2080 | tf_op jit(solution)/shard_map/ppermute | solution.py:22
  87.3 1.2 %collective-permute-done.19 = f32[2,256]{1,0:T(2,128)S(1)} collective-permute-done((f32[2,256]{1,0:T(2,128)S(1)}, f32[2,256]{1,0:T(2,128)S(1)}, u32[]{:S(2)}, u32[]{:S(2)}) %collective-permute-start.19) | collective-permute-done | bytes 2080 | tf_op jit(solution)/shard_map/ppermute | solution.py:22
  88.4 1.5 %collective-permute-start.20 = (f32[2,256]{1,0:T(2,128)S(1)}, f32[2,256]{1,0:T(2,128)S(1)}, u32[]{:S(2)}, u32[]{:S(2)}) collective-permute-start(f32[2,256]{1,0:T(2,128)S(1)} %add.18), channel_id=1, source_target_pairs={{0,2},{2,0},{1,3},{3,1},{4,6},{6,4},{5,7},{7,5},{8,10},{10,8},{9,1... | collective-permute-start | bytes 6152 | tf_op jit(solution)/shard_map/ppermute | solution.py:22
  89.9 2.1 %collective-permute-done.20 = f32[2,256]{1,0:T(2,128)S(1)} collective-permute-done((f32[2,256]{1,0:T(2,128)S(1)}, f32[2,256]{1,0:T(2,128)S(1)}, u32[]{:S(2)}, u32[]{:S(2)}) %collective-permute-start.20) | collective-permute-done | bytes 2080 | tf_op jit(solution)/shard_map/ppermute | solution.py:22
  92.0 0.6 add.19
  (33 shorter events, 2.8 us)
Async XLA Ops:
  1.2 21.6 %collective-permute-start.1 = (bf16[128,2048]{1,0:T(8,128)(2,1)S(1)}, bf16[128,2048]{1,0:T(8,128)(2,1)S(1)}, u32[]{:S(2)}, u32[]{:S(2)}) collective-permute-start(bf16[128,2048]{1,0:T(8,128)(2,1)S(1)} %get-tuple-element.28), channel_id=1, source_target_pairs={{0,4},{4,8},{8,12},{1,5},{5,9},{9,13},{2,6},{6,10},{10,14},{3,7},{... | collective-permute-start | bytes 1572872 | tf_op jit(solution)/shard_map/ppermute | solution.py:26
  6.2 17.7 %collective-permute-start.2 = (bf16[128,2048]{1,0:T(8,128)(2,1)S(1)}, bf16[128,2048]{1,0:T(8,128)(2,1)S(1)}, u32[]{:S(2)}, u32[]{:S(2)}) collective-permute-start(bf16[128,2048]{1,0:T(8,128)(2,1)S(1)} %get-tuple-element.28), channel_id=1, source_target_pairs={{4,0},{8,4},{12,8},{5,1},{9,5},{13,9},{6,2},{10,6},{14,10},{7,3},{... | collective-permute-start | bytes 1572872 | tf_op jit(solution)/shard_map/ppermute | solution.py:27
  7.5 27.3 %collective-permute-start.5 = (bf16[128,1792]{1,0:T(8,128)(2,1)S(1)}, bf16[128,1792]{1,0:T(8,128)(2,1)S(1)}, u32[]{:S(2)}, u32[]{:S(2)}) collective-permute-start(bf16[128,1792]{1,0:T(8,128)(2,1)S(1)} %get-tuple-element.33), channel_id=1, source_target_pairs={{0,12},{4,8},{8,4},{12,0},{1,13},{5,9},{9,5},{13,1},{2,14},{6,10},... | collective-permute-start | bytes 1376264 | tf_op jit(solution)/shard_map/ppermute | solution.py:22
  18.3 24.3 %collective-permute-start = (bf16[1792,128]{1,0:T(8,128)(2,1)S(1)}, bf16[1792,128]{1,0:T(8,128)(2,1)S(1)}, u32[]{:S(2)}, u32[]{:S(2)}) collective-permute-start(bf16[1792,128]{1,0:T(8,128)(2,1)S(1)} %get-tuple-element.27), channel_id=1, source_target_pairs={{0,4},{4,0},{8,12},{12,8},{1,5},{5,1},{9,13},{13,9},{2,6},{6,2},{1... | collective-permute-start | bytes 1376264 | tf_op jit(solution)/shard_map/ppermute | solution.py:22
  23.9 21.1 %collective-permute-start.4 = (bf16[128,2048]{1,0:T(8,128)(2,1)S(1)}, bf16[128,2048]{1,0:T(8,128)(2,1)S(1)}, u32[]{:S(2)}, u32[]{:S(2)}) collective-permute-start(bf16[128,2048]{1,0:T(8,128)(2,1)S(1)} %shard_map.43.refs_0_), channel_id=1, source_target_pairs={{0,1},{1,0},{2,3},{3,2},{4,5},{5,4},{6,7},{7,6},{8,9},{9,8},{10,11... | collective-permute-start | bytes 1572872 | tf_op jit(solution)/shard_map/ppermute | solution.py:22
  24.0 32.1 %collective-permute-start.8 = (bf16[128,2048]{1,0:T(8,128)(2,1)S(1)}, bf16[128,2048]{1,0:T(8,128)(2,1)S(1)}, u32[]{:S(2)}, u32[]{:S(2)}) collective-permute-start(bf16[128,2048]{1,0:T(8,128)(2,1)S(1)} %get-tuple-element.31.refs_2_.refs_0_.refs_1_), channel_id=1, source_target_pairs={{4,0},{8,4},{5,1},{9,5},{6,2},{10,6},{7,3},{11,7},{20,16},{24,20},... | collective-permute-start | bytes 1572872 | tf_op jit(solution)/shard_map/ppermute | solution.py:27
  25.3 30.8 %collective-permute-start.9 = (bf16[128,2048]{1,0:T(8,128)(2,1)S(1)}, bf16[128,2048]{1,0:T(8,128)(2,1)S(1)}, u32[]{:S(2)}, u32[]{:S(2)}) collective-permute-start(bf16[128,2048]{1,0:T(8,128)(2,1)S(1)} %get-tuple-element.30.refs_1_.refs_2_), channel_id=1, source_target_pairs={{4,8},{8,12},{5,9},{9,13},{6,10},{10,14},{7,11},{11,15},{20,24},{2... | collective-permute-start | bytes 1572872 | tf_op jit(solution)/shard_map/ppermute | solution.py:26
  42.6 13.5 %collective-permute-start.6 = (bf16[128,1792]{1,0:T(8,128)(2,1)S(1)}, bf16[128,1792]{1,0:T(8,128)(2,1)S(1)}, u32[]{:S(2)}, u32[]{:S(2)}) collective-permute-start(bf16[128,1792]{1,0:T(8,128)(2,1)S(1)} %shard_map.45.refs_0_.refs_3_), channel_id=1, source_target_pairs={{0,2},{2,0},{1,3},{3,1},{4,6},{6,4},{5,7},{7,5},{8,10},{10,8},{9,1... | collective-permute-start | bytes 1376264 | tf_op jit(solution)/shard_map/ppermute | solution.py:22
  44.1 21.2 %collective-permute-start.3 = (bf16[1792,128]{1,0:T(8,128)(2,1)S(1)}, bf16[1792,128]{1,0:T(8,128)(2,1)S(1)}, u32[]{:S(2)}, u32[]{:S(2)}) collective-permute-start(bf16[1792,128]{1,0:T(8,128)(2,1)S(1)} %shard_map.42.refs_0_), channel_id=1, source_target_pairs={{0,2},{2,0},{1,3},{3,1},{4,6},{6,4},{5,7},{7,5},{8,10},{10,8},{9,1... | collective-permute-start | bytes 1376264 | tf_op jit(solution)/shard_map/ppermute | solution.py:22
  49.4 16.5 %collective-permute-start.14 = (bf16[896,128]{1,0:T(8,128)(2,1)S(1)}, bf16[896,128]{1,0:T(8,128)(2,1)S(1)}, u32[]{:S(2)}, u32[]{:S(2)}) collective-permute-start(bf16[896,128]{1,0:T(8,128)(2,1)S(1)} %shard_map.52), channel_id=1, source_target_pairs={{0,8},{4,12},{8,0},{12,4},{1,9},{5,13},{9,1},{13,5},{2,10},{6,14},... | collective-permute-start | bytes 688136 | tf_op jit(solution)/shard_map/ppermute | solution.py:22
  56.1 11.5 %collective-permute-start.11 = (bf16[128,2048]{1,0:T(8,128)(2,1)S(1)}, bf16[128,2048]{1,0:T(8,128)(2,1)S(1)}, u32[]{:S(2)}, u32[]{:S(2)}) collective-permute-start(bf16[128,2048]{1,0:T(8,128)(2,1)S(1)} %shard_map.48.refs_0_), channel_id=1, source_target_pairs={{0,1},{1,0},{2,3},{3,2},{4,5},{5,4},{6,7},{7,6},{8,9},{9,8},{10,11... | collective-permute-start | bytes 1572872 | tf_op jit(solution)/shard_map/ppermute | solution.py:22
  56.2 23.2 %collective-permute-start.10 = (bf16[128,2048]{1,0:T(8,128)(2,1)S(1)}, bf16[128,2048]{1,0:T(8,128)(2,1)S(1)}, u32[]{:S(2)}, u32[]{:S(2)}) collective-permute-start(bf16[128,2048]{1,0:T(8,128)(2,1)S(1)} %shard_map.48.refs_0_), channel_id=1, source_target_pairs={{4,0},{8,12},{5,1},{9,13},{6,2},{10,14},{7,3},{11,15},{20,16},{24,... | collective-permute-start | bytes 1572872 | tf_op jit(solution)/shard_map/ppermute | solution.py:293
  57.5 15.7 %collective-permute-start.15 = (bf16[896,128]{1,0:T(8,128)(2,1)S(1)}, bf16[896,128]{1,0:T(8,128)(2,1)S(1)}, u32[]{:S(2)}, u32[]{:S(2)}) collective-permute-start(bf16[896,128]{1,0:T(8,128)(2,1)S(1)} %shard_map.54), channel_id=1, source_target_pairs={{0,8},{4,12},{8,0},{12,4},{1,9},{5,13},{9,1},{13,5},{2,10},{6,14},... | collective-permute-start | bytes 688136 | tf_op jit(solution)/shard_map/ppermute | solution.py:22
  66.0 13.5 %collective-permute-start.16 = (bf16[896,128]{1,0:T(8,128)(2,1)S(1)}, bf16[896,128]{1,0:T(8,128)(2,1)S(1)}, u32[]{:S(2)}, u32[]{:S(2)}) collective-permute-start(bf16[896,128]{1,0:T(8,128)(2,1)S(1)} %shard_map.53.refs_0_), channel_id=1, source_target_pairs={{0,2},{2,0},{1,3},{3,1},{4,6},{6,4},{5,7},{7,5},{8,10},{10,8},{9,1... | collective-permute-start | bytes 688136 | tf_op jit(solution)/shard_map/ppermute | solution.py:22
  73.1 6.6 %collective-permute-start.17 = (bf16[896,128]{1,0:T(8,128)(2,1)S(1)}, bf16[896,128]{1,0:T(8,128)(2,1)S(1)}, u32[]{:S(2)}, u32[]{:S(2)}) collective-permute-start(bf16[896,128]{1,0:T(8,128)(2,1)S(1)} %shard_map.55.refs_1_), channel_id=1, source_target_pairs={{0,2},{2,0},{1,3},{3,1},{4,6},{6,4},{5,7},{7,5},{8,10},{10,8},{9,1... | collective-permute-start | bytes 688136 | tf_op jit(solution)/shard_map/ppermute | solution.py:22
  74.6 9.8 %collective-permute-start.7 = (f32[2,256]{1,0:T(2,128)S(1)}, f32[2,256]{1,0:T(2,128)S(1)}, u32[]{:S(2)}, u32[]{:S(2)}) collective-permute-start(f32[2,256]{1,0:T(2,128)S(1)} %shard_map.47.refs_3_.refs_1_), channel_id=1, source_target_pairs={{0,4},{4,0},{8,12},{12,8},{1,5},{5,1},{9,13},{13,9},{2,6},{6,2},{1... | collective-permute-start | bytes 6152 | tf_op jit(solution)/shard_map/ppermute | solution.py:22
  79.4 2.0 %collective-permute-start.12 = (bf16[128,2048]{1,0:T(8,128)(2,1)S(1)}, bf16[128,2048]{1,0:T(8,128)(2,1)S(1)}, u32[]{:S(2)}, u32[]{:S(2)}) collective-permute-start(bf16[128,2048]{1,0:T(8,128)(2,1)S(1)} %shard_map.50.refs_0_), channel_id=1, source_target_pairs={{0,1},{1,0},{2,3},{3,2},{4,5},{5,4},{6,7},{7,6},{8,9},{9,8},{10,11... | collective-permute-start | bytes 1572872 | tf_op jit(solution)/shard_map/ppermute | solution.py:22
  80.4 4.5 %collective-permute-start.18 = (f32[2,256]{1,0:T(2,128)S(1)}, f32[2,256]{1,0:T(2,128)S(1)}, u32[]{:S(2)}, u32[]{:S(2)}) collective-permute-start(f32[2,256]{1,0:T(2,128)S(1)} %shard_map.56), channel_id=1, source_target_pairs={{0,8},{4,12},{8,0},{12,4},{1,9},{5,13},{9,1},{13,5},{2,10},{6,14},... | collective-permute-start | bytes 6152 | tf_op jit(solution)/shard_map/ppermute | solution.py:22
  81.8 5.4 %collective-permute-start.13 = (f32[2,256]{1,0:T(2,128)S(1)}, f32[2,256]{1,0:T(2,128)S(1)}, u32[]{:S(2)}, u32[]{:S(2)}) collective-permute-start(f32[2,256]{1,0:T(2,128)S(1)} %shard_map.51), channel_id=1, source_target_pairs={{0,12},{4,8},{8,4},{12,0},{1,13},{5,9},{9,5},{13,1},{2,14},{6,10},... | collective-permute-start | bytes 6152 | tf_op jit(solution)/shard_map/ppermute | solution.py:22
  87.3 1.2 %collective-permute-start.19 = (f32[2,256]{1,0:T(2,128)S(1)}, f32[2,256]{1,0:T(2,128)S(1)}, u32[]{:S(2)}, u32[]{:S(2)}) collective-permute-start(f32[2,256]{1,0:T(2,128)S(1)} %add_add_fusion), channel_id=1, source_target_pairs={{0,1},{1,0},{2,3},{3,2},{4,5},{5,4},{6,7},{7,6},{8,9},{9,8},{10,11... | collective-permute-start | bytes 6152 | tf_op jit(solution)/shard_map/ppermute | solution.py:22
  88.4 3.6 %collective-permute-start.20 = (f32[2,256]{1,0:T(2,128)S(1)}, f32[2,256]{1,0:T(2,128)S(1)}, u32[]{:S(2)}, u32[]{:S(2)}) collective-permute-start(f32[2,256]{1,0:T(2,128)S(1)} %add.18), channel_id=1, source_target_pairs={{0,2},{2,0},{1,3},{3,1},{4,6},{6,4},{5,7},{7,5},{8,10},{10,8},{9,1... | collective-permute-start | bytes 6152 | tf_op jit(solution)/shard_map/ppermute | solution.py:22

commit v22 on v21

--- a/solution.py
+++ b/solution.py
@@ -309,8 +309,8 @@
 
 
 def over_chips(scores, spread):
-    scores = scores + trade(scores, {"dout": 1})
-    return scores + sum(trade(scores, {"din": r}) for r in range(1, spread))
+    others = [(r, c) for r in range(spread) for c in range(2)][1:]
+    return scores + sum(trade(scores, {"din": r, "dout": c}) for r, c in others)
 
 
 def solution(mesh):

time: 92.8 us -> 93.2 us (level)
    ppermute x16 -> x17, starting transfers between devices: 18.9 us -> 19.6 us  [trade(): return lax.ppermute(block, axes, route[::-1] if backwards else route)]
    ppermute x16 -> x17, waiting for transfers between devices: 30.2 us -> 30 us  [trade(): return lax.ppermute(block, axes, route[::-1] if backwards else route)]
  transfers between devices with their start and end apart: 21 -> 22, of which waited for: 12 -> 12; matrix products, arithmetic and copies ran while one was open for 0% -> 0% of each run, Pallas kernels for 28% -> 28%
where the time goes in v22:
time: 93.2 us; the launch traced here: 93 us
  waiting for transfers between devices  35.8 us (38%)
  starting transfers between devices  29.1 us (31%)
  Pallas kernels  27.3 us (29%)
    ppermute x17, waiting for transfers between devices, trade(): return lax.ppermute(block, axes, route[::-1] if backwards else route)  30 us
    pallas_call x11, Pallas kernels, call(): pl.pallas_call(body, in_specs=[NEAR] * len(arrays) + [ANYWHERE] * skip, o...  20 us
    ppermute x17, starting transfers between devices, trade(): return lax.ppermute(block, axes, route[::-1] if backwards else route)  19.6 us
    pallas_call x2, Pallas kernels, fetch(): pl.pallas_call(kernel, in_specs=[ANYWHERE] * len(arrays), out_specs=[NEAR...  7.3 us
    ppermute x2, starting transfers between devices, pass_on(): lax.ppermute(block[0], 'dp', [(i, i + 1) for i in range(step - 1, count -...  5.65 us
    ppermute x1, waiting for transfers between devices, on_device(): end = lax.ppermute(block, 'dp', [(1, 0), (count - 2, count - 1)])  4.69 us
    ppermute x2, starting transfers between devices, pass_on(): lax.ppermute(block[1], 'dp', [(i, i - 1) for i in range(1, count - step +...  2.58 us
  transfers between devices with their start and end apart: 22, of which 12 were waited for; matrix products, arithmetic and copies ran while one was open for 0% of the time, Pallas kernels for 28%

profile of v22, /device:TPU:0, one launch (start us, length us, event | category | flops | bytes accessed | tf_op | source)
XLA Modules:
  0.0 93.0 jit_solution(16701408738087477841)
XLA Ops:
  0.0 1.2 %shard_map.40 = (bf16[128,2048]{1,0:T(8,128)(2,1)S(1)}, bf16[128,1792]{1,0:T(8,128)(2,1)S(1)}) custom-call(bf16[256,2048]{1,0:T(8,128)(2,1)} %acts_ref.3, bf16[256,7168]{1,0:T(8,128)(2,1)} %grads_ref.3), custom_call_target="tpu_custom_call" | custom-call | flops 1024 | bytes 1024 | tf_op jit(solution)/shard_map/pallas_call | solution.py:53
  1.2 5.0 %collective-permute-start.1 = (bf16[128,2048]{1,0:T(8,128)(2,1)S(1)}, bf16[128,2048]{1,0:T(8,128)(2,1)S(1)}, u32[]{:S(2)}, u32[]{:S(2)}) collective-permute-start(bf16[128,2048]{1,0:T(8,128)(2,1)S(1)} %get-tuple-element.28), channel_id=1, source_target_pairs={{0,4},{4,8},{8,12},{1,5},{5,9},{9,13},{2,6},{6,10},{10,14},{3,7},{... | collective-permute-start | bytes 1572872 | tf_op jit(solution)/shard_map/ppermute | solution.py:26
  6.2 1.3 %collective-permute-start.2 = (bf16[128,2048]{1,0:T(8,128)(2,1)S(1)}, bf16[128,2048]{1,0:T(8,128)(2,1)S(1)}, u32[]{:S(2)}, u32[]{:S(2)}) collective-permute-start(bf16[128,2048]{1,0:T(8,128)(2,1)S(1)} %get-tuple-element.28), channel_id=1, source_target_pairs={{4,0},{8,4},{12,8},{5,1},{9,5},{13,9},{6,2},{10,6},{14,10},{7,3},{... | collective-permute-start | bytes 1572872 | tf_op jit(solution)/shard_map/ppermute | solution.py:27
  7.5 4.7 %collective-permute-start.5 = (bf16[128,1792]{1,0:T(8,128)(2,1)S(1)}, bf16[128,1792]{1,0:T(8,128)(2,1)S(1)}, u32[]{:S(2)}, u32[]{:S(2)}) collective-permute-start(bf16[128,1792]{1,0:T(8,128)(2,1)S(1)} %get-tuple-element.33), channel_id=1, source_target_pairs={{0,12},{4,8},{8,4},{12,0},{1,13},{5,9},{9,5},{13,1},{2,14},{6,10},... | collective-permute-start | bytes 1376264 | tf_op jit(solution)/shard_map/ppermute | solution.py:22
  12.2 6.1 %shard_map.37 = (bf16[2,1,1792,2048]{3,2,1,0:T(8,128)(2,1)S(1)}, bf16[256,2048]{1,0:T(8,128)(2,1)S(1)}, bf16[1792,256]{1,0:T(8,128)(2,1)S(1)}, bf16[1792,128]{1,...) custom-call(bf16[256,2048]{1,0:T(8,128)(2,1)} %acts_ref.3, bf16[256,7168]{1,0:T(8,128)(2,1)} %grads_ref.3, ...), custom_call_target="tpu_custom_call" | custom-call | flops 1024 | bytes 1024 | tf_op jit(solution)/shard_map/pallas_call | solution.py:53
  18.4 4.4 %shard_map.38 = (f32[2,1792,256]{2,1,0:T(8,128)S(1)}, f32[8,128]{1,0:T(8,128)S(1)}) custom-call(bf16[256,2048]{1,0:T(8,128)(2,1)S(1)} %get-tuple-element.24.refs_0_, bf16[2,1,1792,2048]{3,2,1,0:T(8,128)(2,1)S(1)} %get-tuple-element.25.refs_1_.refs_2_), custom_call_target="tpu_custom_call" | custom-call | flops 1000000 | bytes 1024 | tf_op jit(solution)/shard_map/pallas_call | solution.py:41
  22.8 1.0 %collective-permute-done.2.refs_1_ = bf16[128,2048]{1,0:T(8,128)(2,1)S(1)} collective-permute-done((bf16[128,2048]{1,0:T(8,128)(2,1)S(1)}, bf16[128,2048]{1,0:T(8,128)(2,1)S(1)}, u32[]{:S(2)}, u32[]{:S(2)}) %collective-permute-start.2) | collective-permute-done | bytes 524320 | tf_op jit(solution)/shard_map/ppermute | solution.py:27
  24.0 1.3 %collective-permute-start.8 = (bf16[128,2048]{1,0:T(8,128)(2,1)S(1)}, bf16[128,2048]{1,0:T(8,128)(2,1)S(1)}, u32[]{:S(2)}, u32[]{:S(2)}) collective-permute-start(bf16[128,2048]{1,0:T(8,128)(2,1)S(1)} %get-tuple-element.31.refs_2_.refs_0_.refs_1_), channel_id=1, source_target_pairs={{4,0},{8,4},{5,1},{9,5},{6,2},{10,6},{7,3},{11,7},{20,16},{24,20},... | collective-permute-start | bytes 1572872 | tf_op jit(solution)/shard_map/ppermute | solution.py:27
  25.3 0.7 collective-permute-start.9
  26.0 8.8 %collective-permute-done.5.refs_0_ = bf16[128,1792]{1,0:T(8,128)(2,1)S(1)} collective-permute-done((bf16[128,1792]{1,0:T(8,128)(2,1)S(1)}, bf16[128,1792]{1,0:T(8,128)(2,1)S(1)}, u32[]{:S(2)}, u32[]{:S(2)}) %collective-permute-start.5) | collective-permute-done | bytes 458784 | tf_op jit(solution)/shard_map/ppermute | solution.py:22
  34.8 7.8 %collective-permute-done.refs_0_.refs_3_ = bf16[1792,128]{1,0:T(8,128)(2,1)S(1)} collective-permute-done((bf16[1792,128]{1,0:T(8,128)(2,1)S(1)}, bf16[1792,128]{1,0:T(8,128)(2,1)S(1)}, u32[]{:S(2)}, u32[]{:S(2)}) %collective-permute-start) | collective-permute-done | bytes 458784 | tf_op jit(solution)/shard_map/ppermute | solution.py:22
  42.6 1.5 %collective-permute-start.6 = (bf16[128,1792]{1,0:T(8,128)(2,1)S(1)}, bf16[128,1792]{1,0:T(8,128)(2,1)S(1)}, u32[]{:S(2)}, u32[]{:S(2)}) collective-permute-start(bf16[128,1792]{1,0:T(8,128)(2,1)S(1)} %shard_map.45.refs_0_.refs_3_), channel_id=1, source_target_pairs={{0,2},{2,0},{1,3},{3,1},{4,6},{6,4},{5,7},{7,5},{8,10},{10,8},{9,1... | collective-permute-start | bytes 1376264 | tf_op jit(solution)/shard_map/ppermute | solution.py:22
  45.0 4.4 %shard_map.44 = (f32[2,1792,256]{2,1,0:T(8,128)S(1)}, f32[8,128]{1,0:T(8,128)S(1)}) custom-call(bf16[128,2048]{1,0:T(8,128)(2,1)S(1)} %shard_map.43.refs_0_, bf16[128,2048]{1,0:T(8,128)(2,1)S(1)} %collective-permute-done.4.refs_1_, bf16[2,1,1792,2048]{3,2,1,0:T(8,128)(2,1)S(1)} %get-tuple-element.25.refs_1_.refs_2_, f32[2,256]{1,0:T(2,128)S(1)} %shard_map.39.refs_3_), custom_call_target="tpu_custom_call" | custom-call | flops 1000000 | bytes 1024 | tf_op jit(solution)/shard_map/pallas_call | solution.py:41
  49.4 1.2 %collective-permute-start.14 = (bf16[896,128]{1,0:T(8,128)(2,1)S(1)}, bf16[896,128]{1,0:T(8,128)(2,1)S(1)}, u32[]{:S(2)}, u32[]{:S(2)}) collective-permute-start(bf16[896,128]{1,0:T(8,128)(2,1)S(1)} %shard_map.52), channel_id=1, source_target_pairs={{0,8},{4,12},{8,0},{12,4},{1,9},{5,13},{9,1},{13,5},{2,10},{6,14},... | collective-permute-start | bytes 688136 | tf_op jit(solution)/shard_map/ppermute | solution.py:22
  50.6 5.4 %collective-permute-done.6.refs_1_.refs_4_ = bf16[128,1792]{1,0:T(8,128)(2,1)S(1)} collective-permute-done((bf16[128,1792]{1,0:T(8,128)(2,1)S(1)}, bf16[128,1792]{1,0:T(8,128)(2,1)S(1)}, u32[]{:S(2)}, u32[]{:S(2)}) %collective-permute-start.6) | collective-permute-done | bytes 458784 | tf_op jit(solution)/shard_map/ppermute | solution.py:22
  56.2 1.3 %collective-permute-start.10 = (bf16[128,2048]{1,0:T(8,128)(2,1)S(1)}, bf16[128,2048]{1,0:T(8,128)(2,1)S(1)}, u32[]{:S(2)}, u32[]{:S(2)}) collective-permute-start(bf16[128,2048]{1,0:T(8,128)(2,1)S(1)} %shard_map.48.refs_0_), channel_id=1, source_target_pairs={{4,0},{8,12},{5,1},{9,13},{6,2},{10,14},{7,3},{11,15},{20,16},{24,... | collective-permute-start | bytes 1572872 | tf_op jit(solution)/shard_map/ppermute | solution.py:293
  57.5 3.3 %collective-permute-start.15 = (bf16[896,128]{1,0:T(8,128)(2,1)S(1)}, bf16[896,128]{1,0:T(8,128)(2,1)S(1)}, u32[]{:S(2)}, u32[]{:S(2)}) collective-permute-start(bf16[896,128]{1,0:T(8,128)(2,1)S(1)} %shard_map.54), channel_id=1, source_target_pairs={{0,8},{4,12},{8,0},{12,4},{1,9},{5,13},{9,1},{13,5},{2,10},{6,14},... | collective-permute-start | bytes 688136 | tf_op jit(solution)/shard_map/ppermute | solution.py:22
  60.8 4.4 %shard_map.46 = (f32[2,256,2048]{2,1,0:T(8,128)S(1)}, f32[8,128]{1,0:T(8,128)S(1)}) custom-call(bf16[128,1792]{1,0:T(8,128)(2,1)S(1)} %shard_map.45.refs_0_.refs_3_, bf16[128,1792]{1,0:T(8,128)(2,1)S(1)} %collective-permute-done.6.refs_1_.refs_4_, bf16[2,1,1792,2048]{3,2,1,0:T(8,128)(2,1)S(1)} %get-tuple-element.25.refs_1_.refs_2_, ...), custom_call_target="tpu_custom_call" | custom-call | flops 1000000 | bytes 1024 | tf_op jit(solution)/shard_map/pallas_call | solution.py:41
  65.2 0.8 shard_map.47.refs_3_.refs_1_
  66.0 1.6 %collective-permute-start.16 = (bf16[896,128]{1,0:T(8,128)(2,1)S(1)}, bf16[896,128]{1,0:T(8,128)(2,1)S(1)}, u32[]{:S(2)}, u32[]{:S(2)}) collective-permute-start(bf16[896,128]{1,0:T(8,128)(2,1)S(1)} %shard_map.53.refs_0_), channel_id=1, source_target_pairs={{0,2},{2,0},{1,3},{3,1},{4,6},{6,4},{5,7},{7,5},{8,10},{10,8},{9,1... | collective-permute-start | bytes 688136 | tf_op jit(solution)/shard_map/ppermute | solution.py:22
  67.5 4.4 %shard_map.49 = (f32[2,1792,256]{2,1,0:T(8,128)S(1)}, f32[8,128]{1,0:T(8,128)S(1)}) custom-call(bf16[128,2048]{1,0:T(8,128)(2,1)S(1)} %shard_map.48.refs_0_, bf16[128,2048]{1,0:T(8,128)(2,1)S(1)} %collective-permute-done.11.refs_1_, bf16[2,1,1792,2048]{3,2,1,0:T(8,128)(2,1)S(1)} %get-tuple-element.25.refs_1_.refs_2_, f32[2,256]{1,0:T(2,128)S(1)} %shard_map.47.refs_3_.refs_1_), custom_call_target="tpu_custom_call" | custom-call | flops 1000000 | bytes 1024 | tf_op jit(solution)/shard_map/pallas_call | solution.py:41
  71.9 1.2 %collective-permute-done.15.refs_0_ = bf16[896,128]{1,0:T(8,128)(2,1)S(1)} collective-permute-done((bf16[896,128]{1,0:T(8,128)(2,1)S(1)}, bf16[896,128]{1,0:T(8,128)(2,1)S(1)}, u32[]{:S(2)}, u32[]{:S(2)}) %collective-permute-start.15) | collective-permute-done | bytes 229408 | tf_op jit(solution)/shard_map/ppermute | solution.py:22
  73.1 1.5 %collective-permute-start.17 = (bf16[896,128]{1,0:T(8,128)(2,1)S(1)}, bf16[896,128]{1,0:T(8,128)(2,1)S(1)}, u32[]{:S(2)}, u32[]{:S(2)}) collective-permute-start(bf16[896,128]{1,0:T(8,128)(2,1)S(1)} %shard_map.55.refs_1_), channel_id=1, source_target_pairs={{0,2},{2,0},{1,3},{3,1},{4,6},{6,4},{5,7},{7,5},{8,10},{10,8},{9,1... | collective-permute-start | bytes 688136 | tf_op jit(solution)/shard_map/ppermute | solution.py:22
  74.6 4.7 %collective-permute-done.10.refs_0_ = bf16[128,2048]{1,0:T(8,128)(2,1)S(1)} collective-permute-done((bf16[128,2048]{1,0:T(8,128)(2,1)S(1)}, bf16[128,2048]{1,0:T(8,128)(2,1)S(1)}, u32[]{:S(2)}, u32[]{:S(2)}) %collective-permute-start.10) | collective-permute-done | bytes 524320 | tf_op jit(solution)/shard_map/ppermute | solution.py:293
  79.7 0.7 shard_map.56
  80.5 0.8 collective-permute-done.12.refs_1_
  81.8 2.7 %collective-permute-start.13 = (f32[2,256]{1,0:T(2,128)S(1)}, f32[2,256]{1,0:T(2,128)S(1)}, u32[]{:S(2)}, u32[]{:S(2)}) collective-permute-start(f32[2,256]{1,0:T(2,128)S(1)} %shard_map.51), channel_id=1, source_target_pairs={{0,12},{4,8},{8,4},{12,0},{1,13},{5,9},{9,5},{13,1},{2,14},{6,10},... | collective-permute-start | bytes 6152 | tf_op jit(solution)/shard_map/ppermute | solution.py:22
  85.0 2.3 %collective-permute-done.13 = f32[2,256]{1,0:T(2,128)S(1)} collective-permute-done((f32[2,256]{1,0:T(2,128)S(1)}, f32[2,256]{1,0:T(2,128)S(1)}, u32[]{:S(2)}, u32[]{:S(2)}) %collective-permute-start.13) | collective-permute-done | bytes 2080 | tf_op jit(solution)/shard_map/ppermute | solution.py:22
  87.3 1.5 %collective-permute-start.19 = (f32[2,256]{1,0:T(2,128)S(1)}, f32[2,256]{1,0:T(2,128)S(1)}, u32[]{:S(2)}, u32[]{:S(2)}) collective-permute-start(f32[2,256]{1,0:T(2,128)S(1)} %add_add_fusion.1), channel_id=1, source_target_pairs={{0,1},{1,0},{2,3},{3,2},{4,5},{5,4},{6,7},{7,6},{8,9},{9,8},{10,11... | collective-permute-start | bytes 6152 | tf_op jit(solution)/shard_map/ppermute | solution.py:22
  89.4 0.9 collective-permute-done.21
  90.3 2.2 %collective-permute-done.20 = f32[2,256]{1,0:T(2,128)S(1)} collective-permute-done((f32[2,256]{1,0:T(2,128)S(1)}, f32[2,256]{1,0:T(2,128)S(1)}, u32[]{:S(2)}, u32[]{:S(2)}) %collective-permute-start.20) | collective-permute-done | bytes 2080 | tf_op jit(solution)/shard_map/ppermute | solution.py:22
  92.4 0.6 add_add_fusion
  (34 shorter events, 3.4 us)
Async XLA Ops:
  1.2 21.6 %collective-permute-start.1 = (bf16[128,2048]{1,0:T(8,128)(2,1)S(1)}, bf16[128,2048]{1,0:T(8,128)(2,1)S(1)}, u32[]{:S(2)}, u32[]{:S(2)}) collective-permute-start(bf16[128,2048]{1,0:T(8,128)(2,1)S(1)} %get-tuple-element.28), channel_id=1, source_target_pairs={{0,4},{4,8},{8,12},{1,5},{5,9},{9,13},{2,6},{6,10},{10,14},{3,7},{... | collective-permute-start | bytes 1572872 | tf_op jit(solution)/shard_map/ppermute | solution.py:26
  6.2 17.7 %collective-permute-start.2 = (bf16[128,2048]{1,0:T(8,128)(2,1)S(1)}, bf16[128,2048]{1,0:T(8,128)(2,1)S(1)}, u32[]{:S(2)}, u32[]{:S(2)}) collective-permute-start(bf16[128,2048]{1,0:T(8,128)(2,1)S(1)} %get-tuple-element.28), channel_id=1, source_target_pairs={{4,0},{8,4},{12,8},{5,1},{9,5},{13,9},{6,2},{10,6},{14,10},{7,3},{... | collective-permute-start | bytes 1572872 | tf_op jit(solution)/shard_map/ppermute | solution.py:27
  7.5 27.3 %collective-permute-start.5 = (bf16[128,1792]{1,0:T(8,128)(2,1)S(1)}, bf16[128,1792]{1,0:T(8,128)(2,1)S(1)}, u32[]{:S(2)}, u32[]{:S(2)}) collective-permute-start(bf16[128,1792]{1,0:T(8,128)(2,1)S(1)} %get-tuple-element.33), channel_id=1, source_target_pairs={{0,12},{4,8},{8,4},{12,0},{1,13},{5,9},{9,5},{13,1},{2,14},{6,10},... | collective-permute-start | bytes 1376264 | tf_op jit(solution)/shard_map/ppermute | solution.py:22
  18.3 24.3 %collective-permute-start = (bf16[1792,128]{1,0:T(8,128)(2,1)S(1)}, bf16[1792,128]{1,0:T(8,128)(2,1)S(1)}, u32[]{:S(2)}, u32[]{:S(2)}) collective-permute-start(bf16[1792,128]{1,0:T(8,128)(2,1)S(1)} %get-tuple-element.27), channel_id=1, source_target_pairs={{0,4},{4,0},{8,12},{12,8},{1,5},{5,1},{9,13},{13,9},{2,6},{6,2},{1... | collective-permute-start | bytes 1376264 | tf_op jit(solution)/shard_map/ppermute | solution.py:22
  23.9 21.1 %collective-permute-start.4 = (bf16[128,2048]{1,0:T(8,128)(2,1)S(1)}, bf16[128,2048]{1,0:T(8,128)(2,1)S(1)}, u32[]{:S(2)}, u32[]{:S(2)}) collective-permute-start(bf16[128,2048]{1,0:T(8,128)(2,1)S(1)} %shard_map.43.refs_0_), channel_id=1, source_target_pairs={{0,1},{1,0},{2,3},{3,2},{4,5},{5,4},{6,7},{7,6},{8,9},{9,8},{10,11... | collective-permute-start | bytes 1572872 | tf_op jit(solution)/shard_map/ppermute | solution.py:22
  24.0 32.1 %collective-permute-start.8 = (bf16[128,2048]{1,0:T(8,128)(2,1)S(1)}, bf16[128,2048]{1,0:T(8,128)(2,1)S(1)}, u32[]{:S(2)}, u32[]{:S(2)}) collective-permute-start(bf16[128,2048]{1,0:T(8,128)(2,1)S(1)} %get-tuple-element.31.refs_2_.refs_0_.refs_1_), channel_id=1, source_target_pairs={{4,0},{8,4},{5,1},{9,5},{6,2},{10,6},{7,3},{11,7},{20,16},{24,20},... | collective-permute-start | bytes 1572872 | tf_op jit(solution)/shard_map/ppermute | solution.py:27
  25.3 30.8 %collective-permute-start.9 = (bf16[128,2048]{1,0:T(8,128)(2,1)S(1)}, bf16[128,2048]{1,0:T(8,128)(2,1)S(1)}, u32[]{:S(2)}, u32[]{:S(2)}) collective-permute-start(bf16[128,2048]{1,0:T(8,128)(2,1)S(1)} %get-tuple-element.30.refs_1_.refs_2_), channel_id=1, source_target_pairs={{4,8},{8,12},{5,9},{9,13},{6,10},{10,14},{7,11},{11,15},{20,24},{2... | collective-permute-start | bytes 1572872 | tf_op jit(solution)/shard_map/ppermute | solution.py:26
  42.6 13.5 %collective-permute-start.6 = (bf16[128,1792]{1,0:T(8,128)(2,1)S(1)}, bf16[128,1792]{1,0:T(8,128)(2,1)S(1)}, u32[]{:S(2)}, u32[]{:S(2)}) collective-permute-start(bf16[128,1792]{1,0:T(8,128)(2,1)S(1)} %shard_map.45.refs_0_.refs_3_), channel_id=1, source_target_pairs={{0,2},{2,0},{1,3},{3,1},{4,6},{6,4},{5,7},{7,5},{8,10},{10,8},{9,1... | collective-permute-start | bytes 1376264 | tf_op jit(solution)/shard_map/ppermute | solution.py:22
  44.1 21.2 %collective-permute-start.3 = (bf16[1792,128]{1,0:T(8,128)(2,1)S(1)}, bf16[1792,128]{1,0:T(8,128)(2,1)S(1)}, u32[]{:S(2)}, u32[]{:S(2)}) collective-permute-start(bf16[1792,128]{1,0:T(8,128)(2,1)S(1)} %shard_map.42.refs_0_), channel_id=1, source_target_pairs={{0,2},{2,0},{1,3},{3,1},{4,6},{6,4},{5,7},{7,5},{8,10},{10,8},{9,1... | collective-permute-start | bytes 1376264 | tf_op jit(solution)/shard_map/ppermute | solution.py:22
  49.4 16.5 %collective-permute-start.14 = (bf16[896,128]{1,0:T(8,128)(2,1)S(1)}, bf16[896,128]{1,0:T(8,128)(2,1)S(1)}, u32[]{:S(2)}, u32[]{:S(2)}) collective-permute-start(bf16[896,128]{1,0:T(8,128)(2,1)S(1)} %shard_map.52), channel_id=1, source_target_pairs={{0,8},{4,12},{8,0},{12,4},{1,9},{5,13},{9,1},{13,5},{2,10},{6,14},... | collective-permute-start | bytes 688136 | tf_op jit(solution)/shard_map/ppermute | solution.py:22
  56.1 11.5 %collective-permute-start.11 = (bf16[128,2048]{1,0:T(8,128)(2,1)S(1)}, bf16[128,2048]{1,0:T(8,128)(2,1)S(1)}, u32[]{:S(2)}, u32[]{:S(2)}) collective-permute-start(bf16[128,2048]{1,0:T(8,128)(2,1)S(1)} %shard_map.48.refs_0_), channel_id=1, source_target_pairs={{0,1},{1,0},{2,3},{3,2},{4,5},{5,4},{6,7},{7,6},{8,9},{9,8},{10,11... | collective-permute-start | bytes 1572872 | tf_op jit(solution)/shard_map/ppermute | solution.py:22
  56.2 23.2 %collective-permute-start.10 = (bf16[128,2048]{1,0:T(8,128)(2,1)S(1)}, bf16[128,2048]{1,0:T(8,128)(2,1)S(1)}, u32[]{:S(2)}, u32[]{:S(2)}) collective-permute-start(bf16[128,2048]{1,0:T(8,128)(2,1)S(1)} %shard_map.48.refs_0_), channel_id=1, source_target_pairs={{4,0},{8,12},{5,1},{9,13},{6,2},{10,14},{7,3},{11,15},{20,16},{24,... | collective-permute-start | bytes 1572872 | tf_op jit(solution)/shard_map/ppermute | solution.py:293
  57.5 15.7 %collective-permute-start.15 = (bf16[896,128]{1,0:T(8,128)(2,1)S(1)}, bf16[896,128]{1,0:T(8,128)(2,1)S(1)}, u32[]{:S(2)}, u32[]{:S(2)}) collective-permute-start(bf16[896,128]{1,0:T(8,128)(2,1)S(1)} %shard_map.54), channel_id=1, source_target_pairs={{0,8},{4,12},{8,0},{12,4},{1,9},{5,13},{9,1},{13,5},{2,10},{6,14},... | collective-permute-start | bytes 688136 | tf_op jit(solution)/shard_map/ppermute | solution.py:22
  66.0 13.5 %collective-permute-start.16 = (bf16[896,128]{1,0:T(8,128)(2,1)S(1)}, bf16[896,128]{1,0:T(8,128)(2,1)S(1)}, u32[]{:S(2)}, u32[]{:S(2)}) collective-permute-start(bf16[896,128]{1,0:T(8,128)(2,1)S(1)} %shard_map.53.refs_0_), channel_id=1, source_target_pairs={{0,2},{2,0},{1,3},{3,1},{4,6},{6,4},{5,7},{7,5},{8,10},{10,8},{9,1... | collective-permute-start | bytes 688136 | tf_op jit(solution)/shard_map/ppermute | solution.py:22
  73.1 6.6 %collective-permute-start.17 = (bf16[896,128]{1,0:T(8,128)(2,1)S(1)}, bf16[896,128]{1,0:T(8,128)(2,1)S(1)}, u32[]{:S(2)}, u32[]{:S(2)}) collective-permute-start(bf16[896,128]{1,0:T(8,128)(2,1)S(1)} %shard_map.55.refs_1_), channel_id=1, source_target_pairs={{0,2},{2,0},{1,3},{3,1},{4,6},{6,4},{5,7},{7,5},{8,10},{10,8},{9,1... | collective-permute-start | bytes 688136 | tf_op jit(solution)/shard_map/ppermute | solution.py:22
  74.6 9.8 %collective-permute-start.7 = (f32[2,256]{1,0:T(2,128)S(1)}, f32[2,256]{1,0:T(2,128)S(1)}, u32[]{:S(2)}, u32[]{:S(2)}) collective-permute-start(f32[2,256]{1,0:T(2,128)S(1)} %shard_map.47.refs_3_.refs_1_), channel_id=1, source_target_pairs={{0,4},{4,0},{8,12},{12,8},{1,5},{5,1},{9,13},{13,9},{2,6},{6,2},{1... | collective-permute-start | bytes 6152 | tf_op jit(solution)/shard_map/ppermute | solution.py:22
  79.4 2.0 %collective-permute-start.12 = (bf16[128,2048]{1,0:T(8,128)(2,1)S(1)}, bf16[128,2048]{1,0:T(8,128)(2,1)S(1)}, u32[]{:S(2)}, u32[]{:S(2)}) collective-permute-start(bf16[128,2048]{1,0:T(8,128)(2,1)S(1)} %shard_map.50.refs_0_), channel_id=1, source_target_pairs={{0,1},{1,0},{2,3},{3,2},{4,5},{5,4},{6,7},{7,6},{8,9},{9,8},{10,11... | collective-permute-start | bytes 1572872 | tf_op jit(solution)/shard_map/ppermute | solution.py:22
  80.4 4.5 %collective-permute-start.18 = (f32[2,256]{1,0:T(2,128)S(1)}, f32[2,256]{1,0:T(2,128)S(1)}, u32[]{:S(2)}, u32[]{:S(2)}) collective-permute-start(f32[2,256]{1,0:T(2,128)S(1)} %shard_map.56), channel_id=1, source_target_pairs={{0,8},{4,12},{8,0},{12,4},{1,9},{5,13},{9,1},{13,5},{2,10},{6,14},... | collective-permute-start | bytes 6152 | tf_op jit(solution)/shard_map/ppermute | solution.py:22
  81.8 5.4 %collective-permute-start.13 = (f32[2,256]{1,0:T(2,128)S(1)}, f32[2,256]{1,0:T(2,128)S(1)}, u32[]{:S(2)}, u32[]{:S(2)}) collective-permute-start(f32[2,256]{1,0:T(2,128)S(1)} %shard_map.51), channel_id=1, source_target_pairs={{0,12},{4,8},{8,4},{12,0},{1,13},{5,9},{9,5},{13,1},{2,14},{6,10},... | collective-permute-start | bytes 6152 | tf_op jit(solution)/shard_map/ppermute | solution.py:22
  87.3 3.0 %collective-permute-start.21 = (f32[2,256]{1,0:T(2,128)S(1)}, f32[2,256]{1,0:T(2,128)S(1)}, u32[]{:S(2)}, u32[]{:S(2)}) collective-permute-start(f32[2,256]{1,0:T(2,128)S(1)} %add_add_fusion.1), channel_id=1, source_target_pairs={{0,3},{1,2},{2,1},{3,0},{4,7},{5,6},{6,5},{7,4},{8,11},{9,10},{10,... | collective-permute-start | bytes 6152 | tf_op jit(solution)/shard_map/ppermute | solution.py:22
  87.3 2.9 %collective-permute-start.19 = (f32[2,256]{1,0:T(2,128)S(1)}, f32[2,256]{1,0:T(2,128)S(1)}, u32[]{:S(2)}, u32[]{:S(2)}) collective-permute-start(f32[2,256]{1,0:T(2,128)S(1)} %add_add_fusion.1), channel_id=1, source_target_pairs={{0,1},{1,0},{2,3},{3,2},{4,5},{5,4},{6,7},{7,6},{8,9},{9,8},{10,11... | collective-permute-start | bytes 6152 | tf_op jit(solution)/shard_map/ppermute | solution.py:22
  88.9 3.6 %collective-permute-start.20 = (f32[2,256]{1,0:T(2,128)S(1)}, f32[2,256]{1,0:T(2,128)S(1)}, u32[]{:S(2)}, u32[]{:S(2)}) collective-permute-start(f32[2,256]{1,0:T(2,128)S(1)} %add_add_fusion.1), channel_id=1, source_target_pairs={{0,2},{1,3},{2,0},{3,1},{4,6},{5,7},{6,4},{7,5},{8,10},{9,11},{10,... | collective-permute-start | bytes 6152 | tf_op jit(solution)/shard_map/ppermute | solution.py:22

commit v23 on v21

--- a/solution.py
+++ b/solution.py
@@ -9,7 +9,7 @@
 from jax.sharding import PartitionSpec as P
 
 
-LONG, SHORT = 14_000_000_000, 1_000_000
+LONG, MIDDLE, SHORT = 14_000_000_000, 14_000_000_000, 1_000_000
 
 
 def trade(block, steps, backwards=False):
@@ -129,6 +129,12 @@
             out_ref[...] = block[...]
 
 
+def chosen(first, second, where, count, tokens=()):
+    choice = [int(z in where) for z in range(count)]
+    outs = [(first.shape, first.dtype)]
+    return call(functools.partial(pick_kernel, choice), [first, second], outs, tokens=tokens)[0]
+
+
 def from_partner(hops, d, count, tokens=()):
     sources, choice = [], []
     for z in range(count):
@@ -287,11 +293,17 @@
     mixes, token = {}, scores
     for d in early:
         mixes[d], token = mixed(acts_of(from_partner(hops, d, count)), queries, SHORT, [token])
-    tail = [trade(hold([block], [token])[0], {"dp": late}) for block in sent[len(early) :]]
+    tail = list(hold(sent[len(early) :], [token]))
+    inner = range(count // 4, count - count // 4)
+    routes = [[(z, z ^ late) for z in range(count) if (z ^ late in inner) == inward] for inward in (False, True)]
+    outward, = hold([lax.ppermute(tail[0], "dp", routes[0])], [], LONG)
     sides = to_columns(hold([arrived[far]], [*hops[1], *[arrived[d] for d in early]])[0])
     block = from_partner(hops, late, count, [token] + sides)
     end = lax.ppermute(block, "dp", [(1, 0), (count - 2, count - 1)])
     hops.append((end, end))
+    inward = lax.ppermute(chosen(tail[0], tail[0], [], count, [block]), "dp", routes[1])
+    inward, = hold([inward], [], MIDDLE)
+    tail = [chosen(outward, inward, inner, count), trade(tail[1], {"dp": late})]
 
     proj, token = projected(sides, queries, SHORT, [token])
     terms = []

time: 92.8 us -> 99 us (1.067)
  waiting for transfers between devices: 36 us -> 42 us
    ppermute x16 -> x15, waiting for transfers between devices: 30.2 us -> 36.9 us  [trade(): return lax.ppermute(block, axes, route[::-1] if backwards else route)]
    ppermute x0 -> x2, starting transfers between devices: none -> 2.6 us  [the longest x1 1.3 us: on_device(): lax.ppermute(chosen(tail[0], tail[0], [], count, [block]), 'dp', routes[1])]
    ppermute x16 -> x15, starting transfers between devices: 18.9 us -> 16.4 us  [trade(): return lax.ppermute(block, axes, route[::-1] if backwards else route)]
    ppermute x0 -> x2, waiting for transfers between devices: none -> 1.92 us  [the longest x1 1.92 us: on_device(): outward, = hold([lax.ppermute(tail[0], 'dp', routes[0])], [], LONG)]
    ppermute x1, waiting for transfers between devices: 4.69 us -> 3.14 us  [on_device(): end = lax.ppermute(block, 'dp', [(1, 0), (count - 2, count - 1)])]
    ppermute x2, waiting for transfers between devices: 1.05 us -> 0.01 us  [pass_on(): lax.ppermute(block[1], 'dp', [(i, i - 1) for i in range(1, count - step +...]
    pallas_call x11 -> x13, Pallas kernels: 20 us -> 20.1 us  [call(): pl.pallas_call(body, in_specs=[NEAR] * len(arrays) + [ANYWHERE] * skip, o...]
  transfers between devices with their start and end apart: 21 -> 22, of which waited for: 12 -> 11; matrix products, arithmetic and copies ran while one was open for 0% -> 0% of each run, Pallas kernels for 28% -> 27%
where the time goes in v23:
time: 99 us; the launch traced here: 98.8 us
  waiting for transfers between devices  42 us (42%)
  starting transfers between devices  28.5 us (29%)
  Pallas kernels  27.4 us (28%)
    ppermute x15, waiting for transfers between devices, trade(): return lax.ppermute(block, axes, route[::-1] if backwards else route)  36.9 us
    pallas_call x13, Pallas kernels, call(): pl.pallas_call(body, in_specs=[NEAR] * len(arrays) + [ANYWHERE] * skip, o...  20.1 us
    ppermute x15, starting transfers between devices, trade(): return lax.ppermute(block, axes, route[::-1] if backwards else route)  16.4 us
    pallas_call x2, Pallas kernels, fetch(): pl.pallas_call(kernel, in_specs=[ANYWHERE] * len(arrays), out_specs=[NEAR...  7.32 us
    ppermute x2, starting transfers between devices, pass_on(): lax.ppermute(block[0], 'dp', [(i, i + 1) for i in range(step - 1, count -...  5.65 us
    ppermute x1, waiting for transfers between devices, on_device(): end = lax.ppermute(block, 'dp', [(1, 0), (count - 2, count - 1)])  3.14 us
    ppermute x2, starting transfers between devices, pass_on(): lax.ppermute(block[1], 'dp', [(i, i - 1) for i in range(1, count - step +...  2.58 us
  transfers between devices with their start and end apart: 22, of which 11 were waited for; matrix products, arithmetic and copies ran while one was open for 0% of the time, Pallas kernels for 27%

profile of v23, /device:TPU:0, one launch (start us, length us, event | category | flops | bytes accessed | tf_op | source)
XLA Modules:
  0.0 98.8 jit_solution(13723973031526806369)
XLA Ops:
  0.0 1.2 %shard_map.40 = (bf16[128,2048]{1,0:T(8,128)(2,1)S(1)}, bf16[128,1792]{1,0:T(8,128)(2,1)S(1)}) custom-call(bf16[256,2048]{1,0:T(8,128)(2,1)} %acts_ref.3, bf16[256,7168]{1,0:T(8,128)(2,1)} %grads_ref.3), custom_call_target="tpu_custom_call" | custom-call | flops 1024 | bytes 1024 | tf_op jit(solution)/shard_map/pallas_call | solution.py:53
  1.2 5.0 %collective-permute-start.1 = (bf16[128,2048]{1,0:T(8,128)(2,1)S(1)}, bf16[128,2048]{1,0:T(8,128)(2,1)S(1)}, u32[]{:S(2)}, u32[]{:S(2)}) collective-permute-start(bf16[128,2048]{1,0:T(8,128)(2,1)S(1)} %get-tuple-element.30), channel_id=1, source_target_pairs={{0,4},{4,8},{8,12},{1,5},{5,9},{9,13},{2,6},{6,10},{10,14},{3,7},{... | collective-permute-start | bytes 1572872 | tf_op jit(solution)/shard_map/ppermute | solution.py:26
  6.2 1.3 %collective-permute-start.2 = (bf16[128,2048]{1,0:T(8,128)(2,1)S(1)}, bf16[128,2048]{1,0:T(8,128)(2,1)S(1)}, u32[]{:S(2)}, u32[]{:S(2)}) collective-permute-start(bf16[128,2048]{1,0:T(8,128)(2,1)S(1)} %get-tuple-element.30), channel_id=1, source_target_pairs={{4,0},{8,4},{12,8},{5,1},{9,5},{13,9},{6,2},{10,6},{14,10},{7,3},{... | collective-permute-start | bytes 1572872 | tf_op jit(solution)/shard_map/ppermute | solution.py:27
  7.5 6.1 %shard_map.37 = (bf16[2,1,1792,2048]{3,2,1,0:T(8,128)(2,1)S(1)}, bf16[256,2048]{1,0:T(8,128)(2,1)S(1)}, bf16[1792,256]{1,0:T(8,128)(2,1)S(1)}, bf16[1792,128]{1,...) custom-call(bf16[256,2048]{1,0:T(8,128)(2,1)} %acts_ref.3, bf16[256,7168]{1,0:T(8,128)(2,1)} %grads_ref.3, ...), custom_call_target="tpu_custom_call" | custom-call | flops 1024 | bytes 1024 | tf_op jit(solution)/shard_map/pallas_call | solution.py:53
  13.6 2.7 %collective-permute-start = (bf16[1792,128]{1,0:T(8,128)(2,1)S(1)}, bf16[1792,128]{1,0:T(8,128)(2,1)S(1)}, u32[]{:S(2)}, u32[]{:S(2)}) collective-permute-start(bf16[1792,128]{1,0:T(8,128)(2,1)S(1)} %get-tuple-element.29), channel_id=1, source_target_pairs={{0,4},{4,0},{8,12},{12,8},{1,5},{5,1},{9,13},{13,9},{2,6},{6,2},{1... | collective-permute-start | bytes 1376264 | tf_op jit(solution)/shard_map/ppermute | solution.py:22
  16.3 2.4 %collective-permute-start.5 = (bf16[128,1792]{1,0:T(8,128)(2,1)S(1)}, bf16[128,1792]{1,0:T(8,128)(2,1)S(1)}, u32[]{:S(2)}, u32[]{:S(2)}) collective-permute-start(bf16[128,1792]{1,0:T(8,128)(2,1)S(1)} %get-tuple-element.35), channel_id=1, source_target_pairs={{0,12},{4,8},{8,4},{12,0},{1,13},{5,9},{9,5},{13,1},{2,14},{6,10},... | collective-permute-start | bytes 1376264 | tf_op jit(solution)/shard_map/ppermute | solution.py:22
  18.8 4.4 %shard_map.38 = (f32[2,1792,256]{2,1,0:T(8,128)S(1)}, f32[8,128]{1,0:T(8,128)S(1)}) custom-call(bf16[256,2048]{1,0:T(8,128)(2,1)S(1)} %get-tuple-element.26.refs_0_, bf16[2,1,1792,2048]{3,2,1,0:T(8,128)(2,1)S(1)} %get-tuple-element.27.refs_1_.refs_2_), custom_call_target="tpu_custom_call" | custom-call | flops 1000000 | bytes 1024 | tf_op jit(solution)/shard_map/pallas_call | solution.py:41
  23.3 1.3 %collective-permute-start.8 = (bf16[128,2048]{1,0:T(8,128)(2,1)S(1)}, bf16[128,2048]{1,0:T(8,128)(2,1)S(1)}, u32[]{:S(2)}, u32[]{:S(2)}) collective-permute-start(bf16[128,2048]{1,0:T(8,128)(2,1)S(1)} %get-tuple-element.33.refs_2_.refs_0_.refs_1_), channel_id=1, source_target_pairs={{4,0},{8,4},{5,1},{9,5},{6,2},{10,6},{7,3},{11,7},{20,16},{24,20},... | collective-permute-start | bytes 1572872 | tf_op jit(solution)/shard_map/ppermute | solution.py:27
  24.6 0.7 collective-permute-start.9
  25.3 8.4 %collective-permute-done.refs_0_.refs_3_ = bf16[1792,128]{1,0:T(8,128)(2,1)S(1)} collective-permute-done((bf16[1792,128]{1,0:T(8,128)(2,1)S(1)}, bf16[1792,128]{1,0:T(8,128)(2,1)S(1)}, u32[]{:S(2)}, u32[]{:S(2)}) %collective-permute-start) | collective-permute-done | bytes 458784 | tf_op jit(solution)/shard_map/ppermute | solution.py:22
  33.7 9.6 %collective-permute-done.5.refs_0_ = bf16[128,1792]{1,0:T(8,128)(2,1)S(1)} collective-permute-done((bf16[128,1792]{1,0:T(8,128)(2,1)S(1)}, bf16[128,1792]{1,0:T(8,128)(2,1)S(1)}, u32[]{:S(2)}, u32[]{:S(2)}) %collective-permute-start.5) | collective-permute-done | bytes 458784 | tf_op jit(solution)/shard_map/ppermute | solution.py:22
  43.3 1.5 %collective-permute-start.6 = (bf16[128,1792]{1,0:T(8,128)(2,1)S(1)}, bf16[128,1792]{1,0:T(8,128)(2,1)S(1)}, u32[]{:S(2)}, u32[]{:S(2)}) collective-permute-start(bf16[128,1792]{1,0:T(8,128)(2,1)S(1)} %shard_map.45.refs_0_.refs_3_), channel_id=1, source_target_pairs={{0,2},{2,0},{1,3},{3,1},{4,6},{6,4},{5,7},{7,5},{8,10},{10,8},{9,1... | collective-permute-start | bytes 1376264 | tf_op jit(solution)/shard_map/ppermute | solution.py:22
  45.2 4.4 %shard_map.44 = (f32[2,1792,256]{2,1,0:T(8,128)S(1)}, f32[8,128]{1,0:T(8,128)S(1)}) custom-call(bf16[128,2048]{1,0:T(8,128)(2,1)S(1)} %shard_map.43.refs_0_, bf16[128,2048]{1,0:T(8,128)(2,1)S(1)} %collective-permute-done.4.refs_1_, bf16[2,1,1792,2048]{3,2,1,0:T(8,128)(2,1)S(1)} %get-tuple-element.27.refs_1_.refs_2_, f32[2,256]{1,0:T(2,128)S(1)} %shard_map.39.refs_3_), custom_call_target="tpu_custom_call" | custom-call | flops 1000000 | bytes 1024 | tf_op jit(solution)/shard_map/pallas_call | solution.py:41
  49.6 4.6 %collective-permute-done.6.refs_1_.refs_4_ = bf16[128,1792]{1,0:T(8,128)(2,1)S(1)} collective-permute-done((bf16[128,1792]{1,0:T(8,128)(2,1)S(1)}, bf16[128,1792]{1,0:T(8,128)(2,1)S(1)}, u32[]{:S(2)}, u32[]{:S(2)}) %collective-permute-start.6) | collective-permute-done | bytes 458784 | tf_op jit(solution)/shard_map/ppermute | solution.py:22
  54.3 1.3 %collective-permute-start.15 = (bf16[896,128]{1,0:T(8,128)(2,1)S(1)}, bf16[896,128]{1,0:T(8,128)(2,1)S(1)}, u32[]{:S(2)}, u32[]{:S(2)}) collective-permute-start(bf16[896,128]{1,0:T(8,128)(2,1)S(1)} %shard_map.54), channel_id=1, source_target_pairs={{0,8},{12,4},{1,9},{13,5},{2,10},{14,6},{3,11},{15,7},{16,24},{28,... | collective-permute-start | bytes 688136 | tf_op jit(solution)/shard_map/ppermute | solution.py:304
  55.6 1.6 %collective-permute-start.3 = (bf16[1792,128]{1,0:T(8,128)(2,1)S(1)}, bf16[1792,128]{1,0:T(8,128)(2,1)S(1)}, u32[]{:S(2)}, u32[]{:S(2)}) collective-permute-start(bf16[1792,128]{1,0:T(8,128)(2,1)S(1)} %shard_map.42.refs_0_), channel_id=1, source_target_pairs={{0,2},{2,0},{1,3},{3,1},{4,6},{6,4},{5,7},{7,5},{8,10},{10,8},{9,1... | collective-permute-start | bytes 1376264 | tf_op jit(solution)/shard_map/ppermute | solution.py:22
  57.2 1.3 %collective-permute-start.10 = (bf16[128,2048]{1,0:T(8,128)(2,1)S(1)}, bf16[128,2048]{1,0:T(8,128)(2,1)S(1)}, u32[]{:S(2)}, u32[]{:S(2)}) collective-permute-start(bf16[128,2048]{1,0:T(8,128)(2,1)S(1)} %shard_map.48.refs_0_.refs_2_), channel_id=1, source_target_pairs={{4,0},{8,12},{5,1},{9,13},{6,2},{10,14},{7,3},{11,15},{20,16},{24,... | collective-permute-start | bytes 1572872 | tf_op jit(solution)/shard_map/ppermute | solution.py:302
  58.5 1.3 %collective-permute-start.14 = (bf16[896,128]{1,0:T(8,128)(2,1)S(1)}, bf16[896,128]{1,0:T(8,128)(2,1)S(1)}, u32[]{:S(2)}, u32[]{:S(2)}) collective-permute-start(bf16[896,128]{1,0:T(8,128)(2,1)S(1)} %get-tuple-element.42.refs_0_.refs_1_), channel_id=1, source_target_pairs={{4,12},{8,0},{5,13},{9,1},{6,14},{10,2},{7,15},{11,3},{20,28},{24,... | collective-permute-start | bytes 688136 | tf_op jit(solution)/shard_map/ppermute | solution.py:299
  59.8 4.4 %shard_map.46 = (f32[2,256,2048]{2,1,0:T(8,128)S(1)}, f32[8,128]{1,0:T(8,128)S(1)}) custom-call(bf16[128,1792]{1,0:T(8,128)(2,1)S(1)} %shard_map.45.refs_0_.refs_3_, bf16[128,1792]{1,0:T(8,128)(2,1)S(1)} %collective-permute-done.6.refs_1_.refs_4_, bf16[2,1,1792,2048]{3,2,1,0:T(8,128)(2,1)S(1)} %get-tuple-element.27.refs_1_.refs_2_, ...), custom_call_target="tpu_custom_call" | custom-call | flops 1000000 | bytes 1024 | tf_op jit(solution)/shard_map/pallas_call | solution.py:41
  64.2 3.9 %collective-permute-start.16 = (bf16[896,128]{1,0:T(8,128)(2,1)S(1)}, bf16[896,128]{1,0:T(8,128)(2,1)S(1)}, u32[]{:S(2)}, u32[]{:S(2)}) collective-permute-start(bf16[896,128]{1,0:T(8,128)(2,1)S(1)} %get-tuple-element.43), channel_id=1, source_target_pairs={{0,8},{4,12},{8,0},{12,4},{1,9},{5,13},{9,1},{13,5},{2,10},{6,14},... | collective-permute-start | bytes 688136 | tf_op jit(solution)/shard_map/ppermute | solution.py:22
  68.2 1.9 %collective-permute-done.14.refs_0_ = bf16[896,128]{1,0:T(8,128)(2,1)S(1)} collective-permute-done((bf16[896,128]{1,0:T(8,128)(2,1)S(1)}, bf16[896,128]{1,0:T(8,128)(2,1)S(1)}, u32[]{:S(2)}, u32[]{:S(2)}) %collective-permute-start.14) | collective-permute-done | bytes 229408 | tf_op jit(solution)/shard_map/ppermute | solution.py:299
  70.1 0.7 shard_map.47.refs_3_.refs_1_
  71.5 4.4 %shard_map.49 = (f32[2,1792,256]{2,1,0:T(8,128)S(1)}, f32[8,128]{1,0:T(8,128)S(1)}) custom-call(bf16[128,2048]{1,0:T(8,128)(2,1)S(1)} %shard_map.48.refs_0_.refs_2_, bf16[128,2048]{1,0:T(8,128)(2,1)S(1)} %collective-permute-done.11.refs_1_, bf16[2,1,1792,2048]{3,2,1,0:T(8,128)(2,1)S(1)} %get-tuple-element.27.refs_1_.refs_2_, ...), custom_call_target="tpu_custom_call" | custom-call | flops 1000000 | bytes 1024 | tf_op jit(solution)/shard_map/pallas_call | solution.py:41
  75.9 3.7 %collective-permute-done.16.refs_0_ = bf16[896,128]{1,0:T(8,128)(2,1)S(1)} collective-permute-done((bf16[896,128]{1,0:T(8,128)(2,1)S(1)}, bf16[896,128]{1,0:T(8,128)(2,1)S(1)}, u32[]{:S(2)}, u32[]{:S(2)}) %collective-permute-start.16) | collective-permute-done | bytes 229408 | tf_op jit(solution)/shard_map/ppermute | solution.py:22
  80.1 3.1 %collective-permute-done.10.refs_0_ = bf16[128,2048]{1,0:T(8,128)(2,1)S(1)} collective-permute-done((bf16[128,2048]{1,0:T(8,128)(2,1)S(1)}, bf16[128,2048]{1,0:T(8,128)(2,1)S(1)}, u32[]{:S(2)}, u32[]{:S(2)}) %collective-permute-start.10) | collective-permute-done | bytes 524320 | tf_op jit(solution)/shard_map/ppermute | solution.py:302
  83.4 3.4 %collective-permute-done.18.refs_3_ = bf16[896,128]{1,0:T(8,128)(2,1)S(1)} collective-permute-done((bf16[896,128]{1,0:T(8,128)(2,1)S(1)}, bf16[896,128]{1,0:T(8,128)(2,1)S(1)}, u32[]{:S(2)}, u32[]{:S(2)}) %collective-permute-start.18) | collective-permute-done | bytes 229408 | tf_op jit(solution)/shard_map/ppermute | solution.py:22
  86.7 0.7 shard_map.59
  88.0 2.4 %collective-permute-start.13 = (f32[2,256]{1,0:T(2,128)S(1)}, f32[2,256]{1,0:T(2,128)S(1)}, u32[]{:S(2)}, u32[]{:S(2)}) collective-permute-start(f32[2,256]{1,0:T(2,128)S(1)} %shard_map.51), channel_id=1, source_target_pairs={{0,12},{4,8},{8,4},{12,0},{1,13},{5,9},{9,5},{13,1},{2,14},{6,10},... | collective-permute-start | bytes 6152 | tf_op jit(solution)/shard_map/ppermute | solution.py:22
  90.4 1.6 %collective-permute-done.19 = f32[2,256]{1,0:T(2,128)S(1)} collective-permute-done((f32[2,256]{1,0:T(2,128)S(1)}, f32[2,256]{1,0:T(2,128)S(1)}, u32[]{:S(2)}, u32[]{:S(2)}) %collective-permute-start.19) | collective-permute-done | bytes 2080 | tf_op jit(solution)/shard_map/ppermute | solution.py:22
  92.0 1.4 %collective-permute-done.13 = f32[2,256]{1,0:T(2,128)S(1)} collective-permute-done((f32[2,256]{1,0:T(2,128)S(1)}, f32[2,256]{1,0:T(2,128)S(1)}, u32[]{:S(2)}, u32[]{:S(2)}) %collective-permute-start.13) | collective-permute-done | bytes 2080 | tf_op jit(solution)/shard_map/ppermute | solution.py:22
  93.5 1.2 %collective-permute-done.20 = f32[2,256]{1,0:T(2,128)S(1)} collective-permute-done((f32[2,256]{1,0:T(2,128)S(1)}, f32[2,256]{1,0:T(2,128)S(1)}, u32[]{:S(2)}, u32[]{:S(2)}) %collective-permute-start.20) | collective-permute-done | bytes 2080 | tf_op jit(solution)/shard_map/ppermute | solution.py:22
  95.2 3.0 %collective-permute-done.21 = f32[2,256]{1,0:T(2,128)S(1)} collective-permute-done((f32[2,256]{1,0:T(2,128)S(1)}, f32[2,256]{1,0:T(2,128)S(1)}, u32[]{:S(2)}, u32[]{:S(2)}) %collective-permute-start.21) | collective-permute-done | bytes 2080 | tf_op jit(solution)/shard_map/ppermute | solution.py:22
  (38 shorter events, 3.6 us)
Async XLA Ops:
  1.2 21.9 %collective-permute-start.1 = (bf16[128,2048]{1,0:T(8,128)(2,1)S(1)}, bf16[128,2048]{1,0:T(8,128)(2,1)S(1)}, u32[]{:S(2)}, u32[]{:S(2)}) collective-permute-start(bf16[128,2048]{1,0:T(8,128)(2,1)S(1)} %get-tuple-element.30), channel_id=1, source_target_pairs={{0,4},{4,8},{8,12},{1,5},{5,9},{9,13},{2,6},{6,10},{10,14},{3,7},{... | collective-permute-start | bytes 1572872 | tf_op jit(solution)/shard_map/ppermute | solution.py:26
  6.2 17.0 %collective-permute-start.2 = (bf16[128,2048]{1,0:T(8,128)(2,1)S(1)}, bf16[128,2048]{1,0:T(8,128)(2,1)S(1)}, u32[]{:S(2)}, u32[]{:S(2)}) collective-permute-start(bf16[128,2048]{1,0:T(8,128)(2,1)S(1)} %get-tuple-element.30), channel_id=1, source_target_pairs={{4,0},{8,4},{12,8},{5,1},{9,5},{13,9},{6,2},{10,6},{14,10},{7,3},{... | collective-permute-start | bytes 1572872 | tf_op jit(solution)/shard_map/ppermute | solution.py:27
  13.6 20.1 %collective-permute-start = (bf16[1792,128]{1,0:T(8,128)(2,1)S(1)}, bf16[1792,128]{1,0:T(8,128)(2,1)S(1)}, u32[]{:S(2)}, u32[]{:S(2)}) collective-permute-start(bf16[1792,128]{1,0:T(8,128)(2,1)S(1)} %get-tuple-element.29), channel_id=1, source_target_pairs={{0,4},{4,0},{8,12},{12,8},{1,5},{5,1},{9,13},{13,9},{2,6},{6,2},{1... | collective-permute-start | bytes 1376264 | tf_op jit(solution)/shard_map/ppermute | solution.py:22
  16.3 27.0 %collective-permute-start.5 = (bf16[128,1792]{1,0:T(8,128)(2,1)S(1)}, bf16[128,1792]{1,0:T(8,128)(2,1)S(1)}, u32[]{:S(2)}, u32[]{:S(2)}) collective-permute-start(bf16[128,1792]{1,0:T(8,128)(2,1)S(1)} %get-tuple-element.35), channel_id=1, source_target_pairs={{0,12},{4,8},{8,4},{12,0},{1,13},{5,9},{9,5},{13,1},{2,14},{6,10},... | collective-permute-start | bytes 1376264 | tf_op jit(solution)/shard_map/ppermute | solution.py:22
  23.2 22.0 %collective-permute-start.4 = (bf16[128,2048]{1,0:T(8,128)(2,1)S(1)}, bf16[128,2048]{1,0:T(8,128)(2,1)S(1)}, u32[]{:S(2)}, u32[]{:S(2)}) collective-permute-start(bf16[128,2048]{1,0:T(8,128)(2,1)S(1)} %shard_map.43.refs_0_), channel_id=1, source_target_pairs={{0,1},{1,0},{2,3},{3,2},{4,5},{5,4},{6,7},{7,6},{8,9},{9,8},{10,11... | collective-permute-start | bytes 1572872 | tf_op jit(solution)/shard_map/ppermute | solution.py:22
  23.3 30.9 %collective-permute-start.8 = (bf16[128,2048]{1,0:T(8,128)(2,1)S(1)}, bf16[128,2048]{1,0:T(8,128)(2,1)S(1)}, u32[]{:S(2)}, u32[]{:S(2)}) collective-permute-start(bf16[128,2048]{1,0:T(8,128)(2,1)S(1)} %get-tuple-element.33.refs_2_.refs_0_.refs_1_), channel_id=1, source_target_pairs={{4,0},{8,4},{5,1},{9,5},{6,2},{10,6},{7,3},{11,7},{20,16},{24,20},... | collective-permute-start | bytes 1572872 | tf_op jit(solution)/shard_map/ppermute | solution.py:27
  24.6 29.6 %collective-permute-start.9 = (bf16[128,2048]{1,0:T(8,128)(2,1)S(1)}, bf16[128,2048]{1,0:T(8,128)(2,1)S(1)}, u32[]{:S(2)}, u32[]{:S(2)}) collective-permute-start(bf16[128,2048]{1,0:T(8,128)(2,1)S(1)} %get-tuple-element.32.refs_1_.refs_2_), channel_id=1, source_target_pairs={{4,8},{8,12},{5,9},{9,13},{6,10},{10,14},{7,11},{11,15},{20,24},{2... | collective-permute-start | bytes 1572872 | tf_op jit(solution)/shard_map/ppermute | solution.py:26
  43.3 11.0 %collective-permute-start.6 = (bf16[128,1792]{1,0:T(8,128)(2,1)S(1)}, bf16[128,1792]{1,0:T(8,128)(2,1)S(1)}, u32[]{:S(2)}, u32[]{:S(2)}) collective-permute-start(bf16[128,1792]{1,0:T(8,128)(2,1)S(1)} %shard_map.45.refs_0_.refs_3_), channel_id=1, source_target_pairs={{0,2},{2,0},{1,3},{3,1},{4,6},{6,4},{5,7},{7,5},{8,10},{10,8},{9,1... | collective-permute-start | bytes 1376264 | tf_op jit(solution)/shard_map/ppermute | solution.py:22
  54.3 9.9 %collective-permute-start.15 = (bf16[896,128]{1,0:T(8,128)(2,1)S(1)}, bf16[896,128]{1,0:T(8,128)(2,1)S(1)}, u32[]{:S(2)}, u32[]{:S(2)}) collective-permute-start(bf16[896,128]{1,0:T(8,128)(2,1)S(1)} %shard_map.54), channel_id=1, source_target_pairs={{0,8},{12,4},{1,9},{13,5},{2,10},{14,6},{3,11},{15,7},{16,24},{28,... | collective-permute-start | bytes 688136 | tf_op jit(solution)/shard_map/ppermute | solution.py:304
  55.6 14.5 %collective-permute-start.3 = (bf16[1792,128]{1,0:T(8,128)(2,1)S(1)}, bf16[1792,128]{1,0:T(8,128)(2,1)S(1)}, u32[]{:S(2)}, u32[]{:S(2)}) collective-permute-start(bf16[1792,128]{1,0:T(8,128)(2,1)S(1)} %shard_map.42.refs_0_), channel_id=1, source_target_pairs={{0,2},{2,0},{1,3},{3,1},{4,6},{6,4},{5,7},{7,5},{8,10},{10,8},{9,1... | collective-permute-start | bytes 1376264 | tf_op jit(solution)/shard_map/ppermute | solution.py:22
  57.2 14.3 %collective-permute-start.11 = (bf16[128,2048]{1,0:T(8,128)(2,1)S(1)}, bf16[128,2048]{1,0:T(8,128)(2,1)S(1)}, u32[]{:S(2)}, u32[]{:S(2)}) collective-permute-start(bf16[128,2048]{1,0:T(8,128)(2,1)S(1)} %shard_map.48.refs_0_.refs_2_), channel_id=1, source_target_pairs={{0,1},{1,0},{2,3},{3,2},{4,5},{5,4},{6,7},{7,6},{8,9},{9,8},{10,11... | collective-permute-start | bytes 1572872 | tf_op jit(solution)/shard_map/ppermute | solution.py:22
  57.2 26.1 %collective-permute-start.10 = (bf16[128,2048]{1,0:T(8,128)(2,1)S(1)}, bf16[128,2048]{1,0:T(8,128)(2,1)S(1)}, u32[]{:S(2)}, u32[]{:S(2)}) collective-permute-start(bf16[128,2048]{1,0:T(8,128)(2,1)S(1)} %shard_map.48.refs_0_.refs_2_), channel_id=1, source_target_pairs={{4,0},{8,12},{5,1},{9,13},{6,2},{10,14},{7,3},{11,15},{20,16},{24,... | collective-permute-start | bytes 1572872 | tf_op jit(solution)/shard_map/ppermute | solution.py:302
  58.5 11.6 %collective-permute-start.14 = (bf16[896,128]{1,0:T(8,128)(2,1)S(1)}, bf16[896,128]{1,0:T(8,128)(2,1)S(1)}, u32[]{:S(2)}, u32[]{:S(2)}) collective-permute-start(bf16[896,128]{1,0:T(8,128)(2,1)S(1)} %get-tuple-element.42.refs_0_.refs_1_), channel_id=1, source_target_pairs={{4,12},{8,0},{5,13},{9,1},{6,14},{10,2},{7,15},{11,3},{20,28},{24,... | collective-permute-start | bytes 688136 | tf_op jit(solution)/shard_map/ppermute | solution.py:299
  64.2 15.4 %collective-permute-start.16 = (bf16[896,128]{1,0:T(8,128)(2,1)S(1)}, bf16[896,128]{1,0:T(8,128)(2,1)S(1)}, u32[]{:S(2)}, u32[]{:S(2)}) collective-permute-start(bf16[896,128]{1,0:T(8,128)(2,1)S(1)} %get-tuple-element.43), channel_id=1, source_target_pairs={{0,8},{4,12},{8,0},{12,4},{1,9},{5,13},{9,1},{13,5},{2,10},{6,14},... | collective-permute-start | bytes 688136 | tf_op jit(solution)/shard_map/ppermute | solution.py:22
  70.9 12.5 %collective-permute-start.17 = (bf16[896,128]{1,0:T(8,128)(2,1)S(1)}, bf16[896,128]{1,0:T(8,128)(2,1)S(1)}, u32[]{:S(2)}, u32[]{:S(2)}) collective-permute-start(bf16[896,128]{1,0:T(8,128)(2,1)S(1)} %shard_map.57.refs_0_), channel_id=1, source_target_pairs={{0,2},{2,0},{1,3},{3,1},{4,6},{6,4},{5,7},{7,5},{8,10},{10,8},{9,1... | collective-permute-start | bytes 688136 | tf_op jit(solution)/shard_map/ppermute | solution.py:22
  79.6 7.2 %collective-permute-start.18 = (bf16[896,128]{1,0:T(8,128)(2,1)S(1)}, bf16[896,128]{1,0:T(8,128)(2,1)S(1)}, u32[]{:S(2)}, u32[]{:S(2)}) collective-permute-start(bf16[896,128]{1,0:T(8,128)(2,1)S(1)} %shard_map.58.refs_1_), channel_id=1, source_target_pairs={{0,2},{2,0},{1,3},{3,1},{4,6},{6,4},{5,7},{7,5},{8,10},{10,8},{9,1... | collective-permute-start | bytes 688136 | tf_op jit(solution)/shard_map/ppermute | solution.py:22
  80.1 10.3 %collective-permute-start.7 = (f32[2,256]{1,0:T(2,128)S(1)}, f32[2,256]{1,0:T(2,128)S(1)}, u32[]{:S(2)}, u32[]{:S(2)}) collective-permute-start(f32[2,256]{1,0:T(2,128)S(1)} %shard_map.47.refs_3_.refs_1_), channel_id=1, source_target_pairs={{0,4},{4,0},{8,12},{12,8},{1,5},{5,1},{9,13},{13,9},{2,6},{6,2},{1... | collective-permute-start | bytes 6152 | tf_op jit(solution)/shard_map/ppermute | solution.py:22
  83.3 4.2 %collective-permute-start.12 = (bf16[128,2048]{1,0:T(8,128)(2,1)S(1)}, bf16[128,2048]{1,0:T(8,128)(2,1)S(1)}, u32[]{:S(2)}, u32[]{:S(2)}) collective-permute-start(bf16[128,2048]{1,0:T(8,128)(2,1)S(1)} %shard_map.50.refs_0_), channel_id=1, source_target_pairs={{0,1},{1,0},{2,3},{3,2},{4,5},{5,4},{6,7},{7,6},{8,9},{9,8},{10,11... | collective-permute-start | bytes 1572872 | tf_op jit(solution)/shard_map/ppermute | solution.py:22
  87.5 4.5 %collective-permute-start.19 = (f32[2,256]{1,0:T(2,128)S(1)}, f32[2,256]{1,0:T(2,128)S(1)}, u32[]{:S(2)}, u32[]{:S(2)}) collective-permute-start(f32[2,256]{1,0:T(2,128)S(1)} %shard_map.59), channel_id=1, source_target_pairs={{0,8},{4,12},{8,0},{12,4},{1,9},{5,13},{9,1},{13,5},{2,10},{6,14},... | collective-permute-start | bytes 6152 | tf_op jit(solution)/shard_map/ppermute | solution.py:22
  88.0 5.4 %collective-permute-start.13 = (f32[2,256]{1,0:T(2,128)S(1)}, f32[2,256]{1,0:T(2,128)S(1)}, u32[]{:S(2)}, u32[]{:S(2)}) collective-permute-start(f32[2,256]{1,0:T(2,128)S(1)} %shard_map.51), channel_id=1, source_target_pairs={{0,12},{4,8},{8,4},{12,0},{1,13},{5,9},{9,5},{13,1},{2,14},{6,10},... | collective-permute-start | bytes 6152 | tf_op jit(solution)/shard_map/ppermute | solution.py:22
  93.5 1.2 %collective-permute-start.20 = (f32[2,256]{1,0:T(2,128)S(1)}, f32[2,256]{1,0:T(2,128)S(1)}, u32[]{:S(2)}, u32[]{:S(2)}) collective-permute-start(f32[2,256]{1,0:T(2,128)S(1)} %add_add_fusion), channel_id=1, source_target_pairs={{0,1},{1,0},{2,3},{3,2},{4,5},{5,4},{6,7},{7,6},{8,9},{9,8},{10,11... | collective-permute-start | bytes 6152 | tf_op jit(solution)/shard_map/ppermute | solution.py:22
  94.6 3.6 %collective-permute-start.21 = (f32[2,256]{1,0:T(2,128)S(1)}, f32[2,256]{1,0:T(2,128)S(1)}, u32[]{:S(2)}, u32[]{:S(2)}) collective-permute-start(f32[2,256]{1,0:T(2,128)S(1)} %add.18), channel_id=1, source_target_pairs={{0,2},{2,0},{1,3},{3,1},{4,6},{6,4},{5,7},{7,5},{8,10},{10,8},{9,1... | collective-permute-start | bytes 6152 | tf_op jit(solution)/shard_map/ppermute | solution.py:22

commit v24 on v21

--- a/solution.py
+++ b/solution.py
@@ -287,7 +287,7 @@
     mixes, token = {}, scores
     for d in early:
         mixes[d], token = mixed(acts_of(from_partner(hops, d, count)), queries, SHORT, [token])
-    tail = [trade(hold([block], [token])[0], {"dp": late}) for block in sent[len(early) :]]
+    tail = [trade(hold([block], [token, *hops[-1]])[0], {"dp": late}) for block in sent[len(early) :]]
     sides = to_columns(hold([arrived[far]], [*hops[1], *[arrived[d] for d in early]])[0])
     block = from_partner(hops, late, count, [token] + sides)
     end = lax.ppermute(block, "dp", [(1, 0), (count - 2, count - 1)])

time: 92.8 us -> 94.8 us (1.022)
  waiting for transfers between devices: 36 us -> 43.7 us
  starting transfers between devices: 28.5 us -> 22.7 us
    ppermute x16, waiting for transfers between devices: 30.2 us -> 36.3 us  [trade(): return lax.ppermute(block, axes, route[::-1] if backwards else route)]
    ppermute x16, starting transfers between devices: 18.9 us -> 13.1 us  [trade(): return lax.ppermute(block, axes, route[::-1] if backwards else route)]
    ppermute x2, waiting for transfers between devices: 1.05 us -> 3.94 us  [pass_on(): lax.ppermute(block[1], 'dp', [(i, i - 1) for i in range(1, count - step +...]
    ppermute x1, waiting for transfers between devices: 4.69 us -> 3.45 us  [on_device(): end = lax.ppermute(block, 'dp', [(1, 0), (count - 2, count - 1)])]
where the time goes in v24:
time: 94.8 us; the launch traced here: 94.6 us
  waiting for transfers between devices  43.7 us (46%)
  Pallas kernels  27.4 us (29%)
  starting transfers between devices  22.7 us (24%)
    ppermute x16, waiting for transfers between devices, trade(): return lax.ppermute(block, axes, route[::-1] if backwards else route)  36.3 us
    pallas_call x11, Pallas kernels, call(): pl.pallas_call(body, in_specs=[NEAR] * len(arrays) + [ANYWHERE] * skip, o...  20 us
    ppermute x16, starting transfers between devices, trade(): return lax.ppermute(block, axes, route[::-1] if backwards else route)  13.1 us
    pallas_call x2, Pallas kernels, fetch(): pl.pallas_call(kernel, in_specs=[ANYWHERE] * len(arrays), out_specs=[NEAR...  7.3 us
    ppermute x2, starting transfers between devices, pass_on(): lax.ppermute(block[0], 'dp', [(i, i + 1) for i in range(step - 1, count -...  5.65 us
    ppermute x2, waiting for transfers between devices, pass_on(): lax.ppermute(block[1], 'dp', [(i, i - 1) for i in range(1, count - step +...  3.94 us
    ppermute x1, waiting for transfers between devices, on_device(): end = lax.ppermute(block, 'dp', [(1, 0), (count - 2, count - 1)])  3.45 us
    ppermute x2, starting transfers between devices, pass_on(): lax.ppermute(block[1], 'dp', [(i, i - 1) for i in range(1, count - step +...  2.58 us
  transfers between devices with their start and end apart: 21, of which 12 were waited for; matrix products, arithmetic and copies ran while one was open for 0% of the time, Pallas kernels for 28%

profile of v24, /device:TPU:0, one launch (start us, length us, event | category | flops | bytes accessed | tf_op | source)
XLA Modules:
  0.0 94.6 jit_solution(13212789396714738400)
XLA Ops:
  0.0 1.2 %shard_map.40 = (bf16[128,2048]{1,0:T(8,128)(2,1)S(1)}, bf16[128,1792]{1,0:T(8,128)(2,1)S(1)}) custom-call(bf16[256,2048]{1,0:T(8,128)(2,1)} %acts_ref.3, bf16[256,7168]{1,0:T(8,128)(2,1)} %grads_ref.3), custom_call_target="tpu_custom_call" | custom-call | flops 1024 | bytes 1024 | tf_op jit(solution)/shard_map/pallas_call | solution.py:53
  1.2 5.0 %collective-permute-start.1 = (bf16[128,2048]{1,0:T(8,128)(2,1)S(1)}, bf16[128,2048]{1,0:T(8,128)(2,1)S(1)}, u32[]{:S(2)}, u32[]{:S(2)}) collective-permute-start(bf16[128,2048]{1,0:T(8,128)(2,1)S(1)} %get-tuple-element.28), channel_id=1, source_target_pairs={{0,4},{4,8},{8,12},{1,5},{5,9},{9,13},{2,6},{6,10},{10,14},{3,7},{... | collective-permute-start | bytes 1572872 | tf_op jit(solution)/shard_map/ppermute | solution.py:26
  6.2 1.3 %collective-permute-start.2 = (bf16[128,2048]{1,0:T(8,128)(2,1)S(1)}, bf16[128,2048]{1,0:T(8,128)(2,1)S(1)}, u32[]{:S(2)}, u32[]{:S(2)}) collective-permute-start(bf16[128,2048]{1,0:T(8,128)(2,1)S(1)} %get-tuple-element.28), channel_id=1, source_target_pairs={{4,0},{8,4},{12,8},{5,1},{9,5},{13,9},{6,2},{10,6},{14,10},{7,3},{... | collective-permute-start | bytes 1572872 | tf_op jit(solution)/shard_map/ppermute | solution.py:27
  7.5 4.7 %collective-permute-start.5 = (bf16[128,1792]{1,0:T(8,128)(2,1)S(1)}, bf16[128,1792]{1,0:T(8,128)(2,1)S(1)}, u32[]{:S(2)}, u32[]{:S(2)}) collective-permute-start(bf16[128,1792]{1,0:T(8,128)(2,1)S(1)} %get-tuple-element.33), channel_id=1, source_target_pairs={{0,12},{4,8},{8,4},{12,0},{1,13},{5,9},{9,5},{13,1},{2,14},{6,10},... | collective-permute-start | bytes 1376264 | tf_op jit(solution)/shard_map/ppermute | solution.py:22
  12.2 6.1 %shard_map.37 = (bf16[2,1,1792,2048]{3,2,1,0:T(8,128)(2,1)S(1)}, bf16[256,2048]{1,0:T(8,128)(2,1)S(1)}, bf16[1792,256]{1,0:T(8,128)(2,1)S(1)}, bf16[1792,128]{1,...) custom-call(bf16[256,2048]{1,0:T(8,128)(2,1)} %acts_ref.3, bf16[256,7168]{1,0:T(8,128)(2,1)} %grads_ref.3, ...), custom_call_target="tpu_custom_call" | custom-call | flops 1024 | bytes 1024 | tf_op jit(solution)/shard_map/pallas_call | solution.py:53
  18.4 4.4 %shard_map.38 = (f32[2,1792,256]{2,1,0:T(8,128)S(1)}, f32[8,128]{1,0:T(8,128)S(1)}) custom-call(bf16[256,2048]{1,0:T(8,128)(2,1)S(1)} %get-tuple-element.24.refs_0_, bf16[2,1,1792,2048]{3,2,1,0:T(8,128)(2,1)S(1)} %get-tuple-element.25.refs_1_.refs_2_), custom_call_target="tpu_custom_call" | custom-call | flops 1000000 | bytes 1024 | tf_op jit(solution)/shard_map/pallas_call | solution.py:41
  22.8 1.0 %collective-permute-done.2.refs_1_ = bf16[128,2048]{1,0:T(8,128)(2,1)S(1)} collective-permute-done((bf16[128,2048]{1,0:T(8,128)(2,1)S(1)}, bf16[128,2048]{1,0:T(8,128)(2,1)S(1)}, u32[]{:S(2)}, u32[]{:S(2)}) %collective-permute-start.2) | collective-permute-done | bytes 524320 | tf_op jit(solution)/shard_map/ppermute | solution.py:27
  24.0 0.7 collective-permute-start.9
  24.7 1.3 %collective-permute-start.8 = (bf16[128,2048]{1,0:T(8,128)(2,1)S(1)}, bf16[128,2048]{1,0:T(8,128)(2,1)S(1)}, u32[]{:S(2)}, u32[]{:S(2)}) collective-permute-start(bf16[128,2048]{1,0:T(8,128)(2,1)S(1)} %get-tuple-element.31.refs_2_.refs_0_.refs_1_), channel_id=1, source_target_pairs={{4,0},{8,4},{5,1},{9,5},{6,2},{10,6},{7,3},{11,7},{20,16},{24,20},... | collective-permute-start | bytes 1572872 | tf_op jit(solution)/shard_map/ppermute | solution.py:27
  26.0 8.8 %collective-permute-done.5.refs_0_ = bf16[128,1792]{1,0:T(8,128)(2,1)S(1)} collective-permute-done((bf16[128,1792]{1,0:T(8,128)(2,1)S(1)}, bf16[128,1792]{1,0:T(8,128)(2,1)S(1)}, u32[]{:S(2)}, u32[]{:S(2)}) %collective-permute-start.5) | collective-permute-done | bytes 458784 | tf_op jit(solution)/shard_map/ppermute | solution.py:22
  34.8 7.8 %collective-permute-done.refs_0_.refs_3_ = bf16[1792,128]{1,0:T(8,128)(2,1)S(1)} collective-permute-done((bf16[1792,128]{1,0:T(8,128)(2,1)S(1)}, bf16[1792,128]{1,0:T(8,128)(2,1)S(1)}, u32[]{:S(2)}, u32[]{:S(2)}) %collective-permute-start) | collective-permute-done | bytes 458784 | tf_op jit(solution)/shard_map/ppermute | solution.py:22
  42.6 1.5 %collective-permute-start.6 = (bf16[128,1792]{1,0:T(8,128)(2,1)S(1)}, bf16[128,1792]{1,0:T(8,128)(2,1)S(1)}, u32[]{:S(2)}, u32[]{:S(2)}) collective-permute-start(bf16[128,1792]{1,0:T(8,128)(2,1)S(1)} %shard_map.45.refs_0_.refs_3_), channel_id=1, source_target_pairs={{0,2},{2,0},{1,3},{3,1},{4,6},{6,4},{5,7},{7,5},{8,10},{10,8},{9,1... | collective-permute-start | bytes 1376264 | tf_op jit(solution)/shard_map/ppermute | solution.py:22
  45.0 4.4 %shard_map.44 = (f32[2,1792,256]{2,1,0:T(8,128)S(1)}, f32[8,128]{1,0:T(8,128)S(1)}) custom-call(bf16[128,2048]{1,0:T(8,128)(2,1)S(1)} %shard_map.43.refs_0_, bf16[128,2048]{1,0:T(8,128)(2,1)S(1)} %collective-permute-done.4.refs_1_, bf16[2,1,1792,2048]{3,2,1,0:T(8,128)(2,1)S(1)} %get-tuple-element.25.refs_1_.refs_2_, f32[2,256]{1,0:T(2,128)S(1)} %shard_map.39.refs_3_), custom_call_target="tpu_custom_call" | custom-call | flops 1000000 | bytes 1024 | tf_op jit(solution)/shard_map/pallas_call | solution.py:41
  49.4 2.9 %collective-permute-done.8.refs_0_.refs_3_ = bf16[128,2048]{1,0:T(8,128)(2,1)S(1)} collective-permute-done((bf16[128,2048]{1,0:T(8,128)(2,1)S(1)}, bf16[128,2048]{1,0:T(8,128)(2,1)S(1)}, u32[]{:S(2)}, u32[]{:S(2)}) %collective-permute-start.8) | collective-permute-done | bytes 524320 | tf_op jit(solution)/shard_map/ppermute | solution.py:27
  52.9 3.2 %collective-permute-done.6.refs_1_.refs_4_ = bf16[128,1792]{1,0:T(8,128)(2,1)S(1)} collective-permute-done((bf16[128,1792]{1,0:T(8,128)(2,1)S(1)}, bf16[128,1792]{1,0:T(8,128)(2,1)S(1)}, u32[]{:S(2)}, u32[]{:S(2)}) %collective-permute-start.6) | collective-permute-done | bytes 458784 | tf_op jit(solution)/shard_map/ppermute | solution.py:22
  56.2 1.3 %collective-permute-start.10 = (bf16[128,2048]{1,0:T(8,128)(2,1)S(1)}, bf16[128,2048]{1,0:T(8,128)(2,1)S(1)}, u32[]{:S(2)}, u32[]{:S(2)}) collective-permute-start(bf16[128,2048]{1,0:T(8,128)(2,1)S(1)} %shard_map.48.refs_0_), channel_id=1, source_target_pairs={{4,0},{8,12},{5,1},{9,13},{6,2},{10,14},{7,3},{11,15},{20,16},{24,... | collective-permute-start | bytes 1572872 | tf_op jit(solution)/shard_map/ppermute | solution.py:293
  57.5 1.5 %collective-permute-start.15 = (bf16[896,128]{1,0:T(8,128)(2,1)S(1)}, bf16[896,128]{1,0:T(8,128)(2,1)S(1)}, u32[]{:S(2)}, u32[]{:S(2)}) collective-permute-start(bf16[896,128]{1,0:T(8,128)(2,1)S(1)} %shard_map.54), channel_id=1, source_target_pairs={{0,8},{4,12},{8,0},{12,4},{1,9},{5,13},{9,1},{13,5},{2,10},{6,14},... | collective-permute-start | bytes 688136 | tf_op jit(solution)/shard_map/ppermute | solution.py:22
  59.0 4.4 %shard_map.46 = (f32[2,256,2048]{2,1,0:T(8,128)S(1)}, f32[8,128]{1,0:T(8,128)S(1)}) custom-call(bf16[128,1792]{1,0:T(8,128)(2,1)S(1)} %shard_map.45.refs_0_.refs_3_, bf16[128,1792]{1,0:T(8,128)(2,1)S(1)} %collective-permute-done.6.refs_1_.refs_4_, bf16[2,1,1792,2048]{3,2,1,0:T(8,128)(2,1)S(1)} %get-tuple-element.25.refs_1_.refs_2_, ...), custom_call_target="tpu_custom_call" | custom-call | flops 1000000 | bytes 1024 | tf_op jit(solution)/shard_map/pallas_call | solution.py:41
  63.4 0.8 shard_map.47.refs_3_.refs_1_
  64.2 6.4 %collective-permute-done.14.refs_0_ = bf16[896,128]{1,0:T(8,128)(2,1)S(1)} collective-permute-done((bf16[896,128]{1,0:T(8,128)(2,1)S(1)}, bf16[896,128]{1,0:T(8,128)(2,1)S(1)}, u32[]{:S(2)}, u32[]{:S(2)}) %collective-permute-start.14) | collective-permute-done | bytes 229408 | tf_op jit(solution)/shard_map/ppermute | solution.py:22
  70.5 1.5 %collective-permute-start.16 = (bf16[896,128]{1,0:T(8,128)(2,1)S(1)}, bf16[896,128]{1,0:T(8,128)(2,1)S(1)}, u32[]{:S(2)}, u32[]{:S(2)}) collective-permute-start(bf16[896,128]{1,0:T(8,128)(2,1)S(1)} %shard_map.53.refs_0_), channel_id=1, source_target_pairs={{0,2},{2,0},{1,3},{3,1},{4,6},{6,4},{5,7},{7,5},{8,10},{10,8},{9,1... | collective-permute-start | bytes 688136 | tf_op jit(solution)/shard_map/ppermute | solution.py:22
  72.0 4.4 %shard_map.49 = (f32[2,1792,256]{2,1,0:T(8,128)S(1)}, f32[8,128]{1,0:T(8,128)S(1)}) custom-call(bf16[128,2048]{1,0:T(8,128)(2,1)S(1)} %shard_map.48.refs_0_, bf16[128,2048]{1,0:T(8,128)(2,1)S(1)} %collective-permute-done.11.refs_1_, bf16[2,1,1792,2048]{3,2,1,0:T(8,128)(2,1)S(1)} %get-tuple-element.25.refs_1_.refs_2_, f32[2,256]{1,0:T(2,128)S(1)} %shard_map.47.refs_3_.refs_1_), custom_call_target="tpu_custom_call" | custom-call | flops 1000000 | bytes 1024 | tf_op jit(solution)/shard_map/pallas_call | solution.py:41
  76.4 0.6 collective-permute-start.17
  77.0 3.5 %collective-permute-done.10.refs_0_ = bf16[128,2048]{1,0:T(8,128)(2,1)S(1)} collective-permute-done((bf16[128,2048]{1,0:T(8,128)(2,1)S(1)}, bf16[128,2048]{1,0:T(8,128)(2,1)S(1)}, u32[]{:S(2)}, u32[]{:S(2)}) %collective-permute-start.10) | collective-permute-done | bytes 524320 | tf_op jit(solution)/shard_map/ppermute | solution.py:293
  80.7 1.9 %collective-permute-done.17.refs_3_ = bf16[896,128]{1,0:T(8,128)(2,1)S(1)} collective-permute-done((bf16[896,128]{1,0:T(8,128)(2,1)S(1)}, bf16[896,128]{1,0:T(8,128)(2,1)S(1)}, u32[]{:S(2)}, u32[]{:S(2)}) %collective-permute-start.17) | collective-permute-done | bytes 229408 | tf_op jit(solution)/shard_map/ppermute | solution.py:22
  82.5 0.7 shard_map.56
  83.8 1.2 %collective-permute-start.13 = (f32[2,256]{1,0:T(2,128)S(1)}, f32[2,256]{1,0:T(2,128)S(1)}, u32[]{:S(2)}, u32[]{:S(2)}) collective-permute-start(f32[2,256]{1,0:T(2,128)S(1)} %shard_map.51), channel_id=1, source_target_pairs={{0,12},{4,8},{8,4},{12,0},{1,13},{5,9},{9,5},{13,1},{2,14},{6,10},... | collective-permute-start | bytes 6152 | tf_op jit(solution)/shard_map/ppermute | solution.py:22
  85.0 2.8 %collective-permute-done.18 = f32[2,256]{1,0:T(2,128)S(1)} collective-permute-done((f32[2,256]{1,0:T(2,128)S(1)}, f32[2,256]{1,0:T(2,128)S(1)}, u32[]{:S(2)}, u32[]{:S(2)}) %collective-permute-start.18) | collective-permute-done | bytes 2080 | tf_op jit(solution)/shard_map/ppermute | solution.py:22
  87.8 1.4 %collective-permute-done.13 = f32[2,256]{1,0:T(2,128)S(1)} collective-permute-done((f32[2,256]{1,0:T(2,128)S(1)}, f32[2,256]{1,0:T(2,128)S(1)}, u32[]{:S(2)}, u32[]{:S(2)}) %collective-permute-start.13) | collective-permute-done | bytes 2080 | tf_op jit(solution)/shard_map/ppermute | solution.py:22
  89.2 1.2 %collective-permute-done.19 = f32[2,256]{1,0:T(2,128)S(1)} collective-permute-done((f32[2,256]{1,0:T(2,128)S(1)}, f32[2,256]{1,0:T(2,128)S(1)}, u32[]{:S(2)}, u32[]{:S(2)}) %collective-permute-start.19) | collective-permute-done | bytes 2080 | tf_op jit(solution)/shard_map/ppermute | solution.py:22
  90.4 0.7 collective-permute-start.20
  91.1 2.9 %collective-permute-done.20 = f32[2,256]{1,0:T(2,128)S(1)} collective-permute-done((f32[2,256]{1,0:T(2,128)S(1)}, f32[2,256]{1,0:T(2,128)S(1)}, u32[]{:S(2)}, u32[]{:S(2)}) %collective-permute-start.20) | collective-permute-done | bytes 2080 | tf_op jit(solution)/shard_map/ppermute | solution.py:22
  (33 shorter events, 3.1 us)
Async XLA Ops:
  1.2 21.6 %collective-permute-start.1 = (bf16[128,2048]{1,0:T(8,128)(2,1)S(1)}, bf16[128,2048]{1,0:T(8,128)(2,1)S(1)}, u32[]{:S(2)}, u32[]{:S(2)}) collective-permute-start(bf16[128,2048]{1,0:T(8,128)(2,1)S(1)} %get-tuple-element.28), channel_id=1, source_target_pairs={{0,4},{4,8},{8,12},{1,5},{5,9},{9,13},{2,6},{6,10},{10,14},{3,7},{... | collective-permute-start | bytes 1572872 | tf_op jit(solution)/shard_map/ppermute | solution.py:26
  6.2 17.7 %collective-permute-start.2 = (bf16[128,2048]{1,0:T(8,128)(2,1)S(1)}, bf16[128,2048]{1,0:T(8,128)(2,1)S(1)}, u32[]{:S(2)}, u32[]{:S(2)}) collective-permute-start(bf16[128,2048]{1,0:T(8,128)(2,1)S(1)} %get-tuple-element.28), channel_id=1, source_target_pairs={{4,0},{8,4},{12,8},{5,1},{9,5},{13,9},{6,2},{10,6},{14,10},{7,3},{... | collective-permute-start | bytes 1572872 | tf_op jit(solution)/shard_map/ppermute | solution.py:27
  7.5 27.3 %collective-permute-start.5 = (bf16[128,1792]{1,0:T(8,128)(2,1)S(1)}, bf16[128,1792]{1,0:T(8,128)(2,1)S(1)}, u32[]{:S(2)}, u32[]{:S(2)}) collective-permute-start(bf16[128,1792]{1,0:T(8,128)(2,1)S(1)} %get-tuple-element.33), channel_id=1, source_target_pairs={{0,12},{4,8},{8,4},{12,0},{1,13},{5,9},{9,5},{13,1},{2,14},{6,10},... | collective-permute-start | bytes 1376264 | tf_op jit(solution)/shard_map/ppermute | solution.py:22
  18.3 24.3 %collective-permute-start = (bf16[1792,128]{1,0:T(8,128)(2,1)S(1)}, bf16[1792,128]{1,0:T(8,128)(2,1)S(1)}, u32[]{:S(2)}, u32[]{:S(2)}) collective-permute-start(bf16[1792,128]{1,0:T(8,128)(2,1)S(1)} %get-tuple-element.27), channel_id=1, source_target_pairs={{0,4},{4,0},{8,12},{12,8},{1,5},{5,1},{9,13},{13,9},{2,6},{6,2},{1... | collective-permute-start | bytes 1376264 | tf_op jit(solution)/shard_map/ppermute | solution.py:22
  23.9 21.2 %collective-permute-start.4 = (bf16[128,2048]{1,0:T(8,128)(2,1)S(1)}, bf16[128,2048]{1,0:T(8,128)(2,1)S(1)}, u32[]{:S(2)}, u32[]{:S(2)}) collective-permute-start(bf16[128,2048]{1,0:T(8,128)(2,1)S(1)} %shard_map.43.refs_0_), channel_id=1, source_target_pairs={{0,1},{1,0},{2,3},{3,2},{4,5},{5,4},{6,7},{7,6},{8,9},{9,8},{10,11... | collective-permute-start | bytes 1572872 | tf_op jit(solution)/shard_map/ppermute | solution.py:22
  24.0 25.5 %collective-permute-start.9 = (bf16[128,2048]{1,0:T(8,128)(2,1)S(1)}, bf16[128,2048]{1,0:T(8,128)(2,1)S(1)}, u32[]{:S(2)}, u32[]{:S(2)}) collective-permute-start(bf16[128,2048]{1,0:T(8,128)(2,1)S(1)} %get-tuple-element.30.refs_1_.refs_2_), channel_id=1, source_target_pairs={{4,8},{8,12},{5,9},{9,13},{6,10},{10,14},{7,11},{11,15},{20,24},{2... | collective-permute-start | bytes 1572872 | tf_op jit(solution)/shard_map/ppermute | solution.py:26
  24.7 27.7 %collective-permute-start.8 = (bf16[128,2048]{1,0:T(8,128)(2,1)S(1)}, bf16[128,2048]{1,0:T(8,128)(2,1)S(1)}, u32[]{:S(2)}, u32[]{:S(2)}) collective-permute-start(bf16[128,2048]{1,0:T(8,128)(2,1)S(1)} %get-tuple-element.31.refs_2_.refs_0_.refs_1_), channel_id=1, source_target_pairs={{4,0},{8,4},{5,1},{9,5},{6,2},{10,6},{7,3},{11,7},{20,16},{24,20},... | collective-permute-start | bytes 1572872 | tf_op jit(solution)/shard_map/ppermute | solution.py:27
  42.6 13.5 %collective-permute-start.6 = (bf16[128,1792]{1,0:T(8,128)(2,1)S(1)}, bf16[128,1792]{1,0:T(8,128)(2,1)S(1)}, u32[]{:S(2)}, u32[]{:S(2)}) collective-permute-start(bf16[128,1792]{1,0:T(8,128)(2,1)S(1)} %shard_map.45.refs_0_.refs_3_), channel_id=1, source_target_pairs={{0,2},{2,0},{1,3},{3,1},{4,6},{6,4},{5,7},{7,5},{8,10},{10,8},{9,1... | collective-permute-start | bytes 1376264 | tf_op jit(solution)/shard_map/ppermute | solution.py:22
  44.1 19.3 %collective-permute-start.3 = (bf16[1792,128]{1,0:T(8,128)(2,1)S(1)}, bf16[1792,128]{1,0:T(8,128)(2,1)S(1)}, u32[]{:S(2)}, u32[]{:S(2)}) collective-permute-start(bf16[1792,128]{1,0:T(8,128)(2,1)S(1)} %shard_map.42.refs_0_), channel_id=1, source_target_pairs={{0,2},{2,0},{1,3},{3,1},{4,6},{6,4},{5,7},{7,5},{8,10},{10,8},{9,1... | collective-permute-start | bytes 1376264 | tf_op jit(solution)/shard_map/ppermute | solution.py:22
  52.3 18.2 %collective-permute-start.14 = (bf16[896,128]{1,0:T(8,128)(2,1)S(1)}, bf16[896,128]{1,0:T(8,128)(2,1)S(1)}, u32[]{:S(2)}, u32[]{:S(2)}) collective-permute-start(bf16[896,128]{1,0:T(8,128)(2,1)S(1)} %shard_map.52), channel_id=1, source_target_pairs={{0,8},{4,12},{8,0},{12,4},{1,9},{5,13},{9,1},{13,5},{2,10},{6,14},... | collective-permute-start | bytes 688136 | tf_op jit(solution)/shard_map/ppermute | solution.py:22
  56.1 15.9 %collective-permute-start.11 = (bf16[128,2048]{1,0:T(8,128)(2,1)S(1)}, bf16[128,2048]{1,0:T(8,128)(2,1)S(1)}, u32[]{:S(2)}, u32[]{:S(2)}) collective-permute-start(bf16[128,2048]{1,0:T(8,128)(2,1)S(1)} %shard_map.48.refs_0_), channel_id=1, source_target_pairs={{0,1},{1,0},{2,3},{3,2},{4,5},{5,4},{6,7},{7,6},{8,9},{9,8},{10,11... | collective-permute-start | bytes 1572872 | tf_op jit(solution)/shard_map/ppermute | solution.py:22
  56.2 24.3 %collective-permute-start.10 = (bf16[128,2048]{1,0:T(8,128)(2,1)S(1)}, bf16[128,2048]{1,0:T(8,128)(2,1)S(1)}, u32[]{:S(2)}, u32[]{:S(2)}) collective-permute-start(bf16[128,2048]{1,0:T(8,128)(2,1)S(1)} %shard_map.48.refs_0_), channel_id=1, source_target_pairs={{4,0},{8,12},{5,1},{9,13},{6,2},{10,14},{7,3},{11,15},{20,16},{24,... | collective-permute-start | bytes 1572872 | tf_op jit(solution)/shard_map/ppermute | solution.py:293
  57.5 18.9 %collective-permute-start.15 = (bf16[896,128]{1,0:T(8,128)(2,1)S(1)}, bf16[896,128]{1,0:T(8,128)(2,1)S(1)}, u32[]{:S(2)}, u32[]{:S(2)}) collective-permute-start(bf16[896,128]{1,0:T(8,128)(2,1)S(1)} %shard_map.54), channel_id=1, source_target_pairs={{0,8},{4,12},{8,0},{12,4},{1,9},{5,13},{9,1},{13,5},{2,10},{6,14},... | collective-permute-start | bytes 688136 | tf_op jit(solution)/shard_map/ppermute | solution.py:22
  70.5 10.1 %collective-permute-start.16 = (bf16[896,128]{1,0:T(8,128)(2,1)S(1)}, bf16[896,128]{1,0:T(8,128)(2,1)S(1)}, u32[]{:S(2)}, u32[]{:S(2)}) collective-permute-start(bf16[896,128]{1,0:T(8,128)(2,1)S(1)} %shard_map.53.refs_0_), channel_id=1, source_target_pairs={{0,2},{2,0},{1,3},{3,1},{4,6},{6,4},{5,7},{7,5},{8,10},{10,8},{9,1... | collective-permute-start | bytes 688136 | tf_op jit(solution)/shard_map/ppermute | solution.py:22
  76.4 6.1 %collective-permute-start.17 = (bf16[896,128]{1,0:T(8,128)(2,1)S(1)}, bf16[896,128]{1,0:T(8,128)(2,1)S(1)}, u32[]{:S(2)}, u32[]{:S(2)}) collective-permute-start(bf16[896,128]{1,0:T(8,128)(2,1)S(1)} %shard_map.55.refs_1_), channel_id=1, source_target_pairs={{0,2},{2,0},{1,3},{3,1},{4,6},{6,4},{5,7},{7,5},{8,10},{10,8},{9,1... | collective-permute-start | bytes 688136 | tf_op jit(solution)/shard_map/ppermute | solution.py:22
  77.0 7.9 %collective-permute-start.7 = (f32[2,256]{1,0:T(2,128)S(1)}, f32[2,256]{1,0:T(2,128)S(1)}, u32[]{:S(2)}, u32[]{:S(2)}) collective-permute-start(f32[2,256]{1,0:T(2,128)S(1)} %shard_map.47.refs_3_.refs_1_), channel_id=1, source_target_pairs={{0,4},{4,0},{8,12},{12,8},{1,5},{5,1},{9,13},{13,9},{2,6},{6,2},{1... | collective-permute-start | bytes 6152 | tf_op jit(solution)/shard_map/ppermute | solution.py:22
  80.5 2.8 %collective-permute-start.12 = (bf16[128,2048]{1,0:T(8,128)(2,1)S(1)}, bf16[128,2048]{1,0:T(8,128)(2,1)S(1)}, u32[]{:S(2)}, u32[]{:S(2)}) collective-permute-start(bf16[128,2048]{1,0:T(8,128)(2,1)S(1)} %shard_map.50.refs_0_), channel_id=1, source_target_pairs={{0,1},{1,0},{2,3},{3,2},{4,5},{5,4},{6,7},{7,6},{8,9},{9,8},{10,11... | collective-permute-start | bytes 1572872 | tf_op jit(solution)/shard_map/ppermute | solution.py:22
  83.2 4.5 %collective-permute-start.18 = (f32[2,256]{1,0:T(2,128)S(1)}, f32[2,256]{1,0:T(2,128)S(1)}, u32[]{:S(2)}, u32[]{:S(2)}) collective-permute-start(f32[2,256]{1,0:T(2,128)S(1)} %shard_map.56), channel_id=1, source_target_pairs={{0,8},{4,12},{8,0},{12,4},{1,9},{5,13},{9,1},{13,5},{2,10},{6,14},... | collective-permute-start | bytes 6152 | tf_op jit(solution)/shard_map/ppermute | solution.py:22
  83.8 5.4 %collective-permute-start.13 = (f32[2,256]{1,0:T(2,128)S(1)}, f32[2,256]{1,0:T(2,128)S(1)}, u32[]{:S(2)}, u32[]{:S(2)}) collective-permute-start(f32[2,256]{1,0:T(2,128)S(1)} %shard_map.51), channel_id=1, source_target_pairs={{0,12},{4,8},{8,4},{12,0},{1,13},{5,9},{9,5},{13,1},{2,14},{6,10},... | collective-permute-start | bytes 6152 | tf_op jit(solution)/shard_map/ppermute | solution.py:22
  89.2 1.2 %collective-permute-start.19 = (f32[2,256]{1,0:T(2,128)S(1)}, f32[2,256]{1,0:T(2,128)S(1)}, u32[]{:S(2)}, u32[]{:S(2)}) collective-permute-start(f32[2,256]{1,0:T(2,128)S(1)} %add_add_fusion), channel_id=1, source_target_pairs={{0,1},{1,0},{2,3},{3,2},{4,5},{5,4},{6,7},{7,6},{8,9},{9,8},{10,11... | collective-permute-start | bytes 6152 | tf_op jit(solution)/shard_map/ppermute | solution.py:22
  90.4 3.6 %collective-permute-start.20 = (f32[2,256]{1,0:T(2,128)S(1)}, f32[2,256]{1,0:T(2,128)S(1)}, u32[]{:S(2)}, u32[]{:S(2)}) collective-permute-start(f32[2,256]{1,0:T(2,128)S(1)} %add.18), channel_id=1, source_target_pairs={{0,2},{2,0},{1,3},{3,1},{4,6},{6,4},{5,7},{7,5},{8,10},{10,8},{9,1... | collective-permute-start | bytes 6152 | tf_op jit(solution)/shard_map/ppermute | solution.py:22

commit v25 on v24

--- a/solution.py
+++ b/solution.py
@@ -301,7 +301,7 @@
         terms.append(trade(token, {"dp": d}))
 
     mix, done = mixed(acts_of(block), queries, SHORT, [token])
-    tail = [to_columns(hold([piece], [done if p else token], LONG)[0]) for p, piece in enumerate(tail)]
+    tail = [to_columns(hold([piece], [done], LONG)[0]) for piece in tail]
     block = from_partner(hops, far, count, [done])
     terms.append(trade(scores_of_acts(*acts_of(block), proj), {"dp": far}))
     terms.append(trade(scores_of_grads([list(sides) for sides in zip(*tail)], mix, (), LONG), {"dp": late}))

time: 94.8 us -> 98.2 us (1.036)
  waiting for transfers between devices: 43.7 us -> 46.1 us
    ppermute x16, waiting for transfers between devices: 36.3 us -> 43.5 us  [trade(): return lax.ppermute(block, axes, route[::-1] if backwards else route)]
    ppermute x2, waiting for transfers between devices: 3.94 us -> 0.01 us  [pass_on(): lax.ppermute(block[1], 'dp', [(i, i - 1) for i in range(1, count - step +...]
    ppermute x16, starting transfers between devices: 13.1 us -> 14.1 us  [trade(): return lax.ppermute(block, axes, route[::-1] if backwards else route)]
  transfers between devices with their start and end apart: 21 -> 21, of which waited for: 12 -> 12; matrix products, arithmetic and copies ran while one was open for 0% -> 0% of each run, Pallas kernels for 28% -> 27%
where the time goes in v25:
time: 98.2 us; the launch traced here: 98 us
  waiting for transfers between devices  46.1 us (47%)
  Pallas kernels  27.4 us (28%)
  starting transfers between devices  23.6 us (24%)
    ppermute x16, waiting for transfers between devices, trade(): return lax.ppermute(block, axes, route[::-1] if backwards else route)  43.5 us
    pallas_call x11, Pallas kernels, call(): pl.pallas_call(body, in_specs=[NEAR] * len(arrays) + [ANYWHERE] * skip, o...  20.1 us
    ppermute x16, starting transfers between devices, trade(): return lax.ppermute(block, axes, route[::-1] if backwards else route)  14.1 us
    pallas_call x2, Pallas kernels, fetch(): pl.pallas_call(kernel, in_specs=[ANYWHERE] * len(arrays), out_specs=[NEAR...  7.32 us
    ppermute x2, starting transfers between devices, pass_on(): lax.ppermute(block[0], 'dp', [(i, i + 1) for i in range(step - 1, count -...  5.65 us
    ppermute x2, starting transfers between devices, pass_on(): lax.ppermute(block[1], 'dp', [(i, i - 1) for i in range(1, count - step +...  2.58 us
    ppermute x1, waiting for transfers between devices, on_device(): end = lax.ppermute(block, 'dp', [(1, 0), (count - 2, count - 1)])  2.57 us
  transfers between devices with their start and end apart: 21, of which 12 were waited for; matrix products, arithmetic and copies ran while one was open for 0% of the time, Pallas kernels for 27%

profile of v25, /device:TPU:0, one launch (start us, length us, event | category | flops | bytes accessed | tf_op | source)
XLA Modules:
  0.0 98.0 jit_solution(782429669100225150)
XLA Ops:
  0.0 1.2 %shard_map.40 = (bf16[128,2048]{1,0:T(8,128)(2,1)S(1)}, bf16[128,1792]{1,0:T(8,128)(2,1)S(1)}) custom-call(bf16[256,2048]{1,0:T(8,128)(2,1)} %acts_ref.3, bf16[256,7168]{1,0:T(8,128)(2,1)} %grads_ref.3), custom_call_target="tpu_custom_call" | custom-call | flops 1024 | bytes 1024 | tf_op jit(solution)/shard_map/pallas_call | solution.py:53
  1.2 5.0 %collective-permute-start.1 = (bf16[128,2048]{1,0:T(8,128)(2,1)S(1)}, bf16[128,2048]{1,0:T(8,128)(2,1)S(1)}, u32[]{:S(2)}, u32[]{:S(2)}) collective-permute-start(bf16[128,2048]{1,0:T(8,128)(2,1)S(1)} %get-tuple-element.28), channel_id=1, source_target_pairs={{0,4},{4,8},{8,12},{1,5},{5,9},{9,13},{2,6},{6,10},{10,14},{3,7},{... | collective-permute-start | bytes 1572872 | tf_op jit(solution)/shard_map/ppermute | solution.py:26
  6.2 1.3 %collective-permute-start.2 = (bf16[128,2048]{1,0:T(8,128)(2,1)S(1)}, bf16[128,2048]{1,0:T(8,128)(2,1)S(1)}, u32[]{:S(2)}, u32[]{:S(2)}) collective-permute-start(bf16[128,2048]{1,0:T(8,128)(2,1)S(1)} %get-tuple-element.28), channel_id=1, source_target_pairs={{4,0},{8,4},{12,8},{5,1},{9,5},{13,9},{6,2},{10,6},{14,10},{7,3},{... | collective-permute-start | bytes 1572872 | tf_op jit(solution)/shard_map/ppermute | solution.py:27
  7.5 6.1 %shard_map.37 = (bf16[2,1,1792,2048]{3,2,1,0:T(8,128)(2,1)S(1)}, bf16[256,2048]{1,0:T(8,128)(2,1)S(1)}, bf16[1792,256]{1,0:T(8,128)(2,1)S(1)}, bf16[1792,128]{1,...) custom-call(bf16[256,2048]{1,0:T(8,128)(2,1)} %acts_ref.3, bf16[256,7168]{1,0:T(8,128)(2,1)} %grads_ref.3, ...), custom_call_target="tpu_custom_call" | custom-call | flops 1024 | bytes 1024 | tf_op jit(solution)/shard_map/pallas_call | solution.py:53
  13.6 2.7 %collective-permute-start = (bf16[1792,128]{1,0:T(8,128)(2,1)S(1)}, bf16[1792,128]{1,0:T(8,128)(2,1)S(1)}, u32[]{:S(2)}, u32[]{:S(2)}) collective-permute-start(bf16[1792,128]{1,0:T(8,128)(2,1)S(1)} %get-tuple-element.27), channel_id=1, source_target_pairs={{0,4},{4,0},{8,12},{12,8},{1,5},{5,1},{9,13},{13,9},{2,6},{6,2},{1... | collective-permute-start | bytes 1376264 | tf_op jit(solution)/shard_map/ppermute | solution.py:22
  16.3 2.4 %collective-permute-start.5 = (bf16[128,1792]{1,0:T(8,128)(2,1)S(1)}, bf16[128,1792]{1,0:T(8,128)(2,1)S(1)}, u32[]{:S(2)}, u32[]{:S(2)}) collective-permute-start(bf16[128,1792]{1,0:T(8,128)(2,1)S(1)} %get-tuple-element.33), channel_id=1, source_target_pairs={{0,12},{4,8},{8,4},{12,0},{1,13},{5,9},{9,5},{13,1},{2,14},{6,10},... | collective-permute-start | bytes 1376264 | tf_op jit(solution)/shard_map/ppermute | solution.py:22
  18.8 4.4 %shard_map.38 = (f32[2,1792,256]{2,1,0:T(8,128)S(1)}, f32[8,128]{1,0:T(8,128)S(1)}) custom-call(bf16[256,2048]{1,0:T(8,128)(2,1)S(1)} %get-tuple-element.24.refs_0_, bf16[2,1,1792,2048]{3,2,1,0:T(8,128)(2,1)S(1)} %get-tuple-element.25.refs_1_.refs_2_), custom_call_target="tpu_custom_call" | custom-call | flops 1000000 | bytes 1024 | tf_op jit(solution)/shard_map/pallas_call | solution.py:41
  23.3 1.3 %collective-permute-start.8 = (bf16[128,2048]{1,0:T(8,128)(2,1)S(1)}, bf16[128,2048]{1,0:T(8,128)(2,1)S(1)}, u32[]{:S(2)}, u32[]{:S(2)}) collective-permute-start(bf16[128,2048]{1,0:T(8,128)(2,1)S(1)} %get-tuple-element.31.refs_2_.refs_0_.refs_1_), channel_id=1, source_target_pairs={{4,0},{8,4},{5,1},{9,5},{6,2},{10,6},{7,3},{11,7},{20,16},{24,20},... | collective-permute-start | bytes 1572872 | tf_op jit(solution)/shard_map/ppermute | solution.py:27
  24.6 0.7 collective-permute-start.9
  25.3 8.4 %collective-permute-done.refs_0_.refs_3_ = bf16[1792,128]{1,0:T(8,128)(2,1)S(1)} collective-permute-done((bf16[1792,128]{1,0:T(8,128)(2,1)S(1)}, bf16[1792,128]{1,0:T(8,128)(2,1)S(1)}, u32[]{:S(2)}, u32[]{:S(2)}) %collective-permute-start) | collective-permute-done | bytes 458784 | tf_op jit(solution)/shard_map/ppermute | solution.py:22
  33.7 9.6 %collective-permute-done.5.refs_0_ = bf16[128,1792]{1,0:T(8,128)(2,1)S(1)} collective-permute-done((bf16[128,1792]{1,0:T(8,128)(2,1)S(1)}, bf16[128,1792]{1,0:T(8,128)(2,1)S(1)}, u32[]{:S(2)}, u32[]{:S(2)}) %collective-permute-start.5) | collective-permute-done | bytes 458784 | tf_op jit(solution)/shard_map/ppermute | solution.py:22
  43.3 1.5 %collective-permute-start.6 = (bf16[128,1792]{1,0:T(8,128)(2,1)S(1)}, bf16[128,1792]{1,0:T(8,128)(2,1)S(1)}, u32[]{:S(2)}, u32[]{:S(2)}) collective-permute-start(bf16[128,1792]{1,0:T(8,128)(2,1)S(1)} %shard_map.45.refs_0_.refs_3_), channel_id=1, source_target_pairs={{0,2},{2,0},{1,3},{3,1},{4,6},{6,4},{5,7},{7,5},{8,10},{10,8},{9,1... | collective-permute-start | bytes 1376264 | tf_op jit(solution)/shard_map/ppermute | solution.py:22
  45.2 4.4 %shard_map.44 = (f32[2,1792,256]{2,1,0:T(8,128)S(1)}, f32[8,128]{1,0:T(8,128)S(1)}) custom-call(bf16[128,2048]{1,0:T(8,128)(2,1)S(1)} %shard_map.43.refs_0_, bf16[128,2048]{1,0:T(8,128)(2,1)S(1)} %collective-permute-done.4.refs_1_, bf16[2,1,1792,2048]{3,2,1,0:T(8,128)(2,1)S(1)} %get-tuple-element.25.refs_1_.refs_2_, f32[2,256]{1,0:T(2,128)S(1)} %shard_map.39.refs_3_), custom_call_target="tpu_custom_call" | custom-call | flops 1000000 | bytes 1024 | tf_op jit(solution)/shard_map/pallas_call | solution.py:41
  49.6 4.6 %collective-permute-done.6.refs_1_.refs_4_ = bf16[128,1792]{1,0:T(8,128)(2,1)S(1)} collective-permute-done((bf16[128,1792]{1,0:T(8,128)(2,1)S(1)}, bf16[128,1792]{1,0:T(8,128)(2,1)S(1)}, u32[]{:S(2)}, u32[]{:S(2)}) %collective-permute-start.6) | collective-permute-done | bytes 458784 | tf_op jit(solution)/shard_map/ppermute | solution.py:22
  54.4 1.6 %collective-permute-start.3 = (bf16[1792,128]{1,0:T(8,128)(2,1)S(1)}, bf16[1792,128]{1,0:T(8,128)(2,1)S(1)}, u32[]{:S(2)}, u32[]{:S(2)}) collective-permute-start(bf16[1792,128]{1,0:T(8,128)(2,1)S(1)} %shard_map.42.refs_0_), channel_id=1, source_target_pairs={{0,2},{2,0},{1,3},{3,1},{4,6},{6,4},{5,7},{7,5},{8,10},{10,8},{9,1... | collective-permute-start | bytes 1376264 | tf_op jit(solution)/shard_map/ppermute | solution.py:22
  55.9 1.3 %collective-permute-start.10 = (bf16[128,2048]{1,0:T(8,128)(2,1)S(1)}, bf16[128,2048]{1,0:T(8,128)(2,1)S(1)}, u32[]{:S(2)}, u32[]{:S(2)}) collective-permute-start(bf16[128,2048]{1,0:T(8,128)(2,1)S(1)} %shard_map.48.refs_0_), channel_id=1, source_target_pairs={{4,0},{8,12},{5,1},{9,13},{6,2},{10,14},{7,3},{11,15},{20,16},{24,... | collective-permute-start | bytes 1572872 | tf_op jit(solution)/shard_map/ppermute | solution.py:293
  57.2 3.3 %collective-permute-start.14 = (bf16[896,128]{1,0:T(8,128)(2,1)S(1)}, bf16[896,128]{1,0:T(8,128)(2,1)S(1)}, u32[]{:S(2)}, u32[]{:S(2)}) collective-permute-start(bf16[896,128]{1,0:T(8,128)(2,1)S(1)} %shard_map.52), channel_id=1, source_target_pairs={{0,8},{4,12},{8,0},{12,4},{1,9},{5,13},{9,1},{13,5},{2,10},{6,14},... | collective-permute-start | bytes 688136 | tf_op jit(solution)/shard_map/ppermute | solution.py:22
  60.5 4.4 %shard_map.46 = (f32[2,256,2048]{2,1,0:T(8,128)S(1)}, f32[8,128]{1,0:T(8,128)S(1)}) custom-call(bf16[128,1792]{1,0:T(8,128)(2,1)S(1)} %shard_map.45.refs_0_.refs_3_, bf16[128,1792]{1,0:T(8,128)(2,1)S(1)} %collective-permute-done.6.refs_1_.refs_4_, bf16[2,1,1792,2048]{3,2,1,0:T(8,128)(2,1)S(1)} %get-tuple-element.25.refs_1_.refs_2_, ...), custom_call_target="tpu_custom_call" | custom-call | flops 1000000 | bytes 1024 | tf_op jit(solution)/shard_map/pallas_call | solution.py:41
  65.0 2.3 %collective-permute-done.3.refs_1_ = bf16[1792,128]{1,0:T(8,128)(2,1)S(1)} collective-permute-done((bf16[1792,128]{1,0:T(8,128)(2,1)S(1)}, bf16[1792,128]{1,0:T(8,128)(2,1)S(1)}, u32[]{:S(2)}, u32[]{:S(2)}) %collective-permute-start.3) | collective-permute-done | bytes 458784 | tf_op jit(solution)/shard_map/ppermute | solution.py:22
  67.3 0.7 shard_map.47.refs_3_
  68.0 4.4 %shard_map.49 = (f32[2,1792,256]{2,1,0:T(8,128)S(1)}, f32[8,128]{1,0:T(8,128)S(1)}) custom-call(bf16[128,2048]{1,0:T(8,128)(2,1)S(1)} %shard_map.48.refs_0_, bf16[128,2048]{1,0:T(8,128)(2,1)S(1)} %collective-permute-done.11.refs_1_, bf16[2,1,1792,2048]{3,2,1,0:T(8,128)(2,1)S(1)} %get-tuple-element.25.refs_1_.refs_2_, f32[2,256]{1,0:T(2,128)S(1)} %shard_map.47.refs_3_), custom_call_target="tpu_custom_call" | custom-call | flops 1000000 | bytes 1024 | tf_op jit(solution)/shard_map/pallas_call | solution.py:41
  72.4 1.1 %collective-permute-done.15.refs_0_ = bf16[896,128]{1,0:T(8,128)(2,1)S(1)} collective-permute-done((bf16[896,128]{1,0:T(8,128)(2,1)S(1)}, bf16[896,128]{1,0:T(8,128)(2,1)S(1)}, u32[]{:S(2)}, u32[]{:S(2)}) %collective-permute-start.15) | collective-permute-done | bytes 229408 | tf_op jit(solution)/shard_map/ppermute | solution.py:22
  74.1 4.3 %collective-permute-done.14.refs_0_ = bf16[896,128]{1,0:T(8,128)(2,1)S(1)} collective-permute-done((bf16[896,128]{1,0:T(8,128)(2,1)S(1)}, bf16[896,128]{1,0:T(8,128)(2,1)S(1)}, u32[]{:S(2)}, u32[]{:S(2)}) %collective-permute-start.14) | collective-permute-done | bytes 229408 | tf_op jit(solution)/shard_map/ppermute | solution.py:22
  79.0 2.6 %collective-permute-done.10.refs_0_ = bf16[128,2048]{1,0:T(8,128)(2,1)S(1)} collective-permute-done((bf16[128,2048]{1,0:T(8,128)(2,1)S(1)}, bf16[128,2048]{1,0:T(8,128)(2,1)S(1)}, u32[]{:S(2)}, u32[]{:S(2)}) %collective-permute-start.10) | collective-permute-done | bytes 524320 | tf_op jit(solution)/shard_map/ppermute | solution.py:293
  81.7 4.2 %collective-permute-done.16.refs_2_ = bf16[896,128]{1,0:T(8,128)(2,1)S(1)} collective-permute-done((bf16[896,128]{1,0:T(8,128)(2,1)S(1)}, bf16[896,128]{1,0:T(8,128)(2,1)S(1)}, u32[]{:S(2)}, u32[]{:S(2)}) %collective-permute-start.16) | collective-permute-done | bytes 229408 | tf_op jit(solution)/shard_map/ppermute | solution.py:22
  85.9 0.7 shard_map.56
  87.2 0.7 collective-permute-start.13
  87.9 3.3 %collective-permute-done.18 = f32[2,256]{1,0:T(2,128)S(1)} collective-permute-done((f32[2,256]{1,0:T(2,128)S(1)}, f32[2,256]{1,0:T(2,128)S(1)}, u32[]{:S(2)}, u32[]{:S(2)}) %collective-permute-start.18) | collective-permute-done | bytes 2080 | tf_op jit(solution)/shard_map/ppermute | solution.py:22
  91.2 1.4 %collective-permute-done.13 = f32[2,256]{1,0:T(2,128)S(1)} collective-permute-done((f32[2,256]{1,0:T(2,128)S(1)}, f32[2,256]{1,0:T(2,128)S(1)}, u32[]{:S(2)}, u32[]{:S(2)}) %collective-permute-start.13) | collective-permute-done | bytes 2080 | tf_op jit(solution)/shard_map/ppermute | solution.py:22
  92.6 1.2 %collective-permute-done.19 = f32[2,256]{1,0:T(2,128)S(1)} collective-permute-done((f32[2,256]{1,0:T(2,128)S(1)}, f32[2,256]{1,0:T(2,128)S(1)}, u32[]{:S(2)}, u32[]{:S(2)}) %collective-permute-start.19) | collective-permute-done | bytes 2080 | tf_op jit(solution)/shard_map/ppermute | solution.py:22
  94.3 3.0 %collective-permute-done.20 = f32[2,256]{1,0:T(2,128)S(1)} collective-permute-done((f32[2,256]{1,0:T(2,128)S(1)}, f32[2,256]{1,0:T(2,128)S(1)}, u32[]{:S(2)}, u32[]{:S(2)}) %collective-permute-start.20) | collective-permute-done | bytes 2080 | tf_op jit(solution)/shard_map/ppermute | solution.py:22
  97.4 0.6 add.19
  (33 shorter events, 2.9 us)
Async XLA Ops:
  1.2 21.9 %collective-permute-start.1 = (bf16[128,2048]{1,0:T(8,128)(2,1)S(1)}, bf16[128,2048]{1,0:T(8,128)(2,1)S(1)}, u32[]{:S(2)}, u32[]{:S(2)}) collective-permute-start(bf16[128,2048]{1,0:T(8,128)(2,1)S(1)} %get-tuple-element.28), channel_id=1, source_target_pairs={{0,4},{4,8},{8,12},{1,5},{5,9},{9,13},{2,6},{6,10},{10,14},{3,7},{... | collective-permute-start | bytes 1572872 | tf_op jit(solution)/shard_map/ppermute | solution.py:26
  6.2 17.0 %collective-permute-start.2 = (bf16[128,2048]{1,0:T(8,128)(2,1)S(1)}, bf16[128,2048]{1,0:T(8,128)(2,1)S(1)}, u32[]{:S(2)}, u32[]{:S(2)}) collective-permute-start(bf16[128,2048]{1,0:T(8,128)(2,1)S(1)} %get-tuple-element.28), channel_id=1, source_target_pairs={{4,0},{8,4},{12,8},{5,1},{9,5},{13,9},{6,2},{10,6},{14,10},{7,3},{... | collective-permute-start | bytes 1572872 | tf_op jit(solution)/shard_map/ppermute | solution.py:27
  13.6 20.1 %collective-permute-start = (bf16[1792,128]{1,0:T(8,128)(2,1)S(1)}, bf16[1792,128]{1,0:T(8,128)(2,1)S(1)}, u32[]{:S(2)}, u32[]{:S(2)}) collective-permute-start(bf16[1792,128]{1,0:T(8,128)(2,1)S(1)} %get-tuple-element.27), channel_id=1, source_target_pairs={{0,4},{4,0},{8,12},{12,8},{1,5},{5,1},{9,13},{13,9},{2,6},{6,2},{1... | collective-permute-start | bytes 1376264 | tf_op jit(solution)/shard_map/ppermute | solution.py:22
  16.3 27.0 %collective-permute-start.5 = (bf16[128,1792]{1,0:T(8,128)(2,1)S(1)}, bf16[128,1792]{1,0:T(8,128)(2,1)S(1)}, u32[]{:S(2)}, u32[]{:S(2)}) collective-permute-start(bf16[128,1792]{1,0:T(8,128)(2,1)S(1)} %get-tuple-element.33), channel_id=1, source_target_pairs={{0,12},{4,8},{8,4},{12,0},{1,13},{5,9},{9,5},{13,1},{2,14},{6,10},... | collective-permute-start | bytes 1376264 | tf_op jit(solution)/shard_map/ppermute | solution.py:22
  23.2 22.0 %collective-permute-start.4 = (bf16[128,2048]{1,0:T(8,128)(2,1)S(1)}, bf16[128,2048]{1,0:T(8,128)(2,1)S(1)}, u32[]{:S(2)}, u32[]{:S(2)}) collective-permute-start(bf16[128,2048]{1,0:T(8,128)(2,1)S(1)} %shard_map.43.refs_0_), channel_id=1, source_target_pairs={{0,1},{1,0},{2,3},{3,2},{4,5},{5,4},{6,7},{7,6},{8,9},{9,8},{10,11... | collective-permute-start | bytes 1572872 | tf_op jit(solution)/shard_map/ppermute | solution.py:22
  23.3 30.9 %collective-permute-start.8 = (bf16[128,2048]{1,0:T(8,128)(2,1)S(1)}, bf16[128,2048]{1,0:T(8,128)(2,1)S(1)}, u32[]{:S(2)}, u32[]{:S(2)}) collective-permute-start(bf16[128,2048]{1,0:T(8,128)(2,1)S(1)} %get-tuple-element.31.refs_2_.refs_0_.refs_1_), channel_id=1, source_target_pairs={{4,0},{8,4},{5,1},{9,5},{6,2},{10,6},{7,3},{11,7},{20,16},{24,20},... | collective-permute-start | bytes 1572872 | tf_op jit(solution)/shard_map/ppermute | solution.py:27
  24.6 29.6 %collective-permute-start.9 = (bf16[128,2048]{1,0:T(8,128)(2,1)S(1)}, bf16[128,2048]{1,0:T(8,128)(2,1)S(1)}, u32[]{:S(2)}, u32[]{:S(2)}) collective-permute-start(bf16[128,2048]{1,0:T(8,128)(2,1)S(1)} %get-tuple-element.30.refs_1_.refs_2_), channel_id=1, source_target_pairs={{4,8},{8,12},{5,9},{9,13},{6,10},{10,14},{7,11},{11,15},{20,24},{2... | collective-permute-start | bytes 1572872 | tf_op jit(solution)/shard_map/ppermute | solution.py:26
  43.3 11.0 %collective-permute-start.6 = (bf16[128,1792]{1,0:T(8,128)(2,1)S(1)}, bf16[128,1792]{1,0:T(8,128)(2,1)S(1)}, u32[]{:S(2)}, u32[]{:S(2)}) collective-permute-start(bf16[128,1792]{1,0:T(8,128)(2,1)S(1)} %shard_map.45.refs_0_.refs_3_), channel_id=1, source_target_pairs={{0,2},{2,0},{1,3},{3,1},{4,6},{6,4},{5,7},{7,5},{8,10},{10,8},{9,1... | collective-permute-start | bytes 1376264 | tf_op jit(solution)/shard_map/ppermute | solution.py:22
  54.3 13.8 %collective-permute-start.11 = (bf16[128,2048]{1,0:T(8,128)(2,1)S(1)}, bf16[128,2048]{1,0:T(8,128)(2,1)S(1)}, u32[]{:S(2)}, u32[]{:S(2)}) collective-permute-start(bf16[128,2048]{1,0:T(8,128)(2,1)S(1)} %shard_map.48.refs_0_), channel_id=1, source_target_pairs={{0,1},{1,0},{2,3},{3,2},{4,5},{5,4},{6,7},{7,6},{8,9},{9,8},{10,11... | collective-permute-start | bytes 1572872 | tf_op jit(solution)/shard_map/ppermute | solution.py:22
  54.4 12.9 %collective-permute-start.3 = (bf16[1792,128]{1,0:T(8,128)(2,1)S(1)}, bf16[1792,128]{1,0:T(8,128)(2,1)S(1)}, u32[]{:S(2)}, u32[]{:S(2)}) collective-permute-start(bf16[1792,128]{1,0:T(8,128)(2,1)S(1)} %shard_map.42.refs_0_), channel_id=1, source_target_pairs={{0,2},{2,0},{1,3},{3,1},{4,6},{6,4},{5,7},{7,5},{8,10},{10,8},{9,1... | collective-permute-start | bytes 1376264 | tf_op jit(solution)/shard_map/ppermute | solution.py:22
  55.9 17.7 %collective-permute-start.15 = (bf16[896,128]{1,0:T(8,128)(2,1)S(1)}, bf16[896,128]{1,0:T(8,128)(2,1)S(1)}, u32[]{:S(2)}, u32[]{:S(2)}) collective-permute-start(bf16[896,128]{1,0:T(8,128)(2,1)S(1)} %shard_map.54), channel_id=1, source_target_pairs={{0,8},{4,12},{8,0},{12,4},{1,9},{5,13},{9,1},{13,5},{2,10},{6,14},... | collective-permute-start | bytes 688136 | tf_op jit(solution)/shard_map/ppermute | solution.py:22
  55.9 25.6 %collective-permute-start.10 = (bf16[128,2048]{1,0:T(8,128)(2,1)S(1)}, bf16[128,2048]{1,0:T(8,128)(2,1)S(1)}, u32[]{:S(2)}, u32[]{:S(2)}) collective-permute-start(bf16[128,2048]{1,0:T(8,128)(2,1)S(1)} %shard_map.48.refs_0_), channel_id=1, source_target_pairs={{4,0},{8,12},{5,1},{9,13},{6,2},{10,14},{7,3},{11,15},{20,16},{24,... | collective-permute-start | bytes 1572872 | tf_op jit(solution)/shard_map/ppermute | solution.py:293
  57.2 21.2 %collective-permute-start.14 = (bf16[896,128]{1,0:T(8,128)(2,1)S(1)}, bf16[896,128]{1,0:T(8,128)(2,1)S(1)}, u32[]{:S(2)}, u32[]{:S(2)}) collective-permute-start(bf16[896,128]{1,0:T(8,128)(2,1)S(1)} %shard_map.52), channel_id=1, source_target_pairs={{0,8},{4,12},{8,0},{12,4},{1,9},{5,13},{9,1},{13,5},{2,10},{6,14},... | collective-permute-start | bytes 688136 | tf_op jit(solution)/shard_map/ppermute | solution.py:22
  73.6 8.1 %collective-permute-start.17 = (bf16[896,128]{1,0:T(8,128)(2,1)S(1)}, bf16[896,128]{1,0:T(8,128)(2,1)S(1)}, u32[]{:S(2)}, u32[]{:S(2)}) collective-permute-start(bf16[896,128]{1,0:T(8,128)(2,1)S(1)} %shard_map.55.refs_1_), channel_id=1, source_target_pairs={{0,2},{2,0},{1,3},{3,1},{4,6},{6,4},{5,7},{7,5},{8,10},{10,8},{9,1... | collective-permute-start | bytes 688136 | tf_op jit(solution)/shard_map/ppermute | solution.py:22
  78.4 7.5 %collective-permute-start.16 = (bf16[896,128]{1,0:T(8,128)(2,1)S(1)}, bf16[896,128]{1,0:T(8,128)(2,1)S(1)}, u32[]{:S(2)}, u32[]{:S(2)}) collective-permute-start(bf16[896,128]{1,0:T(8,128)(2,1)S(1)} %shard_map.53.refs_0_), channel_id=1, source_target_pairs={{0,2},{2,0},{1,3},{3,1},{4,6},{6,4},{5,7},{7,5},{8,10},{10,8},{9,1... | collective-permute-start | bytes 688136 | tf_op jit(solution)/shard_map/ppermute | solution.py:22
  79.0 8.9 %collective-permute-start.7 = (f32[2,256]{1,0:T(2,128)S(1)}, f32[2,256]{1,0:T(2,128)S(1)}, u32[]{:S(2)}, u32[]{:S(2)}) collective-permute-start(f32[2,256]{1,0:T(2,128)S(1)} %shard_map.47.refs_3_), channel_id=1, source_target_pairs={{0,4},{4,0},{8,12},{12,8},{1,5},{5,1},{9,13},{13,9},{2,6},{6,2},{1... | collective-permute-start | bytes 6152 | tf_op jit(solution)/shard_map/ppermute | solution.py:22
  81.6 5.1 %collective-permute-start.12 = (bf16[128,2048]{1,0:T(8,128)(2,1)S(1)}, bf16[128,2048]{1,0:T(8,128)(2,1)S(1)}, u32[]{:S(2)}, u32[]{:S(2)}) collective-permute-start(bf16[128,2048]{1,0:T(8,128)(2,1)S(1)} %shard_map.50.refs_0_), channel_id=1, source_target_pairs={{0,1},{1,0},{2,3},{3,2},{4,5},{5,4},{6,7},{7,6},{8,9},{9,8},{10,11... | collective-permute-start | bytes 1572872 | tf_op jit(solution)/shard_map/ppermute | solution.py:22
  86.6 4.5 %collective-permute-start.18 = (f32[2,256]{1,0:T(2,128)S(1)}, f32[2,256]{1,0:T(2,128)S(1)}, u32[]{:S(2)}, u32[]{:S(2)}) collective-permute-start(f32[2,256]{1,0:T(2,128)S(1)} %shard_map.56), channel_id=1, source_target_pairs={{0,8},{4,12},{8,0},{12,4},{1,9},{5,13},{9,1},{13,5},{2,10},{6,14},... | collective-permute-start | bytes 6152 | tf_op jit(solution)/shard_map/ppermute | solution.py:22
  87.2 5.4 %collective-permute-start.13 = (f32[2,256]{1,0:T(2,128)S(1)}, f32[2,256]{1,0:T(2,128)S(1)}, u32[]{:S(2)}, u32[]{:S(2)}) collective-permute-start(f32[2,256]{1,0:T(2,128)S(1)} %shard_map.51), channel_id=1, source_target_pairs={{0,12},{4,8},{8,4},{12,0},{1,13},{5,9},{9,5},{13,1},{2,14},{6,10},... | collective-permute-start | bytes 6152 | tf_op jit(solution)/shard_map/ppermute | solution.py:22
  92.6 1.2 %collective-permute-start.19 = (f32[2,256]{1,0:T(2,128)S(1)}, f32[2,256]{1,0:T(2,128)S(1)}, u32[]{:S(2)}, u32[]{:S(2)}) collective-permute-start(f32[2,256]{1,0:T(2,128)S(1)} %add_add_fusion), channel_id=1, source_target_pairs={{0,1},{1,0},{2,3},{3,2},{4,5},{5,4},{6,7},{7,6},{8,9},{9,8},{10,11... | collective-permute-start | bytes 6152 | tf_op jit(solution)/shard_map/ppermute | solution.py:22
  93.8 3.6 %collective-permute-start.20 = (f32[2,256]{1,0:T(2,128)S(1)}, f32[2,256]{1,0:T(2,128)S(1)}, u32[]{:S(2)}, u32[]{:S(2)}) collective-permute-start(f32[2,256]{1,0:T(2,128)S(1)} %add.18), channel_id=1, source_target_pairs={{0,2},{2,0},{1,3},{3,1},{4,6},{6,4},{5,7},{7,5},{8,10},{10,8},{9,1... | collective-permute-start | bytes 6152 | tf_op jit(solution)/shard_map/ppermute | solution.py:22
